TPU v7x, 32 devices: a whole 2x2x4 slice. The times are simulated.
32 devices in a mesh: dp: 8 (over y, x, core), tensor: 4 (over z).
Axes of the slice: x: 2, y: 2, z: 4, core: 2. Of those that a mesh axis runs over, the one named last changes fastest.
Arguments:
- tokens: bfloat16 [8192, 2048], P(('dp', 'tensor')), may hold values from -6 to 6
- cotangent: bfloat16 [8192, 2048], P(('dp', 'tensor')), may hold values from -6 to 6
- seg_ids: int32 [8, 1024], P('dp'), may hold values from 0 to 15, never falling along the last dimension, each value on 1 to 512 neighbouring positions
- keep_mask: int32 [8, 1024], P('dp'), may hold values from 0 to 1, as said below
- routes: int32 [8192, 8], P('dp'), may hold values from 0 to 15, all different within a row; in each aligned block of 1024 rows (0 to 1023, 1024 to 2047, ...) at most 768 rows name the same one
- attn_gain: float32 [2048], replicated, may hold values from 0.1 to 1.9
- w_query: bfloat16 [2048, 2048], P(None, 'tensor'), may hold values from -0.125 to 0.125
- w_key: bfloat16 [2048, 2048], P(None, 'tensor'), may hold values from -0.125 to 0.125
- w_value: bfloat16 [2048, 2048], P(None, 'tensor'), may hold values from -0.125 to 0.125
- w_out: bfloat16 [2048, 2048], P(None, 'tensor'), may hold values from -0.5 to 0.5
- q_gain: float32 [2048], P('tensor'), may hold values from 0.1 to 1.9
- k_gain: float32 [2048], P('tensor'), may hold values from 0.1 to 1.9
- ffn_gain: float32 [2048], replicated, may hold values from 0.1 to 1.9
- router: bfloat16 [2048, 16], replicated, may hold values from -0.06591797 to 0.06591797
- w_gate: bfloat16 [16, 2048, 1024], P(None, None, 'tensor'), may hold values from -0.125 to 0.125
- w_up: bfloat16 [16, 2048, 1024], P(None, None, 'tensor'), may hold values from -0.125 to 0.125
- w_down: bfloat16 [16, 2048, 1024], P(None, None, 'tensor'), may hold values from -1.5 to 1.5
Outputs:
- layer_out: bfloat16 [8192, 2048], P(('dp', 'tensor'))
- tokens_grad: float32 [8192, 2048], P(('dp', 'tensor'))
- w_query_grad: float32 [2048, 2048], P('dp', 'tensor')
- w_key_grad: float32 [2048, 2048], P('dp', 'tensor')
- w_value_grad: float32 [2048, 2048], P('dp', 'tensor')
- w_out_grad: float32 [2048, 2048], P('dp', 'tensor')
- attn_gain_grad: float32 [2048], replicated
- q_gain_grad: float32 [2048], replicated
- k_gain_grad: float32 [2048], replicated
- ffn_gain_grad: float32 [2048], replicated
- router_grad: float32 [2048, 16], replicated
- w_gate_grad: float32 [16, 2048, 1024], P('dp', None, 'tensor')
- w_up_grad: float32 [16, 2048, 1024], P('dp', None, 'tensor')
- w_down_grad: float32 [16, 2048, 1024], P('dp', None, 'tensor')
Inputs may be any that keep to these rules, and one draw needn't show every extreme that they name: `seg_ids`: numbers never fall along a sequence; a run of equal numbers is one document of at most 512 positions. `keep_mask`: the zeros of a sequence, if any, form its tail. `routes`: each row names 8 different experts; within the rows of one index of dp (aligned blocks of 1024 rows) no expert is named by more than 768 rows.
All inputs are finite; a program needn't handle non-finite values.
Results may differ from a plain program's by a relative error of at most 0.015.
Values may be sent and summed in bfloat16 or wider, within the bound.
No kernel may reach another device: no remote copies, remote signals or barrier semaphores. Data moves between devices by JAX's collectives and lax.ppermute only.
A program may use at most 448 MiB of HBM per device.

v0:
```python
import jax
import jax.numpy as jnp
from jax import lax
from jax.sharding import PartitionSpec as P

D = 2048
HEAD = 128
CAP = 768


EPSILON = 1e-05


def rms_scale(values):
    return lax.rsqrt(jnp.mean(values * values, axis=-1, keepdims=True) + EPSILON)


def norm_back(grad_values, values, scale_col, gain_vec):
    weighted = grad_values * gain_vec
    inner_mean = jnp.mean(weighted * values, axis=-1, keepdims=True)
    return scale_col * weighted - values * (scale_col * scale_col * scale_col) * inner_mean


def rope_tables(length, width):
    half_width = width // 2
    frequency = jnp.power(10000.0, -jnp.arange(half_width, dtype=jnp.float32) * 2.0 / width)
    angles = jnp.arange(length, dtype=jnp.float32)[:, None] * frequency[None, :]
    cosine = jnp.concatenate([jnp.cos(angles), jnp.cos(angles)], axis=1)
    sinus_table = jnp.concatenate([jnp.sin(angles), jnp.sin(angles)], axis=1)
    return (cosine[:, None, :], sinus_table[:, None, :])


def rotate(values, cosine, sinus_table):
    half_width = values.shape[-1] // 2
    turned = jnp.concatenate([-values[..., half_width:], values[..., :half_width]], axis=-1)
    return values * cosine + turned * sinus_table


def rotate_back(grad_values, cosine, sinus_table):
    half_width = grad_values.shape[-1] // 2
    scaled = grad_values * sinus_table
    return grad_values * cosine + jnp.concatenate(
        [scaled[..., half_width:], -scaled[..., :half_width]], axis=-1
    )


def mask_block(seg_ids, keep_mask, block_start, block_rows, block_end):
    query_pos = block_start + jnp.arange(block_rows)
    key_pos = jnp.arange(block_end)
    causal = key_pos[None, :] <= query_pos[:, None]
    itself = key_pos[None, :] == query_pos[:, None]
    same_doc = (
        seg_ids[:, block_start : block_start + block_rows, None] == seg_ids[:, None, :block_end]
    )
    live = (keep_mask[:, None, :block_end] == 1) | itself[None]
    return (same_doc & causal[None] & live)[:, None]


def expert_pre(picked_rows, gate_w, up_w):
    pre_gate = jnp.dot(picked_rows, gate_w, preferred_element_type=jnp.float32)
    pre_up = jnp.dot(picked_rows, up_w, preferred_element_type=jnp.float32)
    return (pre_gate, pre_up)


def contract_last(left, right):
    return lax.dot_general(
        left, right, (((1,), (1,)), ((), ())), preferred_element_type=jnp.float32
    )


def contract_first(left, right):
    return lax.dot_general(
        left, right, (((0,), (0,)), ((), ())), preferred_element_type=jnp.float32
    )


def slots_to_rows(slot_values, place_col):
    padding = jnp.zeros((1,) + slot_values.shape[1:], slot_values.dtype)
    return jnp.take(jnp.concatenate([slot_values, padding], axis=0), place_col, axis=0)


def local(
    tokens,
    cotangent,
    seg_ids,
    keep_mask,
    routes,
    attn_gain,
    w_query,
    w_key,
    w_value,
    w_out,
    q_gain,
    k_gain,
    ffn_gain,
    router,
    w_gate,
    w_up,
    w_down,
):
    tensor_parts = lax.axis_size("tensor")
    tensor_index = lax.axis_index("tensor")
    shard_rows = tokens.shape[0]
    group_rows = shard_rows * tensor_parts
    seq_count, length = seg_ids.shape
    local_width = w_query.shape[1]
    local_heads = local_width // HEAD
    expert_count = w_gate.shape[0]
    query_block = min(512, length)
    score_scale = HEAD ** (-0.5)
    shape_four = (seq_count, length, local_heads, HEAD)
    inputs = tokens.astype(jnp.float32)
    first_scale = rms_scale(inputs)
    normed = (inputs * first_scale * attn_gain).astype(jnp.bfloat16)
    normed_all = lax.all_gather(normed, "tensor", axis=0, tiled=True)
    query_raw = jnp.dot(normed_all, w_query, preferred_element_type=jnp.float32)
    key_raw = jnp.dot(normed_all, w_key, preferred_element_type=jnp.float32)
    value_low = jnp.dot(normed_all, w_value, preferred_element_type=jnp.float32).astype(
        jnp.bfloat16
    )
    query_sq, key_sq = lax.psum(
        (jnp.sum(query_raw * query_raw, axis=1), jnp.sum(key_raw * key_raw, axis=1)), "tensor"
    )
    query_scale = lax.rsqrt(query_sq / D + EPSILON)[:, None]
    key_scale = lax.rsqrt(key_sq / D + EPSILON)[:, None]
    cosine, sinus_table = rope_tables(length, HEAD)
    query_low = rotate(
        (query_raw * query_scale * q_gain).reshape(shape_four), cosine, sinus_table
    ).astype(jnp.bfloat16)
    key_low = rotate(
        (key_raw * key_scale * k_gain).reshape(shape_four), cosine, sinus_table
    ).astype(jnp.bfloat16)
    value_heads = value_low.reshape(shape_four)
    outputs = []
    maxima = []
    for block_start in range(0, length, query_block):
        block_end = block_start + query_block
        allowed = mask_block(seg_ids, keep_mask, block_start, query_block, block_end)
        scores = (
            jnp.einsum(
                "sqhd,skhd->shqk",
                query_low[:, block_start:block_end],
                key_low[:, :block_end],
                preferred_element_type=jnp.float32,
            )
            * score_scale
        )
        scores = jnp.where(allowed, scores, -1e30)
        row_max = jnp.max(scores, axis=-1, keepdims=True)
        exp_scores = jnp.exp(scores - row_max)
        row_total = jnp.sum(exp_scores, axis=-1, keepdims=True)
        weights = (exp_scores / row_total).astype(jnp.bfloat16)
        outputs.append(
            jnp.einsum(
                "shqk,skhd->sqhd",
                weights,
                value_heads[:, :block_end],
                preferred_element_type=jnp.float32,
            )
        )
        maxima.append(row_max + jnp.log(row_total))
    attended = (
        jnp.concatenate(outputs, axis=1).astype(jnp.bfloat16).reshape(group_rows, local_width)
    )
    log_totals = jnp.concatenate(maxima, axis=2)
    picked_rows = attended
    attn_sum = lax.psum_scatter(
        contract_last(picked_rows, w_out), "tensor", scatter_dimension=0, tiled=True
    )
    middle = inputs + attn_sum
    second_scale = rms_scale(middle)
    ffn_in = (middle * second_scale * ffn_gain).astype(jnp.bfloat16)
    ffn_all = lax.all_gather(ffn_in, "tensor", axis=0, tiled=True)
    logits = jnp.dot(ffn_all, router, preferred_element_type=jnp.float32)
    expert_probs = jax.nn.softmax(logits, axis=-1)
    expert_ids = jnp.arange(expert_count)
    routed = jnp.sum((routes[:, :, None] == expert_ids[None, None, :]).astype(jnp.float32), axis=1)
    combine = expert_probs * routed
    routed_int = routed.astype(jnp.int32)
    running_count = jnp.cumsum(routed_int, axis=0)
    counts = running_count[-1]
    slot_place = jnp.where(routed_int > 0, running_count - 1, CAP)
    place_cols = slot_place.T
    slot_ids = jnp.arange(CAP, dtype=jnp.int32)

    def table_row(count_col):
        return jnp.sum((count_col[None, :] <= slot_ids[:, None]).astype(jnp.int32), axis=1)

    valid_slots = slot_ids[None, :] < counts[:, None]
    table = jnp.where(valid_slots, lax.map(table_row, running_count.T), 0)
    valid = valid_slots.astype(jnp.float32)
    slot_gate = jnp.take_along_axis(combine.T, table, axis=1) * valid

    def expert_forward(running, operands):
        gate_w, up_w, down_w, picks, gate_col, place_col = operands
        pre_gate, pre_up = expert_pre(ffn_all[picks], gate_w, up_w)
        inner_act = (jax.nn.silu(pre_gate) * pre_up).astype(jnp.bfloat16)
        result = contract_last(inner_act, down_w)
        running = running + slots_to_rows(result * gate_col[:, None], place_col)
        saved_pre = (pre_gate, pre_up)
        return (running, saved_pre)

    expert_total, kept_pre = lax.scan(
        expert_forward,
        jnp.zeros((group_rows, D), jnp.float32),
        (w_gate, w_up, w_down, table, slot_gate, place_cols),
    )
    expert_sum = lax.psum_scatter(expert_total, "tensor", scatter_dimension=0, tiled=True)
    layer_out = (middle + expert_sum).astype(jnp.bfloat16)
    out_grad = cotangent.astype(jnp.float32)
    grad_all = lax.all_gather(cotangent, "tensor", axis=0, tiled=True)
    scan_inputs = (
        w_gate,
        w_up,
        w_down,
        table,
        slot_gate,
        valid,
        place_cols,
        kept_pre[0],
        kept_pre[1],
    )

    def expert_backward(rows_running, operands):
        gate_w, up_w, down_w, picks, gate_col, valid_row, place_col = operands[:7]
        picked_rows = ffn_all[picks]
        pre_gate, pre_up = (operands[7], operands[8])
        sigmoid_gate = jax.nn.sigmoid(pre_gate)
        activated = pre_gate * sigmoid_gate
        inner_act = (activated * pre_up).astype(jnp.bfloat16)
        grad_picked = grad_all[picks]
        back_inner = jnp.dot(grad_picked, down_w, preferred_element_type=jnp.float32)
        slot_dgate = jnp.sum(inner_act.astype(jnp.float32) * back_inner, axis=1) * valid_row
        scaled_grad = (grad_picked.astype(jnp.float32) * gate_col[:, None]).astype(jnp.bfloat16)
        inner_grad = jnp.dot(scaled_grad, down_w, preferred_element_type=jnp.float32)
        down_wgrad = contract_first(scaled_grad, inner_act)
        gate_pre_grad = (
            inner_grad * pre_up * sigmoid_gate * (1.0 + pre_gate * (1.0 - sigmoid_gate))
        ).astype(jnp.bfloat16)
        up_pre_grad = (inner_grad * activated).astype(jnp.bfloat16)
        gate_wgrad = contract_first(picked_rows, gate_pre_grad)
        up_wgrad = contract_first(picked_rows, up_pre_grad)
        back_rows = contract_last(gate_pre_grad, gate_w) + contract_last(up_pre_grad, up_w)
        rows_running = rows_running + slots_to_rows(back_rows, place_col)
        gate_column = slots_to_rows(slot_dgate, place_col)
        return (rows_running, (gate_wgrad, up_wgrad, down_wgrad, gate_column))

    rows_grad, (gate_grads, up_grads, down_grads, gate_columns) = lax.scan(
        expert_backward, jnp.zeros((group_rows, D), jnp.float32), scan_inputs
    )
    gate_grad = gate_columns.T
    gate_done, up_done, down_done = (
        lax.psum_scatter(gate_grads, "dp", scatter_dimension=0, tiled=True),
        lax.psum_scatter(up_grads, "dp", scatter_dimension=0, tiled=True),
        lax.psum_scatter(down_grads, "dp", scatter_dimension=0, tiled=True),
    )
    rows_grad_sum, gate_grad_sum = (
        lax.psum_scatter(rows_grad, "tensor", scatter_dimension=0, tiled=True),
        lax.psum_scatter(gate_grad, "tensor", scatter_dimension=0, tiled=True),
    )
    own_start = tensor_index * shard_rows
    own_probs = lax.dynamic_slice_in_dim(expert_probs, own_start, shard_rows, 0)
    logit_grad = (
        own_probs * (gate_grad_sum - jnp.sum(gate_grad_sum * own_probs, axis=-1, keepdims=True))
    ).astype(jnp.bfloat16)
    ffn_grad = rows_grad_sum + contract_last(logit_grad, router)
    router_part = contract_first(ffn_in, logit_grad)
    ffn_gain_part = jnp.sum(ffn_grad * middle * second_scale, axis=0)
    middle_grad = out_grad + norm_back(ffn_grad, middle, second_scale, ffn_gain)
    middle_all = lax.all_gather(middle_grad.astype(jnp.bfloat16), "tensor", axis=0, tiled=True)
    attended_grad = jnp.dot(middle_all, w_out, preferred_element_type=jnp.float32).astype(
        jnp.bfloat16
    )
    out_wgrad = contract_first(middle_all, attended)
    attended_heads = attended_grad.reshape(shape_four)
    query_parts = []
    key_acc = jnp.zeros(shape_four, jnp.float32)
    value_acc = jnp.zeros(shape_four, jnp.float32)
    for block_start in range(0, length, query_block):
        block_end = block_start + query_block
        allowed = mask_block(seg_ids, keep_mask, block_start, query_block, block_end)
        scores = (
            jnp.einsum(
                "sqhd,skhd->shqk",
                query_low[:, block_start:block_end],
                key_low[:, :block_end],
                preferred_element_type=jnp.float32,
            )
            * score_scale
        )
        weights = jnp.where(allowed, jnp.exp(scores - log_totals[:, :, block_start:block_end]), 0.0)
        prob_grad = jnp.einsum(
            "sqhd,skhd->shqk",
            attended_heads[:, block_start:block_end],
            value_heads[:, :block_end],
            preferred_element_type=jnp.float32,
        )
        row_inner = jnp.sum(prob_grad * weights, axis=-1, keepdims=True)
        score_grad = (weights * (prob_grad - row_inner)).astype(jnp.bfloat16)
        query_parts.append(
            jnp.einsum(
                "shqk,skhd->sqhd",
                score_grad,
                key_low[:, :block_end],
                preferred_element_type=jnp.float32,
            )
            * score_scale
        )
        key_acc = key_acc.at[:, :block_end].add(
            jnp.einsum(
                "shqk,sqhd->skhd",
                score_grad,
                query_low[:, block_start:block_end],
                preferred_element_type=jnp.float32,
            )
            * score_scale
        )
        value_acc = value_acc.at[:, :block_end].add(
            jnp.einsum(
                "shqk,sqhd->skhd",
                weights.astype(jnp.bfloat16),
                attended_heads[:, block_start:block_end],
                preferred_element_type=jnp.float32,
            )
        )
    query_normed_grad = rotate_back(
        jnp.concatenate(query_parts, axis=1), cosine, sinus_table
    ).reshape(group_rows, local_width)
    key_normed_grad = rotate_back(key_acc, cosine, sinus_table).reshape(group_rows, local_width)
    q_gain_part = jnp.sum(query_normed_grad * query_raw * query_scale, axis=0)
    k_gain_part = jnp.sum(key_normed_grad * key_raw * key_scale, axis=0)
    query_weighted = query_normed_grad * q_gain
    key_weighted = key_normed_grad * k_gain
    query_dot, key_dot = lax.psum(
        (jnp.sum(query_weighted * query_raw, axis=1), jnp.sum(key_weighted * key_raw, axis=1)),
        "tensor",
    )
    query_cube = query_scale * query_scale * query_scale
    key_cube = key_scale * key_scale * key_scale
    query_raw_grad = (
        query_scale * query_weighted - query_raw * query_cube * (query_dot / D)[:, None]
    ).astype(jnp.bfloat16)
    key_raw_grad = (key_scale * key_weighted - key_raw * key_cube * (key_dot / D)[:, None]).astype(
        jnp.bfloat16
    )
    value_grad = value_acc.reshape(group_rows, local_width).astype(jnp.bfloat16)
    query_wgrad = contract_first(normed_all, query_raw_grad)
    key_wgrad = contract_first(normed_all, key_raw_grad)
    value_wgrad = contract_first(normed_all, value_grad)
    normed_grad = lax.psum_scatter(
        contract_last(query_raw_grad, w_query)
        + contract_last(key_raw_grad, w_key)
        + contract_last(value_grad, w_value),
        "tensor",
        scatter_dimension=0,
        tiled=True,
    )
    attn_gain_part = jnp.sum(normed_grad * inputs * first_scale, axis=0)
    tokens_grad = middle_grad + norm_back(normed_grad, inputs, first_scale, attn_gain)
    gain_start = tensor_index * local_width
    q_full = lax.dynamic_update_slice_in_dim(
        jnp.zeros((D,), jnp.float32), q_gain_part, gain_start, 0
    )
    k_full = lax.dynamic_update_slice_in_dim(
        jnp.zeros((D,), jnp.float32), k_gain_part, gain_start, 0
    )
    attn_gain_grad, q_gain_grad, k_gain_grad, ffn_gain_grad, router_grad = lax.psum(
        (attn_gain_part, q_full, k_full, ffn_gain_part, router_part), ("dp", "tensor")
    )
    query_done, key_done, value_done, out_done = (
        lax.psum_scatter(query_wgrad, "dp", scatter_dimension=0, tiled=True),
        lax.psum_scatter(key_wgrad, "dp", scatter_dimension=0, tiled=True),
        lax.psum_scatter(value_wgrad, "dp", scatter_dimension=0, tiled=True),
        lax.psum_scatter(out_wgrad, "dp", scatter_dimension=0, tiled=True),
    )
    return (
        layer_out,
        tokens_grad,
        query_done,
        key_done,
        value_done,
        out_done,
        attn_gain_grad,
        q_gain_grad,
        k_gain_grad,
        ffn_gain_grad,
        router_grad,
        gate_done,
        up_done,
        down_done,
    )


def solution(mesh):
    in_specs = (
        P(("dp", "tensor"), None),
        P(("dp", "tensor"), None),
        P("dp", None),
        P("dp", None),
        P("dp", None),
        P(),
        P(None, "tensor"),
        P(None, "tensor"),
        P(None, "tensor"),
        P(None, "tensor"),
        P("tensor"),
        P("tensor"),
        P(),
        P(),
        P(None, None, "tensor"),
        P(None, None, "tensor"),
        P(None, None, "tensor"),
    )
    out_specs = (
        P(("dp", "tensor"), None),
        P(("dp", "tensor"), None),
        P("dp", "tensor"),
        P("dp", "tensor"),
        P("dp", "tensor"),
        P("dp", "tensor"),
        P(),
        P(),
        P(),
        P(),
        P(),
        P("dp", None, "tensor"),
        P("dp", None, "tensor"),
        P("dp", None, "tensor"),
    )
    return jax.shard_map(local, mesh=mesh, in_specs=in_specs, out_specs=out_specs, check_vma=False)
```

profile of v0, /device:TPU:0, one launch (start us, length us, event | category | flops | bytes accessed | tf_op | source)
XLA Modules:
  0.0 3950.9 jit_solution(3432891503416321098)
XLA Ops:
  17.5 78.7 %all-gather.5.cloned.1.call-done = bf16[1024,2048]{1,0:T(8,128)(2,1)} async-done(((bf16[256,2048]{1,0:T(8,128)(2,1)}), bf16[1024,2048]{1,0:T(8,128)(2,1)}) %all-gather.5.cloned.1.call-update) | async-done | bytes 4194320 | tf_op jit(solution)/shard_map/all_gather | solution.py:115
  170.6 143.6 %reduce-scatter.13.cloned.1.call-done = f32[256,2048]{1,0:T(8,128)} async-done(((f32[1024,2048]{1,0:T(8,128)}), f32[256,2048]{1,0:T(8,128)}) %reduce-scatter.13.cloned.1.call-update) | async-done | bytes 2097168 | tf_op jit(solution)/shard_map/reduce_scatter | solution.py:167
  319.5 80.8 %all-gather.7.cloned.1.call-done = bf16[1024,2048]{1,0:T(8,128)(2,1)} async-done(((bf16[256,2048]{1,0:T(8,128)(2,1)}), bf16[1024,2048]{1,0:T(8,128)(2,1)}) %all-gather.7.cloned.1.call-update) | async-done | bytes 4194320 | tf_op jit(solution)/shard_map/all_gather | solution.py:173
  418.3 97.2 %gather_fusion.6 = f32[12288]{0:T(1024)S(1)} fusion(f32[16,1024]{1,0:T(8,128)S(1)} %get-tuple-element.443, s32[12288]{0:T(1024)S(1)} %reshape.1015), kind=kCustom, calls=%fused_computation.6 | custom fusion | bytes 196608 | tf_op jit(solution)/shard_map/jit(take_along_axis)/gather | solution.py:192
  515.7 708.6 %while.55 = (s32[]{:T(128)}, f32[1024,2048]{1,0:T(8,128)}, f32[16,768,256]{2,1,0:T(8,128)}, f32[16,768,256]{2,1,0:T(8,128)}, s32[16,768]{1,0:T(8,128)S(1)}, /*in...) while((s32[]{:T(128)}, f32[1024,2048]{1,0:T(8,128)}, ...), condition=%wide.region_20.22_spmd.clone.clone, body=%wide.region_19.21_spmd.clone.sunk.clone | while | flops 2424976640 | bytes 93910184 | solution.py:203
  538.3 11.8 gather_fusion.1
  579.0 11.8 gather_fusion.1
  623.5 11.8 gather_fusion.1
  668.0 11.8 gather_fusion.1
  712.5 11.8 gather_fusion.1
  757.0 11.8 gather_fusion.1
  801.6 11.8 gather_fusion.1
  846.1 11.8 gather_fusion.1
  890.6 11.8 gather_fusion.1
  935.2 11.8 gather_fusion.1
  979.7 11.8 gather_fusion.1
  1024.3 11.8 gather_fusion.1
  1068.7 11.8 gather_fusion.1
  1113.3 11.8 gather_fusion.1
  1157.9 11.8 gather_fusion.1
  1202.4 11.8 gather_fusion.1
  1224.3 1109.1 %while.56 = (s32[]{:T(128)}, f32[1024,2048]{1,0:T(8,128)}, f32[16,2048,256]{2,1,0:T(8,128)}, f32[16,2048,256]{2,1,0:T(8,128)}, f32[16,2048,256]{2,1,0:T(8,128)},...) while((s32[]{:T(128)}, f32[1024,2048]{1,0:T(8,128)}, ...), condition=%wide.region_24.26_spmd.clone.clone, body=%wide.region_22.25_spmd.clone.sunk.clone | while | flops 5658010624 | bytes 155195680 | solution.py:248
  1264.6 11.8 gather_fusion.3
  1330.2 11.8 gather_fusion.3
  1342.0 10.2 select_add_fusion.7
  1399.7 11.8 gather_fusion.3
  1411.5 10.2 select_add_fusion.7
  1469.2 11.8 gather_fusion.3
  1481.0 10.2 select_add_fusion.7
  1538.8 11.8 gather_fusion.3
  1550.6 10.2 select_add_fusion.7
  1608.3 11.8 gather_fusion.3
  1620.2 10.2 select_add_fusion.7
  1677.9 11.8 gather_fusion.3
  1689.7 10.2 select_add_fusion.7
  1747.4 11.8 gather_fusion.3
  1759.3 10.2 select_add_fusion.7
  1816.9 11.8 gather_fusion.3
  1886.4 11.8 gather_fusion.3
  1898.2 10.2 select_add_fusion.7
  1955.9 11.8 gather_fusion.3
  1967.7 10.2 select_add_fusion.7
  2025.4 11.8 gather_fusion.3
  2037.3 10.2 select_add_fusion.7
  2095.0 11.8 gather_fusion.3
  2106.9 10.2 select_add_fusion.7
  2164.6 11.8 gather_fusion.3
  2234.1 11.8 gather_fusion.3
  2246.0 10.2 select_add_fusion.7
  2303.6 11.8 gather_fusion.3
  2334.9 16.3 reduce-scatter.19.cloned.1.call-done
  2352.6 143.5 %reduce-scatter.17.cloned.1.call-done = f32[256,2048]{1,0:T(8,128)} async-done(((f32[1024,2048]{1,0:T(8,128)}), f32[256,2048]{1,0:T(8,128)}) %reduce-scatter.17.cloned.1.call-update) | async-done | bytes 2097168 | tf_op jit(solution)/shard_map/reduce_scatter | solution.py:258
  2500.4 143.4 %reduce-scatter.15.cloned.1.call-done = f32[256,2048]{1,0:T(8,128)} async-done(((f32[1024,2048]{1,0:T(8,128)}), f32[256,2048]{1,0:T(8,128)}) %reduce-scatter.15.cloned.1.call-update) | async-done | bytes 2097168 | tf_op jit(solution)/shard_map/reduce_scatter | solution.py:208
  2651.0 80.5 %all-gather.11.cloned.1.call-done = bf16[1024,2048]{1,0:T(8,128)(2,1)} async-done(((bf16[256,2048]{1,0:T(8,128)(2,1)}), bf16[1024,2048]{1,0:T(8,128)(2,1)}) %all-gather.11.cloned.1.call-update) | async-done | bytes 4194320 | tf_op jit(solution)/shard_map/all_gather | solution.py:270
  2854.4 108.8 %reduce-scatter.21.cloned.1.call-done = f32[256,2048]{1,0:T(8,128)} async-done(((f32[1024,2048]{1,0:T(8,128)}), f32[256,2048]{1,0:T(8,128)}) %reduce-scatter.21.cloned.1.call-update) | async-done | bytes 2097168 | tf_op jit(solution)/shard_map/reduce_scatter | solution.py:350
  2965.3 42.0 %all-reduce.4 = (f32[2048]{0:T(1024)}, f32[2048]{0:T(1024)}, f32[2048]{0:T(1024)}, f32[2048]{0:T(1024)}) all-reduce(f32[2048]{0:T(1024)S(1)} %get-tuple-element.364, f32[2048]{0:T(1024)S(1)} %dynamic_update_slice.31, f32[2048]{0:T(1024)S(1)} %dynamic_update_slice.32, ...), channel_id=1, replica_groups=mesh['dp'=8,'tensor'=4] {'dp','tensor'}, use_global_device_ids=true, to_apply=%region_42.44 | all-reduce | flops 8192 | bytes 65536 | tf_op jit(solution)/shard_map/psum | solution.py:367
  3011.5 81.8 %all-reduce.9.cloned.1.call-done = f32[2048,16]{0,1:T(8,128)} async-done(((f32[2048,16]{0,1:T(8,128)}), f32[2048,16]{0,1:T(8,128)}) %all-reduce.9.cloned.1.call-update) | async-done | bytes 131088 | tf_op jit(solution)/shard_map/psum | solution.py:367
  3093.3 54.7 %reduce-scatter.29.cloned.1.call-done = f32[256,512]{1,0:T(8,128)} async-done(((f32[2048,512]{1,0:T(8,128)}), f32[256,512]{1,0:T(8,128)}) %reduce-scatter.29.cloned.1.call-update) | async-done | bytes 524304 | tf_op jit(solution)/shard_map/reduce_scatter | solution.py:374
  3148.0 55.1 %reduce-scatter.27.cloned.1.call-done = f32[256,512]{1,0:T(8,128)} async-done(((f32[2048,512]{1,0:T(8,128)}), f32[256,512]{1,0:T(8,128)}) %reduce-scatter.27.cloned.1.call-update) | async-done | bytes 524304 | tf_op jit(solution)/shard_map/reduce_scatter | solution.py:373
  3203.1 55.7 %reduce-scatter.23.cloned.1.call-done = f32[256,512]{1,0:T(8,128)} async-done(((f32[2048,512]{1,0:T(8,128)}), f32[256,512]{1,0:T(8,128)}) %reduce-scatter.23.cloned.1.call-update) | async-done | bytes 524304 | tf_op jit(solution)/shard_map/reduce_scatter | solution.py:371
  3258.8 55.1 %reduce-scatter.25.cloned.1.call-done = f32[256,512]{1,0:T(8,128)} async-done(((f32[2048,512]{1,0:T(8,128)}), f32[256,512]{1,0:T(8,128)}) %reduce-scatter.25.cloned.1.call-update) | async-done | bytes 524304 | tf_op jit(solution)/shard_map/reduce_scatter | solution.py:372
  3313.9 209.7 %reduce-scatter.31.cloned.1.call-done = f32[2,2048,256]{2,1,0:T(8,128)} async-done(((f32[16,2048,256]{2,1,0:T(8,128)}), f32[2,2048,256]{2,1,0:T(8,128)}) %reduce-scatter.31.cloned.1.call-update) | async-done | bytes 4194320 | tf_op jit(solution)/shard_map/reduce_scatter | solution.py:253
  3523.6 209.3 %reduce-scatter.33.cloned.1.call-done = f32[2,2048,256]{2,1,0:T(8,128)} async-done(((f32[16,2048,256]{2,1,0:T(8,128)}), f32[2,2048,256]{2,1,0:T(8,128)}) %reduce-scatter.33.cloned.1.call-update) | async-done | bytes 4194320 | tf_op jit(solution)/shard_map/reduce_scatter | solution.py:254
  3732.9 209.7 %reduce-scatter.35.cloned.1.call-done = f32[2,2048,256]{2,1,0:T(8,128)} async-done(((f32[16,2048,256]{2,1,0:T(8,128)}), f32[2,2048,256]{2,1,0:T(8,128)}) %reduce-scatter.35.cloned.1.call-update) | async-done | bytes 4194320 | tf_op jit(solution)/shard_map/reduce_scatter | solution.py:255
  (1077 shorter events, 1572.7 us)
Async XLA Ops:
  7.2 89.0 %copy-start = (bf16[2048,512]{1,0:T(8,128)(2,1)S(1)}, bf16[2048,512]{1,0:T(8,128)(2,1)}, u32[]{:S(2)}) copy-start(bf16[2048,512]{1,0:T(8,128)(2,1)} %param.43) | copy-start | bytes 6291460
  7.2 89.0 %all-gather.5.cloned.1.call-start = ((), (), s32[]{:S(2)}) async-start(), calls=%async_computation.12 | async-start | bytes 5242880 | tf_op jit(solution)/shard_map/all_gather | solution.py:115
  12.6 301.6 %reduce-scatter.13.cloned.1.call-start = ((), (), s32[]{:S(2)}) async-start(), calls=%async_computation.13 | async-start | bytes 10485760 | tf_op jit(solution)/shard_map/reduce_scatter | solution.py:167
  14.8 139.3 %copy-start.18 = (f32[1024,128]{1,0:T(8,128)}, f32[1024,128]{1,0:T(8,128)S(1)}, u32[]{:S(2)}) copy-start(f32[1024,128]{1,0:T(8,128)S(1)} %pad_maximum_fusion.6) | copy-start | bytes 1572868
  16.2 136.5 %copy-start.33 = (pred[512,512]{0,1:T(8,128)(4,1)}, pred[512,512]{0,1:T(8,128)(4,1)S(1)}, u32[]{:S(2)}) copy-start(pred[512,512]{0,1:T(8,128)(4,1)S(1)} %fusion.97) | copy-start | bytes 786436
  17.5 142.3 %copy-start.20 = (pred[512,1024]{1,0:T(8,128)(4,1)}, pred[512,1024]{1,0:T(8,128)(4,1)S(1)}, u32[]{:S(2)}) copy-start(pred[512,1024]{1,0:T(8,128)(4,1)S(1)} %fusion.79) | copy-start | bytes 1572868
  102.3 13.9 copy-start.67
  116.2 10.4 copy-start.58
  143.0 12.3 copy-start.29
  152.6 7.2 copy-start.35
  154.1 9.9 copy-start.88
  170.5 143.7 %copy-start.10 = (bf16[256,2048]{1,0:T(8,128)(2,1)S(1)}, bf16[256,2048]{1,0:T(8,128)(2,1)}, u32[]{:S(2)}) copy-start(bf16[256,2048]{1,0:T(8,128)(2,1)} %param.37) | copy-start | bytes 3145732
  170.5 147.0 %copy-start.52 = (f32[2048]{0:T(1024)S(1)}, f32[2048]{0:T(1024)}, u32[]{:S(2)}) copy-start(f32[2048]{0:T(1024)} %param.49) | copy-start | bytes 24580
  170.5 229.9 %all-gather.7.cloned.1.call-start = ((), (), s32[]{:S(2)}) async-start(), calls=%async_computation.14 | async-start | bytes 5242880 | tf_op jit(solution)/shard_map/all_gather | solution.py:173
  316.1 84.2 %copy-start.48 = (bf16[2048,16]{0,1:T(8,128)(2,1)S(1)}, bf16[2048,16]{0,1:T(8,128)(2,1)}, u32[]{:S(2)}) copy-start(bf16[2048,16]{0,1:T(8,128)(2,1)} %param.50) | copy-start | bytes 196612
  318.7 905.6 %all-gather.9.cloned.1.call-start = ((), (), s32[]{:S(2)}) async-start(), calls=%async_computation.16 | async-start | bytes 5242880 | tf_op jit(solution)/shard_map/all_gather | solution.py:211
  319.3 2031.8 %reduce-scatter.19.cloned.1.call-start = ((), (), s32[]{:S(2)}) async-start(), calls=%async_computation.18 | async-start | bytes 81920 | tf_op jit(solution)/shard_map/reduce_scatter | solution.py:259
  418.2 97.4 %copy-start.79 = (s32[16]{0:T(128)}, s32[16]{0:T(128)S(1)}, u32[]{:S(2)}) copy-start(s32[16]{0:T(128)S(1)} %slice_reduce_fusion) | copy-start | bytes 196
  515.7 708.6 %copy-start.80 = (s32[16]{0:T(128)S(1)}, s32[16]{0:T(128)}, u32[]{:S(2)}) copy-start(s32[16]{0:T(128)} %copy-done.79) | copy-start | bytes 196
  1276.4 6.3 copy-start.4
  1342.0 10.2 copy-start.4
  1411.5 10.2 copy-start.4
  1481.0 10.2 copy-start.4
  1550.6 10.2 copy-start.4
  1620.2 10.2 copy-start.4
  1689.7 10.2 copy-start.4
  1759.3 10.2 copy-start.4
  1828.7 10.2 copy-start.4
  1898.2 10.2 copy-start.4
  1967.7 10.2 copy-start.4
  2037.3 10.2 copy-start.4
  2106.9 10.2 copy-start.4
  2176.4 10.2 copy-start.4
  2246.0 10.2 copy-start.4
  2315.5 10.2 copy-start.4
  2333.5 162.7 %reduce-scatter.17.cloned.1.call-start = ((), (), s32[]{:S(2)}) async-start(), calls=%async_computation.17 | async-start | bytes 10485760 | tf_op jit(solution)/shard_map/reduce_scatter | solution.py:258
  2334.1 309.8 %reduce-scatter.15.cloned.1.call-start = ((), (), s32[]{:S(2)}) async-start(), calls=%async_computation.15 | async-start | bytes 10485760 | tf_op jit(solution)/shard_map/reduce_scatter | solution.py:208
  2334.1 17.1 copy-start.50
  2334.1 162.1 %copy-start.49 = (bf16[2048,16]{0,1:T(8,128)(2,1)S(1)}, bf16[2048,16]{0,1:T(8,128)(2,1)}, u32[]{:S(2)}) copy-start(bf16[2048,16]{0,1:T(8,128)(2,1)} %param.50) | copy-start | bytes 196612
  2334.1 162.1 %copy-start.53 = (f32[2048]{0:T(1024)S(1)}, f32[2048]{0:T(1024)}, u32[]{:S(2)}) copy-start(f32[2048]{0:T(1024)} %param.49) | copy-start | bytes 24580
  2334.1 162.0 %copy-start.74 = (f32[256]{0:T(256)S(1)}, f32[256]{0:T(256)}, u32[]{:S(2)}) copy-start(f32[256]{0:T(256)} %copy-done.73) | copy-start | bytes 3076
  2334.8 396.8 %all-gather.11.cloned.1.call-start = ((), (), s32[]{:S(2)}) async-start(), calls=%async_computation.19 | async-start | bytes 5242880 | tf_op jit(solution)/shard_map/all_gather | solution.py:270
  2352.6 291.2 %copy-start.82 = (f32[256]{0:T(256)S(1)}, f32[256]{0:T(256)}, u32[]{:S(2)}) copy-start(f32[256]{0:T(256)} %get-tuple-element.480) | copy-start | bytes 3076
  2643.9 7.1 copy-start.61
  2643.9 7.1 copy-start.63
  2643.9 7.1 copy-start.55
  2643.9 7.1 copy-start.66
  2649.9 313.3 %reduce-scatter.21.cloned.1.call-start = ((), (), s32[]{:S(2)}) async-start(), calls=%async_computation.20 | async-start | bytes 10485760 | tf_op jit(solution)/shard_map/reduce_scatter | solution.py:350
  2651.0 85.9 %copy-start.34 = (pred[512,512]{0,1:T(8,128)(4,1)S(1)}, pred[512,512]{0,1:T(8,128)(4,1)}, u32[]{:S(2)}) copy-start(pred[512,512]{0,1:T(8,128)(4,1)} %copy-done.33) | copy-start | bytes 786436
  2738.2 6.5 slice-start
  2756.7 9.2 copy-start.32
  2790.2 14.3 copy-start.77
  2819.6 273.7 %all-reduce.9.cloned.1.call-start = ((), (), s32[]{:S(2)}) async-start(), calls=%async_computation.25 | async-start | bytes 262144 | tf_op jit(solution)/shard_map/psum | solution.py:367
  2821.7 326.3 %reduce-scatter.29.cloned.1.call-start = ((), (), s32[]{:S(2)}) async-start(), calls=%async_computation.24 | async-start | bytes 4718592 | tf_op jit(solution)/shard_map/reduce_scatter | solution.py:374
  2828.6 374.5 %reduce-scatter.27.cloned.1.call-start = ((), (), s32[]{:S(2)}) async-start(), calls=%async_computation.23 | async-start | bytes 4718592 | tf_op jit(solution)/shard_map/reduce_scatter | solution.py:373
  2836.5 422.3 %reduce-scatter.23.cloned.1.call-start = ((), (), s32[]{:S(2)}) async-start(), calls=%async_computation.21 | async-start | bytes 4718592 | tf_op jit(solution)/shard_map/reduce_scatter | solution.py:371
  2844.2 469.6 %reduce-scatter.25.cloned.1.call-start = ((), (), s32[]{:S(2)}) async-start(), calls=%async_computation.22 | async-start | bytes 4718592 | tf_op jit(solution)/shard_map/reduce_scatter | solution.py:372
  2852.0 671.6 %reduce-scatter.31.cloned.1.call-start = ((), (), s32[]{:S(2)}) async-start(), calls=%async_computation.26 | async-start | bytes 37748736 | tf_op jit(solution)/shard_map/reduce_scatter | solution.py:253
  2852.6 880.3 %reduce-scatter.33.cloned.1.call-start = ((), (), s32[]{:S(2)}) async-start(), calls=%async_computation.27 | async-start | bytes 37748736 | tf_op jit(solution)/shard_map/reduce_scatter | solution.py:254
  2853.2 1089.4 %reduce-scatter.35.cloned.1.call-start = ((), (), s32[]{:S(2)}) async-start(), calls=%async_computation.28 | async-start | bytes 37748736 | tf_op jit(solution)/shard_map/reduce_scatter | solution.py:255
  2853.2 110.0 %copy-start.11 = (bf16[256,2048]{1,0:T(8,128)(2,1)S(1)}, bf16[256,2048]{1,0:T(8,128)(2,1)}, u32[]{:S(2)}) copy-start(bf16[256,2048]{1,0:T(8,128)(2,1)} %param.37) | copy-start | bytes 3145732
  2853.3 109.9 %copy-start.51 = (f32[2048]{0:T(1024)S(1)}, f32[2048]{0:T(1024)}, u32[]{:S(2)}) copy-start(f32[2048]{0:T(1024)} %param.42) | copy-start | bytes 24580
  2853.3 109.9 %copy-start.72 = (f32[256]{0:T(256)S(1)}, f32[256]{0:T(256)}, u32[]{:S(2)}) copy-start(f32[256]{0:T(256)} %copy-done.71) | copy-start | bytes 3076
  2853.8 153.6 %copy-start.81 = (f32[256]{0:T(256)S(1)}, f32[256]{0:T(256)}, u32[]{:S(2)}) copy-start(f32[256]{0:T(256)} %get-tuple-element.478) | copy-start | bytes 3076
  (106 other events, 340.0 us)
Sparse Core Ops, SparseCore 0:
  12.7 83.4 all-gather.4
  170.6 143.5 reduce-scatter.12
  318.9 81.4 all-gather.6
  401.8 79.2 all-gather.8
  2333.6 17.5 reduce-scatter.18
  2353.5 142.6 reduce-scatter.16
  2498.6 145.1 reduce-scatter.14
  2650.0 81.4 all-gather.10
  2819.7 143.4 reduce-scatter.20
  2970.1 123.1 all-reduce.8
  3097.6 50.3 reduce-scatter.28
  3151.8 51.2 reduce-scatter.26
  3207.4 51.3 reduce-scatter.22
  3262.6 51.2 reduce-scatter.24
  3318.3 205.2 reduce-scatter.30
  3527.6 205.2 reduce-scatter.32
  3737.3 205.2 reduce-scatter.34
where the time goes:
time: 3970 us; the launch traced here: 3950 us
  waiting for transfers between devices  1730 us (44%)
  local copies, waits for them, and re-layouts  1200 us (30%)
  matrix products  550 us (14%)
  other arithmetic  393 us (10%)
  blocking collectives  61.1 us (2%)
    gather x48, local copies, waits for them, and re-layouts, slots_to_rows(): jnp.take(jnp.concatenate([slot_values, padding], axis=0), place_col, axis=0)  451 us
    reduce_scatter x1, waiting for transfers between devices, local(): lax.psum_scatter(gate_grads, 'dp', scatter_dimension=0, tiled=True)  210 us
    reduce_scatter x1, waiting for transfers between devices, local(): lax.psum_scatter(down_grads, 'dp', scatter_dimension=0, tiled=True)  210 us
    reduce_scatter x1, waiting for transfers between devices, local(): lax.psum_scatter(up_grads, 'dp', scatter_dimension=0, tiled=True)  209 us
    add x16, other arithmetic, expert_backward(): rows_running = rows_running + slots_to_rows(back_rows, place_col)  159 us
    gather x16, local copies, waits for them, and re-layouts, expert_forward(): pre_gate, pre_up = expert_pre(ffn_all[picks], gate_w, up_w)  157 us
    gather x16, local copies, waits for them, and re-layouts, expert_backward(): grad_picked = grad_all[picks]  157 us
    gather x16, local copies, waits for them, and re-layouts, expert_backward(): picked_rows = ffn_all[picks]  157 us
  transfers between devices with their start and end apart: 17, of which 16 were waited for; matrix products, arithmetic and copies ran while one was open for 22% of the time, Pallas kernels for 0%

commit v1 on v0

v1 whole, which is shorter than its diff:
```python
import functools

import jax
import jax.numpy as jnp
from jax import lax
from jax.experimental import pallas as pl
from jax.experimental.pallas import tpu as pltpu
from jax.sharding import PartitionSpec as P

D = 2048
HEAD = 128
DOC = 512
LANES = 128
EPSILON = 1e-05
MASKED = -1e30
CHUNKS = 2
VMEM = 56 * 1024 * 1024
bf16 = jnp.bfloat16
f32 = jnp.float32


def nn(left, right):
    return lax.dot_general(left, right, (((1,), (0,)), ((), ())), preferred_element_type=f32)


def nt(left, right):
    return lax.dot_general(left, right, (((1,), (1,)), ((), ())), preferred_element_type=f32)


def tn(left, right):
    return lax.dot_general(left, right, (((0,), (0,)), ((), ())), preferred_element_type=f32)


def params():
    return pltpu.CompilerParams(vmem_limit_bytes=VMEM)


def cost(flops, moved, special=0):
    return pl.CostEstimate(flops=flops, bytes_accessed=moved, transcendentals=special)


def rms_scale(values):
    return lax.rsqrt(jnp.mean(values * values, axis=-1, keepdims=True) + EPSILON)


def norm_back(grad_values, values, scale_col, gain_vec):
    weighted = grad_values * gain_vec
    inner_mean = jnp.mean(weighted * values, axis=-1, keepdims=True)
    return scale_col * weighted - values * (scale_col * scale_col * scale_col) * inner_mean


def rope_tables(length, width):
    half_width = width // 2
    frequency = jnp.power(10000.0, -jnp.arange(half_width, dtype=f32) * 2.0 / width)
    angles = jnp.arange(length, dtype=f32)[:, None] * frequency[None, :]
    cosine, sine = jnp.cos(angles), jnp.sin(angles)
    return jnp.concatenate([cosine, cosine], axis=1), jnp.concatenate([-sine, sine], axis=1)


def key_start(query_start):
    return max(0, query_start - DOC)


def fill_bias(bias, seg_col, seg_row, keep_row, block):
    length = seg_col.shape[0]
    for start in range(0, length, block):
        first, stop = key_start(start), start + block
        query_pos = start + lax.broadcasted_iota(jnp.int32, (block, stop - first), 0)
        key_pos = first + lax.broadcasted_iota(jnp.int32, (block, stop - first), 1)
        same = seg_col[start:stop, :] == seg_row[:, first:stop]
        live = (keep_row[:, first:stop] == 1) | (key_pos == query_pos)
        allowed = same & live & (key_pos <= query_pos)
        bias[start:stop, : stop - first] = jnp.where(allowed, 0.0, MASKED)


def turned(values):
    return pltpu.roll(values, values.shape[1] // 2, 1)


def attend_kernel(
    block, qraw, kraw, value, q_scale, k_scale, q_gain, k_gain, cosine, sine,
    seg_col, seg_row, keep_row, q_out, k_out, o_out, lse_out, bias,
):
    @pl.when(pl.program_id(0) == 0)
    def _():
        fill_bias(bias, seg_col, seg_row, keep_row, block)

    def rotated(raw, scale, gain):
        normed = raw[...] * scale[...] * gain[...]
        return (normed * cosine[...] + turned(normed) * sine[...]).astype(bf16)

    q_out[...] = rotated(qraw, q_scale, q_gain)
    k_out[...] = rotated(kraw, k_scale, k_gain)
    length = seg_col.shape[0]
    for start in range(0, length, block):
        first, stop = key_start(start), start + block
        scores = nt(q_out[start:stop, :], k_out[first:stop, :]) * HEAD ** (-0.5)
        scores = scores + bias[start:stop, : stop - first]
        top = jnp.max(scores, axis=1, keepdims=True)
        powers = jnp.exp(scores - top)
        total = jnp.sum(powers, axis=1, keepdims=True)
        weights = (powers * (1.0 / total)).astype(bf16)
        o_out[start:stop, :] = nn(weights, value[first:stop, :]).astype(bf16)
        lse_out[start:stop, :] = jnp.broadcast_to(top + jnp.log(total), (block, HEAD))


def attend(qraw, kraw, value, q_scale, k_scale, q_gain, k_gain, cosine, sine, seg, keep):
    length, width = qraw.shape
    block = min(256, length)
    span = min(DOC + block, length)
    head = pl.BlockSpec((length, HEAD), lambda h: (0, h))
    gain = pl.BlockSpec((1, HEAD), lambda h: (0, h))
    whole = lambda *shape: pl.BlockSpec(shape, lambda h: (0, 0))
    return pl.pallas_call(
        functools.partial(attend_kernel, block),
        grid=(width // HEAD,),
        in_specs=[head, head, head, whole(length, 1), whole(length, 1), gain, gain]
        + [whole(length, HEAD), whole(length, HEAD), whole(length, 1), whole(1, length), whole(1, length)],
        out_specs=[head, head, head, head],
        out_shape=[jax.ShapeDtypeStruct((length, width), t) for t in (bf16, bf16, bf16, f32)],
        scratch_shapes=[pltpu.VMEM((length, span), f32)],
        compiler_params=params(),
        cost_estimate=cost(4 * length * span * width, 18 * length * width, length * span * width // HEAD),
        name="attend",
    )(qraw, kraw, value, q_scale, k_scale, q_gain[None], k_gain[None], cosine, sine, seg[:, None], seg[None], keep[None])


def attend_back_kernel(
    block, query, key, value, out_grad, lse, qraw, kraw, q_scale, k_scale, q_gain, k_gain, cosine, sine,
    seg_col, seg_row, keep_row, dq_out, dk_out, dv_out, qdot_out, kdot_out, qg_out, kg_out, bias, dk_sum, dv_sum,
):
    at = pl.program_id(0)

    @pl.when(at == 0)
    def _():
        fill_bias(bias, seg_col, seg_row, keep_row, block)
        qdot_out[...] = jnp.zeros_like(qdot_out)
        kdot_out[...] = jnp.zeros_like(kdot_out)

    dk_sum[...] = jnp.zeros_like(dk_sum)
    dv_sum[...] = jnp.zeros_like(dv_sum)
    length = seg_col.shape[0]
    scale = HEAD ** (-0.5)
    for start in range(0, length, block):
        first, stop = key_start(start), start + block
        rows, keys = slice(start, stop), slice(first, stop)
        scores = nt(query[rows, :], key[keys, :]) * scale + bias[rows, : stop - first]
        weights = jnp.exp(scores - lse[rows, :1])
        prob_grad = nt(out_grad[rows, :], value[keys, :])
        inner = jnp.sum(weights * prob_grad, axis=1, keepdims=True)
        score_grad = (weights * (prob_grad - inner)).astype(bf16)
        dq_out[rows, :] = nn(score_grad, key[keys, :]) * scale
        dk_sum[keys, :] += tn(score_grad, query[rows, :])
        dv_sum[keys, :] += tn(weights.astype(bf16), out_grad[rows, :])

    def unrotated(grad):
        return grad * cosine[...] + turned(grad * sine[...])

    dv_out[...] = dv_sum[...].astype(bf16)
    dq = unrotated(dq_out[...])
    dk = unrotated(dk_sum[...] * scale)
    dq_out[...] = dq
    dk_out[...] = dk
    dq = dq * qraw[...]
    dk = dk * kraw[...]
    qg_out[...] = jnp.sum(dq * q_scale[...], axis=0, keepdims=True)
    kg_out[...] = jnp.sum(dk * k_scale[...], axis=0, keepdims=True)
    qdot_out[...] += jnp.sum(dq * q_gain[...], axis=1, keepdims=True)
    kdot_out[...] += jnp.sum(dk * k_gain[...], axis=1, keepdims=True)


def attend_back(query, key, value, out_grad, lse, qraw, kraw, q_scale, k_scale, q_gain, k_gain, cosine, sine, seg, keep):
    length, width = qraw.shape
    block = min(256, length)
    span = min(DOC + block, length)
    head = pl.BlockSpec((length, HEAD), lambda h: (0, h))
    gain = pl.BlockSpec((1, HEAD), lambda h: (0, h))
    whole = lambda *shape: pl.BlockSpec(shape, lambda h: (0, 0))
    sds = jax.ShapeDtypeStruct
    return pl.pallas_call(
        functools.partial(attend_back_kernel, block),
        grid=(width // HEAD,),
        in_specs=[head] * 7
        + [whole(length, 1), whole(length, 1), gain, gain]
        + [whole(length, HEAD), whole(length, HEAD), whole(length, 1), whole(1, length), whole(1, length)],
        out_specs=[head, head, head, whole(length, 1), whole(length, 1), gain, gain],
        out_shape=[sds((length, width), f32), sds((length, width), f32), sds((length, width), bf16)]
        + [sds((length, 1), f32), sds((length, 1), f32), sds((1, width), f32), sds((1, width), f32)],
        scratch_shapes=[pltpu.VMEM((length, span), f32), pltpu.VMEM((length, HEAD), f32), pltpu.VMEM((length, HEAD), f32)],
        compiler_params=params(),
        cost_estimate=cost(10 * length * span * width, 32 * length * width, length * span * width // HEAD),
        name="attend_back",
    )(query, key, value, out_grad, lse, qraw, kraw, q_scale, k_scale, q_gain[None], k_gain[None], cosine, sine, seg[:, None], seg[None], keep[None])


def up_back_kernel(grad, down_w, out):
    width = down_w.shape[2]
    for at in range(down_w.shape[0]):
        out[:, at * width : (at + 1) * width] = nn(grad[...], down_w[at]).astype(out.dtype)


def up_back(grad, down_w):
    rows, features = grad.shape
    experts, _, width = down_w.shape
    step = 2 if experts % 2 == 0 else 1
    return pl.pallas_call(
        up_back_kernel,
        grid=(experts // step,),
        in_specs=[pl.BlockSpec((rows, features), lambda e: (0, 0)), pl.BlockSpec((step, features, width), lambda e: (e, 0, 0))],
        out_specs=pl.BlockSpec((rows, step * width), lambda e: (0, e)),
        out_shape=jax.ShapeDtypeStruct((rows, experts * width), bf16),
        compiler_params=params(),
        cost_estimate=cost(2 * rows * features * experts * width, 2 * (rows + experts * width) * features),
        name="up_back",
    )(grad, down_w)


def expert_kernel(block, rows_in, back, routed, router, gate_w, up_w, act_out, dgate_out, dup_out, grad_out, comb, dcomb, total):
    at = pl.program_id(0)
    rows, features = rows_in.shape
    lane = lax.broadcasted_iota(jnp.int32, (block, LANES), 1)

    @pl.when(at == 0)
    def _():
        experts = pl.num_programs(0)
        for start in range(0, rows, block):
            here = slice(start, start + block)
            logits = jnp.where(lane < experts, nn(rows_in[here, :], router[...]), MASKED)
            powers = jnp.exp(logits - jnp.max(logits, axis=1, keepdims=True))
            probs = powers / jnp.sum(powers, axis=1, keepdims=True)
            comb[here, :] = probs * routed[here, :]
        total[...] = jnp.zeros_like(total)
        dcomb[...] = jnp.zeros_like(dcomb)

    gate, up = gate_w[0], up_w[0]
    mine = lane == at
    for start in range(0, rows, block):
        here = slice(start, start + block)
        taken = rows_in[here, :]
        pre_gate = nn(taken, gate)
        pre_up = nn(taken, up)
        behind = back[here, :].astype(f32)
        share = jnp.sum(jnp.where(mine, comb[here, :], 0.0), axis=1, keepdims=True)
        sigmoid = 0.5 * jnp.tanh(0.5 * pre_gate) + 0.5
        active = pre_gate * sigmoid
        inner = active * pre_up
        share_grad = jnp.sum(inner * behind, axis=1, keepdims=True)
        dcomb[here, :] = jnp.where(mine, share_grad, dcomb[here, :])
        act_out[here, :] = (inner * share).astype(bf16)
        inner_grad = behind * share
        dgate = (inner_grad * pre_up * (sigmoid + active * (1.0 - sigmoid))).astype(bf16)
        dup = (inner_grad * active).astype(bf16)
        dgate_out[here, :] = dgate
        dup_out[here, :] = dup
        total[here, :] += nt(dgate, gate) + nt(dup, up)

    @pl.when(at == pl.num_programs(0) - 1)
    def _():
        grad_out[:, :features] = total[...].astype(bf16)
        grad_out[:, features:] = dcomb[...].astype(bf16)


def experts_block(rows_in, back, routed, router, gate_w, up_w):
    rows, features = rows_in.shape
    experts, _, width = gate_w.shape
    block = min(512, rows)
    whole = lambda *shape: pl.BlockSpec(shape, lambda e: (0, 0))
    column = pl.BlockSpec((rows, width), lambda e: (0, e))
    weight = pl.BlockSpec((1, features, width), lambda e: (e, 0, 0))
    wide = jax.ShapeDtypeStruct((rows, experts * width), bf16)
    return pl.pallas_call(
        functools.partial(expert_kernel, block),
        grid=(experts,),
        in_specs=[whole(rows, features), column, whole(rows, LANES), whole(features, LANES), weight, weight],
        out_specs=[column, column, column, whole(rows, features + LANES)],
        out_shape=[wide, wide, wide, jax.ShapeDtypeStruct((rows, features + LANES), bf16)],
        scratch_shapes=[pltpu.VMEM((rows, LANES), f32), pltpu.VMEM((rows, LANES), f32), pltpu.VMEM((rows, features), f32)],
        compiler_params=params(),
        cost_estimate=cost(8 * rows * features * experts * width, 4 * experts * width * (features + 2 * rows), rows * experts * width),
        name="experts",
    )(rows_in, back, routed, router, gate_w, up_w)


def wgrad_kernel(count, block, *refs):
    lefts, rights, out = refs[:count], refs[count : 2 * count], refs[2 * count]
    for start in range(0, out.shape[1], block):
        here = slice(start, start + block)
        total = nn(lefts[0][here, :], rights[0][...])
        for left, right in zip(lefts[1:], rights[1:]):
            total = total + nn(left[here, :], right[...])
        out[0, here, :] = total.astype(out.dtype)


def wgrad(lefts, rights, experts):
    features = lefts[0].shape[0]
    width = rights[0].shape[1] // experts
    rows = sum(left.shape[1] for left in lefts)
    return pl.pallas_call(
        functools.partial(wgrad_kernel, len(lefts), min(512, features)),
        grid=(experts,),
        in_specs=[pl.BlockSpec(left.shape, lambda e: (0, 0)) for left in lefts]
        + [pl.BlockSpec((right.shape[0], width), lambda e: (0, e)) for right in rights],
        out_specs=pl.BlockSpec((1, features, width), lambda e: (e, 0, 0)),
        out_shape=jax.ShapeDtypeStruct((experts, features, width), bf16),
        compiler_params=params(),
        cost_estimate=cost(2 * rows * features * experts * width, 2 * (rows + experts * width) * features),
        name="wgrad",
    )(*lefts, *rights)


def down_kernel(act, down_w, out):
    joined = jnp.concatenate([down_w[e] for e in range(down_w.shape[0])], axis=1)
    out[...] = nt(act[...], joined).astype(out.dtype)


def down(act, down_w):
    rows = act.shape[0]
    experts, features, width = down_w.shape
    block = min(256, features)
    return pl.pallas_call(
        down_kernel,
        grid=(features // block,),
        in_specs=[pl.BlockSpec(act.shape, lambda n: (0, 0)), pl.BlockSpec((experts, block, width), lambda n: (0, n, 0))],
        out_specs=pl.BlockSpec((rows, block), lambda n: (0, n)),
        out_shape=jax.ShapeDtypeStruct((rows, features), bf16),
        compiler_params=params(),
        cost_estimate=cost(2 * rows * features * experts * width, 2 * (rows + experts * width) * features),
        name="down",
    )(act, down_w)


def gather_rows(values):
    return lax.all_gather(values, "tensor", axis=0, tiled=True)


def scatter_rows(values):
    return lax.psum_scatter(values, "tensor", scatter_dimension=0, tiled=True)


def dp_scatter(values):
    return lax.psum_scatter(values, "dp", scatter_dimension=0, tiled=True)


def exchange_sum(values, axes):
    for axis in axes:
        size = lax.axis_size(axis)
        step = 1
        while step < size:
            values = values + lax.ppermute(values, axis, [(i, i ^ step) for i in range(size)])
            step *= 2
    return values


def local(
    tokens, cotangent, seg_ids, keep_mask, routes, attn_gain, w_query, w_key, w_value, w_out,
    q_gain, k_gain, ffn_gain, router, w_gate, w_up, w_down,
):
    parts = lax.axis_size("tensor")
    part_at = lax.axis_index("tensor")
    shard_rows, features = tokens.shape
    group_rows = shard_rows * parts
    _, length = seg_ids.shape
    local_width = w_query.shape[1]
    experts = w_gate.shape[0]
    chunk_rows = shard_rows // CHUNKS
    chunks = range(CHUNKS)
    own = [slice(c * chunk_rows, (c + 1) * chunk_rows) for c in chunks]

    def chunk_of(values, c):
        width = values.shape[1]
        return values.reshape(parts, CHUNKS, chunk_rows, width)[:, c].reshape(parts * chunk_rows, width)

    def in_order(pieces):
        width = pieces[0].shape[1]
        stacked = jnp.stack([piece.reshape(parts, chunk_rows, width) for piece in pieces], axis=1)
        return stacked.reshape(group_rows, width)

    inputs = tokens.astype(f32)
    first_scale = rms_scale(inputs)
    normed_all = gather_rows((inputs * first_scale * attn_gain).astype(bf16))
    grad_all = [gather_rows(cotangent[own[c]]) for c in chunks]
    backs = [up_back(grad_all[c], w_down) for c in chunks]

    qraw = nn(normed_all, w_query)
    kraw = nn(normed_all, w_key)
    value = nn(normed_all, w_value).astype(bf16)
    squares = exchange_sum(jnp.stack([jnp.sum(qraw * qraw, axis=1), jnp.sum(kraw * kraw, axis=1)]), ("tensor",))
    q_scale, k_scale = (lax.rsqrt(squares[i] / features + EPSILON)[:, None] for i in range(2))
    cosine, sine = rope_tables(length, HEAD)
    query, key, attended, lse = attend(
        qraw, kraw, value, q_scale, k_scale, q_gain, k_gain, cosine, sine, seg_ids[0], keep_mask[0]
    )

    expert_ids = jnp.arange(LANES)
    routed = jnp.sum((routes[:, :, None] == expert_ids[None, None, :]).astype(f32), axis=1)
    router_wide = jnp.pad(router, ((0, 0), (0, LANES - experts)))
    middles, scales, ffn_own, ffn_all = [], [], [], []
    for c in chunks:
        summed = scatter_rows(nt(chunk_of(attended, c), w_out).astype(bf16))
        middle = inputs[own[c]] + summed.astype(f32)
        scale = rms_scale(middle)
        normed = (middle * scale * ffn_gain).astype(bf16)
        middles.append(middle)
        scales.append(scale)
        ffn_own.append(normed)
        ffn_all.append(gather_rows(normed))

    acts, dgates, dups, middle_grads, middle_all = [], [], [], [], []
    ffn_gain_part = 0.0
    router_part = 0.0
    routed_own = lax.dynamic_slice_in_dim(routed, part_at * shard_rows, shard_rows, 0)[:, :experts]
    for c in chunks:
        act, dgate, dup, grads = experts_block(ffn_all[c], backs[c], chunk_of(routed, c), router_wide, w_gate, w_up)
        acts.append(act)
        dgates.append(dgate)
        dups.append(dup)
        grads = scatter_rows(grads).astype(f32)
        share_grad = grads[:, features : features + experts] * routed_own[own[c]]
        probs = jax.nn.softmax(nn(ffn_own[c], router), axis=-1)
        logit_grad = (probs * (share_grad - jnp.sum(share_grad * probs, axis=-1, keepdims=True))).astype(bf16)
        ffn_grad = grads[:, :features] + nt(logit_grad, router)
        router_part = router_part + tn(ffn_own[c], logit_grad)
        ffn_gain_part = ffn_gain_part + jnp.sum(ffn_grad * middles[c] * scales[c], axis=0)
        middle_grad = cotangent[own[c]].astype(f32) + norm_back(ffn_grad, middles[c], scales[c], ffn_gain)
        middle_grads.append(middle_grad)
        middle_all.append(gather_rows(middle_grad.astype(bf16)))

    layer_out = jnp.concatenate(
        [(middles[c] + scatter_rows(down(acts[c], w_down)).astype(f32)).astype(bf16) for c in chunks]
    )
    ffn_t = [rows.T for rows in ffn_all]
    grad_t = [rows.T for rows in grad_all]
    gate_done = dp_scatter(wgrad(ffn_t, dgates, experts)).astype(f32)
    up_done = dp_scatter(wgrad(ffn_t, dups, experts)).astype(f32)
    down_done = dp_scatter(wgrad(grad_t, acts, experts)).astype(f32)

    attended_grad = in_order([nn(rows, w_out).astype(bf16) for rows in middle_all])
    dqn, dkn, dvalue, qdot, kdot, q_gain_part, k_gain_part = attend_back(
        query, key, value, attended_grad, lse, qraw, kraw, q_scale, k_scale, q_gain, k_gain, cosine, sine,
        seg_ids[0], keep_mask[0],
    )
    dots = exchange_sum(jnp.stack([qdot[:, 0], kdot[:, 0]]), ("tensor",)) / features

    def raw_grad(grad, raw, scale, gain, dot):
        return (scale * gain * grad - raw * (scale * scale * scale) * dot[:, None]).astype(bf16)

    dqraw = raw_grad(dqn, qraw, q_scale, q_gain, dots[0])
    dkraw = raw_grad(dkn, kraw, k_scale, k_gain, dots[1])
    normed_part = nt(dqraw, w_query) + nt(dkraw, w_key) + nt(dvalue, w_value)
    normed_grad = scatter_rows(normed_part.astype(bf16)).astype(f32)
    normed_t = normed_all.T
    attn_grads = [nn(normed_t, dqraw), nn(normed_t, dkraw), nn(normed_t, dvalue)]
    attn_gain_part = sum(
        jnp.sum(grad * weight.astype(f32), axis=1) for grad, weight in zip(attn_grads, (w_query, w_key, w_value))
    ) / attn_gain
    out_grad = sum(tn(middle_all[c], chunk_of(attended, c)) for c in chunks)
    attn_grads = jnp.concatenate([grad.astype(bf16) for grad in attn_grads + [out_grad]], axis=1)
    attn_done = dp_scatter(attn_grads).astype(f32)
    query_done, key_done, value_done, out_done = (
        attn_done[:, i * local_width : (i + 1) * local_width] for i in range(4)
    )
    tokens_grad = jnp.concatenate(middle_grads) + norm_back(normed_grad, inputs, first_scale, attn_gain)

    def placed(part):
        return lax.dynamic_update_slice_in_dim(jnp.zeros((features,), f32), part, part_at * local_width, 0)

    early = exchange_sum(jnp.concatenate([router_part.T, ffn_gain_part[None]]), ("dp", "tensor"))
    late = exchange_sum(jnp.stack([attn_gain_part, placed(q_gain_part[0]), placed(k_gain_part[0])]), ("dp", "tensor"))
    return (
        layer_out, tokens_grad, query_done, key_done, value_done, out_done,
        late[0], late[1], late[2], early[experts], early[:experts].T, gate_done, up_done, down_done,
    )


def solution(mesh):
    rows = P(("dp", "tensor"), None)
    column = P(None, "tensor")
    expert = P(None, None, "tensor")
    in_specs = (
        rows, rows, P("dp", None), P("dp", None), P("dp", None), P(), column, column, column, column,
        P("tensor"), P("tensor"), P(), P(), expert, expert, expert,
    )
    block = P("dp", "tensor")
    expert_out = P("dp", None, "tensor")
    out_specs = (
        rows, rows, block, block, block, block, P(), P(), P(), P(), P(), expert_out, expert_out, expert_out,
    )
    return jax.shard_map(local, mesh=mesh, in_specs=in_specs, out_specs=out_specs, check_vma=False)
```

time: 3970 us -> 1420 us (0.36)
  local copies, waits for them, and re-layouts: 1200 us -> 82.7 us
  waiting for transfers between devices: 1730 us -> 917 us
  matrix products: 550 us -> 57.1 us
  other arithmetic: 393 us -> 53.3 us
  Pallas kernels: 0 us -> 271 us
  blocking collectives: 61.1 us -> 0 us
    reduce_scatter x12 -> x5, waiting for transfers between devices: 1410 us -> 340 us  [the longest x4 340 us: dp_scatter(): return lax.psum_scatter(values, 'dp', scatter_dimension=0, tiled=True)]
    gather x99 -> x0, local copies, waits for them, and re-layouts: 1020 us -> none  [the longest x48 451 us: slots_to_rows(): jnp.take(jnp.concatenate([slot_values, padding], axis=0), place_col, axis=0)]
    dot_general x187 -> x21, matrix products: 550 us -> 57.1 us  [the longest x10 33.1 us: nn(): lax.dot_general(left, right, (((1,), (0,)), ((), ())), preferred_element_...]
    add x37 -> x15, other arithmetic: 322 us -> 3.57 us  [the longest x1 1.92 us: local(): jnp.concatenate(middle_grads)]
    pallas_call x0 -> x11, Pallas kernels: none -> 271 us  [the longest x2 94.9 us: experts_block(): pl.pallas_call(functools.partial(expert_kernel, block), grid=(experts,),...]
    unnamed x17 -> x24, waiting for transfers between devices: 3.43 us -> 248 us
    concatenate x33 -> x0, local copies, waits for them, and re-layouts: 104 us -> none  [the longest x32 101 us: slots_to_rows(): jnp.concatenate([slot_values, padding], axis=0)]
    psum x1 -> x0, waiting for transfers between devices: 81.8 us -> none  [local(): lax.psum((attn_gain_part, q_full, k_full, ffn_gain_part, router_part), ('...]
  transfers between devices with their start and end apart: 17 -> 32, of which waited for: 16 -> 25; matrix products, arithmetic and copies ran while one was open for 22% -> 10% of each run, Pallas kernels for 0% -> 7%
where the time goes in v1:
time: 1420 us; the launch traced here: 1410 us
  waiting for transfers between devices  917 us (65%)
  Pallas kernels  271 us (19%)
  local copies, waits for them, and re-layouts  82.7 us (6%)
  matrix products  57.1 us (4%)
  other arithmetic  53.3 us (4%)
  between operations  15.7 us (1%)
    reduce_scatter x4, waiting for transfers between devices, dp_scatter(): return lax.psum_scatter(values, 'dp', scatter_dimension=0, tiled=True)  340 us
    all_gather x7, waiting for transfers between devices, gather_rows(): return lax.all_gather(values, 'tensor', axis=0, tiled=True)  287 us
    unnamed x24, waiting for transfers between devices  248 us
    pallas_call x2, Pallas kernels, experts_block(): pl.pallas_call(functools.partial(expert_kernel, block), grid=(experts,),...  94.9 us
    pallas_call x3, Pallas kernels, wgrad(): pl.pallas_call(functools.partial(wgrad_kernel, len(lefts), min(512, featu...  75.1 us
    unnamed x158, local copies, waits for them, and re-layouts  46.8 us
    ppermute x14, waiting for transfers between devices, exchange_sum(): lax.ppermute(values, axis, [(i, i ^ step) for i in range(size)])  42 us
    dot_general x10, matrix products, nn(): lax.dot_general(left, right, (((1,), (0,)), ((), ())), preferred_element_...  33.1 us
  transfers between devices with their start and end apart: 32, of which 25 were waited for; matrix products, arithmetic and copies ran while one was open for 10% of the time, Pallas kernels for 7%

profile of v1, /device:TPU:0, one launch (start us, length us, event | category | flops | bytes accessed | tf_op | source)
XLA Modules:
  0.0 1407.0 jit_solution(17256377459115394757)
XLA Ops:
  11.8 2.9 fusion.2
  14.7 80.4 %all-gather.8.cloned.1.call-done = bf16[1024,2048]{0,1:T(8,128)(2,1)} async-done(((bf16[256,2048]{0,1:T(8,128)(2,1)}), bf16[1024,2048]{0,1:T(8,128)(2,1)}) %all-gather.8.cloned.1.call-update) | async-done | bytes 4194320 | tf_op jit(solution)/shard_map/all_gather | solution.py:333
  95.1 6.7 multiply_reduce_fusion.5
  101.8 3.7 multiply_reduce_fusion.4
  110.0 6.2 convolution_convert_fusion.2.value
  116.2 2.9 copy.161.qraw
  119.1 2.9 copy.162.kraw
  124.1 15.7 %attend.1 = (bf16[1024,512]{1,0:T(8,128)(2,1)}, bf16[1024,512]{1,0:T(8,128)(2,1)}, bf16[1024,512]{1,0:T(8,128)(2,1)}, f32[1024,512]{1,0:T(8,128)}) custom-call(f32[1024,512]{1,0:T(8,128)} %copy.161.qraw, f32[1024,512]{1,0:T(8,128)} %copy.162.kraw, bf16[1024,512]{1,0:T(8,128)(2,1)} %convolution_convert_fusion.2.value, f32[1024,1]{1,0:T(8,128)} %copy.163.q_scale, ...), custom_call_target="tpu_custom_call" | custom-call | flops 1610612736 | bytes 9437184 | tf_op jit(solution)/shard_map/attend/pallas_call | solution.py:114
  142.7 2.7 convolution_convert_fusion.1
  145.5 3.6 convolution_convert_fusion
  155.1 34.4 %reduce-scatter.34.cloned.1.call-done = bf16[128,2048]{1,0:T(8,128)(2,1)} async-done(((bf16[512,2048]{1,0:T(8,128)(2,1)}), bf16[128,2048]{1,0:T(8,128)(2,1)}) %reduce-scatter.34.cloned.1.call-update) | async-done | bytes 524304
  191.5 44.2 %reduce-scatter.38.cloned.1.call-done = bf16[128,2048]{1,0:T(8,128)(2,1)} async-done(((bf16[512,2048]{1,0:T(8,128)(2,1)}), bf16[128,2048]{1,0:T(8,128)(2,1)}) %reduce-scatter.38.cloned.1.call-update) | async-done | bytes 524304
  237.8 3.1 multiply_reduce_fusion.12
  246.1 6.7 convert_reduce_fusion
  254.4 28.3 %all-gather.12.cloned.1.call-done = bf16[512,2048]{0,1:T(8,128)(2,1)} async-done(((bf16[128,2048]{0,1:T(8,128)(2,1)}), bf16[512,2048]{0,1:T(8,128)(2,1)}) %all-gather.12.cloned.1.call-update) | async-done | bytes 2097168 | tf_op jit(solution)/shard_map/all_gather | solution.py:333
  282.7 3.9 copy.168.grad
  286.6 15.1 %up_back.2.back = bf16[512,4096]{1,0:T(8,128)(2,1)} custom-call(bf16[512,2048]{1,0:T(8,128)(2,1)} %copy.168.grad, bf16[16,2048,256]{2,1,0:T(8,128)(2,1)} %down_w.7), custom_call_target="tpu_custom_call" | custom-call | flops 8589934592 | bytes 18874368 | tf_op jit(solution)/shard_map/up_back/pallas_call | solution.py:206
  301.7 26.9 %all-gather.10.cloned.1.call-done = bf16[512,2048]{0,1:T(8,128)(2,1)} async-done(((bf16[128,2048]{0,1:T(8,128)(2,1)}), bf16[512,2048]{0,1:T(8,128)(2,1)}) %all-gather.10.cloned.1.call-update) | async-done | bytes 2097168 | tf_op jit(solution)/shard_map/all_gather | solution.py:333
  328.6 3.9 copy.172.rows_in
  332.5 47.5 %experts.2 = (bf16[512,4096]{1,0:T(8,128)(2,1)}, bf16[512,4096]{1,0:T(8,128)(2,1)}, bf16[512,4096]{1,0:T(8,128)(2,1)}, bf16[512,2176]{1,0:T(8,128)(2,1)}) custom-call(bf16[512,2048]{1,0:T(8,128)(2,1)} %copy.172.rows_in, bf16[512,4096]{1,0:T(8,128)(2,1)} %up_back.2.back, f32[512,128]{1,0:T(8,128)} %bitcast.102, bf16[2048,128]{1,0:T(8,128)(2,1)} %pad.4.router, ...), custom_call_target="tpu_custom_call" | custom-call | flops 34359738368 | bytes 50331648 | tf_op jit(solution)/shard_map/experts/pallas_call | solution.py:271
  380.0 15.4 %down.2 = bf16[512,2048]{1,0:T(8,128)(2,1)} custom-call(bf16[512,4096]{1,0:T(8,128)(2,1)} %get-tuple-element.34.act.refs_2_, bf16[16,2048,256]{2,1,0:T(8,128)(2,1)} %down_w.7), custom_call_target="tpu_custom_call" | custom-call | flops 8589934592 | bytes 18874368 | tf_op jit(solution)/shard_map/down/pallas_call | solution.py:320
  401.1 36.6 %reduce-scatter.36.cloned.1.call-done = bf16[128,2048]{1,0:T(8,128)(2,1)} async-done(((bf16[512,2048]{1,0:T(8,128)(2,1)}), bf16[128,2048]{1,0:T(8,128)(2,1)}) %reduce-scatter.36.cloned.1.call-update) | async-done | bytes 524304
  439.7 45.7 %reduce-scatter.42.cloned.1.call-done = bf16[128,2176]{1,0:T(8,128)(2,1)} async-done(((bf16[512,2176]{1,0:T(8,128)(2,1)}), bf16[128,2176]{1,0:T(8,128)(2,1)}) %reduce-scatter.42.cloned.1.call-update) | async-done | bytes 557072
  493.5 39.2 %all-gather.16.cloned.1.call-done = bf16[512,2048]{0,1:T(8,128)(2,1)} async-done(((bf16[128,2048]{0,1:T(8,128)(2,1)}), bf16[512,2048]{0,1:T(8,128)(2,1)}) %all-gather.16.cloned.1.call-update) | async-done | bytes 2097168 | tf_op jit(solution)/shard_map/all_gather | solution.py:333
  532.7 3.9 copy.176.grad
  536.7 15.0 %up_back.3.back = bf16[512,4096]{1,0:T(8,128)(2,1)} custom-call(bf16[512,2048]{1,0:T(8,128)(2,1)} %copy.176.grad, bf16[16,2048,256]{2,1,0:T(8,128)(2,1)} %down_w.7), custom_call_target="tpu_custom_call" | custom-call | flops 8589934592 | bytes 18874368 | tf_op jit(solution)/shard_map/up_back/pallas_call | solution.py:206
  551.7 27.2 %all-gather.14.cloned.1.call-done = bf16[512,2048]{0,1:T(8,128)(2,1)} async-done(((bf16[128,2048]{0,1:T(8,128)(2,1)}), bf16[512,2048]{0,1:T(8,128)(2,1)}) %all-gather.14.cloned.1.call-update) | async-done | bytes 2097168 | tf_op jit(solution)/shard_map/all_gather | solution.py:333
  578.9 3.9 copy.178.rows_in
  582.8 47.5 %experts.3 = (bf16[512,4096]{1,0:T(8,128)(2,1)}, bf16[512,4096]{1,0:T(8,128)(2,1)}, bf16[512,4096]{1,0:T(8,128)(2,1)}, bf16[512,2176]{1,0:T(8,128)(2,1)}) custom-call(bf16[512,2048]{1,0:T(8,128)(2,1)} %copy.178.rows_in, bf16[512,4096]{1,0:T(8,128)(2,1)} %up_back.3.back, f32[512,128]{1,0:T(8,128)} %bitcast.101, bf16[2048,128]{1,0:T(8,128)(2,1)} %pad.4.router, ...), custom_call_target="tpu_custom_call" | custom-call | flops 34359738368 | bytes 50331648 | tf_op jit(solution)/shard_map/experts/pallas_call | solution.py:271
  630.3 15.4 %down.3 = bf16[512,2048]{1,0:T(8,128)(2,1)} custom-call(bf16[512,4096]{1,0:T(8,128)(2,1)} %get-tuple-element.35.act.refs_3_, bf16[16,2048,256]{2,1,0:T(8,128)(2,1)} %down_w.7), custom_call_target="tpu_custom_call" | custom-call | flops 8589934592 | bytes 18874368 | tf_op jit(solution)/shard_map/down/pallas_call | solution.py:320
  648.5 39.5 %reduce-scatter.40.cloned.1.call-done = bf16[128,2048]{1,0:T(8,128)(2,1)} async-done(((bf16[512,2048]{1,0:T(8,128)(2,1)}), bf16[128,2048]{1,0:T(8,128)(2,1)}) %reduce-scatter.40.cloned.1.call-update) | async-done | bytes 524304
  690.0 45.6 %reduce-scatter.44.cloned.1.call-done = bf16[128,2176]{1,0:T(8,128)(2,1)} async-done(((bf16[512,2176]{1,0:T(8,128)(2,1)}), bf16[128,2176]{1,0:T(8,128)(2,1)}) %reduce-scatter.44.cloned.1.call-update) | async-done | bytes 557072
  741.9 40.8 %all-gather.18.cloned.1.call-done = bf16[512,2048]{0,1:T(8,128)(2,1)} async-done(((bf16[128,2048]{0,1:T(8,128)(2,1)}), bf16[512,2048]{0,1:T(8,128)(2,1)}) %all-gather.18.cloned.1.call-update) | async-done | bytes 2097168 | tf_op jit(solution)/shard_map/all_gather | solution.py:333
  782.7 2.9 convolution_convert_fusion.4
  785.6 43.8 %all-gather.20.cloned.1.call-done = bf16[512,2048]{0,1:T(8,128)(2,1)} async-done(((bf16[128,2048]{0,1:T(8,128)(2,1)}), bf16[512,2048]{0,1:T(8,128)(2,1)}) %all-gather.20.cloned.1.call-update) | async-done | bytes 2097168 | tf_op jit(solution)/shard_map/all_gather | solution.py:333
  829.4 2.9 convolution_convert_fusion.3
  833.3 24.1 %attend_back.1 = (f32[1024,512]{1,0:T(8,128)}, f32[1024,512]{1,0:T(8,128)}, bf16[1024,512]{1,0:T(8,128)(2,1)}, f32[1024,1]{1,0:T(8,128)}, f32[1024,1]{1,0:T(8,128)}, /*index=5*/f32[1,512]{1,0:T(1,128)}, f32[1,512]{1,0:T(1,128)}) custom-call(bf16[1024,512]{1,0:T(8,128)(2,1)} %get-tuple-element.38.query, bf16[1024,512]{1,0:T(8,128)(2,1)} %get-tuple-element.39.key, ...), custom_call_target="tpu_custom_call" | custom-call | flops 4026531840 | bytes 16777216 | tf_op jit(solution)/shard_map/attend_back/pallas_call | solution.py:180
  860.2 3.4 collective-permute-done.2
  864.3 3.9 collective-permute-done.3
  870.6 2.4 fusion.26
  877.2 4.8 add_convert_fusion
  882.1 2.6 copy.199
  884.7 4.1 copy.198
  888.7 4.1 copy.197
  892.9 2.5 fusion.28
  898.2 2.7 multiply_reduce_fusion
  901.0 2.7 multiply_reduce_fusion.1
  903.7 2.7 multiply_reduce_fusion.2
  906.5 4.1 pad_maximum_fusion
  910.6 24.9 %wgrad.3 = bf16[16,2048,256]{2,1,0:T(8,128)(2,1)} custom-call(bf16[2048,512]{1,0:T(8,128)(2,1)} %bitcast.88, bf16[2048,512]{1,0:T(8,128)(2,1)} %bitcast.91, bf16[512,4096]{1,0:T(8,128)(2,1)} %get-tuple-element.48.refs_2_, bf16[512,4096]{1,0:T(8,128)(2,1)} %get-tuple-element.49.refs_3_), custom_call_target="tpu_custom_call" | custom-call | flops 17179869184 | bytes 20971520 | tf_op jit(solution)/shard_map/wgrad/pallas_call | solution.py:298
  935.6 25.1 %wgrad.4 = bf16[16,2048,256]{2,1,0:T(8,128)(2,1)} custom-call(bf16[2048,512]{1,0:T(8,128)(2,1)} %bitcast.89, bf16[2048,512]{1,0:T(8,128)(2,1)} %bitcast.92, bf16[512,4096]{1,0:T(8,128)(2,1)} %get-tuple-element.50.refs_2_, bf16[512,4096]{1,0:T(8,128)(2,1)} %get-tuple-element.51.refs_3_), custom_call_target="tpu_custom_call" | custom-call | flops 17179869184 | bytes 20971520 | tf_op jit(solution)/shard_map/wgrad/pallas_call | solution.py:298
  960.7 25.2 %wgrad.5 = bf16[16,2048,256]{2,1,0:T(8,128)(2,1)} custom-call(bf16[2048,512]{1,0:T(8,128)(2,1)} %bitcast.87, bf16[2048,512]{1,0:T(8,128)(2,1)} %bitcast.90, bf16[512,4096]{1,0:T(8,128)(2,1)} %get-tuple-element.34.act.refs_2_, bf16[512,4096]{1,0:T(8,128)(2,1)} %get-tuple-element.35.act.refs_3_), custom_call_target="tpu_custom_call" | custom-call | flops 17179869184 | bytes 20971520 | tf_op jit(solution)/shard_map/wgrad/pallas_call | solution.py:298
  992.4 10.1 collective-permute-done.10
  1005.6 8.4 collective-permute-done.11
  1015.6 4.1 collective-permute-done.12
  1023.4 5.8 collective-permute-done.13
  1031.4 3.5 collective-permute-done.8
  1039.3 2.9 copy.201
  1047.5 109.4 %reduce-scatter.28.cloned.1.call-done = bf16[2,2048,256]{2,1,0:T(8,128)(2,1)} async-done(((bf16[16,2048,256]{2,1,0:T(8,128)(2,1)}), bf16[2,2048,256]{2,1,0:T(8,128)(2,1)}) %reduce-scatter.28.cloned.1.call-update) | async-done | bytes 2097168 | tf_op jit(solution)/shard_map/reduce_scatter | solution.py:341
  1157.0 3.9 convert_element_type.155
  1160.9 115.5 %reduce-scatter.30.cloned.1.call-done = bf16[2,2048,256]{2,1,0:T(8,128)(2,1)} async-done(((bf16[16,2048,256]{2,1,0:T(8,128)(2,1)}), bf16[2,2048,256]{2,1,0:T(8,128)(2,1)}) %reduce-scatter.30.cloned.1.call-update) | async-done | bytes 2097168 | tf_op jit(solution)/shard_map/reduce_scatter | solution.py:341
  1276.4 4.1 convert_element_type.156
  1280.5 115.3 %reduce-scatter.32.cloned.1.call-done = bf16[2,2048,256]{2,1,0:T(8,128)(2,1)} async-done(((bf16[16,2048,256]{2,1,0:T(8,128)(2,1)}), bf16[2,2048,256]{2,1,0:T(8,128)(2,1)}) %reduce-scatter.32.cloned.1.call-update) | async-done | bytes 2097168 | tf_op jit(solution)/shard_map/reduce_scatter | solution.py:341
  1395.8 3.9 convert_element_type.157
  (289 shorter events, 98.2 us)
Async XLA Ops:
  7.2 135.6 %copy-start = (bf16[2048,512]{1,0:T(8,128)(2,1)S(1)}, bf16[2048,512]{1,0:T(8,128)(2,1)}, u32[]{:S(2)}) copy-start(bf16[2048,512]{1,0:T(8,128)(2,1)} %param.26) | copy-start | bytes 6291460
  7.2 3.2 copy-start.46
  7.2 87.9 %all-gather.8.cloned.1.call-start = ((), (), s32[]{:S(2)}) async-start(), calls=%async_computation.11 | async-start | bytes 5242880 | tf_op jit(solution)/shard_map/all_gather | solution.py:333
  8.9 144.8 %copy-start.2 = (bf16[256,2048]{0,1:T(8,128)(2,1)}, bf16[256,2048]{0,1:T(8,128)(2,1)S(1)}, u32[]{:S(2)}) copy-start(bf16[256,2048]{0,1:T(8,128)(2,1)S(1)} %copy.160) | copy-start | bytes 3145732
  11.7 177.8 %reduce-scatter.34.cloned.1.call-start = ((), (), s32[]{:S(2)}) async-start(), calls=%async_computation.23 | async-start | bytes 2621440
  95.1 6.7 copy-start.25
  95.1 6.7 copy-start.66
  101.8 3.9 copy-start.22
  101.8 3.9 copy-start.23
  101.8 3.9 copy-start.24
  105.6 3.7 collective-permute-start
  109.3 12.7 collective-permute-start.1
  145.4 90.3 %reduce-scatter.38.cloned.1.call-start = ((), (), s32[]{:S(2)}) async-start(), calls=%async_computation.25 | async-start | bytes 2621440
  149.1 133.6 %all-gather.12.cloned.1.call-start = ((), (), s32[]{:S(2)}) async-start(), calls=%async_computation.13 | async-start | bytes 2621440 | tf_op jit(solution)/shard_map/all_gather | solution.py:333
  153.6 175.0 %all-gather.10.cloned.1.call-start = ((), (), s32[]{:S(2)}) async-start(), calls=%async_computation.12 | async-start | bytes 2621440 | tf_op jit(solution)/shard_map/all_gather | solution.py:333
  237.8 3.1 copy-start.43
  242.1 195.6 %reduce-scatter.36.cloned.1.call-start = ((), (), s32[]{:S(2)}) async-start(), calls=%async_computation.24 | async-start | bytes 2621440
  395.4 90.0 %reduce-scatter.42.cloned.1.call-start = ((), (), s32[]{:S(2)}) async-start(), calls=%async_computation.27 | async-start | bytes 2785280
  396.2 136.6 %all-gather.16.cloned.1.call-start = ((), (), s32[]{:S(2)}) async-start(), calls=%async_computation.15 | async-start | bytes 2621440 | tf_op jit(solution)/shard_map/all_gather | solution.py:333
  398.3 180.6 %all-gather.14.cloned.1.call-start = ((), (), s32[]{:S(2)}) async-start(), calls=%async_computation.14 | async-start | bytes 2621440 | tf_op jit(solution)/shard_map/all_gather | solution.py:333
  399.7 89.1 %copy-start.48 = (f32[128,16]{0,1:T(8,128)}, f32[128,16]{0,1:T(8,128)S(1)}, u32[]{:S(2)}) copy-start(f32[128,16]{0,1:T(8,128)S(1)} %copy.228) | copy-start | bytes 24580
  401.0 90.3 %copy-start.44 = (f32[128,16]{0,1:T(8,128)}, f32[128,16]{0,1:T(8,128)S(1)}, u32[]{:S(2)}) copy-start(f32[128,16]{0,1:T(8,128)S(1)} %get-tuple-element.164) | copy-start | bytes 24580
  401.0 90.3 %copy-start.53 = (f32[128]{0:T(128)}, f32[128]{0:T(128)S(1)}, u32[]{:S(2)}) copy-start(f32[128]{0:T(128)S(1)} %get-tuple-element.163) | copy-start | bytes 1540
  401.1 90.3 %copy-start.57 = (f32[128]{0:T(128)}, f32[128]{0:T(128)S(1)}, u32[]{:S(2)}) copy-start(f32[128]{0:T(128)S(1)} %fusion.4) | copy-start | bytes 1540
  487.5 3.8 copy-start.6
  487.5 3.8 copy-start.14
  487.5 3.9 copy-start.20
  489.8 3.6 copy-start.61
  493.5 194.5 %reduce-scatter.40.cloned.1.call-start = ((), (), s32[]{:S(2)}) async-start(), calls=%async_computation.26 | async-start | bytes 2621440
  645.7 89.9 %reduce-scatter.44.cloned.1.call-start = ((), (), s32[]{:S(2)}) async-start(), calls=%async_computation.28 | async-start | bytes 2785280
  646.4 136.3 %all-gather.18.cloned.1.call-start = ((), (), s32[]{:S(2)}) async-start(), calls=%async_computation.16 | async-start | bytes 2621440 | tf_op jit(solution)/shard_map/all_gather | solution.py:333
  647.0 182.4 %all-gather.20.cloned.1.call-start = ((), (), s32[]{:S(2)}) async-start(), calls=%async_computation.17 | async-start | bytes 2621440 | tf_op jit(solution)/shard_map/all_gather | solution.py:333
  647.1 91.9 %copy-start.7 = (f32[128,2048]{0,1:T(8,128)S(1)}, f32[128,2048]{0,1:T(8,128)}, u32[]{:S(2)}) copy-start(f32[128,2048]{0,1:T(8,128)} %get-tuple-element.127) | copy-start | bytes 3145732
  741.8 293.7 %reduce-scatter.24.cloned.1.call-start = ((), (), s32[]{:S(2)}) async-start(), calls=%async_computation.18 | async-start | bytes 5242880 | tf_op jit(solution)/shard_map/reduce_scatter | solution.py:337
  833.3 35.0 %copy-start.5 = (f32[1024,512]{1,0:T(8,128)S(1)}, f32[1024,512]{1,0:T(8,128)}, u32[]{:S(2)}) copy-start(f32[1024,512]{1,0:T(8,128)} %copy.161.qraw) | copy-start | bytes 6291460
  833.3 35.0 %copy-start.59 = (f32[512]{0:T(512)S(1)}, f32[512]{0:T(512)}, u32[]{:S(2)}) copy-start(f32[512]{0:T(512)} %param.27) | copy-start | bytes 6148
  859.9 3.7 collective-permute-start.2
  863.6 4.6 collective-permute-start.3
  882.0 160.2 %reduce-scatter.26.cloned.1.call-start = ((), (), s32[]{:S(2)}) async-start(), calls=%async_computation.19 | async-start | bytes 9437184 | tf_op jit(solution)/shard_map/reduce_scatter | solution.py:341
  888.7 4.1 copy-start.8
  910.6 246.4 %reduce-scatter.28.cloned.1.call-start = ((), (), s32[]{:S(2)}) async-start(), calls=%async_computation.20 | async-start | bytes 18874368 | tf_op jit(solution)/shard_map/reduce_scatter | solution.py:341
  935.5 340.9 %reduce-scatter.30.cloned.1.call-start = ((), (), s32[]{:S(2)}) async-start(), calls=%async_computation.21 | async-start | bytes 18874368 | tf_op jit(solution)/shard_map/reduce_scatter | solution.py:341
  960.7 435.1 %reduce-scatter.32.cloned.1.call-start = ((), (), s32[]{:S(2)}) async-start(), calls=%async_computation.22 | async-start | bytes 18874368 | tf_op jit(solution)/shard_map/reduce_scatter | solution.py:341
  987.1 5.1 copy-start.65
  987.1 5.1 copy-start.64
  987.1 5.1 copy-start.47
  988.1 33.7 %copy-start.32 = (bf16[128,2048]{0,1:T(8,128)(2,1)S(1)}, bf16[128,2048]{0,1:T(8,128)(2,1)}, u32[]{:S(2)}) copy-start(bf16[128,2048]{0,1:T(8,128)(2,1)} %get-tuple-element.132) | copy-start | bytes 1572868
  988.1 33.7 %copy-start.35 = (bf16[128,2048]{0,1:T(8,128)(2,1)S(1)}, bf16[128,2048]{0,1:T(8,128)(2,1)}, u32[]{:S(2)}) copy-start(bf16[128,2048]{0,1:T(8,128)(2,1)} %get-tuple-element.133) | copy-start | bytes 1572868
  989.2 1.5 collective-permute-start.9
  990.7 11.7 collective-permute-start.10
  992.3 11.7 collective-permute-start.4
  1002.5 11.5 collective-permute-start.11
  1004.0 10.2 collective-permute-start.5
  1014.0 5.7 collective-permute-start.12
  1014.2 6.2 collective-permute-start.6
  1019.8 9.4 collective-permute-start.13
  1021.0 8.2 collective-permute-start.7
  1021.9 13.6 copy-start.3
  1023.4 14.0 copy-start.15
  1023.4 14.0 copy-start.17
  1023.4 14.0 copy-start.56
  1023.4 14.0 copy-start.63
  1030.0 4.9 collective-permute-start.8
  1276.4 123.3 %copy-start.1 = (bf16[2048,512]{1,0:T(8,128)(2,1)S(1)}, bf16[2048,512]{1,0:T(8,128)(2,1)}, u32[]{:S(2)}) copy-start(bf16[2048,512]{1,0:T(8,128)(2,1)} %param.26) | copy-start | bytes 6291460
  (36 other events, 68.7 us)
Sparse Core Ops, SparseCore 0:
  11.8 83.2 all-gather.7
  145.5 43.9 reduce-scatter.33
  192.5 43.1 reduce-scatter.37
  237.1 45.5 all-gather.11
  284.1 44.4 all-gather.9
  395.5 42.0 reduce-scatter.35
  440.1 45.3 reduce-scatter.41
  487.1 45.6 all-gather.15
  534.4 44.4 all-gather.13
  645.8 42.0 reduce-scatter.39
  690.2 45.3 reduce-scatter.43
  737.0 45.6 all-gather.17
  784.8 44.4 all-gather.19
  882.2 75.0 reduce-scatter.23
  960.9 76.5 reduce-scatter.25
  1041.0 115.9 reduce-scatter.27
  1160.4 115.9 reduce-scatter.29
  1279.8 115.9 reduce-scatter.31

commit v2 on v1

--- a/solution.py
+++ b/solution.py
@@ -35,8 +35,11 @@
     return pltpu.CompilerParams(vmem_limit_bytes=VMEM)
 
 
+PACE = 0.8
+
+
 def cost(flops, moved, special=0):
-    return pl.CostEstimate(flops=flops, bytes_accessed=moved, transcendentals=special)
+    return pl.CostEstimate(flops=int(1.5 * PACE * flops + 6e4 * PACE * special), bytes_accessed=moved // 8, transcendentals=0)
 
 
 def rms_scale(values):
@@ -75,6 +78,122 @@
 
 def turned(values):
     return pltpu.roll(values, values.shape[1] // 2, 1)
+
+
+def project_kernel(rows_in, w_query, w_key, w_value, q_out, k_out, v_out, squares_out):
+    ones = jnp.ones((8, q_out.shape[1]), f32)
+    for at, (weight, out) in enumerate(((w_query, q_out), (w_key, k_out))):
+        raw = nn(rows_in[...], weight[...])
+        out[...] = raw
+        sums = lax.dot_general(
+            ones, raw * raw, (((1,), (1,)), ((), ())), precision=lax.Precision.HIGHEST, preferred_element_type=f32
+        )
+        squares_out[at : at + 1, :] = sums[:1]
+    v_out[...] = nn(rows_in[...], w_value[...]).astype(bf16)
+
+
+def project(rows_in, w_query, w_key, w_value):
+    rows, features = rows_in.shape
+    width = w_query.shape[1]
+    block = min(256, rows)
+    row = lambda columns: pl.BlockSpec((block, columns), lambda r: (r, 0))
+    weight = pl.BlockSpec((features, width), lambda r: (0, 0))
+    sds = jax.ShapeDtypeStruct
+    return pl.pallas_call(
+        project_kernel,
+        grid=(rows // block,),
+        in_specs=[row(features), weight, weight, weight],
+        out_specs=[row(width), row(width), row(width), pl.BlockSpec((2, block), lambda r: (0, r))],
+        out_shape=[sds((rows, width), f32), sds((rows, width), f32), sds((rows, width), bf16), sds((2, rows), f32)],
+        compiler_params=params(),
+        cost_estimate=cost(6 * rows * features * width, 2 * (rows + 3 * width) * features),
+        name="project",
+    )(rows_in, w_query, w_key, w_value)
+
+
+def project_back_kernel(
+    rows_in, dqn, dkn, dvalue, qraw, kraw, q_scale, k_scale, q_dot, k_dot, q_gain, k_gain,
+    w_query, w_key, w_value, part_out, dq_out, dk_out, gain_out,
+):
+    @pl.when(pl.program_id(0) == 0)
+    def _():
+        gain_out[...] = jnp.zeros_like(gain_out)
+
+    def raw_grad(grad, raw, scale, gain, dot):
+        cube = scale[...] * scale[...] * scale[...]
+        return (scale[...] * (gain[...] * grad[...]) - raw[...] * (cube * dot[...])).astype(bf16)
+
+    dq = raw_grad(dqn, qraw, q_scale, q_gain, q_dot)
+    dk = raw_grad(dkn, kraw, k_scale, k_gain, k_dot)
+    dq_out[...] = dq
+    dk_out[...] = dk
+    part = nt(dq, w_query[...]) + nt(dk, w_key[...]) + nt(dvalue[...], w_value[...])
+    part_out[...] = part.astype(bf16)
+    gain_out[...] += jnp.sum(part * rows_in[...].astype(f32), axis=0, keepdims=True)
+
+
+def project_back(rows_in, dqn, dkn, dvalue, qraw, kraw, q_scale, k_scale, q_dot, k_dot, q_gain, k_gain, w_query, w_key, w_value):
+    rows, features = rows_in.shape
+    width = w_query.shape[1]
+    block = min(256, rows)
+    row = lambda columns: pl.BlockSpec((block, columns), lambda r: (r, 0))
+    whole = lambda *shape: pl.BlockSpec(shape, lambda r: (0, 0))
+    sds = jax.ShapeDtypeStruct
+    return pl.pallas_call(
+        project_back_kernel,
+        grid=(rows // block,),
+        in_specs=[row(features)] + [row(width)] * 5 + [row(1)] * 4 + [whole(1, width)] * 2 + [whole(features, width)] * 3,
+        out_specs=[row(features), row(width), row(width), whole(1, features)],
+        out_shape=[sds((rows, features), bf16), sds((rows, width), bf16), sds((rows, width), bf16), sds((1, features), f32)],
+        compiler_params=params(),
+        cost_estimate=cost(6 * rows * features * width, 2 * (rows + 3 * width) * features),
+        name="project_back",
+    )(rows_in, dqn, dkn, dvalue, qraw, kraw, q_scale, k_scale, q_dot, k_dot, q_gain[None], k_gain[None], w_query, w_key, w_value)
+
+
+def attention_wgrad_kernel(count, extra, order, *refs):
+    rows_in = refs[0]
+    middles = refs[1 : 1 + count]
+    sides = refs[1 + count : 4 + count]
+    attended = refs[4 + count : 4 + 2 * count]
+    outs = refs[4 + 2 * count + extra :]
+    totals = [tn(rows_in[...], side[...]) for side in sides]
+    total = tn(middles[0][...], attended[0][...])
+    for left, right in zip(middles[1:], attended[1:]):
+        total = total + tn(left[...], right[...])
+    totals.append(total)
+    half = outs[0].shape[2]
+    for at, total in enumerate(totals):
+        if extra:
+            total = total + refs[4 + 2 * count][0, at].astype(f32)
+        for place, out in enumerate(outs):
+            out[0, at] = total[place * half : (place + 1) * half, :].astype(bf16)
+
+
+def attention_wgrad(rows_in, middles, sides, attended, order, blocks, added=None):
+    features = rows_in.shape[1]
+    width = sides[0].shape[1]
+    block = features // blocks
+    extra = [] if added is None else [added]
+    outs = 1 + len(extra)
+    left = lambda values: pl.BlockSpec((values.shape[0], block), lambda i, ids: (0, ids[i]))
+    right = lambda values: pl.BlockSpec(values.shape, lambda i, ids: (0, 0))
+    out = lambda parts: pl.BlockSpec((1, 4, block // parts, width), lambda i, ids: (i, 0, 0, 0))
+    result = pl.pallas_call(
+        functools.partial(attention_wgrad_kernel, len(middles), len(extra)),
+        grid_spec=pltpu.PrefetchScalarGridSpec(
+            num_scalar_prefetch=1,
+            grid=(order.shape[0],),
+            in_specs=[left(rows_in)] + [left(m) for m in middles] + [right(v) for v in sides] + [right(v) for v in attended]
+            + [out(1) for _ in extra],
+            out_specs=[out(outs)] * outs,
+        ),
+        out_shape=[jax.ShapeDtypeStruct((order.shape[0], 4, block // outs, width), bf16)] * outs,
+        compiler_params=params(),
+        cost_estimate=cost(8 * rows_in.shape[0] * features * width, 4 * features * width),
+        name="attention_wgrad",
+    )(order, rows_in, *middles, *sides, *attended, *extra)
+    return result if extra else result[0]
 
 
 def attend_kernel(
@@ -281,31 +400,69 @@
     )(rows_in, back, routed, router, gate_w, up_w)
 
 
-def wgrad_kernel(count, block, *refs):
-    lefts, rights, out = refs[:count], refs[count : 2 * count], refs[2 * count]
-    for start in range(0, out.shape[1], block):
-        here = slice(start, start + block)
-        total = nn(lefts[0][here, :], rights[0][...])
+def wgrad_kernel(count, extra, per, block, order, *refs):
+    lefts, rights = refs[:count], refs[count : 2 * count]
+    added = refs[2 * count : 2 * count + extra]
+    outs = refs[2 * count + extra :]
+    at = pl.program_id(0)
+    features = lefts[0].shape[1]
+
+    def piece(start, stop):
+        total = tn(lefts[0][:, start:stop], rights[0][...])
         for left, right in zip(lefts[1:], rights[1:]):
-            total = total + nn(left[here, :], right[...])
-        out[0, here, :] = total.astype(out.dtype)
-
-
-def wgrad(lefts, rights, experts):
-    features = lefts[0].shape[0]
-    width = rights[0].shape[1] // experts
-    rows = sum(left.shape[1] for left in lefts)
+            total = total + tn(left[:, start:stop], right[...])
+        return total
+
+    if not added:
+        for place, out in enumerate(outs):
+
+            @pl.when(at // per == place)
+            def _(out=out):
+                for start in range(0, features, block):
+                    out[0, start : start + block, :] = piece(start, start + block).astype(bf16)
+
+        return
+    half = features // 2
+    for place, got in enumerate(added):
+
+        @pl.when(at // per == place)
+        def _(got=got):
+            for start in range(0, features, block):
+                total = piece(start, start + block) + got[0, start : start + block, :].astype(f32)
+                outs[start // half][0, start % half : start % half + block, :] = total.astype(bf16)
+
+
+def wgrad(lefts, rights, order, width, per, added=()):
+    features = lefts[0].shape[1]
+    experts = order.shape[0]
+    groups = experts // per
+    rows = sum(left.shape[0] for left in lefts)
+
+    def group_spec(place):
+        return pl.BlockSpec((1, features, width), lambda i, ids: (jnp.clip(i - place * per, 0, per - 1), 0, 0))
+
+    groups_specs = [group_spec(place) for place in range(groups)]
+    if added:
+        out_specs = [pl.BlockSpec((1, features // 2, width), lambda i, ids: (i, 0, 0))] * 2
+        out_shape = [jax.ShapeDtypeStruct((experts, features // 2, width), bf16)] * 2
+    else:
+        out_specs = groups_specs
+        out_shape = [jax.ShapeDtypeStruct((per, features, width), bf16)] * groups
     return pl.pallas_call(
-        functools.partial(wgrad_kernel, len(lefts), min(512, features)),
-        grid=(experts,),
-        in_specs=[pl.BlockSpec(left.shape, lambda e: (0, 0)) for left in lefts]
-        + [pl.BlockSpec((right.shape[0], width), lambda e: (0, e)) for right in rights],
-        out_specs=pl.BlockSpec((1, features, width), lambda e: (e, 0, 0)),
-        out_shape=jax.ShapeDtypeStruct((experts, features, width), bf16),
+        functools.partial(wgrad_kernel, len(lefts), len(added), per, min(512, features // 2)),
+        grid_spec=pltpu.PrefetchScalarGridSpec(
+            num_scalar_prefetch=1,
+            grid=(experts,),
+            in_specs=[pl.BlockSpec(left.shape, lambda i, ids: (0, 0)) for left in lefts]
+            + [pl.BlockSpec((right.shape[0], width), lambda i, ids: (0, ids[i])) for right in rights]
+            + (groups_specs if added else []),
+            out_specs=out_specs,
+        ),
+        out_shape=out_shape,
         compiler_params=params(),
-        cost_estimate=cost(2 * rows * features * experts * width, 2 * (rows + experts * width) * features),
+        cost_estimate=cost(2 * rows * features * experts * width, 2 * (rows + 2 * experts * width) * features),
         name="wgrad",
-    )(*lefts, *rights)
+    )(order, *lefts, *rights, *added)
 
 
 def down_kernel(act, down_w, out):
@@ -329,6 +486,10 @@
     )(act, down_w)
 
 
+def gate(value, *others):
+    return lax.optimization_barrier((value, others))[0]
+
+
 def gather_rows(values):
     return lax.all_gather(values, "tensor", axis=0, tiled=True)
 
@@ -337,8 +498,119 @@
     return lax.psum_scatter(values, "tensor", scatter_dimension=0, tiled=True)
 
 
-def dp_scatter(values):
-    return lax.psum_scatter(values, "dp", scatter_dimension=0, tiled=True)
+class Chain:
+    def __init__(self, values):
+        self.values = values
+        self.parts = lax.axis_size("tensor")
+        self.ups, self.downs = [values], [values]
+
+    def hop(self, *others):
+        step = len(self.ups)
+        if step < self.parts:
+            up, down = gate((self.ups[-1], self.downs[-1]), *others) if others else (self.ups[-1], self.downs[-1])
+            self.sent = (up, down)
+            self.ups.append(lax.ppermute(up, "tensor", [(i, i + 1) for i in range(step - 1, self.parts - 1)]))
+            self.downs.append(lax.ppermute(down, "tensor", [(i, i - 1) for i in range(1, self.parts - step + 1)]))
+        return self.sent
+
+    def recv(self):
+        return self.ups[-1], self.downs[-1]
+
+    def joined(self):
+        while len(self.ups) < self.parts:
+            self.hop()
+        parts, values = self.parts, self.values
+        at = lax.axis_index("tensor")
+        rows = values.shape[0]
+        whole = jnp.zeros((parts * rows,) + values.shape[1:], values.dtype)
+        whole = lax.dynamic_update_slice_in_dim(whole, values, at * rows, 0)
+        for step in range(1, parts):
+            piece = self.ups[step] + self.downs[parts - step]
+            whole = lax.dynamic_update_slice_in_dim(whole, piece, lax.rem(at - step + parts, parts) * rows, 0)
+        return whole
+
+
+class ScatterChain:
+    def __init__(self, values):
+        self.parts = lax.axis_size("tensor")
+        self.at = lax.axis_index("tensor")
+        self.values = values
+        self.rows = values.shape[0] // self.parts
+        self.step = 0
+        self.up = self.down = self.first = None
+
+    def block(self, place):
+        return lax.dynamic_slice_in_dim(self.values, jnp.clip(place, 0, self.parts - 1) * self.rows, self.rows, 0)
+
+    def hop(self, *others):
+        parts, step = self.parts, self.step
+        if step < parts - 1:
+            if step:
+                self.values = gate(self.values, self.up, self.down, *others)
+            up = self.block(parts - 1 - step + self.at)
+            down = self.block(step - parts + 1 + self.at)
+            if step:
+                up = (up.astype(f32) + self.up.astype(f32)).astype(bf16)
+                down = (down.astype(f32) + self.down.astype(f32)).astype(bf16)
+            self.sent = (up, down)
+            self.first = self.first or self.sent
+            self.up = lax.ppermute(up, "tensor", [(i, i + 1) for i in range(step + 1)])
+            self.down = lax.ppermute(down, "tensor", [(i, i - 1) for i in range(parts - 1 - step, parts)])
+            self.step += 1
+        return self.up, self.down
+
+    def total(self):
+        while self.step < self.parts - 1:
+            self.hop()
+        return self.block(self.at).astype(f32) + self.up.astype(f32) + self.down.astype(f32)
+
+
+def pair_swap(values, step):
+    size = lax.axis_size("dp")
+    return lax.ppermute(values, "dp", [(i, i ^ step) for i in range(size)])
+
+
+class Halving:
+    def __init__(self, values):
+        bits = list(range(values[0].shape[0].bit_length() - 1))
+        self.kept = list(values)
+        self.left = [bits[::-1], bits]
+        self.got = None
+
+    def send(self):
+        if not self.left[0]:
+            return ()
+        self.got = []
+        sent = []
+        for side, downward in ((0, True), (1, False)):
+            bit = self.left[side].pop(0)
+            kept = self.kept[side]
+            half = kept.shape[0] // 2
+            if downward:
+                keep, go = kept[:half], kept[half:]
+            else:
+                view = kept.reshape((half, 2) + kept.shape[1:])
+                keep, go = view[:, 0], view[:, 1]
+            sent.append(go)
+            self.got.append(pair_swap(go, 2 << bit))
+            self.kept[side] = keep
+        return tuple(sent)
+
+    def add(self):
+        if self.got is not None:
+            last = not self.left[0]
+            for side in range(2):
+                total = self.kept[side].astype(f32) + self.got[side].astype(f32)
+                self.kept[side] = total if last else total.astype(bf16)
+            self.got = None
+        return tuple(self.kept)
+
+    def done(self):
+        self.add()
+        while self.left[0]:
+            self.send()
+            self.add()
+        return jnp.concatenate([kept[0].astype(f32) for kept in self.kept], axis=1)
 
 
 def exchange_sum(values, axes):
@@ -357,118 +629,181 @@
 ):
     parts = lax.axis_size("tensor")
     part_at = lax.axis_index("tensor")
+    dp_size = lax.axis_size("dp")
+    low_bit = lax.axis_index("dp") % 2
     shard_rows, features = tokens.shape
     group_rows = shard_rows * parts
     _, length = seg_ids.shape
     local_width = w_query.shape[1]
-    experts = w_gate.shape[0]
+    experts, _, width = w_gate.shape
+    per = experts // dp_size
     chunk_rows = shard_rows // CHUNKS
     chunks = range(CHUNKS)
     own = [slice(c * chunk_rows, (c + 1) * chunk_rows) for c in chunks]
 
     def chunk_of(values, c):
-        width = values.shape[1]
-        return values.reshape(parts, CHUNKS, chunk_rows, width)[:, c].reshape(parts * chunk_rows, width)
+        columns = values.shape[1]
+        return values.reshape(parts, CHUNKS, chunk_rows, columns)[:, c].reshape(parts * chunk_rows, columns)
 
     def in_order(pieces):
-        width = pieces[0].shape[1]
-        stacked = jnp.stack([piece.reshape(parts, chunk_rows, width) for piece in pieces], axis=1)
-        return stacked.reshape(group_rows, width)
+        columns = pieces[0].shape[1]
+        stacked = jnp.stack([piece.reshape(parts, chunk_rows, columns) for piece in pieces], axis=1)
+        return stacked.reshape(group_rows, columns)
 
     inputs = tokens.astype(f32)
     first_scale = rms_scale(inputs)
-    normed_all = gather_rows((inputs * first_scale * attn_gain).astype(bf16))
-    grad_all = [gather_rows(cotangent[own[c]]) for c in chunks]
-    backs = [up_back(grad_all[c], w_down) for c in chunks]
-
-    qraw = nn(normed_all, w_query)
-    kraw = nn(normed_all, w_key)
-    value = nn(normed_all, w_value).astype(bf16)
-    squares = exchange_sum(jnp.stack([jnp.sum(qraw * qraw, axis=1), jnp.sum(kraw * kraw, axis=1)]), ("tensor",))
-    q_scale, k_scale = (lax.rsqrt(squares[i] / features + EPSILON)[:, None] for i in range(2))
-    cosine, sine = rope_tables(length, HEAD)
-    query, key, attended, lse = attend(
-        qraw, kraw, value, q_scale, k_scale, q_gain, k_gain, cosine, sine, seg_ids[0], keep_mask[0]
-    )
+    normed_all = Chain((inputs * first_scale * attn_gain).astype(bf16)).joined()
+    behind = Chain(gate(cotangent, normed_all))
 
     expert_ids = jnp.arange(LANES)
     routed = jnp.sum((routes[:, :, None] == expert_ids[None, None, :]).astype(f32), axis=1)
     router_wide = jnp.pad(router, ((0, 0), (0, LANES - experts)))
-    middles, scales, ffn_own, ffn_all = [], [], [], []
-    for c in chunks:
-        summed = scatter_rows(nt(chunk_of(attended, c), w_out).astype(bf16))
-        middle = inputs[own[c]] + summed.astype(f32)
+    routed_own = lax.dynamic_slice_in_dim(routed, part_at * shard_rows, shard_rows, 0)[:, :experts]
+    cosine, sine = rope_tables(length, HEAD)
+    relative = jnp.arange(dp_size // 2, dtype=jnp.int32) ^ (lax.axis_index("dp") // 2)
+    own_blocks, other_blocks = 2 * relative + low_bit, 2 * relative + 1 - low_bit
+    mine, theirs = (
+        (blocks[:, None] * per + jnp.arange(per, dtype=jnp.int32)).reshape(-1) for blocks in (own_blocks, other_blocks)
+    )
+
+    qraw, kraw, value, squares = project(normed_all, w_query, w_key, w_value)
+    squares = exchange_sum(squares, ("tensor",))
+    behind.hop()
+    q_scale, k_scale = (lax.rsqrt(squares[i] / features + EPSILON)[:, None] for i in range(2))
+    query, key, attended, lse = attend(
+        qraw, kraw, value, q_scale, k_scale, q_gain, k_gain, cosine, sine, gate(seg_ids[0], routed, router_wide, *behind.recv()), keep_mask[0]
+    )
+    attended_parts = [chunk_of(attended, c) for c in chunks]
+    outs = [nt(attended_parts[0], w_out).astype(bf16)]
+    summed = [scatter_rows(outs[0])]
+    outs.append(nt(gate(attended_parts[1], outs[0]), w_out).astype(bf16))
+    summed.append(scatter_rows(outs[1]))
+    behind.hop(outs[1])
+
+    grad_group = behind.joined()
+    grad_all = [chunk_of(grad_group, c) for c in chunks]
+    backs = [up_back(grad_all[c], w_down) for c in chunks]
+
+    middles, scales, ffn_own = [], [], []
+
+    def middle_of(c, total):
+        middle = inputs[own[c]] + total.astype(f32)
         scale = rms_scale(middle)
         normed = (middle * scale * ffn_gain).astype(bf16)
         middles.append(middle)
         scales.append(scale)
         ffn_own.append(normed)
-        ffn_all.append(gather_rows(normed))
-
-    acts, dgates, dups, middle_grads, middle_all = [], [], [], [], []
-    ffn_gain_part = 0.0
-    router_part = 0.0
-    routed_own = lax.dynamic_slice_in_dim(routed, part_at * shard_rows, shard_rows, 0)[:, :experts]
+        return normed
+
+    ahead = Chain(middle_of(0, summed[0]))
+    ahead.hop()
+    after = gather_rows(middle_of(1, gate(summed[1], *ahead.recv())))
+    ahead.hop(backs[0])
+    ahead.hop(backs[1])
+    ffn_all = [ahead.joined(), after]
+    acts, dgates, dups, expert_grads = [], [], [], []
     for c in chunks:
-        act, dgate, dup, grads = experts_block(ffn_all[c], backs[c], chunk_of(routed, c), router_wide, w_gate, w_up)
+        here = gate(chunk_of(routed, c), *backs, *acts[-1:])
+        act, dgate, dup, grads = experts_block(ffn_all[c], backs[c], here, router_wide, w_gate, w_up)
         acts.append(act)
         dgates.append(dgate)
         dups.append(dup)
-        grads = scatter_rows(grads).astype(f32)
+        expert_grads.append(grads)
+    expert_grads[0] = scatter_rows(expert_grads[0])
+    second_sums = ScatterChain(expert_grads[1])
+
+    ffn_gain_parts, router_parts, middle_grads = [], [], []
+
+    def middle_back(c, grads):
         share_grad = grads[:, features : features + experts] * routed_own[own[c]]
         probs = jax.nn.softmax(nn(ffn_own[c], router), axis=-1)
         logit_grad = (probs * (share_grad - jnp.sum(share_grad * probs, axis=-1, keepdims=True))).astype(bf16)
         ffn_grad = grads[:, :features] + nt(logit_grad, router)
-        router_part = router_part + tn(ffn_own[c], logit_grad)
-        ffn_gain_part = ffn_gain_part + jnp.sum(ffn_grad * middles[c] * scales[c], axis=0)
-        middle_grad = cotangent[own[c]].astype(f32) + norm_back(ffn_grad, middles[c], scales[c], ffn_gain)
-        middle_grads.append(middle_grad)
-        middle_all.append(gather_rows(middle_grad.astype(bf16)))
-
-    layer_out = jnp.concatenate(
-        [(middles[c] + scatter_rows(down(acts[c], w_down)).astype(f32)).astype(bf16) for c in chunks]
-    )
-    ffn_t = [rows.T for rows in ffn_all]
-    grad_t = [rows.T for rows in grad_all]
-    gate_done = dp_scatter(wgrad(ffn_t, dgates, experts)).astype(f32)
-    up_done = dp_scatter(wgrad(ffn_t, dups, experts)).astype(f32)
-    down_done = dp_scatter(wgrad(grad_t, acts, experts)).astype(f32)
+        router_parts.append(tn(ffn_own[c], logit_grad))
+        ffn_gain_parts.append(jnp.sum(ffn_grad * middles[c] * scales[c], axis=0))
+        middle_grads.append(cotangent[own[c]].astype(f32) + norm_back(ffn_grad, middles[c], scales[c], ffn_gain))
+        return Chain(middle_grads[c].astype(bf16))
+
+    def expert_sums(lefts, rights, ids, *others, added=()):
+        return wgrad(lefts, rights, gate(ids, *others), width, per, added)
+
+    def core_swap(pieces):
+        return [pair_swap(piece, 1) for piece in pieces]
+
+    def halving(sums):
+        return Halving([half.reshape((dp_size // 2, per) + half.shape[1:]) for half in sums])
+
+    first = middle_back(0, gate(expert_grads[0], acts[1]).astype(f32))
+    second_sums.hop()
+    first.hop()
+    gate_sent = expert_sums(ffn_all, dgates, theirs, first.values, *second_sums.sent)
+    gate_got = core_swap(gate_sent)
+    second_sums.hop(*gate_sent)
+    up_sent = expert_sums(ffn_all, dups, theirs, *first.hop(*gate_sent), *second_sums.sent)
+    up_got = core_swap(up_sent)
+    second_sums.hop(*up_sent)
+    down_sent = expert_sums(grad_all, acts, theirs, *first.hop(*up_sent), *second_sums.sent)
+    down_got = core_swap(down_sent)
+    second = middle_back(1, gate(second_sums.total(), *down_sent))
+    second.hop()
+    gate_sums = expert_sums(ffn_all, dgates, mine, second.values, *first.recv(), added=gate_got)
+    gate_out = halving(gate_sums)
+    up_sums = expert_sums(ffn_all, dups, mine, *second.hop(*gate_sums), *gate_out.send(), added=up_got)
+    up_out = halving(up_sums)
+    moe_0 = down(gate(acts[0], *second.hop(*up_sums), *up_out.send()), w_down)
+    moe_sum_0 = scatter_rows(moe_0)
+    middle_all = [first.joined(), second.joined()]
 
     attended_grad = in_order([nn(rows, w_out).astype(bf16) for rows in middle_all])
+    gate_late = gate_out.add()
+    gate_out.send()
     dqn, dkn, dvalue, qdot, kdot, q_gain_part, k_gain_part = attend_back(
         query, key, value, attended_grad, lse, qraw, kraw, q_scale, k_scale, q_gain, k_gain, cosine, sine,
-        seg_ids[0], keep_mask[0],
+        gate(seg_ids[0], moe_0, *gate_late), keep_mask[0],
     )
     dots = exchange_sum(jnp.stack([qdot[:, 0], kdot[:, 0]]), ("tensor",)) / features
-
-    def raw_grad(grad, raw, scale, gain, dot):
-        return (scale * gain * grad - raw * (scale * scale * scale) * dot[:, None]).astype(bf16)
-
-    dqraw = raw_grad(dqn, qraw, q_scale, q_gain, dots[0])
-    dkraw = raw_grad(dkn, kraw, k_scale, k_gain, dots[1])
-    normed_part = nt(dqraw, w_query) + nt(dkraw, w_key) + nt(dvalue, w_value)
-    normed_grad = scatter_rows(normed_part.astype(bf16)).astype(f32)
-    normed_t = normed_all.T
-    attn_grads = [nn(normed_t, dqraw), nn(normed_t, dkraw), nn(normed_t, dvalue)]
-    attn_gain_part = sum(
-        jnp.sum(grad * weight.astype(f32), axis=1) for grad, weight in zip(attn_grads, (w_query, w_key, w_value))
-    ) / attn_gain
-    out_grad = sum(tn(middle_all[c], chunk_of(attended, c)) for c in chunks)
-    attn_grads = jnp.concatenate([grad.astype(bf16) for grad in attn_grads + [out_grad]], axis=1)
-    attn_done = dp_scatter(attn_grads).astype(f32)
-    query_done, key_done, value_done, out_done = (
-        attn_done[:, i * local_width : (i + 1) * local_width] for i in range(4)
+    moe_1 = down(gate(acts[1], dqn), w_down)
+    moe_sum_1 = scatter_rows(moe_1)
+    up_late = up_out.add()
+    up_out.send()
+    down_sums = expert_sums(grad_all, acts, mine, dqn, moe_1, *up_late, added=down_got)
+    down_out = halving(down_sums)
+    down_out.send()
+    normed_part, dqraw, dkraw, attn_gain_part = project_back(
+        normed_all, dqn, dkn, dvalue, qraw, kraw, q_scale, k_scale, dots[0][:, None], dots[1][:, None],
+        gate(q_gain, *down_sums), k_gain, w_query, w_key, w_value,
     )
-    tokens_grad = jnp.concatenate(middle_grads) + norm_back(normed_grad, inputs, first_scale, attn_gain)
+    halves = [ScatterChain(chunk_of(normed_part, c)) for c in chunks]
+    for _ in range(parts - 1):
+        for half in halves:
+            half.hop()
+    normed_grad = jnp.concatenate([half.total() for half in halves])
+
+    def attention_sums(ids, *others, added=None):
+        return attention_wgrad(
+            normed_all, middle_all, (dqraw, dkraw, dvalue), attended_parts, gate(ids, *others), dp_size, added
+        )
+
+    attn_sent = attention_sums(other_blocks, *(part for half in halves for part in half.first))
+    attn_got = pair_swap(attn_sent, 1)
 
     def placed(part):
         return lax.dynamic_update_slice_in_dim(jnp.zeros((features,), f32), part, part_at * local_width, 0)
 
-    early = exchange_sum(jnp.concatenate([router_part.T, ffn_gain_part[None]]), ("dp", "tensor"))
-    late = exchange_sum(jnp.stack([attn_gain_part, placed(q_gain_part[0]), placed(k_gain_part[0])]), ("dp", "tensor"))
+    smalls = [attn_gain_part[0] / attn_gain, placed(q_gain_part[0]), placed(k_gain_part[0]), sum(ffn_gain_parts)]
+    smalls = gate(jnp.concatenate([jnp.stack(smalls), sum(router_parts).T]), attn_sent)
+    smalls = exchange_sum(smalls, ("dp", "tensor"))
+    attn_out = Halving(attention_sums(own_blocks, attn_sent, added=attn_got))
+    attn_out.send()
+    gate_done = gate_out.done()
+    up_done = up_out.done()
+    down_done = down_out.done()
+    query_done, key_done, value_done, out_done = attn_out.done()
+    layer_out = jnp.concatenate([middles[0] + moe_sum_0.astype(f32), middles[1] + moe_sum_1.astype(f32)]).astype(bf16)
+    tokens_grad = jnp.concatenate(middle_grads) + norm_back(normed_grad, inputs, first_scale, attn_gain)
     return (
         layer_out, tokens_grad, query_done, key_done, value_done, out_done,
-        late[0], late[1], late[2], early[experts], early[:experts].T, gate_done, up_done, down_done,
+        smalls[0], smalls[1], smalls[2], smalls[3], smalls[4:].T, gate_done, up_done, down_done,
     )
 
 

time: 1420 us -> 1100 us (0.77)
  waiting for transfers between devices: 917 us -> 350 us
  starting transfers between devices: 10.5 us -> 188 us
  Pallas kernels: 271 us -> 349 us
  other arithmetic: 53.3 us -> 107 us
  matrix products: 57.1 us -> 16.4 us
  local copies, waits for them, and re-layouts: 82.7 us -> 65.3 us
    reduce_scatter x4 -> x0, waiting for transfers between devices: 340 us -> none  [dp_scatter(): return lax.psum_scatter(values, 'dp', scatter_dimension=0, tiled=True)]
    ppermute x0 -> x77, waiting for transfers between devices: none -> 305 us  [the longest x15 191 us: hop(): lax.ppermute(down, 'tensor', [(i, i - 1) for i in range(1, self.parts - s...]
    all_gather x7 -> x1, waiting for transfers between devices: 287 us -> 0.02 us  [gather_rows(): return lax.all_gather(values, 'tensor', axis=0, tiled=True)]
    unnamed x24 -> x6, waiting for transfers between devices: 248 us -> 0.1 us
    ppermute x0 -> x77, starting transfers between devices: none -> 154 us  [the longest x9 61.8 us: hop(): self.up = lax.ppermute(up, 'tensor', [(i, i + 1) for i in range(step + 1)])]
    pallas_call x3 -> x10, Pallas kernels: 75.1 us -> 153 us  [the longest x6 103 us: wgrad(): pl.pallas_call(functools.partial(wgrad_kernel, len(lefts), len(added), pe...]
    unnamed x158 -> x198, local copies, waits for them, and re-layouts: 46.8 us -> 10.9 us
    dynamic_update_slice x0 -> x19, other arithmetic: none -> 32.4 us  [the longest x15 27.6 us: joined(): lax.dynamic_update_slice_in_dim(whole, piece, lax.rem(at - step + parts,...]
  transfers between devices with their start and end apart: 32 -> 92, of which waited for: 25 -> 30; matrix products, arithmetic and copies ran while one was open for 10% -> 15% of each run, Pallas kernels for 7% -> 30%
where the time goes in v2:
time: 1100 us; the launch traced here: 1090 us
  waiting for transfers between devices  350 us (32%)
  Pallas kernels  349 us (32%)
  starting transfers between devices  188 us (17%)
  other arithmetic  107 us (10%)
  local copies, waits for them, and re-layouts  65.3 us (6%)
  matrix products  16.4 us (1%)
  between operations  16.3 us (1%)
    ppermute x15, waiting for transfers between devices, hop(): lax.ppermute(down, 'tensor', [(i, i - 1) for i in range(1, self.parts - s...  191 us
    pallas_call x6, Pallas kernels, wgrad(): pl.pallas_call(functools.partial(wgrad_kernel, len(lefts), len(added), pe...  103 us
    pallas_call x2, Pallas kernels, experts_block(): pl.pallas_call(functools.partial(expert_kernel, block), grid=(experts,),...  95.1 us
    ppermute x29, waiting for transfers between devices, pair_swap(): return lax.ppermute(values, 'dp', [(i, i ^ step) for i in range(size)])  90 us
    ppermute x9, starting transfers between devices, hop(): self.up = lax.ppermute(up, 'tensor', [(i, i + 1) for i in range(step + 1)])  61.8 us
    ppermute x9, waiting for transfers between devices, exchange_sum(): lax.ppermute(values, axis, [(i, i ^ step) for i in range(size)])  40.9 us
    ppermute x15, starting transfers between devices, hop(): lax.ppermute(up, 'tensor', [(i, i + 1) for i in range(step - 1, self.part...  38.6 us
    ppermute x9, starting transfers between devices, exchange_sum(): lax.ppermute(values, axis, [(i, i ^ step) for i in range(size)])  33.4 us
  transfers between devices with their start and end apart: 92, of which 30 were waited for; matrix products, arithmetic and copies ran while one was open for 15% of the time, Pallas kernels for 30%

profile of v2, /device:TPU:0, one launch (start us, length us, event | category | flops | bytes accessed | tf_op | source)
XLA Modules:
  0.0 1092.0 jit_solution(15685142118393039919)
XLA Ops:
  15.7 6.6 collective-permute-start
  22.2 20.2 %collective-permute-done.1 = bf16[256,2048]{1,0:T(8,128)(2,1)S(1)} collective-permute-done((bf16[256,2048]{1,0:T(8,128)(2,1)S(1)}, bf16[256,2048]{1,0:T(8,128)(2,1)S(1)}, u32[]{:S(2)}, u32[]{:S(2)}) %collective-permute-start.1) | collective-permute-done | bytes 1048608 | tf_op jit(solution)/shard_map/ppermute | solution.py:513
  46.4 23.4 %collective-permute-done.2 = bf16[256,2048]{1,0:T(8,128)(2,1)} collective-permute-done((bf16[256,2048]{1,0:T(8,128)(2,1)S(1)}, bf16[256,2048]{1,0:T(8,128)(2,1)}, u32[]{:S(2)}, u32[]{:S(2)}) %collective-permute-start.2) | collective-permute-done | bytes 1048608 | tf_op jit(solution)/shard_map/ppermute | solution.py:513
  71.3 6.5 convert_reduce_fusion
  78.6 16.8 %collective-permute-done.3 = bf16[256,2048]{1,0:T(8,128)(2,1)} collective-permute-done((bf16[256,2048]{1,0:T(8,128)(2,1)}, bf16[256,2048]{1,0:T(8,128)(2,1)}, u32[]{:S(2)}, u32[]{:S(2)}) %collective-permute-start.3) | collective-permute-done | bytes 1048608 | tf_op jit(solution)/shard_map/ppermute | solution.py:513
  98.3 3.0 add_dynamic-update-slice_fusion.4
  103.9 5.7 collective-permute-start.8
  109.6 16.3 %project.1 = (f32[1024,512]{1,0:T(8,128)}, f32[1024,512]{1,0:T(8,128)}, bf16[1024,512]{1,0:T(8,128)(2,1)}, f32[2,1024]{1,0:T(2,128)}) custom-call(bf16[1024,2048]{1,0:T(8,128)(2,1)} %add_dynamic-update-slice_fusion.3.rows_in.refs_0_, bf16[2048,512]{1,0:T(8,128)(2,1)} %w_query.3, bf16[2048,512]{1,0:T(8,128)(2,1)} %w_key.3, bf16[2048,512]{1,0:T(8,128)(2,1)} %w_value.3), custom_call_target="tpu_custom_call" | custom-call | flops 7730940928 | bytes 1310720 | tf_op jit(solution)/shard_map/project/pallas_call | solution.py:102
  138.2 15.6 %attend.1 = (bf16[1024,512]{1,0:T(8,128)(2,1)}, bf16[1024,512]{1,0:T(8,128)(2,1)}, bf16[1024,512]{1,0:T(8,128)(2,1)}, f32[1024,512]{1,0:T(8,128)}) custom-call(f32[1024,512]{1,0:T(8,128)} %get-tuple-element.102.qraw, f32[1024,512]{1,0:T(8,128)} %get-tuple-element.103.kraw, bf16[1024,512]{1,0:T(8,128)(2,1)} %get-tuple-element.104.value, ...), custom_call_target="tpu_custom_call" | custom-call | flops 152927682560 | bytes 1179648 | tf_op jit(solution)/shard_map/attend/pallas_call | solution.py:233
  164.8 56.5 %collective-permute-done.12 = bf16[256,2048]{1,0:T(8,128)(2,1)} collective-permute-done((bf16[256,2048]{1,0:T(8,128)(2,1)}, bf16[256,2048]{1,0:T(8,128)(2,1)}, u32[]{:S(2)}, u32[]{:S(2)}) %collective-permute-start.12) | collective-permute-done | bytes 1048608 | tf_op jit(solution)/shard_map/ppermute | solution.py:513
  230.1 20.5 %collective-permute-done.13 = bf16[256,2048]{1,0:T(8,128)(2,1)} collective-permute-done((bf16[256,2048]{1,0:T(8,128)(2,1)}, bf16[256,2048]{1,0:T(8,128)(2,1)}, u32[]{:S(2)}, u32[]{:S(2)}) %collective-permute-start.13) | collective-permute-done | bytes 1048608 | tf_op jit(solution)/shard_map/ppermute | solution.py:513
  250.6 2.9 add_dynamic-update-slice_fusion.2
  253.5 2.9 add_dynamic-update-slice_fusion.1
  259.1 4.9 fusion.40
  263.9 15.0 %up_back.3.back = bf16[512,4096]{1,0:T(8,128)(2,1)} custom-call(bf16[512,2048]{1,0:T(8,128)(2,1)} %bitcast.217, bf16[16,2048,256]{2,1,0:T(8,128)(2,1)} %down_w.7), custom_call_target="tpu_custom_call" | custom-call | flops 10307921920 | bytes 2359296 | tf_op jit(solution)/shard_map/up_back/pallas_call | solution.py:325
  284.3 5.4 collective-permute-start.10
  289.6 15.0 %up_back.2.back = bf16[512,4096]{1,0:T(8,128)(2,1)} custom-call(bf16[512,2048]{1,0:T(8,128)(2,1)} %bitcast.214, bf16[16,2048,256]{2,1,0:T(8,128)(2,1)} %down_w.7), custom_call_target="tpu_custom_call" | custom-call | flops 10307921920 | bytes 2359296 | tf_op jit(solution)/shard_map/up_back/pallas_call | solution.py:325
  310.0 27.9 %collective-permute-done.17 = bf16[128,2048]{1,0:T(8,128)(2,1)} collective-permute-done((bf16[128,2048]{1,0:T(8,128)(2,1)S(1)}, bf16[128,2048]{1,0:T(8,128)(2,1)}, u32[]{:S(2)}, u32[]{:S(2)}) %collective-permute-start.17) | collective-permute-done | bytes 524320 | tf_op jit(solution)/shard_map/ppermute | solution.py:513
  343.4 5.8 collective-permute-done.18
  354.5 47.6 %experts.2 = (bf16[512,4096]{1,0:T(8,128)(2,1)}, bf16[512,4096]{1,0:T(8,128)(2,1)}, bf16[512,4096]{1,0:T(8,128)(2,1)}, bf16[512,2176]{1,0:T(8,128)(2,1)}) custom-call(bf16[512,2048]{1,0:T(8,128)(2,1)} %add_dynamic-update-slice_fusion.12.rows_in.refs_0_, bf16[512,4096]{1,0:T(8,128)(2,1)} %up_back.2.back, f32[512,128]{1,0:T(8,128)} %bitcast.232, ...), custom_call_target="tpu_custom_call" | custom-call | flops 141894975488 | bytes 6291456 | tf_op jit(solution)/shard_map/experts/pallas_call | solution.py:390
  402.6 47.5 %experts.3 = (bf16[512,4096]{1,0:T(8,128)(2,1)}, bf16[512,4096]{1,0:T(8,128)(2,1)}, bf16[512,4096]{1,0:T(8,128)(2,1)}, bf16[512,2176]{1,0:T(8,128)(2,1)}) custom-call(bf16[512,2048]{1,0:T(8,128)(2,1)} %all-gather.2.cloned.1.call-done.rows_in.refs_1_, bf16[512,4096]{1,0:T(8,128)(2,1)} %up_back.3.back, f32[512,128]{1,0:T(8,128)} %bitcast.231, ...), custom_call_target="tpu_custom_call" | custom-call | flops 141894975488 | bytes 6291456 | tf_op jit(solution)/shard_map/experts/pallas_call | solution.py:390
  456.4 3.6 reduce-scatter.10.cloned.1.call-done
  467.0 5.3 collective-permute-start.24
  472.3 16.8 %wgrad.6 = (bf16[2,2048,256]{2,1,0:T(8,128)(2,1)}, bf16[2,2048,256]{2,1,0:T(8,128)(2,1)}, bf16[2,2048,256]{2,1,0:T(8,128)(2,1)}, bf16[2,2048,256]{2,1,0:T(8,128)(2,1)}) custom-call(s32[8]{0:T(128)} %add.503.order, bf16[512,2048]{1,0:T(8,128)(2,1)} %add_dynamic-update-slice_fusion.12.rows_in.refs_0_, ...), custom_call_target="tpu_custom_call" | custom-call | flops 10307921920 | bytes 2621440 | tf_op jit(solution)/shard_map/wgrad/pallas_call | solution.py:451
  498.1 16.7 %wgrad.7 = (bf16[2,2048,256]{2,1,0:T(8,128)(2,1)}, bf16[2,2048,256]{2,1,0:T(8,128)(2,1)}, bf16[2,2048,256]{2,1,0:T(8,128)(2,1)}, bf16[2,2048,256]{2,1,0:T(8,128)(2,1)}) custom-call(s32[8]{0:T(128)} %add.503.order, bf16[512,2048]{1,0:T(8,128)(2,1)} %add_dynamic-update-slice_fusion.12.rows_in.refs_0_, ...), custom_call_target="tpu_custom_call" | custom-call | flops 10307921920 | bytes 2621440 | tf_op jit(solution)/shard_map/wgrad/pallas_call | solution.py:451
  518.9 16.4 %collective-permute-start.26 = (bf16[128,2176]{1,0:T(8,128)(2,1)}, bf16[128,2176]{1,0:T(8,128)(2,1)S(1)}, u32[]{:S(2)}, u32[]{:S(2)}) collective-permute-start(bf16[128,2176]{1,0:T(8,128)(2,1)} %get-tuple-element.222), channel_id=1, source_target_pairs={{0,1},{1,2},{2,3},{4,5},{5,6},{6,7},{8,9},{9,10},{10,11},{12,13},{... | collective-permute-start | bytes 1671176 | tf_op jit(solution)/shard_map/ppermute | solution.py:557
  537.6 16.5 %wgrad.8 = (bf16[2,2048,256]{2,1,0:T(8,128)(2,1)}, bf16[2,2048,256]{2,1,0:T(8,128)(2,1)}, bf16[2,2048,256]{2,1,0:T(8,128)(2,1)}, bf16[2,2048,256]{2,1,0:T(8,128)(2,1)}) custom-call(s32[8]{0:T(128)} %add.503.order, bf16[512,2048]{1,0:T(8,128)(2,1)} %bitcast.215, bf16[512,2048]{1,0:T(8,128)(2,1)} %bitcast.218, ...), custom_call_target="tpu_custom_call" | custom-call | flops 10307921920 | bytes 2621440 | tf_op jit(solution)/shard_map/wgrad/pallas_call | solution.py:451
  562.0 8.2 collective-permute-done.33
  572.8 11.1 %collective-permute-done.31 = bf16[128,2048]{1,0:T(8,128)(2,1)S(1)} collective-permute-done((bf16[128,2048]{1,0:T(8,128)(2,1)S(1)}, bf16[128,2048]{1,0:T(8,128)(2,1)S(1)}, u32[]{:S(2)}, u32[]{:S(2)}) %collective-permute-start.31) | collective-permute-done | bytes 524320 | tf_op jit(solution)/shard_map/ppermute | solution.py:513
  588.6 6.3 collective-permute-start.30
  594.8 17.5 %wgrad.9 = (bf16[8,1024,256]{2,1,0:T(8,128)(2,1)}, bf16[8,1024,256]{2,1,0:T(8,128)(2,1)}) custom-call(s32[8]{0:T(128)} %add.523.order, bf16[512,2048]{1,0:T(8,128)(2,1)} %add_dynamic-update-slice_fusion.12.rows_in.refs_0_, bf16[512,2048]{1,0:T(8,128)(2,1)} %all-gather.2.cloned.1.call-done.rows_in.refs_1_, bf16[512,4096]{1,0:T(8,128)(2,1)} %get-tuple-element.125.refs_2_, ...), custom_call_target="tpu_custom_call" | custom-call | flops 10307921920 | bytes 2621440 | tf_op jit(solution)/shard_map/wgrad/pallas_call | solution.py:451
  612.4 3.2 slice_bitcast_fusion.5
  621.5 17.5 %wgrad.10 = (bf16[8,1024,256]{2,1,0:T(8,128)(2,1)}, bf16[8,1024,256]{2,1,0:T(8,128)(2,1)}) custom-call(s32[8]{0:T(128)} %add.523.order, bf16[512,2048]{1,0:T(8,128)(2,1)} %add_dynamic-update-slice_fusion.12.rows_in.refs_0_, bf16[512,2048]{1,0:T(8,128)(2,1)} %all-gather.2.cloned.1.call-done.rows_in.refs_1_, bf16[512,4096]{1,0:T(8,128)(2,1)} %get-tuple-element.135.refs_2_, ...), custom_call_target="tpu_custom_call" | custom-call | flops 10307921920 | bytes 2621440 | tf_op jit(solution)/shard_map/wgrad/pallas_call | solution.py:451
  639.0 4.6 fusion.38
  648.8 15.4 %down.2 = bf16[512,2048]{1,0:T(8,128)(2,1)} custom-call(bf16[512,4096]{1,0:T(8,128)(2,1)} %get-tuple-element.160.refs_2_.act, bf16[16,2048,256]{2,1,0:T(8,128)(2,1)} %down_w.7), custom_call_target="tpu_custom_call" | custom-call | flops 10307921920 | bytes 2359296 | tf_op jit(solution)/shard_map/down/pallas_call | solution.py:477
  670.7 3.2 convolution_convert_fusion.2
  675.3 3.5 fusion.4
  678.9 13.9 %collective-permute-done.46 = bf16[2,2,1024,256]{3,2,1,0:T(8,128)(2,1)} collective-permute-done((bf16[2,2,1024,256]{3,2,1,0:T(8,128)(2,1)}, bf16[2,2,1024,256]{3,2,1,0:T(8,128)(2,1)}, u32[]{:S(2)}, u32[]{:S(2)}) %collective-permute-start.46) | collective-permute-done | bytes 2097184 | tf_op jit(solution)/shard_map/ppermute | solution.py:570
  692.8 3.4 fusion.5
  697.3 23.9 %attend_back.1 = (f32[1024,512]{1,0:T(8,128)}, f32[1024,512]{1,0:T(8,128)}, bf16[1024,512]{1,0:T(8,128)(2,1)}, f32[1024,1]{1,0:T(8,128)}, f32[1024,1]{1,0:T(8,128)}, /*index=5*/f32[1,512]{1,0:T(1,128)}, f32[1,512]{1,0:T(1,128)}) custom-call(bf16[1024,512]{1,0:T(8,128)(2,1)} %get-tuple-element.161.query, bf16[1024,512]{1,0:T(8,128)(2,1)} %get-tuple-element.162.key, ...), custom_call_target="tpu_custom_call" | custom-call | flops 155826782208 | bytes 2097152 | tf_op jit(solution)/shard_map/attend_back/pallas_call | solution.py:299
  723.7 3.7 collective-permute-start.48
  729.0 23.4 %collective-permute-start.49 = (f32[2,1024]{1,0:T(2,128)S(1)}, f32[2,1024]{1,0:T(2,128)S(1)}, u32[]{:S(2)}, u32[]{:S(2)}) collective-permute-start(f32[2,1024]{1,0:T(2,128)S(1)} %fusion.34), channel_id=1, source_target_pairs={{0,2},{1,3},{2,0},{3,1},{4,6},{5,7},{6,4},{7,5},{8,10},{9,11},{10,... | collective-permute-start | bytes 24584 | tf_op jit(solution)/shard_map/ppermute | solution.py:621
  754.9 15.3 %down.3 = bf16[512,2048]{1,0:T(8,128)(2,1)} custom-call(bf16[512,4096]{1,0:T(8,128)(2,1)} %get-tuple-element.166.refs_3_.act, bf16[16,2048,256]{2,1,0:T(8,128)(2,1)} %down_w.7), custom_call_target="tpu_custom_call" | custom-call | flops 10307921920 | bytes 2359296 | tf_op jit(solution)/shard_map/down/pallas_call | solution.py:477
  772.4 4.1 fusion.2
  776.5 3.4 fusion.3
  779.9 17.7 %wgrad.11 = (bf16[8,1024,256]{2,1,0:T(8,128)(2,1)}, bf16[8,1024,256]{2,1,0:T(8,128)(2,1)}) custom-call(s32[8]{0:T(128)} %add.523.order, bf16[512,2048]{1,0:T(8,128)(2,1)} %bitcast.216, bf16[512,2048]{1,0:T(8,128)(2,1)} %bitcast.219, bf16[512,4096]{1,0:T(8,128)(2,1)} %get-tuple-element.160.refs_2_.act, bf16[512,4096]{1,0:T(8,128)(2,1)} %get-tuple-element.166.refs_3_.act, ...), custom_call_target="tpu_custom_call" | custom-call | flops 10307921920 | bytes 2621440 | tf_op jit(solution)/shard_map/wgrad/pallas_call | solution.py:451
  797.7 13.8 %project_back.1 = (bf16[1024,2048]{1,0:T(8,128)(2,1)}, bf16[1024,512]{1,0:T(8,128)(2,1)}, bf16[1024,512]{1,0:T(8,128)(2,1)}, f32[1,2048]{1,0:T(1,128)}) custom-call(bf16[1024,2048]{1,0:T(8,128)(2,1)} %add_dynamic-update-slice_fusion.3.rows_in.refs_0_, f32[1024,512]{1,0:T(8,128)} %get-tuple-element.165.dqn, f32[1024,512]{1,0:T(8,128)} %get-tuple-element.167.dkn, ...), custom_call_target="tpu_custom_call" | custom-call | flops 7730940928 | bytes 1310720 | tf_op jit(solution)/shard_map/project_back/pallas_call | solution.py:142
  817.8 10.0 attention_wgrad.2
  830.8 4.0 collective-permute-start.62
  844.4 14.6 %collective-permute-done.75 = f32[20,2048]{1,0:T(8,128)S(1)} collective-permute-done((f32[20,2048]{1,0:T(8,128)S(1)}, f32[20,2048]{1,0:T(8,128)S(1)}, u32[]{:S(2)}, u32[]{:S(2)}) %collective-permute-start.75) | collective-permute-done | bytes 163872 | tf_op jit(solution)/shard_map/ppermute | solution.py:621
  864.1 14.2 %collective-permute-done.56 = bf16[128,2048]{1,0:T(8,128)(2,1)S(1)} collective-permute-done((bf16[128,2048]{1,0:T(8,128)(2,1)}, bf16[128,2048]{1,0:T(8,128)(2,1)S(1)}, u32[]{:S(2)}, u32[]{:S(2)}) %collective-permute-start.56) | collective-permute-done | bytes 524320 | tf_op jit(solution)/shard_map/ppermute | solution.py:557
  885.4 12.1 %collective-permute-start.58 = (bf16[128,2048]{1,0:T(8,128)(2,1)S(1)}, bf16[128,2048]{1,0:T(8,128)(2,1)S(1)}, u32[]{:S(2)}, u32[]{:S(2)}) collective-permute-start(bf16[128,2048]{1,0:T(8,128)(2,1)S(1)} %get-tuple-element.234), channel_id=1, source_target_pairs={{0,1},{1,2},{4,5},{5,6},{8,9},{9,10},{12,13},{13,14},{16,17},{17,1... | collective-permute-start | bytes 1572872 | tf_op jit(solution)/shard_map/ppermute | solution.py:557
  901.6 20.7 %collective-permute-done.77 = f32[20,2048]{1,0:T(8,128)S(1)} collective-permute-done((f32[20,2048]{1,0:T(8,128)S(1)}, f32[20,2048]{1,0:T(8,128)S(1)}, u32[]{:S(2)}, u32[]{:S(2)}) %collective-permute-start.77) | collective-permute-done | bytes 163872 | tf_op jit(solution)/shard_map/ppermute | solution.py:621
  927.0 15.6 %collective-permute-start.66 = (bf16[128,2048]{1,0:T(8,128)(2,1)S(1)}, bf16[128,2048]{1,0:T(8,128)(2,1)S(1)}, u32[]{:S(2)}, u32[]{:S(2)}) collective-permute-start(bf16[128,2048]{1,0:T(8,128)(2,1)S(1)} %get-tuple-element.238), channel_id=1, source_target_pairs={{0,1},{1,2},{2,3},{4,5},{5,6},{6,7},{8,9},{9,10},{10,11},{12,13},{... | collective-permute-start | bytes 1572872 | tf_op jit(solution)/shard_map/ppermute | solution.py:557
  944.5 5.9 collective-permute-done.80
  950.5 5.9 collective-permute-start.60
  961.9 5.2 collective-permute-done.60
  967.0 5.3 collective-permute-done.61
  972.9 22.2 %collective-permute-done.84 = bf16[2,2,1024,256]{3,2,1,0:T(8,128)(2,1)S(1)} collective-permute-done((bf16[2,2,1024,256]{3,2,1,0:T(8,128)(2,1)S(1)}, bf16[2,2,1024,256]{3,2,1,0:T(8,128)(2,1)S(1)}, u32[]{:S(2)}, u32[]{:S(2)}) %collective-permute-start.84) | collective-permute-done | bytes 2097184 | tf_op jit(solution)/shard_map/ppermute | solution.py:570
  997.1 11.7 %collective-permute-done.82 = bf16[2,2,1024,256]{3,2,1,0:T(8,128)(2,1)S(1)} collective-permute-done((bf16[2,2,1024,256]{3,2,1,0:T(8,128)(2,1)S(1)}, bf16[2,2,1024,256]{3,2,1,0:T(8,128)(2,1)S(1)}, u32[]{:S(2)}, u32[]{:S(2)}) %collective-permute-start.82) | collective-permute-done | bytes 2097184 | tf_op jit(solution)/shard_map/ppermute | solution.py:570
  1016.4 13.0 %collective-permute-done.85 = bf16[1,2,1024,256]{3,2,1,0:T(8,128)(2,1)} collective-permute-done((bf16[1,2,1024,256]{3,2,1,0:T(8,128)(2,1)}, bf16[1,2,1024,256]{3,2,1,0:T(8,128)(2,1)}, u32[]{:S(2)}, u32[]{:S(2)}) %collective-permute-start.85) | collective-permute-done | bytes 1048608 | tf_op jit(solution)/shard_map/ppermute | solution.py:570
  1033.5 10.5 attention_wgrad.3
  1054.0 14.9 %collective-permute-done.69 = bf16[2,4,128,512]{3,2,1,0:T(8,128)(2,1)} collective-permute-done((bf16[2,4,128,512]{3,2,1,0:T(8,128)(2,1)}, bf16[2,4,128,512]{3,2,1,0:T(8,128)(2,1)}, u32[]{:S(2)}, u32[]{:S(2)}) %collective-permute-start.69) | collective-permute-done | bytes 1048608 | tf_op jit(solution)/shard_map/ppermute | solution.py:570
  1076.1 5.8 collective-permute-done.70
  (492 shorter events, 229.6 us)
Async XLA Ops:
  7.2 271.7 %reduce-scatter.6.cloned.1.call-start = ((), (), s32[]{:S(2)}) async-start(), calls=%async_computation.5 | async-start | bytes 2621440 | tf_op jit(solution)/shard_map/reduce_scatter | solution.py:498
  14.4 28.1 %collective-permute-start.1 = (bf16[256,2048]{1,0:T(8,128)(2,1)S(1)}, bf16[256,2048]{1,0:T(8,128)(2,1)S(1)}, u32[]{:S(2)}, u32[]{:S(2)}) collective-permute-start(bf16[256,2048]{1,0:T(8,128)(2,1)S(1)} %get-tuple-element.211), channel_id=1, source_target_pairs={{1,0},{2,1},{3,2},{5,4},{6,5},{7,6},{9,8},{10,9},{11,10},{13,12},{... | collective-permute-start | bytes 3145736 | tf_op jit(solution)/shard_map/ppermute | solution.py:513
  15.7 29.0 %collective-permute-start = (bf16[256,2048]{1,0:T(8,128)(2,1)S(1)}, bf16[256,2048]{1,0:T(8,128)(2,1)}, u32[]{:S(2)}, u32[]{:S(2)}) collective-permute-start(bf16[256,2048]{1,0:T(8,128)(2,1)S(1)} %get-tuple-element.211), channel_id=1, source_target_pairs={{0,1},{1,2},{2,3},{4,5},{5,6},{6,7},{8,9},{9,10},{10,11},{12,13},{... | collective-permute-start | bytes 3145736 | tf_op jit(solution)/shard_map/ppermute | solution.py:512
  43.4 26.3 %collective-permute-start.2 = (bf16[256,2048]{1,0:T(8,128)(2,1)S(1)}, bf16[256,2048]{1,0:T(8,128)(2,1)}, u32[]{:S(2)}, u32[]{:S(2)}) collective-permute-start(bf16[256,2048]{1,0:T(8,128)(2,1)S(1)} %collective-permute-done.1), channel_id=1, source_target_pairs={{1,0},{2,1},{5,4},{6,5},{9,8},{10,9},{13,12},{14,13},{17,16},{18,1... | collective-permute-start | bytes 3145736 | tf_op jit(solution)/shard_map/ppermute | solution.py:513
  44.7 33.1 %collective-permute-start.4 = (bf16[256,2048]{1,0:T(8,128)(2,1)}, bf16[256,2048]{1,0:T(8,128)(2,1)}, u32[]{:S(2)}, u32[]{:S(2)}) collective-permute-start(bf16[256,2048]{1,0:T(8,128)(2,1)} %collective-permute-done), channel_id=1, source_target_pairs={{1,2},{2,3},{5,6},{6,7},{9,10},{10,11},{13,14},{14,15},{17,18},{18... | collective-permute-start | bytes 3145736 | tf_op jit(solution)/shard_map/ppermute | solution.py:512
  69.7 25.6 %collective-permute-start.3 = (bf16[256,2048]{1,0:T(8,128)(2,1)}, bf16[256,2048]{1,0:T(8,128)(2,1)}, u32[]{:S(2)}, u32[]{:S(2)}) collective-permute-start(bf16[256,2048]{1,0:T(8,128)(2,1)} %collective-permute-done.2), channel_id=1, source_target_pairs={{1,0},{5,4},{9,8},{13,12},{17,16},{21,20},{25,24},{29,28}} | collective-permute-start | bytes 3145736 | tf_op jit(solution)/shard_map/ppermute | solution.py:513
  77.8 23.4 %collective-permute-start.5 = (bf16[256,2048]{1,0:T(8,128)(2,1)}, bf16[256,2048]{1,0:T(8,128)(2,1)S(1)}, u32[]{:S(2)}, u32[]{:S(2)}) collective-permute-start(bf16[256,2048]{1,0:T(8,128)(2,1)} %collective-permute-done.4), channel_id=1, source_target_pairs={{2,3},{6,7},{10,11},{14,15},{18,19},{22,23},{26,27},{30,31}} | collective-permute-start | bytes 3145736 | tf_op jit(solution)/shard_map/ppermute | solution.py:512
  102.7 34.5 %collective-permute-start.9 = (bf16[256,2048]{1,0:T(8,128)(2,1)S(1)}, bf16[256,2048]{1,0:T(8,128)(2,1)}, u32[]{:S(2)}, u32[]{:S(2)}) collective-permute-start(bf16[256,2048]{1,0:T(8,128)(2,1)S(1)} %copy-done.28), channel_id=1, source_target_pairs={{1,0},{2,1},{3,2},{5,4},{6,5},{7,6},{9,8},{10,9},{11,10},{13,12},{... | collective-permute-start | bytes 3145736 | tf_op jit(solution)/shard_map/ppermute | solution.py:513
  103.9 33.2 %collective-permute-start.8 = (bf16[256,2048]{1,0:T(8,128)(2,1)S(1)}, bf16[256,2048]{1,0:T(8,128)(2,1)}, u32[]{:S(2)}, u32[]{:S(2)}) collective-permute-start(bf16[256,2048]{1,0:T(8,128)(2,1)S(1)} %copy-done.28), channel_id=1, source_target_pairs={{0,1},{1,2},{2,3},{4,5},{5,6},{6,7},{8,9},{9,10},{10,11},{12,13},{... | collective-permute-start | bytes 3145736 | tf_op jit(solution)/shard_map/ppermute | solution.py:512
  158.6 149.2 %reduce-scatter.8.cloned.1.call-start = ((), (), s32[]{:S(2)}) async-start(), calls=%async_computation.6 | async-start | bytes 2621440 | tf_op jit(solution)/shard_map/reduce_scatter | solution.py:498
  161.3 60.1 %collective-permute-start.12 = (bf16[256,2048]{1,0:T(8,128)(2,1)}, bf16[256,2048]{1,0:T(8,128)(2,1)}, u32[]{:S(2)}, u32[]{:S(2)}) collective-permute-start(bf16[256,2048]{1,0:T(8,128)(2,1)} %collective-permute-done.9), channel_id=1, source_target_pairs={{1,0},{2,1},{5,4},{6,5},{9,8},{10,9},{13,12},{14,13},{17,16},{18,1... | collective-permute-start | bytes 3145736 | tf_op jit(solution)/shard_map/ppermute | solution.py:513
  163.2 66.0 %collective-permute-start.14 = (bf16[256,2048]{1,0:T(8,128)(2,1)}, bf16[256,2048]{1,0:T(8,128)(2,1)}, u32[]{:S(2)}, u32[]{:S(2)}) collective-permute-start(bf16[256,2048]{1,0:T(8,128)(2,1)} %collective-permute-done.8), channel_id=1, source_target_pairs={{1,2},{2,3},{5,6},{6,7},{9,10},{10,11},{13,14},{14,15},{17,18},{18... | collective-permute-start | bytes 3145736 | tf_op jit(solution)/shard_map/ppermute | solution.py:512
  221.3 29.3 %collective-permute-start.13 = (bf16[256,2048]{1,0:T(8,128)(2,1)}, bf16[256,2048]{1,0:T(8,128)(2,1)}, u32[]{:S(2)}, u32[]{:S(2)}) collective-permute-start(bf16[256,2048]{1,0:T(8,128)(2,1)} %collective-permute-done.12), channel_id=1, source_target_pairs={{1,0},{5,4},{9,8},{13,12},{17,16},{21,20},{25,24},{29,28}} | collective-permute-start | bytes 3145736 | tf_op jit(solution)/shard_map/ppermute | solution.py:513
  229.1 173.5 %all-gather.2.cloned.1.call-start = ((), (), s32[]{:S(2)}) async-start(), calls=%async_computation.7 | async-start | bytes 2621440 | tf_op jit(solution)/shard_map/all_gather | solution.py:494
  229.2 27.3 %collective-permute-start.15 = (bf16[256,2048]{1,0:T(8,128)(2,1)}, bf16[256,2048]{1,0:T(8,128)(2,1)S(1)}, u32[]{:S(2)}, u32[]{:S(2)}) collective-permute-start(bf16[256,2048]{1,0:T(8,128)(2,1)} %collective-permute-done.14), channel_id=1, source_target_pairs={{2,3},{6,7},{10,11},{14,15},{18,19},{22,23},{26,27},{30,31}} | collective-permute-start | bytes 3145736 | tf_op jit(solution)/shard_map/ppermute | solution.py:512
  283.0 22.1 %collective-permute-start.11 = (bf16[128,2048]{1,0:T(8,128)(2,1)S(1)}, bf16[128,2048]{1,0:T(8,128)(2,1)S(1)}, u32[]{:S(2)}, u32[]{:S(2)}) collective-permute-start(bf16[128,2048]{1,0:T(8,128)(2,1)S(1)} %get-tuple-element.205), channel_id=1, source_target_pairs={{1,0},{2,1},{3,2},{5,4},{6,5},{7,6},{9,8},{10,9},{11,10},{13,12},{... | collective-permute-start | bytes 1572872 | tf_op jit(solution)/shard_map/ppermute | solution.py:513
  305.8 32.1 %collective-permute-start.17 = (bf16[128,2048]{1,0:T(8,128)(2,1)S(1)}, bf16[128,2048]{1,0:T(8,128)(2,1)}, u32[]{:S(2)}, u32[]{:S(2)}) collective-permute-start(bf16[128,2048]{1,0:T(8,128)(2,1)S(1)} %collective-permute-done.11), channel_id=1, source_target_pairs={{1,0},{2,1},{5,4},{6,5},{9,8},{10,9},{13,12},{14,13},{17,16},{18,1... | collective-permute-start | bytes 1572872 | tf_op jit(solution)/shard_map/ppermute | solution.py:513
  340.1 119.9 %reduce-scatter.10.cloned.1.call-start = ((), (), s32[]{:S(2)}) async-start(), calls=%async_computation.8 | async-start | bytes 2785280 | tf_op jit(solution)/shard_map/reduce_scatter | solution.py:498
  402.1 612.2 %reduce-scatter.12.cloned.1.call-start = ((), (), s32[]{:S(2)}) async-start(), calls=%async_computation.9 | async-start | bytes 2621440 | tf_op jit(solution)/shard_map/reduce_scatter | solution.py:498
  452.6 37.7 %collective-permute-start.20 = (bf16[128,2176]{1,0:T(8,128)(2,1)}, bf16[128,2176]{1,0:T(8,128)(2,1)}, u32[]{:S(2)}, u32[]{:S(2)}) collective-permute-start(bf16[128,2176]{1,0:T(8,128)(2,1)} %get-tuple-element.226), channel_id=1, source_target_pairs={{0,1},{4,5},{8,9},{12,13},{16,17},{20,21},{24,25},{28,29}} | collective-permute-start | bytes 1671176 | tf_op jit(solution)/shard_map/ppermute | solution.py:557
  454.9 36.0 %collective-permute-start.21 = (bf16[128,2176]{1,0:T(8,128)(2,1)}, bf16[128,2176]{1,0:T(8,128)(2,1)}, u32[]{:S(2)}, u32[]{:S(2)}) collective-permute-start(bf16[128,2176]{1,0:T(8,128)(2,1)} %get-tuple-element.227), channel_id=1, source_target_pairs={{3,2},{7,6},{11,10},{15,14},{19,18},{23,22},{27,26},{31,30}} | collective-permute-start | bytes 1671176 | tf_op jit(solution)/shard_map/ppermute | solution.py:558
  465.7 27.6 %collective-permute-start.25 = (bf16[128,2048]{1,0:T(8,128)(2,1)}, bf16[128,2048]{1,0:T(8,128)(2,1)S(1)}, u32[]{:S(2)}, u32[]{:S(2)}) collective-permute-start(bf16[128,2048]{1,0:T(8,128)(2,1)} %get-tuple-element.195), channel_id=1, source_target_pairs={{1,0},{2,1},{3,2},{5,4},{6,5},{7,6},{9,8},{10,9},{11,10},{13,12},{... | collective-permute-start | bytes 1572872 | tf_op jit(solution)/shard_map/ppermute | solution.py:513
  467.0 29.4 %collective-permute-start.24 = (bf16[128,2048]{1,0:T(8,128)(2,1)}, bf16[128,2048]{1,0:T(8,128)(2,1)}, u32[]{:S(2)}, u32[]{:S(2)}) collective-permute-start(bf16[128,2048]{1,0:T(8,128)(2,1)} %get-tuple-element.195), channel_id=1, source_target_pairs={{0,1},{1,2},{2,3},{4,5},{5,6},{6,7},{8,9},{9,10},{10,11},{12,13},{... | collective-permute-start | bytes 1572872 | tf_op jit(solution)/shard_map/ppermute | solution.py:512
  489.1 94.8 %collective-permute-start.34 = (bf16[2,2048,256]{2,1,0:T(8,128)(2,1)}, bf16[2,2048,256]{2,1,0:T(8,128)(2,1)}, u32[]{:S(2)}, u32[]{:S(2)}) collective-permute-start(bf16[2,2048,256]{2,1,0:T(8,128)(2,1)} %get-tuple-element.127), channel_id=1, source_target_pairs={{0,4},{4,0},{8,12},{12,8},{16,20},{20,16},{24,28},{28,24},{1,5},{5... | collective-permute-start | bytes 6291464 | tf_op jit(solution)/shard_map/ppermute | solution.py:570
  490.3 94.2 %collective-permute-start.35 = (bf16[2,2048,256]{2,1,0:T(8,128)(2,1)}, bf16[2,2048,256]{2,1,0:T(8,128)(2,1)}, u32[]{:S(2)}, u32[]{:S(2)}) collective-permute-start(bf16[2,2048,256]{2,1,0:T(8,128)(2,1)} %get-tuple-element.128), channel_id=1, source_target_pairs={{0,4},{4,0},{8,12},{12,8},{16,20},{20,16},{24,28},{28,24},{1,5},{5... | collective-permute-start | bytes 6291464 | tf_op jit(solution)/shard_map/ppermute | solution.py:570
  490.9 93.7 %collective-permute-start.36 = (bf16[2,2048,256]{2,1,0:T(8,128)(2,1)}, bf16[2,2048,256]{2,1,0:T(8,128)(2,1)}, u32[]{:S(2)}, u32[]{:S(2)}) collective-permute-start(bf16[2,2048,256]{2,1,0:T(8,128)(2,1)} %get-tuple-element.129), channel_id=1, source_target_pairs={{0,4},{4,0},{8,12},{12,8},{16,20},{20,16},{24,28},{28,24},{1,5},{5... | collective-permute-start | bytes 6291464 | tf_op jit(solution)/shard_map/ppermute | solution.py:570
  518.9 35.3 %collective-permute-start.26 = (bf16[128,2176]{1,0:T(8,128)(2,1)}, bf16[128,2176]{1,0:T(8,128)(2,1)S(1)}, u32[]{:S(2)}, u32[]{:S(2)}) collective-permute-start(bf16[128,2176]{1,0:T(8,128)(2,1)} %get-tuple-element.222), channel_id=1, source_target_pairs={{0,1},{1,2},{2,3},{4,5},{5,6},{6,7},{8,9},{9,10},{10,11},{12,13},{... | collective-permute-start | bytes 1671176 | tf_op jit(solution)/shard_map/ppermute | solution.py:557
  561.0 26.3 %collective-permute-start.37 = (bf16[2,2048,256]{2,1,0:T(8,128)(2,1)S(1)}, bf16[2,2048,256]{2,1,0:T(8,128)(2,1)S(1)}, u32[]{:S(2)}, u32[]{:S(2)}) collective-permute-start(bf16[2,2048,256]{2,1,0:T(8,128)(2,1)S(1)} %copy-done.96), channel_id=1, source_target_pairs={{0,4},{4,0},{8,12},{12,8},{16,20},{20,16},{24,28},{28,24},{1,5},{5... | collective-permute-start | bytes 6291464 | tf_op jit(solution)/shard_map/ppermute | solution.py:570
  584.0 33.9 %collective-permute-start.40 = (bf16[2,2048,256]{2,1,0:T(8,128)(2,1)}, bf16[2,2048,256]{2,1,0:T(8,128)(2,1)}, u32[]{:S(2)}, u32[]{:S(2)}) collective-permute-start(bf16[2,2048,256]{2,1,0:T(8,128)(2,1)} %get-tuple-element.137), channel_id=1, source_target_pairs={{0,4},{4,0},{8,12},{12,8},{16,20},{20,16},{24,28},{28,24},{1,5},{5... | collective-permute-start | bytes 6291464 | tf_op jit(solution)/shard_map/ppermute | solution.py:570
  584.0 34.3 %collective-permute-start.41 = (bf16[2,2048,256]{2,1,0:T(8,128)(2,1)}, bf16[2,2048,256]{2,1,0:T(8,128)(2,1)}, u32[]{:S(2)}, u32[]{:S(2)}) collective-permute-start(bf16[2,2048,256]{2,1,0:T(8,128)(2,1)} %get-tuple-element.138), channel_id=1, source_target_pairs={{0,4},{4,0},{8,12},{12,8},{16,20},{20,16},{24,28},{28,24},{1,5},{5... | collective-permute-start | bytes 6291464 | tf_op jit(solution)/shard_map/ppermute | solution.py:570
  584.5 34.5 %collective-permute-start.42 = (bf16[2,2048,256]{2,1,0:T(8,128)(2,1)}, bf16[2,2048,256]{2,1,0:T(8,128)(2,1)}, u32[]{:S(2)}, u32[]{:S(2)}) collective-permute-start(bf16[2,2048,256]{2,1,0:T(8,128)(2,1)} %get-tuple-element.139), channel_id=1, source_target_pairs={{0,4},{4,0},{8,12},{12,8},{16,20},{20,16},{24,28},{28,24},{1,5},{5... | collective-permute-start | bytes 6291464 | tf_op jit(solution)/shard_map/ppermute | solution.py:570
  584.6 36.2 %collective-permute-start.43 = (bf16[2,2048,256]{2,1,0:T(8,128)(2,1)}, bf16[2,2048,256]{2,1,0:T(8,128)(2,1)}, u32[]{:S(2)}, u32[]{:S(2)}) collective-permute-start(bf16[2,2048,256]{2,1,0:T(8,128)(2,1)} %get-tuple-element.140), channel_id=1, source_target_pairs={{0,4},{4,0},{8,12},{12,8},{16,20},{20,16},{24,28},{28,24},{1,5},{5... | collective-permute-start | bytes 6291464 | tf_op jit(solution)/shard_map/ppermute | solution.py:570
  588.6 23.8 %collective-permute-start.30 = (bf16[128,2048]{1,0:T(8,128)(2,1)S(1)}, bf16[128,2048]{1,0:T(8,128)(2,1)S(1)}, u32[]{:S(2)}, u32[]{:S(2)}) collective-permute-start(bf16[128,2048]{1,0:T(8,128)(2,1)S(1)} %get-tuple-element.200), channel_id=1, source_target_pairs={{0,1},{1,2},{2,3},{4,5},{5,6},{6,7},{8,9},{9,10},{10,11},{12,13},{... | collective-permute-start | bytes 1572872 | tf_op jit(solution)/shard_map/ppermute | solution.py:512
  612.3 167.6 %collective-permute-start.52 = (bf16[2,2048,256]{2,1,0:T(8,128)(2,1)}, bf16[2,2048,256]{2,1,0:T(8,128)(2,1)}, u32[]{:S(2)}, u32[]{:S(2)}) collective-permute-start(bf16[2,2048,256]{2,1,0:T(8,128)(2,1)} %get-tuple-element.145), channel_id=1, source_target_pairs={{0,4},{4,0},{8,12},{12,8},{16,20},{20,16},{24,28},{28,24},{1,5},{5... | collective-permute-start | bytes 6291464 | tf_op jit(solution)/shard_map/ppermute | solution.py:570
  617.8 162.1 %collective-permute-start.53 = (bf16[2,2048,256]{2,1,0:T(8,128)(2,1)}, bf16[2,2048,256]{2,1,0:T(8,128)(2,1)}, u32[]{:S(2)}, u32[]{:S(2)}) collective-permute-start(bf16[2,2048,256]{2,1,0:T(8,128)(2,1)} %get-tuple-element.146), channel_id=1, source_target_pairs={{0,4},{4,0},{8,12},{12,8},{16,20},{20,16},{24,28},{28,24},{1,5},{5... | collective-permute-start | bytes 6291464 | tf_op jit(solution)/shard_map/ppermute | solution.py:570
  618.3 25.3 %collective-permute-start.38 = (bf16[128,2048]{1,0:T(8,128)(2,1)S(1)}, bf16[128,2048]{1,0:T(8,128)(2,1)S(1)}, u32[]{:S(2)}, u32[]{:S(2)}) collective-permute-start(bf16[128,2048]{1,0:T(8,128)(2,1)S(1)} %collective-permute-done.30), channel_id=1, source_target_pairs={{1,2},{2,3},{5,6},{6,7},{9,10},{10,11},{13,14},{14,15},{17,18},{18... | collective-permute-start | bytes 1572872 | tf_op jit(solution)/shard_map/ppermute | solution.py:512
  619.0 27.0 %collective-permute-start.39 = (bf16[128,2048]{1,0:T(8,128)(2,1)S(1)}, bf16[128,2048]{1,0:T(8,128)(2,1)}, u32[]{:S(2)}, u32[]{:S(2)}) collective-permute-start(bf16[128,2048]{1,0:T(8,128)(2,1)S(1)} %collective-permute-done.31), channel_id=1, source_target_pairs={{1,0},{2,1},{5,4},{6,5},{9,8},{10,9},{13,12},{14,13},{17,16},{18,1... | collective-permute-start | bytes 1572872 | tf_op jit(solution)/shard_map/ppermute | solution.py:513
  620.7 54.3 %collective-permute-start.47 = (bf16[2,2,1024,256]{3,2,1,0:T(8,128)(2,1)}, bf16[2,2,1024,256]{3,2,1,0:T(8,128)(2,1)}, u32[]{:S(2)}, u32[]{:S(2)}) collective-permute-start(bf16[2,2,1024,256]{3,2,1,0:T(8,128)(2,1)} %slice_bitcast_fusion.5), channel_id=1, source_target_pairs={{0,8},{4,12},{8,0},{12,4},{16,24},{20,28},{24,16},{28,20},{1,9},{5... | collective-permute-start | bytes 6291464 | tf_op jit(solution)/shard_map/ppermute | solution.py:570
  643.6 49.2 %collective-permute-start.46 = (bf16[2,2,1024,256]{3,2,1,0:T(8,128)(2,1)}, bf16[2,2,1024,256]{3,2,1,0:T(8,128)(2,1)}, u32[]{:S(2)}, u32[]{:S(2)}) collective-permute-start(bf16[2,2,1024,256]{3,2,1,0:T(8,128)(2,1)} %bitcast.16), channel_id=1, source_target_pairs={{0,16},{4,20},{8,24},{12,28},{16,0},{20,4},{24,8},{28,12},{1,17},{... | collective-permute-start | bytes 6291464 | tf_op jit(solution)/shard_map/ppermute | solution.py:570
  664.2 388.5 %reduce-scatter.14.cloned.1.call-start = ((), (), s32[]{:S(2)}) async-start(), calls=%async_computation.10 | async-start | bytes 2621440 | tf_op jit(solution)/shard_map/reduce_scatter | solution.py:498
  669.4 85.1 %collective-permute-start.51 = (bf16[2,2,1024,256]{3,2,1,0:T(8,128)(2,1)}, bf16[2,2,1024,256]{3,2,1,0:T(8,128)(2,1)}, u32[]{:S(2)}, u32[]{:S(2)}) collective-permute-start(bf16[2,2,1024,256]{3,2,1,0:T(8,128)(2,1)} %slice_bitcast_fusion.4), channel_id=1, source_target_pairs={{0,8},{4,12},{8,0},{12,4},{16,24},{20,28},{24,16},{28,20},{1,9},{5... | collective-permute-start | bytes 6291464 | tf_op jit(solution)/shard_map/ppermute | solution.py:570
  675.1 101.4 %collective-permute-start.50 = (bf16[2,2,1024,256]{3,2,1,0:T(8,128)(2,1)}, bf16[2,2,1024,256]{3,2,1,0:T(8,128)(2,1)}, u32[]{:S(2)}, u32[]{:S(2)}) collective-permute-start(bf16[2,2,1024,256]{3,2,1,0:T(8,128)(2,1)} %bitcast.19), channel_id=1, source_target_pairs={{0,16},{4,20},{8,24},{12,28},{16,0},{20,4},{24,8},{28,12},{1,17},{... | collective-permute-start | bytes 6291464 | tf_op jit(solution)/shard_map/ppermute | solution.py:570
  729.0 25.4 %collective-permute-start.49 = (f32[2,1024]{1,0:T(2,128)S(1)}, f32[2,1024]{1,0:T(2,128)S(1)}, u32[]{:S(2)}, u32[]{:S(2)}) collective-permute-start(f32[2,1024]{1,0:T(2,128)S(1)} %fusion.34), channel_id=1, source_target_pairs={{0,2},{1,3},{2,0},{3,1},{4,6},{5,7},{6,4},{7,5},{8,10},{9,11},{10,... | collective-permute-start | bytes 24584 | tf_op jit(solution)/shard_map/ppermute | solution.py:621
  754.3 25.6 %collective-permute-start.54 = (bf16[2,2048,256]{2,1,0:T(8,128)(2,1)}, bf16[2,2048,256]{2,1,0:T(8,128)(2,1)}, u32[]{:S(2)}, u32[]{:S(2)}) collective-permute-start(bf16[2,2048,256]{2,1,0:T(8,128)(2,1)} %get-tuple-element.147), channel_id=1, source_target_pairs={{0,4},{4,0},{8,12},{12,8},{16,20},{20,16},{24,28},{28,24},{1,5},{5... | collective-permute-start | bytes 6291464 | tf_op jit(solution)/shard_map/ppermute | solution.py:570
  754.4 25.5 %collective-permute-start.55 = (bf16[2,2048,256]{2,1,0:T(8,128)(2,1)}, bf16[2,2048,256]{2,1,0:T(8,128)(2,1)}, u32[]{:S(2)}, u32[]{:S(2)}) collective-permute-start(bf16[2,2048,256]{2,1,0:T(8,128)(2,1)} %get-tuple-element.148), channel_id=1, source_target_pairs={{0,4},{4,0},{8,12},{12,8},{16,20},{20,16},{24,28},{28,24},{1,5},{5... | collective-permute-start | bytes 6291464 | tf_op jit(solution)/shard_map/ppermute | solution.py:570
  828.9 53.7 %collective-permute-start.79 = (bf16[1,2,1024,256]{3,2,1,0:T(8,128)(2,1)}, bf16[1,2,1024,256]{3,2,1,0:T(8,128)(2,1)}, u32[]{:S(2)}, u32[]{:S(2)}) collective-permute-start(bf16[1,2,1024,256]{3,2,1,0:T(8,128)(2,1)} %slice_bitcast_fusion.10), channel_id=1, source_target_pairs={{0,16},{4,20},{8,24},{12,28},{16,0},{20,4},{24,8},{28,12},{1,17},{... | collective-permute-start | bytes 3145736 | tf_op jit(solution)/shard_map/ppermute | solution.py:570
  830.8 29.1 %collective-permute-start.62 = (bf16[128,2048]{1,0:T(8,128)(2,1)}, bf16[128,2048]{1,0:T(8,128)(2,1)S(1)}, u32[]{:S(2)}, u32[]{:S(2)}) collective-permute-start(bf16[128,2048]{1,0:T(8,128)(2,1)} %get-tuple-element.242), channel_id=1, source_target_pairs={{0,1},{4,5},{8,9},{12,13},{16,17},{20,21},{24,25},{28,29}} | collective-permute-start | bytes 1572872 | tf_op jit(solution)/shard_map/ppermute | solution.py:557
  834.8 27.2 %collective-permute-start.63 = (bf16[128,2048]{1,0:T(8,128)(2,1)}, bf16[128,2048]{1,0:T(8,128)(2,1)S(1)}, u32[]{:S(2)}, u32[]{:S(2)}) collective-permute-start(bf16[128,2048]{1,0:T(8,128)(2,1)} %get-tuple-element.243), channel_id=1, source_target_pairs={{3,2},{7,6},{11,10},{15,14},{19,18},{23,22},{27,26},{31,30}} | collective-permute-start | bytes 1572872 | tf_op jit(solution)/shard_map/ppermute | solution.py:558
  835.5 42.8 %collective-permute-start.56 = (bf16[128,2048]{1,0:T(8,128)(2,1)}, bf16[128,2048]{1,0:T(8,128)(2,1)S(1)}, u32[]{:S(2)}, u32[]{:S(2)}) collective-permute-start(bf16[128,2048]{1,0:T(8,128)(2,1)} %get-tuple-element.236), channel_id=1, source_target_pairs={{0,1},{4,5},{8,9},{12,13},{16,17},{20,21},{24,25},{28,29}} | collective-permute-start | bytes 1572872 | tf_op jit(solution)/shard_map/ppermute | solution.py:557
  859.0 21.7 %collective-permute-start.57 = (bf16[128,2048]{1,0:T(8,128)(2,1)S(1)}, bf16[128,2048]{1,0:T(8,128)(2,1)S(1)}, u32[]{:S(2)}, u32[]{:S(2)}) collective-permute-start(bf16[128,2048]{1,0:T(8,128)(2,1)S(1)} %copy-done.72), channel_id=1, source_target_pairs={{3,2},{7,6},{11,10},{15,14},{19,18},{23,22},{27,26},{31,30}} | collective-permute-start | bytes 1572872 | tf_op jit(solution)/shard_map/ppermute | solution.py:558
  859.9 25.5 %collective-permute-start.78 = (bf16[1,2,1024,256]{3,2,1,0:T(8,128)(2,1)S(1)}, bf16[1,2,1024,256]{3,2,1,0:T(8,128)(2,1)S(1)}, u32[]{:S(2)}, u32[]{:S(2)}) collective-permute-start(bf16[1,2,1024,256]{3,2,1,0:T(8,128)(2,1)S(1)} %slice.286), channel_id=1, source_target_pairs={{0,8},{4,12},{8,0},{12,4},{16,24},{20,28},{24,16},{28,20},{1,9},{5... | collective-permute-start | bytes 3145736 | tf_op jit(solution)/shard_map/ppermute | solution.py:570
  861.9 81.0 %collective-permute-start.81 = (bf16[1,2,1024,256]{3,2,1,0:T(8,128)(2,1)S(1)}, bf16[1,2,1024,256]{3,2,1,0:T(8,128)(2,1)S(1)}, u32[]{:S(2)}, u32[]{:S(2)}) collective-permute-start(bf16[1,2,1024,256]{3,2,1,0:T(8,128)(2,1)S(1)} %slice_bitcast_fusion.8), channel_id=1, source_target_pairs={{0,16},{4,20},{8,24},{12,28},{16,0},{20,4},{24,8},{28,12},{1,17},{... | collective-permute-start | bytes 3145736 | tf_op jit(solution)/shard_map/ppermute | solution.py:570
  880.7 43.7 %collective-permute-start.64 = (bf16[128,2048]{1,0:T(8,128)(2,1)S(1)}, bf16[128,2048]{1,0:T(8,128)(2,1)S(1)}, u32[]{:S(2)}, u32[]{:S(2)}) collective-permute-start(bf16[128,2048]{1,0:T(8,128)(2,1)S(1)} %get-tuple-element.240), channel_id=1, source_target_pairs={{0,1},{1,2},{4,5},{5,6},{8,9},{9,10},{12,13},{13,14},{16,17},{17,1... | collective-permute-start | bytes 1572872 | tf_op jit(solution)/shard_map/ppermute | solution.py:557
  882.7 41.7 %collective-permute-start.65 = (bf16[128,2048]{1,0:T(8,128)(2,1)S(1)}, bf16[128,2048]{1,0:T(8,128)(2,1)S(1)}, u32[]{:S(2)}, u32[]{:S(2)}) collective-permute-start(bf16[128,2048]{1,0:T(8,128)(2,1)S(1)} %get-tuple-element.241), channel_id=1, source_target_pairs={{2,1},{3,2},{6,5},{7,6},{10,9},{11,10},{14,13},{15,14},{18,17},{19... | collective-permute-start | bytes 1572872 | tf_op jit(solution)/shard_map/ppermute | solution.py:558
  885.4 41.4 %collective-permute-start.58 = (bf16[128,2048]{1,0:T(8,128)(2,1)S(1)}, bf16[128,2048]{1,0:T(8,128)(2,1)S(1)}, u32[]{:S(2)}, u32[]{:S(2)}) collective-permute-start(bf16[128,2048]{1,0:T(8,128)(2,1)S(1)} %get-tuple-element.234), channel_id=1, source_target_pairs={{0,1},{1,2},{4,5},{5,6},{8,9},{9,10},{12,13},{13,14},{16,17},{17,1... | collective-permute-start | bytes 1572872 | tf_op jit(solution)/shard_map/ppermute | solution.py:557
  897.8 24.5 %collective-permute-start.77 = (f32[20,2048]{1,0:T(8,128)S(1)}, f32[20,2048]{1,0:T(8,128)S(1)}, u32[]{:S(2)}, u32[]{:S(2)}) collective-permute-start(f32[20,2048]{1,0:T(8,128)S(1)} %add.562), channel_id=1, source_target_pairs={{0,2},{1,3},{2,0},{3,1},{4,6},{5,7},{6,4},{7,5},{8,10},{9,11},{10,... | collective-permute-start | bytes 491528 | tf_op jit(solution)/shard_map/ppermute | solution.py:621
  924.4 109.2 %collective-permute-start.68 = (bf16[4,4,256,512]{3,2,1,0:T(8,128)(2,1)}, bf16[4,4,256,512]{3,2,1,0:T(8,128)(2,1)}, u32[]{:S(2)}, u32[]{:S(2)}) collective-permute-start(bf16[4,4,256,512]{3,2,1,0:T(8,128)(2,1)} %attention_wgrad.2), channel_id=1, source_target_pairs={{0,4},{4,0},{8,12},{12,8},{16,20},{20,16},{24,28},{28,24},{1,5},{5... | collective-permute-start | bytes 12582920 | tf_op jit(solution)/shard_map/ppermute | solution.py:570
  924.4 26.1 %collective-permute-start.80 = (bf16[1,2,1024,256]{3,2,1,0:T(8,128)(2,1)S(1)}, bf16[1,2,1024,256]{3,2,1,0:T(8,128)(2,1)S(1)}, u32[]{:S(2)}, u32[]{:S(2)}) collective-permute-start(bf16[1,2,1024,256]{3,2,1,0:T(8,128)(2,1)S(1)} %slice.290), channel_id=1, source_target_pairs={{0,8},{4,12},{8,0},{12,4},{16,24},{20,28},{24,16},{28,20},{1,9},{5... | collective-permute-start | bytes 3145736 | tf_op jit(solution)/shard_map/ppermute | solution.py:570
  926.8 68.3 %collective-permute-start.84 = (bf16[2,2,1024,256]{3,2,1,0:T(8,128)(2,1)S(1)}, bf16[2,2,1024,256]{3,2,1,0:T(8,128)(2,1)S(1)}, u32[]{:S(2)}, u32[]{:S(2)}) collective-permute-start(bf16[2,2,1024,256]{3,2,1,0:T(8,128)(2,1)S(1)} %slice_bitcast_fusion), channel_id=1, source_target_pairs={{0,8},{4,12},{8,0},{12,4},{16,24},{20,28},{24,16},{28,20},{1,9},{5... | collective-permute-start | bytes 6291464 | tf_op jit(solution)/shard_map/ppermute | solution.py:570
  927.0 29.7 %collective-permute-start.66 = (bf16[128,2048]{1,0:T(8,128)(2,1)S(1)}, bf16[128,2048]{1,0:T(8,128)(2,1)S(1)}, u32[]{:S(2)}, u32[]{:S(2)}) collective-permute-start(bf16[128,2048]{1,0:T(8,128)(2,1)S(1)} %get-tuple-element.238), channel_id=1, source_target_pairs={{0,1},{1,2},{2,3},{4,5},{5,6},{6,7},{8,9},{9,10},{10,11},{12,13},{... | collective-permute-start | bytes 1572872 | tf_op jit(solution)/shard_map/ppermute | solution.py:557
  960.2 48.6 %collective-permute-start.82 = (bf16[2,2,1024,256]{3,2,1,0:T(8,128)(2,1)S(1)}, bf16[2,2,1024,256]{3,2,1,0:T(8,128)(2,1)S(1)}, u32[]{:S(2)}, u32[]{:S(2)}) collective-permute-start(bf16[2,2,1024,256]{3,2,1,0:T(8,128)(2,1)S(1)} %bitcast.220), channel_id=1, source_target_pairs={{0,16},{4,20},{8,24},{12,28},{16,0},{20,4},{24,8},{28,12},{1,17},{... | collective-permute-start | bytes 6291464 | tf_op jit(solution)/shard_map/ppermute | solution.py:570
  996.8 32.6 %collective-permute-start.85 = (bf16[1,2,1024,256]{3,2,1,0:T(8,128)(2,1)}, bf16[1,2,1024,256]{3,2,1,0:T(8,128)(2,1)}, u32[]{:S(2)}, u32[]{:S(2)}) collective-permute-start(bf16[1,2,1024,256]{3,2,1,0:T(8,128)(2,1)} %slice_bitcast_fusion.6), channel_id=1, source_target_pairs={{0,16},{4,20},{8,24},{12,28},{16,0},{20,4},{24,8},{28,12},{1,17},{... | collective-permute-start | bytes 3145736 | tf_op jit(solution)/shard_map/ppermute | solution.py:570
  1046.5 22.4 %collective-permute-start.69 = (bf16[2,4,128,512]{3,2,1,0:T(8,128)(2,1)}, bf16[2,4,128,512]{3,2,1,0:T(8,128)(2,1)}, u32[]{:S(2)}, u32[]{:S(2)}) collective-permute-start(bf16[2,4,128,512]{3,2,1,0:T(8,128)(2,1)} %slice.225), channel_id=1, source_target_pairs={{0,16},{4,20},{8,24},{12,28},{16,0},{20,4},{24,8},{28,12},{1,17},{... | collective-permute-start | bytes 3145736 | tf_op jit(solution)/shard_map/ppermute | solution.py:570
  1048.7 23.5 %collective-permute-start.71 = (bf16[2,4,128,512]{3,2,1,0:T(8,128)(2,1)}, bf16[2,4,128,512]{3,2,1,0:T(8,128)(2,1)}, u32[]{:S(2)}, u32[]{:S(2)}) collective-permute-start(bf16[2,4,128,512]{3,2,1,0:T(8,128)(2,1)} %slice_bitcast_fusion.12), channel_id=1, source_target_pairs={{0,8},{4,12},{8,0},{12,4},{16,24},{20,28},{24,16},{28,20},{1,9},{5... | collective-permute-start | bytes 3145736 | tf_op jit(solution)/shard_map/ppermute | solution.py:570
  (126 other events, 1480.9 us)
Sparse Core Ops, SparseCore 0:
  158.7 57.9 reduce-scatter.5
  229.2 51.9 reduce-scatter.7
  340.2 47.1 all-gather.1
  402.2 57.6 reduce-scatter.9
  664.3 53.5 reduce-scatter.11
  830.9 73.1 reduce-scatter.13

commit v3 on v2

--- a/solution.py
+++ b/solution.py
@@ -35,7 +35,7 @@
     return pltpu.CompilerParams(vmem_limit_bytes=VMEM)
 
 
-PACE = 0.8
+PACE = 0.3
 
 
 def cost(flops, moved, special=0):
@@ -498,6 +498,40 @@
     return lax.psum_scatter(values, "tensor", scatter_dimension=0, tiled=True)
 
 
+def join_kernel(parts, slots, own, *refs):
+    ups, downs, out = refs[: parts - 1], refs[parts - 1 : 2 * parts - 2], refs[2 * parts - 2]
+    at = pl.program_id(0)
+
+    @pl.when(at == 0)
+    def _():
+        out[...] = own[...]
+
+    for step in range(1, parts):
+
+        @pl.when(at == step)
+        def _(step=step):
+            out[...] = ups[step - 1][...] + downs[parts - 1 - step][...]
+
+
+def join(slots, own, ups, downs):
+    rows, columns = own.shape
+    parts = len(ups) + 1
+    whole = pl.BlockSpec((rows, columns), lambda i, to: (0, 0))
+    return pl.pallas_call(
+        functools.partial(join_kernel, parts),
+        grid_spec=pltpu.PrefetchScalarGridSpec(
+            num_scalar_prefetch=1,
+            grid=(parts,),
+            in_specs=[whole] * (2 * parts - 1),
+            out_specs=pl.BlockSpec((rows, columns), lambda i, to: (to[i], 0)),
+        ),
+        out_shape=jax.ShapeDtypeStruct((parts * rows, columns), own.dtype),
+        compiler_params=params(),
+        cost_estimate=cost(0, 0),
+        name="join",
+    )(slots, own, *ups, *downs)
+
+
 class Chain:
     def __init__(self, values):
         self.values = values
@@ -519,50 +553,9 @@
     def joined(self):
         while len(self.ups) < self.parts:
             self.hop()
-        parts, values = self.parts, self.values
         at = lax.axis_index("tensor")
-        rows = values.shape[0]
-        whole = jnp.zeros((parts * rows,) + values.shape[1:], values.dtype)
-        whole = lax.dynamic_update_slice_in_dim(whole, values, at * rows, 0)
-        for step in range(1, parts):
-            piece = self.ups[step] + self.downs[parts - step]
-            whole = lax.dynamic_update_slice_in_dim(whole, piece, lax.rem(at - step + parts, parts) * rows, 0)
-        return whole
-
-
-class ScatterChain:
-    def __init__(self, values):
-        self.parts = lax.axis_size("tensor")
-        self.at = lax.axis_index("tensor")
-        self.values = values
-        self.rows = values.shape[0] // self.parts
-        self.step = 0
-        self.up = self.down = self.first = None
-
-    def block(self, place):
-        return lax.dynamic_slice_in_dim(self.values, jnp.clip(place, 0, self.parts - 1) * self.rows, self.rows, 0)
-
-    def hop(self, *others):
-        parts, step = self.parts, self.step
-        if step < parts - 1:
-            if step:
-                self.values = gate(self.values, self.up, self.down, *others)
-            up = self.block(parts - 1 - step + self.at)
-            down = self.block(step - parts + 1 + self.at)
-            if step:
-                up = (up.astype(f32) + self.up.astype(f32)).astype(bf16)
-                down = (down.astype(f32) + self.down.astype(f32)).astype(bf16)
-            self.sent = (up, down)
-            self.first = self.first or self.sent
-            self.up = lax.ppermute(up, "tensor", [(i, i + 1) for i in range(step + 1)])
-            self.down = lax.ppermute(down, "tensor", [(i, i - 1) for i in range(parts - 1 - step, parts)])
-            self.step += 1
-        return self.up, self.down
-
-    def total(self):
-        while self.step < self.parts - 1:
-            self.hop()
-        return self.block(self.at).astype(f32) + self.up.astype(f32) + self.down.astype(f32)
+        slots = lax.rem(at - jnp.arange(self.parts, dtype=jnp.int32) + self.parts, self.parts)
+        return join(slots, self.values, self.ups[1:], self.downs[1:])
 
 
 def pair_swap(values, step):
@@ -652,7 +645,7 @@
 
     inputs = tokens.astype(f32)
     first_scale = rms_scale(inputs)
-    normed_all = Chain((inputs * first_scale * attn_gain).astype(bf16)).joined()
+    normed_all = gather_rows((inputs * first_scale * attn_gain).astype(bf16))
     behind = Chain(gate(cotangent, normed_all))
 
     expert_ids = jnp.arange(LANES)
@@ -660,6 +653,8 @@
     router_wide = jnp.pad(router, ((0, 0), (0, LANES - experts)))
     routed_own = lax.dynamic_slice_in_dim(routed, part_at * shard_rows, shard_rows, 0)[:, :experts]
     cosine, sine = rope_tables(length, HEAD)
+    normed_all = gate(normed_all, routed, router_wide, cosine, sine)
+
     relative = jnp.arange(dp_size // 2, dtype=jnp.int32) ^ (lax.axis_index("dp") // 2)
     own_blocks, other_blocks = 2 * relative + low_bit, 2 * relative + 1 - low_bit
     mine, theirs = (
@@ -671,9 +666,10 @@
     behind.hop()
     q_scale, k_scale = (lax.rsqrt(squares[i] / features + EPSILON)[:, None] for i in range(2))
     query, key, attended, lse = attend(
-        qraw, kraw, value, q_scale, k_scale, q_gain, k_gain, cosine, sine, gate(seg_ids[0], routed, router_wide, *behind.recv()), keep_mask[0]
+        qraw, kraw, value, q_scale, k_scale, q_gain, k_gain, cosine, sine, gate(seg_ids[0], *behind.recv()), keep_mask[0]
     )
-    attended_parts = [chunk_of(attended, c) for c in chunks]
+    behind.hop()
+    attended_parts = [chunk_of(gate(attended, *behind.recv()), c) for c in chunks]
     outs = [nt(attended_parts[0], w_out).astype(bf16)]
     summed = [scatter_rows(outs[0])]
     outs.append(nt(gate(attended_parts[1], outs[0]), w_out).astype(bf16))
@@ -682,7 +678,7 @@
 
     grad_group = behind.joined()
     grad_all = [chunk_of(grad_group, c) for c in chunks]
-    backs = [up_back(grad_all[c], w_down) for c in chunks]
+    backs = [up_back(grad_all[0], w_down)]
 
     middles, scales, ffn_own = [], [], []
 
@@ -695,11 +691,12 @@
         ffn_own.append(normed)
         return normed
 
-    ahead = Chain(middle_of(0, summed[0]))
+    ahead = Chain(middle_of(0, gate(summed[0], backs[0])))
     ahead.hop()
+    backs.append(up_back(gate(grad_all[1], ahead.values), w_down))
     after = gather_rows(middle_of(1, gate(summed[1], *ahead.recv())))
-    ahead.hop(backs[0])
     ahead.hop(backs[1])
+    ahead.hop()
     ffn_all = [ahead.joined(), after]
     acts, dgates, dups, expert_grads = [], [], [], []
     for c in chunks:
@@ -709,8 +706,7 @@
         dgates.append(dgate)
         dups.append(dup)
         expert_grads.append(grads)
-    expert_grads[0] = scatter_rows(expert_grads[0])
-    second_sums = ScatterChain(expert_grads[1])
+    expert_grads = [scatter_rows(grads) for grads in expert_grads]
 
     ffn_gain_parts, router_parts, middle_grads = [], [], []
 
@@ -734,57 +730,50 @@
         return Halving([half.reshape((dp_size // 2, per) + half.shape[1:]) for half in sums])
 
     first = middle_back(0, gate(expert_grads[0], acts[1]).astype(f32))
-    second_sums.hop()
     first.hop()
-    gate_sent = expert_sums(ffn_all, dgates, theirs, first.values, *second_sums.sent)
+    gate_sent = expert_sums(ffn_all, dgates, theirs, first.values)
     gate_got = core_swap(gate_sent)
-    second_sums.hop(*gate_sent)
-    up_sent = expert_sums(ffn_all, dups, theirs, *first.hop(*gate_sent), *second_sums.sent)
+    up_sent = expert_sums(ffn_all, dups, theirs, *first.hop(*gate_sent))
     up_got = core_swap(up_sent)
-    second_sums.hop(*up_sent)
-    down_sent = expert_sums(grad_all, acts, theirs, *first.hop(*up_sent), *second_sums.sent)
-    down_got = core_swap(down_sent)
-    second = middle_back(1, gate(second_sums.total(), *down_sent))
+    moe_0 = down(gate(acts[0], *first.hop(*up_sent)), w_down)
+    moe_sum_0 = scatter_rows(moe_0)
+    second = middle_back(1, gate(expert_grads[1], moe_0, *first.recv()).astype(f32))
     second.hop()
-    gate_sums = expert_sums(ffn_all, dgates, mine, second.values, *first.recv(), added=gate_got)
+    gate_sums = expert_sums(ffn_all, dgates, mine, second.values, added=gate_got)
     gate_out = halving(gate_sums)
     up_sums = expert_sums(ffn_all, dups, mine, *second.hop(*gate_sums), *gate_out.send(), added=up_got)
     up_out = halving(up_sums)
-    moe_0 = down(gate(acts[0], *second.hop(*up_sums), *up_out.send()), w_down)
-    moe_sum_0 = scatter_rows(moe_0)
+    moe_1 = down(gate(acts[1], *second.hop(*up_sums), *up_out.send()), w_down)
+    moe_sum_1 = scatter_rows(moe_1)
     middle_all = [first.joined(), second.joined()]
 
     attended_grad = in_order([nn(rows, w_out).astype(bf16) for rows in middle_all])
+    dqn, dkn, dvalue, qdot, kdot, q_gain_part, k_gain_part = attend_back(
+        query, key, value, attended_grad, lse, qraw, kraw, q_scale, k_scale, q_gain, k_gain, cosine, sine,
+        gate(seg_ids[0], moe_1), keep_mask[0],
+    )
+    dots = exchange_sum(jnp.stack([qdot[:, 0], kdot[:, 0]]), ("tensor",)) / features
     gate_late = gate_out.add()
     gate_out.send()
-    dqn, dkn, dvalue, qdot, kdot, q_gain_part, k_gain_part = attend_back(
-        query, key, value, attended_grad, lse, qraw, kraw, q_scale, k_scale, q_gain, k_gain, cosine, sine,
-        gate(seg_ids[0], moe_0, *gate_late), keep_mask[0],
+    down_sent = expert_sums(grad_all, acts, theirs, dqn, *gate_late)
+    down_got = core_swap(down_sent)
+    normed_part, dqraw, dkraw, attn_gain_part = project_back(
+        normed_all, dqn, dkn, dvalue, qraw, kraw, q_scale, k_scale, dots[0][:, None], dots[1][:, None],
+        gate(q_gain, *down_sent), k_gain, w_query, w_key, w_value,
     )
-    dots = exchange_sum(jnp.stack([qdot[:, 0], kdot[:, 0]]), ("tensor",)) / features
-    moe_1 = down(gate(acts[1], dqn), w_down)
-    moe_sum_1 = scatter_rows(moe_1)
+    normed_grad = scatter_rows(normed_part)
     up_late = up_out.add()
     up_out.send()
-    down_sums = expert_sums(grad_all, acts, mine, dqn, moe_1, *up_late, added=down_got)
+    down_sums = expert_sums(grad_all, acts, mine, normed_part, *up_late, added=down_got)
     down_out = halving(down_sums)
     down_out.send()
-    normed_part, dqraw, dkraw, attn_gain_part = project_back(
-        normed_all, dqn, dkn, dvalue, qraw, kraw, q_scale, k_scale, dots[0][:, None], dots[1][:, None],
-        gate(q_gain, *down_sums), k_gain, w_query, w_key, w_value,
-    )
-    halves = [ScatterChain(chunk_of(normed_part, c)) for c in chunks]
-    for _ in range(parts - 1):
-        for half in halves:
-            half.hop()
-    normed_grad = jnp.concatenate([half.total() for half in halves])
 
     def attention_sums(ids, *others, added=None):
         return attention_wgrad(
             normed_all, middle_all, (dqraw, dkraw, dvalue), attended_parts, gate(ids, *others), dp_size, added
         )
 
-    attn_sent = attention_sums(other_blocks, *(part for half in halves for part in half.first))
+    attn_sent = attention_sums(other_blocks, *down_sums)
     attn_got = pair_swap(attn_sent, 1)
 
     def placed(part):
@@ -794,13 +783,13 @@
     smalls = gate(jnp.concatenate([jnp.stack(smalls), sum(router_parts).T]), attn_sent)
     smalls = exchange_sum(smalls, ("dp", "tensor"))
     attn_out = Halving(attention_sums(own_blocks, attn_sent, added=attn_got))
-    attn_out.send()
+    normed_grad = gate(normed_grad, *attn_out.send())
     gate_done = gate_out.done()
     up_done = up_out.done()
     down_done = down_out.done()
     query_done, key_done, value_done, out_done = attn_out.done()
     layer_out = jnp.concatenate([middles[0] + moe_sum_0.astype(f32), middles[1] + moe_sum_1.astype(f32)]).astype(bf16)
-    tokens_grad = jnp.concatenate(middle_grads) + norm_back(normed_grad, inputs, first_scale, attn_gain)
+    tokens_grad = jnp.concatenate(middle_grads) + norm_back(normed_grad.astype(f32), inputs, first_scale, attn_gain)
     return (
         layer_out, tokens_grad, query_done, key_done, value_done, out_done,
         smalls[0], smalls[1], smalls[2], smalls[3], smalls[4:].T, gate_done, up_done, down_done,

time: 1100 us -> 954 us (0.87)
  starting transfers between devices: 188 us -> 98.4 us
  waiting for transfers between devices: 350 us -> 309 us
  other arithmetic: 107 us -> 79.5 us
  Pallas kernels: 349 us -> 369 us
  local copies, waits for them, and re-layouts: 65.3 us -> 51.2 us
    all_gather x1 -> x2, waiting for transfers between devices: 0.02 us -> 83.6 us  [gather_rows(): return lax.all_gather(values, 'tensor', axis=0, tiled=True)]
    ppermute x18 -> x0, starting transfers between devices: 71.7 us -> none  [the longest x9 61.8 us: hop(): self.up = lax.ppermute(up, 'tensor', [(i, i + 1) for i in range(step + 1)])]
    ppermute x15 -> x12, waiting for transfers between devices: 191 us -> 120 us  [hop(): lax.ppermute(down, 'tensor', [(i, i - 1) for i in range(1, self.parts - s...]
    dynamic_update_slice x19 -> x0, other arithmetic: 32.4 us -> none  [the longest x15 27.6 us: joined(): lax.dynamic_update_slice_in_dim(whole, piece, lax.rem(at - step + parts,...]
    ppermute x18 -> x0, waiting for transfers between devices: 24.7 us -> none  [the longest x9 19.4 us: hop(): self.up = lax.ppermute(up, 'tensor', [(i, i + 1) for i in range(step + 1)])]
    pallas_call x0 -> x4, Pallas kernels: none -> 20.1 us  [join(): pl.pallas_call(functools.partial(join_kernel, parts), grid_spec=pltpu.Pre...]
    ppermute x29, waiting for transfers between devices: 90 us -> 71.6 us  [pair_swap(): return lax.ppermute(values, 'dp', [(i, i ^ step) for i in range(size)])]
    ppermute x9, starting transfers between devices: 33.4 us -> 17.5 us  [exchange_sum(): lax.ppermute(values, axis, [(i, i ^ step) for i in range(size)])]
  transfers between devices with their start and end apart: 92 -> 71, of which waited for: 30 -> 27; matrix products, arithmetic and copies ran while one was open for 15% -> 14% of each run, Pallas kernels for 30% -> 39%
where the time goes in v3:
time: 954 us; the launch traced here: 942 us
  Pallas kernels  369 us (39%)
  waiting for transfers between devices  309 us (32%)
  starting transfers between devices  98.4 us (10%)
  other arithmetic  79.5 us (8%)
  local copies, waits for them, and re-layouts  51.2 us (5%)
  matrix products  21 us (2%)
  between operations  15.1 us (2%)
    ppermute x12, waiting for transfers between devices, hop(): lax.ppermute(down, 'tensor', [(i, i - 1) for i in range(1, self.parts - s...  120 us
    pallas_call x6, Pallas kernels, wgrad(): pl.pallas_call(functools.partial(wgrad_kernel, len(lefts), len(added), pe...  103 us
    pallas_call x2, Pallas kernels, experts_block(): pl.pallas_call(functools.partial(expert_kernel, block), grid=(experts,),...  95 us
    all_gather x2, waiting for transfers between devices, gather_rows(): return lax.all_gather(values, 'tensor', axis=0, tiled=True)  83.6 us
    ppermute x29, waiting for transfers between devices, pair_swap(): return lax.ppermute(values, 'dp', [(i, i ^ step) for i in range(size)])  71.6 us
    ppermute x12, starting transfers between devices, hop(): lax.ppermute(up, 'tensor', [(i, i + 1) for i in range(step - 1, self.part...  43 us
    pallas_call x2, Pallas kernels, down(): pl.pallas_call(down_kernel, grid=(features // block,), in_specs=[pl.Block...  30.7 us
    pallas_call x2, Pallas kernels, up_back(): pl.pallas_call(up_back_kernel, grid=(experts // step,), in_specs=[pl.Bloc...  30.1 us
  transfers between devices with their start and end apart: 71, of which 27 were waited for; matrix products, arithmetic and copies ran while one was open for 14% of the time, Pallas kernels for 39%

profile of v3, /device:TPU:0, one launch (start us, length us, event | category | flops | bytes accessed | tf_op | source)
XLA Modules:
  0.0 942.1 jit_solution(10377064766887327672)
XLA Ops:
  12.7 83.6 %all-gather.3.cloned.1.call-done.rows_in.refs_0_ = bf16[1024,2048]{1,0:T(8,128)(2,1)} async-done(((bf16[256,2048]{1,0:T(8,128)(2,1)}), bf16[1024,2048]{1,0:T(8,128)(2,1)}) %all-gather.3.cloned.1.call-update) | async-done | bytes 4194320 | tf_op jit(solution)/shard_map/all_gather | solution.py:494
  97.5 5.6 collective-permute-start.2
  103.1 2.9 fusion.22
  110.1 2.8 pad_maximum_fusion.6
  112.9 6.6 convert_reduce_fusion
  119.5 16.3 %project.1 = (f32[1024,512]{1,0:T(8,128)}, f32[1024,512]{1,0:T(8,128)}, bf16[1024,512]{1,0:T(8,128)(2,1)}, f32[2,1024]{1,0:T(2,128)}) custom-call(bf16[1024,2048]{1,0:T(8,128)(2,1)} %all-gather.3.cloned.1.call-done.rows_in.refs_0_, bf16[2048,512]{1,0:T(8,128)(2,1)} %w_query.3, bf16[2048,512]{1,0:T(8,128)(2,1)} %w_key.3, bf16[2048,512]{1,0:T(8,128)(2,1)} %w_value.3), custom_call_target="tpu_custom_call" | custom-call | flops 2899102976 | bytes 1310720 | tf_op jit(solution)/shard_map/project/pallas_call | solution.py:102
  135.7 3.9 collective-permute-done
  141.2 3.7 collective-permute-done.1
  150.0 15.6 %attend.1 = (bf16[1024,512]{1,0:T(8,128)(2,1)}, bf16[1024,512]{1,0:T(8,128)(2,1)}, bf16[1024,512]{1,0:T(8,128)(2,1)}, f32[1024,512]{1,0:T(8,128)}) custom-call(f32[1024,512]{1,0:T(8,128)} %get-tuple-element.100.qraw, f32[1024,512]{1,0:T(8,128)} %get-tuple-element.101.kraw, bf16[1024,512]{1,0:T(8,128)(2,1)} %get-tuple-element.102.value, ...), custom_call_target="tpu_custom_call" | custom-call | flops 57347878912 | bytes 1179648 | tf_op jit(solution)/shard_map/attend/pallas_call | solution.py:233
  165.6 6.5 collective-permute-done.5.refs_4_
  174.7 2.6 convolution_convert_fusion.1
  185.5 53.5 %collective-permute-done.7.refs_5_ = bf16[256,2048]{1,0:T(8,128)(2,1)} collective-permute-done((bf16[256,2048]{1,0:T(8,128)(2,1)}, bf16[256,2048]{1,0:T(8,128)(2,1)}, u32[]{:S(2)}, u32[]{:S(2)}) %collective-permute-start.7) | collective-permute-done | bytes 1048608 | tf_op jit(solution)/shard_map/ppermute | solution.py:547
  238.9 6.3 join.4
  245.2 4.9 fusion.42
  250.1 15.0 %up_back.2.back = bf16[512,4096]{1,0:T(8,128)(2,1)} custom-call(bf16[512,2048]{1,0:T(8,128)(2,1)} %bitcast.189, bf16[16,2048,256]{2,1,0:T(8,128)(2,1)} %down_w.7), custom_call_target="tpu_custom_call" | custom-call | flops 3865470464 | bytes 2359296 | tf_op jit(solution)/shard_map/up_back/pallas_call | solution.py:325
  268.3 5.4 collective-permute-start.8
  273.6 15.0 %up_back.3.back = bf16[512,4096]{1,0:T(8,128)(2,1)} custom-call(bf16[512,2048]{1,0:T(8,128)(2,1)} %bitcast.186, bf16[16,2048,256]{2,1,0:T(8,128)(2,1)} %down_w.7), custom_call_target="tpu_custom_call" | custom-call | flops 3865470464 | bytes 2359296 | tf_op jit(solution)/shard_map/up_back/pallas_call | solution.py:325
  297.5 12.4 %collective-permute-done.12.refs_4_ = bf16[128,2048]{1,0:T(8,128)(2,1)} collective-permute-done((bf16[128,2048]{1,0:T(8,128)(2,1)}, bf16[128,2048]{1,0:T(8,128)(2,1)}, u32[]{:S(2)}, u32[]{:S(2)}) %collective-permute-start.12) | collective-permute-done | bytes 524320 | tf_op jit(solution)/shard_map/ppermute | solution.py:547
  312.2 11.9 %collective-permute-done.13.refs_5_ = bf16[128,2048]{1,0:T(8,128)(2,1)} collective-permute-done((bf16[128,2048]{1,0:T(8,128)(2,1)}, bf16[128,2048]{1,0:T(8,128)(2,1)}, u32[]{:S(2)}, u32[]{:S(2)}) %collective-permute-start.13) | collective-permute-done | bytes 524320 | tf_op jit(solution)/shard_map/ppermute | solution.py:547
  324.1 4.6 join.5.rows_in.refs_0_
  328.7 47.6 %experts.2 = (bf16[512,4096]{1,0:T(8,128)(2,1)}, bf16[512,4096]{1,0:T(8,128)(2,1)}, bf16[512,4096]{1,0:T(8,128)(2,1)}, bf16[512,2176]{1,0:T(8,128)(2,1)}) custom-call(bf16[512,2048]{1,0:T(8,128)(2,1)} %join.5.rows_in.refs_0_, bf16[512,4096]{1,0:T(8,128)(2,1)} %up_back.2.back, f32[512,128]{1,0:T(8,128)} %bitcast.221, bf16[2048,128]{1,0:T(8,128)(2,1)} %pad.4.router, ...), custom_call_target="tpu_custom_call" | custom-call | flops 53210619904 | bytes 6291456 | tf_op jit(solution)/shard_map/experts/pallas_call | solution.py:390
  376.4 47.5 %experts.3 = (bf16[512,4096]{1,0:T(8,128)(2,1)}, bf16[512,4096]{1,0:T(8,128)(2,1)}, bf16[512,4096]{1,0:T(8,128)(2,1)}, bf16[512,2176]{1,0:T(8,128)(2,1)}) custom-call(bf16[512,2048]{1,0:T(8,128)(2,1)} %all-gather.5.cloned.1.call-done.rows_in.refs_1_, bf16[512,4096]{1,0:T(8,128)(2,1)} %up_back.3.back, f32[512,128]{1,0:T(8,128)} %bitcast.220, ...), custom_call_target="tpu_custom_call" | custom-call | flops 53210619904 | bytes 6291456 | tf_op jit(solution)/shard_map/experts/pallas_call | solution.py:390
  433.0 5.4 collective-permute-start.14
  439.1 16.6 %wgrad.6 = (bf16[2,2048,256]{2,1,0:T(8,128)(2,1)}, bf16[2,2048,256]{2,1,0:T(8,128)(2,1)}, bf16[2,2048,256]{2,1,0:T(8,128)(2,1)}, bf16[2,2048,256]{2,1,0:T(8,128)(2,1)}) custom-call(s32[8]{0:T(128)} %add.279.order, bf16[512,2048]{1,0:T(8,128)(2,1)} %join.5.rows_in.refs_0_, bf16[512,2048]{1,0:T(8,128)(2,1)} %all-gather.5.cloned.1.call-done.rows_in.refs_1_, ...), custom_call_target="tpu_custom_call" | custom-call | flops 3865470464 | bytes 2621440 | tf_op jit(solution)/shard_map/wgrad/pallas_call | solution.py:451
  455.7 16.4 %collective-permute-done.15.refs_3_ = bf16[128,2048]{1,0:T(8,128)(2,1)} collective-permute-done((bf16[128,2048]{1,0:T(8,128)(2,1)}, bf16[128,2048]{1,0:T(8,128)(2,1)}, u32[]{:S(2)}, u32[]{:S(2)}) %collective-permute-start.15) | collective-permute-done | bytes 524320 | tf_op jit(solution)/shard_map/ppermute | solution.py:547
  476.3 16.7 %wgrad.7 = (bf16[2,2048,256]{2,1,0:T(8,128)(2,1)}, bf16[2,2048,256]{2,1,0:T(8,128)(2,1)}, bf16[2,2048,256]{2,1,0:T(8,128)(2,1)}, bf16[2,2048,256]{2,1,0:T(8,128)(2,1)}) custom-call(s32[8]{0:T(128)} %add.279.order, bf16[512,2048]{1,0:T(8,128)(2,1)} %join.5.rows_in.refs_0_, bf16[512,2048]{1,0:T(8,128)(2,1)} %all-gather.5.cloned.1.call-done.rows_in.refs_1_, ...), custom_call_target="tpu_custom_call" | custom-call | flops 3865470464 | bytes 2621440 | tf_op jit(solution)/shard_map/wgrad/pallas_call | solution.py:451
  500.7 15.3 %down.2 = bf16[512,2048]{1,0:T(8,128)(2,1)} custom-call(bf16[512,4096]{1,0:T(8,128)(2,1)} %get-tuple-element.140.act.refs_2_, bf16[16,2048,256]{2,1,0:T(8,128)(2,1)} %down_w.7), custom_call_target="tpu_custom_call" | custom-call | flops 3865470464 | bytes 2359296 | tf_op jit(solution)/shard_map/down/pallas_call | solution.py:477
  516.2 4.6 join.6.refs_1_
  520.8 3.7 convolution_convert_fusion.3
  532.7 17.5 %wgrad.8 = (bf16[8,1024,256]{2,1,0:T(8,128)(2,1)}, bf16[8,1024,256]{2,1,0:T(8,128)(2,1)}) custom-call(s32[8]{0:T(128)} %add.287.order, bf16[512,2048]{1,0:T(8,128)(2,1)} %join.5.rows_in.refs_0_, bf16[512,2048]{1,0:T(8,128)(2,1)} %all-gather.5.cloned.1.call-done.rows_in.refs_1_, bf16[512,4096]{1,0:T(8,128)(2,1)} %get-tuple-element.123.refs_2_, ...), custom_call_target="tpu_custom_call" | custom-call | flops 3865470464 | bytes 2621440 | tf_op jit(solution)/shard_map/wgrad/pallas_call | solution.py:451
  550.2 3.2 slice_bitcast_fusion.5
  553.4 17.3 %collective-permute-done.21.refs_3_ = bf16[128,2048]{1,0:T(8,128)(2,1)S(1)} collective-permute-done((bf16[128,2048]{1,0:T(8,128)(2,1)S(1)}, bf16[128,2048]{1,0:T(8,128)(2,1)S(1)}, u32[]{:S(2)}, u32[]{:S(2)}) %collective-permute-start.21) | collective-permute-done | bytes 524320 | tf_op jit(solution)/shard_map/ppermute | solution.py:547
  570.7 15.3 %collective-permute-start.20 = (bf16[128,2048]{1,0:T(8,128)(2,1)S(1)}, bf16[128,2048]{1,0:T(8,128)(2,1)S(1)}, u32[]{:S(2)}, u32[]{:S(2)}) collective-permute-start(bf16[128,2048]{1,0:T(8,128)(2,1)S(1)} %get-tuple-element.190.own), channel_id=1, source_target_pairs={{0,1},{1,2},{2,3},{4,5},{5,6},{6,7},{8,9},{9,10},{10,11},{12,13},{... | collective-permute-start | bytes 1572872 | tf_op jit(solution)/shard_map/ppermute | solution.py:546
  589.6 7.5 collective-permute-done.20.refs_0_
  603.0 17.5 %wgrad.9 = (bf16[8,1024,256]{2,1,0:T(8,128)(2,1)}, bf16[8,1024,256]{2,1,0:T(8,128)(2,1)}) custom-call(s32[8]{0:T(128)} %add.287.order, bf16[512,2048]{1,0:T(8,128)(2,1)} %join.5.rows_in.refs_0_, bf16[512,2048]{1,0:T(8,128)(2,1)} %all-gather.5.cloned.1.call-done.rows_in.refs_1_, bf16[512,4096]{1,0:T(8,128)(2,1)} %get-tuple-element.132.refs_2_, ...), custom_call_target="tpu_custom_call" | custom-call | flops 3865470464 | bytes 2621440 | tf_op jit(solution)/shard_map/wgrad/pallas_call | solution.py:451
  620.5 4.7 fusion.40
  630.2 15.3 %down.3 = bf16[512,2048]{1,0:T(8,128)(2,1)} custom-call(bf16[512,4096]{1,0:T(8,128)(2,1)} %get-tuple-element.153.act.refs_3_, bf16[16,2048,256]{2,1,0:T(8,128)(2,1)} %down_w.7), custom_call_target="tpu_custom_call" | custom-call | flops 3865470464 | bytes 2359296 | tf_op jit(solution)/shard_map/down/pallas_call | solution.py:477
  647.7 4.6 join.7.refs_2_
  652.3 2.9 convolution_convert_fusion.2
  656.3 23.8 %attend_back.1 = (f32[1024,512]{1,0:T(8,128)}, f32[1024,512]{1,0:T(8,128)}, bf16[1024,512]{1,0:T(8,128)(2,1)}, f32[1024,1]{1,0:T(8,128)}, f32[1024,1]{1,0:T(8,128)}, /*index=5*/f32[1,512]{1,0:T(1,128)}, f32[1,512]{1,0:T(1,128)}) custom-call(bf16[1024,512]{1,0:T(8,128)(2,1)} %get-tuple-element.154.query, bf16[1024,512]{1,0:T(8,128)(2,1)} %get-tuple-element.155.key, ...), custom_call_target="tpu_custom_call" | custom-call | flops 58435043328 | bytes 2097152 | tf_op jit(solution)/shard_map/attend_back/pallas_call | solution.py:299
  682.6 5.6 collective-permute-start.34
  690.3 4.0 collective-permute-start.35
  696.1 2.7 fusion.4
  704.8 2.7 fusion.5
  707.5 17.0 %wgrad.10 = (bf16[2,2048,256]{2,1,0:T(8,128)(2,1)}, bf16[2,2048,256]{2,1,0:T(8,128)(2,1)}, bf16[2,2048,256]{2,1,0:T(8,128)(2,1)}, bf16[2,2048,256]{2,1,0:T(8,128)(2,1)}) custom-call(s32[8]{0:T(128)} %add.279.order, bf16[512,2048]{1,0:T(8,128)(2,1)} %bitcast.190, bf16[512,2048]{1,0:T(8,128)(2,1)} %bitcast.187, ...), custom_call_target="tpu_custom_call" | custom-call | flops 3865470464 | bytes 2621440 | tf_op jit(solution)/shard_map/wgrad/pallas_call | solution.py:451
  725.6 13.8 %project_back.1 = (bf16[1024,2048]{1,0:T(8,128)(2,1)}, bf16[1024,512]{1,0:T(8,128)(2,1)}, bf16[1024,512]{1,0:T(8,128)(2,1)}, f32[1,2048]{1,0:T(1,128)}) custom-call(bf16[1024,2048]{1,0:T(8,128)(2,1)} %all-gather.3.cloned.1.call-done.rows_in.refs_0_, f32[1024,512]{1,0:T(8,128)} %get-tuple-element.158.dqn, f32[1024,512]{1,0:T(8,128)} %get-tuple-element.159.dkn, ...), custom_call_target="tpu_custom_call" | custom-call | flops 2899102976 | bytes 1310720 | tf_op jit(solution)/shard_map/project_back/pallas_call | solution.py:142
  742.3 2.8 fusion.3
  753.3 12.9 %collective-permute-done.54 = bf16[1,2,1024,256]{3,2,1,0:T(8,128)(2,1)S(1)} collective-permute-done((bf16[1,2,1024,256]{3,2,1,0:T(8,128)(2,1)}, bf16[1,2,1024,256]{3,2,1,0:T(8,128)(2,1)S(1)}, u32[]{:S(2)}, u32[]{:S(2)}) %collective-permute-start.54) | collective-permute-done | bytes 1048608 | tf_op jit(solution)/shard_map/ppermute | solution.py:563
  770.7 17.7 %wgrad.11 = (bf16[8,1024,256]{2,1,0:T(8,128)(2,1)}, bf16[8,1024,256]{2,1,0:T(8,128)(2,1)}) custom-call(s32[8]{0:T(128)} %add.287.order, bf16[512,2048]{1,0:T(8,128)(2,1)} %bitcast.191, bf16[512,2048]{1,0:T(8,128)(2,1)} %bitcast.188, bf16[512,4096]{1,0:T(8,128)(2,1)} %get-tuple-element.140.act.refs_2_, bf16[512,4096]{1,0:T(8,128)(2,1)} %get-tuple-element.153.act.refs_3_, ...), custom_call_target="tpu_custom_call" | custom-call | flops 3865470464 | bytes 2621440 | tf_op jit(solution)/shard_map/wgrad/pallas_call | solution.py:451
  788.3 9.7 %attention_wgrad.2 = bf16[4,4,256,512]{3,2,1,0:T(8,128)(2,1)} custom-call(s32[4]{0:T(128)} %get-tuple-element.173.order, bf16[1024,2048]{1,0:T(8,128)(2,1)} %all-gather.3.cloned.1.call-done.rows_in.refs_0_, bf16[512,2048]{1,0:T(8,128)(2,1)} %join.6.refs_1_, bf16[512,2048]{1,0:T(8,128)(2,1)} %join.7.refs_2_, bf16[1024,512]{1,0:T(8,128)(2,1)} %get-tuple-element.174.refs_3_, ...), custom_call_target="tpu_custom_call" | custom-call | flops 3865470464 | bytes 524288 | tf_op jit(solution)/shard_map/attention_wgrad/pallas_call | solution.py:182
  802.3 3.2 collective-permute-done.49
  807.9 4.6 collective-permute-done.50
  816.2 2.7 collective-permute-done.51
  824.7 3.6 collective-permute-start.53
  830.5 4.0 collective-permute-done.53
  837.0 25.6 %collective-permute-done.60 = bf16[2,2,1024,256]{3,2,1,0:T(8,128)(2,1)} collective-permute-done((bf16[2,2,1024,256]{3,2,1,0:T(8,128)(2,1)}, bf16[2,2,1024,256]{3,2,1,0:T(8,128)(2,1)}, u32[]{:S(2)}, u32[]{:S(2)}) %collective-permute-start.60) | collective-permute-done | bytes 2097184 | tf_op jit(solution)/shard_map/ppermute | solution.py:563
  862.6 2.7 fusion.6
  872.4 10.6 %attention_wgrad.3 = (bf16[4,4,128,512]{3,2,1,0:T(8,128)(2,1)}, bf16[4,4,128,512]{3,2,1,0:T(8,128)(2,1)}) custom-call(s32[4]{0:T(128)} %get-tuple-element.176.order, bf16[1024,2048]{1,0:T(8,128)(2,1)} %all-gather.3.cloned.1.call-done.rows_in.refs_0_, bf16[512,2048]{1,0:T(8,128)(2,1)} %join.6.refs_1_, bf16[512,2048]{1,0:T(8,128)(2,1)} %join.7.refs_2_, ...), custom_call_target="tpu_custom_call" | custom-call | flops 3865470464 | bytes 524288 | tf_op jit(solution)/shard_map/attention_wgrad/pallas_call | solution.py:182
  889.5 3.2 collective-permute-done.61
  894.3 3.9 collective-permute-done.59
  899.6 13.3 %collective-permute-done.45 = bf16[2,4,128,512]{3,2,1,0:T(8,128)(2,1)S(1)} collective-permute-done((bf16[2,4,128,512]{3,2,1,0:T(8,128)(2,1)S(1)}, bf16[2,4,128,512]{3,2,1,0:T(8,128)(2,1)S(1)}, u32[]{:S(2)}, u32[]{:S(2)}) %collective-permute-start.45) | collective-permute-done | bytes 1048608 | tf_op jit(solution)/shard_map/ppermute | solution.py:563
  914.0 4.7 collective-permute-done.47
  922.0 5.6 collective-permute-done.46
  932.2 3.2 maximum_add_fusion
  (336 shorter events, 164.9 us)
Async XLA Ops:
  7.2 89.0 %all-gather.3.cloned.1.call-start = ((), (), s32[]{:S(2)}) async-start(), calls=%async_computation.7 | async-start | bytes 5242880 | tf_op jit(solution)/shard_map/all_gather | solution.py:494
  12.6 252.6 %reduce-scatter.8.cloned.1.call-start = ((), (), s32[]{:S(2)}) async-start(), calls=%async_computation.8 | async-start | bytes 2621440 | tf_op jit(solution)/shard_map/reduce_scatter | solution.py:498
  96.2 50.7 %collective-permute-start.3 = (bf16[256,2048]{1,0:T(8,128)(2,1)S(1)}, bf16[256,2048]{1,0:T(8,128)(2,1)}, u32[]{:S(2)}, u32[]{:S(2)}) collective-permute-start(bf16[256,2048]{1,0:T(8,128)(2,1)S(1)} %copy-done.19), channel_id=1, source_target_pairs={{1,0},{2,1},{3,2},{5,4},{6,5},{7,6},{9,8},{10,9},{11,10},{13,12},{... | collective-permute-start | bytes 3145736 | tf_op jit(solution)/shard_map/ppermute | solution.py:547
  97.5 49.4 %collective-permute-start.2 = (bf16[256,2048]{1,0:T(8,128)(2,1)S(1)}, bf16[256,2048]{1,0:T(8,128)(2,1)}, u32[]{:S(2)}, u32[]{:S(2)}) collective-permute-start(bf16[256,2048]{1,0:T(8,128)(2,1)S(1)} %copy-done.19), channel_id=1, source_target_pairs={{0,1},{1,2},{2,3},{4,5},{5,6},{6,7},{8,9},{9,10},{10,11},{12,13},{... | collective-permute-start | bytes 3145736 | tf_op jit(solution)/shard_map/ppermute | solution.py:546
  148.0 24.1 %collective-permute-start.5 = (bf16[256,2048]{1,0:T(8,128)(2,1)}, bf16[256,2048]{1,0:T(8,128)(2,1)S(1)}, u32[]{:S(2)}, u32[]{:S(2)}) collective-permute-start(bf16[256,2048]{1,0:T(8,128)(2,1)} %collective-permute-done.3.refs_3_), channel_id=1, source_target_pairs={{1,0},{2,1},{5,4},{6,5},{9,8},{10,9},{13,12},{14,13},{17,16},{18,1... | collective-permute-start | bytes 3145736 | tf_op jit(solution)/shard_map/ppermute | solution.py:547
  149.3 22.9 %collective-permute-start.4 = (bf16[256,2048]{1,0:T(8,128)(2,1)}, bf16[256,2048]{1,0:T(8,128)(2,1)S(1)}, u32[]{:S(2)}, u32[]{:S(2)}) collective-permute-start(bf16[256,2048]{1,0:T(8,128)(2,1)} %collective-permute-done.2.refs_0_), channel_id=1, source_target_pairs={{1,2},{2,3},{5,6},{6,7},{9,10},{10,11},{13,14},{14,15},{17,18},{18... | collective-permute-start | bytes 3145736 | tf_op jit(solution)/shard_map/ppermute | solution.py:546
  177.4 117.0 %reduce-scatter.12.cloned.1.call-start = ((), (), s32[]{:S(2)}) async-start(), calls=%async_computation.10 | async-start | bytes 2621440 | tf_op jit(solution)/shard_map/reduce_scatter | solution.py:498
  180.1 196.3 %all-gather.5.cloned.1.call-start = ((), (), s32[]{:S(2)}) async-start(), calls=%async_computation.11 | async-start | bytes 2621440 | tf_op jit(solution)/shard_map/all_gather | solution.py:494
  181.9 57.0 %collective-permute-start.7 = (bf16[256,2048]{1,0:T(8,128)(2,1)}, bf16[256,2048]{1,0:T(8,128)(2,1)}, u32[]{:S(2)}, u32[]{:S(2)}) collective-permute-start(bf16[256,2048]{1,0:T(8,128)(2,1)} %copy-done.37), channel_id=1, source_target_pairs={{1,0},{5,4},{9,8},{13,12},{17,16},{21,20},{25,24},{29,28}} | collective-permute-start | bytes 3145736 | tf_op jit(solution)/shard_map/ppermute | solution.py:547
  267.0 23.8 %collective-permute-start.9 = (bf16[128,2048]{1,0:T(8,128)(2,1)S(1)}, bf16[128,2048]{1,0:T(8,128)(2,1)}, u32[]{:S(2)}, u32[]{:S(2)}) collective-permute-start(bf16[128,2048]{1,0:T(8,128)(2,1)S(1)} %multiply_convert_fusion.2.own), channel_id=1, source_target_pairs={{1,0},{2,1},{3,2},{5,4},{6,5},{7,6},{9,8},{10,9},{11,10},{13,12},{... | collective-permute-start | bytes 1572872 | tf_op jit(solution)/shard_map/ppermute | solution.py:547
  268.3 22.5 %collective-permute-start.8 = (bf16[128,2048]{1,0:T(8,128)(2,1)S(1)}, bf16[128,2048]{1,0:T(8,128)(2,1)}, u32[]{:S(2)}, u32[]{:S(2)}) collective-permute-start(bf16[128,2048]{1,0:T(8,128)(2,1)S(1)} %multiply_convert_fusion.2.own), channel_id=1, source_target_pairs={{0,1},{1,2},{2,3},{4,5},{5,6},{6,7},{8,9},{9,10},{10,11},{12,13},{... | collective-permute-start | bytes 1572872 | tf_op jit(solution)/shard_map/ppermute | solution.py:546
  292.2 17.7 %collective-permute-start.12 = (bf16[128,2048]{1,0:T(8,128)(2,1)}, bf16[128,2048]{1,0:T(8,128)(2,1)}, u32[]{:S(2)}, u32[]{:S(2)}) collective-permute-start(bf16[128,2048]{1,0:T(8,128)(2,1)} %collective-permute-done.9.refs_3_), channel_id=1, source_target_pairs={{1,0},{2,1},{5,4},{6,5},{9,8},{10,9},{13,12},{14,13},{17,16},{18,1... | collective-permute-start | bytes 1572872 | tf_op jit(solution)/shard_map/ppermute | solution.py:547
  296.0 16.3 %collective-permute-start.11 = (bf16[128,2048]{1,0:T(8,128)(2,1)}, bf16[128,2048]{1,0:T(8,128)(2,1)}, u32[]{:S(2)}, u32[]{:S(2)}) collective-permute-start(bf16[128,2048]{1,0:T(8,128)(2,1)} %collective-permute-done.10.refs_1_), channel_id=1, source_target_pairs={{2,3},{6,7},{10,11},{14,15},{18,19},{22,23},{26,27},{30,31}} | collective-permute-start | bytes 1572872 | tf_op jit(solution)/shard_map/ppermute | solution.py:546
  309.9 14.2 %collective-permute-start.13 = (bf16[128,2048]{1,0:T(8,128)(2,1)}, bf16[128,2048]{1,0:T(8,128)(2,1)}, u32[]{:S(2)}, u32[]{:S(2)}) collective-permute-start(bf16[128,2048]{1,0:T(8,128)(2,1)} %collective-permute-done.12.refs_4_), channel_id=1, source_target_pairs={{1,0},{5,4},{9,8},{13,12},{17,16},{21,20},{25,24},{29,28}} | collective-permute-start | bytes 1572872 | tf_op jit(solution)/shard_map/ppermute | solution.py:547
  312.2 114.1 %reduce-scatter.10.cloned.1.call-start = ((), (), s32[]{:S(2)}) async-start(), calls=%async_computation.9 | async-start | bytes 2785280 | tf_op jit(solution)/shard_map/reduce_scatter | solution.py:498
  376.3 148.2 %reduce-scatter.16.cloned.1.call-start = ((), (), s32[]{:S(2)}) async-start(), calls=%async_computation.13 | async-start | bytes 2785280 | tf_op jit(solution)/shard_map/reduce_scatter | solution.py:498
  423.9 374.2 %reduce-scatter.14.cloned.1.call-start = ((), (), s32[]{:S(2)}) async-start(), calls=%async_computation.12 | async-start | bytes 2621440 | tf_op jit(solution)/shard_map/reduce_scatter | solution.py:498
  431.7 40.4 %collective-permute-start.15 = (bf16[128,2048]{1,0:T(8,128)(2,1)}, bf16[128,2048]{1,0:T(8,128)(2,1)}, u32[]{:S(2)}, u32[]{:S(2)}) collective-permute-start(bf16[128,2048]{1,0:T(8,128)(2,1)} %get-tuple-element.194.own), channel_id=1, source_target_pairs={{1,0},{2,1},{3,2},{5,4},{6,5},{7,6},{9,8},{10,9},{11,10},{13,12},{... | collective-permute-start | bytes 1572872 | tf_op jit(solution)/shard_map/ppermute | solution.py:547
  433.0 39.1 %collective-permute-start.14 = (bf16[128,2048]{1,0:T(8,128)(2,1)}, bf16[128,2048]{1,0:T(8,128)(2,1)}, u32[]{:S(2)}, u32[]{:S(2)}) collective-permute-start(bf16[128,2048]{1,0:T(8,128)(2,1)} %get-tuple-element.194.own), channel_id=1, source_target_pairs={{0,1},{1,2},{2,3},{4,5},{5,6},{6,7},{8,9},{9,10},{10,11},{12,13},{... | collective-permute-start | bytes 1572872 | tf_op jit(solution)/shard_map/ppermute | solution.py:546
  472.1 20.8 %collective-permute-start.16 = (bf16[128,2048]{1,0:T(8,128)(2,1)}, bf16[128,2048]{1,0:T(8,128)(2,1)}, u32[]{:S(2)}, u32[]{:S(2)}) collective-permute-start(bf16[128,2048]{1,0:T(8,128)(2,1)} %collective-permute-done.14.refs_0_), channel_id=1, source_target_pairs={{1,2},{2,3},{5,6},{6,7},{9,10},{10,11},{13,14},{14,15},{17,18},{18... | collective-permute-start | bytes 1572872 | tf_op jit(solution)/shard_map/ppermute | solution.py:546
  473.6 19.4 %collective-permute-start.17 = (bf16[128,2048]{1,0:T(8,128)(2,1)}, bf16[128,2048]{1,0:T(8,128)(2,1)}, u32[]{:S(2)}, u32[]{:S(2)}) collective-permute-start(bf16[128,2048]{1,0:T(8,128)(2,1)} %collective-permute-done.15.refs_3_), channel_id=1, source_target_pairs={{1,0},{2,1},{5,4},{6,5},{9,8},{10,9},{13,12},{14,13},{17,16},{18,1... | collective-permute-start | bytes 1572872 | tf_op jit(solution)/shard_map/ppermute | solution.py:547
  475.8 52.9 %collective-permute-start.22 = (bf16[2,2048,256]{2,1,0:T(8,128)(2,1)}, bf16[2,2048,256]{2,1,0:T(8,128)(2,1)}, u32[]{:S(2)}, u32[]{:S(2)}) collective-permute-start(bf16[2,2048,256]{2,1,0:T(8,128)(2,1)} %get-tuple-element.125), channel_id=1, source_target_pairs={{0,4},{4,0},{8,12},{12,8},{16,20},{20,16},{24,28},{28,24},{1,5},{5... | collective-permute-start | bytes 6291464 | tf_op jit(solution)/shard_map/ppermute | solution.py:563
  475.8 53.4 %collective-permute-start.23 = (bf16[2,2048,256]{2,1,0:T(8,128)(2,1)}, bf16[2,2048,256]{2,1,0:T(8,128)(2,1)}, u32[]{:S(2)}, u32[]{:S(2)}) collective-permute-start(bf16[2,2048,256]{2,1,0:T(8,128)(2,1)} %get-tuple-element.126), channel_id=1, source_target_pairs={{0,4},{4,0},{8,12},{12,8},{16,20},{20,16},{24,28},{28,24},{1,5},{5... | collective-permute-start | bytes 6291464 | tf_op jit(solution)/shard_map/ppermute | solution.py:563
  476.3 53.0 %collective-permute-start.24 = (bf16[2,2048,256]{2,1,0:T(8,128)(2,1)}, bf16[2,2048,256]{2,1,0:T(8,128)(2,1)}, u32[]{:S(2)}, u32[]{:S(2)}) collective-permute-start(bf16[2,2048,256]{2,1,0:T(8,128)(2,1)} %get-tuple-element.127), channel_id=1, source_target_pairs={{0,4},{4,0},{8,12},{12,8},{16,20},{20,16},{24,28},{28,24},{1,5},{5... | collective-permute-start | bytes 6291464 | tf_op jit(solution)/shard_map/ppermute | solution.py:563
  496.7 34.5 %collective-permute-start.25 = (bf16[2,2048,256]{2,1,0:T(8,128)(2,1)}, bf16[2,2048,256]{2,1,0:T(8,128)(2,1)}, u32[]{:S(2)}, u32[]{:S(2)}) collective-permute-start(bf16[2,2048,256]{2,1,0:T(8,128)(2,1)} %get-tuple-element.128), channel_id=1, source_target_pairs={{0,4},{4,0},{8,12},{12,8},{16,20},{20,16},{24,28},{28,24},{1,5},{5... | collective-permute-start | bytes 6291464 | tf_op jit(solution)/shard_map/ppermute | solution.py:563
  497.3 18.8 %collective-permute-start.19 = (bf16[128,2048]{1,0:T(8,128)(2,1)}, bf16[128,2048]{1,0:T(8,128)(2,1)}, u32[]{:S(2)}, u32[]{:S(2)}) collective-permute-start(bf16[128,2048]{1,0:T(8,128)(2,1)} %collective-permute-done.17.refs_4_), channel_id=1, source_target_pairs={{1,0},{5,4},{9,8},{13,12},{17,16},{21,20},{25,24},{29,28}} | collective-permute-start | bytes 1572872 | tf_op jit(solution)/shard_map/ppermute | solution.py:547
  516.1 319.7 %reduce-scatter.18.cloned.1.call-start = ((), (), s32[]{:S(2)}) async-start(), calls=%async_computation.14 | async-start | bytes 2621440 | tf_op jit(solution)/shard_map/reduce_scatter | solution.py:498
  516.1 82.6 %collective-permute-start.28 = (bf16[2,2048,256]{2,1,0:T(8,128)(2,1)}, bf16[2,2048,256]{2,1,0:T(8,128)(2,1)}, u32[]{:S(2)}, u32[]{:S(2)}) collective-permute-start(bf16[2,2048,256]{2,1,0:T(8,128)(2,1)} %get-tuple-element.134), channel_id=1, source_target_pairs={{0,4},{4,0},{8,12},{12,8},{16,20},{20,16},{24,28},{28,24},{1,5},{5... | collective-permute-start | bytes 6291464 | tf_op jit(solution)/shard_map/ppermute | solution.py:563
  528.6 71.6 %collective-permute-start.29 = (bf16[2,2048,256]{2,1,0:T(8,128)(2,1)}, bf16[2,2048,256]{2,1,0:T(8,128)(2,1)S(1)}, u32[]{:S(2)}, u32[]{:S(2)}) collective-permute-start(bf16[2,2048,256]{2,1,0:T(8,128)(2,1)} %get-tuple-element.135), channel_id=1, source_target_pairs={{0,4},{4,0},{8,12},{12,8},{16,20},{20,16},{24,28},{28,24},{1,5},{5... | collective-permute-start | bytes 6291464 | tf_op jit(solution)/shard_map/ppermute | solution.py:563
  529.2 72.5 %collective-permute-start.30 = (bf16[2,2048,256]{2,1,0:T(8,128)(2,1)}, bf16[2,2048,256]{2,1,0:T(8,128)(2,1)}, u32[]{:S(2)}, u32[]{:S(2)}) collective-permute-start(bf16[2,2048,256]{2,1,0:T(8,128)(2,1)} %get-tuple-element.136), channel_id=1, source_target_pairs={{0,4},{4,0},{8,12},{12,8},{16,20},{20,16},{24,28},{28,24},{1,5},{5... | collective-permute-start | bytes 6291464 | tf_op jit(solution)/shard_map/ppermute | solution.py:563
  529.3 73.7 %collective-permute-start.31 = (bf16[2,2048,256]{2,1,0:T(8,128)(2,1)}, bf16[2,2048,256]{2,1,0:T(8,128)(2,1)}, u32[]{:S(2)}, u32[]{:S(2)}) collective-permute-start(bf16[2,2048,256]{2,1,0:T(8,128)(2,1)} %get-tuple-element.137), channel_id=1, source_target_pairs={{0,4},{4,0},{8,12},{12,8},{16,20},{20,16},{24,28},{28,24},{1,5},{5... | collective-permute-start | bytes 6291464 | tf_op jit(solution)/shard_map/ppermute | solution.py:563
  531.2 39.5 %collective-permute-start.21 = (bf16[128,2048]{1,0:T(8,128)(2,1)S(1)}, bf16[128,2048]{1,0:T(8,128)(2,1)S(1)}, u32[]{:S(2)}, u32[]{:S(2)}) collective-permute-start(bf16[128,2048]{1,0:T(8,128)(2,1)S(1)} %get-tuple-element.190.own), channel_id=1, source_target_pairs={{1,0},{2,1},{3,2},{5,4},{6,5},{7,6},{9,8},{10,9},{11,10},{13,12},{... | collective-permute-start | bytes 1572872 | tf_op jit(solution)/shard_map/ppermute | solution.py:547
  570.7 26.4 %collective-permute-start.20 = (bf16[128,2048]{1,0:T(8,128)(2,1)S(1)}, bf16[128,2048]{1,0:T(8,128)(2,1)S(1)}, u32[]{:S(2)}, u32[]{:S(2)}) collective-permute-start(bf16[128,2048]{1,0:T(8,128)(2,1)S(1)} %get-tuple-element.190.own), channel_id=1, source_target_pairs={{0,1},{1,2},{2,3},{4,5},{5,6},{6,7},{8,9},{9,10},{10,11},{12,13},{... | collective-permute-start | bytes 1572872 | tf_op jit(solution)/shard_map/ppermute | solution.py:546
  597.1 98.9 %collective-permute-start.37 = (bf16[2,2,1024,256]{3,2,1,0:T(8,128)(2,1)}, bf16[2,2,1024,256]{3,2,1,0:T(8,128)(2,1)}, u32[]{:S(2)}, u32[]{:S(2)}) collective-permute-start(bf16[2,2,1024,256]{3,2,1,0:T(8,128)(2,1)} %slice_bitcast_fusion.5), channel_id=1, source_target_pairs={{0,8},{4,12},{8,0},{12,4},{16,24},{20,28},{24,16},{28,20},{1,9},{5... | collective-permute-start | bytes 6291464 | tf_op jit(solution)/shard_map/ppermute | solution.py:563
  598.7 106.1 %collective-permute-start.36 = (bf16[2,2,1024,256]{3,2,1,0:T(8,128)(2,1)}, bf16[2,2,1024,256]{3,2,1,0:T(8,128)(2,1)}, u32[]{:S(2)}, u32[]{:S(2)}) collective-permute-start(bf16[2,2,1024,256]{3,2,1,0:T(8,128)(2,1)} %bitcast.16), channel_id=1, source_target_pairs={{0,16},{4,20},{8,24},{12,28},{16,0},{20,4},{24,8},{28,12},{1,17},{... | collective-permute-start | bytes 6291464 | tf_op jit(solution)/shard_map/ppermute | solution.py:563
  600.2 25.0 %collective-permute-start.26 = (bf16[128,2048]{1,0:T(8,128)(2,1)S(1)}, bf16[128,2048]{1,0:T(8,128)(2,1)}, u32[]{:S(2)}, u32[]{:S(2)}) collective-permute-start(bf16[128,2048]{1,0:T(8,128)(2,1)S(1)} %collective-permute-done.20.refs_0_), channel_id=1, source_target_pairs={{1,2},{2,3},{5,6},{6,7},{9,10},{10,11},{13,14},{14,15},{17,18},{18... | collective-permute-start | bytes 1572872 | tf_op jit(solution)/shard_map/ppermute | solution.py:546
  601.7 23.5 %collective-permute-start.27 = (bf16[128,2048]{1,0:T(8,128)(2,1)S(1)}, bf16[128,2048]{1,0:T(8,128)(2,1)}, u32[]{:S(2)}, u32[]{:S(2)}) collective-permute-start(bf16[128,2048]{1,0:T(8,128)(2,1)S(1)} %collective-permute-done.21.refs_3_), channel_id=1, source_target_pairs={{1,0},{2,1},{5,4},{6,5},{9,8},{10,9},{13,12},{14,13},{17,16},{18,1... | collective-permute-start | bytes 1572872 | tf_op jit(solution)/shard_map/ppermute | solution.py:547
  625.2 22.1 %collective-permute-start.32 = (bf16[128,2048]{1,0:T(8,128)(2,1)}, bf16[128,2048]{1,0:T(8,128)(2,1)}, u32[]{:S(2)}, u32[]{:S(2)}) collective-permute-start(bf16[128,2048]{1,0:T(8,128)(2,1)} %collective-permute-done.26.refs_1_), channel_id=1, source_target_pairs={{2,3},{6,7},{10,11},{14,15},{18,19},{22,23},{26,27},{30,31}} | collective-permute-start | bytes 1572872 | tf_op jit(solution)/shard_map/ppermute | solution.py:546
  626.6 21.1 %collective-permute-start.33 = (bf16[128,2048]{1,0:T(8,128)(2,1)}, bf16[128,2048]{1,0:T(8,128)(2,1)}, u32[]{:S(2)}, u32[]{:S(2)}) collective-permute-start(bf16[128,2048]{1,0:T(8,128)(2,1)} %collective-permute-done.27.refs_4_), channel_id=1, source_target_pairs={{1,0},{5,4},{9,8},{13,12},{17,16},{21,20},{25,24},{29,28}} | collective-permute-start | bytes 1572872 | tf_op jit(solution)/shard_map/ppermute | solution.py:547
  629.6 95.4 %collective-permute-start.39 = (bf16[2,2,1024,256]{3,2,1,0:T(8,128)(2,1)}, bf16[2,2,1024,256]{3,2,1,0:T(8,128)(2,1)}, u32[]{:S(2)}, u32[]{:S(2)}) collective-permute-start(bf16[2,2,1024,256]{3,2,1,0:T(8,128)(2,1)} %slice_bitcast_fusion.4), channel_id=1, source_target_pairs={{0,8},{4,12},{8,0},{12,4},{16,24},{20,28},{24,16},{28,20},{1,9},{5... | collective-permute-start | bytes 6291464 | tf_op jit(solution)/shard_map/ppermute | solution.py:563
  645.6 284.3 %reduce-scatter.20.cloned.1.call-start = ((), (), s32[]{:S(2)}) async-start(), calls=%async_computation.15 | async-start | bytes 5242880 | tf_op jit(solution)/shard_map/reduce_scatter | solution.py:498
  647.2 77.9 %collective-permute-start.38 = (bf16[2,2,1024,256]{3,2,1,0:T(8,128)(2,1)}, bf16[2,2,1024,256]{3,2,1,0:T(8,128)(2,1)}, u32[]{:S(2)}, u32[]{:S(2)}) collective-permute-start(bf16[2,2,1024,256]{3,2,1,0:T(8,128)(2,1)} %bitcast.215), channel_id=1, source_target_pairs={{0,16},{4,20},{8,24},{12,28},{16,0},{20,4},{24,8},{28,12},{1,17},{... | collective-permute-start | bytes 6291464 | tf_op jit(solution)/shard_map/ppermute | solution.py:563
  682.6 7.7 collective-permute-start.34
  701.2 39.6 %collective-permute-start.55 = (bf16[1,2,1024,256]{3,2,1,0:T(8,128)(2,1)}, bf16[1,2,1024,256]{3,2,1,0:T(8,128)(2,1)}, u32[]{:S(2)}, u32[]{:S(2)}) collective-permute-start(bf16[1,2,1024,256]{3,2,1,0:T(8,128)(2,1)} %slice_bitcast_fusion.10), channel_id=1, source_target_pairs={{0,16},{4,20},{8,24},{12,28},{16,0},{20,4},{24,8},{28,12},{1,17},{... | collective-permute-start | bytes 3145736 | tf_op jit(solution)/shard_map/ppermute | solution.py:563
  724.6 44.5 %collective-permute-start.40 = (bf16[2,2048,256]{2,1,0:T(8,128)(2,1)}, bf16[2,2048,256]{2,1,0:T(8,128)(2,1)}, u32[]{:S(2)}, u32[]{:S(2)}) collective-permute-start(bf16[2,2048,256]{2,1,0:T(8,128)(2,1)} %get-tuple-element.164), channel_id=1, source_target_pairs={{0,4},{4,0},{8,12},{12,8},{16,20},{20,16},{24,28},{28,24},{1,5},{5... | collective-permute-start | bytes 6291464 | tf_op jit(solution)/shard_map/ppermute | solution.py:563
  724.6 46.1 %collective-permute-start.41 = (bf16[2,2048,256]{2,1,0:T(8,128)(2,1)}, bf16[2,2048,256]{2,1,0:T(8,128)(2,1)}, u32[]{:S(2)}, u32[]{:S(2)}) collective-permute-start(bf16[2,2048,256]{2,1,0:T(8,128)(2,1)} %get-tuple-element.165), channel_id=1, source_target_pairs={{0,4},{4,0},{8,12},{12,8},{16,20},{20,16},{24,28},{28,24},{1,5},{5... | collective-permute-start | bytes 6291464 | tf_op jit(solution)/shard_map/ppermute | solution.py:563
  725.1 45.6 %collective-permute-start.42 = (bf16[2,2048,256]{2,1,0:T(8,128)(2,1)}, bf16[2,2048,256]{2,1,0:T(8,128)(2,1)}, u32[]{:S(2)}, u32[]{:S(2)}) collective-permute-start(bf16[2,2048,256]{2,1,0:T(8,128)(2,1)} %get-tuple-element.166), channel_id=1, source_target_pairs={{0,4},{4,0},{8,12},{12,8},{16,20},{20,16},{24,28},{28,24},{1,5},{5... | collective-permute-start | bytes 6291464 | tf_op jit(solution)/shard_map/ppermute | solution.py:563
  725.1 45.5 %collective-permute-start.43 = (bf16[2,2048,256]{2,1,0:T(8,128)(2,1)}, bf16[2,2048,256]{2,1,0:T(8,128)(2,1)}, u32[]{:S(2)}, u32[]{:S(2)}) collective-permute-start(bf16[2,2048,256]{2,1,0:T(8,128)(2,1)} %get-tuple-element.167), channel_id=1, source_target_pairs={{0,4},{4,0},{8,12},{12,8},{16,20},{20,16},{24,28},{28,24},{1,5},{5... | collective-permute-start | bytes 6291464 | tf_op jit(solution)/shard_map/ppermute | solution.py:563
  740.7 25.4 %collective-permute-start.54 = (bf16[1,2,1024,256]{3,2,1,0:T(8,128)(2,1)}, bf16[1,2,1024,256]{3,2,1,0:T(8,128)(2,1)S(1)}, u32[]{:S(2)}, u32[]{:S(2)}) collective-permute-start(bf16[1,2,1024,256]{3,2,1,0:T(8,128)(2,1)} %slice.278), channel_id=1, source_target_pairs={{0,8},{4,12},{8,0},{12,4},{16,24},{20,28},{24,16},{28,20},{1,9},{5... | collective-permute-start | bytes 3145736 | tf_op jit(solution)/shard_map/ppermute | solution.py:563
  766.1 34.5 %collective-permute-start.57 = (bf16[1,2,1024,256]{3,2,1,0:T(8,128)(2,1)}, bf16[1,2,1024,256]{3,2,1,0:T(8,128)(2,1)}, u32[]{:S(2)}, u32[]{:S(2)}) collective-permute-start(bf16[1,2,1024,256]{3,2,1,0:T(8,128)(2,1)} %slice_bitcast_fusion.8), channel_id=1, source_target_pairs={{0,16},{4,20},{8,24},{12,28},{16,0},{20,4},{24,8},{28,12},{1,17},{... | collective-permute-start | bytes 3145736 | tf_op jit(solution)/shard_map/ppermute | solution.py:563
  769.1 37.0 %collective-permute-start.56 = (bf16[1,2,1024,256]{3,2,1,0:T(8,128)(2,1)}, bf16[1,2,1024,256]{3,2,1,0:T(8,128)(2,1)}, u32[]{:S(2)}, u32[]{:S(2)}) collective-permute-start(bf16[1,2,1024,256]{3,2,1,0:T(8,128)(2,1)} %slice.282), channel_id=1, source_target_pairs={{0,8},{4,12},{8,0},{12,4},{16,24},{20,28},{24,16},{28,20},{1,9},{5... | collective-permute-start | bytes 3145736 | tf_op jit(solution)/shard_map/ppermute | solution.py:563
  798.1 74.3 %collective-permute-start.44 = (bf16[4,4,256,512]{3,2,1,0:T(8,128)(2,1)}, bf16[4,4,256,512]{3,2,1,0:T(8,128)(2,1)}, u32[]{:S(2)}, u32[]{:S(2)}) collective-permute-start(bf16[4,4,256,512]{3,2,1,0:T(8,128)(2,1)} %attention_wgrad.2), channel_id=1, source_target_pairs={{0,4},{4,0},{8,12},{12,8},{16,20},{20,16},{24,28},{28,24},{1,5},{5... | collective-permute-start | bytes 12582920 | tf_op jit(solution)/shard_map/ppermute | solution.py:563
  805.5 7.0 collective-permute-start.50
  812.6 6.3 collective-permute-start.51
  815.6 47.0 %collective-permute-start.60 = (bf16[2,2,1024,256]{3,2,1,0:T(8,128)(2,1)}, bf16[2,2,1024,256]{3,2,1,0:T(8,128)(2,1)}, u32[]{:S(2)}, u32[]{:S(2)}) collective-permute-start(bf16[2,2,1024,256]{3,2,1,0:T(8,128)(2,1)} %slice_bitcast_fusion), channel_id=1, source_target_pairs={{0,8},{4,12},{8,0},{12,4},{16,24},{20,28},{24,16},{28,20},{1,9},{5... | collective-permute-start | bytes 6291464 | tf_op jit(solution)/shard_map/ppermute | solution.py:563
  818.9 5.7 collective-permute-start.52
  822.0 46.6 %collective-permute-start.58 = (bf16[2,2,1024,256]{3,2,1,0:T(8,128)(2,1)}, bf16[2,2,1024,256]{3,2,1,0:T(8,128)(2,1)}, u32[]{:S(2)}, u32[]{:S(2)}) collective-permute-start(bf16[2,2,1024,256]{3,2,1,0:T(8,128)(2,1)} %bitcast.67), channel_id=1, source_target_pairs={{0,16},{4,20},{8,24},{12,28},{16,0},{20,4},{24,8},{28,12},{1,17},{... | collective-permute-start | bytes 6291464 | tf_op jit(solution)/shard_map/ppermute | solution.py:563
  824.7 9.8 %collective-permute-start.53 = (f32[20,2048]{1,0:T(8,128)S(1)}, f32[20,2048]{1,0:T(8,128)S(1)}, u32[]{:S(2)}, u32[]{:S(2)}) collective-permute-start(f32[20,2048]{1,0:T(8,128)S(1)} %add.307), channel_id=1, source_target_pairs={{0,2},{1,3},{2,0},{3,1},{4,6},{5,7},{6,4},{7,5},{8,10},{9,11},{10,... | collective-permute-start | bytes 491528 | tf_op jit(solution)/shard_map/ppermute | solution.py:614
  866.4 26.4 %collective-permute-start.61 = (bf16[1,2,1024,256]{3,2,1,0:T(8,128)(2,1)}, bf16[1,2,1024,256]{3,2,1,0:T(8,128)(2,1)}, u32[]{:S(2)}, u32[]{:S(2)}) collective-permute-start(bf16[1,2,1024,256]{3,2,1,0:T(8,128)(2,1)} %slice_bitcast_fusion.6), channel_id=1, source_target_pairs={{0,16},{4,20},{8,24},{12,28},{16,0},{20,4},{24,8},{28,12},{1,17},{... | collective-permute-start | bytes 3145736 | tf_op jit(solution)/shard_map/ppermute | solution.py:563
  871.7 26.4 %collective-permute-start.59 = (bf16[1,2,1024,256]{3,2,1,0:T(8,128)(2,1)}, bf16[1,2,1024,256]{3,2,1,0:T(8,128)(2,1)}, u32[]{:S(2)}, u32[]{:S(2)}) collective-permute-start(bf16[1,2,1024,256]{3,2,1,0:T(8,128)(2,1)} %slice.286), channel_id=1, source_target_pairs={{0,8},{4,12},{8,0},{12,4},{16,24},{20,28},{24,16},{28,20},{1,9},{5... | collective-permute-start | bytes 3145736 | tf_op jit(solution)/shard_map/ppermute | solution.py:563
  884.5 28.4 %collective-permute-start.45 = (bf16[2,4,128,512]{3,2,1,0:T(8,128)(2,1)S(1)}, bf16[2,4,128,512]{3,2,1,0:T(8,128)(2,1)S(1)}, u32[]{:S(2)}, u32[]{:S(2)}) collective-permute-start(bf16[2,4,128,512]{3,2,1,0:T(8,128)(2,1)S(1)} %slice.216), channel_id=1, source_target_pairs={{0,16},{4,20},{8,24},{12,28},{16,0},{20,4},{24,8},{28,12},{1,17},{... | collective-permute-start | bytes 3145736 | tf_op jit(solution)/shard_map/ppermute | solution.py:563
  887.1 31.6 %collective-permute-start.47 = (bf16[2,4,128,512]{3,2,1,0:T(8,128)(2,1)S(1)}, bf16[2,4,128,512]{3,2,1,0:T(8,128)(2,1)S(1)}, u32[]{:S(2)}, u32[]{:S(2)}) collective-permute-start(bf16[2,4,128,512]{3,2,1,0:T(8,128)(2,1)S(1)} %slice_bitcast_fusion.13), channel_id=1, source_target_pairs={{0,8},{4,12},{8,0},{12,4},{16,24},{20,28},{24,16},{28,20},{1,9},{5... | collective-permute-start | bytes 3145736 | tf_op jit(solution)/shard_map/ppermute | solution.py:563
  913.3 14.2 %collective-permute-start.46 = (bf16[1,4,128,512]{3,2,1,0:T(8,128)(2,1)S(1)}, bf16[1,4,128,512]{3,2,1,0:T(8,128)(2,1)S(1)}, u32[]{:S(2)}, u32[]{:S(2)}) collective-permute-start(bf16[1,4,128,512]{3,2,1,0:T(8,128)(2,1)S(1)} %slice.268), channel_id=1, source_target_pairs={{0,8},{4,12},{8,0},{12,4},{16,24},{20,28},{24,16},{28,20},{1,9},{5... | collective-permute-start | bytes 1572872 | tf_op jit(solution)/shard_map/ppermute | solution.py:563
  919.1 9.2 collective-permute-start.48
  (60 other events, 921.4 us)
Sparse Core Ops, SparseCore 0:
  12.7 83.4 all-gather.2
  177.5 59.2 reduce-scatter.7
  239.8 54.2 reduce-scatter.11
  312.3 46.9 all-gather.4
  376.4 43.9 reduce-scatter.9
  424.0 54.7 reduce-scatter.15
  516.2 70.0 reduce-scatter.13
  645.7 48.2 reduce-scatter.17
  740.6 76.3 reduce-scatter.19

commit v4 on v3

--- a/solution.py
+++ b/solution.py
@@ -2,6 +2,7 @@
 
 import jax
 import jax.numpy as jnp
+import numpy as np
 from jax import lax
 from jax.experimental import pallas as pl
 from jax.experimental.pallas import tpu as pltpu
@@ -53,11 +54,9 @@
 
 
 def rope_tables(length, width):
-    half_width = width // 2
-    frequency = jnp.power(10000.0, -jnp.arange(half_width, dtype=f32) * 2.0 / width)
-    angles = jnp.arange(length, dtype=f32)[:, None] * frequency[None, :]
-    cosine, sine = jnp.cos(angles), jnp.sin(angles)
-    return jnp.concatenate([cosine, cosine], axis=1), jnp.concatenate([-sine, sine], axis=1)
+    angles = np.arange(length)[:, None] * 10000.0 ** (-np.arange(width // 2) * 2.0 / width)[None, :]
+    cosine, sine = np.cos(angles).astype(np.float32), np.sin(angles).astype(np.float32)
+    return jnp.asarray(np.concatenate([cosine, cosine], axis=1)), jnp.asarray(np.concatenate([-sine, sine], axis=1))
 
 
 def key_start(query_start):
@@ -151,49 +150,58 @@
     )(rows_in, dqn, dkn, dvalue, qraw, kraw, q_scale, k_scale, q_dot, k_dot, q_gain[None], k_gain[None], w_query, w_key, w_value)
 
 
-def attention_wgrad_kernel(count, extra, order, *refs):
-    rows_in = refs[0]
-    middles = refs[1 : 1 + count]
-    sides = refs[1 + count : 4 + count]
-    attended = refs[4 + count : 4 + 2 * count]
-    outs = refs[4 + 2 * count + extra :]
-    totals = [tn(rows_in[...], side[...]) for side in sides]
-    total = tn(middles[0][...], attended[0][...])
-    for left, right in zip(middles[1:], attended[1:]):
-        total = total + tn(left[...], right[...])
-    totals.append(total)
+def attention_wgrad_kernel(added, order, rows_in, middle, *refs):
+    sides, (attended,), refs = refs[:3], refs[3:4], refs[4:]
+    got, outs = (refs[:added], refs[added:])
+    at = pl.program_id(0)
+    totals = [tn(rows_in[...], side[...]) for side in sides] + [tn(middle[...], attended[...])]
+    if not added:
+        for place, out in enumerate(outs):
+
+            @pl.when(at == place)
+            def _(out=out):
+                for weight, total in enumerate(totals):
+                    out[0, weight] = total.astype(bf16)
+
+        return
     half = outs[0].shape[2]
-    for at, total in enumerate(totals):
-        if extra:
-            total = total + refs[4 + 2 * count][0, at].astype(f32)
-        for place, out in enumerate(outs):
-            out[0, at] = total[place * half : (place + 1) * half, :].astype(bf16)
-
-
-def attention_wgrad(rows_in, middles, sides, attended, order, blocks, added=None):
+    for place, piece in enumerate(got):
+
+        @pl.when(at == place)
+        def _(piece=piece):
+            for weight, total in enumerate(totals):
+                total = total + piece[0, weight].astype(f32)
+                for side, out in enumerate(outs):
+                    out[0, weight] = total[side * half : (side + 1) * half, :].astype(bf16)
+
+
+def attention_wgrad(rows_in, middle, sides, attended, order, blocks, added=()):
     features = rows_in.shape[1]
     width = sides[0].shape[1]
     block = features // blocks
-    extra = [] if added is None else [added]
-    outs = 1 + len(extra)
+    count = order.shape[0]
     left = lambda values: pl.BlockSpec((values.shape[0], block), lambda i, ids: (0, ids[i]))
     right = lambda values: pl.BlockSpec(values.shape, lambda i, ids: (0, 0))
-    out = lambda parts: pl.BlockSpec((1, 4, block // parts, width), lambda i, ids: (i, 0, 0, 0))
-    result = pl.pallas_call(
-        functools.partial(attention_wgrad_kernel, len(middles), len(extra)),
+    group_specs = [pl.BlockSpec((1, 4, block, width), lambda i, ids: (0, 0, 0, 0))] * count
+    if added:
+        out_specs = [pl.BlockSpec((1, 4, block // 2, width), lambda i, ids: (i, 0, 0, 0))] * 2
+        out_shape = [jax.ShapeDtypeStruct((count, 4, block // 2, width), bf16)] * 2
+    else:
+        out_specs = group_specs
+        out_shape = [jax.ShapeDtypeStruct((1, 4, block, width), bf16)] * count
+    return pl.pallas_call(
+        functools.partial(attention_wgrad_kernel, len(added)),
         grid_spec=pltpu.PrefetchScalarGridSpec(
             num_scalar_prefetch=1,
-            grid=(order.shape[0],),
-            in_specs=[left(rows_in)] + [left(m) for m in middles] + [right(v) for v in sides] + [right(v) for v in attended]
-            + [out(1) for _ in extra],
-            out_specs=[out(outs)] * outs,
+            grid=(count,),
+            in_specs=[left(rows_in), left(middle)] + [right(v) for v in sides] + [right(attended)] + (group_specs if added else []),
+            out_specs=out_specs,
         ),
-        out_shape=[jax.ShapeDtypeStruct((order.shape[0], 4, block // outs, width), bf16)] * outs,
+        out_shape=out_shape,
         compiler_params=params(),
         cost_estimate=cost(8 * rows_in.shape[0] * features * width, 4 * features * width),
         name="attention_wgrad",
-    )(order, rows_in, *middles, *sides, *attended, *extra)
-    return result if extra else result[0]
+    )(order, rows_in, middle, *sides, attended, *added)
 
 
 def attend_kernel(
@@ -465,25 +473,32 @@
     )(order, *lefts, *rights, *added)
 
 
-def down_kernel(act, down_w, out):
+def down_kernel(parts, down_w, *refs):
+    acts, out = refs[:-1], refs[-1]
     joined = jnp.concatenate([down_w[e] for e in range(down_w.shape[0])], axis=1)
-    out[...] = nt(act[...], joined).astype(out.dtype)
-
-
-def down(act, down_w):
-    rows = act.shape[0]
+    block = acts[0].shape[0] // parts
+    for at, act in enumerate(acts):
+        result = nt(act[...], joined).astype(out.dtype)
+        for part in range(parts):
+            start = (part * len(acts) + at) * block
+            out[start : start + block, :] = result[part * block : (part + 1) * block, :]
+
+
+def down(acts, down_w, parts):
+    rows = sum(act.shape[0] for act in acts)
     experts, features, width = down_w.shape
     block = min(256, features)
     return pl.pallas_call(
-        down_kernel,
+        functools.partial(down_kernel, parts),
         grid=(features // block,),
-        in_specs=[pl.BlockSpec(act.shape, lambda n: (0, 0)), pl.BlockSpec((experts, block, width), lambda n: (0, n, 0))],
+        in_specs=[pl.BlockSpec((experts, block, width), lambda n: (0, n, 0))]
+        + [pl.BlockSpec(act.shape, lambda n: (0, 0)) for act in acts],
         out_specs=pl.BlockSpec((rows, block), lambda n: (0, n)),
         out_shape=jax.ShapeDtypeStruct((rows, features), bf16),
         compiler_params=params(),
         cost_estimate=cost(2 * rows * features * experts * width, 2 * (rows + experts * width) * features),
         name="down",
-    )(act, down_w)
+    )(down_w, *acts)
 
 
 def gate(value, *others):
@@ -589,8 +604,10 @@
             self.kept[side] = keep
         return tuple(sent)
 
-    def add(self):
+    def add(self, *others):
         if self.got is not None:
+            if others:
+                self.got = gate(tuple(self.got), *others)
             last = not self.left[0]
             for side in range(2):
                 total = self.kept[side].astype(f32) + self.got[side].astype(f32)
@@ -638,22 +655,12 @@
         columns = values.shape[1]
         return values.reshape(parts, CHUNKS, chunk_rows, columns)[:, c].reshape(parts * chunk_rows, columns)
 
-    def in_order(pieces):
-        columns = pieces[0].shape[1]
-        stacked = jnp.stack([piece.reshape(parts, chunk_rows, columns) for piece in pieces], axis=1)
-        return stacked.reshape(group_rows, columns)
-
     inputs = tokens.astype(f32)
     first_scale = rms_scale(inputs)
     normed_all = gather_rows((inputs * first_scale * attn_gain).astype(bf16))
     behind = Chain(gate(cotangent, normed_all))
 
-    expert_ids = jnp.arange(LANES)
-    routed = jnp.sum((routes[:, :, None] == expert_ids[None, None, :]).astype(f32), axis=1)
-    router_wide = jnp.pad(router, ((0, 0), (0, LANES - experts)))
-    routed_own = lax.dynamic_slice_in_dim(routed, part_at * shard_rows, shard_rows, 0)[:, :experts]
     cosine, sine = rope_tables(length, HEAD)
-    normed_all = gate(normed_all, routed, router_wide, cosine, sine)
 
     relative = jnp.arange(dp_size // 2, dtype=jnp.int32) ^ (lax.axis_index("dp") // 2)
     own_blocks, other_blocks = 2 * relative + low_bit, 2 * relative + 1 - low_bit
@@ -676,9 +683,14 @@
     summed.append(scatter_rows(outs[1]))
     behind.hop(outs[1])
 
+    idle_routes, idle_router = gate((routes, router), outs[1])
+    expert_ids = jnp.arange(LANES)
+    routed = jnp.sum((idle_routes[:, :, None] == expert_ids[None, None, :]).astype(f32), axis=1)
+    router_wide = jnp.pad(idle_router, ((0, 0), (0, LANES - experts)))
+    routed_own = lax.dynamic_slice_in_dim(routed, part_at * shard_rows, shard_rows, 0)[:, :experts]
     grad_group = behind.joined()
     grad_all = [chunk_of(grad_group, c) for c in chunks]
-    backs = [up_back(grad_all[0], w_down)]
+    backs = [up_back(gate(rows, routed, router_wide), w_down) for rows in grad_all]
 
     middles, scales, ffn_own = [], [], []
 
@@ -691,13 +703,8 @@
         ffn_own.append(normed)
         return normed
 
-    ahead = Chain(middle_of(0, gate(summed[0], backs[0])))
-    ahead.hop()
-    backs.append(up_back(gate(grad_all[1], ahead.values), w_down))
-    after = gather_rows(middle_of(1, gate(summed[1], *ahead.recv())))
-    ahead.hop(backs[1])
-    ahead.hop()
-    ffn_all = [ahead.joined(), after]
+    ffn_all = [gather_rows(middle_of(0, summed[0]))]
+    ffn_all.append(gather_rows(middle_of(1, gate(summed[1], ffn_own[0], *backs))))
     acts, dgates, dups, expert_grads = [], [], [], []
     for c in chunks:
         here = gate(chunk_of(routed, c), *backs, *acts[-1:])
@@ -718,7 +725,7 @@
         router_parts.append(tn(ffn_own[c], logit_grad))
         ffn_gain_parts.append(jnp.sum(ffn_grad * middles[c] * scales[c], axis=0))
         middle_grads.append(cotangent[own[c]].astype(f32) + norm_back(ffn_grad, middles[c], scales[c], ffn_gain))
-        return Chain(middle_grads[c].astype(bf16))
+        return middle_grads[c].astype(bf16)
 
     def expert_sums(lefts, rights, ids, *others, added=()):
         return wgrad(lefts, rights, gate(ids, *others), width, per, added)
@@ -730,65 +737,62 @@
         return Halving([half.reshape((dp_size // 2, per) + half.shape[1:]) for half in sums])
 
     first = middle_back(0, gate(expert_grads[0], acts[1]).astype(f32))
-    first.hop()
-    gate_sent = expert_sums(ffn_all, dgates, theirs, first.values)
+    gate_sent = expert_sums(ffn_all, dgates, theirs, first)
     gate_got = core_swap(gate_sent)
-    up_sent = expert_sums(ffn_all, dups, theirs, *first.hop(*gate_sent))
+    up_sent = expert_sums(ffn_all, dups, theirs, *gate_sent)
     up_got = core_swap(up_sent)
-    moe_0 = down(gate(acts[0], *first.hop(*up_sent)), w_down)
-    moe_sum_0 = scatter_rows(moe_0)
-    second = middle_back(1, gate(expert_grads[1], moe_0, *first.recv()).astype(f32))
-    second.hop()
-    gate_sums = expert_sums(ffn_all, dgates, mine, second.values, added=gate_got)
+    second = middle_back(1, gate(expert_grads[1], *up_sent).astype(f32))
+    middle_all = gather_rows(jnp.concatenate([first, second]))
+    gate_sums = expert_sums(ffn_all, dgates, mine, second, added=gate_got)
     gate_out = halving(gate_sums)
-    up_sums = expert_sums(ffn_all, dups, mine, *second.hop(*gate_sums), *gate_out.send(), added=up_got)
+    up_sums = expert_sums(ffn_all, dups, mine, *gate_sums, *gate_out.send(), added=up_got)
     up_out = halving(up_sums)
-    moe_1 = down(gate(acts[1], *second.hop(*up_sums), *up_out.send()), w_down)
-    moe_sum_1 = scatter_rows(moe_1)
-    middle_all = [first.joined(), second.joined()]
-
-    attended_grad = in_order([nn(rows, w_out).astype(bf16) for rows in middle_all])
+    moe = down([gate(acts[0], *up_sums, *up_out.send()), acts[1]], w_down, parts)
+    moe_sum = scatter_rows(moe)
+    gate_late = gate_out.add()
+    gate_out.send()
+    down_sent = expert_sums(grad_all, acts, theirs, moe, *gate_late)
+    down_got = core_swap(down_sent)
+
+    attended_grad = nn(gate(middle_all, *down_sent), w_out).astype(bf16)
     dqn, dkn, dvalue, qdot, kdot, q_gain_part, k_gain_part = attend_back(
         query, key, value, attended_grad, lse, qraw, kraw, q_scale, k_scale, q_gain, k_gain, cosine, sine,
-        gate(seg_ids[0], moe_1), keep_mask[0],
+        seg_ids[0], keep_mask[0],
     )
     dots = exchange_sum(jnp.stack([qdot[:, 0], kdot[:, 0]]), ("tensor",)) / features
-    gate_late = gate_out.add()
-    gate_out.send()
-    down_sent = expert_sums(grad_all, acts, theirs, dqn, *gate_late)
-    down_got = core_swap(down_sent)
+    up_late = up_out.add()
+    up_out.send()
+    down_sums = expert_sums(grad_all, acts, mine, dqn, *up_late, added=down_got)
+    down_out = halving(down_sums)
+    down_out.send()
     normed_part, dqraw, dkraw, attn_gain_part = project_back(
         normed_all, dqn, dkn, dvalue, qraw, kraw, q_scale, k_scale, dots[0][:, None], dots[1][:, None],
-        gate(q_gain, *down_sent), k_gain, w_query, w_key, w_value,
+        gate(q_gain, *down_sums), k_gain, w_query, w_key, w_value,
     )
     normed_grad = scatter_rows(normed_part)
-    up_late = up_out.add()
-    up_out.send()
-    down_sums = expert_sums(grad_all, acts, mine, normed_part, *up_late, added=down_got)
-    down_out = halving(down_sums)
-    down_out.send()
-
-    def attention_sums(ids, *others, added=None):
+    def attention_sums(ids, *others, added=()):
         return attention_wgrad(
-            normed_all, middle_all, (dqraw, dkraw, dvalue), attended_parts, gate(ids, *others), dp_size, added
+            normed_all, middle_all, (dqraw, dkraw, dvalue), attended, gate(ids, *others), dp_size, added
         )
 
-    attn_sent = attention_sums(other_blocks, *down_sums)
-    attn_got = pair_swap(attn_sent, 1)
+    attn_sent = attention_sums(other_blocks, normed_part)
+    attn_got = core_swap(attn_sent)
 
     def placed(part):
         return lax.dynamic_update_slice_in_dim(jnp.zeros((features,), f32), part, part_at * local_width, 0)
 
+    attn_sums = attention_sums(own_blocks, *attn_sent, added=attn_got)
+    attn_out = Halving(attn_sums)
+    normed_grad = gate(normed_grad, *attn_out.send())
     smalls = [attn_gain_part[0] / attn_gain, placed(q_gain_part[0]), placed(k_gain_part[0]), sum(ffn_gain_parts)]
-    smalls = gate(jnp.concatenate([jnp.stack(smalls), sum(router_parts).T]), attn_sent)
+    smalls = gate(jnp.concatenate([jnp.stack(smalls), sum(router_parts).T]), normed_grad)
     smalls = exchange_sum(smalls, ("dp", "tensor"))
-    attn_out = Halving(attention_sums(own_blocks, attn_sent, added=attn_got))
-    normed_grad = gate(normed_grad, *attn_out.send())
     gate_done = gate_out.done()
     up_done = up_out.done()
     down_done = down_out.done()
+    attn_out.add(normed_grad)
     query_done, key_done, value_done, out_done = attn_out.done()
-    layer_out = jnp.concatenate([middles[0] + moe_sum_0.astype(f32), middles[1] + moe_sum_1.astype(f32)]).astype(bf16)
+    layer_out = (jnp.concatenate(middles) + moe_sum.astype(f32)).astype(bf16)
     tokens_grad = jnp.concatenate(middle_grads) + norm_back(normed_grad.astype(f32), inputs, first_scale, attn_gain)
     return (
         layer_out, tokens_grad, query_done, key_done, value_done, out_done,

time: 954 us -> 882 us (0.925)
  starting transfers between devices: 98.4 us -> 43.4 us
  Pallas kernels: 369 us -> 352 us
  waiting for transfers between devices: 309 us -> 320 us
    ppermute x12 -> x3, waiting for transfers between devices: 120 us -> 7.02 us  [hop(): lax.ppermute(down, 'tensor', [(i, i - 1) for i in range(1, self.parts - s...]
    reduce_scatter x7 -> x6, waiting for transfers between devices: 0.04 us -> 56.4 us  [scatter_rows(): return lax.psum_scatter(values, 'tensor', scatter_dimension=0, tiled=True)]
    ppermute x12 -> x3, starting transfers between devices: 43 us -> 8.99 us  [hop(): lax.ppermute(up, 'tensor', [(i, i + 1) for i in range(step - 1, self.part...]
    all_gather x2 -> x4, waiting for transfers between devices: 83.6 us -> 117 us  [gather_rows(): return lax.all_gather(values, 'tensor', axis=0, tiled=True)]
    ppermute x29 -> x32, waiting for transfers between devices: 71.6 us -> 104 us  [pair_swap(): return lax.ppermute(values, 'dp', [(i, i ^ step) for i in range(size)])]
    pallas_call x4 -> x1, Pallas kernels: 20.1 us -> 6.34 us  [join(): pl.pallas_call(functools.partial(join_kernel, parts), grid_spec=pltpu.Pre...]
    ppermute x12 -> x3, starting transfers between devices: 16.3 us -> 3.84 us  [hop(): lax.ppermute(down, 'tensor', [(i, i - 1) for i in range(1, self.parts - s...]
    ppermute x9, waiting for transfers between devices: 25.5 us -> 35 us  [exchange_sum(): lax.ppermute(values, axis, [(i, i ^ step) for i in range(size)])]
  transfers between devices with their start and end apart: 71 -> 57, of which waited for: 27 -> 25; matrix products, arithmetic and copies ran while one was open for 14% -> 14% of each run, Pallas kernels for 39% -> 40%
where the time goes in v4:
time: 882 us; the launch traced here: 873 us
  Pallas kernels  352 us (40%)
  waiting for transfers between devices  320 us (36%)
  other arithmetic  73.7 us (8%)
  local copies, waits for them, and re-layouts  50.1 us (6%)
  starting transfers between devices  43.4 us (5%)
  matrix products  18.5 us (2%)
  between operations  15.3 us (2%)
    all_gather x4, waiting for transfers between devices, gather_rows(): return lax.all_gather(values, 'tensor', axis=0, tiled=True)  117 us
    ppermute x32, waiting for transfers between devices, pair_swap(): return lax.ppermute(values, 'dp', [(i, i ^ step) for i in range(size)])  104 us
    pallas_call x6, Pallas kernels, wgrad(): pl.pallas_call(functools.partial(wgrad_kernel, len(lefts), len(added), pe...  104 us
    pallas_call x2, Pallas kernels, experts_block(): pl.pallas_call(functools.partial(expert_kernel, block), grid=(experts,),...  95 us
    reduce_scatter x6, waiting for transfers between devices, scatter_rows(): return lax.psum_scatter(values, 'tensor', scatter_dimension=0, tiled=True)  56.4 us
    ppermute x9, waiting for transfers between devices, exchange_sum(): lax.ppermute(values, axis, [(i, i ^ step) for i in range(size)])  35 us
    pallas_call x2, Pallas kernels, up_back(): pl.pallas_call(up_back_kernel, grid=(experts // step,), in_specs=[pl.Bloc...  30.1 us
    pallas_call x1, Pallas kernels, down(): pl.pallas_call(functools.partial(down_kernel, parts), grid=(features // b...  24.3 us
  transfers between devices with their start and end apart: 57, of which 25 were waited for; matrix products, arithmetic and copies ran while one was open for 14% of the time, Pallas kernels for 40%

profile of v4, /device:TPU:0, one launch (start us, length us, event | category | flops | bytes accessed | tf_op | source)
XLA Modules:
  0.0 872.8 jit_solution(15985515688688002119)
XLA Ops:
  10.1 2.5 multiply_convert_fusion
  12.7 83.6 %all-gather.5.cloned.1.call-done.rows_in = bf16[1024,2048]{1,0:T(8,128)(2,1)} async-done(((bf16[256,2048]{1,0:T(8,128)(2,1)}), bf16[1024,2048]{1,0:T(8,128)(2,1)}) %all-gather.5.cloned.1.call-update) | async-done | bytes 4194320 | tf_op jit(solution)/shard_map/all_gather | solution.py:509
  97.5 5.5 collective-permute-start.2
  103.0 16.3 %project.1 = (f32[1024,512]{1,0:T(8,128)}, f32[1024,512]{1,0:T(8,128)}, bf16[1024,512]{1,0:T(8,128)(2,1)}, f32[2,1024]{1,0:T(2,128)}) custom-call(bf16[1024,2048]{1,0:T(8,128)(2,1)} %all-gather.5.cloned.1.call-done.rows_in, bf16[2048,512]{1,0:T(8,128)(2,1)} %w_query.3, bf16[2048,512]{1,0:T(8,128)(2,1)} %w_key.3, bf16[2048,512]{1,0:T(8,128)(2,1)} %w_value.3), custom_call_target="tpu_custom_call" | custom-call | flops 2899102976 | bytes 1310720 | tf_op jit(solution)/shard_map/project/pallas_call | solution.py:101
  119.3 5.1 collective-permute-done
  127.0 2.6 collective-permute-done.1
  135.7 15.6 %attend.1 = (bf16[1024,512]{1,0:T(8,128)(2,1)}, bf16[1024,512]{1,0:T(8,128)(2,1)}, bf16[1024,512]{1,0:T(8,128)(2,1)}, f32[1024,512]{1,0:T(8,128)}) custom-call(f32[1024,512]{1,0:T(8,128)} %get-tuple-element.95.qraw, f32[1024,512]{1,0:T(8,128)} %get-tuple-element.96.kraw, bf16[1024,512]{1,0:T(8,128)(2,1)} %get-tuple-element.97.value, ...), custom_call_target="tpu_custom_call" | custom-call | flops 57347878912 | bytes 1179648 | tf_op jit(solution)/shard_map/attend/pallas_call | solution.py:241
  151.4 7.0 collective-permute-done.5.refs_4_
  159.7 2.7 convolution_convert_fusion.1
  162.4 2.6 convolution_convert_fusion
  170.9 54.0 %reduce-scatter.7.cloned.1.call-done = bf16[128,2048]{1,0:T(8,128)(2,1)} async-done(((bf16[512,2048]{1,0:T(8,128)(2,1)}), bf16[128,2048]{1,0:T(8,128)(2,1)}) %reduce-scatter.7.cloned.1.call-update) | async-done | bytes 524304 | tf_op jit(solution)/shard_map/reduce_scatter | solution.py:513
  232.4 6.7 convert_reduce_fusion
  240.7 6.3 join.1
  247.1 4.8 fusion.40
  251.9 15.1 %up_back.3.back = bf16[512,4096]{1,0:T(8,128)(2,1)} custom-call(bf16[512,2048]{1,0:T(8,128)(2,1)} %bitcast.172, bf16[16,2048,256]{2,1,0:T(8,128)(2,1)} %down_w.5), custom_call_target="tpu_custom_call" | custom-call | flops 3865470464 | bytes 2359296 | tf_op jit(solution)/shard_map/up_back/pallas_call | solution.py:333
  266.9 15.0 %up_back.2.back = bf16[512,4096]{1,0:T(8,128)(2,1)} custom-call(bf16[512,2048]{1,0:T(8,128)(2,1)} %bitcast.175, bf16[16,2048,256]{2,1,0:T(8,128)(2,1)} %down_w.5), custom_call_target="tpu_custom_call" | custom-call | flops 3865470464 | bytes 2359296 | tf_op jit(solution)/shard_map/up_back/pallas_call | solution.py:333
  285.6 33.6 %all-gather.7.cloned.1.call-done.rows_in.refs_0_ = bf16[512,2048]{1,0:T(8,128)(2,1)} async-done(((bf16[128,2048]{1,0:T(8,128)(2,1)}), bf16[512,2048]{1,0:T(8,128)(2,1)}) %all-gather.7.cloned.1.call-update) | async-done | bytes 2097168 | tf_op jit(solution)/shard_map/all_gather | solution.py:509
  319.2 47.5 %experts.2 = (bf16[512,4096]{1,0:T(8,128)(2,1)}, bf16[512,4096]{1,0:T(8,128)(2,1)}, bf16[512,4096]{1,0:T(8,128)(2,1)}, bf16[512,2176]{1,0:T(8,128)(2,1)}) custom-call(bf16[512,2048]{1,0:T(8,128)(2,1)} %all-gather.7.cloned.1.call-done.rows_in.refs_0_, bf16[512,4096]{1,0:T(8,128)(2,1)} %up_back.2.back, f32[512,128]{1,0:T(8,128)} %bitcast.199, ...), custom_call_target="tpu_custom_call" | custom-call | flops 53210619904 | bytes 6291456 | tf_op jit(solution)/shard_map/experts/pallas_call | solution.py:398
  366.8 47.5 %experts.3 = (bf16[512,4096]{1,0:T(8,128)(2,1)}, bf16[512,4096]{1,0:T(8,128)(2,1)}, bf16[512,4096]{1,0:T(8,128)(2,1)}, bf16[512,2176]{1,0:T(8,128)(2,1)}) custom-call(bf16[512,2048]{1,0:T(8,128)(2,1)} %all-gather.9.cloned.1.call-done.rows_in.refs_1_, bf16[512,4096]{1,0:T(8,128)(2,1)} %up_back.3.back, f32[512,128]{1,0:T(8,128)} %bitcast.198, ...), custom_call_target="tpu_custom_call" | custom-call | flops 53210619904 | bytes 6291456 | tf_op jit(solution)/shard_map/experts/pallas_call | solution.py:398
  424.3 17.1 %wgrad.6 = (bf16[2,2048,256]{2,1,0:T(8,128)(2,1)}, bf16[2,2048,256]{2,1,0:T(8,128)(2,1)}, bf16[2,2048,256]{2,1,0:T(8,128)(2,1)}, bf16[2,2048,256]{2,1,0:T(8,128)(2,1)}) custom-call(s32[8]{0:T(128)} %add.276.order, bf16[512,2048]{1,0:T(8,128)(2,1)} %all-gather.7.cloned.1.call-done.rows_in.refs_0_, ...), custom_call_target="tpu_custom_call" | custom-call | flops 3865470464 | bytes 2621440 | tf_op jit(solution)/shard_map/wgrad/pallas_call | solution.py:459
  441.4 16.7 %wgrad.7 = (bf16[2,2048,256]{2,1,0:T(8,128)(2,1)}, bf16[2,2048,256]{2,1,0:T(8,128)(2,1)}, bf16[2,2048,256]{2,1,0:T(8,128)(2,1)}, bf16[2,2048,256]{2,1,0:T(8,128)(2,1)}) custom-call(s32[8]{0:T(128)} %add.276.order, bf16[512,2048]{1,0:T(8,128)(2,1)} %all-gather.7.cloned.1.call-done.rows_in.refs_0_, ...), custom_call_target="tpu_custom_call" | custom-call | flops 3865470464 | bytes 2621440 | tf_op jit(solution)/shard_map/wgrad/pallas_call | solution.py:459
  458.1 2.4 reduce-scatter.11.cloned.1.call-done
  468.0 3.4 collective-permute-done.8.refs_4_
  471.5 2.9 collective-permute-done.9.refs_5_
  474.5 2.9 collective-permute-done.10.refs_6_
  480.4 17.7 %wgrad.8 = (bf16[8,1024,256]{2,1,0:T(8,128)(2,1)}, bf16[8,1024,256]{2,1,0:T(8,128)(2,1)}) custom-call(s32[8]{0:T(128)} %add.270.order, bf16[512,2048]{1,0:T(8,128)(2,1)} %all-gather.7.cloned.1.call-done.rows_in.refs_0_, bf16[512,2048]{1,0:T(8,128)(2,1)} %all-gather.9.cloned.1.call-done.rows_in.refs_1_, bf16[512,4096]{1,0:T(8,128)(2,1)} %get-tuple-element.119.refs_2_, ...), custom_call_target="tpu_custom_call" | custom-call | flops 3865470464 | bytes 2621440 | tf_op jit(solution)/shard_map/wgrad/pallas_call | solution.py:459
  498.1 3.2 slice_bitcast_fusion.5
  502.8 2.4 fusion.39
  506.6 17.6 %wgrad.9 = (bf16[8,1024,256]{2,1,0:T(8,128)(2,1)}, bf16[8,1024,256]{2,1,0:T(8,128)(2,1)}) custom-call(s32[8]{0:T(128)} %add.270.order, bf16[512,2048]{1,0:T(8,128)(2,1)} %all-gather.7.cloned.1.call-done.rows_in.refs_0_, bf16[512,2048]{1,0:T(8,128)(2,1)} %all-gather.9.cloned.1.call-done.rows_in.refs_1_, bf16[512,4096]{1,0:T(8,128)(2,1)} %get-tuple-element.126.refs_2_, ...), custom_call_target="tpu_custom_call" | custom-call | flops 3865470464 | bytes 2621440 | tf_op jit(solution)/shard_map/wgrad/pallas_call | solution.py:459
  524.3 3.2 slice_bitcast_fusion.4
  527.9 2.3 fusion.38
  530.8 24.3 %down.1 = bf16[1024,2048]{1,0:T(8,128)(2,1)} custom-call(bf16[16,2048,256]{2,1,0:T(8,128)(2,1)} %down_w.5, bf16[512,4096]{1,0:T(8,128)(2,1)} %get-tuple-element.139.refs_0_.refs_2_, bf16[512,4096]{1,0:T(8,128)(2,1)} %get-tuple-element.116.refs_1_.refs_3_), custom_call_target="tpu_custom_call" | custom-call | flops 7730940928 | bytes 2621440 | tf_op jit(solution)/shard_map/down/pallas_call | solution.py:491
  555.2 4.1 fusion.4
  559.3 3.7 fusion.5
  563.0 17.1 %wgrad.10 = (bf16[2,2048,256]{2,1,0:T(8,128)(2,1)}, bf16[2,2048,256]{2,1,0:T(8,128)(2,1)}, bf16[2,2048,256]{2,1,0:T(8,128)(2,1)}, bf16[2,2048,256]{2,1,0:T(8,128)(2,1)}) custom-call(s32[8]{0:T(128)} %add.276.order, bf16[512,2048]{1,0:T(8,128)(2,1)} %bitcast.176, bf16[512,2048]{1,0:T(8,128)(2,1)} %bitcast.173, ...), custom_call_target="tpu_custom_call" | custom-call | flops 3865470464 | bytes 2621440 | tf_op jit(solution)/shard_map/wgrad/pallas_call | solution.py:459
  580.7 13.5 %collective-permute-done.21 = bf16[2,2,1024,256]{3,2,1,0:T(8,128)(2,1)} collective-permute-done((bf16[2,2,1024,256]{3,2,1,0:T(8,128)(2,1)}, bf16[2,2,1024,256]{3,2,1,0:T(8,128)(2,1)}, u32[]{:S(2)}, u32[]{:S(2)}) %collective-permute-start.21) | collective-permute-done | bytes 2097184 | tf_op jit(solution)/shard_map/ppermute | solution.py:578
  594.2 3.4 fusion.2
  597.6 5.5 convolution_convert_fusion.2.out_grad
  603.1 24.0 %attend_back.1 = (f32[1024,512]{1,0:T(8,128)}, f32[1024,512]{1,0:T(8,128)}, bf16[1024,512]{1,0:T(8,128)(2,1)}, f32[1024,1]{1,0:T(8,128)}, f32[1024,1]{1,0:T(8,128)}, /*index=5*/f32[1,512]{1,0:T(1,128)}, f32[1,512]{1,0:T(1,128)}) custom-call(bf16[1024,512]{1,0:T(8,128)(2,1)} %get-tuple-element.140.query, bf16[1024,512]{1,0:T(8,128)(2,1)} %get-tuple-element.141.key, ...), custom_call_target="tpu_custom_call" | custom-call | flops 58435043328 | bytes 2097152 | tf_op jit(solution)/shard_map/attend_back/pallas_call | solution.py:307
  629.7 4.1 fusion.3
  633.8 2.1 collective-permute-start.19
  635.9 17.5 %wgrad.11 = (bf16[8,1024,256]{2,1,0:T(8,128)(2,1)}, bf16[8,1024,256]{2,1,0:T(8,128)(2,1)}) custom-call(s32[8]{0:T(128)} %add.270.order, bf16[512,2048]{1,0:T(8,128)(2,1)} %bitcast.177, bf16[512,2048]{1,0:T(8,128)(2,1)} %bitcast.174, bf16[512,4096]{1,0:T(8,128)(2,1)} %get-tuple-element.139.refs_0_.refs_2_, ...), custom_call_target="tpu_custom_call" | custom-call | flops 3865470464 | bytes 2621440 | tf_op jit(solution)/shard_map/wgrad/pallas_call | solution.py:459
  655.5 13.8 %project_back.1 = (bf16[1024,2048]{1,0:T(8,128)(2,1)}, bf16[1024,512]{1,0:T(8,128)(2,1)}, bf16[1024,512]{1,0:T(8,128)(2,1)}, f32[1,2048]{1,0:T(1,128)}) custom-call(bf16[1024,2048]{1,0:T(8,128)(2,1)} %all-gather.5.cloned.1.call-done.rows_in, f32[1024,512]{1,0:T(8,128)} %get-tuple-element.149.dqn, f32[1024,512]{1,0:T(8,128)} %get-tuple-element.150.dkn, ...), custom_call_target="tpu_custom_call" | custom-call | flops 2899102976 | bytes 1310720 | tf_op jit(solution)/shard_map/project_back/pallas_call | solution.py:141
  669.3 2.3 slice_bitcast_fusion.10
  680.2 17.8 %collective-permute-done.40 = bf16[1,2,1024,256]{3,2,1,0:T(8,128)(2,1)} collective-permute-done((bf16[1,2,1024,256]{3,2,1,0:T(8,128)(2,1)}, bf16[1,2,1024,256]{3,2,1,0:T(8,128)(2,1)}, u32[]{:S(2)}, u32[]{:S(2)}) %collective-permute-start.40) | collective-permute-done | bytes 1048608 | tf_op jit(solution)/shard_map/ppermute | solution.py:578
  704.8 2.4 pad_maximum_fusion
  711.6 8.8 %collective-permute-done.42 = bf16[1,2,1024,256]{3,2,1,0:T(8,128)(2,1)S(1)} collective-permute-done((bf16[1,2,1024,256]{3,2,1,0:T(8,128)(2,1)S(1)}, bf16[1,2,1024,256]{3,2,1,0:T(8,128)(2,1)S(1)}, u32[]{:S(2)}, u32[]{:S(2)}) %collective-permute-start.42) | collective-permute-done | bytes 1048608 | tf_op jit(solution)/shard_map/ppermute | solution.py:578
  720.6 2.8 collective-permute-done.41
  723.6 2.3 pad_maximum_fusion.1
  725.9 11.2 %attention_wgrad.2 = (bf16[1,4,256,512]{3,2,1,0:T(8,128)(2,1)}, bf16[1,4,256,512]{3,2,1,0:T(8,128)(2,1)}, bf16[1,4,256,512]{3,2,1,0:T(8,128)(2,1)}, bf16[1,4,256,512]{3,2,1,0:T(8,128)(2,1)}) custom-call(s32[4]{0:T(128)} %get-tuple-element.159.order, bf16[1024,2048]{1,0:T(8,128)(2,1)} %all-gather.5.cloned.1.call-done.rows_in, ...), custom_call_target="tpu_custom_call" | custom-call | flops 3865470464 | bytes 524288 | tf_op jit(solution)/shard_map/attention_wgrad/pallas_call | solution.py:192
  737.8 29.3 %collective-permute-done.45 = bf16[2,2,1024,256]{3,2,1,0:T(8,128)(2,1)} collective-permute-done((bf16[2,2,1024,256]{3,2,1,0:T(8,128)(2,1)}, bf16[2,2,1024,256]{3,2,1,0:T(8,128)(2,1)}, u32[]{:S(2)}, u32[]{:S(2)}) %collective-permute-start.45) | collective-permute-done | bytes 2097184 | tf_op jit(solution)/shard_map/ppermute | solution.py:578
  767.1 2.7 fusion.6
  775.6 11.4 %attention_wgrad.3 = (bf16[4,4,128,512]{3,2,1,0:T(8,128)(2,1)}, bf16[4,4,128,512]{3,2,1,0:T(8,128)(2,1)}) custom-call(s32[4]{0:T(128)} %get-tuple-element.166.order, bf16[1024,2048]{1,0:T(8,128)(2,1)} %all-gather.5.cloned.1.call-done.rows_in, bf16[1024,2048]{1,0:T(8,128)(2,1)} %all-gather.11.cloned.1.call-done.middle, ...), custom_call_target="tpu_custom_call" | custom-call | flops 3865470464 | bytes 524288 | tf_op jit(solution)/shard_map/attention_wgrad/pallas_call | solution.py:192
  787.0 2.4 slice.216
  792.7 4.5 collective-permute-done.46
  801.4 2.3 pad_maximum_fusion.2
  803.7 2.8 fusion.7
  806.5 12.8 %collective-permute-done.30 = bf16[2,4,128,512]{3,2,1,0:T(8,128)(2,1)} collective-permute-done((bf16[2,4,128,512]{3,2,1,0:T(8,128)(2,1)}, bf16[2,4,128,512]{3,2,1,0:T(8,128)(2,1)}, u32[]{:S(2)}, u32[]{:S(2)}) %collective-permute-start.30) | collective-permute-done | bytes 1048608 | tf_op jit(solution)/shard_map/ppermute | solution.py:578
  819.3 2.3 collective-permute-done.31
  829.6 13.2 %collective-permute-done.35 = f32[20,2048]{1,0:T(8,128)S(1)} collective-permute-done((f32[20,2048]{1,0:T(8,128)S(1)}, f32[20,2048]{1,0:T(8,128)S(1)}, u32[]{:S(2)}, u32[]{:S(2)}) %collective-permute-start.35) | collective-permute-done | bytes 163872 | tf_op jit(solution)/shard_map/ppermute | solution.py:631
  844.6 2.0 maximum_add_fusion.1
  846.6 2.0 collective-permute-done.36
  850.8 4.8 collective-permute-done.37
  857.1 7.3 collective-permute-done.38
  (289 shorter events, 111.3 us)
Async XLA Ops:
  7.2 152.5 %copy-start = (bf16[2048,512]{1,0:T(8,128)(2,1)S(1)}, bf16[2048,512]{1,0:T(8,128)(2,1)}, u32[]{:S(2)}) copy-start(bf16[2048,512]{1,0:T(8,128)(2,1)} %param.28) | copy-start | bytes 6291460
  7.2 89.0 %copy-start.18 = (bf16[256,2048]{1,0:T(8,128)(2,1)S(1)}, bf16[256,2048]{1,0:T(8,128)(2,1)}, u32[]{:S(2)}) copy-start(bf16[256,2048]{1,0:T(8,128)(2,1)} %own) | copy-start | bytes 3145732
  7.2 89.0 %all-gather.5.cloned.1.call-start = ((), (), s32[]{:S(2)}) async-start(), calls=%async_computation.6 | async-start | bytes 5242880 | tf_op jit(solution)/shard_map/all_gather | solution.py:509
  12.6 119.1 %copy-start.40 = (s32[1,1024]{1,0:T(1,128)S(1)}, s32[1,1024]{1,0:T(1,128)}, u32[]{:S(2)}) copy-start(s32[1,1024]{1,0:T(1,128)} %seg_row.1) | copy-start | bytes 12292
  12.6 212.2 %reduce-scatter.7.cloned.1.call-start = ((), (), s32[]{:S(2)}) async-start(), calls=%async_computation.7 | async-start | bytes 2621440 | tf_op jit(solution)/shard_map/reduce_scatter | solution.py:513
  96.2 35.5 %collective-permute-start.3 = (bf16[256,2048]{1,0:T(8,128)(2,1)S(1)}, bf16[256,2048]{1,0:T(8,128)(2,1)}, u32[]{:S(2)}, u32[]{:S(2)}) collective-permute-start(bf16[256,2048]{1,0:T(8,128)(2,1)S(1)} %copy-done.18), channel_id=1, source_target_pairs={{1,0},{2,1},{3,2},{5,4},{6,5},{7,6},{9,8},{10,9},{11,10},{13,12},{... | collective-permute-start | bytes 3145736 | tf_op jit(solution)/shard_map/ppermute | solution.py:562
  97.5 34.2 %collective-permute-start.2 = (bf16[256,2048]{1,0:T(8,128)(2,1)S(1)}, bf16[256,2048]{1,0:T(8,128)(2,1)}, u32[]{:S(2)}, u32[]{:S(2)}) collective-permute-start(bf16[256,2048]{1,0:T(8,128)(2,1)S(1)} %copy-done.18), channel_id=1, source_target_pairs={{0,1},{1,2},{2,3},{4,5},{5,6},{6,7},{8,9},{9,10},{10,11},{12,13},{... | collective-permute-start | bytes 3145736 | tf_op jit(solution)/shard_map/ppermute | solution.py:561
  119.3 5.1 collective-permute-start
  125.1 4.5 collective-permute-start.1
  132.8 25.6 %collective-permute-start.5 = (bf16[256,2048]{1,0:T(8,128)(2,1)}, bf16[256,2048]{1,0:T(8,128)(2,1)}, u32[]{:S(2)}, u32[]{:S(2)}) collective-permute-start(bf16[256,2048]{1,0:T(8,128)(2,1)} %collective-permute-done.3.refs_3_), channel_id=1, source_target_pairs={{1,0},{2,1},{5,4},{6,5},{9,8},{10,9},{13,12},{14,13},{17,16},{18,1... | collective-permute-start | bytes 3145736 | tf_op jit(solution)/shard_map/ppermute | solution.py:562
  134.0 24.3 %collective-permute-start.4 = (bf16[256,2048]{1,0:T(8,128)(2,1)}, bf16[256,2048]{1,0:T(8,128)(2,1)}, u32[]{:S(2)}, u32[]{:S(2)}) collective-permute-start(bf16[256,2048]{1,0:T(8,128)(2,1)} %collective-permute-done.2.refs_0_), channel_id=1, source_target_pairs={{1,2},{2,3},{5,6},{6,7},{9,10},{10,11},{13,14},{14,15},{17,18},{18... | collective-permute-start | bytes 3145736 | tf_op jit(solution)/shard_map/ppermute | solution.py:561
  162.4 119.6 %reduce-scatter.9.cloned.1.call-start = ((), (), s32[]{:S(2)}) async-start(), calls=%async_computation.8 | async-start | bytes 2621440 | tf_op jit(solution)/shard_map/reduce_scatter | solution.py:513
  165.0 154.1 %all-gather.7.cloned.1.call-start = ((), (), s32[]{:S(2)}) async-start(), calls=%async_computation.9 | async-start | bytes 2621440 | tf_op jit(solution)/shard_map/all_gather | solution.py:509
  167.8 58.7 %copy-start.37 = (f32[2048]{0:T(1024)S(1)}, f32[2048]{0:T(1024)}, u32[]{:S(2)}) copy-start(f32[2048]{0:T(1024)} %param.31) | copy-start | bytes 24580
  167.8 60.6 %copy-start.39 = (s32[1024,8]{0,1:T(8,128)S(1)}, s32[1024,8]{0,1:T(8,128)}, u32[]{:S(2)}) copy-start(s32[1024,8]{0,1:T(8,128)} %param.23) | copy-start | bytes 98308
  167.8 61.6 %copy-start.36 = (bf16[2048,16]{0,1:T(8,128)(2,1)S(1)}, bf16[2048,16]{0,1:T(8,128)(2,1)}, u32[]{:S(2)}) copy-start(bf16[2048,16]{0,1:T(8,128)(2,1)} %param.32) | copy-start | bytes 196612
  167.8 72.9 %collective-permute-start.6 = (bf16[256,2048]{1,0:T(8,128)(2,1)}, bf16[256,2048]{1,0:T(8,128)(2,1)}, u32[]{:S(2)}, u32[]{:S(2)}) collective-permute-start(bf16[256,2048]{1,0:T(8,128)(2,1)} %collective-permute-done.4.refs_1_), channel_id=1, source_target_pairs={{2,3},{6,7},{10,11},{14,15},{18,19},{22,23},{26,27},{30,31}} | collective-permute-start | bytes 3145736 | tf_op jit(solution)/shard_map/ppermute | solution.py:561
  169.6 71.2 %collective-permute-start.7 = (bf16[256,2048]{1,0:T(8,128)(2,1)}, bf16[256,2048]{1,0:T(8,128)(2,1)}, u32[]{:S(2)}, u32[]{:S(2)}) collective-permute-start(bf16[256,2048]{1,0:T(8,128)(2,1)} %collective-permute-done.5.refs_4_), channel_id=1, source_target_pairs={{1,0},{5,4},{9,8},{13,12},{17,16},{21,20},{25,24},{29,28}} | collective-permute-start | bytes 3145736 | tf_op jit(solution)/shard_map/ppermute | solution.py:562
  226.5 196.2 %copy-start.3 = (f32[128,2048]{1,0:T(8,128)}, f32[128,2048]{1,0:T(8,128)S(1)}, u32[]{:S(2)}) copy-start(f32[128,2048]{1,0:T(8,128)S(1)} %get-tuple-element.191) | copy-start | bytes 3145732
  227.7 139.1 %all-gather.9.cloned.1.call-start = ((), (), s32[]{:S(2)}) async-start(), calls=%async_computation.10 | async-start | bytes 2621440 | tf_op jit(solution)/shard_map/all_gather | solution.py:509
  285.5 133.3 %reduce-scatter.13.cloned.1.call-start = ((), (), s32[]{:S(2)}) async-start(), calls=%async_computation.12 | async-start | bytes 2785280 | tf_op jit(solution)/shard_map/reduce_scatter | solution.py:513
  366.7 93.8 %reduce-scatter.11.cloned.1.call-start = ((), (), s32[]{:S(2)}) async-start(), calls=%async_computation.11 | async-start | bytes 2785280 | tf_op jit(solution)/shard_map/reduce_scatter | solution.py:513
  414.3 183.4 %all-gather.11.cloned.1.call-start = ((), (), s32[]{:S(2)}) async-start(), calls=%async_computation.14 | async-start | bytes 5242880 | tf_op jit(solution)/shard_map/all_gather | solution.py:509
  466.8 336.9 %reduce-scatter.15.cloned.1.call-start = ((), (), s32[]{:S(2)}) async-start(), calls=%async_computation.13 | async-start | bytes 5242880 | tf_op jit(solution)/shard_map/reduce_scatter | solution.py:513
  466.8 4.6 collective-permute-start.8
  466.9 7.5 collective-permute-start.9
  467.4 10.0 %collective-permute-start.10 = (bf16[2,2048,256]{2,1,0:T(8,128)(2,1)}, bf16[2,2048,256]{2,1,0:T(8,128)(2,1)}, u32[]{:S(2)}, u32[]{:S(2)}) collective-permute-start(bf16[2,2048,256]{2,1,0:T(8,128)(2,1)} %get-tuple-element.123), channel_id=1, source_target_pairs={{0,4},{4,0},{8,12},{12,8},{16,20},{20,16},{24,28},{28,24},{1,5},{5... | collective-permute-start | bytes 6291464 | tf_op jit(solution)/shard_map/ppermute | solution.py:578
  467.5 12.9 %collective-permute-start.11 = (bf16[2,2048,256]{2,1,0:T(8,128)(2,1)}, bf16[2,2048,256]{2,1,0:T(8,128)(2,1)}, u32[]{:S(2)}, u32[]{:S(2)}) collective-permute-start(bf16[2,2048,256]{2,1,0:T(8,128)(2,1)} %get-tuple-element.124), channel_id=1, source_target_pairs={{0,4},{4,0},{8,12},{12,8},{16,20},{20,16},{24,28},{28,24},{1,5},{5... | collective-permute-start | bytes 6291464 | tf_op jit(solution)/shard_map/ppermute | solution.py:578
  467.9 37.2 %collective-permute-start.12 = (bf16[2,2048,256]{2,1,0:T(8,128)(2,1)}, bf16[2,2048,256]{2,1,0:T(8,128)(2,1)}, u32[]{:S(2)}, u32[]{:S(2)}) collective-permute-start(bf16[2,2048,256]{2,1,0:T(8,128)(2,1)} %get-tuple-element.128), channel_id=1, source_target_pairs={{0,4},{4,0},{8,12},{12,8},{16,20},{20,16},{24,28},{28,24},{1,5},{5... | collective-permute-start | bytes 6291464 | tf_op jit(solution)/shard_map/ppermute | solution.py:578
  471.4 35.2 %collective-permute-start.13 = (bf16[2,2048,256]{2,1,0:T(8,128)(2,1)}, bf16[2,2048,256]{2,1,0:T(8,128)(2,1)}, u32[]{:S(2)}, u32[]{:S(2)}) collective-permute-start(bf16[2,2048,256]{2,1,0:T(8,128)(2,1)} %get-tuple-element.129), channel_id=1, source_target_pairs={{0,4},{4,0},{8,12},{12,8},{16,20},{20,16},{24,28},{28,24},{1,5},{5... | collective-permute-start | bytes 6291464 | tf_op jit(solution)/shard_map/ppermute | solution.py:578
  474.4 32.2 %collective-permute-start.14 = (bf16[2,2048,256]{2,1,0:T(8,128)(2,1)}, bf16[2,2048,256]{2,1,0:T(8,128)(2,1)}, u32[]{:S(2)}, u32[]{:S(2)}) collective-permute-start(bf16[2,2048,256]{2,1,0:T(8,128)(2,1)} %get-tuple-element.130), channel_id=1, source_target_pairs={{0,4},{4,0},{8,12},{12,8},{16,20},{20,16},{24,28},{28,24},{1,5},{5... | collective-permute-start | bytes 6291464 | tf_op jit(solution)/shard_map/ppermute | solution.py:578
  477.4 29.2 %collective-permute-start.15 = (bf16[2,2048,256]{2,1,0:T(8,128)(2,1)}, bf16[2,2048,256]{2,1,0:T(8,128)(2,1)}, u32[]{:S(2)}, u32[]{:S(2)}) collective-permute-start(bf16[2,2048,256]{2,1,0:T(8,128)(2,1)} %get-tuple-element.131), channel_id=1, source_target_pairs={{0,4},{4,0},{8,12},{12,8},{16,20},{20,16},{24,28},{28,24},{1,5},{5... | collective-permute-start | bytes 6291464 | tf_op jit(solution)/shard_map/ppermute | solution.py:578
  501.3 53.8 %collective-permute-start.17 = (bf16[2,2,1024,256]{3,2,1,0:T(8,128)(2,1)}, bf16[2,2,1024,256]{3,2,1,0:T(8,128)(2,1)}, u32[]{:S(2)}, u32[]{:S(2)}) collective-permute-start(bf16[2,2,1024,256]{3,2,1,0:T(8,128)(2,1)} %slice_bitcast_fusion.5), channel_id=1, source_target_pairs={{0,8},{4,12},{8,0},{12,4},{16,24},{20,28},{24,16},{28,20},{1,9},{5... | collective-permute-start | bytes 6291464 | tf_op jit(solution)/shard_map/ppermute | solution.py:578
  505.2 54.2 %collective-permute-start.16 = (bf16[2,2,1024,256]{3,2,1,0:T(8,128)(2,1)}, bf16[2,2,1024,256]{3,2,1,0:T(8,128)(2,1)}, u32[]{:S(2)}, u32[]{:S(2)}) collective-permute-start(bf16[2,2,1024,256]{3,2,1,0:T(8,128)(2,1)} %bitcast.16), channel_id=1, source_target_pairs={{0,16},{4,20},{8,24},{12,28},{16,0},{20,4},{24,8},{28,12},{1,17},{... | collective-permute-start | bytes 6291464 | tf_op jit(solution)/shard_map/ppermute | solution.py:578
  527.4 66.8 %collective-permute-start.21 = (bf16[2,2,1024,256]{3,2,1,0:T(8,128)(2,1)}, bf16[2,2,1024,256]{3,2,1,0:T(8,128)(2,1)}, u32[]{:S(2)}, u32[]{:S(2)}) collective-permute-start(bf16[2,2,1024,256]{3,2,1,0:T(8,128)(2,1)} %slice_bitcast_fusion.4), channel_id=1, source_target_pairs={{0,8},{4,12},{8,0},{12,4},{16,24},{20,28},{24,16},{28,20},{1,9},{5... | collective-permute-start | bytes 6291464 | tf_op jit(solution)/shard_map/ppermute | solution.py:578
  530.3 99.4 %collective-permute-start.20 = (bf16[2,2,1024,256]{3,2,1,0:T(8,128)(2,1)}, bf16[2,2,1024,256]{3,2,1,0:T(8,128)(2,1)}, u32[]{:S(2)}, u32[]{:S(2)}) collective-permute-start(bf16[2,2,1024,256]{3,2,1,0:T(8,128)(2,1)} %bitcast.19), channel_id=1, source_target_pairs={{0,16},{4,20},{8,24},{12,28},{16,0},{20,4},{24,8},{28,12},{1,17},{... | collective-permute-start | bytes 6291464 | tf_op jit(solution)/shard_map/ppermute | solution.py:578
  555.1 251.4 %reduce-scatter.17.cloned.1.call-start = ((), (), s32[]{:S(2)}) async-start(), calls=%async_computation.15 | async-start | bytes 5242880 | tf_op jit(solution)/shard_map/reduce_scatter | solution.py:513
  580.1 55.7 %collective-permute-start.22 = (bf16[2,2048,256]{2,1,0:T(8,128)(2,1)}, bf16[2,2048,256]{2,1,0:T(8,128)(2,1)}, u32[]{:S(2)}, u32[]{:S(2)}) collective-permute-start(bf16[2,2048,256]{2,1,0:T(8,128)(2,1)} %get-tuple-element.143), channel_id=1, source_target_pairs={{0,4},{4,0},{8,12},{12,8},{16,20},{20,16},{24,28},{28,24},{1,5},{5... | collective-permute-start | bytes 6291464 | tf_op jit(solution)/shard_map/ppermute | solution.py:578
  580.1 55.7 %collective-permute-start.23 = (bf16[2,2048,256]{2,1,0:T(8,128)(2,1)}, bf16[2,2048,256]{2,1,0:T(8,128)(2,1)}, u32[]{:S(2)}, u32[]{:S(2)}) collective-permute-start(bf16[2,2048,256]{2,1,0:T(8,128)(2,1)} %get-tuple-element.144), channel_id=1, source_target_pairs={{0,4},{4,0},{8,12},{12,8},{16,20},{20,16},{24,28},{28,24},{1,5},{5... | collective-permute-start | bytes 6291464 | tf_op jit(solution)/shard_map/ppermute | solution.py:578
  580.6 55.2 %collective-permute-start.24 = (bf16[2,2048,256]{2,1,0:T(8,128)(2,1)}, bf16[2,2048,256]{2,1,0:T(8,128)(2,1)}, u32[]{:S(2)}, u32[]{:S(2)}) collective-permute-start(bf16[2,2048,256]{2,1,0:T(8,128)(2,1)} %get-tuple-element.145), channel_id=1, source_target_pairs={{0,4},{4,0},{8,12},{12,8},{16,20},{20,16},{24,28},{28,24},{1,5},{5... | collective-permute-start | bytes 6291464 | tf_op jit(solution)/shard_map/ppermute | solution.py:578
  594.2 41.6 %collective-permute-start.25 = (bf16[2,2048,256]{2,1,0:T(8,128)(2,1)}, bf16[2,2048,256]{2,1,0:T(8,128)(2,1)}, u32[]{:S(2)}, u32[]{:S(2)}) collective-permute-start(bf16[2,2048,256]{2,1,0:T(8,128)(2,1)} %get-tuple-element.146), channel_id=1, source_target_pairs={{0,4},{4,0},{8,12},{12,8},{16,20},{20,16},{24,28},{28,24},{1,5},{5... | collective-permute-start | bytes 6291464 | tf_op jit(solution)/shard_map/ppermute | solution.py:578
  629.6 4.1 collective-permute-start.18
  633.8 19.6 %collective-permute-start.19 = (f32[2,1024]{1,0:T(2,128)S(1)}, f32[2,1024]{1,0:T(2,128)S(1)}, u32[]{:S(2)}, u32[]{:S(2)}) collective-permute-start(f32[2,1024]{1,0:T(2,128)S(1)} %fusion.33), channel_id=1, source_target_pairs={{0,2},{1,3},{2,0},{3,1},{4,6},{5,7},{6,4},{7,5},{8,10},{9,11},{10,... | collective-permute-start | bytes 24584 | tf_op jit(solution)/shard_map/ppermute | solution.py:631
  671.7 26.3 %collective-permute-start.40 = (bf16[1,2,1024,256]{3,2,1,0:T(8,128)(2,1)}, bf16[1,2,1024,256]{3,2,1,0:T(8,128)(2,1)}, u32[]{:S(2)}, u32[]{:S(2)}) collective-permute-start(bf16[1,2,1024,256]{3,2,1,0:T(8,128)(2,1)} %slice_bitcast_fusion.10), channel_id=1, source_target_pairs={{0,16},{4,20},{8,24},{12,28},{16,0},{20,4},{24,8},{28,12},{1,17},{... | collective-permute-start | bytes 3145736 | tf_op jit(solution)/shard_map/ppermute | solution.py:578
  674.8 26.1 %collective-permute-start.39 = (bf16[1,2,1024,256]{3,2,1,0:T(8,128)(2,1)S(1)}, bf16[1,2,1024,256]{3,2,1,0:T(8,128)(2,1)S(1)}, u32[]{:S(2)}, u32[]{:S(2)}) collective-permute-start(bf16[1,2,1024,256]{3,2,1,0:T(8,128)(2,1)S(1)} %slice.278), channel_id=1, source_target_pairs={{0,8},{4,12},{8,0},{12,4},{16,24},{20,28},{24,16},{28,20},{1,9},{5... | collective-permute-start | bytes 3145736 | tf_op jit(solution)/shard_map/ppermute | solution.py:578
  678.9 41.5 %collective-permute-start.42 = (bf16[1,2,1024,256]{3,2,1,0:T(8,128)(2,1)S(1)}, bf16[1,2,1024,256]{3,2,1,0:T(8,128)(2,1)S(1)}, u32[]{:S(2)}, u32[]{:S(2)}) collective-permute-start(bf16[1,2,1024,256]{3,2,1,0:T(8,128)(2,1)S(1)} %slice_bitcast_fusion.8), channel_id=1, source_target_pairs={{0,16},{4,20},{8,24},{12,28},{16,0},{20,4},{24,8},{28,12},{1,17},{... | collective-permute-start | bytes 3145736 | tf_op jit(solution)/shard_map/ppermute | solution.py:578
  679.6 43.8 %collective-permute-start.41 = (bf16[1,2,1024,256]{3,2,1,0:T(8,128)(2,1)S(1)}, bf16[1,2,1024,256]{3,2,1,0:T(8,128)(2,1)S(1)}, u32[]{:S(2)}, u32[]{:S(2)}) collective-permute-start(bf16[1,2,1024,256]{3,2,1,0:T(8,128)(2,1)S(1)} %slice.282), channel_id=1, source_target_pairs={{0,8},{4,12},{8,0},{12,4},{16,24},{20,28},{24,16},{28,20},{1,9},{5... | collective-permute-start | bytes 3145736 | tf_op jit(solution)/shard_map/ppermute | solution.py:578
  703.2 64.0 %collective-permute-start.45 = (bf16[2,2,1024,256]{3,2,1,0:T(8,128)(2,1)}, bf16[2,2,1024,256]{3,2,1,0:T(8,128)(2,1)}, u32[]{:S(2)}, u32[]{:S(2)}) collective-permute-start(bf16[2,2,1024,256]{3,2,1,0:T(8,128)(2,1)} %slice_bitcast_fusion), channel_id=1, source_target_pairs={{0,8},{4,12},{8,0},{12,4},{16,24},{20,28},{24,16},{28,20},{1,9},{5... | collective-permute-start | bytes 6291464 | tf_op jit(solution)/shard_map/ppermute | solution.py:578
  710.1 60.8 %collective-permute-start.43 = (bf16[2,2,1024,256]{3,2,1,0:T(8,128)(2,1)}, bf16[2,2,1024,256]{3,2,1,0:T(8,128)(2,1)S(1)}, u32[]{:S(2)}, u32[]{:S(2)}) collective-permute-start(bf16[2,2,1024,256]{3,2,1,0:T(8,128)(2,1)} %bitcast.61), channel_id=1, source_target_pairs={{0,16},{4,20},{8,24},{12,28},{16,0},{20,4},{24,8},{28,12},{1,17},{... | collective-permute-start | bytes 6291464 | tf_op jit(solution)/shard_map/ppermute | solution.py:578
  737.1 36.4 %collective-permute-start.26 = (bf16[1,4,256,512]{3,2,1,0:T(8,128)(2,1)}, bf16[1,4,256,512]{3,2,1,0:T(8,128)(2,1)S(1)}, u32[]{:S(2)}, u32[]{:S(2)}) collective-permute-start(bf16[1,4,256,512]{3,2,1,0:T(8,128)(2,1)} %get-tuple-element.162), channel_id=1, source_target_pairs={{0,4},{4,0},{8,12},{12,8},{16,20},{20,16},{24,28},{28,24},{1,5},{5... | collective-permute-start | bytes 3145736 | tf_op jit(solution)/shard_map/ppermute | solution.py:578
  737.2 38.4 %collective-permute-start.27 = (bf16[1,4,256,512]{3,2,1,0:T(8,128)(2,1)}, bf16[1,4,256,512]{3,2,1,0:T(8,128)(2,1)}, u32[]{:S(2)}, u32[]{:S(2)}) collective-permute-start(bf16[1,4,256,512]{3,2,1,0:T(8,128)(2,1)} %get-tuple-element.163), channel_id=1, source_target_pairs={{0,4},{4,0},{8,12},{12,8},{16,20},{20,16},{24,28},{28,24},{1,5},{5... | collective-permute-start | bytes 3145736 | tf_op jit(solution)/shard_map/ppermute | solution.py:578
  737.7 37.8 %collective-permute-start.28 = (bf16[1,4,256,512]{3,2,1,0:T(8,128)(2,1)}, bf16[1,4,256,512]{3,2,1,0:T(8,128)(2,1)}, u32[]{:S(2)}, u32[]{:S(2)}) collective-permute-start(bf16[1,4,256,512]{3,2,1,0:T(8,128)(2,1)} %get-tuple-element.164), channel_id=1, source_target_pairs={{0,4},{4,0},{8,12},{12,8},{16,20},{20,16},{24,28},{28,24},{1,5},{5... | collective-permute-start | bytes 3145736 | tf_op jit(solution)/shard_map/ppermute | solution.py:578
  767.1 8.4 collective-permute-start.29
  771.0 26.3 %collective-permute-start.46 = (bf16[1,2,1024,256]{3,2,1,0:T(8,128)(2,1)}, bf16[1,2,1024,256]{3,2,1,0:T(8,128)(2,1)}, u32[]{:S(2)}, u32[]{:S(2)}) collective-permute-start(bf16[1,2,1024,256]{3,2,1,0:T(8,128)(2,1)} %slice_bitcast_fusion.6), channel_id=1, source_target_pairs={{0,16},{4,20},{8,24},{12,28},{16,0},{20,4},{24,8},{28,12},{1,17},{... | collective-permute-start | bytes 3145736 | tf_op jit(solution)/shard_map/ppermute | solution.py:578
  773.6 26.3 %collective-permute-start.44 = (bf16[1,2,1024,256]{3,2,1,0:T(8,128)(2,1)}, bf16[1,2,1024,256]{3,2,1,0:T(8,128)(2,1)}, u32[]{:S(2)}, u32[]{:S(2)}) collective-permute-start(bf16[1,2,1024,256]{3,2,1,0:T(8,128)(2,1)} %slice.286), channel_id=1, source_target_pairs={{0,8},{4,12},{8,0},{12,4},{16,24},{20,28},{24,16},{28,20},{1,9},{5... | collective-permute-start | bytes 3145736 | tf_op jit(solution)/shard_map/ppermute | solution.py:578
  789.4 29.9 %collective-permute-start.30 = (bf16[2,4,128,512]{3,2,1,0:T(8,128)(2,1)}, bf16[2,4,128,512]{3,2,1,0:T(8,128)(2,1)}, u32[]{:S(2)}, u32[]{:S(2)}) collective-permute-start(bf16[2,4,128,512]{3,2,1,0:T(8,128)(2,1)} %slice.216), channel_id=1, source_target_pairs={{0,16},{4,20},{8,24},{12,28},{16,0},{20,4},{24,8},{28,12},{1,17},{... | collective-permute-start | bytes 3145736 | tf_op jit(solution)/shard_map/ppermute | solution.py:578
  792.1 29.5 %collective-permute-start.31 = (bf16[2,4,128,512]{3,2,1,0:T(8,128)(2,1)}, bf16[2,4,128,512]{3,2,1,0:T(8,128)(2,1)}, u32[]{:S(2)}, u32[]{:S(2)}) collective-permute-start(bf16[2,4,128,512]{3,2,1,0:T(8,128)(2,1)} %slice_bitcast_fusion.13), channel_id=1, source_target_pairs={{0,8},{4,12},{8,0},{12,4},{16,24},{20,28},{24,16},{28,20},{1,9},{5... | collective-permute-start | bytes 3145736 | tf_op jit(solution)/shard_map/ppermute | solution.py:578
  806.5 22.5 %collective-permute-start.34 = (f32[20,2048]{1,0:T(8,128)S(1)}, f32[20,2048]{1,0:T(8,128)S(1)}, u32[]{:S(2)}, u32[]{:S(2)}) collective-permute-start(f32[20,2048]{1,0:T(8,128)S(1)} %concatenate.28), channel_id=1, source_target_pairs={{0,4},{4,0},{8,12},{12,8},{16,20},{20,16},{24,28},{28,24},{1,5},{5... | collective-permute-start | bytes 491528 | tf_op jit(solution)/shard_map/ppermute | solution.py:631
  825.3 25.2 %collective-permute-start.32 = (bf16[1,4,128,512]{3,2,1,0:T(8,128)(2,1)S(1)}, bf16[1,4,128,512]{3,2,1,0:T(8,128)(2,1)S(1)}, u32[]{:S(2)}, u32[]{:S(2)}) collective-permute-start(bf16[1,4,128,512]{3,2,1,0:T(8,128)(2,1)S(1)} %slice.268), channel_id=1, source_target_pairs={{0,8},{4,12},{8,0},{12,4},{16,24},{20,28},{24,16},{28,20},{1,9},{5... | collective-permute-start | bytes 1572872 | tf_op jit(solution)/shard_map/ppermute | solution.py:578
  827.0 23.6 %collective-permute-start.33 = (bf16[1,4,128,512]{3,2,1,0:T(8,128)(2,1)S(1)}, bf16[1,4,128,512]{3,2,1,0:T(8,128)(2,1)S(1)}, u32[]{:S(2)}, u32[]{:S(2)}) collective-permute-start(bf16[1,4,128,512]{3,2,1,0:T(8,128)(2,1)S(1)} %slice_bitcast_fusion.14), channel_id=1, source_target_pairs={{0,16},{4,20},{8,24},{12,28},{16,0},{20,4},{24,8},{28,12},{1,17},{... | collective-permute-start | bytes 1572872 | tf_op jit(solution)/shard_map/ppermute | solution.py:578
  829.0 13.9 %collective-permute-start.35 = (f32[20,2048]{1,0:T(8,128)S(1)}, f32[20,2048]{1,0:T(8,128)S(1)}, u32[]{:S(2)}, u32[]{:S(2)}) collective-permute-start(f32[20,2048]{1,0:T(8,128)S(1)} %add.298), channel_id=1, source_target_pairs={{0,8},{4,12},{8,0},{12,4},{16,24},{20,28},{24,16},{28,20},{1,9},{5... | collective-permute-start | bytes 491528 | tf_op jit(solution)/shard_map/ppermute | solution.py:631
  842.9 5.7 collective-permute-start.36
  848.6 7.0 collective-permute-start.37
  855.6 8.7 %collective-permute-start.38 = (f32[20,2048]{1,0:T(8,128)S(1)}, f32[20,2048]{1,0:T(8,128)S(1)}, u32[]{:S(2)}, u32[]{:S(2)}) collective-permute-start(f32[20,2048]{1,0:T(8,128)S(1)} %add.301), channel_id=1, source_target_pairs={{0,2},{1,3},{2,0},{3,1},{4,6},{5,7},{6,4},{7,5},{8,10},{9,11},{10,... | collective-permute-start | bytes 491528 | tf_op jit(solution)/shard_map/ppermute | solution.py:631
  (41 other events, 322.1 us)
Sparse Core Ops, SparseCore 0:
  12.7 83.4 all-gather.4
  162.5 62.3 reduce-scatter.6
  227.8 43.9 reduce-scatter.8
  273.9 45.2 all-gather.6
  321.2 44.6 all-gather.8
  368.0 44.7 reduce-scatter.12
  415.1 45.3 reduce-scatter.10
  466.9 80.1 all-gather.10
  555.2 76.2 reduce-scatter.14
  669.4 76.6 reduce-scatter.16

commit v5 on v4

--- a/solution.py
+++ b/solution.py
@@ -749,33 +749,31 @@
     up_out = halving(up_sums)
     moe = down([gate(acts[0], *up_sums, *up_out.send()), acts[1]], w_down, parts)
     moe_sum = scatter_rows(moe)
-    gate_late = gate_out.add()
-    gate_out.send()
-    down_sent = expert_sums(grad_all, acts, theirs, moe, *gate_late)
-    down_got = core_swap(down_sent)
-
-    attended_grad = nn(gate(middle_all, *down_sent), w_out).astype(bf16)
+    attended_grad = nn(gate(middle_all, moe), w_out).astype(bf16)
     dqn, dkn, dvalue, qdot, kdot, q_gain_part, k_gain_part = attend_back(
         query, key, value, attended_grad, lse, qraw, kraw, q_scale, k_scale, q_gain, k_gain, cosine, sine,
         seg_ids[0], keep_mask[0],
     )
     dots = exchange_sum(jnp.stack([qdot[:, 0], kdot[:, 0]]), ("tensor",)) / features
-    up_late = up_out.add()
-    up_out.send()
-    down_sums = expert_sums(grad_all, acts, mine, dqn, *up_late, added=down_got)
-    down_out = halving(down_sums)
-    down_out.send()
+    gate_late = gate_out.add(dqn)
+    gate_out.send()
+    down_sent = expert_sums(grad_all, acts, theirs, *gate_late)
+    down_got = core_swap(down_sent)
     normed_part, dqraw, dkraw, attn_gain_part = project_back(
         normed_all, dqn, dkn, dvalue, qraw, kraw, q_scale, k_scale, dots[0][:, None], dots[1][:, None],
-        gate(q_gain, *down_sums), k_gain, w_query, w_key, w_value,
+        gate(q_gain, *down_sent), k_gain, w_query, w_key, w_value,
     )
     normed_grad = scatter_rows(normed_part)
+    up_late = up_out.add(normed_part)
+    up_out.send()
+    down_sums = expert_sums(grad_all, acts, mine, *up_late, added=down_got)
+    down_out = halving(down_sums)
     def attention_sums(ids, *others, added=()):
         return attention_wgrad(
             normed_all, middle_all, (dqraw, dkraw, dvalue), attended, gate(ids, *others), dp_size, added
         )
 
-    attn_sent = attention_sums(other_blocks, normed_part)
+    attn_sent = attention_sums(other_blocks, *down_out.send())
     attn_got = core_swap(attn_sent)
 
     def placed(part):

time: 882 us -> 848 us (0.961)
  waiting for transfers between devices: 320 us -> 279 us
    ppermute x32, waiting for transfers between devices: 104 us -> 61.8 us  [pair_swap(): return lax.ppermute(values, 'dp', [(i, i ^ step) for i in range(size)])]
  transfers between devices with their start and end apart: 57 -> 57, of which waited for: 25 -> 20; matrix products, arithmetic and copies ran while one was open for 14% -> 15% of each run, Pallas kernels for 40% -> 42%
where the time goes in v5:
time: 848 us; the launch traced here: 839 us
  Pallas kernels  352 us (42%)
  waiting for transfers between devices  279 us (33%)
  other arithmetic  75.1 us (9%)
  local copies, waits for them, and re-layouts  55.9 us (7%)
  starting transfers between devices  43.1 us (5%)
  matrix products  18.5 us (2%)
  between operations  15.4 us (2%)
    all_gather x4, waiting for transfers between devices, gather_rows(): return lax.all_gather(values, 'tensor', axis=0, tiled=True)  117 us
    pallas_call x6, Pallas kernels, wgrad(): pl.pallas_call(functools.partial(wgrad_kernel, len(lefts), len(added), pe...  103 us
    pallas_call x2, Pallas kernels, experts_block(): pl.pallas_call(functools.partial(expert_kernel, block), grid=(experts,),...  95 us
    ppermute x32, waiting for transfers between devices, pair_swap(): return lax.ppermute(values, 'dp', [(i, i ^ step) for i in range(size)])  61.8 us
    reduce_scatter x6, waiting for transfers between devices, scatter_rows(): return lax.psum_scatter(values, 'tensor', scatter_dimension=0, tiled=True)  56.6 us
    ppermute x9, waiting for transfers between devices, exchange_sum(): lax.ppermute(values, axis, [(i, i ^ step) for i in range(size)])  36 us
    pallas_call x2, Pallas kernels, up_back(): pl.pallas_call(up_back_kernel, grid=(experts // step,), in_specs=[pl.Bloc...  30.1 us
    pallas_call x1, Pallas kernels, down(): pl.pallas_call(functools.partial(down_kernel, parts), grid=(features // b...  24.2 us
  transfers between devices with their start and end apart: 57, of which 20 were waited for; matrix products, arithmetic and copies ran while one was open for 15% of the time, Pallas kernels for 42%

profile of v5, /device:TPU:0, one launch (start us, length us, event | category | flops | bytes accessed | tf_op | source)
XLA Modules:
  0.0 838.8 jit_solution(467647656102316847)
XLA Ops:
  10.1 2.5 multiply_convert_fusion
  12.7 83.6 %all-gather.5.cloned.1.call-done.rows_in = bf16[1024,2048]{1,0:T(8,128)(2,1)} async-done(((bf16[256,2048]{1,0:T(8,128)(2,1)}), bf16[1024,2048]{1,0:T(8,128)(2,1)}) %all-gather.5.cloned.1.call-update) | async-done | bytes 4194320 | tf_op jit(solution)/shard_map/all_gather | solution.py:509
  97.5 5.5 collective-permute-start.2
  103.1 16.3 %project.1 = (f32[1024,512]{1,0:T(8,128)}, f32[1024,512]{1,0:T(8,128)}, bf16[1024,512]{1,0:T(8,128)(2,1)}, f32[2,1024]{1,0:T(2,128)}) custom-call(bf16[1024,2048]{1,0:T(8,128)(2,1)} %all-gather.5.cloned.1.call-done.rows_in, bf16[2048,512]{1,0:T(8,128)(2,1)} %w_query.3, bf16[2048,512]{1,0:T(8,128)(2,1)} %w_key.3, bf16[2048,512]{1,0:T(8,128)(2,1)} %w_value.3), custom_call_target="tpu_custom_call" | custom-call | flops 2899102976 | bytes 1310720 | tf_op jit(solution)/shard_map/project/pallas_call | solution.py:101
  119.3 5.1 collective-permute-done
  125.1 1.9 collective-permute-start.1
  127.0 2.6 collective-permute-done.1
  135.8 15.6 %attend.1 = (bf16[1024,512]{1,0:T(8,128)(2,1)}, bf16[1024,512]{1,0:T(8,128)(2,1)}, bf16[1024,512]{1,0:T(8,128)(2,1)}, f32[1024,512]{1,0:T(8,128)}) custom-call(f32[1024,512]{1,0:T(8,128)} %get-tuple-element.99.qraw, f32[1024,512]{1,0:T(8,128)} %get-tuple-element.100.kraw, bf16[1024,512]{1,0:T(8,128)(2,1)} %get-tuple-element.101.value, ...), custom_call_target="tpu_custom_call" | custom-call | flops 57347878912 | bytes 1179648 | tf_op jit(solution)/shard_map/attend/pallas_call | solution.py:241
  151.4 7.0 collective-permute-done.5.refs_4_
  159.7 2.7 convolution_convert_fusion.1
  162.4 2.6 convolution_convert_fusion
  170.9 54.1 %reduce-scatter.7.cloned.1.call-done = bf16[128,2048]{1,0:T(8,128)(2,1)} async-done(((bf16[512,2048]{1,0:T(8,128)(2,1)}), bf16[128,2048]{1,0:T(8,128)(2,1)}) %reduce-scatter.7.cloned.1.call-update) | async-done | bytes 524304 | tf_op jit(solution)/shard_map/reduce_scatter | solution.py:513
  230.5 1.9 pad.4.router
  232.5 6.7 convert_reduce_fusion
  240.9 6.3 join.1
  247.2 4.8 fusion.40
  252.0 15.1 %up_back.3.back = bf16[512,4096]{1,0:T(8,128)(2,1)} custom-call(bf16[512,2048]{1,0:T(8,128)(2,1)} %bitcast.172, bf16[16,2048,256]{2,1,0:T(8,128)(2,1)} %down_w.5), custom_call_target="tpu_custom_call" | custom-call | flops 3865470464 | bytes 2359296 | tf_op jit(solution)/shard_map/up_back/pallas_call | solution.py:333
  267.1 15.1 %up_back.2.back = bf16[512,4096]{1,0:T(8,128)(2,1)} custom-call(bf16[512,2048]{1,0:T(8,128)(2,1)} %bitcast.175, bf16[16,2048,256]{2,1,0:T(8,128)(2,1)} %down_w.5), custom_call_target="tpu_custom_call" | custom-call | flops 3865470464 | bytes 2359296 | tf_op jit(solution)/shard_map/up_back/pallas_call | solution.py:333
  285.8 33.4 %all-gather.7.cloned.1.call-done.rows_in.refs_0_ = bf16[512,2048]{1,0:T(8,128)(2,1)} async-done(((bf16[128,2048]{1,0:T(8,128)(2,1)}), bf16[512,2048]{1,0:T(8,128)(2,1)}) %all-gather.7.cloned.1.call-update) | async-done | bytes 2097168 | tf_op jit(solution)/shard_map/all_gather | solution.py:509
  319.2 47.5 %experts.2 = (bf16[512,4096]{1,0:T(8,128)(2,1)}, bf16[512,4096]{1,0:T(8,128)(2,1)}, bf16[512,4096]{1,0:T(8,128)(2,1)}, bf16[512,2176]{1,0:T(8,128)(2,1)}) custom-call(bf16[512,2048]{1,0:T(8,128)(2,1)} %all-gather.7.cloned.1.call-done.rows_in.refs_0_, bf16[512,4096]{1,0:T(8,128)(2,1)} %up_back.2.back, f32[512,128]{1,0:T(8,128)} %bitcast.199, ...), custom_call_target="tpu_custom_call" | custom-call | flops 53210619904 | bytes 6291456 | tf_op jit(solution)/shard_map/experts/pallas_call | solution.py:398
  366.9 47.5 %experts.3 = (bf16[512,4096]{1,0:T(8,128)(2,1)}, bf16[512,4096]{1,0:T(8,128)(2,1)}, bf16[512,4096]{1,0:T(8,128)(2,1)}, bf16[512,2176]{1,0:T(8,128)(2,1)}) custom-call(bf16[512,2048]{1,0:T(8,128)(2,1)} %all-gather.9.cloned.1.call-done.rows_in.refs_1_, bf16[512,4096]{1,0:T(8,128)(2,1)} %up_back.3.back, f32[512,128]{1,0:T(8,128)} %bitcast.198, ...), custom_call_target="tpu_custom_call" | custom-call | flops 53210619904 | bytes 6291456 | tf_op jit(solution)/shard_map/experts/pallas_call | solution.py:398
  424.2 17.1 %wgrad.6 = (bf16[2,2048,256]{2,1,0:T(8,128)(2,1)}, bf16[2,2048,256]{2,1,0:T(8,128)(2,1)}, bf16[2,2048,256]{2,1,0:T(8,128)(2,1)}, bf16[2,2048,256]{2,1,0:T(8,128)(2,1)}) custom-call(s32[8]{0:T(128)} %add.276.order, bf16[512,2048]{1,0:T(8,128)(2,1)} %all-gather.7.cloned.1.call-done.rows_in.refs_0_, ...), custom_call_target="tpu_custom_call" | custom-call | flops 3865470464 | bytes 2621440 | tf_op jit(solution)/shard_map/wgrad/pallas_call | solution.py:459
  441.3 16.8 %wgrad.7 = (bf16[2,2048,256]{2,1,0:T(8,128)(2,1)}, bf16[2,2048,256]{2,1,0:T(8,128)(2,1)}, bf16[2,2048,256]{2,1,0:T(8,128)(2,1)}, bf16[2,2048,256]{2,1,0:T(8,128)(2,1)}) custom-call(s32[8]{0:T(128)} %add.276.order, bf16[512,2048]{1,0:T(8,128)(2,1)} %all-gather.7.cloned.1.call-done.rows_in.refs_0_, ...), custom_call_target="tpu_custom_call" | custom-call | flops 3865470464 | bytes 2621440 | tf_op jit(solution)/shard_map/wgrad/pallas_call | solution.py:459
  458.1 2.5 reduce-scatter.11.cloned.1.call-done
  468.1 3.4 collective-permute-done.8.refs_4_
  471.6 2.9 collective-permute-done.9.refs_5_
  474.6 2.9 collective-permute-done.10.refs_6_
  480.5 17.7 %wgrad.8 = (bf16[8,1024,256]{2,1,0:T(8,128)(2,1)}, bf16[8,1024,256]{2,1,0:T(8,128)(2,1)}) custom-call(s32[8]{0:T(128)} %add.270.order, bf16[512,2048]{1,0:T(8,128)(2,1)} %all-gather.7.cloned.1.call-done.rows_in.refs_0_, bf16[512,2048]{1,0:T(8,128)(2,1)} %all-gather.9.cloned.1.call-done.rows_in.refs_1_, bf16[512,4096]{1,0:T(8,128)(2,1)} %get-tuple-element.123.refs_2_, ...), custom_call_target="tpu_custom_call" | custom-call | flops 3865470464 | bytes 2621440 | tf_op jit(solution)/shard_map/wgrad/pallas_call | solution.py:459
  498.2 3.2 slice_bitcast_fusion.5
  502.9 2.3 fusion.39
  506.7 17.6 %wgrad.9 = (bf16[8,1024,256]{2,1,0:T(8,128)(2,1)}, bf16[8,1024,256]{2,1,0:T(8,128)(2,1)}) custom-call(s32[8]{0:T(128)} %add.270.order, bf16[512,2048]{1,0:T(8,128)(2,1)} %all-gather.7.cloned.1.call-done.rows_in.refs_0_, bf16[512,2048]{1,0:T(8,128)(2,1)} %all-gather.9.cloned.1.call-done.rows_in.refs_1_, bf16[512,4096]{1,0:T(8,128)(2,1)} %get-tuple-element.130.refs_2_, ...), custom_call_target="tpu_custom_call" | custom-call | flops 3865470464 | bytes 2621440 | tf_op jit(solution)/shard_map/wgrad/pallas_call | solution.py:459
  524.3 3.2 slice_bitcast_fusion.4
  528.0 2.3 fusion.38
  530.8 24.2 %down.1 = bf16[1024,2048]{1,0:T(8,128)(2,1)} custom-call(bf16[16,2048,256]{2,1,0:T(8,128)(2,1)} %down_w.5, bf16[512,4096]{1,0:T(8,128)(2,1)} %get-tuple-element.143.refs_0_.refs_2_, bf16[512,4096]{1,0:T(8,128)(2,1)} %get-tuple-element.120.refs_1_.refs_3_), custom_call_target="tpu_custom_call" | custom-call | flops 7730940928 | bytes 2621440 | tf_op jit(solution)/shard_map/down/pallas_call | solution.py:491
  555.1 5.5 convolution_convert_fusion.2.out_grad
  560.6 24.1 %attend_back.1 = (f32[1024,512]{1,0:T(8,128)}, f32[1024,512]{1,0:T(8,128)}, bf16[1024,512]{1,0:T(8,128)(2,1)}, f32[1024,1]{1,0:T(8,128)}, f32[1024,1]{1,0:T(8,128)}, /*index=5*/f32[1,512]{1,0:T(1,128)}, f32[1,512]{1,0:T(1,128)}) custom-call(bf16[1024,512]{1,0:T(8,128)(2,1)} %get-tuple-element.144.query, bf16[1024,512]{1,0:T(8,128)(2,1)} %get-tuple-element.145.key, ...), custom_call_target="tpu_custom_call" | custom-call | flops 58435043328 | bytes 2097152 | tf_op jit(solution)/shard_map/attend_back/pallas_call | solution.py:307
  587.3 4.2 fusion.4
  591.5 2.1 fusion.5
  593.6 2.6 collective-permute-start.17
  596.3 16.5 %wgrad.10 = (bf16[2,2048,256]{2,1,0:T(8,128)(2,1)}, bf16[2,2048,256]{2,1,0:T(8,128)(2,1)}, bf16[2,2048,256]{2,1,0:T(8,128)(2,1)}, bf16[2,2048,256]{2,1,0:T(8,128)(2,1)}) custom-call(s32[8]{0:T(128)} %add.276.order, bf16[512,2048]{1,0:T(8,128)(2,1)} %bitcast.176, bf16[512,2048]{1,0:T(8,128)(2,1)} %bitcast.173, ...), custom_call_target="tpu_custom_call" | custom-call | flops 3865470464 | bytes 2621440 | tf_op jit(solution)/shard_map/wgrad/pallas_call | solution.py:459
  618.2 14.1 %project_back.1 = (bf16[1024,2048]{1,0:T(8,128)(2,1)}, bf16[1024,512]{1,0:T(8,128)(2,1)}, bf16[1024,512]{1,0:T(8,128)(2,1)}, f32[1,2048]{1,0:T(1,128)}) custom-call(bf16[1024,2048]{1,0:T(8,128)(2,1)} %all-gather.5.cloned.1.call-done.rows_in, f32[1024,512]{1,0:T(8,128)} %get-tuple-element.148.dqn, f32[1024,512]{1,0:T(8,128)} %get-tuple-element.149.dkn, ...), custom_call_target="tpu_custom_call" | custom-call | flops 2899102976 | bytes 1310720 | tf_op jit(solution)/shard_map/project_back/pallas_call | solution.py:141
  632.3 2.4 slice_bitcast_fusion.10
  636.3 2.2 fusion.3
  639.7 2.7 fusion.2
  646.8 17.7 %wgrad.11 = (bf16[8,1024,256]{2,1,0:T(8,128)(2,1)}, bf16[8,1024,256]{2,1,0:T(8,128)(2,1)}) custom-call(s32[8]{0:T(128)} %add.270.order, bf16[512,2048]{1,0:T(8,128)(2,1)} %bitcast.177, bf16[512,2048]{1,0:T(8,128)(2,1)} %bitcast.174, bf16[512,4096]{1,0:T(8,128)(2,1)} %get-tuple-element.143.refs_0_.refs_2_, ...), custom_call_target="tpu_custom_call" | custom-call | flops 3865470464 | bytes 2621440 | tf_op jit(solution)/shard_map/wgrad/pallas_call | solution.py:459
  664.5 4.6 fusion.37
  670.7 11.1 %attention_wgrad.2 = (bf16[1,4,256,512]{3,2,1,0:T(8,128)(2,1)}, bf16[1,4,256,512]{3,2,1,0:T(8,128)(2,1)}, bf16[1,4,256,512]{3,2,1,0:T(8,128)(2,1)}, bf16[1,4,256,512]{3,2,1,0:T(8,128)(2,1)}) custom-call(s32[4]{0:T(128)} %get-tuple-element.167.order, bf16[1024,2048]{1,0:T(8,128)(2,1)} %all-gather.5.cloned.1.call-done.rows_in, ...), custom_call_target="tpu_custom_call" | custom-call | flops 3865470464 | bytes 524288 | tf_op jit(solution)/shard_map/attention_wgrad/pallas_call | solution.py:192
  683.6 2.0 collective-permute-start.45
  692.5 2.3 pad_maximum_fusion
  698.2 2.3 pad_maximum_fusion.1
  702.5 12.1 %attention_wgrad.3 = (bf16[4,4,128,512]{3,2,1,0:T(8,128)(2,1)}, bf16[4,4,128,512]{3,2,1,0:T(8,128)(2,1)}) custom-call(s32[4]{0:T(128)} %get-tuple-element.174.order, bf16[1024,2048]{1,0:T(8,128)(2,1)} %all-gather.5.cloned.1.call-done.rows_in, bf16[1024,2048]{1,0:T(8,128)(2,1)} %all-gather.11.cloned.1.call-done.middle, ...), custom_call_target="tpu_custom_call" | custom-call | flops 3865470464 | bytes 524288 | tf_op jit(solution)/shard_map/attention_wgrad/pallas_call | solution.py:192
  714.6 2.3 slice.219
  718.2 13.9 %collective-permute-done.45 = bf16[2,2,1024,256]{3,2,1,0:T(8,128)(2,1)} collective-permute-done((bf16[2,2,1024,256]{3,2,1,0:T(8,128)(2,1)}, bf16[2,2,1024,256]{3,2,1,0:T(8,128)(2,1)}, u32[]{:S(2)}, u32[]{:S(2)}) %collective-permute-start.45) | collective-permute-done | bytes 2097184 | tf_op jit(solution)/shard_map/ppermute | solution.py:578
  732.2 2.1 fusion.6
  737.9 2.2 fusion.1
  744.4 3.0 fusion.7
  747.3 34.8 %collective-permute-done.46 = bf16[1,2,1024,256]{3,2,1,0:T(8,128)(2,1)} collective-permute-done((bf16[1,2,1024,256]{3,2,1,0:T(8,128)(2,1)}, bf16[1,2,1024,256]{3,2,1,0:T(8,128)(2,1)}, u32[]{:S(2)}, u32[]{:S(2)}) %collective-permute-start.46) | collective-permute-done | bytes 1048608 | tf_op jit(solution)/shard_map/ppermute | solution.py:578
  785.2 2.3 pad_maximum_fusion.2
  788.0 2.0 add_convert_fusion
  795.7 14.1 %collective-permute-done.35 = f32[20,2048]{1,0:T(8,128)S(1)} collective-permute-done((f32[20,2048]{1,0:T(8,128)S(1)}, f32[20,2048]{1,0:T(8,128)S(1)}, u32[]{:S(2)}, u32[]{:S(2)}) %collective-permute-start.35) | collective-permute-done | bytes 163872 | tf_op jit(solution)/shard_map/ppermute | solution.py:631
  811.2 2.0 maximum_add_fusion.1
  813.2 2.5 collective-permute-done.36
  817.2 4.2 collective-permute-done.37
  823.0 7.5 collective-permute-done.38
  (319 shorter events, 108.5 us)
Async XLA Ops:
  7.2 152.5 %copy-start = (bf16[2048,512]{1,0:T(8,128)(2,1)S(1)}, bf16[2048,512]{1,0:T(8,128)(2,1)}, u32[]{:S(2)}) copy-start(bf16[2048,512]{1,0:T(8,128)(2,1)} %param.28) | copy-start | bytes 6291460
  7.2 89.0 %copy-start.22 = (bf16[256,2048]{1,0:T(8,128)(2,1)S(1)}, bf16[256,2048]{1,0:T(8,128)(2,1)}, u32[]{:S(2)}) copy-start(bf16[256,2048]{1,0:T(8,128)(2,1)} %own) | copy-start | bytes 3145732
  7.2 89.0 %all-gather.5.cloned.1.call-start = ((), (), s32[]{:S(2)}) async-start(), calls=%async_computation.6 | async-start | bytes 5242880 | tf_op jit(solution)/shard_map/all_gather | solution.py:509
  12.6 119.1 %copy-start.46 = (s32[1,1024]{1,0:T(1,128)S(1)}, s32[1,1024]{1,0:T(1,128)}, u32[]{:S(2)}) copy-start(s32[1,1024]{1,0:T(1,128)} %seg_row.1) | copy-start | bytes 12292
  12.6 212.3 %reduce-scatter.7.cloned.1.call-start = ((), (), s32[]{:S(2)}) async-start(), calls=%async_computation.7 | async-start | bytes 2621440 | tf_op jit(solution)/shard_map/reduce_scatter | solution.py:513
  96.2 35.5 %collective-permute-start.3 = (bf16[256,2048]{1,0:T(8,128)(2,1)S(1)}, bf16[256,2048]{1,0:T(8,128)(2,1)}, u32[]{:S(2)}, u32[]{:S(2)}) collective-permute-start(bf16[256,2048]{1,0:T(8,128)(2,1)S(1)} %copy-done.22), channel_id=1, source_target_pairs={{1,0},{2,1},{3,2},{5,4},{6,5},{7,6},{9,8},{10,9},{11,10},{13,12},{... | collective-permute-start | bytes 3145736 | tf_op jit(solution)/shard_map/ppermute | solution.py:562
  97.5 34.2 %collective-permute-start.2 = (bf16[256,2048]{1,0:T(8,128)(2,1)S(1)}, bf16[256,2048]{1,0:T(8,128)(2,1)}, u32[]{:S(2)}, u32[]{:S(2)}) collective-permute-start(bf16[256,2048]{1,0:T(8,128)(2,1)S(1)} %copy-done.22), channel_id=1, source_target_pairs={{0,1},{1,2},{2,3},{4,5},{5,6},{6,7},{8,9},{9,10},{10,11},{12,13},{... | collective-permute-start | bytes 3145736 | tf_op jit(solution)/shard_map/ppermute | solution.py:561
  119.3 5.1 collective-permute-start
  125.1 4.5 collective-permute-start.1
  132.8 25.6 %collective-permute-start.5 = (bf16[256,2048]{1,0:T(8,128)(2,1)}, bf16[256,2048]{1,0:T(8,128)(2,1)}, u32[]{:S(2)}, u32[]{:S(2)}) collective-permute-start(bf16[256,2048]{1,0:T(8,128)(2,1)} %collective-permute-done.3.refs_3_), channel_id=1, source_target_pairs={{1,0},{2,1},{5,4},{6,5},{9,8},{10,9},{13,12},{14,13},{17,16},{18,1... | collective-permute-start | bytes 3145736 | tf_op jit(solution)/shard_map/ppermute | solution.py:562
  134.0 24.3 %collective-permute-start.4 = (bf16[256,2048]{1,0:T(8,128)(2,1)}, bf16[256,2048]{1,0:T(8,128)(2,1)}, u32[]{:S(2)}, u32[]{:S(2)}) collective-permute-start(bf16[256,2048]{1,0:T(8,128)(2,1)} %collective-permute-done.2.refs_0_), channel_id=1, source_target_pairs={{1,2},{2,3},{5,6},{6,7},{9,10},{10,11},{13,14},{14,15},{17,18},{18... | collective-permute-start | bytes 3145736 | tf_op jit(solution)/shard_map/ppermute | solution.py:561
  162.4 119.8 %reduce-scatter.9.cloned.1.call-start = ((), (), s32[]{:S(2)}) async-start(), calls=%async_computation.8 | async-start | bytes 2621440 | tf_op jit(solution)/shard_map/reduce_scatter | solution.py:513
  165.0 154.2 %all-gather.7.cloned.1.call-start = ((), (), s32[]{:S(2)}) async-start(), calls=%async_computation.9 | async-start | bytes 2621440 | tf_op jit(solution)/shard_map/all_gather | solution.py:509
  167.8 58.8 %copy-start.43 = (f32[2048]{0:T(1024)S(1)}, f32[2048]{0:T(1024)}, u32[]{:S(2)}) copy-start(f32[2048]{0:T(1024)} %param.31) | copy-start | bytes 24580
  167.8 60.7 %copy-start.45 = (s32[1024,8]{0,1:T(8,128)S(1)}, s32[1024,8]{0,1:T(8,128)}, u32[]{:S(2)}) copy-start(s32[1024,8]{0,1:T(8,128)} %param.23) | copy-start | bytes 98308
  167.8 61.7 %copy-start.42 = (bf16[2048,16]{0,1:T(8,128)(2,1)S(1)}, bf16[2048,16]{0,1:T(8,128)(2,1)}, u32[]{:S(2)}) copy-start(bf16[2048,16]{0,1:T(8,128)(2,1)} %param.32) | copy-start | bytes 196612
  167.8 73.1 %collective-permute-start.6 = (bf16[256,2048]{1,0:T(8,128)(2,1)}, bf16[256,2048]{1,0:T(8,128)(2,1)}, u32[]{:S(2)}, u32[]{:S(2)}) collective-permute-start(bf16[256,2048]{1,0:T(8,128)(2,1)} %collective-permute-done.4.refs_1_), channel_id=1, source_target_pairs={{2,3},{6,7},{10,11},{14,15},{18,19},{22,23},{26,27},{30,31}} | collective-permute-start | bytes 3145736 | tf_op jit(solution)/shard_map/ppermute | solution.py:561
  169.6 71.3 %collective-permute-start.7 = (bf16[256,2048]{1,0:T(8,128)(2,1)}, bf16[256,2048]{1,0:T(8,128)(2,1)}, u32[]{:S(2)}, u32[]{:S(2)}) collective-permute-start(bf16[256,2048]{1,0:T(8,128)(2,1)} %collective-permute-done.5.refs_4_), channel_id=1, source_target_pairs={{1,0},{5,4},{9,8},{13,12},{17,16},{21,20},{25,24},{29,28}} | collective-permute-start | bytes 3145736 | tf_op jit(solution)/shard_map/ppermute | solution.py:562
  226.5 196.2 %copy-start.3 = (f32[128,2048]{1,0:T(8,128)}, f32[128,2048]{1,0:T(8,128)S(1)}, u32[]{:S(2)}) copy-start(f32[128,2048]{1,0:T(8,128)S(1)} %get-tuple-element.199) | copy-start | bytes 3145732
  227.8 139.1 %all-gather.9.cloned.1.call-start = ((), (), s32[]{:S(2)}) async-start(), calls=%async_computation.10 | async-start | bytes 2621440 | tf_op jit(solution)/shard_map/all_gather | solution.py:509
  285.7 133.1 %reduce-scatter.13.cloned.1.call-start = ((), (), s32[]{:S(2)}) async-start(), calls=%async_computation.12 | async-start | bytes 2785280 | tf_op jit(solution)/shard_map/reduce_scatter | solution.py:513
  366.8 93.8 %reduce-scatter.11.cloned.1.call-start = ((), (), s32[]{:S(2)}) async-start(), calls=%async_computation.11 | async-start | bytes 2785280 | tf_op jit(solution)/shard_map/reduce_scatter | solution.py:513
  414.3 140.8 %all-gather.11.cloned.1.call-start = ((), (), s32[]{:S(2)}) async-start(), calls=%async_computation.14 | async-start | bytes 5242880 | tf_op jit(solution)/shard_map/all_gather | solution.py:509
  466.9 277.5 %reduce-scatter.15.cloned.1.call-start = ((), (), s32[]{:S(2)}) async-start(), calls=%async_computation.13 | async-start | bytes 5242880 | tf_op jit(solution)/shard_map/reduce_scatter | solution.py:513
  466.9 4.6 collective-permute-start.8
  467.0 7.5 collective-permute-start.9
  467.5 10.0 %collective-permute-start.10 = (bf16[2,2048,256]{2,1,0:T(8,128)(2,1)}, bf16[2,2048,256]{2,1,0:T(8,128)(2,1)}, u32[]{:S(2)}, u32[]{:S(2)}) collective-permute-start(bf16[2,2048,256]{2,1,0:T(8,128)(2,1)} %get-tuple-element.127), channel_id=1, source_target_pairs={{0,4},{4,0},{8,12},{12,8},{16,20},{20,16},{24,28},{28,24},{1,5},{5... | collective-permute-start | bytes 6291464 | tf_op jit(solution)/shard_map/ppermute | solution.py:578
  467.6 12.9 %collective-permute-start.11 = (bf16[2,2048,256]{2,1,0:T(8,128)(2,1)}, bf16[2,2048,256]{2,1,0:T(8,128)(2,1)}, u32[]{:S(2)}, u32[]{:S(2)}) collective-permute-start(bf16[2,2048,256]{2,1,0:T(8,128)(2,1)} %get-tuple-element.128), channel_id=1, source_target_pairs={{0,4},{4,0},{8,12},{12,8},{16,20},{20,16},{24,28},{28,24},{1,5},{5... | collective-permute-start | bytes 6291464 | tf_op jit(solution)/shard_map/ppermute | solution.py:578
  468.0 37.2 %collective-permute-start.12 = (bf16[2,2048,256]{2,1,0:T(8,128)(2,1)}, bf16[2,2048,256]{2,1,0:T(8,128)(2,1)}, u32[]{:S(2)}, u32[]{:S(2)}) collective-permute-start(bf16[2,2048,256]{2,1,0:T(8,128)(2,1)} %get-tuple-element.132), channel_id=1, source_target_pairs={{0,4},{4,0},{8,12},{12,8},{16,20},{20,16},{24,28},{28,24},{1,5},{5... | collective-permute-start | bytes 6291464 | tf_op jit(solution)/shard_map/ppermute | solution.py:578
  471.5 35.2 %collective-permute-start.13 = (bf16[2,2048,256]{2,1,0:T(8,128)(2,1)}, bf16[2,2048,256]{2,1,0:T(8,128)(2,1)}, u32[]{:S(2)}, u32[]{:S(2)}) collective-permute-start(bf16[2,2048,256]{2,1,0:T(8,128)(2,1)} %get-tuple-element.133), channel_id=1, source_target_pairs={{0,4},{4,0},{8,12},{12,8},{16,20},{20,16},{24,28},{28,24},{1,5},{5... | collective-permute-start | bytes 6291464 | tf_op jit(solution)/shard_map/ppermute | solution.py:578
  474.5 32.2 %collective-permute-start.14 = (bf16[2,2048,256]{2,1,0:T(8,128)(2,1)}, bf16[2,2048,256]{2,1,0:T(8,128)(2,1)}, u32[]{:S(2)}, u32[]{:S(2)}) collective-permute-start(bf16[2,2048,256]{2,1,0:T(8,128)(2,1)} %get-tuple-element.134), channel_id=1, source_target_pairs={{0,4},{4,0},{8,12},{12,8},{16,20},{20,16},{24,28},{28,24},{1,5},{5... | collective-permute-start | bytes 6291464 | tf_op jit(solution)/shard_map/ppermute | solution.py:578
  477.5 29.2 %collective-permute-start.15 = (bf16[2,2048,256]{2,1,0:T(8,128)(2,1)}, bf16[2,2048,256]{2,1,0:T(8,128)(2,1)}, u32[]{:S(2)}, u32[]{:S(2)}) collective-permute-start(bf16[2,2048,256]{2,1,0:T(8,128)(2,1)} %get-tuple-element.135), channel_id=1, source_target_pairs={{0,4},{4,0},{8,12},{12,8},{16,20},{20,16},{24,28},{28,24},{1,5},{5... | collective-permute-start | bytes 6291464 | tf_op jit(solution)/shard_map/ppermute | solution.py:578
  501.4 83.3 %collective-permute-start.19 = (bf16[2,2,1024,256]{3,2,1,0:T(8,128)(2,1)}, bf16[2,2,1024,256]{3,2,1,0:T(8,128)(2,1)}, u32[]{:S(2)}, u32[]{:S(2)}) collective-permute-start(bf16[2,2,1024,256]{3,2,1,0:T(8,128)(2,1)} %slice_bitcast_fusion.5), channel_id=1, source_target_pairs={{0,8},{4,12},{8,0},{12,4},{16,24},{20,28},{24,16},{28,20},{1,9},{5... | collective-permute-start | bytes 6291464 | tf_op jit(solution)/shard_map/ppermute | solution.py:578
  505.2 79.5 %collective-permute-start.18 = (bf16[2,2,1024,256]{3,2,1,0:T(8,128)(2,1)}, bf16[2,2,1024,256]{3,2,1,0:T(8,128)(2,1)}, u32[]{:S(2)}, u32[]{:S(2)}) collective-permute-start(bf16[2,2,1024,256]{3,2,1,0:T(8,128)(2,1)} %bitcast.16), channel_id=1, source_target_pairs={{0,16},{4,20},{8,24},{12,28},{16,0},{20,4},{24,8},{28,12},{1,17},{... | collective-permute-start | bytes 6291464 | tf_op jit(solution)/shard_map/ppermute | solution.py:578
  527.5 85.8 %collective-permute-start.21 = (bf16[2,2,1024,256]{3,2,1,0:T(8,128)(2,1)}, bf16[2,2,1024,256]{3,2,1,0:T(8,128)(2,1)}, u32[]{:S(2)}, u32[]{:S(2)}) collective-permute-start(bf16[2,2,1024,256]{3,2,1,0:T(8,128)(2,1)} %slice_bitcast_fusion.4), channel_id=1, source_target_pairs={{0,8},{4,12},{8,0},{12,4},{16,24},{20,28},{24,16},{28,20},{1,9},{5... | collective-permute-start | bytes 6291464 | tf_op jit(solution)/shard_map/ppermute | solution.py:578
  530.3 104.4 %collective-permute-start.20 = (bf16[2,2,1024,256]{3,2,1,0:T(8,128)(2,1)}, bf16[2,2,1024,256]{3,2,1,0:T(8,128)(2,1)}, u32[]{:S(2)}, u32[]{:S(2)}) collective-permute-start(bf16[2,2,1024,256]{3,2,1,0:T(8,128)(2,1)} %bitcast.19), channel_id=1, source_target_pairs={{0,16},{4,20},{8,24},{12,28},{16,0},{20,4},{24,8},{28,12},{1,17},{... | collective-permute-start | bytes 6291464 | tf_op jit(solution)/shard_map/ppermute | solution.py:578
  555.1 232.4 %reduce-scatter.17.cloned.1.call-start = ((), (), s32[]{:S(2)}) async-start(), calls=%async_computation.15 | async-start | bytes 5242880 | tf_op jit(solution)/shard_map/reduce_scatter | solution.py:513
  587.3 6.3 collective-permute-start.16
  593.6 19.8 %collective-permute-start.17 = (f32[2,1024]{1,0:T(2,128)S(1)}, f32[2,1024]{1,0:T(2,128)S(1)}, u32[]{:S(2)}, u32[]{:S(2)}) collective-permute-start(f32[2,1024]{1,0:T(2,128)S(1)} %fusion.33), channel_id=1, source_target_pairs={{0,2},{1,3},{2,0},{3,1},{4,6},{5,7},{6,4},{7,5},{8,10},{9,11},{10,... | collective-permute-start | bytes 24584 | tf_op jit(solution)/shard_map/ppermute | solution.py:631
  612.8 31.9 %collective-permute-start.22 = (bf16[2,2048,256]{2,1,0:T(8,128)(2,1)}, bf16[2,2048,256]{2,1,0:T(8,128)(2,1)}, u32[]{:S(2)}, u32[]{:S(2)}) collective-permute-start(bf16[2,2048,256]{2,1,0:T(8,128)(2,1)} %get-tuple-element.156), channel_id=1, source_target_pairs={{0,4},{4,0},{8,12},{12,8},{16,20},{20,16},{24,28},{28,24},{1,5},{5... | collective-permute-start | bytes 6291464 | tf_op jit(solution)/shard_map/ppermute | solution.py:578
  612.8 33.3 %collective-permute-start.23 = (bf16[2,2048,256]{2,1,0:T(8,128)(2,1)}, bf16[2,2048,256]{2,1,0:T(8,128)(2,1)}, u32[]{:S(2)}, u32[]{:S(2)}) collective-permute-start(bf16[2,2048,256]{2,1,0:T(8,128)(2,1)} %get-tuple-element.157), channel_id=1, source_target_pairs={{0,4},{4,0},{8,12},{12,8},{16,20},{20,16},{24,28},{28,24},{1,5},{5... | collective-permute-start | bytes 6291464 | tf_op jit(solution)/shard_map/ppermute | solution.py:578
  613.3 32.9 %collective-permute-start.24 = (bf16[2,2048,256]{2,1,0:T(8,128)(2,1)}, bf16[2,2048,256]{2,1,0:T(8,128)(2,1)}, u32[]{:S(2)}, u32[]{:S(2)}) collective-permute-start(bf16[2,2048,256]{2,1,0:T(8,128)(2,1)} %get-tuple-element.158), channel_id=1, source_target_pairs={{0,4},{4,0},{8,12},{12,8},{16,20},{20,16},{24,28},{28,24},{1,5},{5... | collective-permute-start | bytes 6291464 | tf_op jit(solution)/shard_map/ppermute | solution.py:578
  613.4 33.5 %collective-permute-start.25 = (bf16[2,2048,256]{2,1,0:T(8,128)(2,1)}, bf16[2,2048,256]{2,1,0:T(8,128)(2,1)}, u32[]{:S(2)}, u32[]{:S(2)}) collective-permute-start(bf16[2,2048,256]{2,1,0:T(8,128)(2,1)} %get-tuple-element.159), channel_id=1, source_target_pairs={{0,4},{4,0},{8,12},{12,8},{16,20},{20,16},{24,28},{28,24},{1,5},{5... | collective-permute-start | bytes 6291464 | tf_op jit(solution)/shard_map/ppermute | solution.py:578
  634.7 48.8 %collective-permute-start.39 = (bf16[1,2,1024,256]{3,2,1,0:T(8,128)(2,1)}, bf16[1,2,1024,256]{3,2,1,0:T(8,128)(2,1)}, u32[]{:S(2)}, u32[]{:S(2)}) collective-permute-start(bf16[1,2,1024,256]{3,2,1,0:T(8,128)(2,1)} %slice.279), channel_id=1, source_target_pairs={{0,8},{4,12},{8,0},{12,4},{16,24},{20,28},{24,16},{28,20},{1,9},{5... | collective-permute-start | bytes 3145736 | tf_op jit(solution)/shard_map/ppermute | solution.py:578
  644.7 42.7 %collective-permute-start.40 = (bf16[1,2,1024,256]{3,2,1,0:T(8,128)(2,1)}, bf16[1,2,1024,256]{3,2,1,0:T(8,128)(2,1)}, u32[]{:S(2)}, u32[]{:S(2)}) collective-permute-start(bf16[1,2,1024,256]{3,2,1,0:T(8,128)(2,1)} %slice_bitcast_fusion.10), channel_id=1, source_target_pairs={{0,16},{4,20},{8,24},{12,28},{16,0},{20,4},{24,8},{28,12},{1,17},{... | collective-permute-start | bytes 3145736 | tf_op jit(solution)/shard_map/ppermute | solution.py:578
  646.1 44.4 %collective-permute-start.41 = (bf16[1,2,1024,256]{3,2,1,0:T(8,128)(2,1)}, bf16[1,2,1024,256]{3,2,1,0:T(8,128)(2,1)}, u32[]{:S(2)}, u32[]{:S(2)}) collective-permute-start(bf16[1,2,1024,256]{3,2,1,0:T(8,128)(2,1)} %slice.283), channel_id=1, source_target_pairs={{0,8},{4,12},{8,0},{12,4},{16,24},{20,28},{24,16},{28,20},{1,9},{5... | collective-permute-start | bytes 3145736 | tf_op jit(solution)/shard_map/ppermute | solution.py:578
  646.2 45.8 %collective-permute-start.42 = (bf16[1,2,1024,256]{3,2,1,0:T(8,128)(2,1)}, bf16[1,2,1024,256]{3,2,1,0:T(8,128)(2,1)}, u32[]{:S(2)}, u32[]{:S(2)}) collective-permute-start(bf16[1,2,1024,256]{3,2,1,0:T(8,128)(2,1)} %slice_bitcast_fusion.8), channel_id=1, source_target_pairs={{0,16},{4,20},{8,24},{12,28},{16,0},{20,4},{24,8},{28,12},{1,17},{... | collective-permute-start | bytes 3145736 | tf_op jit(solution)/shard_map/ppermute | solution.py:578
  681.7 10.2 %collective-permute-start.26 = (bf16[1,4,256,512]{3,2,1,0:T(8,128)(2,1)}, bf16[1,4,256,512]{3,2,1,0:T(8,128)(2,1)S(1)}, u32[]{:S(2)}, u32[]{:S(2)}) collective-permute-start(bf16[1,4,256,512]{3,2,1,0:T(8,128)(2,1)} %get-tuple-element.170), channel_id=1, source_target_pairs={{0,4},{4,0},{8,12},{12,8},{16,20},{20,16},{24,28},{28,24},{1,5},{5... | collective-permute-start | bytes 3145736 | tf_op jit(solution)/shard_map/ppermute | solution.py:578
  683.6 48.6 %collective-permute-start.45 = (bf16[2,2,1024,256]{3,2,1,0:T(8,128)(2,1)}, bf16[2,2,1024,256]{3,2,1,0:T(8,128)(2,1)}, u32[]{:S(2)}, u32[]{:S(2)}) collective-permute-start(bf16[2,2,1024,256]{3,2,1,0:T(8,128)(2,1)} %slice_bitcast_fusion.1), channel_id=1, source_target_pairs={{0,8},{4,12},{8,0},{12,4},{16,24},{20,28},{24,16},{28,20},{1,9},{5... | collective-permute-start | bytes 6291464 | tf_op jit(solution)/shard_map/ppermute | solution.py:578
  689.1 48.8 %collective-permute-start.43 = (bf16[2,2,1024,256]{3,2,1,0:T(8,128)(2,1)}, bf16[2,2,1024,256]{3,2,1,0:T(8,128)(2,1)}, u32[]{:S(2)}, u32[]{:S(2)}) collective-permute-start(bf16[2,2,1024,256]{3,2,1,0:T(8,128)(2,1)} %bitcast.30), channel_id=1, source_target_pairs={{0,16},{4,20},{8,24},{12,28},{16,0},{20,4},{24,8},{28,12},{1,17},{... | collective-permute-start | bytes 6291464 | tf_op jit(solution)/shard_map/ppermute | solution.py:578
  690.4 10.1 %collective-permute-start.27 = (bf16[1,4,256,512]{3,2,1,0:T(8,128)(2,1)S(1)}, bf16[1,4,256,512]{3,2,1,0:T(8,128)(2,1)S(1)}, u32[]{:S(2)}, u32[]{:S(2)}) collective-permute-start(bf16[1,4,256,512]{3,2,1,0:T(8,128)(2,1)S(1)} %copy-done.62), channel_id=1, source_target_pairs={{0,4},{4,0},{8,12},{12,8},{16,20},{20,16},{24,28},{28,24},{1,5},{5... | collective-permute-start | bytes 3145736 | tf_op jit(solution)/shard_map/ppermute | solution.py:578
  692.0 8.6 %collective-permute-start.28 = (bf16[1,4,256,512]{3,2,1,0:T(8,128)(2,1)S(1)}, bf16[1,4,256,512]{3,2,1,0:T(8,128)(2,1)S(1)}, u32[]{:S(2)}, u32[]{:S(2)}) collective-permute-start(bf16[1,4,256,512]{3,2,1,0:T(8,128)(2,1)S(1)} %copy-done.61), channel_id=1, source_target_pairs={{0,4},{4,0},{8,12},{12,8},{16,20},{20,16},{24,28},{28,24},{1,5},{5... | collective-permute-start | bytes 3145736 | tf_op jit(solution)/shard_map/ppermute | solution.py:578
  692.0 10.5 %collective-permute-start.29 = (bf16[1,4,256,512]{3,2,1,0:T(8,128)(2,1)S(1)}, bf16[1,4,256,512]{3,2,1,0:T(8,128)(2,1)}, u32[]{:S(2)}, u32[]{:S(2)}) collective-permute-start(bf16[1,4,256,512]{3,2,1,0:T(8,128)(2,1)S(1)} %copy-done.60), channel_id=1, source_target_pairs={{0,4},{4,0},{8,12},{12,8},{16,20},{20,16},{24,28},{28,24},{1,5},{5... | collective-permute-start | bytes 3145736 | tf_op jit(solution)/shard_map/ppermute | solution.py:578
  716.8 70.6 %collective-permute-start.30 = (bf16[2,4,128,512]{3,2,1,0:T(8,128)(2,1)}, bf16[2,4,128,512]{3,2,1,0:T(8,128)(2,1)}, u32[]{:S(2)}, u32[]{:S(2)}) collective-permute-start(bf16[2,4,128,512]{3,2,1,0:T(8,128)(2,1)} %slice.219), channel_id=1, source_target_pairs={{0,16},{4,20},{8,24},{12,28},{16,0},{20,4},{24,8},{28,12},{1,17},{... | collective-permute-start | bytes 3145736 | tf_op jit(solution)/shard_map/ppermute | solution.py:578
  735.3 46.9 %collective-permute-start.46 = (bf16[1,2,1024,256]{3,2,1,0:T(8,128)(2,1)}, bf16[1,2,1024,256]{3,2,1,0:T(8,128)(2,1)}, u32[]{:S(2)}, u32[]{:S(2)}) collective-permute-start(bf16[1,2,1024,256]{3,2,1,0:T(8,128)(2,1)} %slice_bitcast_fusion.6), channel_id=1, source_target_pairs={{0,16},{4,20},{8,24},{12,28},{16,0},{20,4},{24,8},{28,12},{1,17},{... | collective-permute-start | bytes 3145736 | tf_op jit(solution)/shard_map/ppermute | solution.py:578
  741.3 42.4 %collective-permute-start.44 = (bf16[1,2,1024,256]{3,2,1,0:T(8,128)(2,1)}, bf16[1,2,1024,256]{3,2,1,0:T(8,128)(2,1)}, u32[]{:S(2)}, u32[]{:S(2)}) collective-permute-start(bf16[1,2,1024,256]{3,2,1,0:T(8,128)(2,1)} %slice.287), channel_id=1, source_target_pairs={{0,8},{4,12},{8,0},{12,4},{16,24},{20,28},{24,16},{28,20},{1,9},{5... | collective-permute-start | bytes 3145736 | tf_op jit(solution)/shard_map/ppermute | solution.py:578
  743.1 44.8 %collective-permute-start.31 = (bf16[2,4,128,512]{3,2,1,0:T(8,128)(2,1)}, bf16[2,4,128,512]{3,2,1,0:T(8,128)(2,1)}, u32[]{:S(2)}, u32[]{:S(2)}) collective-permute-start(bf16[2,4,128,512]{3,2,1,0:T(8,128)(2,1)} %slice_bitcast_fusion.13), channel_id=1, source_target_pairs={{0,8},{4,12},{8,0},{12,4},{16,24},{20,28},{24,16},{28,20},{1,9},{5... | collective-permute-start | bytes 3145736 | tf_op jit(solution)/shard_map/ppermute | solution.py:578
  787.5 7.6 collective-permute-start.34
  791.8 25.1 %collective-permute-start.32 = (bf16[1,4,128,512]{3,2,1,0:T(8,128)(2,1)S(1)}, bf16[1,4,128,512]{3,2,1,0:T(8,128)(2,1)S(1)}, u32[]{:S(2)}, u32[]{:S(2)}) collective-permute-start(bf16[1,4,128,512]{3,2,1,0:T(8,128)(2,1)S(1)} %slice.269), channel_id=1, source_target_pairs={{0,8},{4,12},{8,0},{12,4},{16,24},{20,28},{24,16},{28,20},{1,9},{5... | collective-permute-start | bytes 1572872 | tf_op jit(solution)/shard_map/ppermute | solution.py:578
  793.3 23.7 %collective-permute-start.33 = (bf16[1,4,128,512]{3,2,1,0:T(8,128)(2,1)S(1)}, bf16[1,4,128,512]{3,2,1,0:T(8,128)(2,1)S(1)}, u32[]{:S(2)}, u32[]{:S(2)}) collective-permute-start(bf16[1,4,128,512]{3,2,1,0:T(8,128)(2,1)S(1)} %slice_bitcast_fusion.14), channel_id=1, source_target_pairs={{0,16},{4,20},{8,24},{12,28},{16,0},{20,4},{24,8},{28,12},{1,17},{... | collective-permute-start | bytes 1572872 | tf_op jit(solution)/shard_map/ppermute | solution.py:578
  795.1 14.6 %collective-permute-start.35 = (f32[20,2048]{1,0:T(8,128)S(1)}, f32[20,2048]{1,0:T(8,128)S(1)}, u32[]{:S(2)}, u32[]{:S(2)}) collective-permute-start(f32[20,2048]{1,0:T(8,128)S(1)} %add.298), channel_id=1, source_target_pairs={{0,8},{4,12},{8,0},{12,4},{16,24},{20,28},{24,16},{28,20},{1,9},{5... | collective-permute-start | bytes 491528 | tf_op jit(solution)/shard_map/ppermute | solution.py:631
  809.8 5.9 collective-permute-start.36
  815.7 5.7 collective-permute-start.37
  821.5 8.9 %collective-permute-start.38 = (f32[20,2048]{1,0:T(8,128)S(1)}, f32[20,2048]{1,0:T(8,128)S(1)}, u32[]{:S(2)}, u32[]{:S(2)}) collective-permute-start(f32[20,2048]{1,0:T(8,128)S(1)} %add.301), channel_id=1, source_target_pairs={{0,2},{1,3},{2,0},{3,1},{4,6},{5,7},{6,4},{7,5},{8,10},{9,11},{10,... | collective-permute-start | bytes 491528 | tf_op jit(solution)/shard_map/ppermute | solution.py:631
  (56 other events, 548.1 us)
Sparse Core Ops, SparseCore 0:
  12.7 83.4 all-gather.4
  162.5 62.4 reduce-scatter.6
  227.9 43.9 reduce-scatter.8
  273.9 45.2 all-gather.6
  321.2 44.6 all-gather.8
  368.1 44.6 reduce-scatter.12
  415.1 45.3 reduce-scatter.10
  467.0 80.1 all-gather.10
  555.2 76.5 reduce-scatter.14
  634.1 77.2 reduce-scatter.16

commit v6 on v5

--- a/solution.py
+++ b/solution.py
@@ -40,7 +40,7 @@
 
 
 def cost(flops, moved, special=0):
-    return pl.CostEstimate(flops=int(1.5 * PACE * flops + 6e4 * PACE * special), bytes_accessed=moved // 8, transcendentals=0)
+    return pl.CostEstimate(flops=int(1.5 * PACE * flops), bytes_accessed=moved // 8, transcendentals=0)
 
 
 def rms_scale(values):
@@ -199,7 +199,7 @@
         ),
         out_shape=out_shape,
         compiler_params=params(),
-        cost_estimate=cost(8 * rows_in.shape[0] * features * width, 4 * features * width),
+        cost_estimate=cost(0, 0),
         name="attention_wgrad",
     )(order, rows_in, middle, *sides, attended, *added)
 
@@ -342,7 +342,8 @@
     )(grad, down_w)
 
 
-def expert_kernel(block, rows_in, back, routed, router, gate_w, up_w, act_out, dgate_out, dup_out, grad_out, comb, dcomb, total):
+def expert_kernel(block, peers, per, order, rows_in, back, routed, router, gate_w, up_w, *refs):
+    acts, (dgate_out, dup_out, grad_out, comb, dcomb, total) = refs[-6 - peers : -6], refs[-6:]
     at = pl.program_id(0)
     rows, features = rows_in.shape
     lane = lax.broadcasted_iota(jnp.int32, (block, LANES), 1)
@@ -360,7 +361,7 @@
         dcomb[...] = jnp.zeros_like(dcomb)
 
     gate, up = gate_w[0], up_w[0]
-    mine = lane == at
+    mine = lane == order[at]
     for start in range(0, rows, block):
         here = slice(start, start + block)
         taken = rows_in[here, :]
@@ -373,7 +374,13 @@
         inner = active * pre_up
         share_grad = jnp.sum(inner * behind, axis=1, keepdims=True)
         dcomb[here, :] = jnp.where(mine, share_grad, dcomb[here, :])
-        act_out[here, :] = (inner * share).astype(bf16)
+        act = (inner * share).astype(bf16)
+        for peer in range(peers):
+
+            @pl.when(at // per == peer)
+            def _(peer=peer):
+                acts[peer][here, :] = act
+
         inner_grad = behind * share
         dgate = (inner_grad * pre_up * (sigmoid + active * (1.0 - sigmoid))).astype(bf16)
         dup = (inner_grad * active).astype(bf16)
@@ -387,38 +394,50 @@
         grad_out[:, features:] = dcomb[...].astype(bf16)
 
 
-def experts_block(rows_in, back, routed, router, gate_w, up_w):
+def experts_chunk(chunk, order, per, rows_in, back, routed, router, gate_w, up_w, filled=()):
     rows, features = rows_in.shape
     experts, _, width = gate_w.shape
+    peers = experts // per
     block = min(512, rows)
-    whole = lambda *shape: pl.BlockSpec(shape, lambda e: (0, 0))
-    column = pl.BlockSpec((rows, width), lambda e: (0, e))
-    weight = pl.BlockSpec((1, features, width), lambda e: (e, 0, 0))
-    wide = jax.ShapeDtypeStruct((rows, experts * width), bf16)
-    return pl.pallas_call(
-        functools.partial(expert_kernel, block),
-        grid=(experts,),
-        in_specs=[whole(rows, features), column, whole(rows, LANES), whole(features, LANES), weight, weight],
-        out_specs=[column, column, column, whole(rows, features + LANES)],
-        out_shape=[wide, wide, wide, jax.ShapeDtypeStruct((rows, features + LANES), bf16)],
-        scratch_shapes=[pltpu.VMEM((rows, LANES), f32), pltpu.VMEM((rows, LANES), f32), pltpu.VMEM((rows, features), f32)],
-        compiler_params=params(),
-        cost_estimate=cost(8 * rows * features * experts * width, 4 * experts * width * (features + 2 * rows), rows * experts * width),
+    whole = lambda *shape: pl.BlockSpec(shape, lambda i, ids: (0, 0))
+    column = pl.BlockSpec((rows, width), lambda i, ids: (chunk, ids[i]))
+    act = lambda peer: pl.BlockSpec((rows, width), lambda i, ids: (chunk, jnp.clip(i - peer * per, 0, per - 1)))
+    weight = pl.BlockSpec((1, features, width), lambda i, ids: (ids[i], 0, 0))
+    sds = lambda *shape: jax.ShapeDtypeStruct(shape, bf16)
+    result = pl.pallas_call(
+        functools.partial(expert_kernel, block, peers, per),
+        grid_spec=pltpu.PrefetchScalarGridSpec(
+            num_scalar_prefetch=1,
+            grid=(experts,),
+            in_specs=[whole(rows, features), column, whole(rows, LANES), whole(features, LANES), weight, weight]
+            + [pl.BlockSpec(memory_space=pl.ANY)] * len(filled),
+            out_specs=[act(peer) for peer in range(peers)] + [column, column, whole(rows, features + LANES)],
+            scratch_shapes=[pltpu.VMEM((rows, LANES), f32), pltpu.VMEM((rows, LANES), f32), pltpu.VMEM((rows, features), f32)],
+        ),
+        out_shape=[sds(CHUNKS * rows, per * width)] * peers
+        + [sds(CHUNKS * rows, experts * width)] * 2
+        + [sds(rows, features + LANES)],
+        input_output_aliases={7 + at: at for at in range(len(filled))},
+        compiler_params=params(),
+        cost_estimate=cost(8 * rows * features * experts * width, 4 * experts * width * (features + 2 * rows)),
         name="experts",
-    )(rows_in, back, routed, router, gate_w, up_w)
+    )(order, rows_in, back, routed, router, gate_w, up_w, *filled)
+    return result[:-1], result[-1]
 
 
 def wgrad_kernel(count, extra, per, block, order, *refs):
-    lefts, rights = refs[:count], refs[count : 2 * count]
-    added = refs[2 * count : 2 * count + extra]
-    outs = refs[2 * count + extra :]
+    lefts, right = refs[:count], refs[count]
+    added = refs[count + 1 : count + 1 + extra]
+    outs = refs[count + 1 + extra :]
     at = pl.program_id(0)
     features = lefts[0].shape[1]
 
     def piece(start, stop):
-        total = tn(lefts[0][:, start:stop], rights[0][...])
-        for left, right in zip(lefts[1:], rights[1:]):
-            total = total + tn(left[:, start:stop], right[...])
+        total, row = None, 0
+        for left in lefts:
+            part = tn(left[:, start:stop], right[row : row + left.shape[0], :])
+            total = part if total is None else total + part
+            row += left.shape[0]
         return total
 
     if not added:
@@ -440,7 +459,7 @@
                 outs[start // half][0, start % half : start % half + block, :] = total.astype(bf16)
 
 
-def wgrad(lefts, rights, order, width, per, added=()):
+def wgrad(lefts, right, order, width, per, added=()):
     features = lefts[0].shape[1]
     experts = order.shape[0]
     groups = experts // per
@@ -462,7 +481,7 @@
             num_scalar_prefetch=1,
             grid=(experts,),
             in_specs=[pl.BlockSpec(left.shape, lambda i, ids: (0, 0)) for left in lefts]
-            + [pl.BlockSpec((right.shape[0], width), lambda i, ids: (0, ids[i])) for right in rights]
+            + [pl.BlockSpec((right.shape[0], width), lambda i, ids: (0, ids[i]))]
             + (groups_specs if added else []),
             out_specs=out_specs,
         ),
@@ -470,35 +489,68 @@
         compiler_params=params(),
         cost_estimate=cost(2 * rows * features * experts * width, 2 * (rows + 2 * experts * width) * features),
         name="wgrad",
-    )(order, *lefts, *rights, *added)
-
-
-def down_kernel(parts, down_w, *refs):
+    )(order, *lefts, right, *added)
+
+
+def down_kernel(parts, per, order, down_w, *refs):
     acts, out = refs[:-1], refs[-1]
-    joined = jnp.concatenate([down_w[e] for e in range(down_w.shape[0])], axis=1)
-    block = acts[0].shape[0] // parts
-    for at, act in enumerate(acts):
-        result = nt(act[...], joined).astype(out.dtype)
+    total = None
+    for peer, act in enumerate(acts):
+        joined = jnp.concatenate([down_w[order[peer * per + at]] for at in range(per)], axis=1)
+        part = nt(act[...], joined)
+        total = part if total is None else total + part
+    block = total.shape[0] // (parts * CHUNKS)
+    for chunk in range(CHUNKS):
         for part in range(parts):
-            start = (part * len(acts) + at) * block
-            out[start : start + block, :] = result[part * block : (part + 1) * block, :]
-
-
-def down(acts, down_w, parts):
-    rows = sum(act.shape[0] for act in acts)
+            to, start = (part * CHUNKS + chunk) * block, (chunk * parts + part) * block
+            out[to : to + block, :] = total[start : start + block, :].astype(out.dtype)
+
+
+def down(acts, order, down_w, parts):
+    rows = acts[0].shape[0]
     experts, features, width = down_w.shape
     block = min(256, features)
     return pl.pallas_call(
-        functools.partial(down_kernel, parts),
-        grid=(features // block,),
-        in_specs=[pl.BlockSpec((experts, block, width), lambda n: (0, n, 0))]
-        + [pl.BlockSpec(act.shape, lambda n: (0, 0)) for act in acts],
-        out_specs=pl.BlockSpec((rows, block), lambda n: (0, n)),
+        functools.partial(down_kernel, parts, experts // len(acts)),
+        grid_spec=pltpu.PrefetchScalarGridSpec(
+            num_scalar_prefetch=1,
+            grid=(features // block,),
+            in_specs=[pl.BlockSpec((experts, block, width), lambda n, ids: (0, n, 0))]
+            + [pl.BlockSpec(act.shape, lambda n, ids: (0, 0)) for act in acts],
+            out_specs=pl.BlockSpec((rows, block), lambda n, ids: (0, n)),
+        ),
         out_shape=jax.ShapeDtypeStruct((rows, features), bf16),
         compiler_params=params(),
         cost_estimate=cost(2 * rows * features * experts * width, 2 * (rows + experts * width) * features),
         name="down",
-    )(down_w, *acts)
+    )(order, down_w, *acts)
+
+
+def owner_wgrad_kernel(count, *refs):
+    lefts, rights, out = refs[:count], refs[count : 2 * count], refs[2 * count]
+    width = out.shape[2]
+    total = tn(lefts[0][...], rights[0][...])
+    for left, right in zip(lefts[1:], rights[1:]):
+        total = total + tn(left[...], right[...])
+    for at in range(out.shape[0]):
+        out[at] = total[:, at * width : (at + 1) * width]
+
+
+def owner_wgrad(lefts, rights, width):
+    rows, features = lefts[0].shape
+    columns = rights[0].shape[1]
+    block = min(256, features)
+    return pl.pallas_call(
+        functools.partial(owner_wgrad_kernel, len(lefts)),
+        grid=(features // block,),
+        in_specs=[pl.BlockSpec((rows, block), lambda n: (0, n)) for _ in lefts]
+        + [pl.BlockSpec((rows, columns), lambda n: (0, 0)) for _ in rights],
+        out_specs=pl.BlockSpec((columns // width, block, width), lambda n: (0, n, 0)),
+        out_shape=jax.ShapeDtypeStruct((columns // width, features, width), f32),
+        compiler_params=params(),
+        cost_estimate=cost(0, 0),
+        name="owner_wgrad",
+    )(*lefts, *rights)
 
 
 def gate(value, *others):
@@ -529,22 +581,23 @@
 
 
 def join(slots, own, ups, downs):
+    parts = len(ups) + 1
     rows, columns = own.shape
-    parts = len(ups) + 1
-    whole = pl.BlockSpec((rows, columns), lambda i, to: (0, 0))
+    split = (CHUNKS, rows // CHUNKS, columns)
+    whole = pl.BlockSpec(split, lambda i, to: (0, 0, 0))
     return pl.pallas_call(
         functools.partial(join_kernel, parts),
         grid_spec=pltpu.PrefetchScalarGridSpec(
             num_scalar_prefetch=1,
             grid=(parts,),
             in_specs=[whole] * (2 * parts - 1),
-            out_specs=pl.BlockSpec((rows, columns), lambda i, to: (to[i], 0)),
+            out_specs=pl.BlockSpec(split, lambda i, to: (0, to[i], 0)),
         ),
-        out_shape=jax.ShapeDtypeStruct((parts * rows, columns), own.dtype),
+        out_shape=jax.ShapeDtypeStruct((CHUNKS, parts * rows // CHUNKS, columns), own.dtype),
         compiler_params=params(),
         cost_estimate=cost(0, 0),
         name="join",
-    )(slots, own, *ups, *downs)
+    )(slots, *(piece.reshape(split) for piece in (own, *ups, *downs)))
 
 
 class Chain:
@@ -623,6 +676,33 @@
         return jnp.concatenate([kept[0].astype(f32) for kept in self.kept], axis=1)
 
 
+class Spread:
+    def __init__(self, values):
+        self.pieces = {0: values}
+        self.steps = sorted((k for k in range(2, lax.axis_size("dp"), 2)), key=lambda k: (k.bit_count(), k))
+
+    def first(self):
+        near = [k for k in self.steps if k.bit_count() == 1]
+        for k in near:
+            self.pieces[k] = pair_swap(self.pieces[0], k)
+        return [self.pieces[k] for k in near]
+
+    def rest(self):
+        half = self.pieces[0].shape[0] // 2
+        got = []
+        for k in self.steps:
+            if k not in self.pieces:
+                low, high = k & -k, 1 << (k.bit_length() - 1)
+                got += [pair_swap(self.pieces[k ^ high][:half], high), pair_swap(self.pieces[k ^ low][half:], low)]
+                self.pieces[k] = jnp.concatenate(got[-2:])
+        return got
+
+    def all(self):
+        for k in [0] + self.steps:
+            self.pieces[k ^ 1] = pair_swap(self.pieces[k], 1)
+        return [self.pieces[k] for k in range(len(self.pieces))]
+
+
 def exchange_sum(values, axes):
     for axis in axes:
         size = lax.axis_size(axis)
@@ -688,9 +768,10 @@
     routed = jnp.sum((idle_routes[:, :, None] == expert_ids[None, None, :]).astype(f32), axis=1)
     router_wide = jnp.pad(idle_router, ((0, 0), (0, LANES - experts)))
     routed_own = lax.dynamic_slice_in_dim(routed, part_at * shard_rows, shard_rows, 0)[:, :experts]
-    grad_group = behind.joined()
-    grad_all = [chunk_of(grad_group, c) for c in chunks]
-    backs = [up_back(gate(rows, routed, router_wide), w_down) for rows in grad_all]
+    grad_rows = behind.joined().reshape(group_rows, features)
+    back = up_back(gate(grad_rows, routed, router_wide), w_down)
+    spread = Spread(grad_rows)
+    spread_first = spread.first()
 
     middles, scales, ffn_own = [], [], []
 
@@ -704,16 +785,20 @@
         return normed
 
     ffn_all = [gather_rows(middle_of(0, summed[0]))]
-    ffn_all.append(gather_rows(middle_of(1, gate(summed[1], ffn_own[0], *backs))))
-    acts, dgates, dups, expert_grads = [], [], [], []
+    ffn_all.append(gather_rows(middle_of(1, gate(summed[1], ffn_own[0], back))))
+    dp_at = lax.axis_index("dp")
+    owners = jnp.arange(dp_size, dtype=jnp.int32) ^ dp_at
+    order = (owners[:, None] * per + jnp.arange(per, dtype=jnp.int32)).reshape(-1)
+    filled, expert_grads = (), []
     for c in chunks:
-        here = gate(chunk_of(routed, c), *backs, *acts[-1:])
-        act, dgate, dup, grads = experts_block(ffn_all[c], backs[c], here, router_wide, w_gate, w_up)
-        acts.append(act)
-        dgates.append(dgate)
-        dups.append(dup)
-        expert_grads.append(grads)
-    expert_grads = [scatter_rows(grads) for grads in expert_grads]
+        here = gate(chunk_of(routed, c), back, *filled, *(spread_first if c else ()))
+        filled, grads = experts_chunk(c, order, per, ffn_all[c], back, here, router_wide, w_gate, w_up, filled)
+        expert_grads.append(scatter_rows(grads))
+    acts, (dgates, dups) = filled[:-2], filled[-2:]
+    spread_rest = spread.rest()
+    peers = sorted(range(1, dp_size), key=lambda k: (k.bit_count(), k))
+    act_pieces = {k: pair_swap(acts[k], k) for k in peers}
+    act_slots = [[act_pieces[k] for k in peers[at * 3 * dp_size // 8 : (at + 1) * 3 * dp_size // 8]] for at in range(3)]
 
     ffn_gain_parts, router_parts, middle_grads = [], [], []
 
@@ -736,20 +821,21 @@
     def halving(sums):
         return Halving([half.reshape((dp_size // 2, per) + half.shape[1:]) for half in sums])
 
-    first = middle_back(0, gate(expert_grads[0], acts[1]).astype(f32))
+    first = middle_back(0, gate(expert_grads[0], dups, *spread_rest).astype(f32))
     gate_sent = expert_sums(ffn_all, dgates, theirs, first)
     gate_got = core_swap(gate_sent)
-    up_sent = expert_sums(ffn_all, dups, theirs, *gate_sent)
+    up_sent = expert_sums(ffn_all, dups, theirs, *gate_sent, *act_slots[0])
     up_got = core_swap(up_sent)
     second = middle_back(1, gate(expert_grads[1], *up_sent).astype(f32))
     middle_all = gather_rows(jnp.concatenate([first, second]))
-    gate_sums = expert_sums(ffn_all, dgates, mine, second, added=gate_got)
+    gate_sums = expert_sums(ffn_all, dgates, mine, second, *act_slots[1], added=gate_got)
     gate_out = halving(gate_sums)
-    up_sums = expert_sums(ffn_all, dups, mine, *gate_sums, *gate_out.send(), added=up_got)
+    moe = down(acts, gate(order, *gate_sums, *gate_out.send(), *act_slots[2]), w_down, parts)
+    moe_sum = scatter_rows(moe)
+    up_sums = expert_sums(ffn_all, dups, mine, moe, added=up_got)
     up_out = halving(up_sums)
-    moe = down([gate(acts[0], *up_sums, *up_out.send()), acts[1]], w_down, parts)
-    moe_sum = scatter_rows(moe)
-    attended_grad = nn(gate(middle_all, moe), w_out).astype(bf16)
+
+    attended_grad = nn(gate(middle_all, *up_out.send()), w_out).astype(bf16)
     dqn, dkn, dvalue, qdot, kdot, q_gain_part, k_gain_part = attend_back(
         query, key, value, attended_grad, lse, qraw, kraw, q_scale, k_scale, q_gain, k_gain, cosine, sine,
         seg_ids[0], keep_mask[0],
@@ -757,29 +843,29 @@
     dots = exchange_sum(jnp.stack([qdot[:, 0], kdot[:, 0]]), ("tensor",)) / features
     gate_late = gate_out.add(dqn)
     gate_out.send()
-    down_sent = expert_sums(grad_all, acts, theirs, *gate_late)
-    down_got = core_swap(down_sent)
     normed_part, dqraw, dkraw, attn_gain_part = project_back(
         normed_all, dqn, dkn, dvalue, qraw, kraw, q_scale, k_scale, dots[0][:, None], dots[1][:, None],
-        gate(q_gain, *down_sent), k_gain, w_query, w_key, w_value,
+        gate(q_gain, *gate_late), k_gain, w_query, w_key, w_value,
     )
     normed_grad = scatter_rows(normed_part)
-    up_late = up_out.add(normed_part)
-    up_out.send()
-    down_sums = expert_sums(grad_all, acts, mine, *up_late, added=down_got)
-    down_out = halving(down_sums)
+
     def attention_sums(ids, *others, added=()):
         return attention_wgrad(
             normed_all, middle_all, (dqraw, dkraw, dvalue), attended, gate(ids, *others), dp_size, added
         )
 
-    attn_sent = attention_sums(other_blocks, *down_out.send())
+    attn_sent = attention_sums(other_blocks, normed_part, moe_sum)
     attn_got = core_swap(attn_sent)
+    up_late = up_out.add(*attn_sent)
+    up_out.send()
+    down_done = owner_wgrad(
+        spread.all(), [gate(acts[0], *up_late)] + [act_pieces[k] for k in range(1, dp_size)], width
+    )
 
     def placed(part):
         return lax.dynamic_update_slice_in_dim(jnp.zeros((features,), f32), part, part_at * local_width, 0)
 
-    attn_sums = attention_sums(own_blocks, *attn_sent, added=attn_got)
+    attn_sums = attention_sums(own_blocks, down_done, added=attn_got)
     attn_out = Halving(attn_sums)
     normed_grad = gate(normed_grad, *attn_out.send())
     smalls = [attn_gain_part[0] / attn_gain, placed(q_gain_part[0]), placed(k_gain_part[0]), sum(ffn_gain_parts)]
@@ -787,7 +873,6 @@
     smalls = exchange_sum(smalls, ("dp", "tensor"))
     gate_done = gate_out.done()
     up_done = up_out.done()
-    down_done = down_out.done()
     attn_out.add(normed_grad)
     query_done, key_done, value_done, out_done = attn_out.done()
     layer_out = (jnp.concatenate(middles) + moe_sum.astype(f32)).astype(bf16)

time: 848 us -> 990 us (1.17)
  waiting for transfers between devices: 279 us -> 434 us
    ppermute x32 -> x39, waiting for transfers between devices: 61.8 us -> 200 us  [pair_swap(): return lax.ppermute(values, 'dp', [(i, i ^ step) for i in range(size)])]
    ppermute x3, waiting for transfers between devices: 6.99 us -> 50.7 us  [hop(): lax.ppermute(down, 'tensor', [(i, i - 1) for i in range(1, self.parts - s...]
    pallas_call x3 -> x4, Pallas kernels: 119 us -> 159 us  [the longest x2 109 us: experts_chunk(): pl.pallas_call(functools.partial(expert_kernel, block, peers, per), grid_...]
    pallas_call x6 -> x4, Pallas kernels: 103 us -> 68.4 us  [wgrad(): pl.pallas_call(functools.partial(wgrad_kernel, len(lefts), len(added), pe...]
    all_gather x4, waiting for transfers between devices: 117 us -> 90.7 us  [gather_rows(): return lax.all_gather(values, 'tensor', axis=0, tiled=True)]
    reduce_scatter x6, waiting for transfers between devices: 56.6 us -> 35.5 us  [scatter_rows(): return lax.psum_scatter(values, 'tensor', scatter_dimension=0, tiled=True)]
    ppermute x3, waiting for transfers between devices: 0.01 us -> 20.3 us  [hop(): lax.ppermute(up, 'tensor', [(i, i + 1) for i in range(step - 1, self.part...]
    pallas_call x2 -> x1, Pallas kernels: 30.1 us -> 22.7 us  [up_back(): pl.pallas_call(up_back_kernel, grid=(experts // step,), in_specs=[pl.Bloc...]
  transfers between devices with their start and end apart: 57 -> 64, of which waited for: 20 -> 31; matrix products, arithmetic and copies ran while one was open for 15% -> 12% of each run, Pallas kernels for 42% -> 36%
where the time goes in v6:
time: 990 us; the launch traced here: 982 us
  waiting for transfers between devices  434 us (44%)
  Pallas kernels  350 us (35%)
  other arithmetic  66.5 us (7%)
  local copies, waits for them, and re-layouts  52.6 us (5%)
  starting transfers between devices  43.6 us (4%)
  matrix products  19.6 us (2%)
  between operations  15.1 us (2%)
    ppermute x39, waiting for transfers between devices, pair_swap(): return lax.ppermute(values, 'dp', [(i, i ^ step) for i in range(size)])  200 us
    pallas_call x2, Pallas kernels, experts_chunk(): pl.pallas_call(functools.partial(expert_kernel, block, peers, per), grid_...  109 us
    all_gather x4, waiting for transfers between devices, gather_rows(): return lax.all_gather(values, 'tensor', axis=0, tiled=True)  90.7 us
    pallas_call x4, Pallas kernels, wgrad(): pl.pallas_call(functools.partial(wgrad_kernel, len(lefts), len(added), pe...  68.4 us
    ppermute x3, waiting for transfers between devices, hop(): lax.ppermute(down, 'tensor', [(i, i - 1) for i in range(1, self.parts - s...  50.7 us
    ppermute x9, waiting for transfers between devices, exchange_sum(): lax.ppermute(values, axis, [(i, i ^ step) for i in range(size)])  36.6 us
    reduce_scatter x6, waiting for transfers between devices, scatter_rows(): return lax.psum_scatter(values, 'tensor', scatter_dimension=0, tiled=True)  35.5 us
    pallas_call x1, Pallas kernels, owner_wgrad(): pl.pallas_call(functools.partial(owner_wgrad_kernel, len(lefts)), grid=(f...  25.3 us
  transfers between devices with their start and end apart: 64, of which 31 were waited for; matrix products, arithmetic and copies ran while one was open for 12% of the time, Pallas kernels for 36%

profile of v6, /device:TPU:0, one launch (start us, length us, event | category | flops | bytes accessed | tf_op | source)
XLA Modules:
  0.0 981.5 jit_solution(7342356628891146113)
XLA Ops:
  10.1 2.5 multiply_convert_fusion
  12.7 83.6 %all-gather.5.cloned.1.call-done.rows_in = bf16[1024,2048]{1,0:T(8,128)(2,1)} async-done(((bf16[256,2048]{1,0:T(8,128)(2,1)}), bf16[1024,2048]{1,0:T(8,128)(2,1)}) %all-gather.5.cloned.1.call-update) | async-done | bytes 4194320 | tf_op jit(solution)/shard_map/all_gather | solution.py:561
  96.2 2.4 collective-permute-start.2
  99.9 20.3 %collective-permute-done.2 = bf16[256,2048]{1,0:T(8,128)(2,1)} collective-permute-done((bf16[256,2048]{1,0:T(8,128)(2,1)S(1)}, bf16[256,2048]{1,0:T(8,128)(2,1)}, u32[]{:S(2)}, u32[]{:S(2)}) %collective-permute-start.2) | collective-permute-done | bytes 1048608 | tf_op jit(solution)/shard_map/ppermute | solution.py:614
  121.9 3.6 collective-permute-done.3
  126.8 16.3 %project.1 = (f32[1024,512]{1,0:T(8,128)}, f32[1024,512]{1,0:T(8,128)}, bf16[1024,512]{1,0:T(8,128)(2,1)}, f32[2,1024]{1,0:T(2,128)}) custom-call(bf16[1024,2048]{1,0:T(8,128)(2,1)} %all-gather.5.cloned.1.call-done.rows_in, bf16[2048,512]{1,0:T(8,128)(2,1)} %w_query.3, bf16[2048,512]{1,0:T(8,128)(2,1)} %w_key.3, bf16[2048,512]{1,0:T(8,128)(2,1)} %w_value.3), custom_call_target="tpu_custom_call" | custom-call | flops 2899102976 | bytes 1310720 | tf_op jit(solution)/shard_map/project/pallas_call | solution.py:101
  143.1 2.7 collective-permute-start
  145.8 6.1 collective-permute-done
  152.6 4.5 collective-permute-done.1
  160.2 15.7 %attend.1 = (bf16[1024,512]{1,0:T(8,128)(2,1)}, bf16[1024,512]{1,0:T(8,128)(2,1)}, bf16[1024,512]{1,0:T(8,128)(2,1)}, f32[1024,512]{1,0:T(8,128)}) custom-call(f32[1024,512]{1,0:T(8,128)} %get-tuple-element.105.qraw, f32[1024,512]{1,0:T(8,128)} %get-tuple-element.106.kraw, bf16[1024,512]{1,0:T(8,128)(2,1)} %get-tuple-element.107.value, ...), custom_call_target="tpu_custom_call" | custom-call | flops 724775744 | bytes 1179648 | tf_op jit(solution)/shard_map/attend/pallas_call | solution.py:241
  175.9 2.4 fusion.35
  178.4 2.7 convolution_convert_fusion.1
  182.1 2.6 convolution_convert_fusion
  187.7 35.5 %reduce-scatter.7.cloned.1.call-done = bf16[128,2048]{1,0:T(8,128)(2,1)} async-done(((bf16[512,2048]{1,0:T(8,128)(2,1)}), bf16[128,2048]{1,0:T(8,128)(2,1)}) %reduce-scatter.7.cloned.1.call-update) | async-done | bytes 524304 | tf_op jit(solution)/shard_map/reduce_scatter | solution.py:565
  233.8 7.5 convert_reduce_fusion
  241.3 47.2 %collective-permute-done.7 = bf16[256,2048]{1,0:T(8,128)(2,1)} collective-permute-done((bf16[256,2048]{1,0:T(8,128)(2,1)}, bf16[256,2048]{1,0:T(8,128)(2,1)}, u32[]{:S(2)}, u32[]{:S(2)}) %collective-permute-start.7) | collective-permute-done | bytes 1048608 | tf_op jit(solution)/shard_map/ppermute | solution.py:615
  288.4 6.3 join.1
  294.7 22.7 %up_back.1.back = bf16[1024,4096]{1,0:T(8,128)(2,1)} custom-call(bf16[1024,2048]{1,0:T(8,128)(2,1)} %bitcast.145, bf16[16,2048,256]{2,1,0:T(8,128)(2,1)} %down_w.3), custom_call_target="tpu_custom_call" | custom-call | flops 7730940928 | bytes 2621440 | tf_op jit(solution)/shard_map/up_back/pallas_call | solution.py:333
  325.6 7.1 all-gather.9.cloned.1.call-done.rows_in.refs_0_
  332.7 54.5 %experts.2 = (bf16[1024,512]{1,0:T(8,128)(2,1)}, bf16[1024,512]{1,0:T(8,128)(2,1)}, bf16[1024,512]{1,0:T(8,128)(2,1)}, bf16[1024,512]{1,0:T(8,128)(2,1)}, bf16[1...) custom-call(s32[16]{0:T(128)} %add.272.order, ...), custom_call_target="tpu_custom_call" | custom-call | flops 15461881856 | bytes 6291456 | tf_op jit(solution)/shard_map/experts/pallas_call | solution.py:407
  387.3 27.1 %collective-permute-done.8.refs_2_ = bf16[1024,2048]{1,0:T(8,128)(2,1)} collective-permute-done((bf16[1024,2048]{1,0:T(8,128)(2,1)}, bf16[1024,2048]{1,0:T(8,128)(2,1)}, u32[]{:S(2)}, u32[]{:S(2)}) %collective-permute-start.8) | collective-permute-done | bytes 4194336 | tf_op jit(solution)/shard_map/ppermute | solution.py:631
  415.6 54.6 %experts.3 = (bf16[1024,512]{1,0:T(8,128)(2,1)}, bf16[1024,512]{1,0:T(8,128)(2,1)}, bf16[1024,512]{1,0:T(8,128)(2,1)}, bf16[1024,512]{1,0:T(8,128)(2,1)}, bf16[1...) custom-call(s32[16]{0:T(128)} %add.272.order, ...), custom_call_target="tpu_custom_call", output_to_operand_aliasing={{0}: (7, {}), {1}: (8, {}), {2}: (9, {}), {3}: (10, {}), {4... | custom-call | flops 15461881856 | bytes 6291456 | tf_op jit(solution)/shard_map/experts/pallas_call | solution.py:407
  470.8 3.2 slice.217
  475.4 3.1 slice.218
  485.7 37.1 %collective-permute-done.10 = bf16[512,2048]{1,0:T(8,128)(2,1)} collective-permute-done((bf16[512,2048]{1,0:T(8,128)(2,1)}, bf16[512,2048]{1,0:T(8,128)(2,1)}, u32[]{:S(2)}, u32[]{:S(2)}) %collective-permute-start.10) | collective-permute-done | bytes 2097184 | tf_op jit(solution)/shard_map/ppermute | solution.py:631
  522.8 4.7 collective-permute-done.11
  533.4 16.5 %wgrad.4 = (bf16[2,2048,256]{2,1,0:T(8,128)(2,1)}, bf16[2,2048,256]{2,1,0:T(8,128)(2,1)}, bf16[2,2048,256]{2,1,0:T(8,128)(2,1)}, bf16[2,2048,256]{2,1,0:T(8,128)(2,1)}) custom-call(s32[8]{0:T(128)} %add.285.order, bf16[512,2048]{1,0:T(8,128)(2,1)} %all-gather.9.cloned.1.call-done.rows_in.refs_0_, ...), custom_call_target="tpu_custom_call" | custom-call | flops 3865470464 | bytes 2621440 | tf_op jit(solution)/shard_map/wgrad/pallas_call | solution.py:478
  549.9 16.4 %wgrad.5 = (bf16[2,2048,256]{2,1,0:T(8,128)(2,1)}, bf16[2,2048,256]{2,1,0:T(8,128)(2,1)}, bf16[2,2048,256]{2,1,0:T(8,128)(2,1)}, bf16[2,2048,256]{2,1,0:T(8,128)(2,1)}) custom-call(s32[8]{0:T(128)} %add.285.order, bf16[512,2048]{1,0:T(8,128)(2,1)} %all-gather.9.cloned.1.call-done.rows_in.refs_0_, ...), custom_call_target="tpu_custom_call" | custom-call | flops 3865470464 | bytes 2621440 | tf_op jit(solution)/shard_map/wgrad/pallas_call | solution.py:478
  574.5 23.3 %collective-permute-done.15.refs_11_ = bf16[1024,512]{1,0:T(8,128)(2,1)} collective-permute-done((bf16[1024,512]{1,0:T(8,128)(2,1)}, bf16[1024,512]{1,0:T(8,128)(2,1)}, u32[]{:S(2)}, u32[]{:S(2)}) %collective-permute-start.15) | collective-permute-done | bytes 1048608 | tf_op jit(solution)/shard_map/ppermute | solution.py:631
  600.5 24.6 %collective-permute-done.17.refs_14_ = bf16[1024,512]{1,0:T(8,128)(2,1)} collective-permute-done((bf16[1024,512]{1,0:T(8,128)(2,1)}, bf16[1024,512]{1,0:T(8,128)(2,1)}, u32[]{:S(2)}, u32[]{:S(2)}) %collective-permute-start.17) | collective-permute-done | bytes 1048608 | tf_op jit(solution)/shard_map/ppermute | solution.py:631
  626.2 17.7 %wgrad.6 = (bf16[8,1024,256]{2,1,0:T(8,128)(2,1)}, bf16[8,1024,256]{2,1,0:T(8,128)(2,1)}) custom-call(s32[8]{0:T(128)} %add.279.order, bf16[512,2048]{1,0:T(8,128)(2,1)} %all-gather.9.cloned.1.call-done.rows_in.refs_0_, bf16[512,2048]{1,0:T(8,128)(2,1)} %all-gather.7.cloned.1.call-done.rows_in.refs_1_, bf16[1024,4096]{1,0:T(8,128)(2,1)} %get-tuple-element.137.refs_2_, ...), custom_call_target="tpu_custom_call" | custom-call | flops 3865470464 | bytes 2621440 | tf_op jit(solution)/shard_map/wgrad/pallas_call | solution.py:478
  644.0 3.2 slice_bitcast_fusion.3
  647.2 2.3 fusion.34
  651.7 24.7 %down.1 = bf16[1024,2048]{1,0:T(8,128)(2,1)} custom-call(s32[16]{0:T(128)} %add.272.order, bf16[16,2048,256]{2,1,0:T(8,128)(2,1)} %down_w.3, bf16[1024,512]{1,0:T(8,128)(2,1)} %get-tuple-element.185.refs_0_.refs_8_, bf16[1024,512]{1,0:T(8,128)(2,1)} %get-tuple-element.142.refs_1_, bf16[1024,512]{1,0:T(8,128)(2,1)} %get-tuple-element.143.refs_2_, ...), custom_call_target="tpu_custom_call" | custom-call | flops 7730940928 | bytes 2621440 | tf_op jit(solution)/shard_map/down/pallas_call | solution.py:513
  678.2 3.0 collective-permute-done.23.refs_3_
  684.3 2.9 collective-permute-done.25.refs_5_
  687.2 3.0 collective-permute-done.26.refs_6_
  690.2 17.7 %wgrad.7 = (bf16[8,1024,256]{2,1,0:T(8,128)(2,1)}, bf16[8,1024,256]{2,1,0:T(8,128)(2,1)}) custom-call(s32[8]{0:T(128)} %add.279.order, bf16[512,2048]{1,0:T(8,128)(2,1)} %all-gather.9.cloned.1.call-done.rows_in.refs_0_, bf16[512,2048]{1,0:T(8,128)(2,1)} %all-gather.7.cloned.1.call-done.rows_in.refs_1_, bf16[1024,4096]{1,0:T(8,128)(2,1)} %get-tuple-element.134.refs_2_, ...), custom_call_target="tpu_custom_call" | custom-call | flops 3865470464 | bytes 2621440 | tf_op jit(solution)/shard_map/wgrad/pallas_call | solution.py:478
  707.9 3.2 slice_bitcast_fusion.2
  711.2 2.3 fusion.33
  713.5 5.6 convolution_convert_fusion.2.out_grad
  719.1 24.1 %attend_back.1 = (f32[1024,512]{1,0:T(8,128)}, f32[1024,512]{1,0:T(8,128)}, bf16[1024,512]{1,0:T(8,128)(2,1)}, f32[1024,1]{1,0:T(8,128)}, f32[1024,1]{1,0:T(8,128)}, /*index=5*/f32[1,512]{1,0:T(1,128)}, f32[1,512]{1,0:T(1,128)}) custom-call(bf16[1024,512]{1,0:T(8,128)(2,1)} %get-tuple-element.160.query, bf16[1024,512]{1,0:T(8,128)(2,1)} %get-tuple-element.161.key, ...), custom_call_target="tpu_custom_call" | custom-call | flops 1811939328 | bytes 2097152 | tf_op jit(solution)/shard_map/attend_back/pallas_call | solution.py:307
  745.8 4.1 fusion.2
  750.6 3.4 fusion.3
  756.7 13.9 %project_back.1 = (bf16[1024,2048]{1,0:T(8,128)(2,1)}, bf16[1024,512]{1,0:T(8,128)(2,1)}, bf16[1024,512]{1,0:T(8,128)(2,1)}, f32[1,2048]{1,0:T(1,128)}) custom-call(bf16[1024,2048]{1,0:T(8,128)(2,1)} %all-gather.5.cloned.1.call-done.rows_in, f32[1024,512]{1,0:T(8,128)} %get-tuple-element.167.dqn, f32[1024,512]{1,0:T(8,128)} %get-tuple-element.168.dkn, ...), custom_call_target="tpu_custom_call" | custom-call | flops 2899102976 | bytes 1310720 | tf_op jit(solution)/shard_map/project_back/pallas_call | solution.py:141
  771.2 3.3 constant_dynamic-update-slice_fusion.1
  776.9 3.2 constant_dynamic-update-slice_fusion.refs_6_
  780.0 19.7 %collective-permute-done.50 = bf16[1,2,1024,256]{3,2,1,0:T(8,128)(2,1)S(1)} collective-permute-done((bf16[1,2,1024,256]{3,2,1,0:T(8,128)(2,1)S(1)}, bf16[1,2,1024,256]{3,2,1,0:T(8,128)(2,1)S(1)}, u32[]{:S(2)}, u32[]{:S(2)}) %collective-permute-start.50) | collective-permute-done | bytes 1048608 | tf_op jit(solution)/shard_map/ppermute | solution.py:631
  806.3 3.3 add_bitcast_fusion.1
  811.1 11.5 %attention_wgrad.2 = (bf16[1,4,256,512]{3,2,1,0:T(8,128)(2,1)}, bf16[1,4,256,512]{3,2,1,0:T(8,128)(2,1)}, bf16[1,4,256,512]{3,2,1,0:T(8,128)(2,1)}, bf16[1,4,256,512]{3,2,1,0:T(8,128)(2,1)}) custom-call(s32[4]{0:T(128)} %get-tuple-element.176.order, bf16[1024,2048]{1,0:T(8,128)(2,1)} %all-gather.5.cloned.1.call-done.rows_in, ...), custom_call_target="tpu_custom_call" | custom-call | tf_op jit(solution)/shard_map/attention_wgrad/pallas_call | solution.py:192
  823.2 23.7 %collective-permute-done.35 = bf16[2,2,1024,256]{3,2,1,0:T(8,128)(2,1)} collective-permute-done((bf16[2,2,1024,256]{3,2,1,0:T(8,128)(2,1)}, bf16[2,2,1024,256]{3,2,1,0:T(8,128)(2,1)}, u32[]{:S(2)}, u32[]{:S(2)}) %collective-permute-start.35) | collective-permute-done | bytes 2097184 | tf_op jit(solution)/shard_map/ppermute | solution.py:631
  846.9 2.6 collective-permute-done.36
  849.5 2.3 pad_maximum_fusion
  851.8 2.3 fusion.1
  858.0 25.3 %owner_wgrad.1 = f32[2,2048,256]{2,1,0:T(8,128)} custom-call(bf16[1024,2048]{1,0:T(8,128)(2,1)} %bitcast.149, bf16[1024,2048]{1,0:T(8,128)(2,1)} %collective-permute-done.31.refs_1_, bf16[1024,2048]{1,0:T(8,128)(2,1)} %collective-permute-done.8.refs_2_, bf16[1024,2048]{1,0:T(8,128)(2,1)} %collective-permute-done.32.refs_3_, ...), custom_call_target="tpu_custom_call" | custom-call | tf_op jit(solution)/shard_map/owner_wgrad/pallas_call | solution.py:543
  885.8 11.9 %attention_wgrad.3 = (bf16[4,4,128,512]{3,2,1,0:T(8,128)(2,1)}, bf16[4,4,128,512]{3,2,1,0:T(8,128)(2,1)}) custom-call(s32[4]{0:T(128)} %get-tuple-element.186.order, bf16[1024,2048]{1,0:T(8,128)(2,1)} %all-gather.5.cloned.1.call-done.rows_in, bf16[1024,2048]{1,0:T(8,128)(2,1)} %all-gather.11.cloned.1.call-done.middle, ...), custom_call_target="tpu_custom_call" | custom-call | tf_op jit(solution)/shard_map/attention_wgrad/pallas_call | solution.py:192
  897.7 2.4 slice.188
  905.9 4.7 collective-permute-done.53
  912.1 2.3 pad_maximum_fusion.1
  914.4 17.9 %collective-permute-done.41 = bf16[2,4,128,512]{3,2,1,0:T(8,128)(2,1)} collective-permute-done((bf16[2,4,128,512]{3,2,1,0:T(8,128)(2,1)}, bf16[2,4,128,512]{3,2,1,0:T(8,128)(2,1)}, u32[]{:S(2)}, u32[]{:S(2)}) %collective-permute-start.41) | collective-permute-done | bytes 1048608 | tf_op jit(solution)/shard_map/ppermute | solution.py:631
  940.0 11.7 %collective-permute-done.46 = f32[20,2048]{1,0:T(8,128)S(1)} collective-permute-done((f32[20,2048]{1,0:T(8,128)S(1)}, f32[20,2048]{1,0:T(8,128)S(1)}, u32[]{:S(2)}, u32[]{:S(2)}) %collective-permute-start.46) | collective-permute-done | bytes 163872 | tf_op jit(solution)/shard_map/ppermute | solution.py:711
  955.1 2.3 collective-permute-done.47
  959.7 4.8 collective-permute-done.48
  966.6 6.7 collective-permute-done.49
  (292 shorter events, 116.8 us)
Async XLA Ops:
  7.2 89.0 %all-gather.5.cloned.1.call-start = ((), (), s32[]{:S(2)}) async-start(), calls=%async_computation.6 | async-start | bytes 5242880 | tf_op jit(solution)/shard_map/all_gather | solution.py:561
  12.6 210.6 %reduce-scatter.7.cloned.1.call-start = ((), (), s32[]{:S(2)}) async-start(), calls=%async_computation.7 | async-start | bytes 2621440 | tf_op jit(solution)/shard_map/reduce_scatter | solution.py:565
  96.2 24.0 %collective-permute-start.2 = (bf16[256,2048]{1,0:T(8,128)(2,1)S(1)}, bf16[256,2048]{1,0:T(8,128)(2,1)}, u32[]{:S(2)}, u32[]{:S(2)}) collective-permute-start(bf16[256,2048]{1,0:T(8,128)(2,1)S(1)} %copy-done.14), channel_id=1, source_target_pairs={{0,1},{1,2},{2,3},{4,5},{5,6},{6,7},{8,9},{9,10},{10,11},{12,13},{... | collective-permute-start | bytes 3145736 | tf_op jit(solution)/shard_map/ppermute | solution.py:614
  98.6 26.9 %collective-permute-start.3 = (bf16[256,2048]{1,0:T(8,128)(2,1)S(1)}, bf16[256,2048]{1,0:T(8,128)(2,1)}, u32[]{:S(2)}, u32[]{:S(2)}) collective-permute-start(bf16[256,2048]{1,0:T(8,128)(2,1)S(1)} %copy-done.14), channel_id=1, source_target_pairs={{1,0},{2,1},{3,2},{5,4},{6,5},{7,6},{9,8},{10,9},{11,10},{13,12},{... | collective-permute-start | bytes 3145736 | tf_op jit(solution)/shard_map/ppermute | solution.py:615
  120.2 55.7 %collective-permute-start.4 = (bf16[256,2048]{1,0:T(8,128)(2,1)}, bf16[256,2048]{1,0:T(8,128)(2,1)}, u32[]{:S(2)}, u32[]{:S(2)}) collective-permute-start(bf16[256,2048]{1,0:T(8,128)(2,1)} %collective-permute-done.2), channel_id=1, source_target_pairs={{1,2},{2,3},{5,6},{6,7},{9,10},{10,11},{13,14},{14,15},{17,18},{18... | collective-permute-start | bytes 3145736 | tf_op jit(solution)/shard_map/ppermute | solution.py:614
  125.5 50.4 %collective-permute-start.5 = (bf16[256,2048]{1,0:T(8,128)(2,1)}, bf16[256,2048]{1,0:T(8,128)(2,1)S(1)}, u32[]{:S(2)}, u32[]{:S(2)}) collective-permute-start(bf16[256,2048]{1,0:T(8,128)(2,1)} %collective-permute-done.3), channel_id=1, source_target_pairs={{1,0},{2,1},{5,4},{6,5},{9,8},{10,9},{13,12},{14,13},{17,16},{18,1... | collective-permute-start | bytes 3145736 | tf_op jit(solution)/shard_map/ppermute | solution.py:615
  143.1 8.8 collective-permute-start
  152.6 4.5 collective-permute-start.1
  181.1 136.3 %reduce-scatter.9.cloned.1.call-start = ((), (), s32[]{:S(2)}) async-start(), calls=%async_computation.8 | async-start | bytes 2621440 | tf_op jit(solution)/shard_map/reduce_scatter | solution.py:565
  184.7 148.0 %all-gather.9.cloned.1.call-start = ((), (), s32[]{:S(2)}) async-start(), calls=%async_computation.10 | async-start | bytes 2621440 | tf_op jit(solution)/shard_map/all_gather | solution.py:561
  226.0 189.5 %all-gather.7.cloned.1.call-start = ((), (), s32[]{:S(2)}) async-start(), calls=%async_computation.9 | async-start | bytes 2621440 | tf_op jit(solution)/shard_map/all_gather | solution.py:561
  226.1 15.2 %collective-permute-start.6 = (bf16[256,2048]{1,0:T(8,128)(2,1)}, bf16[256,2048]{1,0:T(8,128)(2,1)}, u32[]{:S(2)}, u32[]{:S(2)}) collective-permute-start(bf16[256,2048]{1,0:T(8,128)(2,1)} %collective-permute-done.4), channel_id=1, source_target_pairs={{2,3},{6,7},{10,11},{14,15},{18,19},{22,23},{26,27},{30,31}} | collective-permute-start | bytes 3145736 | tf_op jit(solution)/shard_map/ppermute | solution.py:614
  227.8 60.6 %collective-permute-start.7 = (bf16[256,2048]{1,0:T(8,128)(2,1)}, bf16[256,2048]{1,0:T(8,128)(2,1)}, u32[]{:S(2)}, u32[]{:S(2)}) collective-permute-start(bf16[256,2048]{1,0:T(8,128)(2,1)} %copy-done.27), channel_id=1, source_target_pairs={{1,0},{5,4},{9,8},{13,12},{17,16},{21,20},{25,24},{29,28}} | collective-permute-start | bytes 3145736 | tf_op jit(solution)/shard_map/ppermute | solution.py:615
  320.0 207.4 %reduce-scatter.13.cloned.1.call-start = ((), (), s32[]{:S(2)}) async-start(), calls=%async_computation.12 | async-start | bytes 2785280 | tf_op jit(solution)/shard_map/reduce_scatter | solution.py:565
  322.6 91.8 %collective-permute-start.8 = (bf16[1024,2048]{1,0:T(8,128)(2,1)}, bf16[1024,2048]{1,0:T(8,128)(2,1)}, u32[]{:S(2)}, u32[]{:S(2)}) collective-permute-start(bf16[1024,2048]{1,0:T(8,128)(2,1)} %bitcast.146), channel_id=1, source_target_pairs={{0,8},{4,12},{8,0},{12,4},{16,24},{20,28},{24,16},{28,20},{1,9},{5... | collective-permute-start | bytes 12582920 | tf_op jit(solution)/shard_map/ppermute | solution.py:631
  324.1 91.5 %collective-permute-start.9 = (bf16[1024,2048]{1,0:T(8,128)(2,1)}, bf16[1024,2048]{1,0:T(8,128)(2,1)}, u32[]{:S(2)}, u32[]{:S(2)}) collective-permute-start(bf16[1024,2048]{1,0:T(8,128)(2,1)} %bitcast.147), channel_id=1, source_target_pairs={{0,16},{4,20},{8,24},{12,28},{16,0},{20,4},{24,8},{28,12},{1,17},{... | collective-permute-start | bytes 12582920 | tf_op jit(solution)/shard_map/ppermute | solution.py:631
  387.2 179.1 %reduce-scatter.11.cloned.1.call-start = ((), (), s32[]{:S(2)}) async-start(), calls=%async_computation.11 | async-start | bytes 2785280 | tf_op jit(solution)/shard_map/reduce_scatter | solution.py:565
  470.2 243.2 %all-gather.11.cloned.1.call-start = ((), (), s32[]{:S(2)}) async-start(), calls=%async_computation.14 | async-start | bytes 5242880 | tf_op jit(solution)/shard_map/all_gather | solution.py:561
  473.9 48.9 %collective-permute-start.10 = (bf16[512,2048]{1,0:T(8,128)(2,1)}, bf16[512,2048]{1,0:T(8,128)(2,1)}, u32[]{:S(2)}, u32[]{:S(2)}) collective-permute-start(bf16[512,2048]{1,0:T(8,128)(2,1)} %slice.217), channel_id=1, source_target_pairs={{0,16},{4,20},{8,24},{12,28},{16,0},{20,4},{24,8},{28,12},{1,17},{... | collective-permute-start | bytes 6291464 | tf_op jit(solution)/shard_map/ppermute | solution.py:631
  478.6 48.9 %collective-permute-start.11 = (bf16[512,2048]{1,0:T(8,128)(2,1)}, bf16[512,2048]{1,0:T(8,128)(2,1)}, u32[]{:S(2)}, u32[]{:S(2)}) collective-permute-start(bf16[512,2048]{1,0:T(8,128)(2,1)} %slice.218), channel_id=1, source_target_pairs={{0,8},{4,12},{8,0},{12,4},{16,24},{20,28},{24,16},{28,20},{1,9},{5... | collective-permute-start | bytes 6291464 | tf_op jit(solution)/shard_map/ppermute | solution.py:631
  483.5 66.3 %collective-permute-start.12 = (bf16[1024,512]{1,0:T(8,128)(2,1)}, bf16[1024,512]{1,0:T(8,128)(2,1)}, u32[]{:S(2)}, u32[]{:S(2)}) collective-permute-start(bf16[1024,512]{1,0:T(8,128)(2,1)} %get-tuple-element.142.refs_1_), channel_id=1, source_target_pairs={{0,4},{4,0},{8,12},{12,8},{16,20},{20,16},{24,28},{28,24},{1,5},{5... | collective-permute-start | bytes 3145736 | tf_op jit(solution)/shard_map/ppermute | solution.py:631
  483.6 66.3 %collective-permute-start.13 = (bf16[1024,512]{1,0:T(8,128)(2,1)}, bf16[1024,512]{1,0:T(8,128)(2,1)}, u32[]{:S(2)}, u32[]{:S(2)}) collective-permute-start(bf16[1024,512]{1,0:T(8,128)(2,1)} %get-tuple-element.143.refs_2_), channel_id=1, source_target_pairs={{0,8},{4,12},{8,0},{12,4},{16,24},{20,28},{24,16},{28,20},{1,9},{5... | collective-permute-start | bytes 3145736 | tf_op jit(solution)/shard_map/ppermute | solution.py:631
  485.2 64.7 %collective-permute-start.14 = (bf16[1024,512]{1,0:T(8,128)(2,1)}, bf16[1024,512]{1,0:T(8,128)(2,1)}, u32[]{:S(2)}, u32[]{:S(2)}) collective-permute-start(bf16[1024,512]{1,0:T(8,128)(2,1)} %get-tuple-element.144.refs_4_), channel_id=1, source_target_pairs={{0,16},{4,20},{8,24},{12,28},{16,0},{20,4},{24,8},{28,12},{1,17},{... | collective-permute-start | bytes 3145736 | tf_op jit(solution)/shard_map/ppermute | solution.py:631
  572.6 238.5 %reduce-scatter.15.cloned.1.call-start = ((), (), s32[]{:S(2)}) async-start(), calls=%async_computation.13 | async-start | bytes 5242880 | tf_op jit(solution)/shard_map/reduce_scatter | solution.py:565
  572.9 24.9 %collective-permute-start.15 = (bf16[1024,512]{1,0:T(8,128)(2,1)}, bf16[1024,512]{1,0:T(8,128)(2,1)}, u32[]{:S(2)}, u32[]{:S(2)}) collective-permute-start(bf16[1024,512]{1,0:T(8,128)(2,1)} %get-tuple-element.151.refs_3_), channel_id=1, source_target_pairs={{0,12},{4,8},{8,4},{12,0},{16,28},{20,24},{24,20},{28,16},{1,13},{... | collective-permute-start | bytes 3145736 | tf_op jit(solution)/shard_map/ppermute | solution.py:631
  572.9 25.1 %collective-permute-start.16 = (bf16[1024,512]{1,0:T(8,128)(2,1)}, bf16[1024,512]{1,0:T(8,128)(2,1)}, u32[]{:S(2)}, u32[]{:S(2)}) collective-permute-start(bf16[1024,512]{1,0:T(8,128)(2,1)} %get-tuple-element.152.refs_5_), channel_id=1, source_target_pairs={{0,20},{4,16},{8,28},{12,24},{16,4},{20,0},{24,12},{28,8},{1,21},{... | collective-permute-start | bytes 3145736 | tf_op jit(solution)/shard_map/ppermute | solution.py:631
  574.0 52.3 %collective-permute-start.18 = (bf16[2,2048,256]{2,1,0:T(8,128)(2,1)}, bf16[2,2048,256]{2,1,0:T(8,128)(2,1)}, u32[]{:S(2)}, u32[]{:S(2)}) collective-permute-start(bf16[2,2048,256]{2,1,0:T(8,128)(2,1)} %get-tuple-element.138), channel_id=1, source_target_pairs={{0,4},{4,0},{8,12},{12,8},{16,20},{20,16},{24,28},{28,24},{1,5},{5... | collective-permute-start | bytes 6291464 | tf_op jit(solution)/shard_map/ppermute | solution.py:631
  574.0 52.3 %collective-permute-start.19 = (bf16[2,2048,256]{2,1,0:T(8,128)(2,1)}, bf16[2,2048,256]{2,1,0:T(8,128)(2,1)}, u32[]{:S(2)}, u32[]{:S(2)}) collective-permute-start(bf16[2,2048,256]{2,1,0:T(8,128)(2,1)} %get-tuple-element.139), channel_id=1, source_target_pairs={{0,4},{4,0},{8,12},{12,8},{16,20},{20,16},{24,28},{28,24},{1,5},{5... | collective-permute-start | bytes 6291464 | tf_op jit(solution)/shard_map/ppermute | solution.py:631
  574.5 51.8 %collective-permute-start.20 = (bf16[2,2048,256]{2,1,0:T(8,128)(2,1)}, bf16[2,2048,256]{2,1,0:T(8,128)(2,1)}, u32[]{:S(2)}, u32[]{:S(2)}) collective-permute-start(bf16[2,2048,256]{2,1,0:T(8,128)(2,1)} %get-tuple-element.140), channel_id=1, source_target_pairs={{0,4},{4,0},{8,12},{12,8},{16,20},{20,16},{24,28},{28,24},{1,5},{5... | collective-permute-start | bytes 6291464 | tf_op jit(solution)/shard_map/ppermute | solution.py:631
  597.8 28.4 %collective-permute-start.21 = (bf16[2,2048,256]{2,1,0:T(8,128)(2,1)}, bf16[2,2048,256]{2,1,0:T(8,128)(2,1)}, u32[]{:S(2)}, u32[]{:S(2)}) collective-permute-start(bf16[2,2048,256]{2,1,0:T(8,128)(2,1)} %get-tuple-element.141), channel_id=1, source_target_pairs={{0,4},{4,0},{8,12},{12,8},{16,20},{20,16},{24,28},{28,24},{1,5},{5... | collective-permute-start | bytes 6291464 | tf_op jit(solution)/shard_map/ppermute | solution.py:631
  598.0 27.1 %collective-permute-start.17 = (bf16[1024,512]{1,0:T(8,128)(2,1)}, bf16[1024,512]{1,0:T(8,128)(2,1)}, u32[]{:S(2)}, u32[]{:S(2)}) collective-permute-start(bf16[1024,512]{1,0:T(8,128)(2,1)} %get-tuple-element.153.refs_6_), channel_id=1, source_target_pairs={{0,24},{4,28},{8,16},{12,20},{16,8},{20,12},{24,0},{28,4},{1,25},{... | collective-permute-start | bytes 3145736 | tf_op jit(solution)/shard_map/ppermute | solution.py:631
  625.2 26.5 %collective-permute-start.22 = (bf16[1024,512]{1,0:T(8,128)(2,1)}, bf16[1024,512]{1,0:T(8,128)(2,1)}, u32[]{:S(2)}, u32[]{:S(2)}) collective-permute-start(bf16[1024,512]{1,0:T(8,128)(2,1)} %get-tuple-element.157.refs_7_), channel_id=1, source_target_pairs={{0,28},{4,24},{8,20},{12,16},{16,12},{20,8},{24,4},{28,0},{1,29},{... | collective-permute-start | bytes 3145736 | tf_op jit(solution)/shard_map/ppermute | solution.py:631
  676.4 238.0 %reduce-scatter.17.cloned.1.call-start = ((), (), s32[]{:S(2)}) async-start(), calls=%async_computation.15 | async-start | bytes 5242880 | tf_op jit(solution)/shard_map/reduce_scatter | solution.py:565
  676.6 4.6 collective-permute-start.23
  676.8 7.4 collective-permute-start.24
  677.2 10.0 %collective-permute-start.25 = (bf16[2,2048,256]{2,1,0:T(8,128)(2,1)}, bf16[2,2048,256]{2,1,0:T(8,128)(2,1)}, u32[]{:S(2)}, u32[]{:S(2)}) collective-permute-start(bf16[2,2048,256]{2,1,0:T(8,128)(2,1)} %get-tuple-element.148), channel_id=1, source_target_pairs={{0,4},{4,0},{8,12},{12,8},{16,20},{20,16},{24,28},{28,24},{1,5},{5... | collective-permute-start | bytes 6291464 | tf_op jit(solution)/shard_map/ppermute | solution.py:631
  677.3 12.9 %collective-permute-start.26 = (bf16[2,2048,256]{2,1,0:T(8,128)(2,1)}, bf16[2,2048,256]{2,1,0:T(8,128)(2,1)}, u32[]{:S(2)}, u32[]{:S(2)}) collective-permute-start(bf16[2,2048,256]{2,1,0:T(8,128)(2,1)} %get-tuple-element.149), channel_id=1, source_target_pairs={{0,4},{4,0},{8,12},{12,8},{16,20},{20,16},{24,28},{28,24},{1,5},{5... | collective-permute-start | bytes 6291464 | tf_op jit(solution)/shard_map/ppermute | solution.py:631
  677.7 65.5 %collective-permute-start.29 = (bf16[2,2,1024,256]{3,2,1,0:T(8,128)(2,1)}, bf16[2,2,1024,256]{3,2,1,0:T(8,128)(2,1)}, u32[]{:S(2)}, u32[]{:S(2)}) collective-permute-start(bf16[2,2,1024,256]{3,2,1,0:T(8,128)(2,1)} %bitcast.165), channel_id=1, source_target_pairs={{0,16},{4,20},{8,24},{12,28},{16,0},{20,4},{24,8},{28,12},{1,17},{... | collective-permute-start | bytes 6291464 | tf_op jit(solution)/shard_map/ppermute | solution.py:631
  681.2 62.0 %collective-permute-start.30 = (bf16[2,2,1024,256]{3,2,1,0:T(8,128)(2,1)}, bf16[2,2,1024,256]{3,2,1,0:T(8,128)(2,1)}, u32[]{:S(2)}, u32[]{:S(2)}) collective-permute-start(bf16[2,2,1024,256]{3,2,1,0:T(8,128)(2,1)} %slice_bitcast_fusion.3), channel_id=1, source_target_pairs={{0,8},{4,12},{8,0},{12,4},{16,24},{20,28},{24,16},{28,20},{1,9},{5... | collective-permute-start | bytes 6291464 | tf_op jit(solution)/shard_map/ppermute | solution.py:631
  684.2 95.8 %collective-permute-start.31 = (bf16[1024,2048]{1,0:T(8,128)(2,1)}, bf16[1024,2048]{1,0:T(8,128)(2,1)}, u32[]{:S(2)}, u32[]{:S(2)}) collective-permute-start(bf16[1024,2048]{1,0:T(8,128)(2,1)} %bitcast.148), channel_id=1, source_target_pairs={{0,4},{4,0},{8,12},{12,8},{16,20},{20,16},{24,28},{28,24},{1,5},{5... | collective-permute-start | bytes 12582920 | tf_op jit(solution)/shard_map/ppermute | solution.py:631
  745.8 4.2 collective-permute-start.27
  750.0 4.6 collective-permute-start.28
  770.7 51.9 %collective-permute-start.32 = (bf16[1024,2048]{1,0:T(8,128)(2,1)}, bf16[1024,2048]{1,0:T(8,128)(2,1)}, u32[]{:S(2)}, u32[]{:S(2)}) collective-permute-start(bf16[1024,2048]{1,0:T(8,128)(2,1)} %collective-permute-done.8.refs_2_), channel_id=1, source_target_pairs={{0,4},{4,0},{8,12},{12,8},{16,20},{20,16},{24,28},{28,24},{1,5},{5... | collective-permute-start | bytes 12582920 | tf_op jit(solution)/shard_map/ppermute | solution.py:631
  770.7 51.9 %collective-permute-start.33 = (bf16[1024,2048]{1,0:T(8,128)(2,1)}, bf16[1024,2048]{1,0:T(8,128)(2,1)}, u32[]{:S(2)}, u32[]{:S(2)}) collective-permute-start(bf16[1024,2048]{1,0:T(8,128)(2,1)} %collective-permute-done.9.refs_4_), channel_id=1, source_target_pairs={{0,4},{4,0},{8,12},{12,8},{16,20},{20,16},{24,28},{28,24},{1,5},{5... | collective-permute-start | bytes 12582920 | tf_op jit(solution)/shard_map/ppermute | solution.py:631
  774.6 25.2 %collective-permute-start.50 = (bf16[1,2,1024,256]{3,2,1,0:T(8,128)(2,1)S(1)}, bf16[1,2,1024,256]{3,2,1,0:T(8,128)(2,1)S(1)}, u32[]{:S(2)}, u32[]{:S(2)}) collective-permute-start(bf16[1,2,1024,256]{3,2,1,0:T(8,128)(2,1)S(1)} %slice.241), channel_id=1, source_target_pairs={{0,8},{4,12},{8,0},{12,4},{16,24},{20,28},{24,16},{28,20},{1,9},{5... | collective-permute-start | bytes 3145736 | tf_op jit(solution)/shard_map/ppermute | solution.py:631
  776.2 25.1 %collective-permute-start.51 = (bf16[1,2,1024,256]{3,2,1,0:T(8,128)(2,1)S(1)}, bf16[1,2,1024,256]{3,2,1,0:T(8,128)(2,1)S(1)}, u32[]{:S(2)}, u32[]{:S(2)}) collective-permute-start(bf16[1,2,1024,256]{3,2,1,0:T(8,128)(2,1)S(1)} %slice_bitcast_fusion.6), channel_id=1, source_target_pairs={{0,16},{4,20},{8,24},{12,28},{16,0},{20,4},{24,8},{28,12},{1,17},{... | collective-permute-start | bytes 3145736 | tf_op jit(solution)/shard_map/ppermute | solution.py:631
  780.0 77.2 %collective-permute-start.34 = (bf16[1024,2048]{1,0:T(8,128)(2,1)}, bf16[1024,2048]{1,0:T(8,128)(2,1)}, u32[]{:S(2)}, u32[]{:S(2)}) collective-permute-start(bf16[1024,2048]{1,0:T(8,128)(2,1)} %constant_dynamic-update-slice_fusion.refs_6_), channel_id=1, source_target_pairs={{0,4},{4,0},{8,12},{12,8},{16,20},{20,16},{24,28},{28,24},{1,5},{5... | collective-permute-start | bytes 12582920 | tf_op jit(solution)/shard_map/ppermute | solution.py:631
  799.7 47.1 %collective-permute-start.35 = (bf16[2,2,1024,256]{3,2,1,0:T(8,128)(2,1)}, bf16[2,2,1024,256]{3,2,1,0:T(8,128)(2,1)}, u32[]{:S(2)}, u32[]{:S(2)}) collective-permute-start(bf16[2,2,1024,256]{3,2,1,0:T(8,128)(2,1)} %bitcast.24), channel_id=1, source_target_pairs={{0,16},{4,20},{8,24},{12,28},{16,0},{20,4},{24,8},{28,12},{1,17},{... | collective-permute-start | bytes 6291464 | tf_op jit(solution)/shard_map/ppermute | solution.py:631
  802.3 47.1 %collective-permute-start.36 = (bf16[2,2,1024,256]{3,2,1,0:T(8,128)(2,1)}, bf16[2,2,1024,256]{3,2,1,0:T(8,128)(2,1)}, u32[]{:S(2)}, u32[]{:S(2)}) collective-permute-start(bf16[2,2,1024,256]{3,2,1,0:T(8,128)(2,1)} %slice_bitcast_fusion.2), channel_id=1, source_target_pairs={{0,8},{4,12},{8,0},{12,4},{16,24},{20,28},{24,16},{28,20},{1,9},{5... | collective-permute-start | bytes 6291464 | tf_op jit(solution)/shard_map/ppermute | solution.py:631
  822.6 61.7 %collective-permute-start.37 = (bf16[1,4,256,512]{3,2,1,0:T(8,128)(2,1)}, bf16[1,4,256,512]{3,2,1,0:T(8,128)(2,1)}, u32[]{:S(2)}, u32[]{:S(2)}) collective-permute-start(bf16[1,4,256,512]{3,2,1,0:T(8,128)(2,1)} %get-tuple-element.179), channel_id=1, source_target_pairs={{0,4},{4,0},{8,12},{12,8},{16,20},{20,16},{24,28},{28,24},{1,5},{5... | collective-permute-start | bytes 3145736 | tf_op jit(solution)/shard_map/ppermute | solution.py:631
  822.7 63.1 %collective-permute-start.38 = (bf16[1,4,256,512]{3,2,1,0:T(8,128)(2,1)}, bf16[1,4,256,512]{3,2,1,0:T(8,128)(2,1)}, u32[]{:S(2)}, u32[]{:S(2)}) collective-permute-start(bf16[1,4,256,512]{3,2,1,0:T(8,128)(2,1)} %get-tuple-element.180), channel_id=1, source_target_pairs={{0,4},{4,0},{8,12},{12,8},{16,20},{20,16},{24,28},{28,24},{1,5},{5... | collective-permute-start | bytes 3145736 | tf_op jit(solution)/shard_map/ppermute | solution.py:631
  846.9 38.9 %collective-permute-start.39 = (bf16[1,4,256,512]{3,2,1,0:T(8,128)(2,1)}, bf16[1,4,256,512]{3,2,1,0:T(8,128)(2,1)}, u32[]{:S(2)}, u32[]{:S(2)}) collective-permute-start(bf16[1,4,256,512]{3,2,1,0:T(8,128)(2,1)} %get-tuple-element.181), channel_id=1, source_target_pairs={{0,4},{4,0},{8,12},{12,8},{16,20},{20,16},{24,28},{28,24},{1,5},{5... | collective-permute-start | bytes 3145736 | tf_op jit(solution)/shard_map/ppermute | solution.py:631
  849.4 36.3 %collective-permute-start.40 = (bf16[1,4,256,512]{3,2,1,0:T(8,128)(2,1)}, bf16[1,4,256,512]{3,2,1,0:T(8,128)(2,1)}, u32[]{:S(2)}, u32[]{:S(2)}) collective-permute-start(bf16[1,4,256,512]{3,2,1,0:T(8,128)(2,1)} %get-tuple-element.182), channel_id=1, source_target_pairs={{0,4},{4,0},{8,12},{12,8},{16,20},{20,16},{24,28},{28,24},{1,5},{5... | collective-permute-start | bytes 3145736 | tf_op jit(solution)/shard_map/ppermute | solution.py:631
  857.3 47.2 %collective-permute-start.52 = (bf16[1,2,1024,256]{3,2,1,0:T(8,128)(2,1)}, bf16[1,2,1024,256]{3,2,1,0:T(8,128)(2,1)}, u32[]{:S(2)}, u32[]{:S(2)}) collective-permute-start(bf16[1,2,1024,256]{3,2,1,0:T(8,128)(2,1)} %slice.245), channel_id=1, source_target_pairs={{0,8},{4,12},{8,0},{12,4},{16,24},{20,28},{24,16},{28,20},{1,9},{5... | collective-permute-start | bytes 3145736 | tf_op jit(solution)/shard_map/ppermute | solution.py:631
  884.3 26.3 %collective-permute-start.53 = (bf16[1,2,1024,256]{3,2,1,0:T(8,128)(2,1)}, bf16[1,2,1024,256]{3,2,1,0:T(8,128)(2,1)}, u32[]{:S(2)}, u32[]{:S(2)}) collective-permute-start(bf16[1,2,1024,256]{3,2,1,0:T(8,128)(2,1)} %slice_bitcast_fusion.4), channel_id=1, source_target_pairs={{0,16},{4,20},{8,24},{12,28},{16,0},{20,4},{24,8},{28,12},{1,17},{... | collective-permute-start | bytes 3145736 | tf_op jit(solution)/shard_map/ppermute | solution.py:631
  900.1 32.2 %collective-permute-start.41 = (bf16[2,4,128,512]{3,2,1,0:T(8,128)(2,1)}, bf16[2,4,128,512]{3,2,1,0:T(8,128)(2,1)}, u32[]{:S(2)}, u32[]{:S(2)}) collective-permute-start(bf16[2,4,128,512]{3,2,1,0:T(8,128)(2,1)} %slice.188), channel_id=1, source_target_pairs={{0,16},{4,20},{8,24},{12,28},{16,0},{20,4},{24,8},{28,12},{1,17},{... | collective-permute-start | bytes 3145736 | tf_op jit(solution)/shard_map/ppermute | solution.py:631
  901.8 30.5 %collective-permute-start.42 = (bf16[2,4,128,512]{3,2,1,0:T(8,128)(2,1)}, bf16[2,4,128,512]{3,2,1,0:T(8,128)(2,1)}, u32[]{:S(2)}, u32[]{:S(2)}) collective-permute-start(bf16[2,4,128,512]{3,2,1,0:T(8,128)(2,1)} %slice_bitcast_fusion.9), channel_id=1, source_target_pairs={{0,8},{4,12},{8,0},{12,4},{16,24},{20,28},{24,16},{28,20},{1,9},{5... | collective-permute-start | bytes 3145736 | tf_op jit(solution)/shard_map/ppermute | solution.py:631
  914.4 24.0 %collective-permute-start.45 = (f32[20,2048]{1,0:T(8,128)S(1)}, f32[20,2048]{1,0:T(8,128)S(1)}, u32[]{:S(2)}, u32[]{:S(2)}) collective-permute-start(f32[20,2048]{1,0:T(8,128)S(1)} %concatenate.29), channel_id=1, source_target_pairs={{0,4},{4,0},{8,12},{12,8},{16,20},{20,16},{24,28},{28,24},{1,5},{5... | collective-permute-start | bytes 491528 | tf_op jit(solution)/shard_map/ppermute | solution.py:711
  934.2 25.2 %collective-permute-start.43 = (bf16[1,4,128,512]{3,2,1,0:T(8,128)(2,1)S(1)}, bf16[1,4,128,512]{3,2,1,0:T(8,128)(2,1)S(1)}, u32[]{:S(2)}, u32[]{:S(2)}) collective-permute-start(bf16[1,4,128,512]{3,2,1,0:T(8,128)(2,1)S(1)} %slice.231), channel_id=1, source_target_pairs={{0,8},{4,12},{8,0},{12,4},{16,24},{20,28},{24,16},{28,20},{1,9},{5... | collective-permute-start | bytes 1572872 | tf_op jit(solution)/shard_map/ppermute | solution.py:631
  937.3 22.3 %collective-permute-start.44 = (bf16[1,4,128,512]{3,2,1,0:T(8,128)(2,1)S(1)}, bf16[1,4,128,512]{3,2,1,0:T(8,128)(2,1)S(1)}, u32[]{:S(2)}, u32[]{:S(2)}) collective-permute-start(bf16[1,4,128,512]{3,2,1,0:T(8,128)(2,1)S(1)} %slice_bitcast_fusion.10), channel_id=1, source_target_pairs={{0,16},{4,20},{8,24},{12,28},{16,0},{20,4},{24,8},{28,12},{1,17},{... | collective-permute-start | bytes 1572872 | tf_op jit(solution)/shard_map/ppermute | solution.py:631
  938.4 13.2 %collective-permute-start.46 = (f32[20,2048]{1,0:T(8,128)S(1)}, f32[20,2048]{1,0:T(8,128)S(1)}, u32[]{:S(2)}, u32[]{:S(2)}) collective-permute-start(f32[20,2048]{1,0:T(8,128)S(1)} %add.307), channel_id=1, source_target_pairs={{0,8},{4,12},{8,0},{12,4},{16,24},{20,28},{24,16},{28,20},{1,9},{5... | collective-permute-start | bytes 491528 | tf_op jit(solution)/shard_map/ppermute | solution.py:711
  951.7 5.7 collective-permute-start.47
  957.4 7.0 collective-permute-start.48
  964.5 8.7 collective-permute-start.49
  (45 other events, 967.6 us)
Sparse Core Ops, SparseCore 0:
  12.7 83.4 all-gather.4
  181.2 41.9 reduce-scatter.6
  226.2 58.9 reduce-scatter.8
  286.6 46.0 all-gather.8
  334.7 44.6 all-gather.6
  387.4 44.7 reduce-scatter.12
  470.4 43.2 reduce-scatter.10
  572.7 77.2 all-gather.10
  676.5 74.0 reduce-scatter.14
  770.8 76.1 reduce-scatter.16

commit v7 on v4

--- a/solution.py
+++ b/solution.py
@@ -150,7 +150,7 @@
     )(rows_in, dqn, dkn, dvalue, qraw, kraw, q_scale, k_scale, q_dot, k_dot, q_gain[None], k_gain[None], w_query, w_key, w_value)
 
 
-def attention_wgrad_kernel(added, order, rows_in, middle, *refs):
+def attention_wgrad_kernel(added, order, tables, rows_in, middle, *refs):
     sides, (attended,), refs = refs[:3], refs[3:4], refs[4:]
     got, outs = (refs[:added], refs[added:])
     at = pl.program_id(0)
@@ -164,15 +164,21 @@
                     out[0, weight] = total.astype(bf16)
 
         return
+    scratch, outs = outs[-1], outs[:-1]
     half = outs[0].shape[2]
     for place, piece in enumerate(got):
 
         @pl.when(at == place)
         def _(piece=piece):
             for weight, total in enumerate(totals):
-                total = total + piece[0, weight].astype(f32)
-                for side, out in enumerate(outs):
-                    out[0, weight] = total[side * half : (side + 1) * half, :].astype(bf16)
+                scratch[weight] = (total + piece[0, weight].astype(f32)).astype(bf16)
+
+    for side, out in enumerate(outs):
+        start = side * 2 // len(outs) * half
+
+        @pl.when(tables[1, side, at] == 1)
+        def _(out=out, start=start):
+            out[0] = scratch[:, start : start + half, :]
 
 
 def attention_wgrad(rows_in, middle, sides, attended, order, blocks, added=()):
@@ -180,28 +186,34 @@
     width = sides[0].shape[1]
     block = features // blocks
     count = order.shape[0]
-    left = lambda values: pl.BlockSpec((values.shape[0], block), lambda i, ids: (0, ids[i]))
-    right = lambda values: pl.BlockSpec(values.shape, lambda i, ids: (0, 0))
-    group_specs = [pl.BlockSpec((1, 4, block, width), lambda i, ids: (0, 0, 0, 0))] * count
+    tables, sizes = split_tables(count, 1)
+    left = lambda values: pl.BlockSpec((values.shape[0], block), lambda i, ids, to: (0, ids[i]))
+    right = lambda values: pl.BlockSpec(values.shape, lambda i, ids, to: (0, 0))
+
+    def half_spec(side):
+        return pl.BlockSpec((1, 4, block // 2, width), lambda i, ids, to: (to[0, side, i], 0, 0, 0))
+
+    group_specs = [pl.BlockSpec((1, 4, block, width), lambda i, ids, to: (0, 0, 0, 0))] * count
     if added:
-        out_specs = [pl.BlockSpec((1, 4, block // 2, width), lambda i, ids: (i, 0, 0, 0))] * 2
-        out_shape = [jax.ShapeDtypeStruct((count, 4, block // 2, width), bf16)] * 2
+        out_specs = [half_spec(side) for side in range(len(sizes))]
+        out_shape = [jax.ShapeDtypeStruct((size, 4, block // 2, width), bf16) for size in sizes]
     else:
         out_specs = group_specs
         out_shape = [jax.ShapeDtypeStruct((1, 4, block, width), bf16)] * count
     return pl.pallas_call(
         functools.partial(attention_wgrad_kernel, len(added)),
         grid_spec=pltpu.PrefetchScalarGridSpec(
-            num_scalar_prefetch=1,
+            num_scalar_prefetch=2,
             grid=(count,),
             in_specs=[left(rows_in), left(middle)] + [right(v) for v in sides] + [right(attended)] + (group_specs if added else []),
             out_specs=out_specs,
+            scratch_shapes=[pltpu.VMEM((4, block, width), bf16)] if added else [],
         ),
         out_shape=out_shape,
         compiler_params=params(),
-        cost_estimate=cost(8 * rows_in.shape[0] * features * width, 4 * features * width),
+        cost_estimate=cost(0, 0),
         name="attention_wgrad",
-    )(order, rows_in, middle, *sides, attended, *added)
+    )(order, tables, rows_in, middle, *sides, attended, *added)
 
 
 def attend_kernel(
@@ -315,9 +327,75 @@
         + [sds((length, 1), f32), sds((length, 1), f32), sds((1, width), f32), sds((1, width), f32)],
         scratch_shapes=[pltpu.VMEM((length, span), f32), pltpu.VMEM((length, HEAD), f32), pltpu.VMEM((length, HEAD), f32)],
         compiler_params=params(),
-        cost_estimate=cost(10 * length * span * width, 32 * length * width, length * span * width // HEAD),
+        cost_estimate=cost(20 * length * span * width, 0),
         name="attend_back",
     )(query, key, value, out_grad, lse, qraw, kraw, q_scale, k_scale, q_gain[None], k_gain[None], cosine, sine, seg[:, None], seg[None], keep[None])
+
+
+def middle_kernel(tokens, summed, gain, middle_out, scale_out, normed_out):
+    middle = tokens[...].astype(f32) + summed[...].astype(f32)
+    scale = lax.rsqrt(jnp.mean(middle * middle, axis=1, keepdims=True) + EPSILON)
+    middle_out[...] = middle
+    scale_out[...] = scale
+    normed_out[...] = (middle * scale * gain[...]).astype(bf16)
+
+
+def middle_rows(chunk, tokens, summed, gain):
+    rows, features = summed.shape
+    sds = jax.ShapeDtypeStruct
+    whole = lambda *shape: pl.BlockSpec(shape, lambda i: (0, 0))
+    return pl.pallas_call(
+        middle_kernel,
+        grid=(1,),
+        in_specs=[pl.BlockSpec((rows, features), lambda i: (chunk, 0)), whole(rows, features), whole(1, features)],
+        out_specs=[whole(rows, features), whole(rows, 1), whole(rows, features)],
+        out_shape=[sds((rows, features), f32), sds((rows, 1), f32), sds((rows, features), bf16)],
+        compiler_params=params(),
+        cost_estimate=cost(0, 0),
+        name="middle",
+    )(tokens, summed, gain[None])
+
+
+def middle_back_kernel(
+    experts, grads, middle, scale, normed, routed, router, cotangent, gain, *refs
+):
+    grad_out, low_out, gain_out, logit_out = refs[-4:]
+    features = middle.shape[1]
+    lane = lax.broadcasted_iota(jnp.int32, routed.shape, 1)
+    logits = jnp.where(lane < experts, nn(normed[...], router[...]), MASKED)
+    powers = jnp.exp(logits - jnp.max(logits, axis=1, keepdims=True))
+    probs = powers / jnp.sum(powers, axis=1, keepdims=True)
+    share_grad = grads[:, features:].astype(f32) * routed[...]
+    logit_grad = (probs * (share_grad - jnp.sum(share_grad * probs, axis=1, keepdims=True))).astype(bf16)
+    logit_out[...] = logit_grad
+    ffn_grad = grads[:, :features].astype(f32) + nt(logit_grad, router[...])
+    along = middle[...] * scale[...]
+    gain_out[...] = jnp.sum(ffn_grad * along, axis=0, keepdims=True)
+    weighted = ffn_grad * gain[...]
+    inner = jnp.mean(weighted * along, axis=1, keepdims=True)
+    total = cotangent[...].astype(f32) + scale[...] * (weighted - along * inner)
+    grad_out[...] = total
+    low_out[...] = total.astype(bf16)
+
+
+def middle_back(chunk, grads, middle, scale, normed, routed, router, cotangent, gain, experts, filled=()):
+    rows, features = middle.shape
+    sds = jax.ShapeDtypeStruct
+    whole = lambda *shape: pl.BlockSpec(shape, lambda i: (0, 0))
+    part = lambda columns: pl.BlockSpec((rows, columns), lambda i: (chunk, 0))
+    return pl.pallas_call(
+        functools.partial(middle_back_kernel, experts),
+        grid=(1,),
+        in_specs=[whole(rows, features + LANES), whole(rows, features), whole(rows, 1), whole(rows, features), part(LANES)]
+        + [whole(features, LANES), part(features), whole(1, features)]
+        + [pl.BlockSpec(memory_space=pl.ANY)] * len(filled),
+        out_specs=[part(features), part(features), whole(1, features), whole(rows, LANES)],
+        out_shape=[sds(cotangent.shape, f32), sds(cotangent.shape, bf16), sds((1, features), f32), sds((rows, LANES), bf16)],
+        input_output_aliases={8 + at: at for at in range(len(filled))},
+        compiler_params=params(),
+        cost_estimate=cost(0, 0),
+        name="middle_back",
+    )(grads, middle, scale, normed, routed, router, cotangent, gain[None], *filled)
 
 
 def up_back_kernel(grad, down_w, out):
@@ -387,7 +465,7 @@
         grad_out[:, features:] = dcomb[...].astype(bf16)
 
 
-def experts_block(rows_in, back, routed, router, gate_w, up_w):
+def experts_block(chunk, rows_in, back, routed, router, gate_w, up_w):
     rows, features = rows_in.shape
     experts, _, width = gate_w.shape
     block = min(512, rows)
@@ -398,7 +476,7 @@
     return pl.pallas_call(
         functools.partial(expert_kernel, block),
         grid=(experts,),
-        in_specs=[whole(rows, features), column, whole(rows, LANES), whole(features, LANES), weight, weight],
+        in_specs=[whole(rows, features), pl.BlockSpec((rows, width), lambda e: (chunk, e)), whole(rows, LANES), whole(features, LANES), weight, weight],
         out_specs=[column, column, column, whole(rows, features + LANES)],
         out_shape=[wide, wide, wide, jax.ShapeDtypeStruct((rows, features + LANES), bf16)],
         scratch_shapes=[pltpu.VMEM((rows, LANES), f32), pltpu.VMEM((rows, LANES), f32), pltpu.VMEM((rows, features), f32)],
@@ -408,7 +486,30 @@
     )(rows_in, back, routed, router, gate_w, up_w)
 
 
-def wgrad_kernel(count, extra, per, block, order, *refs):
+def block_order(blocks):
+    return [3, 2, 0, 1] if blocks == 4 else list(range(blocks))
+
+
+def split_tables(blocks, per):
+    order = block_order(blocks)
+    if blocks == 4:
+        picks = [{0: 0, 1: 1}, {2: 0, 3: 1}, {0: 0, 2: 1}, {1: 0, 3: 1}]
+    else:
+        picks = [{block: block for block in order}] * 2
+    places, fills = [], []
+    for pick in picks:
+        filled = [pick[block] * per + at if block in pick else None for block in order for at in range(per)]
+        last = next(place for place in filled if place is not None)
+        row = []
+        for place in filled:
+            last = last if place is None else place
+            row.append(last)
+        places.append(row)
+        fills.append([int(place is not None) for place in filled])
+    return jnp.asarray(np.array([places, fills], np.int32)), [len(pick) for pick in picks]
+
+
+def wgrad_kernel(count, extra, per, block, order, tables, *refs):
     lefts, rights = refs[:count], refs[count : 2 * count]
     added = refs[2 * count : 2 * count + extra]
     outs = refs[2 * count + extra :]
@@ -431,46 +532,59 @@
 
         return
     half = features // 2
-    for place, got in enumerate(added):
+    got = outs[-1]
+    outs = outs[:-1]
+    for place, arrived in enumerate(added):
 
         @pl.when(at // per == place)
-        def _(got=got):
+        def _(arrived=arrived):
             for start in range(0, features, block):
-                total = piece(start, start + block) + got[0, start : start + block, :].astype(f32)
-                outs[start // half][0, start % half : start % half + block, :] = total.astype(bf16)
+                total = piece(start, start + block) + arrived[0, start : start + block, :].astype(f32)
+                got[start : start + block, :] = total.astype(bf16)
+
+    for side, out in enumerate(outs):
+        start = side * 2 // len(outs) * half
+
+        @pl.when(tables[1, side, at] == 1)
+        def _(out=out, start=start):
+            out[0] = got[start : start + half, :]
 
 
 def wgrad(lefts, rights, order, width, per, added=()):
-    features = lefts[0].shape[1]
+    features = lefts[0][0].shape[1]
     experts = order.shape[0]
     groups = experts // per
-    rows = sum(left.shape[0] for left in lefts)
+    tables, sizes = split_tables(groups, per)
 
     def group_spec(place):
-        return pl.BlockSpec((1, features, width), lambda i, ids: (jnp.clip(i - place * per, 0, per - 1), 0, 0))
+        return pl.BlockSpec((1, features, width), lambda i, ids, to: (jnp.clip(i - place * per, 0, per - 1), 0, 0))
+
+    def half_spec(side):
+        return pl.BlockSpec((1, features // 2, width), lambda i, ids, to: (to[0, side, i], 0, 0))
 
     groups_specs = [group_spec(place) for place in range(groups)]
     if added:
-        out_specs = [pl.BlockSpec((1, features // 2, width), lambda i, ids: (i, 0, 0))] * 2
-        out_shape = [jax.ShapeDtypeStruct((experts, features // 2, width), bf16)] * 2
+        out_specs = [half_spec(side) for side in range(len(sizes))]
+        out_shape = [jax.ShapeDtypeStruct((size * per, features // 2, width), bf16) for size in sizes]
     else:
         out_specs = groups_specs
         out_shape = [jax.ShapeDtypeStruct((per, features, width), bf16)] * groups
     return pl.pallas_call(
         functools.partial(wgrad_kernel, len(lefts), len(added), per, min(512, features // 2)),
         grid_spec=pltpu.PrefetchScalarGridSpec(
-            num_scalar_prefetch=1,
+            num_scalar_prefetch=2,
             grid=(experts,),
-            in_specs=[pl.BlockSpec(left.shape, lambda i, ids: (0, 0)) for left in lefts]
-            + [pl.BlockSpec((right.shape[0], width), lambda i, ids: (0, ids[i])) for right in rights]
+            in_specs=[pl.BlockSpec((right.shape[0], features), lambda i, ids, to, at=at: (at, 0)) for (_, at), right in zip(lefts, rights)]
+            + [pl.BlockSpec((right.shape[0], width), lambda i, ids, to: (0, ids[i])) for right in rights]
             + (groups_specs if added else []),
             out_specs=out_specs,
+            scratch_shapes=[pltpu.VMEM((features, width), bf16)] if added else [],
         ),
         out_shape=out_shape,
         compiler_params=params(),
-        cost_estimate=cost(2 * rows * features * experts * width, 2 * (rows + 2 * experts * width) * features),
+        cost_estimate=cost(2 * sum(right.shape[0] for right in rights) * features * experts * width, 0),
         name="wgrad",
-    )(order, *lefts, *rights, *added)
+    )(order, tables, *(left for left, _ in lefts), *rights, *added)
 
 
 def down_kernel(parts, down_w, *refs):
@@ -529,22 +643,23 @@
 
 
 def join(slots, own, ups, downs):
+    parts = len(ups) + 1
     rows, columns = own.shape
-    parts = len(ups) + 1
-    whole = pl.BlockSpec((rows, columns), lambda i, to: (0, 0))
+    split = (CHUNKS, rows // CHUNKS, columns)
+    whole = pl.BlockSpec(split, lambda i, to: (0, 0, 0))
     return pl.pallas_call(
         functools.partial(join_kernel, parts),
         grid_spec=pltpu.PrefetchScalarGridSpec(
             num_scalar_prefetch=1,
             grid=(parts,),
             in_specs=[whole] * (2 * parts - 1),
-            out_specs=pl.BlockSpec((rows, columns), lambda i, to: (to[i], 0)),
+            out_specs=pl.BlockSpec(split, lambda i, to: (0, to[i], 0)),
         ),
-        out_shape=jax.ShapeDtypeStruct((parts * rows, columns), own.dtype),
+        out_shape=jax.ShapeDtypeStruct((CHUNKS, parts * rows // CHUNKS, columns), own.dtype),
         compiler_params=params(),
         cost_estimate=cost(0, 0),
         name="join",
-    )(slots, own, *ups, *downs)
+    )(slots, *(piece.reshape(split) for piece in (own, *ups, *downs)))
 
 
 class Chain:
@@ -580,8 +695,12 @@
 
 class Halving:
     def __init__(self, values):
-        bits = list(range(values[0].shape[0].bit_length() - 1))
-        self.kept = list(values)
+        if len(values) == 2:
+            self.kept = list(values)
+            self.going = None
+        else:
+            self.kept, self.going = list(values[::2]), list(values[1::2])
+        bits = list(range(values[0].shape[0].bit_length() - (1 if self.going is None else 0)))
         self.left = [bits[::-1], bits]
         self.got = None
 
@@ -592,16 +711,19 @@
         sent = []
         for side, downward in ((0, True), (1, False)):
             bit = self.left[side].pop(0)
-            kept = self.kept[side]
-            half = kept.shape[0] // 2
-            if downward:
-                keep, go = kept[:half], kept[half:]
+            if self.going is not None:
+                go = self.going[side]
             else:
-                view = kept.reshape((half, 2) + kept.shape[1:])
-                keep, go = view[:, 0], view[:, 1]
+                kept = self.kept[side]
+                half = kept.shape[0] // 2
+                if downward:
+                    self.kept[side], go = kept[:half], kept[half:]
+                else:
+                    view = kept.reshape((half, 2) + kept.shape[1:])
+                    self.kept[side], go = view[:, 0], view[:, 1]
             sent.append(go)
             self.got.append(pair_swap(go, 2 << bit))
-            self.kept[side] = keep
+        self.going = None
         return tuple(sent)
 
     def add(self, *others):
@@ -662,7 +784,7 @@
 
     cosine, sine = rope_tables(length, HEAD)
 
-    relative = jnp.arange(dp_size // 2, dtype=jnp.int32) ^ (lax.axis_index("dp") // 2)
+    relative = jnp.asarray(block_order(dp_size // 2), jnp.int32) ^ (lax.axis_index("dp") // 2)
     own_blocks, other_blocks = 2 * relative + low_bit, 2 * relative + 1 - low_bit
     mine, theirs = (
         (blocks[:, None] * per + jnp.arange(per, dtype=jnp.int32)).reshape(-1) for blocks in (own_blocks, other_blocks)
@@ -687,45 +809,28 @@
     expert_ids = jnp.arange(LANES)
     routed = jnp.sum((idle_routes[:, :, None] == expert_ids[None, None, :]).astype(f32), axis=1)
     router_wide = jnp.pad(idle_router, ((0, 0), (0, LANES - experts)))
-    routed_own = lax.dynamic_slice_in_dim(routed, part_at * shard_rows, shard_rows, 0)[:, :experts]
-    grad_group = behind.joined()
-    grad_all = [chunk_of(grad_group, c) for c in chunks]
-    backs = [up_back(gate(rows, routed, router_wide), w_down) for rows in grad_all]
-
-    middles, scales, ffn_own = [], [], []
-
-    def middle_of(c, total):
-        middle = inputs[own[c]] + total.astype(f32)
-        scale = rms_scale(middle)
-        normed = (middle * scale * ffn_gain).astype(bf16)
-        middles.append(middle)
-        scales.append(scale)
-        ffn_own.append(normed)
-        return normed
-
-    ffn_all = [gather_rows(middle_of(0, summed[0]))]
-    ffn_all.append(gather_rows(middle_of(1, gate(summed[1], ffn_own[0], *backs))))
+    routed_own = lax.dynamic_slice_in_dim(routed, part_at * shard_rows, shard_rows, 0)
+    grad_rows = behind.joined().reshape(group_rows, features)
+    back = up_back(gate(grad_rows, routed, router_wide), w_down)
+    grad_parts = [(grad_rows, c) for c in chunks]
+
+    norms = [middle_rows(0, tokens, summed[0], ffn_gain)]
+    ffn_all = [gather_rows(norms[0][2])]
+    norms.append(middle_rows(1, tokens, gate(summed[1], norms[0][2], back), ffn_gain))
+    ffn_all.append(gather_rows(norms[1][2]))
+    ffn_parts = [(rows, 0) for rows in ffn_all]
     acts, dgates, dups, expert_grads = [], [], [], []
     for c in chunks:
-        here = gate(chunk_of(routed, c), *backs, *acts[-1:])
-        act, dgate, dup, grads = experts_block(ffn_all[c], backs[c], here, router_wide, w_gate, w_up)
+        here = gate(chunk_of(routed, c), back, *acts[-1:])
+        act, dgate, dup, grads = experts_block(c, ffn_all[c], back, here, router_wide, w_gate, w_up)
         acts.append(act)
         dgates.append(dgate)
         dups.append(dup)
         expert_grads.append(grads)
     expert_grads = [scatter_rows(grads) for grads in expert_grads]
 
-    ffn_gain_parts, router_parts, middle_grads = [], [], []
-
-    def middle_back(c, grads):
-        share_grad = grads[:, features : features + experts] * routed_own[own[c]]
-        probs = jax.nn.softmax(nn(ffn_own[c], router), axis=-1)
-        logit_grad = (probs * (share_grad - jnp.sum(share_grad * probs, axis=-1, keepdims=True))).astype(bf16)
-        ffn_grad = grads[:, :features] + nt(logit_grad, router)
-        router_parts.append(tn(ffn_own[c], logit_grad))
-        ffn_gain_parts.append(jnp.sum(ffn_grad * middles[c] * scales[c], axis=0))
-        middle_grads.append(cotangent[own[c]].astype(f32) + norm_back(ffn_grad, middles[c], scales[c], ffn_gain))
-        return middle_grads[c].astype(bf16)
+    def back_of(c, grads, filled=()):
+        return middle_back(c, grads, *norms[c], routed_own, router_wide, cotangent, ffn_gain, experts, filled)
 
     def expert_sums(lefts, rights, ids, *others, added=()):
         return wgrad(lefts, rights, gate(ids, *others), width, per, added)
@@ -734,24 +839,27 @@
         return [pair_swap(piece, 1) for piece in pieces]
 
     def halving(sums):
-        return Halving([half.reshape((dp_size // 2, per) + half.shape[1:]) for half in sums])
-
-    first = middle_back(0, gate(expert_grads[0], acts[1]).astype(f32))
-    gate_sent = expert_sums(ffn_all, dgates, theirs, first)
+        return Halving([part.reshape((part.shape[0] // per, per) + part.shape[1:]) for part in sums])
+
+    first = back_of(0, gate(expert_grads[0], acts[1]))
+    gate_sent = expert_sums(ffn_parts, dgates, theirs, first[1])
     gate_got = core_swap(gate_sent)
-    up_sent = expert_sums(ffn_all, dups, theirs, *gate_sent)
+    up_sent = expert_sums(ffn_parts, dups, theirs, *gate_sent)
     up_got = core_swap(up_sent)
-    second = middle_back(1, gate(expert_grads[1], *up_sent).astype(f32))
-    middle_all = gather_rows(jnp.concatenate([first, second]))
-    gate_sums = expert_sums(ffn_all, dgates, mine, second, added=gate_got)
+    second = back_of(1, gate(expert_grads[1], *up_sent), first[:2])
+    middle_grad, middle_low = second[:2]
+    middle_all = gather_rows(middle_low)
+    gate_sums = expert_sums(ffn_parts, dgates, mine, middle_low, added=gate_got)
     gate_out = halving(gate_sums)
-    up_sums = expert_sums(ffn_all, dups, mine, *gate_sums, *gate_out.send(), added=up_got)
+    gate_out.send()
+    up_sums = expert_sums(ffn_parts, dups, mine, *gate_sums, added=up_got)
     up_out = halving(up_sums)
-    moe = down([gate(acts[0], *up_sums, *up_out.send()), acts[1]], w_down, parts)
-    moe_sum = scatter_rows(moe)
-    gate_late = gate_out.add()
+    up_out.send()
+    moe = down([gate(acts[0], *up_sums), acts[1]], w_down, parts)
+    gate_late = gate_out.add(moe)
     gate_out.send()
-    down_sent = expert_sums(grad_all, acts, theirs, moe, *gate_late)
+    moe_sum = scatter_rows(gate(moe, *gate_late))
+    down_sent = expert_sums(grad_parts, acts, theirs, moe, *gate_late)
     down_got = core_swap(down_sent)
 
     attended_grad = nn(gate(middle_all, *down_sent), w_out).astype(bf16)
@@ -760,14 +868,14 @@
         seg_ids[0], keep_mask[0],
     )
     dots = exchange_sum(jnp.stack([qdot[:, 0], kdot[:, 0]]), ("tensor",)) / features
-    up_late = up_out.add()
+    up_late = up_out.add(dqn)
     up_out.send()
-    down_sums = expert_sums(grad_all, acts, mine, dqn, *up_late, added=down_got)
+    down_sums = expert_sums(grad_parts, acts, mine, *up_late, added=down_got)
     down_out = halving(down_sums)
     down_out.send()
     normed_part, dqraw, dkraw, attn_gain_part = project_back(
         normed_all, dqn, dkn, dvalue, qraw, kraw, q_scale, k_scale, dots[0][:, None], dots[1][:, None],
-        gate(q_gain, *down_sums), k_gain, w_query, w_key, w_value,
+        gate(q_gain, *down_sums, *gate_out.got), k_gain, w_query, w_key, w_value,
     )
     normed_grad = scatter_rows(normed_part)
     def attention_sums(ids, *others, added=()):
@@ -784,16 +892,19 @@
     attn_sums = attention_sums(own_blocks, *attn_sent, added=attn_got)
     attn_out = Halving(attn_sums)
     normed_grad = gate(normed_grad, *attn_out.send())
-    smalls = [attn_gain_part[0] / attn_gain, placed(q_gain_part[0]), placed(k_gain_part[0]), sum(ffn_gain_parts)]
-    smalls = gate(jnp.concatenate([jnp.stack(smalls), sum(router_parts).T]), normed_grad)
+    down_out.add(*attn_sums)
+    down_out.send()
+    smalls = [attn_gain_part[0] / attn_gain, placed(q_gain_part[0]), placed(k_gain_part[0]), (first[2] + second[2])[0]]
+    router_part = sum(tn(late[3], norms[c][2]) for c, late in enumerate((first, second)))[:experts]
+    smalls = gate(jnp.concatenate([jnp.stack(smalls), router_part]), normed_grad)
     smalls = exchange_sum(smalls, ("dp", "tensor"))
     gate_done = gate_out.done()
     up_done = up_out.done()
     down_done = down_out.done()
     attn_out.add(normed_grad)
     query_done, key_done, value_done, out_done = attn_out.done()
-    layer_out = (jnp.concatenate(middles) + moe_sum.astype(f32)).astype(bf16)
-    tokens_grad = jnp.concatenate(middle_grads) + norm_back(normed_grad.astype(f32), inputs, first_scale, attn_gain)
+    layer_out = (jnp.concatenate([norms[c][0] for c in chunks]) + moe_sum.astype(f32)).astype(bf16)
+    tokens_grad = middle_grad + norm_back(normed_grad.astype(f32), inputs, first_scale, attn_gain)
     return (
         layer_out, tokens_grad, query_done, key_done, value_done, out_done,
         smalls[0], smalls[1], smalls[2], smalls[3], smalls[4:].T, gate_done, up_done, down_done,

time: 882 us -> 857 us (0.972)
  local copies, waits for them, and re-layouts: 50.1 us -> 24.8 us
  waiting for transfers between devices: 320 us -> 341 us
  other arithmetic: 73.7 us -> 53.5 us
  Pallas kernels: 352 us -> 363 us
    ppermute x3, waiting for transfers between devices: 7.02 us -> 59.3 us  [hop(): lax.ppermute(down, 'tensor', [(i, i - 1) for i in range(1, self.parts - s...]
    all_gather x4, waiting for transfers between devices: 117 us -> 97 us  [gather_rows(): return lax.all_gather(values, 'tensor', axis=0, tiled=True)]
    pallas_call x0 -> x4, Pallas kernels: none -> 13.5 us  [the longest x2 8.42 us: middle_back(): pl.pallas_call(functools.partial(middle_back_kernel, experts), grid=(1,),...]
    squeeze x8 -> x4, local copies, waits for them, and re-layouts: 12.6 us -> 1.62 us  [send(): self.kept[side], go = (view[:, 0], view[:, 1])]
    slice x8 -> x4, local copies, waits for them, and re-layouts: 11.3 us -> 1.21 us  [send(): self.kept[side], go = (kept[:half], kept[half:])]
    reduce_scatter x6, waiting for transfers between devices: 56.4 us -> 46.6 us  [scatter_rows(): return lax.psum_scatter(values, 'tensor', scatter_dimension=0, tiled=True)]
    convert_element_type x8 -> x1, other arithmetic: 11.9 us -> 2.8 us  [local(): (jnp.concatenate([norms[c][0] for c in chunks]) + moe_sum.astype(f32)).as...]
    pallas_call x2 -> x1, Pallas kernels: 30.1 us -> 22.8 us  [up_back(): pl.pallas_call(up_back_kernel, grid=(experts // step,), in_specs=[pl.Bloc...]
  transfers between devices with their start and end apart: 57 -> 57, of which waited for: 25 -> 26; matrix products, arithmetic and copies ran while one was open for 14% -> 8% of each run, Pallas kernels for 40% -> 42%
where the time goes in v7:
time: 857 us; the launch traced here: 848 us
  Pallas kernels  363 us (42%)
  waiting for transfers between devices  341 us (40%)
  other arithmetic  53.5 us (6%)
  starting transfers between devices  39.4 us (5%)
  local copies, waits for them, and re-layouts  24.8 us (3%)
  between operations  15.2 us (2%)
  matrix products  11.4 us (1%)
    pallas_call x6, Pallas kernels, wgrad(): pl.pallas_call(functools.partial(wgrad_kernel, len(lefts), len(added), pe...  107 us
    ppermute x32, waiting for transfers between devices, pair_swap(): return lax.ppermute(values, 'dp', [(i, i ^ step) for i in range(size)])  98.9 us
    all_gather x4, waiting for transfers between devices, gather_rows(): return lax.all_gather(values, 'tensor', axis=0, tiled=True)  97 us
    pallas_call x2, Pallas kernels, experts_block(): pl.pallas_call(functools.partial(expert_kernel, block), grid=(experts,),...  95 us
    ppermute x3, waiting for transfers between devices, hop(): lax.ppermute(down, 'tensor', [(i, i - 1) for i in range(1, self.parts - s...  59.3 us
    reduce_scatter x6, waiting for transfers between devices, scatter_rows(): return lax.psum_scatter(values, 'tensor', scatter_dimension=0, tiled=True)  46.6 us
    ppermute x9, waiting for transfers between devices, exchange_sum(): lax.ppermute(values, axis, [(i, i ^ step) for i in range(size)])  39 us
    pallas_call x2, Pallas kernels, attention_wgrad(): pl.pallas_call(functools.partial(attention_wgrad_kernel, len(added)), gri...  24.4 us
  transfers between devices with their start and end apart: 57, of which 26 were waited for; matrix products, arithmetic and copies ran while one was open for 8% of the time, Pallas kernels for 42%

profile of v7, /device:TPU:0, one launch (start us, length us, event | category | flops | bytes accessed | tf_op | source)
XLA Modules:
  0.0 848.5 jit_solution(4716414307183490603)
XLA Ops:
  7.3 1.7 fusion.6
  10.1 2.5 fusion.8
  12.7 83.6 %all-gather.5.cloned.1.call-done.rows_in = bf16[1024,2048]{1,0:T(8,128)(2,1)} async-done(((bf16[256,2048]{1,0:T(8,128)(2,1)}), bf16[1024,2048]{1,0:T(8,128)(2,1)}) %all-gather.5.cloned.1.call-update) | async-done | bytes 4194320 | tf_op jit(solution)/shard_map/all_gather | solution.py:623
  96.2 2.3 collective-permute-start.2
  99.8 16.3 %project.1 = (f32[1024,512]{1,0:T(8,128)}, f32[1024,512]{1,0:T(8,128)}, bf16[1024,512]{1,0:T(8,128)(2,1)}, f32[2,1024]{1,0:T(2,128)}) custom-call(bf16[1024,2048]{1,0:T(8,128)(2,1)} %all-gather.5.cloned.1.call-done.rows_in, bf16[2048,512]{1,0:T(8,128)(2,1)} %w_query.3, bf16[2048,512]{1,0:T(8,128)(2,1)} %w_key.3, bf16[2048,512]{1,0:T(8,128)(2,1)} %w_value.3), custom_call_target="tpu_custom_call" | custom-call | flops 2899102976 | bytes 1310720 | tf_op jit(solution)/shard_map/project/pallas_call | solution.py:101
  116.1 2.6 collective-permute-start
  118.7 6.8 collective-permute-done
  126.9 3.8 collective-permute-done.1
  136.8 15.7 %attend.1 = (bf16[1024,512]{1,0:T(8,128)(2,1)}, bf16[1024,512]{1,0:T(8,128)(2,1)}, bf16[1024,512]{1,0:T(8,128)(2,1)}, f32[1024,512]{1,0:T(8,128)}) custom-call(f32[1024,512]{1,0:T(8,128)} %get-tuple-element.123.qraw, f32[1024,512]{1,0:T(8,128)} %get-tuple-element.124.kraw, bf16[1024,512]{1,0:T(8,128)(2,1)} %get-tuple-element.125.value, ...), custom_call_target="tpu_custom_call" | custom-call | flops 57347878912 | bytes 1179648 | tf_op jit(solution)/shard_map/attend/pallas_call | solution.py:253
  152.4 8.6 %collective-permute-done.5 = bf16[256,2048]{1,0:T(8,128)(2,1)} collective-permute-done((bf16[256,2048]{1,0:T(8,128)(2,1)}, bf16[256,2048]{1,0:T(8,128)(2,1)}, u32[]{:S(2)}, u32[]{:S(2)}) %collective-permute-start.5) | collective-permute-done | bytes 1048608 | tf_op jit(solution)/shard_map/ppermute | solution.py:677
  162.4 2.7 convolution_convert_fusion.1
  165.1 2.6 convolution_convert_fusion
  167.8 40.8 %reduce-scatter.7.cloned.1.call-done.summed = bf16[128,2048]{1,0:T(8,128)(2,1)} async-done(((bf16[512,2048]{1,0:T(8,128)(2,1)}), bf16[128,2048]{1,0:T(8,128)(2,1)}) %reduce-scatter.7.cloned.1.call-update) | async-done | bytes 524304 | tf_op jit(solution)/shard_map/reduce_scatter | solution.py:627
  208.6 2.5 middle.2
  216.3 5.7 convert_reduce_fusion
  222.9 50.6 %collective-permute-done.7 = bf16[256,2048]{1,0:T(8,128)(2,1)} collective-permute-done((bf16[256,2048]{1,0:T(8,128)(2,1)}, bf16[256,2048]{1,0:T(8,128)(2,1)}, u32[]{:S(2)}, u32[]{:S(2)}) %collective-permute-start.7) | collective-permute-done | bytes 1048608 | tf_op jit(solution)/shard_map/ppermute | solution.py:677
  273.5 6.3 join.1
  279.8 22.8 %up_back.1.back = bf16[1024,4096]{1,0:T(8,128)(2,1)} custom-call(bf16[1024,2048]{1,0:T(8,128)(2,1)} %bitcast.130, bf16[16,2048,256]{2,1,0:T(8,128)(2,1)} %down_w.3), custom_call_target="tpu_custom_call" | custom-call | flops 7730940928 | bytes 2621440 | tf_op jit(solution)/shard_map/up_back/pallas_call | solution.py:411
  302.6 2.5 middle.3
  305.2 13.4 %all-gather.7.cloned.1.call-done.rows_in.refs_0_ = bf16[512,2048]{1,0:T(8,128)(2,1)} async-done(((bf16[128,2048]{1,0:T(8,128)(2,1)}), bf16[512,2048]{1,0:T(8,128)(2,1)}) %all-gather.7.cloned.1.call-update) | async-done | bytes 2097168 | tf_op jit(solution)/shard_map/all_gather | solution.py:623
  318.7 47.4 %experts.2 = (bf16[512,4096]{1,0:T(8,128)(2,1)}, bf16[512,4096]{1,0:T(8,128)(2,1)}, bf16[512,4096]{1,0:T(8,128)(2,1)}, bf16[512,2176]{1,0:T(8,128)(2,1)}) custom-call(bf16[512,2048]{1,0:T(8,128)(2,1)} %all-gather.7.cloned.1.call-done.rows_in.refs_0_, bf16[1024,4096]{1,0:T(8,128)(2,1)} %up_back.1.back, f32[512,128]{1,0:T(8,128)} %bitcast.151, ...), custom_call_target="tpu_custom_call" | custom-call | flops 53210619904 | bytes 6291456 | tf_op jit(solution)/shard_map/experts/pallas_call | solution.py:476
  366.2 47.6 %experts.3 = (bf16[512,4096]{1,0:T(8,128)(2,1)}, bf16[512,4096]{1,0:T(8,128)(2,1)}, bf16[512,4096]{1,0:T(8,128)(2,1)}, bf16[512,2176]{1,0:T(8,128)(2,1)}) custom-call(bf16[512,2048]{1,0:T(8,128)(2,1)} %all-gather.9.cloned.1.call-done.rows_in.refs_1_, bf16[1024,4096]{1,0:T(8,128)(2,1)} %up_back.1.back, f32[512,128]{1,0:T(8,128)} %bitcast.150, ...), custom_call_target="tpu_custom_call" | custom-call | flops 53210619904 | bytes 6291456 | tf_op jit(solution)/shard_map/experts/pallas_call | solution.py:476
  416.3 4.2 middle_back.2
  420.5 17.0 %wgrad.6 = (bf16[2,2048,256]{2,1,0:T(8,128)(2,1)}, bf16[2,2048,256]{2,1,0:T(8,128)(2,1)}, bf16[2,2048,256]{2,1,0:T(8,128)(2,1)}, bf16[2,2048,256]{2,1,0:T(8,128)(2,1)}) custom-call(s32[8]{0:T(128)} %add.213.order, s32[2,4,8]{2,1,0:T(4,128)} %constant.82.clone.tables, bf16[512,2048]{1,0:T(8,128)(2,1)} %all-gather.7.cloned.1.call-done.rows_in.refs_0_, ...), custom_call_target="tpu_custom_call" | custom-call | flops 3865470464 | tf_op jit(solution)/shard_map/wgrad/pallas_call | solution.py:572
  437.6 16.7 %wgrad.7 = (bf16[2,2048,256]{2,1,0:T(8,128)(2,1)}, bf16[2,2048,256]{2,1,0:T(8,128)(2,1)}, bf16[2,2048,256]{2,1,0:T(8,128)(2,1)}, bf16[2,2048,256]{2,1,0:T(8,128)(2,1)}) custom-call(s32[8]{0:T(128)} %add.213.order, s32[2,4,8]{2,1,0:T(4,128)} %constant.82.clone.tables, bf16[512,2048]{1,0:T(8,128)(2,1)} %all-gather.7.cloned.1.call-done.rows_in.refs_0_, ...), custom_call_target="tpu_custom_call" | custom-call | flops 3865470464 | tf_op jit(solution)/shard_map/wgrad/pallas_call | solution.py:572
  454.2 5.8 reduce-scatter.11.cloned.1.call-done.grads
  460.0 4.2 middle_back.3
  465.6 3.4 collective-permute-done.10.refs_6_
  469.2 2.9 collective-permute-done.11.refs_7_
  472.2 2.9 collective-permute-done.8.refs_4_
  475.8 2.2 collective-permute-done.9.refs_5_
  478.0 18.7 %wgrad.8 = (bf16[4,1024,256]{2,1,0:T(8,128)(2,1)}, bf16[4,1024,256]{2,1,0:T(8,128)(2,1)}, bf16[4,1024,256]{2,1,0:T(8,128)(2,1)}, bf16[4,1024,256]{2,1,0:T(8,128)(2,1)}) custom-call(s32[8]{0:T(128)} %add.208.order, s32[2,4,8]{2,1,0:T(4,128)} %constant.82.clone.tables, bf16[512,2048]{1,0:T(8,128)(2,1)} %all-gather.7.cloned.1.call-done.rows_in.refs_0_, ...), custom_call_target="tpu_custom_call" | custom-call | flops 3865470464 | tf_op jit(solution)/shard_map/wgrad/pallas_call | solution.py:572
  499.7 18.7 %wgrad.9 = (bf16[4,1024,256]{2,1,0:T(8,128)(2,1)}, bf16[4,1024,256]{2,1,0:T(8,128)(2,1)}, bf16[4,1024,256]{2,1,0:T(8,128)(2,1)}, bf16[4,1024,256]{2,1,0:T(8,128)(2,1)}) custom-call(s32[8]{0:T(128)} %add.208.order, s32[2,4,8]{2,1,0:T(4,128)} %constant.82.clone.tables, bf16[512,2048]{1,0:T(8,128)(2,1)} %all-gather.7.cloned.1.call-done.rows_in.refs_0_, ...), custom_call_target="tpu_custom_call" | custom-call | flops 3865470464 | tf_op jit(solution)/shard_map/wgrad/pallas_call | solution.py:572
  518.4 24.4 %down.1 = bf16[1024,2048]{1,0:T(8,128)(2,1)} custom-call(bf16[16,2048,256]{2,1,0:T(8,128)(2,1)} %down_w.3, bf16[512,4096]{1,0:T(8,128)(2,1)} %get-tuple-element.179.refs_0_.refs_2_, bf16[512,4096]{1,0:T(8,128)(2,1)} %get-tuple-element.147.refs_1_.refs_3_), custom_call_target="tpu_custom_call" | custom-call | flops 7730940928 | bytes 2621440 | tf_op jit(solution)/shard_map/down/pallas_call | solution.py:605
  542.8 1.9 collective-permute-done.16
  545.9 4.2 fusion.4
  550.1 3.4 fusion.5
  555.7 17.3 %wgrad.10 = (bf16[2,2048,256]{2,1,0:T(8,128)(2,1)}, bf16[2,2048,256]{2,1,0:T(8,128)(2,1)}, bf16[2,2048,256]{2,1,0:T(8,128)(2,1)}, bf16[2,2048,256]{2,1,0:T(8,128)(2,1)}) custom-call(s32[8]{0:T(128)} %add.213.order, s32[2,4,8]{2,1,0:T(4,128)} %constant.82.clone.tables, bf16[1024,2048]{1,0:T(8,128)(2,1)} %bitcast.131, bf16[1024,2048]{1,0:T(8,128)(2,1)} %bitcast.132, ...), custom_call_target="tpu_custom_call" | custom-call | flops 3865470464 | tf_op jit(solution)/shard_map/wgrad/pallas_call | solution.py:572
  574.5 25.9 %collective-permute-done.20 = bf16[2,2,1024,256]{3,2,1,0:T(8,128)(2,1)} collective-permute-done((bf16[2,2,1024,256]{3,2,1,0:T(8,128)(2,1)}, bf16[2,2,1024,256]{3,2,1,0:T(8,128)(2,1)}, u32[]{:S(2)}, u32[]{:S(2)}) %collective-permute-start.20) | collective-permute-done | bytes 2097184 | tf_op jit(solution)/shard_map/ppermute | solution.py:693
  600.5 5.5 convolution_convert_fusion.2.out_grad
  606.0 24.0 %attend_back.1 = (f32[1024,512]{1,0:T(8,128)}, f32[1024,512]{1,0:T(8,128)}, bf16[1024,512]{1,0:T(8,128)(2,1)}, f32[1024,1]{1,0:T(8,128)}, f32[1024,1]{1,0:T(8,128)}, /*index=5*/f32[1,512]{1,0:T(1,128)}, f32[1,512]{1,0:T(1,128)}) custom-call(bf16[1024,512]{1,0:T(8,128)(2,1)} %get-tuple-element.184.query, bf16[1024,512]{1,0:T(8,128)(2,1)} %get-tuple-element.185.key, ...), custom_call_target="tpu_custom_call" | custom-call | flops 3623878656 | tf_op jit(solution)/shard_map/attend_back/pallas_call | solution.py:319
  637.8 3.5 fusion.2
  641.3 3.5 fusion.3
  644.8 1.9 collective-permute-start.19
  646.7 18.6 %wgrad.11 = (bf16[4,1024,256]{2,1,0:T(8,128)(2,1)}, bf16[4,1024,256]{2,1,0:T(8,128)(2,1)}, bf16[4,1024,256]{2,1,0:T(8,128)(2,1)}, bf16[4,1024,256]{2,1,0:T(8,128)(2,1)}) custom-call(s32[8]{0:T(128)} %add.208.order, s32[2,4,8]{2,1,0:T(4,128)} %constant.82.clone.tables, bf16[1024,2048]{1,0:T(8,128)(2,1)} %bitcast.133, bf16[1024,2048]{1,0:T(8,128)(2,1)} %bitcast.134, ...), custom_call_target="tpu_custom_call" | custom-call | flops 3865470464 | tf_op jit(solution)/shard_map/wgrad/pallas_call | solution.py:572
  669.4 13.8 %project_back.1 = (bf16[1024,2048]{1,0:T(8,128)(2,1)}, bf16[1024,512]{1,0:T(8,128)(2,1)}, bf16[1024,512]{1,0:T(8,128)(2,1)}, f32[1,2048]{1,0:T(1,128)}) custom-call(bf16[1024,2048]{1,0:T(8,128)(2,1)} %all-gather.5.cloned.1.call-done.rows_in, f32[1024,512]{1,0:T(8,128)} %get-tuple-element.193.dqn, f32[1024,512]{1,0:T(8,128)} %get-tuple-element.194.dkn, ...), custom_call_target="tpu_custom_call" | custom-call | flops 2899102976 | bytes 1310720 | tf_op jit(solution)/shard_map/project_back/pallas_call | solution.py:141
  685.8 12.0 %attention_wgrad.2 = (bf16[1,4,256,512]{3,2,1,0:T(8,128)(2,1)}, bf16[1,4,256,512]{3,2,1,0:T(8,128)(2,1)}, bf16[1,4,256,512]{3,2,1,0:T(8,128)(2,1)}, bf16[1,4,256,512]{3,2,1,0:T(8,128)(2,1)}) custom-call(s32[4]{0:T(128)} %get-tuple-element.207.order, s32[2,4,4]{2,1,0:T(4,128)} %constant.83.clone.tables, ...), custom_call_target="tpu_custom_call" | custom-call | tf_op jit(solution)/shard_map/attention_wgrad/pallas_call | solution.py:203
  701.7 2.3 pad_maximum_fusion
  709.7 12.4 %attention_wgrad.3 = (bf16[2,4,128,512]{3,2,1,0:T(8,128)(2,1)}, bf16[2,4,128,512]{3,2,1,0:T(8,128)(2,1)}, bf16[2,4,128,512]{3,2,1,0:T(8,128)(2,1)}, bf16[2,4,128,512]{3,2,1,0:T(8,128)(2,1)}) custom-call(s32[4]{0:T(128)} %get-tuple-element.214.order, s32[2,4,4]{2,1,0:T(4,128)} %constant.83.clone.tables, ...), custom_call_target="tpu_custom_call" | custom-call | tf_op jit(solution)/shard_map/attention_wgrad/pallas_call | solution.py:203
  722.1 11.4 %collective-permute-done.43 = bf16[2,2,1024,256]{3,2,1,0:T(8,128)(2,1)} collective-permute-done((bf16[2,2,1024,256]{3,2,1,0:T(8,128)(2,1)}, bf16[2,2,1024,256]{3,2,1,0:T(8,128)(2,1)}, u32[]{:S(2)}, u32[]{:S(2)}) %collective-permute-start.43) | collective-permute-done | bytes 2097184 | tf_op jit(solution)/shard_map/ppermute | solution.py:693
  734.1 2.1 fusion.1
  737.8 2.1 fusion.13
  741.4 15.1 %collective-permute-done.41 = bf16[1,2,1024,256]{3,2,1,0:T(8,128)(2,1)} collective-permute-done((bf16[1,2,1024,256]{3,2,1,0:T(8,128)(2,1)}, bf16[1,2,1024,256]{3,2,1,0:T(8,128)(2,1)}, u32[]{:S(2)}, u32[]{:S(2)}) %collective-permute-start.41) | collective-permute-done | bytes 1048608 | tf_op jit(solution)/shard_map/ppermute | solution.py:693
  758.4 2.3 pad_maximum_fusion.1
  762.6 16.4 %collective-permute-done.45 = bf16[1,2,1024,256]{3,2,1,0:T(8,128)(2,1)S(1)} collective-permute-done((bf16[1,2,1024,256]{3,2,1,0:T(8,128)(2,1)S(1)}, bf16[1,2,1024,256]{3,2,1,0:T(8,128)(2,1)S(1)}, u32[]{:S(2)}, u32[]{:S(2)}) %collective-permute-start.45) | collective-permute-done | bytes 1048608 | tf_op jit(solution)/shard_map/ppermute | solution.py:693
  779.5 2.3 pad_maximum_fusion.2
  781.8 2.8 fusion.14
  784.6 14.1 %collective-permute-done.32 = bf16[2,4,128,512]{3,2,1,0:T(8,128)(2,1)} collective-permute-done((bf16[2,4,128,512]{3,2,1,0:T(8,128)(2,1)}, bf16[2,4,128,512]{3,2,1,0:T(8,128)(2,1)}, u32[]{:S(2)}, u32[]{:S(2)}) %collective-permute-start.32) | collective-permute-done | bytes 1048608 | tf_op jit(solution)/shard_map/ppermute | solution.py:693
  799.6 1.8 add_convert_fusion.1
  806.6 11.2 %collective-permute-done.37 = f32[20,2048]{1,0:T(8,128)S(1)} collective-permute-done((f32[20,2048]{1,0:T(8,128)S(1)}, f32[20,2048]{1,0:T(8,128)S(1)}, u32[]{:S(2)}, u32[]{:S(2)}) %collective-permute-start.37) | collective-permute-done | bytes 163872 | tf_op jit(solution)/shard_map/ppermute | solution.py:753
  818.4 2.0 fusion.11
  820.4 3.1 collective-permute-done.38
  825.4 6.0 collective-permute-done.39
  833.1 7.0 collective-permute-done.40
  (250 shorter events, 73.6 us)
Async XLA Ops:
  7.2 155.2 %copy-start = (bf16[2048,512]{1,0:T(8,128)(2,1)S(1)}, bf16[2048,512]{1,0:T(8,128)(2,1)}, u32[]{:S(2)}) copy-start(bf16[2048,512]{1,0:T(8,128)(2,1)} %param.37) | copy-start | bytes 6291460
  7.2 89.0 %copy-start.2 = (bf16[256,2048]{1,0:T(8,128)(2,1)S(1)}, bf16[256,2048]{1,0:T(8,128)(2,1)}, u32[]{:S(2)}) copy-start(bf16[256,2048]{1,0:T(8,128)(2,1)} %cotangent.3) | copy-start | bytes 3145732
  7.2 89.0 %all-gather.5.cloned.1.call-start = ((), (), s32[]{:S(2)}) async-start(), calls=%async_computation.6 | async-start | bytes 5242880 | tf_op jit(solution)/shard_map/all_gather | solution.py:623
  12.6 120.2 %copy-start.31 = (s32[1,1024]{1,0:T(1,128)S(1)}, s32[1,1024]{1,0:T(1,128)}, u32[]{:S(2)}) copy-start(s32[1,1024]{1,0:T(1,128)} %seg_row.1) | copy-start | bytes 12292
  12.6 196.0 %reduce-scatter.7.cloned.1.call-start = ((), (), s32[]{:S(2)}) async-start(), calls=%async_computation.7 | async-start | bytes 2621440 | tf_op jit(solution)/shard_map/reduce_scatter | solution.py:627
  96.2 36.6 %collective-permute-start.2 = (bf16[256,2048]{1,0:T(8,128)(2,1)S(1)}, bf16[256,2048]{1,0:T(8,128)(2,1)}, u32[]{:S(2)}, u32[]{:S(2)}) collective-permute-start(bf16[256,2048]{1,0:T(8,128)(2,1)S(1)} %copy-done.2), channel_id=1, source_target_pairs={{0,1},{1,2},{2,3},{4,5},{5,6},{6,7},{8,9},{9,10},{10,11},{12,13},{... | collective-permute-start | bytes 3145736 | tf_op jit(solution)/shard_map/ppermute | solution.py:676
  98.5 34.3 %collective-permute-start.3 = (bf16[256,2048]{1,0:T(8,128)(2,1)S(1)}, bf16[256,2048]{1,0:T(8,128)(2,1)}, u32[]{:S(2)}, u32[]{:S(2)}) collective-permute-start(bf16[256,2048]{1,0:T(8,128)(2,1)S(1)} %copy-done.2), channel_id=1, source_target_pairs={{1,0},{2,1},{3,2},{5,4},{6,5},{7,6},{9,8},{10,9},{11,10},{13,12},{... | collective-permute-start | bytes 3145736 | tf_op jit(solution)/shard_map/ppermute | solution.py:677
  116.1 9.4 %collective-permute-start = (f32[2,1024]{1,0:T(2,128)}, f32[2,1024]{1,0:T(2,128)S(1)}, u32[]{:S(2)}, u32[]{:S(2)}) collective-permute-start(f32[2,1024]{1,0:T(2,128)} %get-tuple-element.126), channel_id=1, source_target_pairs={{0,1},{1,0},{2,3},{3,2},{4,5},{5,4},{6,7},{7,6},{8,9},{9,8},{10,11... | collective-permute-start | bytes 24584 | tf_op jit(solution)/shard_map/ppermute | solution.py:753
  126.2 4.5 collective-permute-start.1
  133.9 18.6 %collective-permute-start.4 = (bf16[256,2048]{1,0:T(8,128)(2,1)}, bf16[256,2048]{1,0:T(8,128)(2,1)}, u32[]{:S(2)}, u32[]{:S(2)}) collective-permute-start(bf16[256,2048]{1,0:T(8,128)(2,1)} %collective-permute-done.2), channel_id=1, source_target_pairs={{1,2},{2,3},{5,6},{6,7},{9,10},{10,11},{13,14},{14,15},{17,18},{18... | collective-permute-start | bytes 3145736 | tf_op jit(solution)/shard_map/ppermute | solution.py:676
  135.5 25.6 %collective-permute-start.5 = (bf16[256,2048]{1,0:T(8,128)(2,1)}, bf16[256,2048]{1,0:T(8,128)(2,1)}, u32[]{:S(2)}, u32[]{:S(2)}) collective-permute-start(bf16[256,2048]{1,0:T(8,128)(2,1)} %collective-permute-done.3), channel_id=1, source_target_pairs={{1,0},{2,1},{5,4},{6,5},{9,8},{10,9},{13,12},{14,13},{17,16},{18,1... | collective-permute-start | bytes 3145736 | tf_op jit(solution)/shard_map/ppermute | solution.py:677
  165.1 137.6 %reduce-scatter.9.cloned.1.call-start = ((), (), s32[]{:S(2)}) async-start(), calls=%async_computation.8 | async-start | bytes 2621440 | tf_op jit(solution)/shard_map/reduce_scatter | solution.py:627
  167.7 47.2 %copy-start.27 = (bf16[2048,16]{0,1:T(8,128)(2,1)S(1)}, bf16[2048,16]{0,1:T(8,128)(2,1)}, u32[]{:S(2)}) copy-start(bf16[2048,16]{0,1:T(8,128)(2,1)} %param.41) | copy-start | bytes 196612
  167.7 47.5 %copy-start.28 = (s32[1024,8]{0,1:T(8,128)S(1)}, s32[1024,8]{0,1:T(8,128)}, u32[]{:S(2)}) copy-start(s32[1024,8]{0,1:T(8,128)} %param.32) | copy-start | bytes 98308
  167.7 150.9 %all-gather.7.cloned.1.call-start = ((), (), s32[]{:S(2)}) async-start(), calls=%async_computation.9 | async-start | bytes 2621440 | tf_op jit(solution)/shard_map/all_gather | solution.py:623
  211.2 155.0 %all-gather.9.cloned.1.call-start = ((), (), s32[]{:S(2)}) async-start(), calls=%async_computation.10 | async-start | bytes 2621440 | tf_op jit(solution)/shard_map/all_gather | solution.py:623
  211.2 11.7 %collective-permute-start.6 = (bf16[256,2048]{1,0:T(8,128)(2,1)}, bf16[256,2048]{1,0:T(8,128)(2,1)}, u32[]{:S(2)}, u32[]{:S(2)}) collective-permute-start(bf16[256,2048]{1,0:T(8,128)(2,1)} %collective-permute-done.4), channel_id=1, source_target_pairs={{2,3},{6,7},{10,11},{14,15},{18,19},{22,23},{26,27},{30,31}} | collective-permute-start | bytes 3145736 | tf_op jit(solution)/shard_map/ppermute | solution.py:676
  212.9 60.6 %collective-permute-start.7 = (bf16[256,2048]{1,0:T(8,128)(2,1)}, bf16[256,2048]{1,0:T(8,128)(2,1)}, u32[]{:S(2)}, u32[]{:S(2)}) collective-permute-start(bf16[256,2048]{1,0:T(8,128)(2,1)} %collective-permute-done.5), channel_id=1, source_target_pairs={{1,0},{5,4},{9,8},{13,12},{17,16},{21,20},{25,24},{29,28}} | collective-permute-start | bytes 3145736 | tf_op jit(solution)/shard_map/ppermute | solution.py:677
  305.2 111.1 %reduce-scatter.13.cloned.1.call-start = ((), (), s32[]{:S(2)}) async-start(), calls=%async_computation.12 | async-start | bytes 2785280 | tf_op jit(solution)/shard_map/reduce_scatter | solution.py:627
  366.1 93.9 %reduce-scatter.11.cloned.1.call-start = ((), (), s32[]{:S(2)}) async-start(), calls=%async_computation.11 | async-start | bytes 2785280 | tf_op jit(solution)/shard_map/reduce_scatter | solution.py:627
  413.8 160.7 %all-gather.11.cloned.1.call-start = ((), (), s32[]{:S(2)}) async-start(), calls=%async_computation.14 | async-start | bytes 5242880 | tf_op jit(solution)/shard_map/all_gather | solution.py:623
  464.2 317.5 %reduce-scatter.15.cloned.1.call-start = ((), (), s32[]{:S(2)}) async-start(), calls=%async_computation.13 | async-start | bytes 5242880 | tf_op jit(solution)/shard_map/reduce_scatter | solution.py:627
  464.5 4.6 collective-permute-start.10
  464.6 7.5 collective-permute-start.11
  465.0 10.0 %collective-permute-start.8 = (bf16[2,2048,256]{2,1,0:T(8,128)(2,1)}, bf16[2,2048,256]{2,1,0:T(8,128)(2,1)}, u32[]{:S(2)}, u32[]{:S(2)}) collective-permute-start(bf16[2,2048,256]{2,1,0:T(8,128)(2,1)} %get-tuple-element.154), channel_id=1, source_target_pairs={{0,4},{4,0},{8,12},{12,8},{16,20},{20,16},{24,28},{28,24},{1,5},{5... | collective-permute-start | bytes 6291464 | tf_op jit(solution)/shard_map/ppermute | solution.py:693
  465.1 12.9 %collective-permute-start.9 = (bf16[2,2048,256]{2,1,0:T(8,128)(2,1)}, bf16[2,2048,256]{2,1,0:T(8,128)(2,1)}, u32[]{:S(2)}, u32[]{:S(2)}) collective-permute-start(bf16[2,2048,256]{2,1,0:T(8,128)(2,1)} %get-tuple-element.155), channel_id=1, source_target_pairs={{0,4},{4,0},{8,12},{12,8},{16,20},{20,16},{24,28},{28,24},{1,5},{5... | collective-permute-start | bytes 6291464 | tf_op jit(solution)/shard_map/ppermute | solution.py:693
  465.6 32.7 %collective-permute-start.12 = (bf16[2,2048,256]{2,1,0:T(8,128)(2,1)}, bf16[2,2048,256]{2,1,0:T(8,128)(2,1)}, u32[]{:S(2)}, u32[]{:S(2)}) collective-permute-start(bf16[2,2048,256]{2,1,0:T(8,128)(2,1)} %get-tuple-element.161), channel_id=1, source_target_pairs={{0,4},{4,0},{8,12},{12,8},{16,20},{20,16},{24,28},{28,24},{1,5},{5... | collective-permute-start | bytes 6291464 | tf_op jit(solution)/shard_map/ppermute | solution.py:693
  469.0 30.7 %collective-permute-start.13 = (bf16[2,2048,256]{2,1,0:T(8,128)(2,1)}, bf16[2,2048,256]{2,1,0:T(8,128)(2,1)}, u32[]{:S(2)}, u32[]{:S(2)}) collective-permute-start(bf16[2,2048,256]{2,1,0:T(8,128)(2,1)} %get-tuple-element.162), channel_id=1, source_target_pairs={{0,4},{4,0},{8,12},{12,8},{16,20},{20,16},{24,28},{28,24},{1,5},{5... | collective-permute-start | bytes 6291464 | tf_op jit(solution)/shard_map/ppermute | solution.py:693
  472.0 27.7 %collective-permute-start.14 = (bf16[2,2048,256]{2,1,0:T(8,128)(2,1)}, bf16[2,2048,256]{2,1,0:T(8,128)(2,1)}, u32[]{:S(2)}, u32[]{:S(2)}) collective-permute-start(bf16[2,2048,256]{2,1,0:T(8,128)(2,1)} %get-tuple-element.163), channel_id=1, source_target_pairs={{0,4},{4,0},{8,12},{12,8},{16,20},{20,16},{24,28},{28,24},{1,5},{5... | collective-permute-start | bytes 6291464 | tf_op jit(solution)/shard_map/ppermute | solution.py:693
  475.0 24.7 %collective-permute-start.15 = (bf16[2,2048,256]{2,1,0:T(8,128)(2,1)}, bf16[2,2048,256]{2,1,0:T(8,128)(2,1)}, u32[]{:S(2)}, u32[]{:S(2)}) collective-permute-start(bf16[2,2048,256]{2,1,0:T(8,128)(2,1)} %get-tuple-element.164), channel_id=1, source_target_pairs={{0,4},{4,0},{8,12},{12,8},{16,20},{20,16},{24,28},{28,24},{1,5},{5... | collective-permute-start | bytes 6291464 | tf_op jit(solution)/shard_map/ppermute | solution.py:693
  496.7 48.0 %collective-permute-start.16 = (bf16[2,2,1024,256]{3,2,1,0:T(8,128)(2,1)}, bf16[2,2,1024,256]{3,2,1,0:T(8,128)(2,1)}, u32[]{:S(2)}, u32[]{:S(2)}) collective-permute-start(bf16[2,2,1024,256]{3,2,1,0:T(8,128)(2,1)} %bitcast.181), channel_id=1, source_target_pairs={{0,16},{4,20},{8,24},{12,28},{16,0},{20,4},{24,8},{28,12},{1,17},{... | collective-permute-start | bytes 6291464 | tf_op jit(solution)/shard_map/ppermute | solution.py:693
  498.2 47.7 %collective-permute-start.17 = (bf16[2,2,1024,256]{3,2,1,0:T(8,128)(2,1)}, bf16[2,2,1024,256]{3,2,1,0:T(8,128)(2,1)}, u32[]{:S(2)}, u32[]{:S(2)}) collective-permute-start(bf16[2,2,1024,256]{3,2,1,0:T(8,128)(2,1)} %bitcast.180), channel_id=1, source_target_pairs={{0,8},{4,12},{8,0},{12,4},{16,24},{20,28},{24,16},{28,20},{1,9},{5... | collective-permute-start | bytes 6291464 | tf_op jit(solution)/shard_map/ppermute | solution.py:693
  553.5 231.0 %reduce-scatter.17.cloned.1.call-start = ((), (), s32[]{:S(2)}) async-start(), calls=%async_computation.15 | async-start | bytes 5242880 | tf_op jit(solution)/shard_map/reduce_scatter | solution.py:627
  553.6 46.9 %collective-permute-start.20 = (bf16[2,2,1024,256]{3,2,1,0:T(8,128)(2,1)}, bf16[2,2,1024,256]{3,2,1,0:T(8,128)(2,1)}, u32[]{:S(2)}, u32[]{:S(2)}) collective-permute-start(bf16[2,2,1024,256]{3,2,1,0:T(8,128)(2,1)} %bitcast.179), channel_id=1, source_target_pairs={{0,16},{4,20},{8,24},{12,28},{16,0},{20,4},{24,8},{28,12},{1,17},{... | collective-permute-start | bytes 6291464 | tf_op jit(solution)/shard_map/ppermute | solution.py:693
  554.2 18.8 %copy-start.32 = (s32[1,1024]{1,0:T(1,128)S(1)}, s32[1,1024]{1,0:T(1,128)}, u32[]{:S(2)}) copy-start(s32[1,1024]{1,0:T(1,128)} %seg_row.1) | copy-start | bytes 12292
  554.2 78.3 %collective-permute-start.21 = (bf16[2,2,1024,256]{3,2,1,0:T(8,128)(2,1)}, bf16[2,2,1024,256]{3,2,1,0:T(8,128)(2,1)}, u32[]{:S(2)}, u32[]{:S(2)}) collective-permute-start(bf16[2,2,1024,256]{3,2,1,0:T(8,128)(2,1)} %bitcast.178), channel_id=1, source_target_pairs={{0,8},{4,12},{8,0},{12,4},{16,24},{20,28},{24,16},{28,20},{1,9},{5... | collective-permute-start | bytes 6291464 | tf_op jit(solution)/shard_map/ppermute | solution.py:693
  573.0 61.5 %collective-permute-start.22 = (bf16[2,2048,256]{2,1,0:T(8,128)(2,1)}, bf16[2,2048,256]{2,1,0:T(8,128)(2,1)}, u32[]{:S(2)}, u32[]{:S(2)}) collective-permute-start(bf16[2,2048,256]{2,1,0:T(8,128)(2,1)} %get-tuple-element.187), channel_id=1, source_target_pairs={{0,4},{4,0},{8,12},{12,8},{16,20},{20,16},{24,28},{28,24},{1,5},{5... | collective-permute-start | bytes 6291464 | tf_op jit(solution)/shard_map/ppermute | solution.py:693
  574.0 70.7 %collective-permute-start.23 = (bf16[2,2048,256]{2,1,0:T(8,128)(2,1)}, bf16[2,2048,256]{2,1,0:T(8,128)(2,1)}, u32[]{:S(2)}, u32[]{:S(2)}) collective-permute-start(bf16[2,2048,256]{2,1,0:T(8,128)(2,1)} %get-tuple-element.188), channel_id=1, source_target_pairs={{0,4},{4,0},{8,12},{12,8},{16,20},{20,16},{24,28},{28,24},{1,5},{5... | collective-permute-start | bytes 6291464 | tf_op jit(solution)/shard_map/ppermute | solution.py:693
  574.5 72.2 %collective-permute-start.24 = (bf16[2,2048,256]{2,1,0:T(8,128)(2,1)}, bf16[2,2048,256]{2,1,0:T(8,128)(2,1)}, u32[]{:S(2)}, u32[]{:S(2)}) collective-permute-start(bf16[2,2048,256]{2,1,0:T(8,128)(2,1)} %get-tuple-element.189), channel_id=1, source_target_pairs={{0,4},{4,0},{8,12},{12,8},{16,20},{20,16},{24,28},{28,24},{1,5},{5... | collective-permute-start | bytes 6291464 | tf_op jit(solution)/shard_map/ppermute | solution.py:693
  600.5 46.2 %collective-permute-start.25 = (bf16[2,2048,256]{2,1,0:T(8,128)(2,1)}, bf16[2,2048,256]{2,1,0:T(8,128)(2,1)}, u32[]{:S(2)}, u32[]{:S(2)}) collective-permute-start(bf16[2,2048,256]{2,1,0:T(8,128)(2,1)} %get-tuple-element.190), channel_id=1, source_target_pairs={{0,4},{4,0},{8,12},{12,8},{16,20},{20,16},{24,28},{28,24},{1,5},{5... | collective-permute-start | bytes 6291464 | tf_op jit(solution)/shard_map/ppermute | solution.py:693
  632.6 3.7 collective-permute-start.18
  634.5 30.8 %collective-permute-start.27 = (bf16[1,2,1024,256]{3,2,1,0:T(8,128)(2,1)S(1)}, bf16[1,2,1024,256]{3,2,1,0:T(8,128)(2,1)S(1)}, u32[]{:S(2)}, u32[]{:S(2)}) collective-permute-start(bf16[1,2,1024,256]{3,2,1,0:T(8,128)(2,1)S(1)} %slice_bitcast_fusion.5), channel_id=1, source_target_pairs={{0,16},{4,20},{8,24},{12,28},{16,0},{20,4},{24,8},{28,12},{1,17},{... | collective-permute-start | bytes 3145736 | tf_op jit(solution)/shard_map/ppermute | solution.py:693
  636.3 29.1 %collective-permute-start.26 = (bf16[1,2,1024,256]{3,2,1,0:T(8,128)(2,1)S(1)}, bf16[1,2,1024,256]{3,2,1,0:T(8,128)(2,1)S(1)}, u32[]{:S(2)}, u32[]{:S(2)}) collective-permute-start(bf16[1,2,1024,256]{3,2,1,0:T(8,128)(2,1)S(1)} %slice.128), channel_id=1, source_target_pairs={{0,8},{4,12},{8,0},{12,4},{16,24},{20,28},{24,16},{28,20},{1,9},{5... | collective-permute-start | bytes 3145736 | tf_op jit(solution)/shard_map/ppermute | solution.py:693
  644.8 22.5 %collective-permute-start.19 = (f32[2,1024]{1,0:T(2,128)S(1)}, f32[2,1024]{1,0:T(2,128)S(1)}, u32[]{:S(2)}, u32[]{:S(2)}) collective-permute-start(f32[2,1024]{1,0:T(2,128)S(1)} %fusion.35), channel_id=1, source_target_pairs={{0,2},{1,3},{2,0},{3,1},{4,6},{5,7},{6,4},{7,5},{8,10},{9,11},{10,... | collective-permute-start | bytes 24584 | tf_op jit(solution)/shard_map/ppermute | solution.py:753
  684.6 48.9 %collective-permute-start.43 = (bf16[2,2,1024,256]{3,2,1,0:T(8,128)(2,1)}, bf16[2,2,1024,256]{3,2,1,0:T(8,128)(2,1)}, u32[]{:S(2)}, u32[]{:S(2)}) collective-permute-start(bf16[2,2,1024,256]{3,2,1,0:T(8,128)(2,1)} %bitcast.177), channel_id=1, source_target_pairs={{0,16},{4,20},{8,24},{12,28},{16,0},{20,4},{24,8},{28,12},{1,17},{... | collective-permute-start | bytes 6291464 | tf_op jit(solution)/shard_map/ppermute | solution.py:693
  685.2 48.9 %collective-permute-start.44 = (bf16[2,2,1024,256]{3,2,1,0:T(8,128)(2,1)}, bf16[2,2,1024,256]{3,2,1,0:T(8,128)(2,1)}, u32[]{:S(2)}, u32[]{:S(2)}) collective-permute-start(bf16[2,2,1024,256]{3,2,1,0:T(8,128)(2,1)} %bitcast.176), channel_id=1, source_target_pairs={{0,8},{4,12},{8,0},{12,4},{16,24},{20,28},{24,16},{28,20},{1,9},{5... | collective-permute-start | bytes 6291464 | tf_op jit(solution)/shard_map/ppermute | solution.py:693
  697.8 3.0 collective-permute-start.28
  700.2 6.1 collective-permute-start.29
  700.2 8.0 collective-permute-start.30
  700.7 9.0 %collective-permute-start.31 = (bf16[1,4,256,512]{3,2,1,0:T(8,128)(2,1)}, bf16[1,4,256,512]{3,2,1,0:T(8,128)(2,1)}, u32[]{:S(2)}, u32[]{:S(2)}) collective-permute-start(bf16[1,4,256,512]{3,2,1,0:T(8,128)(2,1)} %get-tuple-element.213), channel_id=1, source_target_pairs={{0,4},{4,0},{8,12},{12,8},{16,20},{20,16},{24,28},{28,24},{1,5},{5... | collective-permute-start | bytes 3145736 | tf_op jit(solution)/shard_map/ppermute | solution.py:693
  706.3 50.3 %collective-permute-start.41 = (bf16[1,2,1024,256]{3,2,1,0:T(8,128)(2,1)}, bf16[1,2,1024,256]{3,2,1,0:T(8,128)(2,1)}, u32[]{:S(2)}, u32[]{:S(2)}) collective-permute-start(bf16[1,2,1024,256]{3,2,1,0:T(8,128)(2,1)} %slice.144), channel_id=1, source_target_pairs={{0,8},{4,12},{8,0},{12,4},{16,24},{20,28},{24,16},{28,20},{1,9},{5... | collective-permute-start | bytes 3145736 | tf_op jit(solution)/shard_map/ppermute | solution.py:693
  708.2 25.9 %copy-start.16 = (bf16[4,1024,256]{2,1,0:T(8,128)(2,1)S(1)}, bf16[4,1024,256]{2,1,0:T(8,128)(2,1)}, u32[]{:S(2)}) copy-start(bf16[4,1024,256]{2,1,0:T(8,128)(2,1)} %get-tuple-element.201) | copy-start | bytes 6291460
  708.2 49.9 %collective-permute-start.42 = (bf16[1,2,1024,256]{3,2,1,0:T(8,128)(2,1)S(1)}, bf16[1,2,1024,256]{3,2,1,0:T(8,128)(2,1)S(1)}, u32[]{:S(2)}, u32[]{:S(2)}) collective-permute-start(bf16[1,2,1024,256]{3,2,1,0:T(8,128)(2,1)S(1)} %slice_bitcast_fusion.2), channel_id=1, source_target_pairs={{0,16},{4,20},{8,24},{12,28},{16,0},{20,4},{24,8},{28,12},{1,17},{... | collective-permute-start | bytes 3145736 | tf_op jit(solution)/shard_map/ppermute | solution.py:693
  736.3 42.7 %collective-permute-start.45 = (bf16[1,2,1024,256]{3,2,1,0:T(8,128)(2,1)S(1)}, bf16[1,2,1024,256]{3,2,1,0:T(8,128)(2,1)S(1)}, u32[]{:S(2)}, u32[]{:S(2)}) collective-permute-start(bf16[1,2,1024,256]{3,2,1,0:T(8,128)(2,1)S(1)} %slice.148), channel_id=1, source_target_pairs={{0,8},{4,12},{8,0},{12,4},{16,24},{20,28},{24,16},{28,20},{1,9},{5... | collective-permute-start | bytes 3145736 | tf_op jit(solution)/shard_map/ppermute | solution.py:693
  739.9 39.3 %collective-permute-start.46 = (bf16[1,2,1024,256]{3,2,1,0:T(8,128)(2,1)S(1)}, bf16[1,2,1024,256]{3,2,1,0:T(8,128)(2,1)S(1)}, u32[]{:S(2)}, u32[]{:S(2)}) collective-permute-start(bf16[1,2,1024,256]{3,2,1,0:T(8,128)(2,1)S(1)} %slice_bitcast_fusion), channel_id=1, source_target_pairs={{0,16},{4,20},{8,24},{12,28},{16,0},{20,4},{24,8},{28,12},{1,17},{... | collective-permute-start | bytes 3145736 | tf_op jit(solution)/shard_map/ppermute | solution.py:693
  760.6 38.0 %collective-permute-start.32 = (bf16[2,4,128,512]{3,2,1,0:T(8,128)(2,1)}, bf16[2,4,128,512]{3,2,1,0:T(8,128)(2,1)}, u32[]{:S(2)}, u32[]{:S(2)}) collective-permute-start(bf16[2,4,128,512]{3,2,1,0:T(8,128)(2,1)} %get-tuple-element.215), channel_id=1, source_target_pairs={{0,16},{4,20},{8,24},{12,28},{16,0},{20,4},{24,8},{28,12},{1,17},{... | collective-permute-start | bytes 3145736 | tf_op jit(solution)/shard_map/ppermute | solution.py:693
  762.1 37.5 %collective-permute-start.33 = (bf16[2,4,128,512]{3,2,1,0:T(8,128)(2,1)}, bf16[2,4,128,512]{3,2,1,0:T(8,128)(2,1)}, u32[]{:S(2)}, u32[]{:S(2)}) collective-permute-start(bf16[2,4,128,512]{3,2,1,0:T(8,128)(2,1)} %get-tuple-element.216), channel_id=1, source_target_pairs={{0,8},{4,12},{8,0},{12,4},{16,24},{20,28},{24,16},{28,20},{1,9},{5... | collective-permute-start | bytes 3145736 | tf_op jit(solution)/shard_map/ppermute | solution.py:693
  784.6 20.5 %collective-permute-start.36 = (f32[20,2048]{1,0:T(8,128)S(1)}, f32[20,2048]{1,0:T(8,128)S(1)}, u32[]{:S(2)}, u32[]{:S(2)}) collective-permute-start(f32[20,2048]{1,0:T(8,128)S(1)} %concatenate.20), channel_id=1, source_target_pairs={{0,4},{4,0},{8,12},{12,8},{16,20},{20,16},{24,28},{28,24},{1,5},{5... | collective-permute-start | bytes 491528 | tf_op jit(solution)/shard_map/ppermute | solution.py:753
  801.5 23.6 %collective-permute-start.34 = (bf16[1,4,128,512]{3,2,1,0:T(8,128)(2,1)S(1)}, bf16[1,4,128,512]{3,2,1,0:T(8,128)(2,1)S(1)}, u32[]{:S(2)}, u32[]{:S(2)}) collective-permute-start(bf16[1,4,128,512]{3,2,1,0:T(8,128)(2,1)S(1)} %slice.131), channel_id=1, source_target_pairs={{0,8},{4,12},{8,0},{12,4},{16,24},{20,28},{24,16},{28,20},{1,9},{5... | collective-permute-start | bytes 1572872 | tf_op jit(solution)/shard_map/ppermute | solution.py:693
  803.7 21.5 %collective-permute-start.35 = (bf16[1,4,128,512]{3,2,1,0:T(8,128)(2,1)S(1)}, bf16[1,4,128,512]{3,2,1,0:T(8,128)(2,1)S(1)}, u32[]{:S(2)}, u32[]{:S(2)}) collective-permute-start(bf16[1,4,128,512]{3,2,1,0:T(8,128)(2,1)S(1)} %slice_bitcast_fusion.6), channel_id=1, source_target_pairs={{0,16},{4,20},{8,24},{12,28},{16,0},{20,4},{24,8},{28,12},{1,17},{... | collective-permute-start | bytes 1572872 | tf_op jit(solution)/shard_map/ppermute | solution.py:693
  805.1 12.7 %collective-permute-start.37 = (f32[20,2048]{1,0:T(8,128)S(1)}, f32[20,2048]{1,0:T(8,128)S(1)}, u32[]{:S(2)}, u32[]{:S(2)}) collective-permute-start(f32[20,2048]{1,0:T(8,128)S(1)} %add.230), channel_id=1, source_target_pairs={{0,8},{4,12},{8,0},{12,4},{16,24},{20,28},{24,16},{28,20},{1,9},{5... | collective-permute-start | bytes 491528 | tf_op jit(solution)/shard_map/ppermute | solution.py:753
  817.8 5.7 collective-permute-start.38
  823.6 7.8 collective-permute-start.39
  831.4 8.7 %collective-permute-start.40 = (f32[20,2048]{1,0:T(8,128)S(1)}, f32[20,2048]{1,0:T(8,128)S(1)}, u32[]{:S(2)}, u32[]{:S(2)}) collective-permute-start(f32[20,2048]{1,0:T(8,128)S(1)} %add.233), channel_id=1, source_target_pairs={{0,2},{1,3},{2,0},{3,1},{4,6},{5,7},{6,4},{7,5},{8,10},{9,11},{10,... | collective-permute-start | bytes 491528 | tf_op jit(solution)/shard_map/ppermute | solution.py:753
  (36 other events, 191.6 us)
Sparse Core Ops, SparseCore 0:
  12.7 83.4 all-gather.4
  165.2 43.3 reduce-scatter.6
  211.6 58.9 reduce-scatter.8
  272.6 46.0 all-gather.6
  320.7 44.6 all-gather.8
  367.5 44.6 reduce-scatter.12
  414.6 45.3 reduce-scatter.10
  464.4 80.1 all-gather.10
  553.7 75.2 reduce-scatter.14
  683.4 74.4 reduce-scatter.16

commit v8 on v7

--- a/solution.py
+++ b/solution.py
@@ -444,7 +444,7 @@
         taken = rows_in[here, :]
         pre_gate = nn(taken, gate)
         pre_up = nn(taken, up)
-        behind = back[here, :].astype(f32)
+        behind = back[...].reshape(rows, back.shape[3])[here, :].astype(f32)
         share = jnp.sum(jnp.where(mine, comb[here, :], 0.0), axis=1, keepdims=True)
         sigmoid = 0.5 * jnp.tanh(0.5 * pre_gate) + 0.5
         active = pre_gate * sigmoid
@@ -467,6 +467,7 @@
 
 def experts_block(chunk, rows_in, back, routed, router, gate_w, up_w):
     rows, features = rows_in.shape
+    parts, _, chunk_rows, _ = back.shape
     experts, _, width = gate_w.shape
     block = min(512, rows)
     whole = lambda *shape: pl.BlockSpec(shape, lambda e: (0, 0))
@@ -476,7 +477,7 @@
     return pl.pallas_call(
         functools.partial(expert_kernel, block),
         grid=(experts,),
-        in_specs=[whole(rows, features), pl.BlockSpec((rows, width), lambda e: (chunk, e)), whole(rows, LANES), whole(features, LANES), weight, weight],
+        in_specs=[whole(rows, features), pl.BlockSpec((parts, 1, chunk_rows, width), lambda e: (0, chunk, 0, e)), whole(rows, LANES), whole(features, LANES), weight, weight],
         out_specs=[column, column, column, whole(rows, features + LANES)],
         out_shape=[wide, wide, wide, jax.ShapeDtypeStruct((rows, features + LANES), bf16)],
         scratch_shapes=[pltpu.VMEM((rows, LANES), f32), pltpu.VMEM((rows, LANES), f32), pltpu.VMEM((rows, features), f32)],
@@ -514,12 +515,14 @@
     added = refs[2 * count : 2 * count + extra]
     outs = refs[2 * count + extra :]
     at = pl.program_id(0)
-    features = lefts[0].shape[1]
+    features = lefts[0].shape[-1]
 
     def piece(start, stop):
-        total = tn(lefts[0][:, start:stop], rights[0][...])
-        for left, right in zip(lefts[1:], rights[1:]):
-            total = total + tn(left[:, start:stop], right[...])
+        total = None
+        for left, right in zip(lefts, rights):
+            columns = left[:, start:stop] if len(left.shape) == 2 else left[:, :, :, start:stop].reshape(-1, stop - start)
+            part = tn(columns, right[...])
+            total = part if total is None else total + part
         return total
 
     if not added:
@@ -550,8 +553,8 @@
             out[0] = got[start : start + half, :]
 
 
-def wgrad(lefts, rights, order, width, per, added=()):
-    features = lefts[0][0].shape[1]
+def wgrad(lefts, rights, order, width, per, added=(), weight=1):
+    features = lefts[0][0].shape[-1]
     experts = order.shape[0]
     groups = experts // per
     tables, sizes = split_tables(groups, per)
@@ -561,6 +564,11 @@
 
     def half_spec(side):
         return pl.BlockSpec((1, features // 2, width), lambda i, ids, to: (to[0, side, i], 0, 0))
+
+    def left_spec(left, chunk):
+        if left.ndim == 2:
+            return pl.BlockSpec(left.shape, lambda i, ids, to: (0, 0))
+        return pl.BlockSpec((left.shape[0], 1) + left.shape[2:], lambda i, ids, to: (0, chunk, 0, 0))
 
     groups_specs = [group_spec(place) for place in range(groups)]
     if added:
@@ -574,7 +582,7 @@
         grid_spec=pltpu.PrefetchScalarGridSpec(
             num_scalar_prefetch=2,
             grid=(experts,),
-            in_specs=[pl.BlockSpec((right.shape[0], features), lambda i, ids, to, at=at: (at, 0)) for (_, at), right in zip(lefts, rights)]
+            in_specs=[left_spec(*left) for left in lefts]
             + [pl.BlockSpec((right.shape[0], width), lambda i, ids, to: (0, ids[i])) for right in rights]
             + (groups_specs if added else []),
             out_specs=out_specs,
@@ -582,7 +590,7 @@
         ),
         out_shape=out_shape,
         compiler_params=params(),
-        cost_estimate=cost(2 * sum(right.shape[0] for right in rights) * features * experts * width, 0),
+        cost_estimate=cost(2 * weight * sum(right.shape[0] for right in rights) * features * experts * width, 0),
         name="wgrad",
     )(order, tables, *(left for left, _ in lefts), *rights, *added)
 
@@ -625,67 +633,6 @@
 
 def scatter_rows(values):
     return lax.psum_scatter(values, "tensor", scatter_dimension=0, tiled=True)
-
-
-def join_kernel(parts, slots, own, *refs):
-    ups, downs, out = refs[: parts - 1], refs[parts - 1 : 2 * parts - 2], refs[2 * parts - 2]
-    at = pl.program_id(0)
-
-    @pl.when(at == 0)
-    def _():
-        out[...] = own[...]
-
-    for step in range(1, parts):
-
-        @pl.when(at == step)
-        def _(step=step):
-            out[...] = ups[step - 1][...] + downs[parts - 1 - step][...]
-
-
-def join(slots, own, ups, downs):
-    parts = len(ups) + 1
-    rows, columns = own.shape
-    split = (CHUNKS, rows // CHUNKS, columns)
-    whole = pl.BlockSpec(split, lambda i, to: (0, 0, 0))
-    return pl.pallas_call(
-        functools.partial(join_kernel, parts),
-        grid_spec=pltpu.PrefetchScalarGridSpec(
-            num_scalar_prefetch=1,
-            grid=(parts,),
-            in_specs=[whole] * (2 * parts - 1),
-            out_specs=pl.BlockSpec(split, lambda i, to: (0, to[i], 0)),
-        ),
-        out_shape=jax.ShapeDtypeStruct((CHUNKS, parts * rows // CHUNKS, columns), own.dtype),
-        compiler_params=params(),
-        cost_estimate=cost(0, 0),
-        name="join",
-    )(slots, *(piece.reshape(split) for piece in (own, *ups, *downs)))
-
-
-class Chain:
-    def __init__(self, values):
-        self.values = values
-        self.parts = lax.axis_size("tensor")
-        self.ups, self.downs = [values], [values]
-
-    def hop(self, *others):
-        step = len(self.ups)
-        if step < self.parts:
-            up, down = gate((self.ups[-1], self.downs[-1]), *others) if others else (self.ups[-1], self.downs[-1])
-            self.sent = (up, down)
-            self.ups.append(lax.ppermute(up, "tensor", [(i, i + 1) for i in range(step - 1, self.parts - 1)]))
-            self.downs.append(lax.ppermute(down, "tensor", [(i, i - 1) for i in range(1, self.parts - step + 1)]))
-        return self.sent
-
-    def recv(self):
-        return self.ups[-1], self.downs[-1]
-
-    def joined(self):
-        while len(self.ups) < self.parts:
-            self.hop()
-        at = lax.axis_index("tensor")
-        slots = lax.rem(at - jnp.arange(self.parts, dtype=jnp.int32) + self.parts, self.parts)
-        return join(slots, self.values, self.ups[1:], self.downs[1:])
 
 
 def pair_swap(values, step):
@@ -780,7 +727,7 @@
     inputs = tokens.astype(f32)
     first_scale = rms_scale(inputs)
     normed_all = gather_rows((inputs * first_scale * attn_gain).astype(bf16))
-    behind = Chain(gate(cotangent, normed_all))
+    grad_rows = gather_rows(gate(cotangent, normed_all))
 
     cosine, sine = rope_tables(length, HEAD)
 
@@ -792,26 +739,23 @@
 
     qraw, kraw, value, squares = project(normed_all, w_query, w_key, w_value)
     squares = exchange_sum(squares, ("tensor",))
-    behind.hop()
     q_scale, k_scale = (lax.rsqrt(squares[i] / features + EPSILON)[:, None] for i in range(2))
     query, key, attended, lse = attend(
-        qraw, kraw, value, q_scale, k_scale, q_gain, k_gain, cosine, sine, gate(seg_ids[0], *behind.recv()), keep_mask[0]
+        qraw, kraw, value, q_scale, k_scale, q_gain, k_gain, cosine, sine, seg_ids[0], keep_mask[0]
     )
-    behind.hop()
-    attended_parts = [chunk_of(gate(attended, *behind.recv()), c) for c in chunks]
+    attended_parts = [chunk_of(gate(attended, grad_rows), c) for c in chunks]
     outs = [nt(attended_parts[0], w_out).astype(bf16)]
     summed = [scatter_rows(outs[0])]
     outs.append(nt(gate(attended_parts[1], outs[0]), w_out).astype(bf16))
     summed.append(scatter_rows(outs[1]))
-    behind.hop(outs[1])
 
     idle_routes, idle_router = gate((routes, router), outs[1])
     expert_ids = jnp.arange(LANES)
     routed = jnp.sum((idle_routes[:, :, None] == expert_ids[None, None, :]).astype(f32), axis=1)
     router_wide = jnp.pad(idle_router, ((0, 0), (0, LANES - experts)))
     routed_own = lax.dynamic_slice_in_dim(routed, part_at * shard_rows, shard_rows, 0)
-    grad_rows = behind.joined().reshape(group_rows, features)
-    back = up_back(gate(grad_rows, routed, router_wide), w_down)
+    back = up_back(gate(grad_rows, routed, router_wide), w_down).reshape(parts, CHUNKS, chunk_rows, -1)
+    grad_rows = grad_rows.reshape(parts, CHUNKS, chunk_rows, features)
     grad_parts = [(grad_rows, c) for c in chunks]
 
     norms = [middle_rows(0, tokens, summed[0], ffn_gain)]
@@ -832,8 +776,8 @@
     def back_of(c, grads, filled=()):
         return middle_back(c, grads, *norms[c], routed_own, router_wide, cotangent, ffn_gain, experts, filled)
 
-    def expert_sums(lefts, rights, ids, *others, added=()):
-        return wgrad(lefts, rights, gate(ids, *others), width, per, added)
+    def expert_sums(lefts, rights, ids, *others, added=(), weight=1):
+        return wgrad(lefts, rights, gate(ids, *others), width, per, added, weight)
 
     def core_swap(pieces):
         return [pair_swap(piece, 1) for piece in pieces]
@@ -856,26 +800,25 @@
     up_out = halving(up_sums)
     up_out.send()
     moe = down([gate(acts[0], *up_sums), acts[1]], w_down, parts)
-    gate_late = gate_out.add(moe)
-    gate_out.send()
-    moe_sum = scatter_rows(gate(moe, *gate_late))
-    down_sent = expert_sums(grad_parts, acts, theirs, moe, *gate_late)
-    down_got = core_swap(down_sent)
-
-    attended_grad = nn(gate(middle_all, *down_sent), w_out).astype(bf16)
+    moe_sum = scatter_rows(moe)
+    attended_grad = nn(gate(middle_all, moe), w_out).astype(bf16)
     dqn, dkn, dvalue, qdot, kdot, q_gain_part, k_gain_part = attend_back(
         query, key, value, attended_grad, lse, qraw, kraw, q_scale, k_scale, q_gain, k_gain, cosine, sine,
         seg_ids[0], keep_mask[0],
     )
     dots = exchange_sum(jnp.stack([qdot[:, 0], kdot[:, 0]]), ("tensor",)) / features
-    up_late = up_out.add(dqn)
+    gate_late = gate_out.add(dqn)
+    gate_out.send()
+    down_sent = expert_sums(grad_parts, acts, theirs, *gate_late)
+    down_got = core_swap(down_sent)
+    up_late = up_out.add(*down_sent)
     up_out.send()
-    down_sums = expert_sums(grad_parts, acts, mine, *up_late, added=down_got)
+    down_sums = expert_sums(grad_parts, acts, mine, *up_late, *gate_out.got, added=down_got, weight=13.0)
     down_out = halving(down_sums)
     down_out.send()
     normed_part, dqraw, dkraw, attn_gain_part = project_back(
         normed_all, dqn, dkn, dvalue, qraw, kraw, q_scale, k_scale, dots[0][:, None], dots[1][:, None],
-        gate(q_gain, *down_sums, *gate_out.got), k_gain, w_query, w_key, w_value,
+        gate(q_gain, *down_sums, *up_out.got), k_gain, w_query, w_key, w_value,
     )
     normed_grad = scatter_rows(normed_part)
     def attention_sums(ids, *others, added=()):
@@ -896,14 +839,15 @@
     down_out.send()
     smalls = [attn_gain_part[0] / attn_gain, placed(q_gain_part[0]), placed(k_gain_part[0]), (first[2] + second[2])[0]]
     router_part = sum(tn(late[3], norms[c][2]) for c, late in enumerate((first, second)))[:experts]
-    smalls = gate(jnp.concatenate([jnp.stack(smalls), router_part]), normed_grad)
+    smalls = gate(jnp.concatenate([jnp.stack(smalls), router_part]), *attn_sums)
     smalls = exchange_sum(smalls, ("dp", "tensor"))
+    late_got = tuple(down_out.got)
     gate_done = gate_out.done()
     up_done = up_out.done()
     down_done = down_out.done()
     attn_out.add(normed_grad)
     query_done, key_done, value_done, out_done = attn_out.done()
-    layer_out = (jnp.concatenate([norms[c][0] for c in chunks]) + moe_sum.astype(f32)).astype(bf16)
+    layer_out = (jnp.concatenate([norms[c][0] for c in chunks]) + gate(moe_sum, *late_got).astype(f32)).astype(bf16)
     tokens_grad = middle_grad + norm_back(normed_grad.astype(f32), inputs, first_scale, attn_gain)
     return (
         layer_out, tokens_grad, query_done, key_done, value_done, out_done,

time: 857 us -> 843 us (0.984)
    all_gather x4 -> x5, waiting for transfers between devices: 97 us -> 164 us  [gather_rows(): return lax.all_gather(values, 'tensor', axis=0, tiled=True)]
    ppermute x6 -> x0, waiting for transfers between devices: 59.3 us -> none  [the longest x3 59.3 us: hop(): lax.ppermute(down, 'tensor', [(i, i - 1) for i in range(1, self.parts - s...]
    ppermute x32, waiting for transfers between devices: 98.9 us -> 75 us  [pair_swap(): return lax.ppermute(values, 'dp', [(i, i ^ step) for i in range(size)])]
    reduce_scatter x6, waiting for transfers between devices: 46.6 us -> 58.2 us  [scatter_rows(): return lax.psum_scatter(values, 'tensor', scatter_dimension=0, tiled=True)]
    ppermute x9, waiting for transfers between devices: 39 us -> 48.7 us  [exchange_sum(): lax.ppermute(values, axis, [(i, i ^ step) for i in range(size)])]
    ppermute x6 -> x0, starting transfers between devices: 9.62 us -> none  [the longest x3 5.57 us: hop(): lax.ppermute(up, 'tensor', [(i, i + 1) for i in range(step - 1, self.part...]
  transfers between devices with their start and end apart: 57 -> 52, of which waited for: 26 -> 28; matrix products, arithmetic and copies ran while one was open for 8% -> 8% of each run, Pallas kernels for 42% -> 42%
where the time goes in v8:
time: 843 us; the launch traced here: 835 us
  Pallas kernels  357 us (42%)
  waiting for transfers between devices  346 us (41%)
  other arithmetic  52.1 us (6%)
  starting transfers between devices  33.2 us (4%)
  local copies, waits for them, and re-layouts  20.5 us (2%)
  between operations  15 us (2%)
  matrix products  11.4 us (1%)
    all_gather x5, waiting for transfers between devices, gather_rows(): return lax.all_gather(values, 'tensor', axis=0, tiled=True)  164 us
    pallas_call x6, Pallas kernels, wgrad(): pl.pallas_call(functools.partial(wgrad_kernel, len(lefts), len(added), pe...  107 us
    pallas_call x2, Pallas kernels, experts_block(): pl.pallas_call(functools.partial(expert_kernel, block), grid=(experts,),...  94.8 us
    ppermute x32, waiting for transfers between devices, pair_swap(): return lax.ppermute(values, 'dp', [(i, i ^ step) for i in range(size)])  75 us
    reduce_scatter x6, waiting for transfers between devices, scatter_rows(): return lax.psum_scatter(values, 'tensor', scatter_dimension=0, tiled=True)  58.2 us
    ppermute x9, waiting for transfers between devices, exchange_sum(): lax.ppermute(values, axis, [(i, i ^ step) for i in range(size)])  48.7 us
    pallas_call x1, Pallas kernels, attend_back(): pl.pallas_call(functools.partial(attend_back_kernel, block), grid=(width...  24.6 us
    ppermute x32, starting transfers between devices, pair_swap(): return lax.ppermute(values, 'dp', [(i, i ^ step) for i in range(size)])  24.6 us
  transfers between devices with their start and end apart: 52, of which 28 were waited for; matrix products, arithmetic and copies ran while one was open for 8% of the time, Pallas kernels for 42%

profile of v8, /device:TPU:0, one launch (start us, length us, event | category | flops | bytes accessed | tf_op | source)
XLA Modules:
  0.0 835.1 jit_solution(5313300010473327204)
XLA Ops:
  7.2 1.6 fusion.6
  10.0 2.5 fusion.8
  12.6 83.6 %all-gather.6.cloned.1.call-done.rows_in = bf16[1024,2048]{1,0:T(8,128)(2,1)} async-done(((bf16[256,2048]{1,0:T(8,128)(2,1)}), bf16[1024,2048]{1,0:T(8,128)(2,1)}) %all-gather.6.cloned.1.call-update) | async-done | bytes 4194320 | tf_op jit(solution)/shard_map/all_gather | solution.py:631
  96.3 16.3 %project.1 = (f32[1024,512]{1,0:T(8,128)}, f32[1024,512]{1,0:T(8,128)}, bf16[1024,512]{1,0:T(8,128)(2,1)}, f32[2,1024]{1,0:T(2,128)}) custom-call(bf16[1024,2048]{1,0:T(8,128)(2,1)} %all-gather.6.cloned.1.call-done.rows_in, bf16[2048,512]{1,0:T(8,128)(2,1)} %w_query.3, bf16[2048,512]{1,0:T(8,128)(2,1)} %w_key.3, bf16[2048,512]{1,0:T(8,128)(2,1)} %w_value.3), custom_call_target="tpu_custom_call" | custom-call | flops 2899102976 | bytes 1310720 | tf_op jit(solution)/shard_map/project/pallas_call | solution.py:101
  112.6 4.0 collective-permute-done
  119.2 4.8 collective-permute-done.1
  126.1 15.7 %attend.1 = (bf16[1024,512]{1,0:T(8,128)(2,1)}, bf16[1024,512]{1,0:T(8,128)(2,1)}, bf16[1024,512]{1,0:T(8,128)(2,1)}, f32[1024,512]{1,0:T(8,128)}) custom-call(f32[1024,512]{1,0:T(8,128)} %get-tuple-element.120.qraw, f32[1024,512]{1,0:T(8,128)} %get-tuple-element.121.kraw, bf16[1024,512]{1,0:T(8,128)(2,1)} %get-tuple-element.122.value, ...), custom_call_target="tpu_custom_call" | custom-call | flops 57347878912 | bytes 1179648 | tf_op jit(solution)/shard_map/attend/pallas_call | solution.py:253
  141.8 35.6 %all-gather.8.cloned.1.call-done.grad = bf16[1024,2048]{1,0:T(8,128)(2,1)} async-done(((bf16[256,2048]{1,0:T(8,128)(2,1)}), bf16[1024,2048]{1,0:T(8,128)(2,1)}) %all-gather.8.cloned.1.call-update) | async-done | bytes 4194320 | tf_op jit(solution)/shard_map/all_gather | solution.py:631
  178.7 2.7 convolution_convert_fusion.1
  181.4 2.6 convolution_convert_fusion
  184.1 39.8 %reduce-scatter.7.cloned.1.call-done.summed = bf16[128,2048]{1,0:T(8,128)(2,1)} async-done(((bf16[512,2048]{1,0:T(8,128)(2,1)}), bf16[128,2048]{1,0:T(8,128)(2,1)}) %reduce-scatter.7.cloned.1.call-update) | async-done | bytes 524304 | tf_op jit(solution)/shard_map/reduce_scatter | solution.py:635
  223.9 2.6 middle.2
  228.2 5.7 convert_reduce_fusion
  234.8 22.6 %up_back.1 = bf16[1024,4096]{1,0:T(8,128)(2,1)} custom-call(bf16[1024,2048]{1,0:T(8,128)(2,1)} %all-gather.8.cloned.1.call-done.grad, bf16[16,2048,256]{2,1,0:T(8,128)(2,1)} %down_w.3), custom_call_target="tpu_custom_call" | custom-call | flops 7730940928 | bytes 2621440 | tf_op jit(solution)/shard_map/up_back/pallas_call | solution.py:411
  257.4 12.5 %reduce-scatter.9.cloned.1.call-done.summed = bf16[128,2048]{1,0:T(8,128)(2,1)} async-done(((bf16[512,2048]{1,0:T(8,128)(2,1)}), bf16[128,2048]{1,0:T(8,128)(2,1)}) %reduce-scatter.9.cloned.1.call-update) | async-done | bytes 524304 | tf_op jit(solution)/shard_map/reduce_scatter | solution.py:635
  269.9 2.5 middle.3
  272.5 44.2 %all-gather.10.cloned.1.call-done.rows_in.refs_0_ = bf16[512,2048]{1,0:T(8,128)(2,1)} async-done(((bf16[128,2048]{1,0:T(8,128)(2,1)}), bf16[512,2048]{1,0:T(8,128)(2,1)}) %all-gather.10.cloned.1.call-update) | async-done | bytes 2097168 | tf_op jit(solution)/shard_map/all_gather | solution.py:631
  316.7 47.4 %experts.2 = (bf16[512,4096]{1,0:T(8,128)(2,1)}, bf16[512,4096]{1,0:T(8,128)(2,1)}, bf16[512,4096]{1,0:T(8,128)(2,1)}, bf16[512,2176]{1,0:T(8,128)(2,1)}) custom-call(bf16[512,2048]{1,0:T(8,128)(2,1)} %all-gather.10.cloned.1.call-done.rows_in.refs_0_, bf16[4,2,128,4096]{3,2,1,0:T(8,128)(2,1)} %bitcast.126, f32[512,128]{1,0:T(8,128)} %bitcast.142, ...), custom_call_target="tpu_custom_call" | custom-call | flops 53210619904 | bytes 6291456 | tf_op jit(solution)/shard_map/experts/pallas_call | solution.py:477
  364.2 47.4 %experts.3 = (bf16[512,4096]{1,0:T(8,128)(2,1)}, bf16[512,4096]{1,0:T(8,128)(2,1)}, bf16[512,4096]{1,0:T(8,128)(2,1)}, bf16[512,2176]{1,0:T(8,128)(2,1)}) custom-call(bf16[512,2048]{1,0:T(8,128)(2,1)} %all-gather.12.cloned.1.call-done.rows_in.refs_1_, bf16[4,2,128,4096]{3,2,1,0:T(8,128)(2,1)} %bitcast.127, f32[512,128]{1,0:T(8,128)} %bitcast.141, ...), custom_call_target="tpu_custom_call" | custom-call | flops 53210619904 | bytes 6291456 | tf_op jit(solution)/shard_map/experts/pallas_call | solution.py:477
  414.2 4.2 middle_back.2
  418.4 17.2 %wgrad.6 = (bf16[2,2048,256]{2,1,0:T(8,128)(2,1)}, bf16[2,2048,256]{2,1,0:T(8,128)(2,1)}, bf16[2,2048,256]{2,1,0:T(8,128)(2,1)}, bf16[2,2048,256]{2,1,0:T(8,128)(2,1)}) custom-call(s32[8]{0:T(128)} %add.209.order, s32[2,4,8]{2,1,0:T(4,128)} %constant.77.clone.tables, bf16[512,2048]{1,0:T(8,128)(2,1)} %all-gather.10.cloned.1.call-done.rows_in.refs_0_, ...), custom_call_target="tpu_custom_call" | custom-call | flops 3865470464 | tf_op jit(solution)/shard_map/wgrad/pallas_call | solution.py:580
  435.5 16.7 %wgrad.7 = (bf16[2,2048,256]{2,1,0:T(8,128)(2,1)}, bf16[2,2048,256]{2,1,0:T(8,128)(2,1)}, bf16[2,2048,256]{2,1,0:T(8,128)(2,1)}, bf16[2,2048,256]{2,1,0:T(8,128)(2,1)}) custom-call(s32[8]{0:T(128)} %add.209.order, s32[2,4,8]{2,1,0:T(4,128)} %constant.77.clone.tables, bf16[512,2048]{1,0:T(8,128)(2,1)} %all-gather.10.cloned.1.call-done.rows_in.refs_0_, ...), custom_call_target="tpu_custom_call" | custom-call | flops 3865470464 | tf_op jit(solution)/shard_map/wgrad/pallas_call | solution.py:580
  452.2 5.9 reduce-scatter.11.cloned.1.call-done.grads
  458.2 4.2 middle_back.3
  463.8 3.4 collective-permute-done.2.refs_4_
  467.3 2.9 collective-permute-done.3.refs_5_
  470.3 2.9 collective-permute-done.4.refs_6_
  474.0 2.2 collective-permute-done.5.refs_7_
  476.2 18.7 %wgrad.8 = (bf16[4,1024,256]{2,1,0:T(8,128)(2,1)}, bf16[4,1024,256]{2,1,0:T(8,128)(2,1)}, bf16[4,1024,256]{2,1,0:T(8,128)(2,1)}, bf16[4,1024,256]{2,1,0:T(8,128)(2,1)}) custom-call(s32[8]{0:T(128)} %add.204.order, s32[2,4,8]{2,1,0:T(4,128)} %constant.77.clone.tables, bf16[512,2048]{1,0:T(8,128)(2,1)} %all-gather.10.cloned.1.call-done.rows_in.refs_0_, ...), custom_call_target="tpu_custom_call" | custom-call | flops 3865470464 | tf_op jit(solution)/shard_map/wgrad/pallas_call | solution.py:580
  497.9 18.7 %wgrad.9 = (bf16[4,1024,256]{2,1,0:T(8,128)(2,1)}, bf16[4,1024,256]{2,1,0:T(8,128)(2,1)}, bf16[4,1024,256]{2,1,0:T(8,128)(2,1)}, bf16[4,1024,256]{2,1,0:T(8,128)(2,1)}) custom-call(s32[8]{0:T(128)} %add.204.order, s32[2,4,8]{2,1,0:T(4,128)} %constant.77.clone.tables, bf16[512,2048]{1,0:T(8,128)(2,1)} %all-gather.10.cloned.1.call-done.rows_in.refs_0_, ...), custom_call_target="tpu_custom_call" | custom-call | flops 3865470464 | tf_op jit(solution)/shard_map/wgrad/pallas_call | solution.py:580
  517.8 24.3 %down.1 = bf16[1024,2048]{1,0:T(8,128)(2,1)} custom-call(bf16[16,2048,256]{2,1,0:T(8,128)(2,1)} %down_w.3, bf16[512,4096]{1,0:T(8,128)(2,1)} %get-tuple-element.173.refs_0_.refs_2_, bf16[512,4096]{1,0:T(8,128)(2,1)} %get-tuple-element.141.refs_1_.refs_3_), custom_call_target="tpu_custom_call" | custom-call | flops 7730940928 | bytes 2621440 | tf_op jit(solution)/shard_map/down/pallas_call | solution.py:613
  542.7 5.5 convolution_convert_fusion.2.out_grad
  548.2 24.6 %attend_back.1 = (f32[1024,512]{1,0:T(8,128)}, f32[1024,512]{1,0:T(8,128)}, bf16[1024,512]{1,0:T(8,128)(2,1)}, f32[1024,1]{1,0:T(8,128)}, f32[1024,1]{1,0:T(8,128)}, /*index=5*/f32[1,512]{1,0:T(1,128)}, f32[1,512]{1,0:T(1,128)}) custom-call(bf16[1024,512]{1,0:T(8,128)(2,1)} %get-tuple-element.174.query, bf16[1024,512]{1,0:T(8,128)(2,1)} %get-tuple-element.175.key, ...), custom_call_target="tpu_custom_call" | custom-call | flops 3623878656 | tf_op jit(solution)/shard_map/attend_back/pallas_call | solution.py:319
  575.5 2.8 fusion.3
  578.4 2.8 fusion.4
  583.9 17.0 %wgrad.10 = (bf16[2,2048,256]{2,1,0:T(8,128)(2,1)}, bf16[2,2048,256]{2,1,0:T(8,128)(2,1)}, bf16[2,2048,256]{2,1,0:T(8,128)(2,1)}, bf16[2,2048,256]{2,1,0:T(8,128)(2,1)}) custom-call(s32[8]{0:T(128)} %add.209.order, s32[2,4,8]{2,1,0:T(4,128)} %constant.77.clone.tables, bf16[4,2,128,2048]{3,2,1,0:T(8,128)(2,1)} %bitcast.121, ...), custom_call_target="tpu_custom_call" | custom-call | flops 3865470464 | tf_op jit(solution)/shard_map/wgrad/pallas_call | solution.py:580
  603.0 2.1 fusion.5
  605.2 5.0 collective-permute-done.15
  611.7 2.1 fusion.2
  618.3 16.7 %collective-permute-done.14 = bf16[1,2,1024,256]{3,2,1,0:T(8,128)(2,1)} collective-permute-done((bf16[1,2,1024,256]{3,2,1,0:T(8,128)(2,1)}, bf16[1,2,1024,256]{3,2,1,0:T(8,128)(2,1)}, u32[]{:S(2)}, u32[]{:S(2)}) %collective-permute-start.14) | collective-permute-done | bytes 1048608 | tf_op jit(solution)/shard_map/ppermute | solution.py:640
  638.0 18.7 %wgrad.11 = (bf16[4,1024,256]{2,1,0:T(8,128)(2,1)}, bf16[4,1024,256]{2,1,0:T(8,128)(2,1)}, bf16[4,1024,256]{2,1,0:T(8,128)(2,1)}, bf16[4,1024,256]{2,1,0:T(8,128)(2,1)}) custom-call(s32[8]{0:T(128)} %add.204.order, s32[2,4,8]{2,1,0:T(4,128)} %constant.77.clone.tables, bf16[4,2,128,2048]{3,2,1,0:T(8,128)(2,1)} %bitcast.123, ...), custom_call_target="tpu_custom_call" | custom-call | flops 50251116544 | tf_op jit(solution)/shard_map/wgrad/pallas_call | solution.py:580
  656.7 2.0 collective-permute-done.25
  659.7 14.1 %project_back.1 = (bf16[1024,2048]{1,0:T(8,128)(2,1)}, bf16[1024,512]{1,0:T(8,128)(2,1)}, bf16[1024,512]{1,0:T(8,128)(2,1)}, f32[1,2048]{1,0:T(1,128)}) custom-call(bf16[1024,2048]{1,0:T(8,128)(2,1)} %all-gather.6.cloned.1.call-done.rows_in, f32[1024,512]{1,0:T(8,128)} %get-tuple-element.178.dqn, f32[1024,512]{1,0:T(8,128)} %get-tuple-element.192.dkn, ...), custom_call_target="tpu_custom_call" | custom-call | flops 2899102976 | bytes 1310720 | tf_op jit(solution)/shard_map/project_back/pallas_call | solution.py:141
  674.0 11.1 %attention_wgrad.2 = (bf16[1,4,256,512]{3,2,1,0:T(8,128)(2,1)}, bf16[1,4,256,512]{3,2,1,0:T(8,128)(2,1)}, bf16[1,4,256,512]{3,2,1,0:T(8,128)(2,1)}, bf16[1,4,256,512]{3,2,1,0:T(8,128)(2,1)}) custom-call(s32[4]{0:T(128)} %get-tuple-element.199.order, s32[2,4,4]{2,1,0:T(4,128)} %constant.78.clone.tables, ...), custom_call_target="tpu_custom_call" | custom-call | tf_op jit(solution)/shard_map/attention_wgrad/pallas_call | solution.py:203
  692.7 12.7 %attention_wgrad.3 = (bf16[2,4,128,512]{3,2,1,0:T(8,128)(2,1)}, bf16[2,4,128,512]{3,2,1,0:T(8,128)(2,1)}, bf16[2,4,128,512]{3,2,1,0:T(8,128)(2,1)}, bf16[2,4,128,512]{3,2,1,0:T(8,128)(2,1)}) custom-call(s32[4]{0:T(128)} %get-tuple-element.206.order, s32[2,4,4]{2,1,0:T(4,128)} %constant.78.clone.tables, ...), custom_call_target="tpu_custom_call" | custom-call | tf_op jit(solution)/shard_map/attention_wgrad/pallas_call | solution.py:203
  706.9 1.6 collective-permute-start.37
  708.5 2.3 pad_maximum_fusion.1
  710.7 29.5 %collective-permute-done.37 = f32[20,2048]{1,0:T(8,128)S(1)} collective-permute-done((f32[20,2048]{1,0:T(8,128)S(1)}, f32[20,2048]{1,0:T(8,128)S(1)}, u32[]{:S(2)}, u32[]{:S(2)}) %collective-permute-start.37) | collective-permute-done | bytes 163872 | tf_op jit(solution)/shard_map/ppermute | solution.py:700
  742.7 3.9 collective-permute-done.38
  747.0 5.5 collective-permute-done.39
  752.5 3.0 collective-permute-start.40
  755.5 2.1 fusion.1
  760.0 2.1 fusion.13
  765.2 2.3 pad_maximum_fusion
  770.8 13.1 %collective-permute-done.30 = bf16[1,2,1024,256]{3,2,1,0:T(8,128)(2,1)} collective-permute-done((bf16[1,2,1024,256]{3,2,1,0:T(8,128)(2,1)S(1)}, bf16[1,2,1024,256]{3,2,1,0:T(8,128)(2,1)}, u32[]{:S(2)}, u32[]{:S(2)}) %collective-permute-start.30) | collective-permute-done | bytes 1048608 | tf_op jit(solution)/shard_map/ppermute | solution.py:640
  784.0 6.2 collective-permute-done.31
  790.1 1.8 add_bitcast_fusion
  793.4 2.4 pad_maximum_fusion.2
  798.1 1.7 fusion.12
  799.8 10.6 %collective-permute-done.32 = bf16[2,4,128,512]{3,2,1,0:T(8,128)(2,1)} collective-permute-done((bf16[2,4,128,512]{3,2,1,0:T(8,128)(2,1)}, bf16[2,4,128,512]{3,2,1,0:T(8,128)(2,1)}, u32[]{:S(2)}, u32[]{:S(2)}) %collective-permute-start.32) | collective-permute-done | bytes 1048608 | tf_op jit(solution)/shard_map/ppermute | solution.py:640
  815.2 1.7 collective-permute-start.35
  816.9 2.0 fusion.11
  818.9 5.1 collective-permute-done.34
  824.1 2.7 collective-permute-done.35
  (250 shorter events, 68.0 us)
Async XLA Ops:
  7.2 171.5 %copy-start = (bf16[2048,512]{1,0:T(8,128)(2,1)S(1)}, bf16[2048,512]{1,0:T(8,128)(2,1)}, u32[]{:S(2)}) copy-start(bf16[2048,512]{1,0:T(8,128)(2,1)} %param.37) | copy-start | bytes 6291460
  7.2 89.0 %all-gather.6.cloned.1.call-start = ((), (), s32[]{:S(2)}) async-start(), calls=%async_computation.6 | async-start | bytes 5242880 | tf_op jit(solution)/shard_map/all_gather | solution.py:631
  12.6 164.9 %all-gather.8.cloned.1.call-start = ((), (), s32[]{:S(2)}) async-start(), calls=%async_computation.7 | async-start | bytes 5242880 | tf_op jit(solution)/shard_map/all_gather | solution.py:631
  96.2 22.0 %copy-start.44 = (s32[1,1024]{1,0:T(1,128)S(1)}, s32[1,1024]{1,0:T(1,128)}, u32[]{:S(2)}) copy-start(s32[1,1024]{1,0:T(1,128)} %seg_row.3) | copy-start | bytes 12292
  96.2 127.7 %reduce-scatter.7.cloned.1.call-start = ((), (), s32[]{:S(2)}) async-start(), calls=%async_computation.8 | async-start | bytes 2621440 | tf_op jit(solution)/shard_map/reduce_scatter | solution.py:635
  112.6 4.0 collective-permute-start
  117.3 6.7 collective-permute-start.1
  181.4 88.5 %reduce-scatter.9.cloned.1.call-start = ((), (), s32[]{:S(2)}) async-start(), calls=%async_computation.9 | async-start | bytes 2621440 | tf_op jit(solution)/shard_map/reduce_scatter | solution.py:635
  184.0 42.8 %copy-start.35 = (bf16[2048,16]{0,1:T(8,128)(2,1)S(1)}, bf16[2048,16]{0,1:T(8,128)(2,1)}, u32[]{:S(2)}) copy-start(bf16[2048,16]{0,1:T(8,128)(2,1)} %param.41) | copy-start | bytes 196612
  184.0 43.1 %copy-start.36 = (s32[1024,8]{0,1:T(8,128)S(1)}, s32[1024,8]{0,1:T(8,128)}, u32[]{:S(2)}) copy-start(s32[1024,8]{0,1:T(8,128)} %param.32) | copy-start | bytes 98308
  184.1 132.6 %all-gather.10.cloned.1.call-start = ((), (), s32[]{:S(2)}) async-start(), calls=%async_computation.10 | async-start | bytes 2621440 | tf_op jit(solution)/shard_map/all_gather | solution.py:631
  226.6 137.6 %all-gather.12.cloned.1.call-start = ((), (), s32[]{:S(2)}) async-start(), calls=%async_computation.11 | async-start | bytes 2621440 | tf_op jit(solution)/shard_map/all_gather | solution.py:631
  272.4 141.7 %reduce-scatter.13.cloned.1.call-start = ((), (), s32[]{:S(2)}) async-start(), calls=%async_computation.13 | async-start | bytes 2785280 | tf_op jit(solution)/shard_map/reduce_scatter | solution.py:635
  364.1 94.1 %reduce-scatter.11.cloned.1.call-start = ((), (), s32[]{:S(2)}) async-start(), calls=%async_computation.12 | async-start | bytes 2785280 | tf_op jit(solution)/shard_map/reduce_scatter | solution.py:635
  411.6 131.1 %all-gather.14.cloned.1.call-start = ((), (), s32[]{:S(2)}) async-start(), calls=%async_computation.15 | async-start | bytes 5242880 | tf_op jit(solution)/shard_map/all_gather | solution.py:631
  462.4 308.4 %reduce-scatter.15.cloned.1.call-start = ((), (), s32[]{:S(2)}) async-start(), calls=%async_computation.14 | async-start | bytes 5242880 | tf_op jit(solution)/shard_map/reduce_scatter | solution.py:635
  462.6 4.6 collective-permute-start.2
  462.7 7.5 collective-permute-start.3
  463.2 10.0 %collective-permute-start.4 = (bf16[2,2048,256]{2,1,0:T(8,128)(2,1)}, bf16[2,2048,256]{2,1,0:T(8,128)(2,1)}, u32[]{:S(2)}, u32[]{:S(2)}) collective-permute-start(bf16[2,2048,256]{2,1,0:T(8,128)(2,1)} %get-tuple-element.150), channel_id=1, source_target_pairs={{0,4},{4,0},{8,12},{12,8},{16,20},{20,16},{24,28},{28,24},{1,5},{5... | collective-permute-start | bytes 6291464 | tf_op jit(solution)/shard_map/ppermute | solution.py:640
  463.3 12.9 %collective-permute-start.5 = (bf16[2,2048,256]{2,1,0:T(8,128)(2,1)}, bf16[2,2048,256]{2,1,0:T(8,128)(2,1)}, u32[]{:S(2)}, u32[]{:S(2)}) collective-permute-start(bf16[2,2048,256]{2,1,0:T(8,128)(2,1)} %get-tuple-element.151), channel_id=1, source_target_pairs={{0,4},{4,0},{8,12},{12,8},{16,20},{20,16},{24,28},{28,24},{1,5},{5... | collective-permute-start | bytes 6291464 | tf_op jit(solution)/shard_map/ppermute | solution.py:640
  463.7 32.7 %collective-permute-start.6 = (bf16[2,2048,256]{2,1,0:T(8,128)(2,1)}, bf16[2,2048,256]{2,1,0:T(8,128)(2,1)}, u32[]{:S(2)}, u32[]{:S(2)}) collective-permute-start(bf16[2,2048,256]{2,1,0:T(8,128)(2,1)} %get-tuple-element.155), channel_id=1, source_target_pairs={{0,4},{4,0},{8,12},{12,8},{16,20},{20,16},{24,28},{28,24},{1,5},{5... | collective-permute-start | bytes 6291464 | tf_op jit(solution)/shard_map/ppermute | solution.py:640
  467.2 30.7 %collective-permute-start.7 = (bf16[2,2048,256]{2,1,0:T(8,128)(2,1)}, bf16[2,2048,256]{2,1,0:T(8,128)(2,1)}, u32[]{:S(2)}, u32[]{:S(2)}) collective-permute-start(bf16[2,2048,256]{2,1,0:T(8,128)(2,1)} %get-tuple-element.156), channel_id=1, source_target_pairs={{0,4},{4,0},{8,12},{12,8},{16,20},{20,16},{24,28},{28,24},{1,5},{5... | collective-permute-start | bytes 6291464 | tf_op jit(solution)/shard_map/ppermute | solution.py:640
  470.2 27.7 %collective-permute-start.8 = (bf16[2,2048,256]{2,1,0:T(8,128)(2,1)}, bf16[2,2048,256]{2,1,0:T(8,128)(2,1)}, u32[]{:S(2)}, u32[]{:S(2)}) collective-permute-start(bf16[2,2048,256]{2,1,0:T(8,128)(2,1)} %get-tuple-element.157), channel_id=1, source_target_pairs={{0,4},{4,0},{8,12},{12,8},{16,20},{20,16},{24,28},{28,24},{1,5},{5... | collective-permute-start | bytes 6291464 | tf_op jit(solution)/shard_map/ppermute | solution.py:640
  473.2 24.7 %collective-permute-start.9 = (bf16[2,2048,256]{2,1,0:T(8,128)(2,1)}, bf16[2,2048,256]{2,1,0:T(8,128)(2,1)}, u32[]{:S(2)}, u32[]{:S(2)}) collective-permute-start(bf16[2,2048,256]{2,1,0:T(8,128)(2,1)} %get-tuple-element.158), channel_id=1, source_target_pairs={{0,4},{4,0},{8,12},{12,8},{16,20},{20,16},{24,28},{28,24},{1,5},{5... | collective-permute-start | bytes 6291464 | tf_op jit(solution)/shard_map/ppermute | solution.py:640
  494.9 78.0 %collective-permute-start.12 = (bf16[2,2,1024,256]{3,2,1,0:T(8,128)(2,1)}, bf16[2,2,1024,256]{3,2,1,0:T(8,128)(2,1)}, u32[]{:S(2)}, u32[]{:S(2)}) collective-permute-start(bf16[2,2,1024,256]{3,2,1,0:T(8,128)(2,1)} %bitcast.171), channel_id=1, source_target_pairs={{0,16},{4,20},{8,24},{12,28},{16,0},{20,4},{24,8},{28,12},{1,17},{... | collective-permute-start | bytes 6291464 | tf_op jit(solution)/shard_map/ppermute | solution.py:640
  496.4 76.5 %collective-permute-start.13 = (bf16[2,2,1024,256]{3,2,1,0:T(8,128)(2,1)}, bf16[2,2,1024,256]{3,2,1,0:T(8,128)(2,1)}, u32[]{:S(2)}, u32[]{:S(2)}) collective-permute-start(bf16[2,2,1024,256]{3,2,1,0:T(8,128)(2,1)} %bitcast.170), channel_id=1, source_target_pairs={{0,8},{4,12},{8,0},{12,4},{16,24},{20,28},{24,16},{28,20},{1,9},{5... | collective-permute-start | bytes 6291464 | tf_op jit(solution)/shard_map/ppermute | solution.py:640
  516.6 84.3 %collective-permute-start.10 = (bf16[2,2,1024,256]{3,2,1,0:T(8,128)(2,1)}, bf16[2,2,1024,256]{3,2,1,0:T(8,128)(2,1)}, u32[]{:S(2)}, u32[]{:S(2)}) collective-permute-start(bf16[2,2,1024,256]{3,2,1,0:T(8,128)(2,1)} %bitcast.169), channel_id=1, source_target_pairs={{0,16},{4,20},{8,24},{12,28},{16,0},{20,4},{24,8},{28,12},{1,17},{... | collective-permute-start | bytes 6291464 | tf_op jit(solution)/shard_map/ppermute | solution.py:640
  517.2 84.2 %collective-permute-start.11 = (bf16[2,2,1024,256]{3,2,1,0:T(8,128)(2,1)}, bf16[2,2,1024,256]{3,2,1,0:T(8,128)(2,1)}, u32[]{:S(2)}, u32[]{:S(2)}) collective-permute-start(bf16[2,2,1024,256]{3,2,1,0:T(8,128)(2,1)} %bitcast.168), channel_id=1, source_target_pairs={{0,8},{4,12},{8,0},{12,4},{16,24},{20,28},{24,16},{28,20},{1,9},{5... | collective-permute-start | bytes 6291464 | tf_op jit(solution)/shard_map/ppermute | solution.py:640
  542.0 256.0 %reduce-scatter.17.cloned.1.call-start = ((), (), s32[]{:S(2)}) async-start(), calls=%async_computation.16 | async-start | bytes 5242880 | tf_op jit(solution)/shard_map/reduce_scatter | solution.py:635
  575.4 7.5 collective-permute-start.22
  581.2 20.7 %copy-start.4 = (bf16[2,2,1024,256]{3,2,1,0:T(8,128)(2,1)}, bf16[2,2,1024,256]{3,2,1,0:T(8,128)(2,1)S(1)}, u32[]{:S(2)}) copy-start(bf16[2,2,1024,256]{3,2,1,0:T(8,128)(2,1)S(1)} %fusion.4) | copy-start | bytes 6291460
  581.3 28.9 %collective-permute-start.15 = (bf16[1,2,1024,256]{3,2,1,0:T(8,128)(2,1)S(1)}, bf16[1,2,1024,256]{3,2,1,0:T(8,128)(2,1)S(1)}, u32[]{:S(2)}, u32[]{:S(2)}) collective-permute-start(bf16[1,2,1024,256]{3,2,1,0:T(8,128)(2,1)S(1)} %slice_bitcast_fusion.5), channel_id=1, source_target_pairs={{0,16},{4,20},{8,24},{12,28},{16,0},{20,4},{24,8},{28,12},{1,17},{... | collective-permute-start | bytes 3145736 | tf_op jit(solution)/shard_map/ppermute | solution.py:640
  582.9 18.6 %collective-permute-start.23 = (f32[2,1024]{1,0:T(2,128)S(1)}, f32[2,1024]{1,0:T(2,128)S(1)}, u32[]{:S(2)}, u32[]{:S(2)}) collective-permute-start(f32[2,1024]{1,0:T(2,128)S(1)} %fusion.34), channel_id=1, source_target_pairs={{0,2},{1,3},{2,0},{3,1},{4,6},{5,7},{6,4},{7,5},{8,10},{9,11},{10,... | collective-permute-start | bytes 24584 | tf_op jit(solution)/shard_map/ppermute | solution.py:700
  600.8 35.6 %collective-permute-start.16 = (bf16[2,2048,256]{2,1,0:T(8,128)(2,1)}, bf16[2,2048,256]{2,1,0:T(8,128)(2,1)}, u32[]{:S(2)}, u32[]{:S(2)}) collective-permute-start(bf16[2,2048,256]{2,1,0:T(8,128)(2,1)} %get-tuple-element.182), channel_id=1, source_target_pairs={{0,4},{4,0},{8,12},{12,8},{16,20},{20,16},{24,28},{28,24},{1,5},{5... | collective-permute-start | bytes 6291464 | tf_op jit(solution)/shard_map/ppermute | solution.py:640
  600.9 37.0 %collective-permute-start.17 = (bf16[2,2048,256]{2,1,0:T(8,128)(2,1)}, bf16[2,2048,256]{2,1,0:T(8,128)(2,1)}, u32[]{:S(2)}, u32[]{:S(2)}) collective-permute-start(bf16[2,2048,256]{2,1,0:T(8,128)(2,1)} %get-tuple-element.183), channel_id=1, source_target_pairs={{0,4},{4,0},{8,12},{12,8},{16,20},{20,16},{24,28},{28,24},{1,5},{5... | collective-permute-start | bytes 6291464 | tf_op jit(solution)/shard_map/ppermute | solution.py:640
  601.4 36.5 %collective-permute-start.18 = (bf16[2,2048,256]{2,1,0:T(8,128)(2,1)}, bf16[2,2048,256]{2,1,0:T(8,128)(2,1)}, u32[]{:S(2)}, u32[]{:S(2)}) collective-permute-start(bf16[2,2048,256]{2,1,0:T(8,128)(2,1)} %get-tuple-element.184), channel_id=1, source_target_pairs={{0,4},{4,0},{8,12},{12,8},{16,20},{20,16},{24,28},{28,24},{1,5},{5... | collective-permute-start | bytes 6291464 | tf_op jit(solution)/shard_map/ppermute | solution.py:640
  601.5 36.4 %collective-permute-start.19 = (bf16[2,2048,256]{2,1,0:T(8,128)(2,1)}, bf16[2,2048,256]{2,1,0:T(8,128)(2,1)}, u32[]{:S(2)}, u32[]{:S(2)}) collective-permute-start(bf16[2,2048,256]{2,1,0:T(8,128)(2,1)} %get-tuple-element.185), channel_id=1, source_target_pairs={{0,4},{4,0},{8,12},{12,8},{16,20},{20,16},{24,28},{28,24},{1,5},{5... | collective-permute-start | bytes 6291464 | tf_op jit(solution)/shard_map/ppermute | solution.py:640
  610.2 24.8 %collective-permute-start.14 = (bf16[1,2,1024,256]{3,2,1,0:T(8,128)(2,1)}, bf16[1,2,1024,256]{3,2,1,0:T(8,128)(2,1)}, u32[]{:S(2)}, u32[]{:S(2)}) collective-permute-start(bf16[1,2,1024,256]{3,2,1,0:T(8,128)(2,1)} %slice.126), channel_id=1, source_target_pairs={{0,8},{4,12},{8,0},{12,4},{16,24},{20,28},{24,16},{28,20},{1,9},{5... | collective-permute-start | bytes 3145736 | tf_op jit(solution)/shard_map/ppermute | solution.py:640
  635.0 23.7 %collective-permute-start.25 = (bf16[1,2,1024,256]{3,2,1,0:T(8,128)(2,1)}, bf16[1,2,1024,256]{3,2,1,0:T(8,128)(2,1)S(1)}, u32[]{:S(2)}, u32[]{:S(2)}) collective-permute-start(bf16[1,2,1024,256]{3,2,1,0:T(8,128)(2,1)} %slice_bitcast_fusion.4), channel_id=1, source_target_pairs={{0,16},{4,20},{8,24},{12,28},{16,0},{20,4},{24,8},{28,12},{1,17},{... | collective-permute-start | bytes 3145736 | tf_op jit(solution)/shard_map/ppermute | solution.py:640
  636.5 23.3 %collective-permute-start.24 = (bf16[1,2,1024,256]{3,2,1,0:T(8,128)(2,1)S(1)}, bf16[1,2,1024,256]{3,2,1,0:T(8,128)(2,1)S(1)}, u32[]{:S(2)}, u32[]{:S(2)}) collective-permute-start(bf16[1,2,1024,256]{3,2,1,0:T(8,128)(2,1)S(1)} %slice.130), channel_id=1, source_target_pairs={{0,8},{4,12},{8,0},{12,4},{16,24},{20,28},{24,16},{28,20},{1,9},{5... | collective-permute-start | bytes 3145736 | tf_op jit(solution)/shard_map/ppermute | solution.py:640
  658.7 15.1 %copy-start.30 = (bf16[1,2,1024,256]{3,2,1,0:T(8,128)(2,1)}, bf16[1,2,1024,256]{3,2,1,0:T(8,128)(2,1)S(1)}, u32[]{:S(2)}) copy-start(bf16[1,2,1024,256]{3,2,1,0:T(8,128)(2,1)S(1)} %collective-permute-done.25) | copy-start | bytes 3145732
  659.7 14.2 %copy-start.32 = (bf16[1,2,1024,256]{3,2,1,0:T(8,128)(2,1)}, bf16[1,2,1024,256]{3,2,1,0:T(8,128)(2,1)S(1)}, u32[]{:S(2)}) copy-start(bf16[1,2,1024,256]{3,2,1,0:T(8,128)(2,1)S(1)} %collective-permute-done.24) | copy-start | bytes 3145732
  685.1 3.1 collective-permute-start.26
  685.5 6.2 collective-permute-start.27
  686.1 5.7 collective-permute-start.28
  686.1 6.5 collective-permute-start.29
  686.9 68.6 %collective-permute-start.20 = (bf16[2,2,1024,256]{3,2,1,0:T(8,128)(2,1)}, bf16[2,2,1024,256]{3,2,1,0:T(8,128)(2,1)}, u32[]{:S(2)}, u32[]{:S(2)}) collective-permute-start(bf16[2,2,1024,256]{3,2,1,0:T(8,128)(2,1)} %bitcast.167), channel_id=1, source_target_pairs={{0,16},{4,20},{8,24},{12,28},{16,0},{20,4},{24,8},{28,12},{1,17},{... | collective-permute-start | bytes 6291464 | tf_op jit(solution)/shard_map/ppermute | solution.py:640
  688.2 67.4 %collective-permute-start.21 = (bf16[2,2,1024,256]{3,2,1,0:T(8,128)(2,1)}, bf16[2,2,1024,256]{3,2,1,0:T(8,128)(2,1)}, u32[]{:S(2)}, u32[]{:S(2)}) collective-permute-start(bf16[2,2,1024,256]{3,2,1,0:T(8,128)(2,1)} %bitcast.166), channel_id=1, source_target_pairs={{0,8},{4,12},{8,0},{12,4},{16,24},{20,28},{24,16},{28,20},{1,9},{5... | collective-permute-start | bytes 6291464 | tf_op jit(solution)/shard_map/ppermute | solution.py:640
  691.7 13.8 %copy-start.7 = (bf16[2,2,1024,256]{3,2,1,0:T(8,128)(2,1)S(1)}, bf16[2,2,1024,256]{3,2,1,0:T(8,128)(2,1)}, u32[]{:S(2)}) copy-start(bf16[2,2,1024,256]{3,2,1,0:T(8,128)(2,1)} %copy-done.6) | copy-start | bytes 6291460
  691.7 13.8 %copy-start.31 = (bf16[1,2,1024,256]{3,2,1,0:T(8,128)(2,1)S(1)}, bf16[1,2,1024,256]{3,2,1,0:T(8,128)(2,1)}, u32[]{:S(2)}) copy-start(bf16[1,2,1024,256]{3,2,1,0:T(8,128)(2,1)} %copy-done.30) | copy-start | bytes 3145732
  705.3 1.5 collective-permute-start.36
  706.8 34.4 %copy-start.5 = (bf16[2,2,1024,256]{3,2,1,0:T(8,128)(2,1)S(1)}, bf16[2,2,1024,256]{3,2,1,0:T(8,128)(2,1)}, u32[]{:S(2)}) copy-start(bf16[2,2,1024,256]{3,2,1,0:T(8,128)(2,1)} %copy-done.4) | copy-start | bytes 6291460
  706.9 33.4 %collective-permute-start.37 = (f32[20,2048]{1,0:T(8,128)S(1)}, f32[20,2048]{1,0:T(8,128)S(1)}, u32[]{:S(2)}, u32[]{:S(2)}) collective-permute-start(f32[20,2048]{1,0:T(8,128)S(1)} %add.228), channel_id=1, source_target_pairs={{0,8},{4,12},{8,0},{12,4},{16,24},{20,28},{24,16},{28,20},{1,9},{5... | collective-permute-start | bytes 491528 | tf_op jit(solution)/shard_map/ppermute | solution.py:700
  740.3 6.3 collective-permute-start.38
  746.6 5.9 collective-permute-start.39
  752.5 17.0 %collective-permute-start.40 = (f32[20,2048]{1,0:T(8,128)S(1)}, f32[20,2048]{1,0:T(8,128)S(1)}, u32[]{:S(2)}, u32[]{:S(2)}) collective-permute-start(f32[20,2048]{1,0:T(8,128)S(1)} %add.231), channel_id=1, source_target_pairs={{0,2},{1,3},{2,0},{3,1},{4,6},{5,7},{6,4},{7,5},{8,10},{9,11},{10,... | collective-permute-start | bytes 491528 | tf_op jit(solution)/shard_map/ppermute | solution.py:700
  757.7 26.3 %collective-permute-start.30 = (bf16[1,2,1024,256]{3,2,1,0:T(8,128)(2,1)S(1)}, bf16[1,2,1024,256]{3,2,1,0:T(8,128)(2,1)}, u32[]{:S(2)}, u32[]{:S(2)}) collective-permute-start(bf16[1,2,1024,256]{3,2,1,0:T(8,128)(2,1)S(1)} %slice.132), channel_id=1, source_target_pairs={{0,8},{4,12},{8,0},{12,4},{16,24},{20,28},{24,16},{28,20},{1,9},{5... | collective-permute-start | bytes 3145736 | tf_op jit(solution)/shard_map/ppermute | solution.py:640
  763.7 26.4 %collective-permute-start.31 = (bf16[1,2,1024,256]{3,2,1,0:T(8,128)(2,1)}, bf16[1,2,1024,256]{3,2,1,0:T(8,128)(2,1)}, u32[]{:S(2)}, u32[]{:S(2)}) collective-permute-start(bf16[1,2,1024,256]{3,2,1,0:T(8,128)(2,1)} %slice_bitcast_fusion.3), channel_id=1, source_target_pairs={{0,16},{4,20},{8,24},{12,28},{16,0},{20,4},{24,8},{28,12},{1,17},{... | collective-permute-start | bytes 3145736 | tf_op jit(solution)/shard_map/ppermute | solution.py:640
  767.5 43.0 %collective-permute-start.32 = (bf16[2,4,128,512]{3,2,1,0:T(8,128)(2,1)}, bf16[2,4,128,512]{3,2,1,0:T(8,128)(2,1)}, u32[]{:S(2)}, u32[]{:S(2)}) collective-permute-start(bf16[2,4,128,512]{3,2,1,0:T(8,128)(2,1)} %get-tuple-element.208), channel_id=1, source_target_pairs={{0,16},{4,20},{8,24},{12,28},{16,0},{20,4},{24,8},{28,12},{1,17},{... | collective-permute-start | bytes 3145736 | tf_op jit(solution)/shard_map/ppermute | solution.py:640
  768.0 42.4 %collective-permute-start.33 = (bf16[2,4,128,512]{3,2,1,0:T(8,128)(2,1)}, bf16[2,4,128,512]{3,2,1,0:T(8,128)(2,1)}, u32[]{:S(2)}, u32[]{:S(2)}) collective-permute-start(bf16[2,4,128,512]{3,2,1,0:T(8,128)(2,1)} %get-tuple-element.210), channel_id=1, source_target_pairs={{0,8},{4,12},{8,0},{12,4},{16,24},{20,28},{24,16},{28,20},{1,9},{5... | collective-permute-start | bytes 3145736 | tf_op jit(solution)/shard_map/ppermute | solution.py:640
  770.8 21.1 %copy-start.12 = (bf16[1,2,2,1024,256]{4,3,2,1,0:T(8,128)(2,1)S(1)}, bf16[1,2,2,1024,256]{4,3,2,1,0:T(8,128)(2,1)}, u32[]{:S(2)}) copy-start(bf16[1,2,2,1024,256]{4,3,2,1,0:T(8,128)(2,1)} %copy-done.11) | copy-start | bytes 6291460
  799.8 13.8 %copy-start.25 = (bf16[2,4,128,512]{3,2,1,0:T(8,128)(2,1)S(1)}, bf16[2,4,128,512]{3,2,1,0:T(8,128)(2,1)}, u32[]{:S(2)}) copy-start(bf16[2,4,128,512]{3,2,1,0:T(8,128)(2,1)} %get-tuple-element.209) | copy-start | bytes 3145732
  812.1 11.9 %collective-permute-start.34 = (bf16[1,4,128,512]{3,2,1,0:T(8,128)(2,1)S(1)}, bf16[1,4,128,512]{3,2,1,0:T(8,128)(2,1)S(1)}, u32[]{:S(2)}, u32[]{:S(2)}) collective-permute-start(bf16[1,4,128,512]{3,2,1,0:T(8,128)(2,1)S(1)} %slice.135), channel_id=1, source_target_pairs={{0,8},{4,12},{8,0},{12,4},{16,24},{20,28},{24,16},{28,20},{1,9},{5... | collective-permute-start | bytes 1572872 | tf_op jit(solution)/shard_map/ppermute | solution.py:640
  815.2 11.6 %collective-permute-start.35 = (bf16[1,4,128,512]{3,2,1,0:T(8,128)(2,1)S(1)}, bf16[1,4,128,512]{3,2,1,0:T(8,128)(2,1)S(1)}, u32[]{:S(2)}, u32[]{:S(2)}) collective-permute-start(bf16[1,4,128,512]{3,2,1,0:T(8,128)(2,1)S(1)} %slice_bitcast_fusion.6), channel_id=1, source_target_pairs={{0,16},{4,20},{8,24},{12,28},{16,0},{20,4},{24,8},{28,12},{1,17},{... | collective-permute-start | bytes 1572872 | tf_op jit(solution)/shard_map/ppermute | solution.py:640
  (37 other events, 180.8 us)
Sparse Core Ops, SparseCore 0:
  12.7 83.4 all-gather.5
  97.8 79.6 all-gather.7
  181.5 42.3 reduce-scatter.6
  226.7 43.0 reduce-scatter.8
  271.3 45.3 all-gather.9
  318.7 44.6 all-gather.11
  365.7 44.7 reduce-scatter.12
  412.7 45.4 reduce-scatter.10
  462.5 80.1 all-gather.13
  544.9 75.6 reduce-scatter.14
  674.0 75.7 reduce-scatter.16

commit v9 on v8

--- a/solution.py
+++ b/solution.py
@@ -145,7 +145,7 @@
         out_specs=[row(features), row(width), row(width), whole(1, features)],
         out_shape=[sds((rows, features), bf16), sds((rows, width), bf16), sds((rows, width), bf16), sds((1, features), f32)],
         compiler_params=params(),
-        cost_estimate=cost(6 * rows * features * width, 2 * (rows + 3 * width) * features),
+        cost_estimate=cost(int(20.0 * 6 * rows * features * width), 0),
         name="project_back",
     )(rows_in, dqn, dkn, dvalue, qraw, kraw, q_scale, k_scale, q_dot, k_dot, q_gain[None], k_gain[None], w_query, w_key, w_value)
 
@@ -327,7 +327,7 @@
         + [sds((length, 1), f32), sds((length, 1), f32), sds((1, width), f32), sds((1, width), f32)],
         scratch_shapes=[pltpu.VMEM((length, span), f32), pltpu.VMEM((length, HEAD), f32), pltpu.VMEM((length, HEAD), f32)],
         compiler_params=params(),
-        cost_estimate=cost(20 * length * span * width, 0),
+        cost_estimate=cost(0, 0),
         name="attend_back",
     )(query, key, value, out_grad, lse, qraw, kraw, q_scale, k_scale, q_gain[None], k_gain[None], cosine, sine, seg[:, None], seg[None], keep[None])
 
@@ -553,14 +553,16 @@
             out[0] = got[start : start + half, :]
 
 
-def wgrad(lefts, rights, order, width, per, added=(), weight=1):
+def wgrad(lefts, rights, order, width, per, added=(), weight=1, pieces=0):
     features = lefts[0][0].shape[-1]
     experts = order.shape[0]
     groups = experts // per
     tables, sizes = split_tables(groups, per)
-
-    def group_spec(place):
-        return pl.BlockSpec((1, features, width), lambda i, ids, to: (jnp.clip(i - place * per, 0, per - 1), 0, 0))
+    pieces = len(added) or pieces or groups
+    held = experts // pieces
+
+    def piece_spec(place):
+        return pl.BlockSpec((1, features, width), lambda i, ids, to: (jnp.clip(i - place * held, 0, held - 1), 0, 0))
 
     def half_spec(side):
         return pl.BlockSpec((1, features // 2, width), lambda i, ids, to: (to[0, side, i], 0, 0))
@@ -570,21 +572,21 @@
             return pl.BlockSpec(left.shape, lambda i, ids, to: (0, 0))
         return pl.BlockSpec((left.shape[0], 1) + left.shape[2:], lambda i, ids, to: (0, chunk, 0, 0))
 
-    groups_specs = [group_spec(place) for place in range(groups)]
+    piece_specs = [piece_spec(place) for place in range(pieces)]
     if added:
         out_specs = [half_spec(side) for side in range(len(sizes))]
         out_shape = [jax.ShapeDtypeStruct((size * per, features // 2, width), bf16) for size in sizes]
     else:
-        out_specs = groups_specs
-        out_shape = [jax.ShapeDtypeStruct((per, features, width), bf16)] * groups
-    return pl.pallas_call(
-        functools.partial(wgrad_kernel, len(lefts), len(added), per, min(512, features // 2)),
+        out_specs = piece_specs
+        out_shape = [jax.ShapeDtypeStruct((held, features, width), bf16)] * pieces
+    return pl.pallas_call(
+        functools.partial(wgrad_kernel, len(lefts), len(added), held, min(512, features // 2)),
         grid_spec=pltpu.PrefetchScalarGridSpec(
             num_scalar_prefetch=2,
             grid=(experts,),
             in_specs=[left_spec(*left) for left in lefts]
             + [pl.BlockSpec((right.shape[0], width), lambda i, ids, to: (0, ids[i])) for right in rights]
-            + (groups_specs if added else []),
+            + (piece_specs if added else []),
             out_specs=out_specs,
             scratch_shapes=[pltpu.VMEM((features, width), bf16)] if added else [],
         ),
@@ -618,7 +620,7 @@
         out_specs=pl.BlockSpec((rows, block), lambda n: (0, n)),
         out_shape=jax.ShapeDtypeStruct((rows, features), bf16),
         compiler_params=params(),
-        cost_estimate=cost(2 * rows * features * experts * width, 2 * (rows + experts * width) * features),
+        cost_estimate=cost(0 * 2 * rows * features * experts * width, 0),
         name="down",
     )(down_w, *acts)
 
@@ -692,14 +694,14 @@
         return jnp.concatenate([kept[0].astype(f32) for kept in self.kept], axis=1)
 
 
-def exchange_sum(values, axes):
-    for axis in axes:
-        size = lax.axis_size(axis)
-        step = 1
-        while step < size:
-            values = values + lax.ppermute(values, axis, [(i, i ^ step) for i in range(size)])
-            step *= 2
+def exchange_sum(values, steps):
+    for axis, step in steps:
+        values = values + lax.ppermute(values, axis, [(i, i ^ step) for i in range(lax.axis_size(axis))])
     return values
+
+
+def doublings(axis):
+    return [(axis, 1 << bit) for bit in range(lax.axis_size(axis).bit_length() - 1)]
 
 
 def local(
@@ -738,7 +740,7 @@
     )
 
     qraw, kraw, value, squares = project(normed_all, w_query, w_key, w_value)
-    squares = exchange_sum(squares, ("tensor",))
+    squares = exchange_sum(squares, doublings("tensor"))
     q_scale, k_scale = (lax.rsqrt(squares[i] / features + EPSILON)[:, None] for i in range(2))
     query, key, attended, lse = attend(
         qraw, kraw, value, q_scale, k_scale, q_gain, k_gain, cosine, sine, seg_ids[0], keep_mask[0]
@@ -776,8 +778,8 @@
     def back_of(c, grads, filled=()):
         return middle_back(c, grads, *norms[c], routed_own, router_wide, cotangent, ffn_gain, experts, filled)
 
-    def expert_sums(lefts, rights, ids, *others, added=(), weight=1):
-        return wgrad(lefts, rights, gate(ids, *others), width, per, added, weight)
+    def expert_sums(lefts, rights, ids, *others, added=(), weight=1, pieces=0):
+        return wgrad(lefts, rights, gate(ids, *others), width, per, added, weight, pieces)
 
     def core_swap(pieces):
         return [pair_swap(piece, 1) for piece in pieces]
@@ -786,53 +788,53 @@
         return Halving([part.reshape((part.shape[0] // per, per) + part.shape[1:]) for part in sums])
 
     first = back_of(0, gate(expert_grads[0], acts[1]))
-    gate_sent = expert_sums(ffn_parts, dgates, theirs, first[1])
+    gate_sent = expert_sums(ffn_parts, dgates, theirs, first[1], weight=0)
     gate_got = core_swap(gate_sent)
-    up_sent = expert_sums(ffn_parts, dups, theirs, *gate_sent)
+    up_sent = expert_sums(ffn_parts, dups, theirs, *gate_sent, weight=4)
     up_got = core_swap(up_sent)
-    second = back_of(1, gate(expert_grads[1], *up_sent), first[:2])
+    gate_sums = expert_sums(ffn_parts, dgates, mine, *up_sent, added=gate_got, weight=4)
+    gate_out = halving(gate_sums)
+    gate_out.send()
+    second = back_of(1, gate(expert_grads[1], *gate_sums), first[:2])
     middle_grad, middle_low = second[:2]
     middle_all = gather_rows(middle_low)
-    gate_sums = expert_sums(ffn_parts, dgates, mine, middle_low, added=gate_got)
-    gate_out = halving(gate_sums)
-    gate_out.send()
-    up_sums = expert_sums(ffn_parts, dups, mine, *gate_sums, added=up_got)
+    up_sums = expert_sums(ffn_parts, dups, mine, middle_low, added=up_got, weight=0)
     up_out = halving(up_sums)
     up_out.send()
     moe = down([gate(acts[0], *up_sums), acts[1]], w_down, parts)
     moe_sum = scatter_rows(moe)
-    attended_grad = nn(gate(middle_all, moe), w_out).astype(bf16)
+    gate_late = gate_out.add(moe)
+    gate_out.send()
+    down_sent = expert_sums(grad_parts, acts, theirs, *gate_late, pieces=4, weight=0.0)
+    down_got = core_swap(down_sent)
+    attended_grad = nn(gate(middle_all, *down_sent), w_out).astype(bf16)
     dqn, dkn, dvalue, qdot, kdot, q_gain_part, k_gain_part = attend_back(
         query, key, value, attended_grad, lse, qraw, kraw, q_scale, k_scale, q_gain, k_gain, cosine, sine,
         seg_ids[0], keep_mask[0],
     )
-    dots = exchange_sum(jnp.stack([qdot[:, 0], kdot[:, 0]]), ("tensor",)) / features
-    gate_late = gate_out.add(dqn)
-    gate_out.send()
-    down_sent = expert_sums(grad_parts, acts, theirs, *gate_late)
-    down_got = core_swap(down_sent)
-    up_late = up_out.add(*down_sent)
+    dots = exchange_sum(jnp.stack([qdot[:, 0], kdot[:, 0]]), doublings("tensor")) / features
+    up_late = up_out.add(dqn)
     up_out.send()
-    down_sums = expert_sums(grad_parts, acts, mine, *up_late, *gate_out.got, added=down_got, weight=13.0)
+    normed_part, dqraw, dkraw, attn_gain_part = project_back(
+        normed_all, dqn, dkn, dvalue, qraw, kraw, q_scale, k_scale, dots[0][:, None], dots[1][:, None],
+        gate(q_gain, *up_late, *gate_out.got), k_gain, w_query, w_key, w_value,
+    )
+    normed_grad = scatter_rows(normed_part)
+    down_sums = expert_sums(grad_parts, acts, mine, normed_part, added=down_got, weight=0.0)
     down_out = halving(down_sums)
     down_out.send()
-    normed_part, dqraw, dkraw, attn_gain_part = project_back(
-        normed_all, dqn, dkn, dvalue, qraw, kraw, q_scale, k_scale, dots[0][:, None], dots[1][:, None],
-        gate(q_gain, *down_sums, *up_out.got), k_gain, w_query, w_key, w_value,
-    )
-    normed_grad = scatter_rows(normed_part)
     def attention_sums(ids, *others, added=()):
         return attention_wgrad(
             normed_all, middle_all, (dqraw, dkraw, dvalue), attended, gate(ids, *others), dp_size, added
         )
 
-    attn_sent = attention_sums(other_blocks, normed_part)
+    attn_sent = attention_sums(other_blocks, *down_sums)
     attn_got = core_swap(attn_sent)
 
     def placed(part):
         return lax.dynamic_update_slice_in_dim(jnp.zeros((features,), f32), part, part_at * local_width, 0)
 
-    attn_sums = attention_sums(own_blocks, *attn_sent, added=attn_got)
+    attn_sums = attention_sums(own_blocks, *attn_sent, *up_out.got, added=attn_got)
     attn_out = Halving(attn_sums)
     normed_grad = gate(normed_grad, *attn_out.send())
     down_out.add(*attn_sums)
@@ -840,12 +842,14 @@
     smalls = [attn_gain_part[0] / attn_gain, placed(q_gain_part[0]), placed(k_gain_part[0]), (first[2] + second[2])[0]]
     router_part = sum(tn(late[3], norms[c][2]) for c, late in enumerate((first, second)))[:experts]
     smalls = gate(jnp.concatenate([jnp.stack(smalls), router_part]), *attn_sums)
-    smalls = exchange_sum(smalls, ("dp", "tensor"))
+    smalls = exchange_sum(smalls, doublings("dp")[:1] + doublings("tensor"))
+    attn_late = attn_out.add()
+    attn_out.send()
+    smalls = exchange_sum(gate(smalls, *attn_late), doublings("dp")[1:])
     late_got = tuple(down_out.got)
     gate_done = gate_out.done()
     up_done = up_out.done()
     down_done = down_out.done()
-    attn_out.add(normed_grad)
     query_done, key_done, value_done, out_done = attn_out.done()
     layer_out = (jnp.concatenate([norms[c][0] for c in chunks]) + gate(moe_sum, *late_got).astype(f32)).astype(bf16)
     tokens_grad = middle_grad + norm_back(normed_grad.astype(f32), inputs, first_scale, attn_gain)

time: 843 us -> 805 us (0.955)
  waiting for transfers between devices: 346 us -> 302 us
    ppermute x32, waiting for transfers between devices: 75 us -> 22.5 us  [pair_swap(): return lax.ppermute(values, 'dp', [(i, i ^ step) for i in range(size)])]
    ppermute x9, waiting for transfers between devices: 48.7 us -> 64.3 us  [exchange_sum(): lax.ppermute(values, axis, [(i, i ^ step) for i in range(lax.axis_size(ax...]
  transfers between devices with their start and end apart: 52 -> 52, of which waited for: 28 -> 19; matrix products, arithmetic and copies ran while one was open for 8% -> 9% of each run, Pallas kernels for 42% -> 44%
where the time goes in v9:
time: 805 us; the launch traced here: 798 us
  Pallas kernels  356 us (44%)
  waiting for transfers between devices  302 us (38%)
  other arithmetic  55.1 us (7%)
  starting transfers between devices  32.5 us (4%)
  local copies, waits for them, and re-layouts  24.5 us (3%)
  between operations  15.2 us (2%)
  matrix products  11.6 us (1%)
    all_gather x5, waiting for transfers between devices, gather_rows(): return lax.all_gather(values, 'tensor', axis=0, tiled=True)  163 us
    pallas_call x6, Pallas kernels, wgrad(): pl.pallas_call(functools.partial(wgrad_kernel, len(lefts), len(added), he...  107 us
    pallas_call x2, Pallas kernels, experts_block(): pl.pallas_call(functools.partial(expert_kernel, block), grid=(experts,),...  94.8 us
    ppermute x9, waiting for transfers between devices, exchange_sum(): lax.ppermute(values, axis, [(i, i ^ step) for i in range(lax.axis_size(ax...  64.3 us
    reduce_scatter x6, waiting for transfers between devices, scatter_rows(): return lax.psum_scatter(values, 'tensor', scatter_dimension=0, tiled=True)  52.1 us
    pallas_call x1, Pallas kernels, attend_back(): pl.pallas_call(functools.partial(attend_back_kernel, block), grid=(width...  24 us
    pallas_call x1, Pallas kernels, down(): pl.pallas_call(functools.partial(down_kernel, parts), grid=(features // b...  24 us
    pallas_call x2, Pallas kernels, attention_wgrad(): pl.pallas_call(functools.partial(attention_wgrad_kernel, len(added)), gri...  23.9 us
  transfers between devices with their start and end apart: 52, of which 19 were waited for; matrix products, arithmetic and copies ran while one was open for 9% of the time, Pallas kernels for 44%

profile of v9, /device:TPU:0, one launch (start us, length us, event | category | flops | bytes accessed | tf_op | source)
XLA Modules:
  0.0 797.5 jit_solution(17639485289242080786)
XLA Ops:
  7.2 1.6 fusion.6
  10.1 2.5 fusion.8
  12.7 83.6 %all-gather.6.cloned.1.call-done.rows_in = bf16[1024,2048]{1,0:T(8,128)(2,1)} async-done(((bf16[256,2048]{1,0:T(8,128)(2,1)}), bf16[1024,2048]{1,0:T(8,128)(2,1)}) %all-gather.6.cloned.1.call-update) | async-done | bytes 4194320 | tf_op jit(solution)/shard_map/all_gather | solution.py:633
  96.3 16.3 %project.1 = (f32[1024,512]{1,0:T(8,128)}, f32[1024,512]{1,0:T(8,128)}, bf16[1024,512]{1,0:T(8,128)(2,1)}, f32[2,1024]{1,0:T(2,128)}) custom-call(bf16[1024,2048]{1,0:T(8,128)(2,1)} %all-gather.6.cloned.1.call-done.rows_in, bf16[2048,512]{1,0:T(8,128)(2,1)} %w_query.3, bf16[2048,512]{1,0:T(8,128)(2,1)} %w_key.3, bf16[2048,512]{1,0:T(8,128)(2,1)} %w_value.3), custom_call_target="tpu_custom_call" | custom-call | flops 2899102976 | bytes 1310720 | tf_op jit(solution)/shard_map/project/pallas_call | solution.py:101
  112.6 4.0 collective-permute-done
  119.3 4.8 collective-permute-done.1
  126.1 15.7 %attend.1 = (bf16[1024,512]{1,0:T(8,128)(2,1)}, bf16[1024,512]{1,0:T(8,128)(2,1)}, bf16[1024,512]{1,0:T(8,128)(2,1)}, f32[1024,512]{1,0:T(8,128)}) custom-call(f32[1024,512]{1,0:T(8,128)} %get-tuple-element.119.qraw, f32[1024,512]{1,0:T(8,128)} %get-tuple-element.120.kraw, bf16[1024,512]{1,0:T(8,128)(2,1)} %get-tuple-element.121.value, ...), custom_call_target="tpu_custom_call" | custom-call | flops 57347878912 | bytes 1179648 | tf_op jit(solution)/shard_map/attend/pallas_call | solution.py:253
  141.9 35.6 %all-gather.8.cloned.1.call-done.grad = bf16[1024,2048]{1,0:T(8,128)(2,1)} async-done(((bf16[256,2048]{1,0:T(8,128)(2,1)}), bf16[1024,2048]{1,0:T(8,128)(2,1)}) %all-gather.8.cloned.1.call-update) | async-done | bytes 4194320 | tf_op jit(solution)/shard_map/all_gather | solution.py:633
  178.8 2.7 convolution_convert_fusion.1
  181.5 2.6 convolution_convert_fusion
  184.2 39.8 %reduce-scatter.7.cloned.1.call-done.summed = bf16[128,2048]{1,0:T(8,128)(2,1)} async-done(((bf16[512,2048]{1,0:T(8,128)(2,1)}), bf16[128,2048]{1,0:T(8,128)(2,1)}) %reduce-scatter.7.cloned.1.call-update) | async-done | bytes 524304 | tf_op jit(solution)/shard_map/reduce_scatter | solution.py:637
  223.9 2.6 middle.2
  228.4 5.7 convert_reduce_fusion
  235.1 22.6 %up_back.1 = bf16[1024,4096]{1,0:T(8,128)(2,1)} custom-call(bf16[1024,2048]{1,0:T(8,128)(2,1)} %all-gather.8.cloned.1.call-done.grad, bf16[16,2048,256]{2,1,0:T(8,128)(2,1)} %down_w.3), custom_call_target="tpu_custom_call" | custom-call | flops 7730940928 | bytes 2621440 | tf_op jit(solution)/shard_map/up_back/pallas_call | solution.py:411
  257.7 12.3 %reduce-scatter.9.cloned.1.call-done.summed = bf16[128,2048]{1,0:T(8,128)(2,1)} async-done(((bf16[512,2048]{1,0:T(8,128)(2,1)}), bf16[128,2048]{1,0:T(8,128)(2,1)}) %reduce-scatter.9.cloned.1.call-update) | async-done | bytes 524304 | tf_op jit(solution)/shard_map/reduce_scatter | solution.py:637
  270.0 2.5 middle.3
  272.6 44.1 %all-gather.10.cloned.1.call-done.rows_in.refs_0_ = bf16[512,2048]{1,0:T(8,128)(2,1)} async-done(((bf16[128,2048]{1,0:T(8,128)(2,1)}), bf16[512,2048]{1,0:T(8,128)(2,1)}) %all-gather.10.cloned.1.call-update) | async-done | bytes 2097168 | tf_op jit(solution)/shard_map/all_gather | solution.py:633
  316.7 47.4 %experts.2 = (bf16[512,4096]{1,0:T(8,128)(2,1)}, bf16[512,4096]{1,0:T(8,128)(2,1)}, bf16[512,4096]{1,0:T(8,128)(2,1)}, bf16[512,2176]{1,0:T(8,128)(2,1)}) custom-call(bf16[512,2048]{1,0:T(8,128)(2,1)} %all-gather.10.cloned.1.call-done.rows_in.refs_0_, bf16[4,2,128,4096]{3,2,1,0:T(8,128)(2,1)} %bitcast.125, f32[512,128]{1,0:T(8,128)} %bitcast.143, ...), custom_call_target="tpu_custom_call" | custom-call | flops 53210619904 | bytes 6291456 | tf_op jit(solution)/shard_map/experts/pallas_call | solution.py:477
  364.2 47.4 %experts.3 = (bf16[512,4096]{1,0:T(8,128)(2,1)}, bf16[512,4096]{1,0:T(8,128)(2,1)}, bf16[512,4096]{1,0:T(8,128)(2,1)}, bf16[512,2176]{1,0:T(8,128)(2,1)}) custom-call(bf16[512,2048]{1,0:T(8,128)(2,1)} %all-gather.12.cloned.1.call-done.rows_in.refs_1_, bf16[4,2,128,4096]{3,2,1,0:T(8,128)(2,1)} %bitcast.126, f32[512,128]{1,0:T(8,128)} %bitcast.142, ...), custom_call_target="tpu_custom_call" | custom-call | flops 53210619904 | bytes 6291456 | tf_op jit(solution)/shard_map/experts/pallas_call | solution.py:477
  414.1 4.3 middle_back.2
  418.4 16.7 %wgrad.6 = (bf16[2,2048,256]{2,1,0:T(8,128)(2,1)}, bf16[2,2048,256]{2,1,0:T(8,128)(2,1)}, bf16[2,2048,256]{2,1,0:T(8,128)(2,1)}, bf16[2,2048,256]{2,1,0:T(8,128)(2,1)}) custom-call(s32[8]{0:T(128)} %add.209.order, s32[2,4,8]{2,1,0:T(4,128)} %constant.77.clone.tables, bf16[512,2048]{1,0:T(8,128)(2,1)} %all-gather.10.cloned.1.call-done.rows_in.refs_0_, ...), custom_call_target="tpu_custom_call" | custom-call | tf_op jit(solution)/shard_map/wgrad/pallas_call | solution.py:582
  436.8 16.7 %wgrad.7 = (bf16[2,2048,256]{2,1,0:T(8,128)(2,1)}, bf16[2,2048,256]{2,1,0:T(8,128)(2,1)}, bf16[2,2048,256]{2,1,0:T(8,128)(2,1)}, bf16[2,2048,256]{2,1,0:T(8,128)(2,1)}) custom-call(s32[8]{0:T(128)} %add.209.order, s32[2,4,8]{2,1,0:T(4,128)} %constant.77.clone.tables, bf16[512,2048]{1,0:T(8,128)(2,1)} %all-gather.10.cloned.1.call-done.rows_in.refs_0_, ...), custom_call_target="tpu_custom_call" | custom-call | flops 15461881856 | tf_op jit(solution)/shard_map/wgrad/pallas_call | solution.py:582
  453.5 19.0 %wgrad.8 = (bf16[4,1024,256]{2,1,0:T(8,128)(2,1)}, bf16[4,1024,256]{2,1,0:T(8,128)(2,1)}, bf16[4,1024,256]{2,1,0:T(8,128)(2,1)}, bf16[4,1024,256]{2,1,0:T(8,128)(2,1)}) custom-call(s32[8]{0:T(128)} %add.204.order, s32[2,4,8]{2,1,0:T(4,128)} %constant.77.clone.tables, bf16[512,2048]{1,0:T(8,128)(2,1)} %all-gather.10.cloned.1.call-done.rows_in.refs_0_, ...), custom_call_target="tpu_custom_call" | custom-call | flops 15461881856 | tf_op jit(solution)/shard_map/wgrad/pallas_call | solution.py:582
  472.5 4.2 middle_back.3
  479.3 1.9 collective-permute-done.6.refs_4_
  482.7 4.5 collective-permute-done.7.refs_5_
  487.4 3.0 collective-permute-done.9.refs_7_
  490.4 19.1 %wgrad.9 = (bf16[4,1024,256]{2,1,0:T(8,128)(2,1)}, bf16[4,1024,256]{2,1,0:T(8,128)(2,1)}, bf16[4,1024,256]{2,1,0:T(8,128)(2,1)}, bf16[4,1024,256]{2,1,0:T(8,128)(2,1)}) custom-call(s32[8]{0:T(128)} %add.204.order, s32[2,4,8]{2,1,0:T(4,128)} %constant.77.clone.tables, bf16[512,2048]{1,0:T(8,128)(2,1)} %all-gather.10.cloned.1.call-done.rows_in.refs_0_, ...), custom_call_target="tpu_custom_call" | custom-call | tf_op jit(solution)/shard_map/wgrad/pallas_call | solution.py:582
  509.5 1.5 collective-permute-start.14
  512.5 24.0 %down.1 = bf16[1024,2048]{1,0:T(8,128)(2,1)} custom-call(bf16[16,2048,256]{2,1,0:T(8,128)(2,1)} %down_w.3, bf16[512,4096]{1,0:T(8,128)(2,1)} %get-tuple-element.172.refs_0_.refs_2_, bf16[512,4096]{1,0:T(8,128)(2,1)} %get-tuple-element.140.refs_1_.refs_3_), custom_call_target="tpu_custom_call" | custom-call | tf_op jit(solution)/shard_map/down/pallas_call | solution.py:615
  536.5 2.7 fusion.5
  539.3 2.3 copy-done.20
  541.6 2.1 fusion.4
  546.7 17.0 %wgrad.10 = (bf16[2,2048,256]{2,1,0:T(8,128)(2,1)}, bf16[2,2048,256]{2,1,0:T(8,128)(2,1)}, bf16[2,2048,256]{2,1,0:T(8,128)(2,1)}, bf16[2,2048,256]{2,1,0:T(8,128)(2,1)}) custom-call(s32[8]{0:T(128)} %add.209.order, s32[2,4,8]{2,1,0:T(4,128)} %constant.77.clone.tables, bf16[4,2,128,2048]{3,2,1,0:T(8,128)(2,1)} %bitcast.120, ...), custom_call_target="tpu_custom_call" | custom-call | tf_op jit(solution)/shard_map/wgrad/pallas_call | solution.py:582
  563.7 5.7 convolution_convert_fusion.2.out_grad
  569.4 24.0 %attend_back.1 = (f32[1024,512]{1,0:T(8,128)}, f32[1024,512]{1,0:T(8,128)}, bf16[1024,512]{1,0:T(8,128)(2,1)}, f32[1024,1]{1,0:T(8,128)}, f32[1024,1]{1,0:T(8,128)}, /*index=5*/f32[1,512]{1,0:T(1,128)}, f32[1,512]{1,0:T(1,128)}) custom-call(bf16[1024,512]{1,0:T(8,128)(2,1)} %get-tuple-element.173.query, bf16[1024,512]{1,0:T(8,128)(2,1)} %get-tuple-element.174.key, ...), custom_call_target="tpu_custom_call" | custom-call | tf_op jit(solution)/shard_map/attend_back/pallas_call | solution.py:319
  597.3 2.9 fusion.3
  600.5 2.0 collective-permute-start.13
  602.5 3.4 fusion.2
  610.1 13.9 %project_back.1 = (bf16[1024,2048]{1,0:T(8,128)(2,1)}, bf16[1024,512]{1,0:T(8,128)(2,1)}, bf16[1024,512]{1,0:T(8,128)(2,1)}, f32[1,2048]{1,0:T(1,128)}) custom-call(bf16[1024,2048]{1,0:T(8,128)(2,1)} %all-gather.6.cloned.1.call-done.rows_in, f32[1024,512]{1,0:T(8,128)} %get-tuple-element.184.dqn, f32[1024,512]{1,0:T(8,128)} %get-tuple-element.185.dkn, ...), custom_call_target="tpu_custom_call" | custom-call | flops 57982058496 | tf_op jit(solution)/shard_map/project_back/pallas_call | solution.py:141
  624.1 2.3 slice_bitcast_fusion.4
  627.9 19.0 %wgrad.11 = (bf16[4,1024,256]{2,1,0:T(8,128)(2,1)}, bf16[4,1024,256]{2,1,0:T(8,128)(2,1)}, bf16[4,1024,256]{2,1,0:T(8,128)(2,1)}, bf16[4,1024,256]{2,1,0:T(8,128)(2,1)}) custom-call(s32[8]{0:T(128)} %add.204.order, s32[2,4,8]{2,1,0:T(4,128)} %constant.77.clone.tables, bf16[4,2,128,2048]{3,2,1,0:T(8,128)(2,1)} %bitcast.122, ...), custom_call_target="tpu_custom_call" | custom-call | tf_op jit(solution)/shard_map/wgrad/pallas_call | solution.py:582
  646.9 11.3 %attention_wgrad.2 = (bf16[1,4,256,512]{3,2,1,0:T(8,128)(2,1)}, bf16[1,4,256,512]{3,2,1,0:T(8,128)(2,1)}, bf16[1,4,256,512]{3,2,1,0:T(8,128)(2,1)}, bf16[1,4,256,512]{3,2,1,0:T(8,128)(2,1)}) custom-call(s32[4]{0:T(128)} %get-tuple-element.198.order, s32[2,4,4]{2,1,0:T(4,128)} %constant.78.clone.tables, ...), custom_call_target="tpu_custom_call" | custom-call | tf_op jit(solution)/shard_map/attention_wgrad/pallas_call | solution.py:203
  659.5 1.5 collective-permute-start.23
  661.6 1.6 fusion.17
  665.0 2.3 pad_maximum_fusion
  668.7 12.6 %attention_wgrad.3 = (bf16[2,4,128,512]{3,2,1,0:T(8,128)(2,1)}, bf16[2,4,128,512]{3,2,1,0:T(8,128)(2,1)}, bf16[2,4,128,512]{3,2,1,0:T(8,128)(2,1)}, bf16[2,4,128,512]{3,2,1,0:T(8,128)(2,1)}) custom-call(s32[4]{0:T(128)} %get-tuple-element.205.order, s32[2,4,4]{2,1,0:T(4,128)} %constant.78.clone.tables, ...), custom_call_target="tpu_custom_call" | custom-call | tf_op jit(solution)/shard_map/attention_wgrad/pallas_call | solution.py:203
  682.7 1.6 fusion.16
  688.0 13.4 %collective-permute-done.37 = f32[20,2048]{1,0:T(8,128)S(1)} collective-permute-done((f32[20,2048]{1,0:T(8,128)S(1)}, f32[20,2048]{1,0:T(8,128)S(1)}, u32[]{:S(2)}, u32[]{:S(2)}) %collective-permute-start.37) | collective-permute-done | bytes 163872 | tf_op jit(solution)/shard_map/ppermute | solution.py:699
  702.4 2.3 pad_maximum_fusion.1
  704.7 17.6 %collective-permute-done.38 = f32[20,2048]{1,0:T(8,128)S(1)} collective-permute-done((f32[20,2048]{1,0:T(8,128)S(1)}, f32[20,2048]{1,0:T(8,128)S(1)}, u32[]{:S(2)}, u32[]{:S(2)}) %collective-permute-start.38) | collective-permute-done | bytes 163872 | tf_op jit(solution)/shard_map/ppermute | solution.py:699
  722.4 2.2 fusion.1
  724.6 1.5 collective-permute-start.30
  726.2 3.7 collective-permute-done.32
  731.0 1.6 collective-permute-start.39
  732.6 2.1 fusion.13
  737.1 19.5 %collective-permute-done.39 = f32[20,2048]{1,0:T(8,128)S(1)} collective-permute-done((f32[20,2048]{1,0:T(8,128)S(1)}, f32[20,2048]{1,0:T(8,128)S(1)}, u32[]{:S(2)}, u32[]{:S(2)}) %collective-permute-start.39) | collective-permute-done | bytes 163872 | tf_op jit(solution)/shard_map/ppermute | solution.py:699
  756.6 1.7 collective-permute-start.40
  760.3 4.9 collective-permute-done.40
  766.5 8.8 %collective-permute-done.35 = bf16[1,4,128,512]{3,2,1,0:T(8,128)(2,1)S(1)} collective-permute-done((bf16[1,4,128,512]{3,2,1,0:T(8,128)(2,1)S(1)}, bf16[1,4,128,512]{3,2,1,0:T(8,128)(2,1)S(1)}, u32[]{:S(2)}, u32[]{:S(2)}) %collective-permute-start.35) | collective-permute-done | bytes 524320 | tf_op jit(solution)/shard_map/ppermute | solution.py:642
  777.1 1.9 fusion.15
  780.8 2.4 pad_maximum_fusion.2
  785.5 1.8 fusion.12
  787.4 3.2 fusion.11
  (238 shorter events, 57.1 us)
Async XLA Ops:
  7.2 171.6 %copy-start = (bf16[2048,512]{1,0:T(8,128)(2,1)S(1)}, bf16[2048,512]{1,0:T(8,128)(2,1)}, u32[]{:S(2)}) copy-start(bf16[2048,512]{1,0:T(8,128)(2,1)} %param.37) | copy-start | bytes 6291460
  7.2 89.0 %all-gather.6.cloned.1.call-start = ((), (), s32[]{:S(2)}) async-start(), calls=%async_computation.6 | async-start | bytes 5242880 | tf_op jit(solution)/shard_map/all_gather | solution.py:633
  12.6 164.9 %all-gather.8.cloned.1.call-start = ((), (), s32[]{:S(2)}) async-start(), calls=%async_computation.7 | async-start | bytes 5242880 | tf_op jit(solution)/shard_map/all_gather | solution.py:633
  96.3 22.0 %copy-start.32 = (s32[1,1024]{1,0:T(1,128)S(1)}, s32[1,1024]{1,0:T(1,128)}, u32[]{:S(2)}) copy-start(s32[1,1024]{1,0:T(1,128)} %seg_row.3) | copy-start | bytes 12292
  96.3 127.7 %reduce-scatter.7.cloned.1.call-start = ((), (), s32[]{:S(2)}) async-start(), calls=%async_computation.8 | async-start | bytes 2621440 | tf_op jit(solution)/shard_map/reduce_scatter | solution.py:637
  112.6 4.0 collective-permute-start
  117.3 6.8 collective-permute-start.1
  181.4 88.6 %reduce-scatter.9.cloned.1.call-start = ((), (), s32[]{:S(2)}) async-start(), calls=%async_computation.9 | async-start | bytes 2621440 | tf_op jit(solution)/shard_map/reduce_scatter | solution.py:637
  184.1 42.9 %copy-start.29 = (s32[1024,8]{0,1:T(8,128)S(1)}, s32[1024,8]{0,1:T(8,128)}, u32[]{:S(2)}) copy-start(s32[1024,8]{0,1:T(8,128)} %param.32) | copy-start | bytes 98308
  184.1 43.1 %copy-start.28 = (bf16[2048,16]{0,1:T(8,128)(2,1)S(1)}, bf16[2048,16]{0,1:T(8,128)(2,1)}, u32[]{:S(2)}) copy-start(bf16[2048,16]{0,1:T(8,128)(2,1)} %param.41) | copy-start | bytes 196612
  184.1 132.6 %all-gather.10.cloned.1.call-start = ((), (), s32[]{:S(2)}) async-start(), calls=%async_computation.10 | async-start | bytes 2621440 | tf_op jit(solution)/shard_map/all_gather | solution.py:633
  226.5 137.7 %all-gather.12.cloned.1.call-start = ((), (), s32[]{:S(2)}) async-start(), calls=%async_computation.11 | async-start | bytes 2621440 | tf_op jit(solution)/shard_map/all_gather | solution.py:633
  272.6 141.6 %reduce-scatter.13.cloned.1.call-start = ((), (), s32[]{:S(2)}) async-start(), calls=%async_computation.13 | async-start | bytes 2785280 | tf_op jit(solution)/shard_map/reduce_scatter | solution.py:637
  364.1 108.4 %reduce-scatter.11.cloned.1.call-start = ((), (), s32[]{:S(2)}) async-start(), calls=%async_computation.12 | async-start | bytes 2785280 | tf_op jit(solution)/shard_map/reduce_scatter | solution.py:637
  411.7 152.0 %all-gather.14.cloned.1.call-start = ((), (), s32[]{:S(2)}) async-start(), calls=%async_computation.15 | async-start | bytes 5242880 | tf_op jit(solution)/shard_map/all_gather | solution.py:633
  435.1 18.4 %collective-permute-start.2 = (bf16[2,2048,256]{2,1,0:T(8,128)(2,1)}, bf16[2,2048,256]{2,1,0:T(8,128)(2,1)}, u32[]{:S(2)}, u32[]{:S(2)}) collective-permute-start(bf16[2,2048,256]{2,1,0:T(8,128)(2,1)} %get-tuple-element.147), channel_id=1, source_target_pairs={{0,4},{4,0},{8,12},{12,8},{16,20},{20,16},{24,28},{28,24},{1,5},{5... | collective-permute-start | bytes 6291464 | tf_op jit(solution)/shard_map/ppermute | solution.py:642
  435.1 18.4 %collective-permute-start.3 = (bf16[2,2048,256]{2,1,0:T(8,128)(2,1)}, bf16[2,2048,256]{2,1,0:T(8,128)(2,1)}, u32[]{:S(2)}, u32[]{:S(2)}) collective-permute-start(bf16[2,2048,256]{2,1,0:T(8,128)(2,1)} %get-tuple-element.148), channel_id=1, source_target_pairs={{0,4},{4,0},{8,12},{12,8},{16,20},{20,16},{24,28},{28,24},{1,5},{5... | collective-permute-start | bytes 6291464 | tf_op jit(solution)/shard_map/ppermute | solution.py:642
  435.6 17.9 %collective-permute-start.4 = (bf16[2,2048,256]{2,1,0:T(8,128)(2,1)}, bf16[2,2048,256]{2,1,0:T(8,128)(2,1)}, u32[]{:S(2)}, u32[]{:S(2)}) collective-permute-start(bf16[2,2048,256]{2,1,0:T(8,128)(2,1)} %get-tuple-element.149), channel_id=1, source_target_pairs={{0,4},{4,0},{8,12},{12,8},{16,20},{20,16},{24,28},{28,24},{1,5},{5... | collective-permute-start | bytes 6291464 | tf_op jit(solution)/shard_map/ppermute | solution.py:642
  435.6 17.9 %collective-permute-start.5 = (bf16[2,2048,256]{2,1,0:T(8,128)(2,1)}, bf16[2,2048,256]{2,1,0:T(8,128)(2,1)}, u32[]{:S(2)}, u32[]{:S(2)}) collective-permute-start(bf16[2,2048,256]{2,1,0:T(8,128)(2,1)} %get-tuple-element.150), channel_id=1, source_target_pairs={{0,4},{4,0},{8,12},{12,8},{16,20},{20,16},{24,28},{28,24},{1,5},{5... | collective-permute-start | bytes 6291464 | tf_op jit(solution)/shard_map/ppermute | solution.py:642
  476.7 300.3 %reduce-scatter.15.cloned.1.call-start = ((), (), s32[]{:S(2)}) async-start(), calls=%async_computation.14 | async-start | bytes 5242880 | tf_op jit(solution)/shard_map/reduce_scatter | solution.py:637
  476.8 4.4 collective-permute-start.6
  476.9 10.3 %collective-permute-start.7 = (bf16[2,2048,256]{2,1,0:T(8,128)(2,1)}, bf16[2,2048,256]{2,1,0:T(8,128)(2,1)S(1)}, u32[]{:S(2)}, u32[]{:S(2)}) collective-permute-start(bf16[2,2048,256]{2,1,0:T(8,128)(2,1)} %get-tuple-element.155), channel_id=1, source_target_pairs={{0,4},{4,0},{8,12},{12,8},{16,20},{20,16},{24,28},{28,24},{1,5},{5... | collective-permute-start | bytes 6291464 | tf_op jit(solution)/shard_map/ppermute | solution.py:642
  477.4 10.0 %collective-permute-start.8 = (bf16[2,2048,256]{2,1,0:T(8,128)(2,1)}, bf16[2,2048,256]{2,1,0:T(8,128)(2,1)}, u32[]{:S(2)}, u32[]{:S(2)}) collective-permute-start(bf16[2,2048,256]{2,1,0:T(8,128)(2,1)} %get-tuple-element.156), channel_id=1, source_target_pairs={{0,4},{4,0},{8,12},{12,8},{16,20},{20,16},{24,28},{28,24},{1,5},{5... | collective-permute-start | bytes 6291464 | tf_op jit(solution)/shard_map/ppermute | solution.py:642
  477.4 12.9 %collective-permute-start.9 = (bf16[2,2048,256]{2,1,0:T(8,128)(2,1)}, bf16[2,2048,256]{2,1,0:T(8,128)(2,1)}, u32[]{:S(2)}, u32[]{:S(2)}) collective-permute-start(bf16[2,2048,256]{2,1,0:T(8,128)(2,1)} %get-tuple-element.157), channel_id=1, source_target_pairs={{0,4},{4,0},{8,12},{12,8},{16,20},{20,16},{24,28},{28,24},{1,5},{5... | collective-permute-start | bytes 6291464 | tf_op jit(solution)/shard_map/ppermute | solution.py:642
  477.9 58.6 %collective-permute-start.10 = (bf16[2,2,1024,256]{3,2,1,0:T(8,128)(2,1)}, bf16[2,2,1024,256]{3,2,1,0:T(8,128)(2,1)}, u32[]{:S(2)}, u32[]{:S(2)}) collective-permute-start(bf16[2,2,1024,256]{3,2,1,0:T(8,128)(2,1)} %bitcast.170), channel_id=1, source_target_pairs={{0,16},{4,20},{8,24},{12,28},{16,0},{20,4},{24,8},{28,12},{1,17},{... | collective-permute-start | bytes 6291464 | tf_op jit(solution)/shard_map/ppermute | solution.py:642
  481.2 55.3 %collective-permute-start.11 = (bf16[2,2,1024,256]{3,2,1,0:T(8,128)(2,1)}, bf16[2,2,1024,256]{3,2,1,0:T(8,128)(2,1)}, u32[]{:S(2)}, u32[]{:S(2)}) collective-permute-start(bf16[2,2,1024,256]{3,2,1,0:T(8,128)(2,1)} %bitcast.169), channel_id=1, source_target_pairs={{0,8},{4,12},{8,0},{12,4},{16,24},{20,28},{24,16},{28,20},{1,9},{5... | collective-permute-start | bytes 6291464 | tf_op jit(solution)/shard_map/ppermute | solution.py:642
  509.5 86.4 %collective-permute-start.14 = (bf16[2,2,1024,256]{3,2,1,0:T(8,128)(2,1)}, bf16[2,2,1024,256]{3,2,1,0:T(8,128)(2,1)}, u32[]{:S(2)}, u32[]{:S(2)}) collective-permute-start(bf16[2,2,1024,256]{3,2,1,0:T(8,128)(2,1)} %bitcast.172), channel_id=1, source_target_pairs={{0,16},{4,20},{8,24},{12,28},{16,0},{20,4},{24,8},{28,12},{1,17},{... | collective-permute-start | bytes 6291464 | tf_op jit(solution)/shard_map/ppermute | solution.py:642
  511.0 85.5 %collective-permute-start.15 = (bf16[2,2,1024,256]{3,2,1,0:T(8,128)(2,1)}, bf16[2,2,1024,256]{3,2,1,0:T(8,128)(2,1)}, u32[]{:S(2)}, u32[]{:S(2)}) collective-permute-start(bf16[2,2,1024,256]{3,2,1,0:T(8,128)(2,1)} %bitcast.171), channel_id=1, source_target_pairs={{0,8},{4,12},{8,0},{12,4},{16,24},{20,28},{24,16},{28,20},{1,9},{5... | collective-permute-start | bytes 6291464 | tf_op jit(solution)/shard_map/ppermute | solution.py:642
  536.4 249.0 %reduce-scatter.17.cloned.1.call-start = ((), (), s32[]{:S(2)}) async-start(), calls=%async_computation.16 | async-start | bytes 5242880 | tf_op jit(solution)/shard_map/reduce_scatter | solution.py:637
  543.7 63.3 %collective-permute-start.16 = (bf16[1,2,1024,256]{3,2,1,0:T(8,128)(2,1)S(1)}, bf16[1,2,1024,256]{3,2,1,0:T(8,128)(2,1)}, u32[]{:S(2)}, u32[]{:S(2)}) collective-permute-start(bf16[1,2,1024,256]{3,2,1,0:T(8,128)(2,1)S(1)} %slice.128), channel_id=1, source_target_pairs={{0,8},{4,12},{8,0},{12,4},{16,24},{20,28},{24,16},{28,20},{1,9},{5... | collective-permute-start | bytes 3145736 | tf_op jit(solution)/shard_map/ppermute | solution.py:642
  546.1 60.9 %collective-permute-start.17 = (bf16[1,2,1024,256]{3,2,1,0:T(8,128)(2,1)}, bf16[1,2,1024,256]{3,2,1,0:T(8,128)(2,1)}, u32[]{:S(2)}, u32[]{:S(2)}) collective-permute-start(bf16[1,2,1024,256]{3,2,1,0:T(8,128)(2,1)} %slice_bitcast_fusion.5), channel_id=1, source_target_pairs={{0,16},{4,20},{8,24},{12,28},{16,0},{20,4},{24,8},{28,12},{1,17},{... | collective-permute-start | bytes 3145736 | tf_op jit(solution)/shard_map/ppermute | solution.py:642
  563.7 62.7 %collective-permute-start.18 = (bf16[2,2048,256]{2,1,0:T(8,128)(2,1)}, bf16[2,2048,256]{2,1,0:T(8,128)(2,1)}, u32[]{:S(2)}, u32[]{:S(2)}) collective-permute-start(bf16[2,2048,256]{2,1,0:T(8,128)(2,1)} %get-tuple-element.178), channel_id=1, source_target_pairs={{0,4},{4,0},{8,12},{12,8},{16,20},{20,16},{24,28},{28,24},{1,5},{5... | collective-permute-start | bytes 6291464 | tf_op jit(solution)/shard_map/ppermute | solution.py:642
  595.9 31.9 %collective-permute-start.19 = (bf16[2,2048,256]{2,1,0:T(8,128)(2,1)}, bf16[2,2048,256]{2,1,0:T(8,128)(2,1)}, u32[]{:S(2)}, u32[]{:S(2)}) collective-permute-start(bf16[2,2048,256]{2,1,0:T(8,128)(2,1)} %get-tuple-element.179), channel_id=1, source_target_pairs={{0,4},{4,0},{8,12},{12,8},{16,20},{20,16},{24,28},{28,24},{1,5},{5... | collective-permute-start | bytes 6291464 | tf_op jit(solution)/shard_map/ppermute | solution.py:642
  596.5 4.0 collective-permute-start.12
  600.5 7.0 collective-permute-start.13
  607.0 20.9 %collective-permute-start.20 = (bf16[2,2048,256]{2,1,0:T(8,128)(2,1)}, bf16[2,2048,256]{2,1,0:T(8,128)(2,1)}, u32[]{:S(2)}, u32[]{:S(2)}) collective-permute-start(bf16[2,2048,256]{2,1,0:T(8,128)(2,1)} %get-tuple-element.180), channel_id=1, source_target_pairs={{0,4},{4,0},{8,12},{12,8},{16,20},{20,16},{24,28},{28,24},{1,5},{5... | collective-permute-start | bytes 6291464 | tf_op jit(solution)/shard_map/ppermute | solution.py:642
  607.0 20.9 %collective-permute-start.21 = (bf16[2,2048,256]{2,1,0:T(8,128)(2,1)}, bf16[2,2048,256]{2,1,0:T(8,128)(2,1)}, u32[]{:S(2)}, u32[]{:S(2)}) collective-permute-start(bf16[2,2048,256]{2,1,0:T(8,128)(2,1)} %get-tuple-element.181), channel_id=1, source_target_pairs={{0,4},{4,0},{8,12},{12,8},{16,20},{20,16},{24,28},{28,24},{1,5},{5... | collective-permute-start | bytes 6291464 | tf_op jit(solution)/shard_map/ppermute | solution.py:642
  607.5 53.5 %collective-permute-start.24 = (bf16[1,2,1024,256]{3,2,1,0:T(8,128)(2,1)}, bf16[1,2,1024,256]{3,2,1,0:T(8,128)(2,1)}, u32[]{:S(2)}, u32[]{:S(2)}) collective-permute-start(bf16[1,2,1024,256]{3,2,1,0:T(8,128)(2,1)} %slice.130), channel_id=1, source_target_pairs={{0,8},{4,12},{8,0},{12,4},{16,24},{20,28},{24,16},{28,20},{1,9},{5... | collective-permute-start | bytes 3145736 | tf_op jit(solution)/shard_map/ppermute | solution.py:642
  626.3 34.7 %collective-permute-start.25 = (bf16[1,2,1024,256]{3,2,1,0:T(8,128)(2,1)}, bf16[1,2,1024,256]{3,2,1,0:T(8,128)(2,1)}, u32[]{:S(2)}, u32[]{:S(2)}) collective-permute-start(bf16[1,2,1024,256]{3,2,1,0:T(8,128)(2,1)} %slice_bitcast_fusion.4), channel_id=1, source_target_pairs={{0,16},{4,20},{8,24},{12,28},{16,0},{20,4},{24,8},{28,12},{1,17},{... | collective-permute-start | bytes 3145736 | tf_op jit(solution)/shard_map/ppermute | solution.py:642
  646.9 11.5 %copy-start.30 = (bf16[128,128]{1,0:T(8,128)(2,1)S(1)}, bf16[128,128]{1,0:T(8,128)(2,1)}, u32[]{:S(2)}) copy-start(bf16[128,128]{1,0:T(8,128)(2,1)} %get-tuple-element.220) | copy-start | bytes 98308
  646.9 11.8 %copy-start.35 = (f32[1,2048]{1,0:T(1,128)S(1)}, f32[1,2048]{1,0:T(1,128)}, u32[]{:S(2)}) copy-start(f32[1,2048]{1,0:T(1,128)} %get-tuple-element.218) | copy-start | bytes 24580
  646.9 11.8 %copy-start.36 = (f32[1,2048]{1,0:T(1,128)S(1)}, f32[1,2048]{1,0:T(1,128)}, u32[]{:S(2)}) copy-start(f32[1,2048]{1,0:T(1,128)} %get-tuple-element.219) | copy-start | bytes 24580
  646.9 11.8 %copy-start.14 = (bf16[128,2048]{1,0:T(8,128)(2,1)S(1)}, bf16[128,2048]{1,0:T(8,128)(2,1)}, u32[]{:S(2)}) copy-start(bf16[128,2048]{1,0:T(8,128)(2,1)} %get-tuple-element.136.normed) | copy-start | bytes 1572868
  646.9 11.8 %copy-start.31 = (bf16[128,128]{1,0:T(8,128)(2,1)S(1)}, bf16[128,128]{1,0:T(8,128)(2,1)}, u32[]{:S(2)}) copy-start(bf16[128,128]{1,0:T(8,128)(2,1)} %get-tuple-element.221) | copy-start | bytes 98308
  658.3 3.3 collective-permute-start.26
  659.1 63.2 %collective-permute-start.22 = (bf16[2,2,1024,256]{3,2,1,0:T(8,128)(2,1)}, bf16[2,2,1024,256]{3,2,1,0:T(8,128)(2,1)}, u32[]{:S(2)}, u32[]{:S(2)}) collective-permute-start(bf16[2,2,1024,256]{3,2,1,0:T(8,128)(2,1)} %bitcast.168), channel_id=1, source_target_pairs={{0,16},{4,20},{8,24},{12,28},{16,0},{20,4},{24,8},{28,12},{1,17},{... | collective-permute-start | bytes 6291464 | tf_op jit(solution)/shard_map/ppermute | solution.py:642
  659.5 62.8 %collective-permute-start.23 = (bf16[2,2,1024,256]{3,2,1,0:T(8,128)(2,1)}, bf16[2,2,1024,256]{3,2,1,0:T(8,128)(2,1)}, u32[]{:S(2)}, u32[]{:S(2)}) collective-permute-start(bf16[2,2,1024,256]{3,2,1,0:T(8,128)(2,1)} %bitcast.167), channel_id=1, source_target_pairs={{0,8},{4,12},{8,0},{12,4},{16,24},{20,28},{24,16},{28,20},{1,9},{5... | collective-permute-start | bytes 6291464 | tf_op jit(solution)/shard_map/ppermute | solution.py:642
  661.0 6.7 collective-permute-start.27
  661.0 6.7 collective-permute-start.28
  661.6 6.2 collective-permute-start.29
  667.7 15.0 %copy-start.8 = (bf16[2,2,1024,256]{3,2,1,0:T(8,128)(2,1)S(1)}, bf16[2,2,1024,256]{3,2,1,0:T(8,128)(2,1)}, u32[]{:S(2)}) copy-start(bf16[2,2,1024,256]{3,2,1,0:T(8,128)(2,1)} %fusion.2) | copy-start | bytes 6291460
  681.3 48.5 %collective-permute-start.32 = (bf16[2,4,128,512]{3,2,1,0:T(8,128)(2,1)}, bf16[2,4,128,512]{3,2,1,0:T(8,128)(2,1)S(1)}, u32[]{:S(2)}, u32[]{:S(2)}) collective-permute-start(bf16[2,4,128,512]{3,2,1,0:T(8,128)(2,1)} %get-tuple-element.207), channel_id=1, source_target_pairs={{0,16},{4,20},{8,24},{12,28},{16,0},{20,4},{24,8},{28,12},{1,17},{... | collective-permute-start | bytes 3145736 | tf_op jit(solution)/shard_map/ppermute | solution.py:642
  682.6 2.5 collective-permute-start.36
  684.3 46.4 %collective-permute-start.34 = (bf16[2,4,128,512]{3,2,1,0:T(8,128)(2,1)S(1)}, bf16[2,4,128,512]{3,2,1,0:T(8,128)(2,1)S(1)}, u32[]{:S(2)}, u32[]{:S(2)}) collective-permute-start(bf16[2,4,128,512]{3,2,1,0:T(8,128)(2,1)S(1)} %copy-done.42), channel_id=1, source_target_pairs={{0,8},{4,12},{8,0},{12,4},{16,24},{20,28},{24,16},{28,20},{1,9},{5... | collective-permute-start | bytes 3145736 | tf_op jit(solution)/shard_map/ppermute | solution.py:642
  685.2 16.2 %collective-permute-start.37 = (f32[20,2048]{1,0:T(8,128)S(1)}, f32[20,2048]{1,0:T(8,128)S(1)}, u32[]{:S(2)}, u32[]{:S(2)}) collective-permute-start(f32[20,2048]{1,0:T(8,128)S(1)} %add.228), channel_id=1, source_target_pairs={{0,1},{1,0},{2,3},{3,2},{4,5},{5,4},{6,7},{7,6},{8,9},{9,8},{10,11... | collective-permute-start | bytes 491528 | tf_op jit(solution)/shard_map/ppermute | solution.py:699
  701.4 21.0 %copy-start.18 = (bf16[4,1024,256]{2,1,0:T(8,128)(2,1)S(1)}, bf16[4,1024,256]{2,1,0:T(8,128)(2,1)}, u32[]{:S(2)}) copy-start(bf16[4,1024,256]{2,1,0:T(8,128)(2,1)} %get-tuple-element.194) | copy-start | bytes 6291460
  701.4 20.9 %collective-permute-start.38 = (f32[20,2048]{1,0:T(8,128)S(1)}, f32[20,2048]{1,0:T(8,128)S(1)}, u32[]{:S(2)}, u32[]{:S(2)}) collective-permute-start(f32[20,2048]{1,0:T(8,128)S(1)} %add.229), channel_id=1, source_target_pairs={{0,2},{1,3},{2,0},{3,1},{4,6},{5,7},{6,4},{7,5},{8,10},{9,11},{10,... | collective-permute-start | bytes 491528 | tf_op jit(solution)/shard_map/ppermute | solution.py:699
  724.6 52.4 %collective-permute-start.30 = (bf16[1,2,1024,256]{3,2,1,0:T(8,128)(2,1)S(1)}, bf16[1,2,1024,256]{3,2,1,0:T(8,128)(2,1)}, u32[]{:S(2)}, u32[]{:S(2)}) collective-permute-start(bf16[1,2,1024,256]{3,2,1,0:T(8,128)(2,1)S(1)} %slice.132), channel_id=1, source_target_pairs={{0,8},{4,12},{8,0},{12,4},{16,24},{20,28},{24,16},{28,20},{1,9},{5... | collective-permute-start | bytes 3145736 | tf_op jit(solution)/shard_map/ppermute | solution.py:642
  731.0 25.6 %collective-permute-start.39 = (f32[20,2048]{1,0:T(8,128)S(1)}, f32[20,2048]{1,0:T(8,128)S(1)}, u32[]{:S(2)}, u32[]{:S(2)}) collective-permute-start(f32[20,2048]{1,0:T(8,128)S(1)} %add.230), channel_id=1, source_target_pairs={{0,8},{4,12},{8,0},{12,4},{16,24},{20,28},{24,16},{28,20},{1,9},{5... | collective-permute-start | bytes 491528 | tf_op jit(solution)/shard_map/ppermute | solution.py:699
  734.7 30.6 %copy-start.11 = (bf16[1,2,2,1024,256]{4,3,2,1,0:T(8,128)(2,1)}, bf16[1,2,2,1024,256]{4,3,2,1,0:T(8,128)(2,1)S(1)}, u32[]{:S(2)}) copy-start(bf16[1,2,2,1024,256]{4,3,2,1,0:T(8,128)(2,1)S(1)} %fusion.13) | copy-start | bytes 6291460
  735.8 41.3 %collective-permute-start.31 = (bf16[1,2,1024,256]{3,2,1,0:T(8,128)(2,1)}, bf16[1,2,1024,256]{3,2,1,0:T(8,128)(2,1)}, u32[]{:S(2)}, u32[]{:S(2)}) collective-permute-start(bf16[1,2,1024,256]{3,2,1,0:T(8,128)(2,1)} %slice_bitcast_fusion.3), channel_id=1, source_target_pairs={{0,16},{4,20},{8,24},{12,28},{16,0},{20,4},{24,8},{28,12},{1,17},{... | collective-permute-start | bytes 3145736 | tf_op jit(solution)/shard_map/ppermute | solution.py:642
  756.6 8.6 %collective-permute-start.40 = (f32[20,2048]{1,0:T(8,128)S(1)}, f32[20,2048]{1,0:T(8,128)S(1)}, u32[]{:S(2)}, u32[]{:S(2)}) collective-permute-start(f32[20,2048]{1,0:T(8,128)S(1)} %add.231), channel_id=1, source_target_pairs={{0,16},{4,20},{8,24},{12,28},{16,0},{20,4},{24,8},{28,12},{1,17},{... | collective-permute-start | bytes 491528 | tf_op jit(solution)/shard_map/ppermute | solution.py:699
  758.4 17.0 %collective-permute-start.35 = (bf16[1,4,128,512]{3,2,1,0:T(8,128)(2,1)S(1)}, bf16[1,4,128,512]{3,2,1,0:T(8,128)(2,1)S(1)}, u32[]{:S(2)}, u32[]{:S(2)}) collective-permute-start(bf16[1,4,128,512]{3,2,1,0:T(8,128)(2,1)S(1)} %slice_bitcast_fusion.6), channel_id=1, source_target_pairs={{0,16},{4,20},{8,24},{12,28},{16,0},{20,4},{24,8},{28,12},{1,17},{... | collective-permute-start | bytes 1572872 | tf_op jit(solution)/shard_map/ppermute | solution.py:642
  758.8 16.7 %collective-permute-start.33 = (bf16[1,4,128,512]{3,2,1,0:T(8,128)(2,1)S(1)}, bf16[1,4,128,512]{3,2,1,0:T(8,128)(2,1)S(1)}, u32[]{:S(2)}, u32[]{:S(2)}) collective-permute-start(bf16[1,4,128,512]{3,2,1,0:T(8,128)(2,1)S(1)} %slice.135), channel_id=1, source_target_pairs={{0,8},{4,12},{8,0},{12,4},{16,24},{20,28},{24,16},{28,20},{1,9},{5... | collective-permute-start | bytes 1572872 | tf_op jit(solution)/shard_map/ppermute | solution.py:642
  (31 other events, 101.8 us)
Sparse Core Ops, SparseCore 0:
  12.7 83.4 all-gather.5
  97.8 79.6 all-gather.7
  181.6 42.3 reduce-scatter.6
  226.8 43.1 reduce-scatter.8
  271.4 45.2 all-gather.9
  318.7 44.6 all-gather.11
  365.7 44.7 reduce-scatter.12
  412.7 45.4 reduce-scatter.10
  476.9 79.8 all-gather.13
  558.9 75.6 reduce-scatter.14
  637.0 85.3 reduce-scatter.16

commit v10 on v9

--- a/solution.py
+++ b/solution.py
@@ -150,7 +150,7 @@
     )(rows_in, dqn, dkn, dvalue, qraw, kraw, q_scale, k_scale, q_dot, k_dot, q_gain[None], k_gain[None], w_query, w_key, w_value)
 
 
-def attention_wgrad_kernel(added, order, tables, rows_in, middle, *refs):
+def attention_wgrad_kernel(added, held, order, tables, rows_in, middle, *refs):
     sides, (attended,), refs = refs[:3], refs[3:4], refs[4:]
     got, outs = (refs[:added], refs[added:])
     at = pl.program_id(0)
@@ -158,7 +158,7 @@
     if not added:
         for place, out in enumerate(outs):
 
-            @pl.when(at == place)
+            @pl.when(at // held == place)
             def _(out=out):
                 for weight, total in enumerate(totals):
                     out[0, weight] = total.astype(bf16)
@@ -168,7 +168,7 @@
     half = outs[0].shape[2]
     for place, piece in enumerate(got):
 
-        @pl.when(at == place)
+        @pl.when(at // held == place)
         def _(piece=piece):
             for weight, total in enumerate(totals):
                 scratch[weight] = (total + piece[0, weight].astype(f32)).astype(bf16)
@@ -193,15 +193,21 @@
     def half_spec(side):
         return pl.BlockSpec((1, 4, block // 2, width), lambda i, ids, to: (to[0, side, i], 0, 0, 0))
 
-    group_specs = [pl.BlockSpec((1, 4, block, width), lambda i, ids, to: (0, 0, 0, 0))] * count
+    pieces = min(2, count)
+    held = count // pieces
+
+    def piece_spec(place):
+        return pl.BlockSpec((1, 4, block, width), lambda i, ids, to: (jnp.clip(i - place * held, 0, held - 1), 0, 0, 0))
+
+    group_specs = [piece_spec(place) for place in range(pieces)]
     if added:
         out_specs = [half_spec(side) for side in range(len(sizes))]
         out_shape = [jax.ShapeDtypeStruct((size, 4, block // 2, width), bf16) for size in sizes]
     else:
         out_specs = group_specs
-        out_shape = [jax.ShapeDtypeStruct((1, 4, block, width), bf16)] * count
-    return pl.pallas_call(
-        functools.partial(attention_wgrad_kernel, len(added)),
+        out_shape = [jax.ShapeDtypeStruct((held, 4, block, width), bf16)] * pieces
+    return pl.pallas_call(
+        functools.partial(attention_wgrad_kernel, len(added), held),
         grid_spec=pltpu.PrefetchScalarGridSpec(
             num_scalar_prefetch=2,
             grid=(count,),
@@ -805,7 +811,7 @@
     moe_sum = scatter_rows(moe)
     gate_late = gate_out.add(moe)
     gate_out.send()
-    down_sent = expert_sums(grad_parts, acts, theirs, *gate_late, pieces=4, weight=0.0)
+    down_sent = expert_sums(grad_parts, acts, theirs, *gate_late, pieces=2, weight=0.0)
     down_got = core_swap(down_sent)
     attended_grad = nn(gate(middle_all, *down_sent), w_out).astype(bf16)
     dqn, dkn, dvalue, qdot, kdot, q_gain_part, k_gain_part = attend_back(
@@ -820,7 +826,7 @@
         gate(q_gain, *up_late, *gate_out.got), k_gain, w_query, w_key, w_value,
     )
     normed_grad = scatter_rows(normed_part)
-    down_sums = expert_sums(grad_parts, acts, mine, normed_part, added=down_got, weight=0.0)
+    down_sums = expert_sums(grad_parts, acts, mine, normed_part, *up_out.got, added=down_got, weight=0.0)
     down_out = halving(down_sums)
     down_out.send()
     def attention_sums(ids, *others, added=()):
@@ -830,15 +836,15 @@
 
     attn_sent = attention_sums(other_blocks, *down_sums)
     attn_got = core_swap(attn_sent)
+    down_late = down_out.add(*attn_sent)
+    down_out.send()
 
     def placed(part):
         return lax.dynamic_update_slice_in_dim(jnp.zeros((features,), f32), part, part_at * local_width, 0)
 
-    attn_sums = attention_sums(own_blocks, *attn_sent, *up_out.got, added=attn_got)
+    attn_sums = attention_sums(own_blocks, *down_late, added=attn_got)
     attn_out = Halving(attn_sums)
     normed_grad = gate(normed_grad, *attn_out.send())
-    down_out.add(*attn_sums)
-    down_out.send()
     smalls = [attn_gain_part[0] / attn_gain, placed(q_gain_part[0]), placed(k_gain_part[0]), (first[2] + second[2])[0]]
     router_part = sum(tn(late[3], norms[c][2]) for c, late in enumerate((first, second)))[:experts]
     smalls = gate(jnp.concatenate([jnp.stack(smalls), router_part]), *attn_sums)

time: 805 us -> 797 us (0.990)
    ppermute x9, waiting for transfers between devices: 64.3 us -> 34.4 us  [exchange_sum(): lax.ppermute(values, axis, [(i, i ^ step) for i in range(lax.axis_size(ax...]
    ppermute x32 -> x28, waiting for transfers between devices: 22.5 us -> 45.2 us  [pair_swap(): return lax.ppermute(values, 'dp', [(i, i ^ step) for i in range(size)])]
    convert_element_type x7 -> x8, other arithmetic: 13.9 us -> 18 us  [add(): self.kept[side] = total if last else total.astype(bf16)]
    ppermute x32 -> x28, starting transfers between devices: 21.9 us -> 22.2 us  [pair_swap(): return lax.ppermute(values, 'dp', [(i, i ^ step) for i in range(size)])]
  transfers between devices with their start and end apart: 52 -> 48, of which waited for: 19 -> 22; matrix products, arithmetic and copies ran while one was open for 9% -> 9% of each run, Pallas kernels for 44% -> 44%
where the time goes in v10:
time: 797 us; the launch traced here: 790 us
  Pallas kernels  352 us (44%)
  waiting for transfers between devices  296 us (37%)
  other arithmetic  56.9 us (7%)
  starting transfers between devices  31.4 us (4%)
  local copies, waits for them, and re-layouts  26.1 us (3%)
  between operations  15.2 us (2%)
  matrix products  12.2 us (2%)
    all_gather x5, waiting for transfers between devices, gather_rows(): return lax.all_gather(values, 'tensor', axis=0, tiled=True)  163 us
    pallas_call x6, Pallas kernels, wgrad(): pl.pallas_call(functools.partial(wgrad_kernel, len(lefts), len(added), he...  105 us
    pallas_call x2, Pallas kernels, experts_block(): pl.pallas_call(functools.partial(expert_kernel, block), grid=(experts,),...  94.7 us
    reduce_scatter x6, waiting for transfers between devices, scatter_rows(): return lax.psum_scatter(values, 'tensor', scatter_dimension=0, tiled=True)  52.5 us
    ppermute x28, waiting for transfers between devices, pair_swap(): return lax.ppermute(values, 'dp', [(i, i ^ step) for i in range(size)])  45.2 us
    ppermute x9, waiting for transfers between devices, exchange_sum(): lax.ppermute(values, axis, [(i, i ^ step) for i in range(lax.axis_size(ax...  34.4 us
    pallas_call x1, Pallas kernels, down(): pl.pallas_call(functools.partial(down_kernel, parts), grid=(features // b...  24 us
    pallas_call x1, Pallas kernels, attend_back(): pl.pallas_call(functools.partial(attend_back_kernel, block), grid=(width...  23.8 us
  transfers between devices with their start and end apart: 48, of which 22 were waited for; matrix products, arithmetic and copies ran while one was open for 9% of the time, Pallas kernels for 44%

profile of v10, /device:TPU:0, one launch (start us, length us, event | category | flops | bytes accessed | tf_op | source)
XLA Modules:
  0.0 789.7 jit_solution(16586958156272100664)
XLA Ops:
  7.2 1.6 fusion.6
  10.1 2.5 fusion.8
  12.7 83.6 %all-gather.6.cloned.1.call-done.rows_in = bf16[1024,2048]{1,0:T(8,128)(2,1)} async-done(((bf16[256,2048]{1,0:T(8,128)(2,1)}), bf16[1024,2048]{1,0:T(8,128)(2,1)}) %all-gather.6.cloned.1.call-update) | async-done | bytes 4194320 | tf_op jit(solution)/shard_map/all_gather | solution.py:639
  96.3 16.3 %project.1 = (f32[1024,512]{1,0:T(8,128)}, f32[1024,512]{1,0:T(8,128)}, bf16[1024,512]{1,0:T(8,128)(2,1)}, f32[2,1024]{1,0:T(2,128)}) custom-call(bf16[1024,2048]{1,0:T(8,128)(2,1)} %all-gather.6.cloned.1.call-done.rows_in, bf16[2048,512]{1,0:T(8,128)(2,1)} %w_query.3, bf16[2048,512]{1,0:T(8,128)(2,1)} %w_key.3, bf16[2048,512]{1,0:T(8,128)(2,1)} %w_value.3), custom_call_target="tpu_custom_call" | custom-call | flops 2899102976 | bytes 1310720 | tf_op jit(solution)/shard_map/project/pallas_call | solution.py:101
  112.6 4.0 collective-permute-done
  119.3 4.8 collective-permute-done.1
  126.1 15.6 %attend.1 = (bf16[1024,512]{1,0:T(8,128)(2,1)}, bf16[1024,512]{1,0:T(8,128)(2,1)}, bf16[1024,512]{1,0:T(8,128)(2,1)}, f32[1024,512]{1,0:T(8,128)}) custom-call(f32[1024,512]{1,0:T(8,128)} %get-tuple-element.115.qraw, f32[1024,512]{1,0:T(8,128)} %get-tuple-element.116.kraw, bf16[1024,512]{1,0:T(8,128)(2,1)} %get-tuple-element.117.value, ...), custom_call_target="tpu_custom_call" | custom-call | flops 57347878912 | bytes 1179648 | tf_op jit(solution)/shard_map/attend/pallas_call | solution.py:259
  141.8 35.7 %all-gather.8.cloned.1.call-done.grad = bf16[1024,2048]{1,0:T(8,128)(2,1)} async-done(((bf16[256,2048]{1,0:T(8,128)(2,1)}), bf16[1024,2048]{1,0:T(8,128)(2,1)}) %all-gather.8.cloned.1.call-update) | async-done | bytes 4194320 | tf_op jit(solution)/shard_map/all_gather | solution.py:639
  178.8 2.7 convolution_convert_fusion.1
  181.5 2.6 convolution_convert_fusion
  184.2 39.8 %reduce-scatter.7.cloned.1.call-done.summed = bf16[128,2048]{1,0:T(8,128)(2,1)} async-done(((bf16[512,2048]{1,0:T(8,128)(2,1)}), bf16[128,2048]{1,0:T(8,128)(2,1)}) %reduce-scatter.7.cloned.1.call-update) | async-done | bytes 524304 | tf_op jit(solution)/shard_map/reduce_scatter | solution.py:643
  223.9 2.5 middle.2
  228.1 5.7 convert_reduce_fusion
  234.7 22.6 %up_back.1 = bf16[1024,4096]{1,0:T(8,128)(2,1)} custom-call(bf16[1024,2048]{1,0:T(8,128)(2,1)} %all-gather.8.cloned.1.call-done.grad, bf16[16,2048,256]{2,1,0:T(8,128)(2,1)} %down_w.3), custom_call_target="tpu_custom_call" | custom-call | flops 7730940928 | bytes 2621440 | tf_op jit(solution)/shard_map/up_back/pallas_call | solution.py:417
  257.3 12.7 %reduce-scatter.9.cloned.1.call-done.summed = bf16[128,2048]{1,0:T(8,128)(2,1)} async-done(((bf16[512,2048]{1,0:T(8,128)(2,1)}), bf16[128,2048]{1,0:T(8,128)(2,1)}) %reduce-scatter.9.cloned.1.call-update) | async-done | bytes 524304 | tf_op jit(solution)/shard_map/reduce_scatter | solution.py:643
  270.0 2.5 middle.3
  272.6 44.1 %all-gather.10.cloned.1.call-done.rows_in.refs_0_ = bf16[512,2048]{1,0:T(8,128)(2,1)} async-done(((bf16[128,2048]{1,0:T(8,128)(2,1)}), bf16[512,2048]{1,0:T(8,128)(2,1)}) %all-gather.10.cloned.1.call-update) | async-done | bytes 2097168 | tf_op jit(solution)/shard_map/all_gather | solution.py:639
  316.7 47.3 %experts.2 = (bf16[512,4096]{1,0:T(8,128)(2,1)}, bf16[512,4096]{1,0:T(8,128)(2,1)}, bf16[512,4096]{1,0:T(8,128)(2,1)}, bf16[512,2176]{1,0:T(8,128)(2,1)}) custom-call(bf16[512,2048]{1,0:T(8,128)(2,1)} %all-gather.10.cloned.1.call-done.rows_in.refs_0_, bf16[4,2,128,4096]{3,2,1,0:T(8,128)(2,1)} %bitcast.124, f32[512,128]{1,0:T(8,128)} %bitcast.144, ...), custom_call_target="tpu_custom_call" | custom-call | flops 53210619904 | bytes 6291456 | tf_op jit(solution)/shard_map/experts/pallas_call | solution.py:483
  364.1 47.4 %experts.3 = (bf16[512,4096]{1,0:T(8,128)(2,1)}, bf16[512,4096]{1,0:T(8,128)(2,1)}, bf16[512,4096]{1,0:T(8,128)(2,1)}, bf16[512,2176]{1,0:T(8,128)(2,1)}) custom-call(bf16[512,2048]{1,0:T(8,128)(2,1)} %all-gather.12.cloned.1.call-done.rows_in.refs_1_, bf16[4,2,128,4096]{3,2,1,0:T(8,128)(2,1)} %bitcast.125, f32[512,128]{1,0:T(8,128)} %bitcast.143, ...), custom_call_target="tpu_custom_call" | custom-call | flops 53210619904 | bytes 6291456 | tf_op jit(solution)/shard_map/experts/pallas_call | solution.py:483
  414.1 4.2 middle_back.2
  418.3 16.7 %wgrad.6 = (bf16[2,2048,256]{2,1,0:T(8,128)(2,1)}, bf16[2,2048,256]{2,1,0:T(8,128)(2,1)}, bf16[2,2048,256]{2,1,0:T(8,128)(2,1)}, bf16[2,2048,256]{2,1,0:T(8,128)(2,1)}) custom-call(s32[8]{0:T(128)} %add.209.order, s32[2,4,8]{2,1,0:T(4,128)} %constant.77.clone.tables, bf16[512,2048]{1,0:T(8,128)(2,1)} %all-gather.10.cloned.1.call-done.rows_in.refs_0_, ...), custom_call_target="tpu_custom_call" | custom-call | tf_op jit(solution)/shard_map/wgrad/pallas_call | solution.py:588
  436.6 16.7 %wgrad.7 = (bf16[2,2048,256]{2,1,0:T(8,128)(2,1)}, bf16[2,2048,256]{2,1,0:T(8,128)(2,1)}, bf16[2,2048,256]{2,1,0:T(8,128)(2,1)}, bf16[2,2048,256]{2,1,0:T(8,128)(2,1)}) custom-call(s32[8]{0:T(128)} %add.209.order, s32[2,4,8]{2,1,0:T(4,128)} %constant.77.clone.tables, bf16[512,2048]{1,0:T(8,128)(2,1)} %all-gather.10.cloned.1.call-done.rows_in.refs_0_, ...), custom_call_target="tpu_custom_call" | custom-call | flops 15461881856 | tf_op jit(solution)/shard_map/wgrad/pallas_call | solution.py:588
  453.3 19.1 %wgrad.8 = (bf16[4,1024,256]{2,1,0:T(8,128)(2,1)}, bf16[4,1024,256]{2,1,0:T(8,128)(2,1)}, bf16[4,1024,256]{2,1,0:T(8,128)(2,1)}, bf16[4,1024,256]{2,1,0:T(8,128)(2,1)}) custom-call(s32[8]{0:T(128)} %add.204.order, s32[2,4,8]{2,1,0:T(4,128)} %constant.77.clone.tables, bf16[512,2048]{1,0:T(8,128)(2,1)} %all-gather.10.cloned.1.call-done.rows_in.refs_0_, ...), custom_call_target="tpu_custom_call" | custom-call | flops 15461881856 | tf_op jit(solution)/shard_map/wgrad/pallas_call | solution.py:588
  472.5 4.2 middle_back.3
  479.3 1.9 collective-permute-done.6.refs_4_
  482.7 4.5 collective-permute-done.7.refs_5_
  487.3 3.0 collective-permute-done.9.refs_7_
  490.3 18.8 %wgrad.9 = (bf16[4,1024,256]{2,1,0:T(8,128)(2,1)}, bf16[4,1024,256]{2,1,0:T(8,128)(2,1)}, bf16[4,1024,256]{2,1,0:T(8,128)(2,1)}, bf16[4,1024,256]{2,1,0:T(8,128)(2,1)}) custom-call(s32[8]{0:T(128)} %add.204.order, s32[2,4,8]{2,1,0:T(4,128)} %constant.77.clone.tables, bf16[512,2048]{1,0:T(8,128)(2,1)} %all-gather.10.cloned.1.call-done.rows_in.refs_0_, ...), custom_call_target="tpu_custom_call" | custom-call | tf_op jit(solution)/shard_map/wgrad/pallas_call | solution.py:588
  509.1 1.6 collective-permute-start.14
  512.1 24.0 %down.1 = bf16[1024,2048]{1,0:T(8,128)(2,1)} custom-call(bf16[16,2048,256]{2,1,0:T(8,128)(2,1)} %down_w.3, bf16[512,4096]{1,0:T(8,128)(2,1)} %get-tuple-element.168.refs_0_.refs_2_, bf16[512,4096]{1,0:T(8,128)(2,1)} %get-tuple-element.136.refs_1_.refs_3_), custom_call_target="tpu_custom_call" | custom-call | tf_op jit(solution)/shard_map/down/pallas_call | solution.py:621
  536.2 2.7 fusion.5
  539.0 2.3 copy-done.18
  541.3 2.1 fusion.4
  546.3 15.9 %wgrad.10 = (bf16[4,2048,256]{2,1,0:T(8,128)(2,1)}, bf16[4,2048,256]{2,1,0:T(8,128)(2,1)}) custom-call(s32[8]{0:T(128)} %add.209.order, s32[2,4,8]{2,1,0:T(4,128)} %constant.77.clone.tables, bf16[4,2,128,2048]{3,2,1,0:T(8,128)(2,1)} %bitcast.119, bf16[4,2,128,2048]{3,2,1,0:T(8,128)(2,1)} %bitcast.120, bf16[512,4096]{1,0:T(8,128)(2,1)} %get-tuple-element.168.refs_0_.refs_2_, ...), custom_call_target="tpu_custom_call" | custom-call | tf_op jit(solution)/shard_map/wgrad/pallas_call | solution.py:588
  562.3 6.3 convolution_convert_fusion.2.out_grad
  568.6 23.8 %attend_back.1 = (f32[1024,512]{1,0:T(8,128)}, f32[1024,512]{1,0:T(8,128)}, bf16[1024,512]{1,0:T(8,128)(2,1)}, f32[1024,1]{1,0:T(8,128)}, f32[1024,1]{1,0:T(8,128)}, /*index=5*/f32[1,512]{1,0:T(1,128)}, f32[1,512]{1,0:T(1,128)}) custom-call(bf16[1024,512]{1,0:T(8,128)(2,1)} %get-tuple-element.169.query, bf16[1024,512]{1,0:T(8,128)(2,1)} %get-tuple-element.170.key, ...), custom_call_target="tpu_custom_call" | custom-call | tf_op jit(solution)/shard_map/attend_back/pallas_call | solution.py:325
  595.4 2.8 fusion.3
  598.3 2.8 fusion.2
  602.7 1.7 collective-permute-start.13
  606.9 3.5 collective-permute-done.13
  612.5 14.0 %project_back.1 = (bf16[1024,2048]{1,0:T(8,128)(2,1)}, bf16[1024,512]{1,0:T(8,128)(2,1)}, bf16[1024,512]{1,0:T(8,128)(2,1)}, f32[1,2048]{1,0:T(1,128)}) custom-call(bf16[1024,2048]{1,0:T(8,128)(2,1)} %all-gather.6.cloned.1.call-done.rows_in, f32[1024,512]{1,0:T(8,128)} %get-tuple-element.178.dqn, f32[1024,512]{1,0:T(8,128)} %get-tuple-element.179.dkn, ...), custom_call_target="tpu_custom_call" | custom-call | flops 57982058496 | tf_op jit(solution)/shard_map/project_back/pallas_call | solution.py:141
  627.8 2.4 collective-permute-done.19
  630.1 18.0 %wgrad.11 = (bf16[4,1024,256]{2,1,0:T(8,128)(2,1)}, bf16[4,1024,256]{2,1,0:T(8,128)(2,1)}, bf16[4,1024,256]{2,1,0:T(8,128)(2,1)}, bf16[4,1024,256]{2,1,0:T(8,128)(2,1)}) custom-call(s32[8]{0:T(128)} %add.204.order, s32[2,4,8]{2,1,0:T(4,128)} %constant.77.clone.tables, bf16[4,2,128,2048]{3,2,1,0:T(8,128)(2,1)} %bitcast.121, ...), custom_call_target="tpu_custom_call" | custom-call | tf_op jit(solution)/shard_map/wgrad/pallas_call | solution.py:588
  648.1 1.5 collective-permute-start.22
  651.7 10.6 %attention_wgrad.2 = (bf16[2,4,256,512]{3,2,1,0:T(8,128)(2,1)}, bf16[2,4,256,512]{3,2,1,0:T(8,128)(2,1)}) custom-call(s32[4]{0:T(128)} %get-tuple-element.192.order, s32[2,4,4]{2,1,0:T(4,128)} %constant.78.clone.tables, bf16[1024,2048]{1,0:T(8,128)(2,1)} %all-gather.6.cloned.1.call-done.rows_in, bf16[1024,2048]{1,0:T(8,128)(2,1)} %all-gather.14.cloned.1.call-done.middle, ...), custom_call_target="tpu_custom_call" | custom-call | tf_op jit(solution)/shard_map/attention_wgrad/pallas_call | solution.py:209
  662.8 1.6 fusion.16
  665.9 2.3 pad_maximum_fusion
  668.2 25.9 %collective-permute-done.22 = bf16[2,2,1024,256]{3,2,1,0:T(8,128)(2,1)} collective-permute-done((bf16[2,2,1024,256]{3,2,1,0:T(8,128)(2,1)}, bf16[2,2,1024,256]{3,2,1,0:T(8,128)(2,1)}, u32[]{:S(2)}, u32[]{:S(2)}) %collective-permute-start.22) | collective-permute-done | bytes 2097184 | tf_op jit(solution)/shard_map/ppermute | solution.py:648
  695.3 2.2 fusion.1
  700.2 2.1 fusion
  706.6 12.1 %attention_wgrad.3 = (bf16[2,4,128,512]{3,2,1,0:T(8,128)(2,1)}, bf16[2,4,128,512]{3,2,1,0:T(8,128)(2,1)}, bf16[2,4,128,512]{3,2,1,0:T(8,128)(2,1)}, bf16[2,4,128,512]{3,2,1,0:T(8,128)(2,1)}) custom-call(s32[4]{0:T(128)} %get-tuple-element.201.order, s32[2,4,4]{2,1,0:T(4,128)} %constant.78.clone.tables, ...), custom_call_target="tpu_custom_call" | custom-call | tf_op jit(solution)/shard_map/attention_wgrad/pallas_call | solution.py:209
  720.7 1.9 fusion.15
  727.2 3.9 collective-permute-done.33
  731.1 2.4 collective-permute-start.34
  733.5 2.3 pad_maximum_fusion.1
  735.8 6.7 collective-permute-done.34
  743.2 1.8 add_convert_fusion
  745.9 4.4 collective-permute-done.28
  751.8 1.7 collective-permute-start.29
  758.9 9.4 %collective-permute-done.35 = f32[20,2048]{1,0:T(8,128)S(1)} collective-permute-done((f32[20,2048]{1,0:T(8,128)S(1)}, f32[20,2048]{1,0:T(8,128)S(1)}, u32[]{:S(2)}, u32[]{:S(2)}) %collective-permute-start.35) | collective-permute-done | bytes 163872 | tf_op jit(solution)/shard_map/ppermute | solution.py:705
  769.7 2.3 pad_maximum_fusion.2
  772.0 2.1 collective-permute-done.36
  777.6 1.8 fusion.12
  779.5 3.2 fusion.11
  (228 shorter events, 65.5 us)
Async XLA Ops:
  7.2 171.6 %copy-start = (bf16[2048,512]{1,0:T(8,128)(2,1)S(1)}, bf16[2048,512]{1,0:T(8,128)(2,1)}, u32[]{:S(2)}) copy-start(bf16[2048,512]{1,0:T(8,128)(2,1)} %param.37) | copy-start | bytes 6291460
  7.2 89.0 %all-gather.6.cloned.1.call-start = ((), (), s32[]{:S(2)}) async-start(), calls=%async_computation.6 | async-start | bytes 5242880 | tf_op jit(solution)/shard_map/all_gather | solution.py:639
  12.6 164.9 %all-gather.8.cloned.1.call-start = ((), (), s32[]{:S(2)}) async-start(), calls=%async_computation.7 | async-start | bytes 5242880 | tf_op jit(solution)/shard_map/all_gather | solution.py:639
  96.2 22.0 %copy-start.32 = (s32[1,1024]{1,0:T(1,128)S(1)}, s32[1,1024]{1,0:T(1,128)}, u32[]{:S(2)}) copy-start(s32[1,1024]{1,0:T(1,128)} %seg_row.3) | copy-start | bytes 12292
  96.3 127.7 %reduce-scatter.7.cloned.1.call-start = ((), (), s32[]{:S(2)}) async-start(), calls=%async_computation.8 | async-start | bytes 2621440 | tf_op jit(solution)/shard_map/reduce_scatter | solution.py:643
  112.6 4.0 collective-permute-start
  117.3 6.7 collective-permute-start.1
  181.4 88.5 %reduce-scatter.9.cloned.1.call-start = ((), (), s32[]{:S(2)}) async-start(), calls=%async_computation.9 | async-start | bytes 2621440 | tf_op jit(solution)/shard_map/reduce_scatter | solution.py:643
  184.1 42.6 %copy-start.29 = (s32[1024,8]{0,1:T(8,128)S(1)}, s32[1024,8]{0,1:T(8,128)}, u32[]{:S(2)}) copy-start(s32[1024,8]{0,1:T(8,128)} %param.32) | copy-start | bytes 98308
  184.1 42.8 %copy-start.28 = (bf16[2048,16]{0,1:T(8,128)(2,1)S(1)}, bf16[2048,16]{0,1:T(8,128)(2,1)}, u32[]{:S(2)}) copy-start(bf16[2048,16]{0,1:T(8,128)(2,1)} %param.41) | copy-start | bytes 196612
  184.1 132.6 %all-gather.10.cloned.1.call-start = ((), (), s32[]{:S(2)}) async-start(), calls=%async_computation.10 | async-start | bytes 2621440 | tf_op jit(solution)/shard_map/all_gather | solution.py:639
  226.5 137.6 %all-gather.12.cloned.1.call-start = ((), (), s32[]{:S(2)}) async-start(), calls=%async_computation.11 | async-start | bytes 2621440 | tf_op jit(solution)/shard_map/all_gather | solution.py:639
  272.5 141.6 %reduce-scatter.13.cloned.1.call-start = ((), (), s32[]{:S(2)}) async-start(), calls=%async_computation.13 | async-start | bytes 2785280 | tf_op jit(solution)/shard_map/reduce_scatter | solution.py:643
  364.1 108.4 %reduce-scatter.11.cloned.1.call-start = ((), (), s32[]{:S(2)}) async-start(), calls=%async_computation.12 | async-start | bytes 2785280 | tf_op jit(solution)/shard_map/reduce_scatter | solution.py:643
  411.6 150.7 %all-gather.14.cloned.1.call-start = ((), (), s32[]{:S(2)}) async-start(), calls=%async_computation.15 | async-start | bytes 5242880 | tf_op jit(solution)/shard_map/all_gather | solution.py:639
  435.0 18.4 %collective-permute-start.2 = (bf16[2,2048,256]{2,1,0:T(8,128)(2,1)}, bf16[2,2048,256]{2,1,0:T(8,128)(2,1)}, u32[]{:S(2)}, u32[]{:S(2)}) collective-permute-start(bf16[2,2048,256]{2,1,0:T(8,128)(2,1)} %get-tuple-element.143), channel_id=1, source_target_pairs={{0,4},{4,0},{8,12},{12,8},{16,20},{20,16},{24,28},{28,24},{1,5},{5... | collective-permute-start | bytes 6291464 | tf_op jit(solution)/shard_map/ppermute | solution.py:648
  435.0 18.4 %collective-permute-start.3 = (bf16[2,2048,256]{2,1,0:T(8,128)(2,1)}, bf16[2,2048,256]{2,1,0:T(8,128)(2,1)}, u32[]{:S(2)}, u32[]{:S(2)}) collective-permute-start(bf16[2,2048,256]{2,1,0:T(8,128)(2,1)} %get-tuple-element.144), channel_id=1, source_target_pairs={{0,4},{4,0},{8,12},{12,8},{16,20},{20,16},{24,28},{28,24},{1,5},{5... | collective-permute-start | bytes 6291464 | tf_op jit(solution)/shard_map/ppermute | solution.py:648
  435.5 17.9 %collective-permute-start.4 = (bf16[2,2048,256]{2,1,0:T(8,128)(2,1)}, bf16[2,2048,256]{2,1,0:T(8,128)(2,1)}, u32[]{:S(2)}, u32[]{:S(2)}) collective-permute-start(bf16[2,2048,256]{2,1,0:T(8,128)(2,1)} %get-tuple-element.145), channel_id=1, source_target_pairs={{0,4},{4,0},{8,12},{12,8},{16,20},{20,16},{24,28},{28,24},{1,5},{5... | collective-permute-start | bytes 6291464 | tf_op jit(solution)/shard_map/ppermute | solution.py:648
  435.5 17.8 %collective-permute-start.5 = (bf16[2,2048,256]{2,1,0:T(8,128)(2,1)}, bf16[2,2048,256]{2,1,0:T(8,128)(2,1)}, u32[]{:S(2)}, u32[]{:S(2)}) collective-permute-start(bf16[2,2048,256]{2,1,0:T(8,128)(2,1)} %get-tuple-element.146), channel_id=1, source_target_pairs={{0,4},{4,0},{8,12},{12,8},{16,20},{20,16},{24,28},{28,24},{1,5},{5... | collective-permute-start | bytes 6291464 | tf_op jit(solution)/shard_map/ppermute | solution.py:648
  476.7 265.8 %reduce-scatter.15.cloned.1.call-start = ((), (), s32[]{:S(2)}) async-start(), calls=%async_computation.14 | async-start | bytes 5242880 | tf_op jit(solution)/shard_map/reduce_scatter | solution.py:643
  476.7 4.4 collective-permute-start.6
  476.9 10.3 %collective-permute-start.7 = (bf16[2,2048,256]{2,1,0:T(8,128)(2,1)}, bf16[2,2048,256]{2,1,0:T(8,128)(2,1)S(1)}, u32[]{:S(2)}, u32[]{:S(2)}) collective-permute-start(bf16[2,2048,256]{2,1,0:T(8,128)(2,1)} %get-tuple-element.151), channel_id=1, source_target_pairs={{0,4},{4,0},{8,12},{12,8},{16,20},{20,16},{24,28},{28,24},{1,5},{5... | collective-permute-start | bytes 6291464 | tf_op jit(solution)/shard_map/ppermute | solution.py:648
  477.3 10.0 %collective-permute-start.8 = (bf16[2,2048,256]{2,1,0:T(8,128)(2,1)}, bf16[2,2048,256]{2,1,0:T(8,128)(2,1)}, u32[]{:S(2)}, u32[]{:S(2)}) collective-permute-start(bf16[2,2048,256]{2,1,0:T(8,128)(2,1)} %get-tuple-element.152), channel_id=1, source_target_pairs={{0,4},{4,0},{8,12},{12,8},{16,20},{20,16},{24,28},{28,24},{1,5},{5... | collective-permute-start | bytes 6291464 | tf_op jit(solution)/shard_map/ppermute | solution.py:648
  477.4 12.9 %collective-permute-start.9 = (bf16[2,2048,256]{2,1,0:T(8,128)(2,1)}, bf16[2,2048,256]{2,1,0:T(8,128)(2,1)}, u32[]{:S(2)}, u32[]{:S(2)}) collective-permute-start(bf16[2,2048,256]{2,1,0:T(8,128)(2,1)} %get-tuple-element.153), channel_id=1, source_target_pairs={{0,4},{4,0},{8,12},{12,8},{16,20},{20,16},{24,28},{28,24},{1,5},{5... | collective-permute-start | bytes 6291464 | tf_op jit(solution)/shard_map/ppermute | solution.py:648
  477.8 58.3 %collective-permute-start.10 = (bf16[2,2,1024,256]{3,2,1,0:T(8,128)(2,1)}, bf16[2,2,1024,256]{3,2,1,0:T(8,128)(2,1)}, u32[]{:S(2)}, u32[]{:S(2)}) collective-permute-start(bf16[2,2,1024,256]{3,2,1,0:T(8,128)(2,1)} %bitcast.169), channel_id=1, source_target_pairs={{0,16},{4,20},{8,24},{12,28},{16,0},{20,4},{24,8},{28,12},{1,17},{... | collective-permute-start | bytes 6291464 | tf_op jit(solution)/shard_map/ppermute | solution.py:648
  481.2 9.1 %copy-start.22 = (bf16[2,2048,256]{2,1,0:T(8,128)(2,1)}, bf16[2,2048,256]{2,1,0:T(8,128)(2,1)S(1)}, u32[]{:S(2)}) copy-start(bf16[2,2048,256]{2,1,0:T(8,128)(2,1)S(1)} %collective-permute-done.6.refs_4_) | copy-start | bytes 6291460
  481.2 55.0 %collective-permute-start.11 = (bf16[2,2,1024,256]{3,2,1,0:T(8,128)(2,1)}, bf16[2,2,1024,256]{3,2,1,0:T(8,128)(2,1)}, u32[]{:S(2)}, u32[]{:S(2)}) collective-permute-start(bf16[2,2,1024,256]{3,2,1,0:T(8,128)(2,1)} %bitcast.168), channel_id=1, source_target_pairs={{0,8},{4,12},{8,0},{12,4},{16,24},{20,28},{24,16},{28,20},{1,9},{5... | collective-permute-start | bytes 6291464 | tf_op jit(solution)/shard_map/ppermute | solution.py:648
  509.1 85.8 %collective-permute-start.14 = (bf16[2,2,1024,256]{3,2,1,0:T(8,128)(2,1)}, bf16[2,2,1024,256]{3,2,1,0:T(8,128)(2,1)}, u32[]{:S(2)}, u32[]{:S(2)}) collective-permute-start(bf16[2,2,1024,256]{3,2,1,0:T(8,128)(2,1)} %bitcast.171), channel_id=1, source_target_pairs={{0,16},{4,20},{8,24},{12,28},{16,0},{20,4},{24,8},{28,12},{1,17},{... | collective-permute-start | bytes 6291464 | tf_op jit(solution)/shard_map/ppermute | solution.py:648
  510.7 84.8 %collective-permute-start.15 = (bf16[2,2,1024,256]{3,2,1,0:T(8,128)(2,1)}, bf16[2,2,1024,256]{3,2,1,0:T(8,128)(2,1)}, u32[]{:S(2)}, u32[]{:S(2)}) collective-permute-start(bf16[2,2,1024,256]{3,2,1,0:T(8,128)(2,1)} %bitcast.170), channel_id=1, source_target_pairs={{0,8},{4,12},{8,0},{12,4},{16,24},{20,28},{24,16},{28,20},{1,9},{5... | collective-permute-start | bytes 6291464 | tf_op jit(solution)/shard_map/ppermute | solution.py:648
  536.1 241.0 %reduce-scatter.17.cloned.1.call-start = ((), (), s32[]{:S(2)}) async-start(), calls=%async_computation.16 | async-start | bytes 5242880 | tf_op jit(solution)/shard_map/reduce_scatter | solution.py:643
  543.3 58.9 %collective-permute-start.16 = (bf16[1,2,1024,256]{3,2,1,0:T(8,128)(2,1)S(1)}, bf16[1,2,1024,256]{3,2,1,0:T(8,128)(2,1)}, u32[]{:S(2)}, u32[]{:S(2)}) collective-permute-start(bf16[1,2,1024,256]{3,2,1,0:T(8,128)(2,1)S(1)} %slice.128), channel_id=1, source_target_pairs={{0,8},{4,12},{8,0},{12,4},{16,24},{20,28},{24,16},{28,20},{1,9},{5... | collective-permute-start | bytes 3145736 | tf_op jit(solution)/shard_map/ppermute | solution.py:648
  545.8 56.5 %collective-permute-start.17 = (bf16[1,2,1024,256]{3,2,1,0:T(8,128)(2,1)}, bf16[1,2,1024,256]{3,2,1,0:T(8,128)(2,1)}, u32[]{:S(2)}, u32[]{:S(2)}) collective-permute-start(bf16[1,2,1024,256]{3,2,1,0:T(8,128)(2,1)} %slice_bitcast_fusion.5), channel_id=1, source_target_pairs={{0,16},{4,20},{8,24},{12,28},{16,0},{20,4},{24,8},{28,12},{1,17},{... | collective-permute-start | bytes 3145736 | tf_op jit(solution)/shard_map/ppermute | solution.py:648
  562.3 67.9 %collective-permute-start.20 = (bf16[4,2048,256]{2,1,0:T(8,128)(2,1)}, bf16[4,2048,256]{2,1,0:T(8,128)(2,1)}, u32[]{:S(2)}, u32[]{:S(2)}) collective-permute-start(bf16[4,2048,256]{2,1,0:T(8,128)(2,1)} %get-tuple-element.174), channel_id=1, source_target_pairs={{0,4},{4,0},{8,12},{12,8},{16,20},{20,16},{24,28},{28,24},{1,5},{5... | collective-permute-start | bytes 12582920 | tf_op jit(solution)/shard_map/ppermute | solution.py:648
  594.9 35.2 %collective-permute-start.21 = (bf16[4,2048,256]{2,1,0:T(8,128)(2,1)}, bf16[4,2048,256]{2,1,0:T(8,128)(2,1)}, u32[]{:S(2)}, u32[]{:S(2)}) collective-permute-start(bf16[4,2048,256]{2,1,0:T(8,128)(2,1)} %get-tuple-element.175), channel_id=1, source_target_pairs={{0,4},{4,0},{8,12},{12,8},{16,20},{20,16},{24,28},{28,24},{1,5},{5... | collective-permute-start | bytes 12582920 | tf_op jit(solution)/shard_map/ppermute | solution.py:648
  595.4 7.3 collective-permute-start.12
  602.3 25.5 %collective-permute-start.18 = (bf16[1,2,1024,256]{3,2,1,0:T(8,128)(2,1)}, bf16[1,2,1024,256]{3,2,1,0:T(8,128)(2,1)}, u32[]{:S(2)}, u32[]{:S(2)}) collective-permute-start(bf16[1,2,1024,256]{3,2,1,0:T(8,128)(2,1)} %slice.130), channel_id=1, source_target_pairs={{0,8},{4,12},{8,0},{12,4},{16,24},{20,28},{24,16},{28,20},{1,9},{5... | collective-permute-start | bytes 3145736 | tf_op jit(solution)/shard_map/ppermute | solution.py:648
  602.7 7.7 collective-permute-start.13
  605.5 24.6 %collective-permute-start.19 = (bf16[1,2,1024,256]{3,2,1,0:T(8,128)(2,1)}, bf16[1,2,1024,256]{3,2,1,0:T(8,128)(2,1)}, u32[]{:S(2)}, u32[]{:S(2)}) collective-permute-start(bf16[1,2,1024,256]{3,2,1,0:T(8,128)(2,1)} %slice_bitcast_fusion.4), channel_id=1, source_target_pairs={{0,16},{4,20},{8,24},{12,28},{16,0},{20,4},{24,8},{28,12},{1,17},{... | collective-permute-start | bytes 3145736 | tf_op jit(solution)/shard_map/ppermute | solution.py:648
  626.6 24.4 %copy-start.14 = (bf16[128,2048]{1,0:T(8,128)(2,1)S(1)}, bf16[128,2048]{1,0:T(8,128)(2,1)}, u32[]{:S(2)}) copy-start(bf16[128,2048]{1,0:T(8,128)(2,1)} %get-tuple-element.124.normed) | copy-start | bytes 1572868
  626.6 24.4 %copy-start.30 = (bf16[128,128]{1,0:T(8,128)(2,1)S(1)}, bf16[128,128]{1,0:T(8,128)(2,1)}, u32[]{:S(2)}) copy-start(bf16[128,128]{1,0:T(8,128)(2,1)} %get-tuple-element.212) | copy-start | bytes 98308
  626.6 24.7 %copy-start.35 = (f32[1,2048]{1,0:T(1,128)S(1)}, f32[1,2048]{1,0:T(1,128)}, u32[]{:S(2)}) copy-start(f32[1,2048]{1,0:T(1,128)} %get-tuple-element.210) | copy-start | bytes 24580
  626.6 24.7 %copy-start.36 = (f32[1,2048]{1,0:T(1,128)S(1)}, f32[1,2048]{1,0:T(1,128)}, u32[]{:S(2)}) copy-start(f32[1,2048]{1,0:T(1,128)} %get-tuple-element.211) | copy-start | bytes 24580
  626.6 24.7 %copy-start.15 = (bf16[128,2048]{1,0:T(8,128)(2,1)S(1)}, bf16[128,2048]{1,0:T(8,128)(2,1)}, u32[]{:S(2)}) copy-start(bf16[128,2048]{1,0:T(8,128)(2,1)} %get-tuple-element.132.normed) | copy-start | bytes 1572868
  626.6 24.7 %copy-start.31 = (bf16[128,128]{1,0:T(8,128)(2,1)S(1)}, bf16[128,128]{1,0:T(8,128)(2,1)}, u32[]{:S(2)}) copy-start(bf16[128,128]{1,0:T(8,128)(2,1)} %get-tuple-element.213) | copy-start | bytes 98308
  648.1 46.0 %collective-permute-start.22 = (bf16[2,2,1024,256]{3,2,1,0:T(8,128)(2,1)}, bf16[2,2,1024,256]{3,2,1,0:T(8,128)(2,1)}, u32[]{:S(2)}, u32[]{:S(2)}) collective-permute-start(bf16[2,2,1024,256]{3,2,1,0:T(8,128)(2,1)} %bitcast.173), channel_id=1, source_target_pairs={{0,16},{4,20},{8,24},{12,28},{16,0},{20,4},{24,8},{28,12},{1,17},{... | collective-permute-start | bytes 6291464 | tf_op jit(solution)/shard_map/ppermute | solution.py:648
  649.7 45.6 %collective-permute-start.23 = (bf16[2,2,1024,256]{3,2,1,0:T(8,128)(2,1)}, bf16[2,2,1024,256]{3,2,1,0:T(8,128)(2,1)}, u32[]{:S(2)}, u32[]{:S(2)}) collective-permute-start(bf16[2,2,1024,256]{3,2,1,0:T(8,128)(2,1)} %bitcast.172), channel_id=1, source_target_pairs={{0,8},{4,12},{8,0},{12,4},{16,24},{20,28},{24,16},{28,20},{1,9},{5... | collective-permute-start | bytes 6291464 | tf_op jit(solution)/shard_map/ppermute | solution.py:648
  651.7 11.1 %copy-start.8 = (bf16[2,2,1024,256]{3,2,1,0:T(8,128)(2,1)S(1)}, bf16[2,2,1024,256]{3,2,1,0:T(8,128)(2,1)}, u32[]{:S(2)}) copy-start(bf16[2,2,1024,256]{3,2,1,0:T(8,128)(2,1)} %copy-done.7) | copy-start | bytes 6291460
  662.3 43.0 %collective-permute-start.26 = (bf16[2,4,256,512]{3,2,1,0:T(8,128)(2,1)}, bf16[2,4,256,512]{3,2,1,0:T(8,128)(2,1)S(1)}, u32[]{:S(2)}, u32[]{:S(2)}) collective-permute-start(bf16[2,4,256,512]{3,2,1,0:T(8,128)(2,1)} %get-tuple-element.195), channel_id=1, source_target_pairs={{0,4},{4,0},{8,12},{12,8},{16,20},{20,16},{24,28},{28,24},{1,5},{5... | collective-permute-start | bytes 6291464 | tf_op jit(solution)/shard_map/ppermute | solution.py:648
  662.3 43.0 %collective-permute-start.27 = (bf16[2,4,256,512]{3,2,1,0:T(8,128)(2,1)}, bf16[2,4,256,512]{3,2,1,0:T(8,128)(2,1)}, u32[]{:S(2)}, u32[]{:S(2)}) collective-permute-start(bf16[2,4,256,512]{3,2,1,0:T(8,128)(2,1)} %get-tuple-element.196), channel_id=1, source_target_pairs={{0,4},{4,0},{8,12},{12,8},{16,20},{20,16},{24,28},{28,24},{1,5},{5... | collective-permute-start | bytes 6291464 | tf_op jit(solution)/shard_map/ppermute | solution.py:648
  665.9 29.4 %copy-start.21 = (bf16[4,1024,256]{2,1,0:T(8,128)(2,1)S(1)}, bf16[4,1024,256]{2,1,0:T(8,128)(2,1)}, u32[]{:S(2)}) copy-start(bf16[4,1024,256]{2,1,0:T(8,128)(2,1)} %get-tuple-element.188) | copy-start | bytes 6291460
  698.5 44.0 %collective-permute-start.24 = (bf16[1,2,1024,256]{3,2,1,0:T(8,128)(2,1)}, bf16[1,2,1024,256]{3,2,1,0:T(8,128)(2,1)}, u32[]{:S(2)}, u32[]{:S(2)}) collective-permute-start(bf16[1,2,1024,256]{3,2,1,0:T(8,128)(2,1)} %slice.132), channel_id=1, source_target_pairs={{0,8},{4,12},{8,0},{12,4},{16,24},{20,28},{24,16},{28,20},{1,9},{5... | collective-permute-start | bytes 3145736 | tf_op jit(solution)/shard_map/ppermute | solution.py:648
  704.7 37.8 %collective-permute-start.25 = (bf16[1,2,1024,256]{3,2,1,0:T(8,128)(2,1)}, bf16[1,2,1024,256]{3,2,1,0:T(8,128)(2,1)}, u32[]{:S(2)}, u32[]{:S(2)}) collective-permute-start(bf16[1,2,1024,256]{3,2,1,0:T(8,128)(2,1)} %slice_bitcast_fusion.3), channel_id=1, source_target_pairs={{0,16},{4,20},{8,24},{12,28},{16,0},{20,4},{24,8},{28,12},{1,17},{... | collective-permute-start | bytes 3145736 | tf_op jit(solution)/shard_map/ppermute | solution.py:648
  705.3 14.7 %copy-start.39 = (f32[1,512]{1,0:T(1,128)S(1)}, f32[1,512]{1,0:T(1,128)}, u32[]{:S(2)}) copy-start(f32[1,512]{1,0:T(1,128)} %get-tuple-element.209) | copy-start | bytes 6148
  705.3 14.8 %copy-start.27 = (f32[2048]{0:T(1024)S(1)}, f32[2048]{0:T(1024)}, u32[]{:S(2)}) copy-start(f32[2048]{0:T(1024)} %param.33) | copy-start | bytes 24580
  705.3 14.8 %copy-start.37 = (f32[1,2048]{1,0:T(1,128)S(1)}, f32[1,2048]{1,0:T(1,128)}, u32[]{:S(2)}) copy-start(f32[1,2048]{1,0:T(1,128)} %get-tuple-element.207) | copy-start | bytes 24580
  718.7 24.5 %collective-permute-start.30 = (bf16[2,4,128,512]{3,2,1,0:T(8,128)(2,1)}, bf16[2,4,128,512]{3,2,1,0:T(8,128)(2,1)}, u32[]{:S(2)}, u32[]{:S(2)}) collective-permute-start(bf16[2,4,128,512]{3,2,1,0:T(8,128)(2,1)} %get-tuple-element.203), channel_id=1, source_target_pairs={{0,8},{4,12},{8,0},{12,4},{16,24},{20,28},{24,16},{28,20},{1,9},{5... | collective-permute-start | bytes 3145736 | tf_op jit(solution)/shard_map/ppermute | solution.py:648
  720.6 3.5 collective-permute-start.32
  722.6 27.6 %collective-permute-start.28 = (bf16[2,4,128,512]{3,2,1,0:T(8,128)(2,1)}, bf16[2,4,128,512]{3,2,1,0:T(8,128)(2,1)}, u32[]{:S(2)}, u32[]{:S(2)}) collective-permute-start(bf16[2,4,128,512]{3,2,1,0:T(8,128)(2,1)} %get-tuple-element.202), channel_id=1, source_target_pairs={{0,16},{4,20},{8,24},{12,28},{16,0},{20,4},{24,8},{28,12},{1,17},{... | collective-permute-start | bytes 3145736 | tf_op jit(solution)/shard_map/ppermute | solution.py:648
  724.1 6.9 collective-permute-start.33
  731.1 11.3 %collective-permute-start.34 = (f32[20,2048]{1,0:T(8,128)S(1)}, f32[20,2048]{1,0:T(8,128)S(1)}, u32[]{:S(2)}, u32[]{:S(2)}) collective-permute-start(f32[20,2048]{1,0:T(8,128)S(1)} %add.229), channel_id=1, source_target_pairs={{0,2},{1,3},{2,0},{3,1},{4,6},{5,7},{6,4},{7,5},{8,10},{9,11},{10,... | collective-permute-start | bytes 491528 | tf_op jit(solution)/shard_map/ppermute | solution.py:705
  745.1 30.3 %collective-permute-start.31 = (bf16[1,4,128,512]{3,2,1,0:T(8,128)(2,1)S(1)}, bf16[1,4,128,512]{3,2,1,0:T(8,128)(2,1)S(1)}, u32[]{:S(2)}, u32[]{:S(2)}) collective-permute-start(bf16[1,4,128,512]{3,2,1,0:T(8,128)(2,1)S(1)} %slice_bitcast_fusion.6), channel_id=1, source_target_pairs={{0,16},{4,20},{8,24},{12,28},{16,0},{20,4},{24,8},{28,12},{1,17},{... | collective-permute-start | bytes 1572872 | tf_op jit(solution)/shard_map/ppermute | solution.py:648
  751.8 23.7 %collective-permute-start.29 = (bf16[1,4,128,512]{3,2,1,0:T(8,128)(2,1)S(1)}, bf16[1,4,128,512]{3,2,1,0:T(8,128)(2,1)S(1)}, u32[]{:S(2)}, u32[]{:S(2)}) collective-permute-start(bf16[1,4,128,512]{3,2,1,0:T(8,128)(2,1)S(1)} %slice.135), channel_id=1, source_target_pairs={{0,8},{4,12},{8,0},{12,4},{16,24},{20,28},{24,16},{28,20},{1,9},{5... | collective-permute-start | bytes 1572872 | tf_op jit(solution)/shard_map/ppermute | solution.py:648
  753.6 14.7 %collective-permute-start.35 = (f32[20,2048]{1,0:T(8,128)S(1)}, f32[20,2048]{1,0:T(8,128)S(1)}, u32[]{:S(2)}, u32[]{:S(2)}) collective-permute-start(f32[20,2048]{1,0:T(8,128)S(1)} %add.230), channel_id=1, source_target_pairs={{0,8},{4,12},{8,0},{12,4},{16,24},{20,28},{24,16},{28,20},{1,9},{5... | collective-permute-start | bytes 491528 | tf_op jit(solution)/shard_map/ppermute | solution.py:705
  768.3 5.7 collective-permute-start.36
  (26 other events, 80.1 us)
Sparse Core Ops, SparseCore 0:
  12.7 83.4 all-gather.5
  97.8 79.6 all-gather.7
  181.6 42.3 reduce-scatter.6
  226.8 43.1 reduce-scatter.8
  271.4 45.2 all-gather.9
  318.7 44.6 all-gather.11
  365.7 44.7 reduce-scatter.12
  412.7 45.3 reduce-scatter.10
  476.8 79.8 all-gather.13
  558.9 75.6 reduce-scatter.14
  637.0 77.2 reduce-scatter.16

commit v11 on v10

--- a/solution.py
+++ b/solution.py
@@ -751,11 +751,11 @@
     query, key, attended, lse = attend(
         qraw, kraw, value, q_scale, k_scale, q_gain, k_gain, cosine, sine, seg_ids[0], keep_mask[0]
     )
-    attended_parts = [chunk_of(gate(attended, grad_rows), c) for c in chunks]
+    attended_parts = [chunk_of(attended, c) for c in chunks]
     outs = [nt(attended_parts[0], w_out).astype(bf16)]
-    summed = [scatter_rows(outs[0])]
+    summed = [scatter_rows(gate(outs[0], grad_rows))]
     outs.append(nt(gate(attended_parts[1], outs[0]), w_out).astype(bf16))
-    summed.append(scatter_rows(outs[1]))
+    summed.append(scatter_rows(gate(outs[1], grad_rows)))
 
     idle_routes, idle_router = gate((routes, router), outs[1])
     expert_ids = jnp.arange(LANES)
@@ -796,7 +796,7 @@
     first = back_of(0, gate(expert_grads[0], acts[1]))
     gate_sent = expert_sums(ffn_parts, dgates, theirs, first[1], weight=0)
     gate_got = core_swap(gate_sent)
-    up_sent = expert_sums(ffn_parts, dups, theirs, *gate_sent, weight=4)
+    up_sent = expert_sums(ffn_parts, dups, theirs, *gate_sent, pieces=2, weight=4)
     up_got = core_swap(up_sent)
     gate_sums = expert_sums(ffn_parts, dgates, mine, *up_sent, added=gate_got, weight=4)
     gate_out = halving(gate_sums)

time: 797 us -> 795 us (level)
    ppermute x28 -> x26, starting transfers between devices: 22.2 us -> 21.7 us  [pair_swap(): return lax.ppermute(values, 'dp', [(i, i ^ step) for i in range(size)])]
    ppermute x28 -> x26, waiting for transfers between devices: 45.2 us -> 45.7 us  [pair_swap(): return lax.ppermute(values, 'dp', [(i, i ^ step) for i in range(size)])]
  transfers between devices with their start and end apart: 48 -> 46, of which waited for: 22 -> 20; matrix products, arithmetic and copies ran while one was open for 9% -> 10% of each run, Pallas kernels for 44% -> 44%
where the time goes in v11:
time: 795 us; the launch traced here: 787 us
  Pallas kernels  351 us (44%)
  waiting for transfers between devices  295 us (37%)
  other arithmetic  56.8 us (7%)
  starting transfers between devices  31.2 us (4%)
  local copies, waits for them, and re-layouts  26.8 us (3%)
  between operations  14.9 us (2%)
  matrix products  12.1 us (2%)
    all_gather x5, waiting for transfers between devices, gather_rows(): return lax.all_gather(values, 'tensor', axis=0, tiled=True)  159 us
    pallas_call x6, Pallas kernels, wgrad(): pl.pallas_call(functools.partial(wgrad_kernel, len(lefts), len(added), he...  103 us
    pallas_call x2, Pallas kernels, experts_block(): pl.pallas_call(functools.partial(expert_kernel, block), grid=(experts,),...  94.9 us
    reduce_scatter x6, waiting for transfers between devices, scatter_rows(): return lax.psum_scatter(values, 'tensor', scatter_dimension=0, tiled=True)  55 us
    ppermute x26, waiting for transfers between devices, pair_swap(): return lax.ppermute(values, 'dp', [(i, i ^ step) for i in range(size)])  45.7 us
    ppermute x9, waiting for transfers between devices, exchange_sum(): lax.ppermute(values, axis, [(i, i ^ step) for i in range(lax.axis_size(ax...  34.3 us
    pallas_call x1, Pallas kernels, down(): pl.pallas_call(functools.partial(down_kernel, parts), grid=(features // b...  23.9 us
    pallas_call x1, Pallas kernels, attend_back(): pl.pallas_call(functools.partial(attend_back_kernel, block), grid=(width...  23.9 us
  transfers between devices with their start and end apart: 46, of which 20 were waited for; matrix products, arithmetic and copies ran while one was open for 10% of the time, Pallas kernels for 44%

profile of v11, /device:TPU:0, one launch (start us, length us, event | category | flops | bytes accessed | tf_op | source)
XLA Modules:
  0.0 787.1 jit_solution(10278082818132344127)
XLA Ops:
  7.2 1.6 fusion.6
  10.1 2.5 fusion.8
  12.6 83.6 %all-gather.6.cloned.1.call-done.rows_in = bf16[1024,2048]{1,0:T(8,128)(2,1)} async-done(((bf16[256,2048]{1,0:T(8,128)(2,1)}), bf16[1024,2048]{1,0:T(8,128)(2,1)}) %all-gather.6.cloned.1.call-update) | async-done | bytes 4194320 | tf_op jit(solution)/shard_map/all_gather | solution.py:639
  96.3 16.3 %project.1 = (f32[1024,512]{1,0:T(8,128)}, f32[1024,512]{1,0:T(8,128)}, bf16[1024,512]{1,0:T(8,128)(2,1)}, f32[2,1024]{1,0:T(2,128)}) custom-call(bf16[1024,2048]{1,0:T(8,128)(2,1)} %all-gather.6.cloned.1.call-done.rows_in, bf16[2048,512]{1,0:T(8,128)(2,1)} %w_query.3, bf16[2048,512]{1,0:T(8,128)(2,1)} %w_key.3, bf16[2048,512]{1,0:T(8,128)(2,1)} %w_value.3), custom_call_target="tpu_custom_call" | custom-call | flops 2899102976 | bytes 1310720 | tf_op jit(solution)/shard_map/project/pallas_call | solution.py:101
  112.6 4.0 collective-permute-done
  119.3 4.8 collective-permute-done.1
  126.1 15.7 %attend.1 = (bf16[1024,512]{1,0:T(8,128)(2,1)}, bf16[1024,512]{1,0:T(8,128)(2,1)}, bf16[1024,512]{1,0:T(8,128)(2,1)}, f32[1024,512]{1,0:T(8,128)}) custom-call(f32[1024,512]{1,0:T(8,128)} %get-tuple-element.114.qraw, f32[1024,512]{1,0:T(8,128)} %get-tuple-element.115.kraw, bf16[1024,512]{1,0:T(8,128)(2,1)} %get-tuple-element.116.value, ...), custom_call_target="tpu_custom_call" | custom-call | flops 57347878912 | bytes 1179648 | tf_op jit(solution)/shard_map/attend/pallas_call | solution.py:259
  143.1 2.7 convolution_convert_fusion.1
  145.7 31.7 %all-gather.8.cloned.1.call-done.grad = bf16[1024,2048]{1,0:T(8,128)(2,1)} async-done(((bf16[256,2048]{1,0:T(8,128)(2,1)}), bf16[1024,2048]{1,0:T(8,128)(2,1)}) %all-gather.8.cloned.1.call-update) | async-done | bytes 4194320 | tf_op jit(solution)/shard_map/all_gather | solution.py:639
  177.5 2.6 convolution_convert_fusion
  180.2 42.5 %reduce-scatter.7.cloned.1.call-done.summed = bf16[128,2048]{1,0:T(8,128)(2,1)} async-done(((bf16[512,2048]{1,0:T(8,128)(2,1)}), bf16[128,2048]{1,0:T(8,128)(2,1)}) %reduce-scatter.7.cloned.1.call-update) | async-done | bytes 524304 | tf_op jit(solution)/shard_map/reduce_scatter | solution.py:643
  222.7 2.5 middle.2
  227.0 5.7 convert_reduce_fusion
  233.6 22.6 %up_back.1 = bf16[1024,4096]{1,0:T(8,128)(2,1)} custom-call(bf16[1024,2048]{1,0:T(8,128)(2,1)} %all-gather.8.cloned.1.call-done.grad, bf16[16,2048,256]{2,1,0:T(8,128)(2,1)} %down_w.3), custom_call_target="tpu_custom_call" | custom-call | flops 7730940928 | bytes 2621440 | tf_op jit(solution)/shard_map/up_back/pallas_call | solution.py:417
  256.3 12.5 %reduce-scatter.9.cloned.1.call-done.summed = bf16[128,2048]{1,0:T(8,128)(2,1)} async-done(((bf16[512,2048]{1,0:T(8,128)(2,1)}), bf16[128,2048]{1,0:T(8,128)(2,1)}) %reduce-scatter.9.cloned.1.call-update) | async-done | bytes 524304 | tf_op jit(solution)/shard_map/reduce_scatter | solution.py:643
  268.8 2.5 middle.3
  271.4 44.1 %all-gather.10.cloned.1.call-done.rows_in.refs_0_ = bf16[512,2048]{1,0:T(8,128)(2,1)} async-done(((bf16[128,2048]{1,0:T(8,128)(2,1)}), bf16[512,2048]{1,0:T(8,128)(2,1)}) %all-gather.10.cloned.1.call-update) | async-done | bytes 2097168 | tf_op jit(solution)/shard_map/all_gather | solution.py:639
  315.5 47.4 %experts.2 = (bf16[512,4096]{1,0:T(8,128)(2,1)}, bf16[512,4096]{1,0:T(8,128)(2,1)}, bf16[512,4096]{1,0:T(8,128)(2,1)}, bf16[512,2176]{1,0:T(8,128)(2,1)}) custom-call(bf16[512,2048]{1,0:T(8,128)(2,1)} %all-gather.10.cloned.1.call-done.rows_in.refs_0_, bf16[4,2,128,4096]{3,2,1,0:T(8,128)(2,1)} %bitcast.124, f32[512,128]{1,0:T(8,128)} %bitcast.144, ...), custom_call_target="tpu_custom_call" | custom-call | flops 53210619904 | bytes 6291456 | tf_op jit(solution)/shard_map/experts/pallas_call | solution.py:483
  362.9 47.5 %experts.3 = (bf16[512,4096]{1,0:T(8,128)(2,1)}, bf16[512,4096]{1,0:T(8,128)(2,1)}, bf16[512,4096]{1,0:T(8,128)(2,1)}, bf16[512,2176]{1,0:T(8,128)(2,1)}) custom-call(bf16[512,2048]{1,0:T(8,128)(2,1)} %all-gather.12.cloned.1.call-done.rows_in.refs_1_, bf16[4,2,128,4096]{3,2,1,0:T(8,128)(2,1)} %bitcast.125, f32[512,128]{1,0:T(8,128)} %bitcast.143, ...), custom_call_target="tpu_custom_call" | custom-call | flops 53210619904 | bytes 6291456 | tf_op jit(solution)/shard_map/experts/pallas_call | solution.py:483
  413.0 4.3 middle_back.2
  417.3 16.6 %wgrad.6 = (bf16[2,2048,256]{2,1,0:T(8,128)(2,1)}, bf16[2,2048,256]{2,1,0:T(8,128)(2,1)}, bf16[2,2048,256]{2,1,0:T(8,128)(2,1)}, bf16[2,2048,256]{2,1,0:T(8,128)(2,1)}) custom-call(s32[8]{0:T(128)} %add.209.order, s32[2,4,8]{2,1,0:T(4,128)} %constant.77.clone.tables, bf16[512,2048]{1,0:T(8,128)(2,1)} %all-gather.10.cloned.1.call-done.rows_in.refs_0_, ...), custom_call_target="tpu_custom_call" | custom-call | tf_op jit(solution)/shard_map/wgrad/pallas_call | solution.py:588
  435.7 15.6 %wgrad.7 = (bf16[4,2048,256]{2,1,0:T(8,128)(2,1)}, bf16[4,2048,256]{2,1,0:T(8,128)(2,1)}) custom-call(s32[8]{0:T(128)} %add.209.order, s32[2,4,8]{2,1,0:T(4,128)} %constant.77.clone.tables, bf16[512,2048]{1,0:T(8,128)(2,1)} %all-gather.10.cloned.1.call-done.rows_in.refs_0_, bf16[512,2048]{1,0:T(8,128)(2,1)} %all-gather.12.cloned.1.call-done.rows_in.refs_1_, ...), custom_call_target="tpu_custom_call" | custom-call | flops 15461881856 | tf_op jit(solution)/shard_map/wgrad/pallas_call | solution.py:588
  451.3 18.9 %wgrad.8 = (bf16[4,1024,256]{2,1,0:T(8,128)(2,1)}, bf16[4,1024,256]{2,1,0:T(8,128)(2,1)}, bf16[4,1024,256]{2,1,0:T(8,128)(2,1)}, bf16[4,1024,256]{2,1,0:T(8,128)(2,1)}) custom-call(s32[8]{0:T(128)} %add.204.order, s32[2,4,8]{2,1,0:T(4,128)} %constant.77.clone.tables, bf16[512,2048]{1,0:T(8,128)(2,1)} %all-gather.10.cloned.1.call-done.rows_in.refs_0_, ...), custom_call_target="tpu_custom_call" | custom-call | flops 15461881856 | tf_op jit(solution)/shard_map/wgrad/pallas_call | solution.py:588
  470.3 4.2 middle_back.3
  478.1 9.1 %collective-permute-done.6.refs_4_ = bf16[4,2048,256]{2,1,0:T(8,128)(2,1)S(1)} collective-permute-done((bf16[4,2048,256]{2,1,0:T(8,128)(2,1)}, bf16[4,2048,256]{2,1,0:T(8,128)(2,1)S(1)}, u32[]{:S(2)}, u32[]{:S(2)}) %collective-permute-start.6) | collective-permute-done | bytes 4194336 | tf_op jit(solution)/shard_map/ppermute | solution.py:648
  489.2 17.9 %wgrad.9 = (bf16[4,1024,256]{2,1,0:T(8,128)(2,1)}, bf16[4,1024,256]{2,1,0:T(8,128)(2,1)}, bf16[4,1024,256]{2,1,0:T(8,128)(2,1)}, bf16[4,1024,256]{2,1,0:T(8,128)(2,1)}) custom-call(s32[8]{0:T(128)} %add.204.order, s32[2,4,8]{2,1,0:T(4,128)} %constant.77.clone.tables, bf16[512,2048]{1,0:T(8,128)(2,1)} %all-gather.10.cloned.1.call-done.rows_in.refs_0_, ...), custom_call_target="tpu_custom_call" | custom-call | tf_op jit(solution)/shard_map/wgrad/pallas_call | solution.py:588
  510.0 23.9 %down.1 = bf16[1024,2048]{1,0:T(8,128)(2,1)} custom-call(bf16[16,2048,256]{2,1,0:T(8,128)(2,1)} %down_w.3, bf16[512,4096]{1,0:T(8,128)(2,1)} %get-tuple-element.166.refs_0_.refs_2_, bf16[512,4096]{1,0:T(8,128)(2,1)} %get-tuple-element.136.refs_1_.refs_3_), custom_call_target="tpu_custom_call" | custom-call | tf_op jit(solution)/shard_map/down/pallas_call | solution.py:621
  534.0 2.7 fusion.5
  536.8 2.3 copy-done.20
  539.1 2.1 fusion.4
  544.2 15.9 %wgrad.10 = (bf16[4,2048,256]{2,1,0:T(8,128)(2,1)}, bf16[4,2048,256]{2,1,0:T(8,128)(2,1)}) custom-call(s32[8]{0:T(128)} %add.209.order, s32[2,4,8]{2,1,0:T(4,128)} %constant.77.clone.tables, bf16[4,2,128,2048]{3,2,1,0:T(8,128)(2,1)} %bitcast.119, bf16[4,2,128,2048]{3,2,1,0:T(8,128)(2,1)} %bitcast.120, bf16[512,4096]{1,0:T(8,128)(2,1)} %get-tuple-element.166.refs_0_.refs_2_, ...), custom_call_target="tpu_custom_call" | custom-call | tf_op jit(solution)/shard_map/wgrad/pallas_call | solution.py:588
  560.2 6.2 convolution_convert_fusion.2.out_grad
  566.4 23.9 %attend_back.1 = (f32[1024,512]{1,0:T(8,128)}, f32[1024,512]{1,0:T(8,128)}, bf16[1024,512]{1,0:T(8,128)(2,1)}, f32[1024,1]{1,0:T(8,128)}, f32[1024,1]{1,0:T(8,128)}, /*index=5*/f32[1,512]{1,0:T(1,128)}, f32[1,512]{1,0:T(1,128)}) custom-call(bf16[1024,512]{1,0:T(8,128)(2,1)} %get-tuple-element.167.query, bf16[1024,512]{1,0:T(8,128)(2,1)} %get-tuple-element.168.key, ...), custom_call_target="tpu_custom_call" | custom-call | tf_op jit(solution)/shard_map/attend_back/pallas_call | solution.py:325
  593.3 2.8 fusion.3
  596.2 2.8 fusion.2
  600.7 1.7 collective-permute-start.11
  604.8 3.6 collective-permute-done.11
  610.5 14.2 %project_back.1 = (bf16[1024,2048]{1,0:T(8,128)(2,1)}, bf16[1024,512]{1,0:T(8,128)(2,1)}, bf16[1024,512]{1,0:T(8,128)(2,1)}, f32[1,2048]{1,0:T(1,128)}) custom-call(bf16[1024,2048]{1,0:T(8,128)(2,1)} %all-gather.6.cloned.1.call-done.rows_in, f32[1024,512]{1,0:T(8,128)} %get-tuple-element.176.dqn, f32[1024,512]{1,0:T(8,128)} %get-tuple-element.177.dkn, ...), custom_call_target="tpu_custom_call" | custom-call | flops 57982058496 | tf_op jit(solution)/shard_map/project_back/pallas_call | solution.py:141
  625.7 2.3 collective-permute-done.17
  628.0 18.0 %wgrad.11 = (bf16[4,1024,256]{2,1,0:T(8,128)(2,1)}, bf16[4,1024,256]{2,1,0:T(8,128)(2,1)}, bf16[4,1024,256]{2,1,0:T(8,128)(2,1)}, bf16[4,1024,256]{2,1,0:T(8,128)(2,1)}) custom-call(s32[8]{0:T(128)} %add.204.order, s32[2,4,8]{2,1,0:T(4,128)} %constant.77.clone.tables, bf16[4,2,128,2048]{3,2,1,0:T(8,128)(2,1)} %bitcast.121, ...), custom_call_target="tpu_custom_call" | custom-call | tf_op jit(solution)/shard_map/wgrad/pallas_call | solution.py:588
  646.0 1.5 collective-permute-start.20
  649.6 10.5 %attention_wgrad.2 = (bf16[2,4,256,512]{3,2,1,0:T(8,128)(2,1)}, bf16[2,4,256,512]{3,2,1,0:T(8,128)(2,1)}) custom-call(s32[4]{0:T(128)} %get-tuple-element.190.order, s32[2,4,4]{2,1,0:T(4,128)} %constant.78.clone.tables, bf16[1024,2048]{1,0:T(8,128)(2,1)} %all-gather.6.cloned.1.call-done.rows_in, bf16[1024,2048]{1,0:T(8,128)(2,1)} %all-gather.14.cloned.1.call-done.middle, ...), custom_call_target="tpu_custom_call" | custom-call | tf_op jit(solution)/shard_map/attention_wgrad/pallas_call | solution.py:209
  660.7 1.6 fusion.16
  663.8 2.3 pad_maximum_fusion
  666.1 25.9 %collective-permute-done.20 = bf16[2,2,1024,256]{3,2,1,0:T(8,128)(2,1)} collective-permute-done((bf16[2,2,1024,256]{3,2,1,0:T(8,128)(2,1)}, bf16[2,2,1024,256]{3,2,1,0:T(8,128)(2,1)}, u32[]{:S(2)}, u32[]{:S(2)}) %collective-permute-start.20) | collective-permute-done | bytes 2097184 | tf_op jit(solution)/shard_map/ppermute | solution.py:648
  693.1 2.2 fusion.1
  698.1 2.1 fusion
  704.4 12.1 %attention_wgrad.3 = (bf16[2,4,128,512]{3,2,1,0:T(8,128)(2,1)}, bf16[2,4,128,512]{3,2,1,0:T(8,128)(2,1)}, bf16[2,4,128,512]{3,2,1,0:T(8,128)(2,1)}, bf16[2,4,128,512]{3,2,1,0:T(8,128)(2,1)}) custom-call(s32[4]{0:T(128)} %get-tuple-element.199.order, s32[2,4,4]{2,1,0:T(4,128)} %constant.78.clone.tables, ...), custom_call_target="tpu_custom_call" | custom-call | tf_op jit(solution)/shard_map/attention_wgrad/pallas_call | solution.py:209
  718.4 1.9 fusion.15
  720.3 1.5 collective-permute-start.26
  724.7 4.1 collective-permute-done.31
  728.8 2.3 collective-permute-start.32
  731.1 2.3 pad_maximum_fusion.1
  733.4 6.8 collective-permute-done.32
  741.1 1.8 add_convert_fusion
  743.7 4.5 collective-permute-done.26
  748.2 1.5 add_convert_fusion.1
  749.8 1.7 collective-permute-start.27
  756.9 9.1 %collective-permute-done.33 = f32[20,2048]{1,0:T(8,128)S(1)} collective-permute-done((f32[20,2048]{1,0:T(8,128)S(1)}, f32[20,2048]{1,0:T(8,128)S(1)}, u32[]{:S(2)}, u32[]{:S(2)}) %collective-permute-start.33) | collective-permute-done | bytes 163872 | tf_op jit(solution)/shard_map/ppermute | solution.py:705
  766.0 1.5 collective-permute-start.34
  767.5 2.3 pad_maximum_fusion.2
  769.8 1.9 collective-permute-done.34
  775.3 1.8 fusion.12
  777.2 3.2 fusion.11
  (222 shorter events, 63.8 us)
Async XLA Ops:
  7.2 135.9 %copy-start = (bf16[2048,512]{1,0:T(8,128)(2,1)S(1)}, bf16[2048,512]{1,0:T(8,128)(2,1)}, u32[]{:S(2)}) copy-start(bf16[2048,512]{1,0:T(8,128)(2,1)} %param.37) | copy-start | bytes 6291460
  7.2 89.0 %all-gather.6.cloned.1.call-start = ((), (), s32[]{:S(2)}) async-start(), calls=%async_computation.6 | async-start | bytes 5242880 | tf_op jit(solution)/shard_map/all_gather | solution.py:639
  12.6 164.9 %all-gather.8.cloned.1.call-start = ((), (), s32[]{:S(2)}) async-start(), calls=%async_computation.7 | async-start | bytes 5242880 | tf_op jit(solution)/shard_map/all_gather | solution.py:639
  96.2 22.0 %copy-start.31 = (s32[1,1024]{1,0:T(1,128)S(1)}, s32[1,1024]{1,0:T(1,128)}, u32[]{:S(2)}) copy-start(s32[1,1024]{1,0:T(1,128)} %seg_row.3) | copy-start | bytes 12292
  96.2 126.5 %reduce-scatter.7.cloned.1.call-start = ((), (), s32[]{:S(2)}) async-start(), calls=%async_computation.8 | async-start | bytes 2621440 | tf_op jit(solution)/shard_map/reduce_scatter | solution.py:643
  112.6 4.0 collective-permute-start
  117.3 6.7 collective-permute-start.1
  177.5 91.3 %reduce-scatter.9.cloned.1.call-start = ((), (), s32[]{:S(2)}) async-start(), calls=%async_computation.9 | async-start | bytes 2621440 | tf_op jit(solution)/shard_map/reduce_scatter | solution.py:643
  180.1 45.5 %copy-start.28 = (s32[1024,8]{0,1:T(8,128)S(1)}, s32[1024,8]{0,1:T(8,128)}, u32[]{:S(2)}) copy-start(s32[1024,8]{0,1:T(8,128)} %param.32) | copy-start | bytes 98308
  180.1 45.7 %copy-start.27 = (bf16[2048,16]{0,1:T(8,128)(2,1)S(1)}, bf16[2048,16]{0,1:T(8,128)(2,1)}, u32[]{:S(2)}) copy-start(bf16[2048,16]{0,1:T(8,128)(2,1)} %param.41) | copy-start | bytes 196612
  180.1 135.3 %all-gather.10.cloned.1.call-start = ((), (), s32[]{:S(2)}) async-start(), calls=%async_computation.10 | async-start | bytes 2621440 | tf_op jit(solution)/shard_map/all_gather | solution.py:639
  225.2 137.7 %all-gather.12.cloned.1.call-start = ((), (), s32[]{:S(2)}) async-start(), calls=%async_computation.11 | async-start | bytes 2621440 | tf_op jit(solution)/shard_map/all_gather | solution.py:639
  271.3 141.7 %reduce-scatter.13.cloned.1.call-start = ((), (), s32[]{:S(2)}) async-start(), calls=%async_computation.13 | async-start | bytes 2785280 | tf_op jit(solution)/shard_map/reduce_scatter | solution.py:643
  362.9 107.4 %reduce-scatter.11.cloned.1.call-start = ((), (), s32[]{:S(2)}) async-start(), calls=%async_computation.12 | async-start | bytes 2785280 | tf_op jit(solution)/shard_map/reduce_scatter | solution.py:643
  410.5 149.6 %all-gather.14.cloned.1.call-start = ((), (), s32[]{:S(2)}) async-start(), calls=%async_computation.15 | async-start | bytes 5242880 | tf_op jit(solution)/shard_map/all_gather | solution.py:639
  433.9 17.4 %collective-permute-start.2 = (bf16[2,2048,256]{2,1,0:T(8,128)(2,1)}, bf16[2,2048,256]{2,1,0:T(8,128)(2,1)}, u32[]{:S(2)}, u32[]{:S(2)}) collective-permute-start(bf16[2,2048,256]{2,1,0:T(8,128)(2,1)} %get-tuple-element.143), channel_id=1, source_target_pairs={{0,4},{4,0},{8,12},{12,8},{16,20},{20,16},{24,28},{28,24},{1,5},{5... | collective-permute-start | bytes 6291464 | tf_op jit(solution)/shard_map/ppermute | solution.py:648
  433.9 17.4 %collective-permute-start.3 = (bf16[2,2048,256]{2,1,0:T(8,128)(2,1)}, bf16[2,2048,256]{2,1,0:T(8,128)(2,1)}, u32[]{:S(2)}, u32[]{:S(2)}) collective-permute-start(bf16[2,2048,256]{2,1,0:T(8,128)(2,1)} %get-tuple-element.144), channel_id=1, source_target_pairs={{0,4},{4,0},{8,12},{12,8},{16,20},{20,16},{24,28},{28,24},{1,5},{5... | collective-permute-start | bytes 6291464 | tf_op jit(solution)/shard_map/ppermute | solution.py:648
  434.4 16.9 %collective-permute-start.4 = (bf16[2,2048,256]{2,1,0:T(8,128)(2,1)}, bf16[2,2048,256]{2,1,0:T(8,128)(2,1)}, u32[]{:S(2)}, u32[]{:S(2)}) collective-permute-start(bf16[2,2048,256]{2,1,0:T(8,128)(2,1)} %get-tuple-element.145), channel_id=1, source_target_pairs={{0,4},{4,0},{8,12},{12,8},{16,20},{20,16},{24,28},{28,24},{1,5},{5... | collective-permute-start | bytes 6291464 | tf_op jit(solution)/shard_map/ppermute | solution.py:648
  434.5 16.8 %collective-permute-start.5 = (bf16[2,2048,256]{2,1,0:T(8,128)(2,1)}, bf16[2,2048,256]{2,1,0:T(8,128)(2,1)}, u32[]{:S(2)}, u32[]{:S(2)}) collective-permute-start(bf16[2,2048,256]{2,1,0:T(8,128)(2,1)} %get-tuple-element.146), channel_id=1, source_target_pairs={{0,4},{4,0},{8,12},{12,8},{16,20},{20,16},{24,28},{28,24},{1,5},{5... | collective-permute-start | bytes 6291464 | tf_op jit(solution)/shard_map/ppermute | solution.py:648
  474.5 265.7 %reduce-scatter.15.cloned.1.call-start = ((), (), s32[]{:S(2)}) async-start(), calls=%async_computation.14 | async-start | bytes 5242880 | tf_op jit(solution)/shard_map/reduce_scatter | solution.py:643
  474.6 12.6 %collective-permute-start.6 = (bf16[4,2048,256]{2,1,0:T(8,128)(2,1)}, bf16[4,2048,256]{2,1,0:T(8,128)(2,1)S(1)}, u32[]{:S(2)}, u32[]{:S(2)}) collective-permute-start(bf16[4,2048,256]{2,1,0:T(8,128)(2,1)} %get-tuple-element.150), channel_id=1, source_target_pairs={{0,4},{4,0},{8,12},{12,8},{16,20},{20,16},{24,28},{28,24},{1,5},{5... | collective-permute-start | bytes 12582920 | tf_op jit(solution)/shard_map/ppermute | solution.py:648
  474.7 13.4 %collective-permute-start.7 = (bf16[4,2048,256]{2,1,0:T(8,128)(2,1)}, bf16[4,2048,256]{2,1,0:T(8,128)(2,1)}, u32[]{:S(2)}, u32[]{:S(2)}) collective-permute-start(bf16[4,2048,256]{2,1,0:T(8,128)(2,1)} %get-tuple-element.151), channel_id=1, source_target_pairs={{0,4},{4,0},{8,12},{12,8},{16,20},{20,16},{24,28},{28,24},{1,5},{5... | collective-permute-start | bytes 12582920 | tf_op jit(solution)/shard_map/ppermute | solution.py:648
  475.1 58.9 %collective-permute-start.8 = (bf16[2,2,1024,256]{3,2,1,0:T(8,128)(2,1)}, bf16[2,2,1024,256]{3,2,1,0:T(8,128)(2,1)}, u32[]{:S(2)}, u32[]{:S(2)}) collective-permute-start(bf16[2,2,1024,256]{3,2,1,0:T(8,128)(2,1)} %bitcast.170), channel_id=1, source_target_pairs={{0,16},{4,20},{8,24},{12,28},{16,0},{20,4},{24,8},{28,12},{1,17},{... | collective-permute-start | bytes 6291464 | tf_op jit(solution)/shard_map/ppermute | solution.py:648
  476.6 57.4 %collective-permute-start.9 = (bf16[2,2,1024,256]{3,2,1,0:T(8,128)(2,1)}, bf16[2,2,1024,256]{3,2,1,0:T(8,128)(2,1)}, u32[]{:S(2)}, u32[]{:S(2)}) collective-permute-start(bf16[2,2,1024,256]{3,2,1,0:T(8,128)(2,1)} %bitcast.169), channel_id=1, source_target_pairs={{0,8},{4,12},{8,0},{12,4},{16,24},{20,28},{24,16},{28,20},{1,9},{5... | collective-permute-start | bytes 6291464 | tf_op jit(solution)/shard_map/ppermute | solution.py:648
  507.1 85.7 %collective-permute-start.12 = (bf16[2,2,1024,256]{3,2,1,0:T(8,128)(2,1)}, bf16[2,2,1024,256]{3,2,1,0:T(8,128)(2,1)}, u32[]{:S(2)}, u32[]{:S(2)}) collective-permute-start(bf16[2,2,1024,256]{3,2,1,0:T(8,128)(2,1)} %bitcast.171), channel_id=1, source_target_pairs={{0,16},{4,20},{8,24},{12,28},{16,0},{20,4},{24,8},{28,12},{1,17},{... | collective-permute-start | bytes 6291464 | tf_op jit(solution)/shard_map/ppermute | solution.py:648
  508.6 84.7 %collective-permute-start.13 = (bf16[2,2,1024,256]{3,2,1,0:T(8,128)(2,1)}, bf16[2,2,1024,256]{3,2,1,0:T(8,128)(2,1)}, u32[]{:S(2)}, u32[]{:S(2)}) collective-permute-start(bf16[2,2,1024,256]{3,2,1,0:T(8,128)(2,1)} %bitcast.168), channel_id=1, source_target_pairs={{0,8},{4,12},{8,0},{12,4},{16,24},{20,28},{24,16},{28,20},{1,9},{5... | collective-permute-start | bytes 6291464 | tf_op jit(solution)/shard_map/ppermute | solution.py:648
  534.0 240.8 %reduce-scatter.17.cloned.1.call-start = ((), (), s32[]{:S(2)}) async-start(), calls=%async_computation.16 | async-start | bytes 5242880 | tf_op jit(solution)/shard_map/reduce_scatter | solution.py:643
  541.2 59.0 %collective-permute-start.14 = (bf16[1,2,1024,256]{3,2,1,0:T(8,128)(2,1)S(1)}, bf16[1,2,1024,256]{3,2,1,0:T(8,128)(2,1)}, u32[]{:S(2)}, u32[]{:S(2)}) collective-permute-start(bf16[1,2,1024,256]{3,2,1,0:T(8,128)(2,1)S(1)} %slice.128), channel_id=1, source_target_pairs={{0,8},{4,12},{8,0},{12,4},{16,24},{20,28},{24,16},{28,20},{1,9},{5... | collective-permute-start | bytes 3145736 | tf_op jit(solution)/shard_map/ppermute | solution.py:648
  543.5 56.6 %collective-permute-start.15 = (bf16[1,2,1024,256]{3,2,1,0:T(8,128)(2,1)}, bf16[1,2,1024,256]{3,2,1,0:T(8,128)(2,1)}, u32[]{:S(2)}, u32[]{:S(2)}) collective-permute-start(bf16[1,2,1024,256]{3,2,1,0:T(8,128)(2,1)} %slice_bitcast_fusion.5), channel_id=1, source_target_pairs={{0,16},{4,20},{8,24},{12,28},{16,0},{20,4},{24,8},{28,12},{1,17},{... | collective-permute-start | bytes 3145736 | tf_op jit(solution)/shard_map/ppermute | solution.py:648
  560.1 67.9 %collective-permute-start.18 = (bf16[4,2048,256]{2,1,0:T(8,128)(2,1)}, bf16[4,2048,256]{2,1,0:T(8,128)(2,1)}, u32[]{:S(2)}, u32[]{:S(2)}) collective-permute-start(bf16[4,2048,256]{2,1,0:T(8,128)(2,1)} %get-tuple-element.172), channel_id=1, source_target_pairs={{0,4},{4,0},{8,12},{12,8},{16,20},{20,16},{24,28},{28,24},{1,5},{5... | collective-permute-start | bytes 12582920 | tf_op jit(solution)/shard_map/ppermute | solution.py:648
  592.8 35.2 %collective-permute-start.19 = (bf16[4,2048,256]{2,1,0:T(8,128)(2,1)}, bf16[4,2048,256]{2,1,0:T(8,128)(2,1)}, u32[]{:S(2)}, u32[]{:S(2)}) collective-permute-start(bf16[4,2048,256]{2,1,0:T(8,128)(2,1)} %get-tuple-element.173), channel_id=1, source_target_pairs={{0,4},{4,0},{8,12},{12,8},{16,20},{20,16},{24,28},{28,24},{1,5},{5... | collective-permute-start | bytes 12582920 | tf_op jit(solution)/shard_map/ppermute | solution.py:648
  593.3 7.4 collective-permute-start.10
  600.2 25.5 %collective-permute-start.16 = (bf16[1,2,1024,256]{3,2,1,0:T(8,128)(2,1)}, bf16[1,2,1024,256]{3,2,1,0:T(8,128)(2,1)}, u32[]{:S(2)}, u32[]{:S(2)}) collective-permute-start(bf16[1,2,1024,256]{3,2,1,0:T(8,128)(2,1)} %slice.130), channel_id=1, source_target_pairs={{0,8},{4,12},{8,0},{12,4},{16,24},{20,28},{24,16},{28,20},{1,9},{5... | collective-permute-start | bytes 3145736 | tf_op jit(solution)/shard_map/ppermute | solution.py:648
  600.7 7.7 collective-permute-start.11
  603.4 24.6 %collective-permute-start.17 = (bf16[1,2,1024,256]{3,2,1,0:T(8,128)(2,1)}, bf16[1,2,1024,256]{3,2,1,0:T(8,128)(2,1)}, u32[]{:S(2)}, u32[]{:S(2)}) collective-permute-start(bf16[1,2,1024,256]{3,2,1,0:T(8,128)(2,1)} %slice_bitcast_fusion.4), channel_id=1, source_target_pairs={{0,16},{4,20},{8,24},{12,28},{16,0},{20,4},{24,8},{28,12},{1,17},{... | collective-permute-start | bytes 3145736 | tf_op jit(solution)/shard_map/ppermute | solution.py:648
  624.7 24.1 %copy-start.14 = (bf16[128,2048]{1,0:T(8,128)(2,1)S(1)}, bf16[128,2048]{1,0:T(8,128)(2,1)}, u32[]{:S(2)}) copy-start(bf16[128,2048]{1,0:T(8,128)(2,1)} %get-tuple-element.124.normed) | copy-start | bytes 1572868
  624.7 24.1 %copy-start.29 = (bf16[128,128]{1,0:T(8,128)(2,1)S(1)}, bf16[128,128]{1,0:T(8,128)(2,1)}, u32[]{:S(2)}) copy-start(bf16[128,128]{1,0:T(8,128)(2,1)} %get-tuple-element.210) | copy-start | bytes 98308
  624.8 24.4 %copy-start.34 = (f32[1,2048]{1,0:T(1,128)S(1)}, f32[1,2048]{1,0:T(1,128)}, u32[]{:S(2)}) copy-start(f32[1,2048]{1,0:T(1,128)} %get-tuple-element.208) | copy-start | bytes 24580
  624.8 24.4 %copy-start.35 = (f32[1,2048]{1,0:T(1,128)S(1)}, f32[1,2048]{1,0:T(1,128)}, u32[]{:S(2)}) copy-start(f32[1,2048]{1,0:T(1,128)} %get-tuple-element.209) | copy-start | bytes 24580
  624.8 24.4 %copy-start.15 = (bf16[128,2048]{1,0:T(8,128)(2,1)S(1)}, bf16[128,2048]{1,0:T(8,128)(2,1)}, u32[]{:S(2)}) copy-start(bf16[128,2048]{1,0:T(8,128)(2,1)} %get-tuple-element.132.normed) | copy-start | bytes 1572868
  624.8 24.4 %copy-start.30 = (bf16[128,128]{1,0:T(8,128)(2,1)S(1)}, bf16[128,128]{1,0:T(8,128)(2,1)}, u32[]{:S(2)}) copy-start(bf16[128,128]{1,0:T(8,128)(2,1)} %get-tuple-element.211) | copy-start | bytes 98308
  646.0 46.0 %collective-permute-start.20 = (bf16[2,2,1024,256]{3,2,1,0:T(8,128)(2,1)}, bf16[2,2,1024,256]{3,2,1,0:T(8,128)(2,1)}, u32[]{:S(2)}, u32[]{:S(2)}) collective-permute-start(bf16[2,2,1024,256]{3,2,1,0:T(8,128)(2,1)} %bitcast.173), channel_id=1, source_target_pairs={{0,16},{4,20},{8,24},{12,28},{16,0},{20,4},{24,8},{28,12},{1,17},{... | collective-permute-start | bytes 6291464 | tf_op jit(solution)/shard_map/ppermute | solution.py:648
  647.5 45.6 %collective-permute-start.21 = (bf16[2,2,1024,256]{3,2,1,0:T(8,128)(2,1)}, bf16[2,2,1024,256]{3,2,1,0:T(8,128)(2,1)}, u32[]{:S(2)}, u32[]{:S(2)}) collective-permute-start(bf16[2,2,1024,256]{3,2,1,0:T(8,128)(2,1)} %bitcast.172), channel_id=1, source_target_pairs={{0,8},{4,12},{8,0},{12,4},{16,24},{20,28},{24,16},{28,20},{1,9},{5... | collective-permute-start | bytes 6291464 | tf_op jit(solution)/shard_map/ppermute | solution.py:648
  649.6 11.1 %copy-start.8 = (bf16[2,2,1024,256]{3,2,1,0:T(8,128)(2,1)S(1)}, bf16[2,2,1024,256]{3,2,1,0:T(8,128)(2,1)}, u32[]{:S(2)}) copy-start(bf16[2,2,1024,256]{3,2,1,0:T(8,128)(2,1)} %copy-done.7) | copy-start | bytes 6291460
  660.1 43.0 %collective-permute-start.24 = (bf16[2,4,256,512]{3,2,1,0:T(8,128)(2,1)}, bf16[2,4,256,512]{3,2,1,0:T(8,128)(2,1)S(1)}, u32[]{:S(2)}, u32[]{:S(2)}) collective-permute-start(bf16[2,4,256,512]{3,2,1,0:T(8,128)(2,1)} %get-tuple-element.193), channel_id=1, source_target_pairs={{0,4},{4,0},{8,12},{12,8},{16,20},{20,16},{24,28},{28,24},{1,5},{5... | collective-permute-start | bytes 6291464 | tf_op jit(solution)/shard_map/ppermute | solution.py:648
  660.2 43.0 %collective-permute-start.25 = (bf16[2,4,256,512]{3,2,1,0:T(8,128)(2,1)}, bf16[2,4,256,512]{3,2,1,0:T(8,128)(2,1)}, u32[]{:S(2)}, u32[]{:S(2)}) collective-permute-start(bf16[2,4,256,512]{3,2,1,0:T(8,128)(2,1)} %get-tuple-element.194), channel_id=1, source_target_pairs={{0,4},{4,0},{8,12},{12,8},{16,20},{20,16},{24,28},{28,24},{1,5},{5... | collective-permute-start | bytes 6291464 | tf_op jit(solution)/shard_map/ppermute | solution.py:648
  663.8 29.4 %copy-start.22 = (bf16[4,1024,256]{2,1,0:T(8,128)(2,1)S(1)}, bf16[4,1024,256]{2,1,0:T(8,128)(2,1)}, u32[]{:S(2)}) copy-start(bf16[4,1024,256]{2,1,0:T(8,128)(2,1)} %get-tuple-element.186) | copy-start | bytes 6291460
  696.4 43.9 %collective-permute-start.22 = (bf16[1,2,1024,256]{3,2,1,0:T(8,128)(2,1)}, bf16[1,2,1024,256]{3,2,1,0:T(8,128)(2,1)}, u32[]{:S(2)}, u32[]{:S(2)}) collective-permute-start(bf16[1,2,1024,256]{3,2,1,0:T(8,128)(2,1)} %slice.132), channel_id=1, source_target_pairs={{0,8},{4,12},{8,0},{12,4},{16,24},{20,28},{24,16},{28,20},{1,9},{5... | collective-permute-start | bytes 3145736 | tf_op jit(solution)/shard_map/ppermute | solution.py:648
  702.5 37.8 %collective-permute-start.23 = (bf16[1,2,1024,256]{3,2,1,0:T(8,128)(2,1)}, bf16[1,2,1024,256]{3,2,1,0:T(8,128)(2,1)}, u32[]{:S(2)}, u32[]{:S(2)}) collective-permute-start(bf16[1,2,1024,256]{3,2,1,0:T(8,128)(2,1)} %slice_bitcast_fusion.3), channel_id=1, source_target_pairs={{0,16},{4,20},{8,24},{12,28},{16,0},{20,4},{24,8},{28,12},{1,17},{... | collective-permute-start | bytes 3145736 | tf_op jit(solution)/shard_map/ppermute | solution.py:648
  703.1 14.7 %copy-start.38 = (f32[1,512]{1,0:T(1,128)S(1)}, f32[1,512]{1,0:T(1,128)}, u32[]{:S(2)}) copy-start(f32[1,512]{1,0:T(1,128)} %get-tuple-element.207) | copy-start | bytes 6148
  703.1 14.8 %copy-start.26 = (f32[2048]{0:T(1024)S(1)}, f32[2048]{0:T(1024)}, u32[]{:S(2)}) copy-start(f32[2048]{0:T(1024)} %param.33) | copy-start | bytes 24580
  703.1 14.8 %copy-start.36 = (f32[1,2048]{1,0:T(1,128)S(1)}, f32[1,2048]{1,0:T(1,128)}, u32[]{:S(2)}) copy-start(f32[1,2048]{1,0:T(1,128)} %get-tuple-element.205) | copy-start | bytes 24580
  716.6 24.5 %collective-permute-start.28 = (bf16[2,4,128,512]{3,2,1,0:T(8,128)(2,1)}, bf16[2,4,128,512]{3,2,1,0:T(8,128)(2,1)}, u32[]{:S(2)}, u32[]{:S(2)}) collective-permute-start(bf16[2,4,128,512]{3,2,1,0:T(8,128)(2,1)} %get-tuple-element.201), channel_id=1, source_target_pairs={{0,8},{4,12},{8,0},{12,4},{16,24},{20,28},{24,16},{28,20},{1,9},{5... | collective-permute-start | bytes 3145736 | tf_op jit(solution)/shard_map/ppermute | solution.py:648
  718.3 4.9 copy-start.3
  718.3 3.5 collective-permute-start.30
  720.3 27.9 %collective-permute-start.26 = (bf16[2,4,128,512]{3,2,1,0:T(8,128)(2,1)}, bf16[2,4,128,512]{3,2,1,0:T(8,128)(2,1)}, u32[]{:S(2)}, u32[]{:S(2)}) collective-permute-start(bf16[2,4,128,512]{3,2,1,0:T(8,128)(2,1)} %get-tuple-element.200), channel_id=1, source_target_pairs={{0,16},{4,20},{8,24},{12,28},{16,0},{20,4},{24,8},{28,12},{1,17},{... | collective-permute-start | bytes 3145736 | tf_op jit(solution)/shard_map/ppermute | solution.py:648
  721.9 6.9 collective-permute-start.31
  728.8 11.3 %collective-permute-start.32 = (f32[20,2048]{1,0:T(8,128)S(1)}, f32[20,2048]{1,0:T(8,128)S(1)}, u32[]{:S(2)}, u32[]{:S(2)}) collective-permute-start(f32[20,2048]{1,0:T(8,128)S(1)} %add.229), channel_id=1, source_target_pairs={{0,2},{1,3},{2,0},{3,1},{4,6},{5,7},{6,4},{7,5},{8,10},{9,11},{10,... | collective-permute-start | bytes 491528 | tf_op jit(solution)/shard_map/ppermute | solution.py:705
  740.2 8.0 %copy-start.24 = (bf16[2,4,128,512]{3,2,1,0:T(8,128)(2,1)S(1)}, bf16[2,4,128,512]{3,2,1,0:T(8,128)(2,1)}, u32[]{:S(2)}) copy-start(bf16[2,4,128,512]{3,2,1,0:T(8,128)(2,1)} %get-tuple-element.203) | copy-start | bytes 3145732
  743.0 8.9 %copy-start.12 = (bf16[2,2,1024,256]{3,2,1,0:T(8,128)(2,1)S(1)}, bf16[2,2,1024,256]{3,2,1,0:T(8,128)(2,1)}, u32[]{:S(2)}) copy-start(bf16[2,2,1024,256]{3,2,1,0:T(8,128)(2,1)} %copy-done.11) | copy-start | bytes 6291460
  743.0 30.1 %collective-permute-start.29 = (bf16[1,4,128,512]{3,2,1,0:T(8,128)(2,1)S(1)}, bf16[1,4,128,512]{3,2,1,0:T(8,128)(2,1)S(1)}, u32[]{:S(2)}, u32[]{:S(2)}) collective-permute-start(bf16[1,4,128,512]{3,2,1,0:T(8,128)(2,1)S(1)} %slice_bitcast_fusion.6), channel_id=1, source_target_pairs={{0,16},{4,20},{8,24},{12,28},{16,0},{20,4},{24,8},{28,12},{1,17},{... | collective-permute-start | bytes 1572872 | tf_op jit(solution)/shard_map/ppermute | solution.py:648
  749.8 23.5 %collective-permute-start.27 = (bf16[1,4,128,512]{3,2,1,0:T(8,128)(2,1)S(1)}, bf16[1,4,128,512]{3,2,1,0:T(8,128)(2,1)S(1)}, u32[]{:S(2)}, u32[]{:S(2)}) collective-permute-start(bf16[1,4,128,512]{3,2,1,0:T(8,128)(2,1)S(1)} %slice.135), channel_id=1, source_target_pairs={{0,8},{4,12},{8,0},{12,4},{16,24},{20,28},{24,16},{28,20},{1,9},{5... | collective-permute-start | bytes 1572872 | tf_op jit(solution)/shard_map/ppermute | solution.py:648
  751.5 14.5 %collective-permute-start.33 = (f32[20,2048]{1,0:T(8,128)S(1)}, f32[20,2048]{1,0:T(8,128)S(1)}, u32[]{:S(2)}, u32[]{:S(2)}) collective-permute-start(f32[20,2048]{1,0:T(8,128)S(1)} %add.230), channel_id=1, source_target_pairs={{0,8},{4,12},{8,0},{12,4},{16,24},{20,28},{24,16},{28,20},{1,9},{5... | collective-permute-start | bytes 491528 | tf_op jit(solution)/shard_map/ppermute | solution.py:705
  766.0 5.7 collective-permute-start.34
  (23 other events, 57.2 us)
Sparse Core Ops, SparseCore 0:
  12.7 83.4 all-gather.5
  97.8 79.6 all-gather.7
  180.3 42.3 reduce-scatter.6
  225.5 43.1 reduce-scatter.8
  270.2 45.2 all-gather.9
  317.5 44.6 all-gather.11
  364.5 44.7 reduce-scatter.12
  411.5 45.4 reduce-scatter.10
  474.6 79.9 all-gather.13
  556.7 75.6 reduce-scatter.14
  634.8 77.2 reduce-scatter.16

commit v12 on v11

--- a/solution.py
+++ b/solution.py
@@ -804,12 +804,12 @@
     second = back_of(1, gate(expert_grads[1], *gate_sums), first[:2])
     middle_grad, middle_low = second[:2]
     middle_all = gather_rows(middle_low)
-    up_sums = expert_sums(ffn_parts, dups, mine, middle_low, added=up_got, weight=0)
+    moe = down([gate(acts[0], middle_low), acts[1]], w_down, parts)
+    up_sums = expert_sums(ffn_parts, dups, mine, moe, added=up_got, weight=0)
     up_out = halving(up_sums)
     up_out.send()
-    moe = down([gate(acts[0], *up_sums), acts[1]], w_down, parts)
     moe_sum = scatter_rows(moe)
-    gate_late = gate_out.add(moe)
+    gate_late = gate_out.add(*up_sums)
     gate_out.send()
     down_sent = expert_sums(grad_parts, acts, theirs, *gate_late, pieces=2, weight=0.0)
     down_got = core_swap(down_sent)

time: 795 us -> 789 us (level)
  transfers between devices with their start and end apart: 46 -> 46, of which waited for: 20 -> 21; matrix products, arithmetic and copies ran while one was open for 10% -> 10% of each run, Pallas kernels for 44% -> 44%
where the time goes in v12:
time: 789 us; the launch traced here: 781 us
  Pallas kernels  352 us (45%)
  waiting for transfers between devices  293 us (37%)
  other arithmetic  56.9 us (7%)
  starting transfers between devices  27.9 us (4%)
  local copies, waits for them, and re-layouts  25.8 us (3%)
  between operations  14.9 us (2%)
  matrix products  11.4 us (1%)
    all_gather x5, waiting for transfers between devices, gather_rows(): return lax.all_gather(values, 'tensor', axis=0, tiled=True)  162 us
    pallas_call x6, Pallas kernels, wgrad(): pl.pallas_call(functools.partial(wgrad_kernel, len(lefts), len(added), he...  103 us
    pallas_call x2, Pallas kernels, experts_block(): pl.pallas_call(functools.partial(expert_kernel, block), grid=(experts,),...  94.7 us
    reduce_scatter x6, waiting for transfers between devices, scatter_rows(): return lax.psum_scatter(values, 'tensor', scatter_dimension=0, tiled=True)  54.9 us
    ppermute x26, waiting for transfers between devices, pair_swap(): return lax.ppermute(values, 'dp', [(i, i ^ step) for i in range(size)])  43.7 us
    ppermute x9, waiting for transfers between devices, exchange_sum(): lax.ppermute(values, axis, [(i, i ^ step) for i in range(lax.axis_size(ax...  31.5 us
    pallas_call x1, Pallas kernels, attend_back(): pl.pallas_call(functools.partial(attend_back_kernel, block), grid=(width...  24.6 us
    pallas_call x1, Pallas kernels, down(): pl.pallas_call(functools.partial(down_kernel, parts), grid=(features // b...  24.5 us
  transfers between devices with their start and end apart: 46, of which 21 were waited for; matrix products, arithmetic and copies ran while one was open for 10% of the time, Pallas kernels for 44%

profile of v12, /device:TPU:0, one launch (start us, length us, event | category | flops | bytes accessed | tf_op | source)
XLA Modules:
  0.0 781.2 jit_solution(1769554233016212330)
XLA Ops:
  7.2 1.6 fusion.6
  10.1 2.5 fusion.8
  12.7 83.6 %all-gather.6.cloned.1.call-done.rows_in = bf16[1024,2048]{1,0:T(8,128)(2,1)} async-done(((bf16[256,2048]{1,0:T(8,128)(2,1)}), bf16[1024,2048]{1,0:T(8,128)(2,1)}) %all-gather.6.cloned.1.call-update) | async-done | bytes 4194320 | tf_op jit(solution)/shard_map/all_gather | solution.py:639
  96.3 16.3 %project.1 = (f32[1024,512]{1,0:T(8,128)}, f32[1024,512]{1,0:T(8,128)}, bf16[1024,512]{1,0:T(8,128)(2,1)}, f32[2,1024]{1,0:T(2,128)}) custom-call(bf16[1024,2048]{1,0:T(8,128)(2,1)} %all-gather.6.cloned.1.call-done.rows_in, bf16[2048,512]{1,0:T(8,128)(2,1)} %w_query.3, bf16[2048,512]{1,0:T(8,128)(2,1)} %w_key.3, bf16[2048,512]{1,0:T(8,128)(2,1)} %w_value.3), custom_call_target="tpu_custom_call" | custom-call | flops 2899102976 | bytes 1310720 | tf_op jit(solution)/shard_map/project/pallas_call | solution.py:101
  112.6 4.0 collective-permute-done
  119.3 4.8 collective-permute-done.1
  126.1 15.7 %attend.1 = (bf16[1024,512]{1,0:T(8,128)(2,1)}, bf16[1024,512]{1,0:T(8,128)(2,1)}, bf16[1024,512]{1,0:T(8,128)(2,1)}, f32[1024,512]{1,0:T(8,128)}) custom-call(f32[1024,512]{1,0:T(8,128)} %get-tuple-element.114.qraw, f32[1024,512]{1,0:T(8,128)} %get-tuple-element.115.kraw, bf16[1024,512]{1,0:T(8,128)(2,1)} %get-tuple-element.116.value, ...), custom_call_target="tpu_custom_call" | custom-call | flops 57347878912 | bytes 1179648 | tf_op jit(solution)/shard_map/attend/pallas_call | solution.py:259
  143.1 2.7 convolution_convert_fusion.1
  145.7 31.7 %all-gather.8.cloned.1.call-done.grad = bf16[1024,2048]{1,0:T(8,128)(2,1)} async-done(((bf16[256,2048]{1,0:T(8,128)(2,1)}), bf16[1024,2048]{1,0:T(8,128)(2,1)}) %all-gather.8.cloned.1.call-update) | async-done | bytes 4194320 | tf_op jit(solution)/shard_map/all_gather | solution.py:639
  177.5 2.6 convolution_convert_fusion
  180.2 42.5 %reduce-scatter.7.cloned.1.call-done.summed = bf16[128,2048]{1,0:T(8,128)(2,1)} async-done(((bf16[512,2048]{1,0:T(8,128)(2,1)}), bf16[128,2048]{1,0:T(8,128)(2,1)}) %reduce-scatter.7.cloned.1.call-update) | async-done | bytes 524304 | tf_op jit(solution)/shard_map/reduce_scatter | solution.py:643
  222.7 2.6 middle.2
  227.1 5.7 convert_reduce_fusion
  233.7 22.6 %up_back.1 = bf16[1024,4096]{1,0:T(8,128)(2,1)} custom-call(bf16[1024,2048]{1,0:T(8,128)(2,1)} %all-gather.8.cloned.1.call-done.grad, bf16[16,2048,256]{2,1,0:T(8,128)(2,1)} %down_w.3), custom_call_target="tpu_custom_call" | custom-call | flops 7730940928 | bytes 2621440 | tf_op jit(solution)/shard_map/up_back/pallas_call | solution.py:417
  256.3 12.4 %reduce-scatter.9.cloned.1.call-done.summed = bf16[128,2048]{1,0:T(8,128)(2,1)} async-done(((bf16[512,2048]{1,0:T(8,128)(2,1)}), bf16[128,2048]{1,0:T(8,128)(2,1)}) %reduce-scatter.9.cloned.1.call-update) | async-done | bytes 524304 | tf_op jit(solution)/shard_map/reduce_scatter | solution.py:643
  268.7 2.5 middle.3
  271.3 44.2 %all-gather.10.cloned.1.call-done.rows_in.refs_0_ = bf16[512,2048]{1,0:T(8,128)(2,1)} async-done(((bf16[128,2048]{1,0:T(8,128)(2,1)}), bf16[512,2048]{1,0:T(8,128)(2,1)}) %all-gather.10.cloned.1.call-update) | async-done | bytes 2097168 | tf_op jit(solution)/shard_map/all_gather | solution.py:639
  315.5 47.4 %experts.2 = (bf16[512,4096]{1,0:T(8,128)(2,1)}, bf16[512,4096]{1,0:T(8,128)(2,1)}, bf16[512,4096]{1,0:T(8,128)(2,1)}, bf16[512,2176]{1,0:T(8,128)(2,1)}) custom-call(bf16[512,2048]{1,0:T(8,128)(2,1)} %all-gather.10.cloned.1.call-done.rows_in.refs_0_, bf16[4,2,128,4096]{3,2,1,0:T(8,128)(2,1)} %bitcast.124, f32[512,128]{1,0:T(8,128)} %bitcast.144, ...), custom_call_target="tpu_custom_call" | custom-call | flops 53210619904 | bytes 6291456 | tf_op jit(solution)/shard_map/experts/pallas_call | solution.py:483
  363.0 47.4 %experts.3 = (bf16[512,4096]{1,0:T(8,128)(2,1)}, bf16[512,4096]{1,0:T(8,128)(2,1)}, bf16[512,4096]{1,0:T(8,128)(2,1)}, bf16[512,2176]{1,0:T(8,128)(2,1)}) custom-call(bf16[512,2048]{1,0:T(8,128)(2,1)} %all-gather.12.cloned.1.call-done.rows_in.refs_1_, bf16[4,2,128,4096]{3,2,1,0:T(8,128)(2,1)} %bitcast.125, f32[512,128]{1,0:T(8,128)} %bitcast.143, ...), custom_call_target="tpu_custom_call" | custom-call | flops 53210619904 | bytes 6291456 | tf_op jit(solution)/shard_map/experts/pallas_call | solution.py:483
  412.9 4.2 middle_back.2
  417.1 16.6 %wgrad.6 = (bf16[2,2048,256]{2,1,0:T(8,128)(2,1)}, bf16[2,2048,256]{2,1,0:T(8,128)(2,1)}, bf16[2,2048,256]{2,1,0:T(8,128)(2,1)}, bf16[2,2048,256]{2,1,0:T(8,128)(2,1)}) custom-call(s32[8]{0:T(128)} %add.209.order, s32[2,4,8]{2,1,0:T(4,128)} %constant.77.clone.tables, bf16[512,2048]{1,0:T(8,128)(2,1)} %all-gather.10.cloned.1.call-done.rows_in.refs_0_, ...), custom_call_target="tpu_custom_call" | custom-call | tf_op jit(solution)/shard_map/wgrad/pallas_call | solution.py:588
  435.5 15.6 %wgrad.7 = (bf16[4,2048,256]{2,1,0:T(8,128)(2,1)}, bf16[4,2048,256]{2,1,0:T(8,128)(2,1)}) custom-call(s32[8]{0:T(128)} %add.209.order, s32[2,4,8]{2,1,0:T(4,128)} %constant.77.clone.tables, bf16[512,2048]{1,0:T(8,128)(2,1)} %all-gather.10.cloned.1.call-done.rows_in.refs_0_, bf16[512,2048]{1,0:T(8,128)(2,1)} %all-gather.12.cloned.1.call-done.rows_in.refs_1_, ...), custom_call_target="tpu_custom_call" | custom-call | flops 15461881856 | tf_op jit(solution)/shard_map/wgrad/pallas_call | solution.py:588
  451.1 18.9 %wgrad.8 = (bf16[4,1024,256]{2,1,0:T(8,128)(2,1)}, bf16[4,1024,256]{2,1,0:T(8,128)(2,1)}, bf16[4,1024,256]{2,1,0:T(8,128)(2,1)}, bf16[4,1024,256]{2,1,0:T(8,128)(2,1)}) custom-call(s32[8]{0:T(128)} %add.204.order, s32[2,4,8]{2,1,0:T(4,128)} %constant.77.clone.tables, bf16[512,2048]{1,0:T(8,128)(2,1)} %all-gather.10.cloned.1.call-done.rows_in.refs_0_, ...), custom_call_target="tpu_custom_call" | custom-call | flops 15461881856 | tf_op jit(solution)/shard_map/wgrad/pallas_call | solution.py:588
  470.1 4.2 middle_back.3
  477.9 24.5 %down.1 = bf16[1024,2048]{1,0:T(8,128)(2,1)} custom-call(bf16[16,2048,256]{2,1,0:T(8,128)(2,1)} %down_w.3, bf16[512,4096]{1,0:T(8,128)(2,1)} %get-tuple-element.161.refs_0_.refs_2_, bf16[512,4096]{1,0:T(8,128)(2,1)} %get-tuple-element.136.refs_1_.refs_3_), custom_call_target="tpu_custom_call" | custom-call | tf_op jit(solution)/shard_map/down/pallas_call | solution.py:621
  502.4 17.9 %wgrad.9 = (bf16[4,1024,256]{2,1,0:T(8,128)(2,1)}, bf16[4,1024,256]{2,1,0:T(8,128)(2,1)}, bf16[4,1024,256]{2,1,0:T(8,128)(2,1)}, bf16[4,1024,256]{2,1,0:T(8,128)(2,1)}) custom-call(s32[8]{0:T(128)} %add.204.order, s32[2,4,8]{2,1,0:T(4,128)} %constant.77.clone.tables, bf16[512,2048]{1,0:T(8,128)(2,1)} %all-gather.10.cloned.1.call-done.rows_in.refs_0_, ...), custom_call_target="tpu_custom_call" | custom-call | tf_op jit(solution)/shard_map/wgrad/pallas_call | solution.py:588
  520.8 2.5 collective-permute-done.6
  523.2 2.0 collective-permute-done.7
  525.3 2.7 fusion.5
  528.1 2.3 copy-done.19
  530.3 2.1 fusion.4
  535.7 15.9 %wgrad.10 = (bf16[4,2048,256]{2,1,0:T(8,128)(2,1)}, bf16[4,2048,256]{2,1,0:T(8,128)(2,1)}) custom-call(s32[8]{0:T(128)} %add.209.order, s32[2,4,8]{2,1,0:T(4,128)} %constant.77.clone.tables, bf16[4,2,128,2048]{3,2,1,0:T(8,128)(2,1)} %bitcast.119, bf16[4,2,128,2048]{3,2,1,0:T(8,128)(2,1)} %bitcast.120, bf16[512,4096]{1,0:T(8,128)(2,1)} %get-tuple-element.161.refs_0_.refs_2_, ...), custom_call_target="tpu_custom_call" | custom-call | tf_op jit(solution)/shard_map/wgrad/pallas_call | solution.py:588
  551.6 2.7 all-gather.14.cloned.1.call-done.middle
  554.3 5.5 convolution_convert_fusion.2.out_grad
  559.8 24.6 %attend_back.1 = (f32[1024,512]{1,0:T(8,128)}, f32[1024,512]{1,0:T(8,128)}, bf16[1024,512]{1,0:T(8,128)(2,1)}, f32[1024,1]{1,0:T(8,128)}, f32[1024,1]{1,0:T(8,128)}, /*index=5*/f32[1,512]{1,0:T(1,128)}, f32[1,512]{1,0:T(1,128)}) custom-call(bf16[1024,512]{1,0:T(8,128)(2,1)} %get-tuple-element.162.query, bf16[1024,512]{1,0:T(8,128)(2,1)} %get-tuple-element.163.key, ...), custom_call_target="tpu_custom_call" | custom-call | tf_op jit(solution)/shard_map/attend_back/pallas_call | solution.py:325
  587.2 2.8 fusion.3
  590.0 2.8 fusion.2
  594.0 1.5 collective-permute-start.16
  598.7 3.8 collective-permute-done.11
  604.6 14.3 %project_back.1 = (bf16[1024,2048]{1,0:T(8,128)(2,1)}, bf16[1024,512]{1,0:T(8,128)(2,1)}, bf16[1024,512]{1,0:T(8,128)(2,1)}, f32[1,2048]{1,0:T(1,128)}) custom-call(bf16[1024,2048]{1,0:T(8,128)(2,1)} %all-gather.6.cloned.1.call-done.rows_in, f32[1024,512]{1,0:T(8,128)} %get-tuple-element.176.dqn, f32[1024,512]{1,0:T(8,128)} %get-tuple-element.177.dkn, ...), custom_call_target="tpu_custom_call" | custom-call | flops 57982058496 | tf_op jit(solution)/shard_map/project_back/pallas_call | solution.py:141
  619.8 2.4 collective-permute-done.17
  622.2 17.8 %wgrad.11 = (bf16[4,1024,256]{2,1,0:T(8,128)(2,1)}, bf16[4,1024,256]{2,1,0:T(8,128)(2,1)}, bf16[4,1024,256]{2,1,0:T(8,128)(2,1)}, bf16[4,1024,256]{2,1,0:T(8,128)(2,1)}) custom-call(s32[8]{0:T(128)} %add.204.order, s32[2,4,8]{2,1,0:T(4,128)} %constant.77.clone.tables, bf16[4,2,128,2048]{3,2,1,0:T(8,128)(2,1)} %bitcast.121, ...), custom_call_target="tpu_custom_call" | custom-call | tf_op jit(solution)/shard_map/wgrad/pallas_call | solution.py:588
  642.8 10.5 %attention_wgrad.2 = (bf16[2,4,256,512]{3,2,1,0:T(8,128)(2,1)}, bf16[2,4,256,512]{3,2,1,0:T(8,128)(2,1)}) custom-call(s32[4]{0:T(128)} %get-tuple-element.190.order, s32[2,4,4]{2,1,0:T(4,128)} %constant.78.clone.tables, bf16[1024,2048]{1,0:T(8,128)(2,1)} %all-gather.6.cloned.1.call-done.rows_in, bf16[1024,2048]{1,0:T(8,128)(2,1)} %all-gather.14.cloned.1.call-done.middle, ...), custom_call_target="tpu_custom_call" | custom-call | tf_op jit(solution)/shard_map/attention_wgrad/pallas_call | solution.py:209
  653.9 1.6 fusion.16
  657.0 2.3 pad_maximum_fusion
  659.3 27.3 %collective-permute-done.20 = bf16[2,2,1024,256]{3,2,1,0:T(8,128)(2,1)} collective-permute-done((bf16[2,2,1024,256]{3,2,1,0:T(8,128)(2,1)}, bf16[2,2,1024,256]{3,2,1,0:T(8,128)(2,1)}, u32[]{:S(2)}, u32[]{:S(2)}) %collective-permute-start.20) | collective-permute-done | bytes 2097184 | tf_op jit(solution)/shard_map/ppermute | solution.py:648
  687.8 2.2 fusion.1
  692.7 2.1 fusion
  699.1 12.1 %attention_wgrad.3 = (bf16[2,4,128,512]{3,2,1,0:T(8,128)(2,1)}, bf16[2,4,128,512]{3,2,1,0:T(8,128)(2,1)}, bf16[2,4,128,512]{3,2,1,0:T(8,128)(2,1)}, bf16[2,4,128,512]{3,2,1,0:T(8,128)(2,1)}) custom-call(s32[4]{0:T(128)} %get-tuple-element.199.order, s32[2,4,4]{2,1,0:T(4,128)} %constant.78.clone.tables, ...), custom_call_target="tpu_custom_call" | custom-call | tf_op jit(solution)/shard_map/attention_wgrad/pallas_call | solution.py:209
  712.5 1.9 fusion.15
  715.9 2.0 collective-permute-start.31
  719.4 3.6 collective-permute-done.31
  723.0 2.8 collective-permute-start.32
  725.8 2.3 pad_maximum_fusion.1
  728.1 6.4 collective-permute-done.32
  734.6 1.8 collective-permute-done.28
  736.4 1.8 add_convert_fusion
  738.9 5.8 collective-permute-done.26
  746.3 2.0 collective-permute-start.33
  753.3 6.8 collective-permute-done.33
  761.6 2.3 pad_maximum_fusion.2
  763.9 2.0 collective-permute-done.34
  769.4 1.8 fusion.12
  771.3 3.2 fusion.11
  (220 shorter events, 61.3 us)
Async XLA Ops:
  7.2 135.9 %copy-start = (bf16[2048,512]{1,0:T(8,128)(2,1)S(1)}, bf16[2048,512]{1,0:T(8,128)(2,1)}, u32[]{:S(2)}) copy-start(bf16[2048,512]{1,0:T(8,128)(2,1)} %param.37) | copy-start | bytes 6291460
  7.2 89.0 %all-gather.6.cloned.1.call-start = ((), (), s32[]{:S(2)}) async-start(), calls=%async_computation.6 | async-start | bytes 5242880 | tf_op jit(solution)/shard_map/all_gather | solution.py:639
  12.6 164.9 %all-gather.8.cloned.1.call-start = ((), (), s32[]{:S(2)}) async-start(), calls=%async_computation.7 | async-start | bytes 5242880 | tf_op jit(solution)/shard_map/all_gather | solution.py:639
  96.3 22.0 %copy-start.30 = (s32[1,1024]{1,0:T(1,128)S(1)}, s32[1,1024]{1,0:T(1,128)}, u32[]{:S(2)}) copy-start(s32[1,1024]{1,0:T(1,128)} %seg_row.3) | copy-start | bytes 12292
  96.3 126.5 %reduce-scatter.7.cloned.1.call-start = ((), (), s32[]{:S(2)}) async-start(), calls=%async_computation.8 | async-start | bytes 2621440 | tf_op jit(solution)/shard_map/reduce_scatter | solution.py:643
  112.6 4.0 collective-permute-start
  117.3 6.7 collective-permute-start.1
  177.5 91.2 %reduce-scatter.9.cloned.1.call-start = ((), (), s32[]{:S(2)}) async-start(), calls=%async_computation.9 | async-start | bytes 2621440 | tf_op jit(solution)/shard_map/reduce_scatter | solution.py:643
  180.2 45.6 %copy-start.27 = (s32[1024,8]{0,1:T(8,128)S(1)}, s32[1024,8]{0,1:T(8,128)}, u32[]{:S(2)}) copy-start(s32[1024,8]{0,1:T(8,128)} %param.32) | copy-start | bytes 98308
  180.2 45.8 %copy-start.26 = (bf16[2048,16]{0,1:T(8,128)(2,1)S(1)}, bf16[2048,16]{0,1:T(8,128)(2,1)}, u32[]{:S(2)}) copy-start(bf16[2048,16]{0,1:T(8,128)(2,1)} %param.41) | copy-start | bytes 196612
  180.2 135.3 %all-gather.10.cloned.1.call-start = ((), (), s32[]{:S(2)}) async-start(), calls=%async_computation.10 | async-start | bytes 2621440 | tf_op jit(solution)/shard_map/all_gather | solution.py:639
  225.4 137.6 %all-gather.12.cloned.1.call-start = ((), (), s32[]{:S(2)}) async-start(), calls=%async_computation.11 | async-start | bytes 2621440 | tf_op jit(solution)/shard_map/all_gather | solution.py:639
  271.3 141.7 %reduce-scatter.13.cloned.1.call-start = ((), (), s32[]{:S(2)}) async-start(), calls=%async_computation.13 | async-start | bytes 2785280 | tf_op jit(solution)/shard_map/reduce_scatter | solution.py:643
  362.9 107.2 %reduce-scatter.11.cloned.1.call-start = ((), (), s32[]{:S(2)}) async-start(), calls=%async_computation.12 | async-start | bytes 2785280 | tf_op jit(solution)/shard_map/reduce_scatter | solution.py:643
  410.4 143.9 %all-gather.14.cloned.1.call-start = ((), (), s32[]{:S(2)}) async-start(), calls=%async_computation.15 | async-start | bytes 5242880 | tf_op jit(solution)/shard_map/all_gather | solution.py:639
  433.7 17.4 %collective-permute-start.2 = (bf16[2,2048,256]{2,1,0:T(8,128)(2,1)}, bf16[2,2048,256]{2,1,0:T(8,128)(2,1)}, u32[]{:S(2)}, u32[]{:S(2)}) collective-permute-start(bf16[2,2048,256]{2,1,0:T(8,128)(2,1)} %get-tuple-element.143), channel_id=1, source_target_pairs={{0,4},{4,0},{8,12},{12,8},{16,20},{20,16},{24,28},{28,24},{1,5},{5... | collective-permute-start | bytes 6291464 | tf_op jit(solution)/shard_map/ppermute | solution.py:648
  433.8 17.4 %collective-permute-start.3 = (bf16[2,2048,256]{2,1,0:T(8,128)(2,1)}, bf16[2,2048,256]{2,1,0:T(8,128)(2,1)}, u32[]{:S(2)}, u32[]{:S(2)}) collective-permute-start(bf16[2,2048,256]{2,1,0:T(8,128)(2,1)} %get-tuple-element.144), channel_id=1, source_target_pairs={{0,4},{4,0},{8,12},{12,8},{16,20},{20,16},{24,28},{28,24},{1,5},{5... | collective-permute-start | bytes 6291464 | tf_op jit(solution)/shard_map/ppermute | solution.py:648
  434.3 16.9 %collective-permute-start.4 = (bf16[2,2048,256]{2,1,0:T(8,128)(2,1)}, bf16[2,2048,256]{2,1,0:T(8,128)(2,1)}, u32[]{:S(2)}, u32[]{:S(2)}) collective-permute-start(bf16[2,2048,256]{2,1,0:T(8,128)(2,1)} %get-tuple-element.145), channel_id=1, source_target_pairs={{0,4},{4,0},{8,12},{12,8},{16,20},{20,16},{24,28},{28,24},{1,5},{5... | collective-permute-start | bytes 6291464 | tf_op jit(solution)/shard_map/ppermute | solution.py:648
  434.3 16.8 %collective-permute-start.5 = (bf16[2,2048,256]{2,1,0:T(8,128)(2,1)}, bf16[2,2048,256]{2,1,0:T(8,128)(2,1)}, u32[]{:S(2)}, u32[]{:S(2)}) collective-permute-start(bf16[2,2048,256]{2,1,0:T(8,128)(2,1)} %get-tuple-element.146), channel_id=1, source_target_pairs={{0,4},{4,0},{8,12},{12,8},{16,20},{20,16},{24,28},{28,24},{1,5},{5... | collective-permute-start | bytes 6291464 | tf_op jit(solution)/shard_map/ppermute | solution.py:648
  474.3 260.3 %reduce-scatter.15.cloned.1.call-start = ((), (), s32[]{:S(2)}) async-start(), calls=%async_computation.14 | async-start | bytes 5242880 | tf_op jit(solution)/shard_map/reduce_scatter | solution.py:643
  474.4 28.1 %collective-permute-start.8 = (bf16[4,2048,256]{2,1,0:T(8,128)(2,1)}, bf16[4,2048,256]{2,1,0:T(8,128)(2,1)}, u32[]{:S(2)}, u32[]{:S(2)}) collective-permute-start(bf16[4,2048,256]{2,1,0:T(8,128)(2,1)} %get-tuple-element.150), channel_id=1, source_target_pairs={{0,4},{4,0},{8,12},{12,8},{16,20},{20,16},{24,28},{28,24},{1,5},{5... | collective-permute-start | bytes 12582920 | tf_op jit(solution)/shard_map/ppermute | solution.py:648
  474.5 27.9 %collective-permute-start.9 = (bf16[4,2048,256]{2,1,0:T(8,128)(2,1)}, bf16[4,2048,256]{2,1,0:T(8,128)(2,1)}, u32[]{:S(2)}, u32[]{:S(2)}) collective-permute-start(bf16[4,2048,256]{2,1,0:T(8,128)(2,1)} %get-tuple-element.151), channel_id=1, source_target_pairs={{0,4},{4,0},{8,12},{12,8},{16,20},{20,16},{24,28},{28,24},{1,5},{5... | collective-permute-start | bytes 12582920 | tf_op jit(solution)/shard_map/ppermute | solution.py:648
  474.9 48.3 %collective-permute-start.6 = (bf16[2,2,1024,256]{3,2,1,0:T(8,128)(2,1)}, bf16[2,2,1024,256]{3,2,1,0:T(8,128)(2,1)}, u32[]{:S(2)}, u32[]{:S(2)}) collective-permute-start(bf16[2,2,1024,256]{3,2,1,0:T(8,128)(2,1)} %bitcast.170), channel_id=1, source_target_pairs={{0,16},{4,20},{8,24},{12,28},{16,0},{20,4},{24,8},{28,12},{1,17},{... | collective-permute-start | bytes 6291464 | tf_op jit(solution)/shard_map/ppermute | solution.py:648
  476.4 48.8 %collective-permute-start.7 = (bf16[2,2,1024,256]{3,2,1,0:T(8,128)(2,1)}, bf16[2,2,1024,256]{3,2,1,0:T(8,128)(2,1)}, u32[]{:S(2)}, u32[]{:S(2)}) collective-permute-start(bf16[2,2,1024,256]{3,2,1,0:T(8,128)(2,1)} %bitcast.169), channel_id=1, source_target_pairs={{0,8},{4,12},{8,0},{12,4},{16,24},{20,28},{24,16},{28,20},{1,9},{5... | collective-permute-start | bytes 6291464 | tf_op jit(solution)/shard_map/ppermute | solution.py:648
  520.3 66.7 %collective-permute-start.12 = (bf16[2,2,1024,256]{3,2,1,0:T(8,128)(2,1)}, bf16[2,2,1024,256]{3,2,1,0:T(8,128)(2,1)}, u32[]{:S(2)}, u32[]{:S(2)}) collective-permute-start(bf16[2,2,1024,256]{3,2,1,0:T(8,128)(2,1)} %bitcast.171), channel_id=1, source_target_pairs={{0,16},{4,20},{8,24},{12,28},{16,0},{20,4},{24,8},{28,12},{1,17},{... | collective-permute-start | bytes 6291464 | tf_op jit(solution)/shard_map/ppermute | solution.py:648
  520.4 66.7 %collective-permute-start.13 = (bf16[2,2,1024,256]{3,2,1,0:T(8,128)(2,1)}, bf16[2,2,1024,256]{3,2,1,0:T(8,128)(2,1)}, u32[]{:S(2)}, u32[]{:S(2)}) collective-permute-start(bf16[2,2,1024,256]{3,2,1,0:T(8,128)(2,1)} %bitcast.168), channel_id=1, source_target_pairs={{0,8},{4,12},{8,0},{12,4},{16,24},{20,28},{24,16},{28,20},{1,9},{5... | collective-permute-start | bytes 6291464 | tf_op jit(solution)/shard_map/ppermute | solution.py:648
  520.7 248.2 %reduce-scatter.17.cloned.1.call-start = ((), (), s32[]{:S(2)}) async-start(), calls=%async_computation.16 | async-start | bytes 5242880 | tf_op jit(solution)/shard_map/reduce_scatter | solution.py:643
  532.4 61.6 %collective-permute-start.14 = (bf16[1,2,1024,256]{3,2,1,0:T(8,128)(2,1)S(1)}, bf16[1,2,1024,256]{3,2,1,0:T(8,128)(2,1)}, u32[]{:S(2)}, u32[]{:S(2)}) collective-permute-start(bf16[1,2,1024,256]{3,2,1,0:T(8,128)(2,1)S(1)} %slice.128), channel_id=1, source_target_pairs={{0,8},{4,12},{8,0},{12,4},{16,24},{20,28},{24,16},{28,20},{1,9},{5... | collective-permute-start | bytes 3145736 | tf_op jit(solution)/shard_map/ppermute | solution.py:648
  535.1 58.9 %collective-permute-start.15 = (bf16[1,2,1024,256]{3,2,1,0:T(8,128)(2,1)}, bf16[1,2,1024,256]{3,2,1,0:T(8,128)(2,1)}, u32[]{:S(2)}, u32[]{:S(2)}) collective-permute-start(bf16[1,2,1024,256]{3,2,1,0:T(8,128)(2,1)} %slice_bitcast_fusion.5), channel_id=1, source_target_pairs={{0,16},{4,20},{8,24},{12,28},{16,0},{20,4},{24,8},{28,12},{1,17},{... | collective-permute-start | bytes 3145736 | tf_op jit(solution)/shard_map/ppermute | solution.py:648
  551.6 70.7 %collective-permute-start.18 = (bf16[4,2048,256]{2,1,0:T(8,128)(2,1)}, bf16[4,2048,256]{2,1,0:T(8,128)(2,1)}, u32[]{:S(2)}, u32[]{:S(2)}) collective-permute-start(bf16[4,2048,256]{2,1,0:T(8,128)(2,1)} %get-tuple-element.172), channel_id=1, source_target_pairs={{0,4},{4,0},{8,12},{12,8},{16,20},{20,16},{24,28},{28,24},{1,5},{5... | collective-permute-start | bytes 12582920 | tf_op jit(solution)/shard_map/ppermute | solution.py:648
  587.0 35.3 %collective-permute-start.19 = (bf16[4,2048,256]{2,1,0:T(8,128)(2,1)}, bf16[4,2048,256]{2,1,0:T(8,128)(2,1)}, u32[]{:S(2)}, u32[]{:S(2)}) collective-permute-start(bf16[4,2048,256]{2,1,0:T(8,128)(2,1)} %get-tuple-element.173), channel_id=1, source_target_pairs={{0,4},{4,0},{8,12},{12,8},{16,20},{20,16},{24,28},{28,24},{1,5},{5... | collective-permute-start | bytes 12582920 | tf_op jit(solution)/shard_map/ppermute | solution.py:648
  587.1 8.5 %collective-permute-start.10 = (f32[2,1024]{1,0:T(2,128)S(1)}, f32[2,1024]{1,0:T(2,128)S(1)}, u32[]{:S(2)}, u32[]{:S(2)}) collective-permute-start(f32[2,1024]{1,0:T(2,128)S(1)} %pad_maximum_fusion.4), channel_id=1, source_target_pairs={{0,1},{1,0},{2,3},{3,2},{4,5},{5,4},{6,7},{7,6},{8,9},{9,8},{10,11... | collective-permute-start | bytes 24584 | tf_op jit(solution)/shard_map/ppermute | solution.py:705
  594.0 25.8 %collective-permute-start.16 = (bf16[1,2,1024,256]{3,2,1,0:T(8,128)(2,1)}, bf16[1,2,1024,256]{3,2,1,0:T(8,128)(2,1)}, u32[]{:S(2)}, u32[]{:S(2)}) collective-permute-start(bf16[1,2,1024,256]{3,2,1,0:T(8,128)(2,1)} %slice.130), channel_id=1, source_target_pairs={{0,8},{4,12},{8,0},{12,4},{16,24},{20,28},{24,16},{28,20},{1,9},{5... | collective-permute-start | bytes 3145736 | tf_op jit(solution)/shard_map/ppermute | solution.py:648
  595.6 7.0 collective-permute-start.11
  597.3 25.0 %collective-permute-start.17 = (bf16[1,2,1024,256]{3,2,1,0:T(8,128)(2,1)}, bf16[1,2,1024,256]{3,2,1,0:T(8,128)(2,1)}, u32[]{:S(2)}, u32[]{:S(2)}) collective-permute-start(bf16[1,2,1024,256]{3,2,1,0:T(8,128)(2,1)} %slice_bitcast_fusion.4), channel_id=1, source_target_pairs={{0,16},{4,20},{8,24},{12,28},{16,0},{20,4},{24,8},{28,12},{1,17},{... | collective-permute-start | bytes 3145736 | tf_op jit(solution)/shard_map/ppermute | solution.py:648
  618.9 23.1 %copy-start.14 = (bf16[128,2048]{1,0:T(8,128)(2,1)S(1)}, bf16[128,2048]{1,0:T(8,128)(2,1)}, u32[]{:S(2)}) copy-start(bf16[128,2048]{1,0:T(8,128)(2,1)} %get-tuple-element.124.normed) | copy-start | bytes 1572868
  619.0 23.1 %copy-start.28 = (bf16[128,128]{1,0:T(8,128)(2,1)S(1)}, bf16[128,128]{1,0:T(8,128)(2,1)}, u32[]{:S(2)}) copy-start(bf16[128,128]{1,0:T(8,128)(2,1)} %get-tuple-element.210) | copy-start | bytes 98308
  619.0 23.4 %copy-start.33 = (f32[1,2048]{1,0:T(1,128)S(1)}, f32[1,2048]{1,0:T(1,128)}, u32[]{:S(2)}) copy-start(f32[1,2048]{1,0:T(1,128)} %get-tuple-element.208) | copy-start | bytes 24580
  619.0 23.4 %copy-start.34 = (f32[1,2048]{1,0:T(1,128)S(1)}, f32[1,2048]{1,0:T(1,128)}, u32[]{:S(2)}) copy-start(f32[1,2048]{1,0:T(1,128)} %get-tuple-element.209) | copy-start | bytes 24580
  619.0 23.4 %copy-start.15 = (bf16[128,2048]{1,0:T(8,128)(2,1)S(1)}, bf16[128,2048]{1,0:T(8,128)(2,1)}, u32[]{:S(2)}) copy-start(bf16[128,2048]{1,0:T(8,128)(2,1)} %get-tuple-element.132.normed) | copy-start | bytes 1572868
  619.0 23.4 %copy-start.29 = (bf16[128,128]{1,0:T(8,128)(2,1)S(1)}, bf16[128,128]{1,0:T(8,128)(2,1)}, u32[]{:S(2)}) copy-start(bf16[128,128]{1,0:T(8,128)(2,1)} %get-tuple-element.211) | copy-start | bytes 98308
  640.0 46.6 %collective-permute-start.20 = (bf16[2,2,1024,256]{3,2,1,0:T(8,128)(2,1)}, bf16[2,2,1024,256]{3,2,1,0:T(8,128)(2,1)}, u32[]{:S(2)}, u32[]{:S(2)}) collective-permute-start(bf16[2,2,1024,256]{3,2,1,0:T(8,128)(2,1)} %bitcast.173), channel_id=1, source_target_pairs={{0,16},{4,20},{8,24},{12,28},{16,0},{20,4},{24,8},{28,12},{1,17},{... | collective-permute-start | bytes 6291464 | tf_op jit(solution)/shard_map/ppermute | solution.py:648
  641.5 46.3 %collective-permute-start.21 = (bf16[2,2,1024,256]{3,2,1,0:T(8,128)(2,1)}, bf16[2,2,1024,256]{3,2,1,0:T(8,128)(2,1)}, u32[]{:S(2)}, u32[]{:S(2)}) collective-permute-start(bf16[2,2,1024,256]{3,2,1,0:T(8,128)(2,1)} %bitcast.172), channel_id=1, source_target_pairs={{0,8},{4,12},{8,0},{12,4},{16,24},{20,28},{24,16},{28,20},{1,9},{5... | collective-permute-start | bytes 6291464 | tf_op jit(solution)/shard_map/ppermute | solution.py:648
  642.8 11.1 %copy-start.8 = (bf16[2,2,1024,256]{3,2,1,0:T(8,128)(2,1)S(1)}, bf16[2,2,1024,256]{3,2,1,0:T(8,128)(2,1)}, u32[]{:S(2)}) copy-start(bf16[2,2,1024,256]{3,2,1,0:T(8,128)(2,1)} %copy-done.7) | copy-start | bytes 6291460
  653.3 44.4 %collective-permute-start.24 = (bf16[2,4,256,512]{3,2,1,0:T(8,128)(2,1)}, bf16[2,4,256,512]{3,2,1,0:T(8,128)(2,1)S(1)}, u32[]{:S(2)}, u32[]{:S(2)}) collective-permute-start(bf16[2,4,256,512]{3,2,1,0:T(8,128)(2,1)} %get-tuple-element.193), channel_id=1, source_target_pairs={{0,4},{4,0},{8,12},{12,8},{16,20},{20,16},{24,28},{28,24},{1,5},{5... | collective-permute-start | bytes 6291464 | tf_op jit(solution)/shard_map/ppermute | solution.py:648
  653.4 44.4 %collective-permute-start.25 = (bf16[2,4,256,512]{3,2,1,0:T(8,128)(2,1)}, bf16[2,4,256,512]{3,2,1,0:T(8,128)(2,1)}, u32[]{:S(2)}, u32[]{:S(2)}) collective-permute-start(bf16[2,4,256,512]{3,2,1,0:T(8,128)(2,1)} %get-tuple-element.194), channel_id=1, source_target_pairs={{0,4},{4,0},{8,12},{12,8},{16,20},{20,16},{24,28},{28,24},{1,5},{5... | collective-permute-start | bytes 6291464 | tf_op jit(solution)/shard_map/ppermute | solution.py:648
  657.0 30.8 %copy-start.21 = (bf16[4,1024,256]{2,1,0:T(8,128)(2,1)S(1)}, bf16[4,1024,256]{2,1,0:T(8,128)(2,1)}, u32[]{:S(2)}) copy-start(bf16[4,1024,256]{2,1,0:T(8,128)(2,1)} %get-tuple-element.186) | copy-start | bytes 6291460
  691.0 43.6 %collective-permute-start.22 = (bf16[1,2,1024,256]{3,2,1,0:T(8,128)(2,1)}, bf16[1,2,1024,256]{3,2,1,0:T(8,128)(2,1)}, u32[]{:S(2)}, u32[]{:S(2)}) collective-permute-start(bf16[1,2,1024,256]{3,2,1,0:T(8,128)(2,1)} %slice.132), channel_id=1, source_target_pairs={{0,8},{4,12},{8,0},{12,4},{16,24},{20,28},{24,16},{28,20},{1,9},{5... | collective-permute-start | bytes 3145736 | tf_op jit(solution)/shard_map/ppermute | solution.py:648
  697.1 37.5 %collective-permute-start.23 = (bf16[1,2,1024,256]{3,2,1,0:T(8,128)(2,1)}, bf16[1,2,1024,256]{3,2,1,0:T(8,128)(2,1)}, u32[]{:S(2)}, u32[]{:S(2)}) collective-permute-start(bf16[1,2,1024,256]{3,2,1,0:T(8,128)(2,1)} %slice_bitcast_fusion.3), channel_id=1, source_target_pairs={{0,16},{4,20},{8,24},{12,28},{16,0},{20,4},{24,8},{28,12},{1,17},{... | collective-permute-start | bytes 3145736 | tf_op jit(solution)/shard_map/ppermute | solution.py:648
  697.7 14.2 %copy-start.37 = (f32[1,512]{1,0:T(1,128)S(1)}, f32[1,512]{1,0:T(1,128)}, u32[]{:S(2)}) copy-start(f32[1,512]{1,0:T(1,128)} %get-tuple-element.207) | copy-start | bytes 6148
  697.7 14.2 %copy-start.25 = (f32[2048]{0:T(1024)S(1)}, f32[2048]{0:T(1024)}, u32[]{:S(2)}) copy-start(f32[2048]{0:T(1024)} %param.33) | copy-start | bytes 24580
  697.7 14.2 %copy-start.35 = (f32[1,2048]{1,0:T(1,128)S(1)}, f32[1,2048]{1,0:T(1,128)}, u32[]{:S(2)}) copy-start(f32[1,2048]{1,0:T(1,128)} %get-tuple-element.205) | copy-start | bytes 24580
  711.2 25.2 %collective-permute-start.28 = (bf16[2,4,128,512]{3,2,1,0:T(8,128)(2,1)}, bf16[2,4,128,512]{3,2,1,0:T(8,128)(2,1)}, u32[]{:S(2)}, u32[]{:S(2)}) collective-permute-start(bf16[2,4,128,512]{3,2,1,0:T(8,128)(2,1)} %get-tuple-element.201), channel_id=1, source_target_pairs={{0,8},{4,12},{8,0},{12,4},{16,24},{20,28},{24,16},{28,20},{1,9},{5... | collective-permute-start | bytes 3145736 | tf_op jit(solution)/shard_map/ppermute | solution.py:648
  712.4 5.4 copy-start.3
  712.4 3.4 collective-permute-start.30
  714.4 30.2 %collective-permute-start.26 = (bf16[2,4,128,512]{3,2,1,0:T(8,128)(2,1)}, bf16[2,4,128,512]{3,2,1,0:T(8,128)(2,1)}, u32[]{:S(2)}, u32[]{:S(2)}) collective-permute-start(bf16[2,4,128,512]{3,2,1,0:T(8,128)(2,1)} %get-tuple-element.200), channel_id=1, source_target_pairs={{0,16},{4,20},{8,24},{12,28},{16,0},{20,4},{24,8},{28,12},{1,17},{... | collective-permute-start | bytes 3145736 | tf_op jit(solution)/shard_map/ppermute | solution.py:648
  715.9 7.1 collective-permute-start.31
  723.0 11.5 %collective-permute-start.32 = (f32[20,2048]{1,0:T(8,128)S(1)}, f32[20,2048]{1,0:T(8,128)S(1)}, u32[]{:S(2)}, u32[]{:S(2)}) collective-permute-start(f32[20,2048]{1,0:T(8,128)S(1)} %add.229), channel_id=1, source_target_pairs={{0,2},{1,3},{2,0},{3,1},{4,6},{5,7},{6,4},{7,5},{8,10},{9,11},{10,... | collective-permute-start | bytes 491528 | tf_op jit(solution)/shard_map/ppermute | solution.py:705
  734.5 10.1 %copy-start.23 = (bf16[2,4,128,512]{3,2,1,0:T(8,128)(2,1)S(1)}, bf16[2,4,128,512]{3,2,1,0:T(8,128)(2,1)}, u32[]{:S(2)}) copy-start(bf16[2,4,128,512]{3,2,1,0:T(8,128)(2,1)} %get-tuple-element.203) | copy-start | bytes 3145732
  738.3 10.1 %copy-start.12 = (bf16[2,2,1024,256]{3,2,1,0:T(8,128)(2,1)S(1)}, bf16[2,2,1024,256]{3,2,1,0:T(8,128)(2,1)}, u32[]{:S(2)}) copy-start(bf16[2,2,1024,256]{3,2,1,0:T(8,128)(2,1)} %copy-done.11) | copy-start | bytes 6291460
  738.3 28.9 %collective-permute-start.29 = (bf16[1,4,128,512]{3,2,1,0:T(8,128)(2,1)S(1)}, bf16[1,4,128,512]{3,2,1,0:T(8,128)(2,1)S(1)}, u32[]{:S(2)}, u32[]{:S(2)}) collective-permute-start(bf16[1,4,128,512]{3,2,1,0:T(8,128)(2,1)S(1)} %slice_bitcast_fusion.6), channel_id=1, source_target_pairs={{0,16},{4,20},{8,24},{12,28},{16,0},{20,4},{24,8},{28,12},{1,17},{... | collective-permute-start | bytes 1572872 | tf_op jit(solution)/shard_map/ppermute | solution.py:648
  746.3 21.1 %collective-permute-start.27 = (bf16[1,4,128,512]{3,2,1,0:T(8,128)(2,1)S(1)}, bf16[1,4,128,512]{3,2,1,0:T(8,128)(2,1)S(1)}, u32[]{:S(2)}, u32[]{:S(2)}) collective-permute-start(bf16[1,4,128,512]{3,2,1,0:T(8,128)(2,1)S(1)} %slice.135), channel_id=1, source_target_pairs={{0,8},{4,12},{8,0},{12,4},{16,24},{20,28},{24,16},{28,20},{1,9},{5... | collective-permute-start | bytes 1572872 | tf_op jit(solution)/shard_map/ppermute | solution.py:648
  746.3 13.8 %collective-permute-start.33 = (f32[20,2048]{1,0:T(8,128)S(1)}, f32[20,2048]{1,0:T(8,128)S(1)}, u32[]{:S(2)}, u32[]{:S(2)}) collective-permute-start(f32[20,2048]{1,0:T(8,128)S(1)} %add.230), channel_id=1, source_target_pairs={{0,8},{4,12},{8,0},{12,4},{16,24},{20,28},{24,16},{28,20},{1,9},{5... | collective-permute-start | bytes 491528 | tf_op jit(solution)/shard_map/ppermute | solution.py:705
  760.1 5.7 collective-permute-start.34
  (22 other events, 55.5 us)
Sparse Core Ops, SparseCore 0:
  12.7 83.4 all-gather.5
  97.8 79.6 all-gather.7
  180.3 42.3 reduce-scatter.6
  225.5 43.1 reduce-scatter.8
  270.1 45.3 all-gather.9
  317.5 44.6 all-gather.11
  364.5 44.7 reduce-scatter.12
  411.6 45.3 reduce-scatter.10
  474.4 79.8 all-gather.13
  556.5 75.6 reduce-scatter.14
  634.5 77.2 reduce-scatter.16

commit v13 on v12

--- a/solution.py
+++ b/solution.py
@@ -522,6 +522,7 @@
     outs = refs[2 * count + extra :]
     at = pl.program_id(0)
     features = lefts[0].shape[-1]
+    width = outs[0].shape[2]
 
     def piece(start, stop):
         total = None
@@ -537,7 +538,9 @@
             @pl.when(at // per == place)
             def _(out=out):
                 for start in range(0, features, block):
-                    out[0, start : start + block, :] = piece(start, start + block).astype(bf16)
+                    total = piece(start, start + block).astype(bf16)
+                    for entry in range(out.shape[0]):
+                        out[entry, start : start + block, :] = total[:, entry * width : (entry + 1) * width]
 
         return
     half = features // 2
@@ -548,30 +551,32 @@
         @pl.when(at // per == place)
         def _(arrived=arrived):
             for start in range(0, features, block):
-                total = piece(start, start + block) + arrived[0, start : start + block, :].astype(f32)
-                got[start : start + block, :] = total.astype(bf16)
+                total = piece(start, start + block)
+                for entry in range(got.shape[0]):
+                    part = total[:, entry * width : (entry + 1) * width]
+                    got[entry, start : start + block, :] = (part + arrived[entry, start : start + block, :].astype(f32)).astype(bf16)
 
     for side, out in enumerate(outs):
         start = side * 2 // len(outs) * half
 
         @pl.when(tables[1, side, at] == 1)
         def _(out=out, start=start):
-            out[0] = got[start : start + half, :]
+            out[...] = got[:, start : start + half, :]
 
 
 def wgrad(lefts, rights, order, width, per, added=(), weight=1, pieces=0):
     features = lefts[0][0].shape[-1]
-    experts = order.shape[0]
-    groups = experts // per
-    tables, sizes = split_tables(groups, per)
+    groups = order.shape[0]
+    experts = groups * per
+    tables, sizes = split_tables(groups, 1)
     pieces = len(added) or pieces or groups
-    held = experts // pieces
+    held = groups // pieces
 
     def piece_spec(place):
-        return pl.BlockSpec((1, features, width), lambda i, ids, to: (jnp.clip(i - place * held, 0, held - 1), 0, 0))
+        return pl.BlockSpec((per, features, width), lambda i, ids, to: (jnp.clip(i - place * held, 0, held - 1), 0, 0))
 
     def half_spec(side):
-        return pl.BlockSpec((1, features // 2, width), lambda i, ids, to: (to[0, side, i], 0, 0))
+        return pl.BlockSpec((per, features // 2, width), lambda i, ids, to: (to[0, side, i], 0, 0))
 
     def left_spec(left, chunk):
         if left.ndim == 2:
@@ -584,17 +589,17 @@
         out_shape = [jax.ShapeDtypeStruct((size * per, features // 2, width), bf16) for size in sizes]
     else:
         out_specs = piece_specs
-        out_shape = [jax.ShapeDtypeStruct((held, features, width), bf16)] * pieces
+        out_shape = [jax.ShapeDtypeStruct((held * per, features, width), bf16)] * pieces
     return pl.pallas_call(
         functools.partial(wgrad_kernel, len(lefts), len(added), held, min(512, features // 2)),
         grid_spec=pltpu.PrefetchScalarGridSpec(
             num_scalar_prefetch=2,
-            grid=(experts,),
+            grid=(groups,),
             in_specs=[left_spec(*left) for left in lefts]
-            + [pl.BlockSpec((right.shape[0], width), lambda i, ids, to: (0, ids[i])) for right in rights]
+            + [pl.BlockSpec((right.shape[0], per * width), lambda i, ids, to: (0, ids[i])) for right in rights]
             + (piece_specs if added else []),
             out_specs=out_specs,
-            scratch_shapes=[pltpu.VMEM((features, width), bf16)] if added else [],
+            scratch_shapes=[pltpu.VMEM((per, features, width), bf16)] if added else [],
         ),
         out_shape=out_shape,
         compiler_params=params(),
@@ -741,9 +746,7 @@
 
     relative = jnp.asarray(block_order(dp_size // 2), jnp.int32) ^ (lax.axis_index("dp") // 2)
     own_blocks, other_blocks = 2 * relative + low_bit, 2 * relative + 1 - low_bit
-    mine, theirs = (
-        (blocks[:, None] * per + jnp.arange(per, dtype=jnp.int32)).reshape(-1) for blocks in (own_blocks, other_blocks)
-    )
+    mine, theirs = own_blocks, other_blocks
 
     qraw, kraw, value, squares = project(normed_all, w_query, w_key, w_value)
     squares = exchange_sum(squares, doublings("tensor"))

time: 789 us -> 788 us (level)
  no operation moved by 1% of the time
where the time goes in v13:
time: 788 us; the launch traced here: 780 us
  Pallas kernels  349 us (44%)
  waiting for transfers between devices  294 us (37%)
  other arithmetic  56.7 us (7%)
  starting transfers between devices  27.6 us (4%)
  local copies, waits for them, and re-layouts  26.7 us (3%)
  between operations  15 us (2%)
  matrix products  11.4 us (1%)
    all_gather x5, waiting for transfers between devices, gather_rows(): return lax.all_gather(values, 'tensor', axis=0, tiled=True)  162 us
    pallas_call x6, Pallas kernels, wgrad(): pl.pallas_call(functools.partial(wgrad_kernel, len(lefts), len(added), he...  100 us
    pallas_call x2, Pallas kernels, experts_block(): pl.pallas_call(functools.partial(expert_kernel, block), grid=(experts,),...  94.7 us
    reduce_scatter x6, waiting for transfers between devices, scatter_rows(): return lax.psum_scatter(values, 'tensor', scatter_dimension=0, tiled=True)  55 us
    ppermute x26, waiting for transfers between devices, pair_swap(): return lax.ppermute(values, 'dp', [(i, i ^ step) for i in range(size)])  44.4 us
    ppermute x9, waiting for transfers between devices, exchange_sum(): lax.ppermute(values, axis, [(i, i ^ step) for i in range(lax.axis_size(ax...  31.7 us
    pallas_call x1, Pallas kernels, attend_back(): pl.pallas_call(functools.partial(attend_back_kernel, block), grid=(width...  24.6 us
    pallas_call x1, Pallas kernels, down(): pl.pallas_call(functools.partial(down_kernel, parts), grid=(features // b...  24.5 us
  transfers between devices with their start and end apart: 46, of which 21 were waited for; matrix products, arithmetic and copies ran while one was open for 10% of the time, Pallas kernels for 44%

profile of v13, /device:TPU:0, one launch (start us, length us, event | category | flops | bytes accessed | tf_op | source)
XLA Modules:
  0.0 780.2 jit_solution(7688876203502642923)
XLA Ops:
  7.2 1.6 fusion.6
  10.1 2.5 fusion.8
  12.6 83.6 %all-gather.6.cloned.1.call-done.rows_in = bf16[1024,2048]{1,0:T(8,128)(2,1)} async-done(((bf16[256,2048]{1,0:T(8,128)(2,1)}), bf16[1024,2048]{1,0:T(8,128)(2,1)}) %all-gather.6.cloned.1.call-update) | async-done | bytes 4194320 | tf_op jit(solution)/shard_map/all_gather | solution.py:644
  96.3 16.3 %project.1 = (f32[1024,512]{1,0:T(8,128)}, f32[1024,512]{1,0:T(8,128)}, bf16[1024,512]{1,0:T(8,128)(2,1)}, f32[2,1024]{1,0:T(2,128)}) custom-call(bf16[1024,2048]{1,0:T(8,128)(2,1)} %all-gather.6.cloned.1.call-done.rows_in, bf16[2048,512]{1,0:T(8,128)(2,1)} %w_query.3, bf16[2048,512]{1,0:T(8,128)(2,1)} %w_key.3, bf16[2048,512]{1,0:T(8,128)(2,1)} %w_value.3), custom_call_target="tpu_custom_call" | custom-call | flops 2899102976 | bytes 1310720 | tf_op jit(solution)/shard_map/project/pallas_call | solution.py:101
  112.6 4.0 collective-permute-done
  119.3 4.8 collective-permute-done.1
  126.1 15.7 %attend.1 = (bf16[1024,512]{1,0:T(8,128)(2,1)}, bf16[1024,512]{1,0:T(8,128)(2,1)}, bf16[1024,512]{1,0:T(8,128)(2,1)}, f32[1024,512]{1,0:T(8,128)}) custom-call(f32[1024,512]{1,0:T(8,128)} %get-tuple-element.114.qraw, f32[1024,512]{1,0:T(8,128)} %get-tuple-element.115.kraw, bf16[1024,512]{1,0:T(8,128)(2,1)} %get-tuple-element.116.value, ...), custom_call_target="tpu_custom_call" | custom-call | flops 57347878912 | bytes 1179648 | tf_op jit(solution)/shard_map/attend/pallas_call | solution.py:259
  143.1 2.7 convolution_convert_fusion.1
  145.7 31.7 %all-gather.8.cloned.1.call-done.grad = bf16[1024,2048]{1,0:T(8,128)(2,1)} async-done(((bf16[256,2048]{1,0:T(8,128)(2,1)}), bf16[1024,2048]{1,0:T(8,128)(2,1)}) %all-gather.8.cloned.1.call-update) | async-done | bytes 4194320 | tf_op jit(solution)/shard_map/all_gather | solution.py:644
  177.5 2.6 convolution_convert_fusion
  180.2 42.5 %reduce-scatter.7.cloned.1.call-done.summed = bf16[128,2048]{1,0:T(8,128)(2,1)} async-done(((bf16[512,2048]{1,0:T(8,128)(2,1)}), bf16[128,2048]{1,0:T(8,128)(2,1)}) %reduce-scatter.7.cloned.1.call-update) | async-done | bytes 524304 | tf_op jit(solution)/shard_map/reduce_scatter | solution.py:648
  222.7 2.6 middle.2
  227.0 5.7 convert_reduce_fusion
  233.6 22.6 %up_back.1 = bf16[1024,4096]{1,0:T(8,128)(2,1)} custom-call(bf16[1024,2048]{1,0:T(8,128)(2,1)} %all-gather.8.cloned.1.call-done.grad, bf16[16,2048,256]{2,1,0:T(8,128)(2,1)} %down_w.3), custom_call_target="tpu_custom_call" | custom-call | flops 7730940928 | bytes 2621440 | tf_op jit(solution)/shard_map/up_back/pallas_call | solution.py:417
  256.3 12.5 %reduce-scatter.9.cloned.1.call-done.summed = bf16[128,2048]{1,0:T(8,128)(2,1)} async-done(((bf16[512,2048]{1,0:T(8,128)(2,1)}), bf16[128,2048]{1,0:T(8,128)(2,1)}) %reduce-scatter.9.cloned.1.call-update) | async-done | bytes 524304 | tf_op jit(solution)/shard_map/reduce_scatter | solution.py:648
  268.8 2.5 middle.3
  271.4 44.1 %all-gather.10.cloned.1.call-done.rows_in.refs_0_ = bf16[512,2048]{1,0:T(8,128)(2,1)} async-done(((bf16[128,2048]{1,0:T(8,128)(2,1)}), bf16[512,2048]{1,0:T(8,128)(2,1)}) %all-gather.10.cloned.1.call-update) | async-done | bytes 2097168 | tf_op jit(solution)/shard_map/all_gather | solution.py:644
  315.5 47.4 %experts.2 = (bf16[512,4096]{1,0:T(8,128)(2,1)}, bf16[512,4096]{1,0:T(8,128)(2,1)}, bf16[512,4096]{1,0:T(8,128)(2,1)}, bf16[512,2176]{1,0:T(8,128)(2,1)}) custom-call(bf16[512,2048]{1,0:T(8,128)(2,1)} %all-gather.10.cloned.1.call-done.rows_in.refs_0_, bf16[4,2,128,4096]{3,2,1,0:T(8,128)(2,1)} %bitcast.124, f32[512,128]{1,0:T(8,128)} %bitcast.144, ...), custom_call_target="tpu_custom_call" | custom-call | flops 53210619904 | bytes 6291456 | tf_op jit(solution)/shard_map/experts/pallas_call | solution.py:483
  362.9 47.4 %experts.3 = (bf16[512,4096]{1,0:T(8,128)(2,1)}, bf16[512,4096]{1,0:T(8,128)(2,1)}, bf16[512,4096]{1,0:T(8,128)(2,1)}, bf16[512,2176]{1,0:T(8,128)(2,1)}) custom-call(bf16[512,2048]{1,0:T(8,128)(2,1)} %all-gather.12.cloned.1.call-done.rows_in.refs_1_, bf16[4,2,128,4096]{3,2,1,0:T(8,128)(2,1)} %bitcast.125, f32[512,128]{1,0:T(8,128)} %bitcast.143, ...), custom_call_target="tpu_custom_call" | custom-call | flops 53210619904 | bytes 6291456 | tf_op jit(solution)/shard_map/experts/pallas_call | solution.py:483
  412.3 4.2 middle_back.2
  416.4 16.3 %wgrad.6 = (bf16[2,2048,256]{2,1,0:T(8,128)(2,1)}, bf16[2,2048,256]{2,1,0:T(8,128)(2,1)}, bf16[2,2048,256]{2,1,0:T(8,128)(2,1)}, bf16[2,2048,256]{2,1,0:T(8,128)(2,1)}) custom-call(s32[4]{0:T(128)} %get-tuple-element.190.order, s32[2,4,4]{2,1,0:T(4,128)} %constant.74.clone.tables, bf16[512,2048]{1,0:T(8,128)(2,1)} %all-gather.10.cloned.1.call-done.rows_in.refs_0_, ...), custom_call_target="tpu_custom_call" | custom-call | tf_op jit(solution)/shard_map/wgrad/pallas_call | solution.py:593
  433.7 15.1 %wgrad.7 = (bf16[4,2048,256]{2,1,0:T(8,128)(2,1)}, bf16[4,2048,256]{2,1,0:T(8,128)(2,1)}) custom-call(s32[4]{0:T(128)} %get-tuple-element.190.order, s32[2,4,4]{2,1,0:T(4,128)} %constant.74.clone.tables, bf16[512,2048]{1,0:T(8,128)(2,1)} %all-gather.10.cloned.1.call-done.rows_in.refs_0_, bf16[512,2048]{1,0:T(8,128)(2,1)} %all-gather.12.cloned.1.call-done.rows_in.refs_1_, ...), custom_call_target="tpu_custom_call" | custom-call | flops 15461881856 | tf_op jit(solution)/shard_map/wgrad/pallas_call | solution.py:593
  450.9 18.7 %wgrad.8 = (bf16[4,1024,256]{2,1,0:T(8,128)(2,1)}, bf16[4,1024,256]{2,1,0:T(8,128)(2,1)}, bf16[4,1024,256]{2,1,0:T(8,128)(2,1)}, bf16[4,1024,256]{2,1,0:T(8,128)(2,1)}) custom-call(s32[4]{0:T(128)} %get-tuple-element.199.order, s32[2,4,4]{2,1,0:T(4,128)} %constant.74.clone.tables, bf16[512,2048]{1,0:T(8,128)(2,1)} %all-gather.10.cloned.1.call-done.rows_in.refs_0_, ...), custom_call_target="tpu_custom_call" | custom-call | flops 15461881856 | tf_op jit(solution)/shard_map/wgrad/pallas_call | solution.py:593
  469.6 4.2 middle_back.3
  474.4 1.5 collective-permute-start.6
  477.4 24.5 %down.1 = bf16[1024,2048]{1,0:T(8,128)(2,1)} custom-call(bf16[16,2048,256]{2,1,0:T(8,128)(2,1)} %down_w.3, bf16[512,4096]{1,0:T(8,128)(2,1)} %get-tuple-element.161.refs_0_.refs_2_, bf16[512,4096]{1,0:T(8,128)(2,1)} %get-tuple-element.136.refs_1_.refs_3_), custom_call_target="tpu_custom_call" | custom-call | tf_op jit(solution)/shard_map/down/pallas_call | solution.py:626
  501.9 17.4 %wgrad.9 = (bf16[4,1024,256]{2,1,0:T(8,128)(2,1)}, bf16[4,1024,256]{2,1,0:T(8,128)(2,1)}, bf16[4,1024,256]{2,1,0:T(8,128)(2,1)}, bf16[4,1024,256]{2,1,0:T(8,128)(2,1)}) custom-call(s32[4]{0:T(128)} %get-tuple-element.199.order, s32[2,4,4]{2,1,0:T(4,128)} %constant.74.clone.tables, bf16[512,2048]{1,0:T(8,128)(2,1)} %all-gather.10.cloned.1.call-done.rows_in.refs_0_, ...), custom_call_target="tpu_custom_call" | custom-call | tf_op jit(solution)/shard_map/wgrad/pallas_call | solution.py:593
  519.8 3.3 collective-permute-done.6
  523.1 1.6 collective-permute-done.7
  524.8 2.7 fusion.5
  527.6 2.3 copy-done.19
  529.9 2.1 fusion.4
  535.2 15.6 %wgrad.10 = (bf16[4,2048,256]{2,1,0:T(8,128)(2,1)}, bf16[4,2048,256]{2,1,0:T(8,128)(2,1)}) custom-call(s32[4]{0:T(128)} %get-tuple-element.190.order, s32[2,4,4]{2,1,0:T(4,128)} %constant.74.clone.tables, bf16[4,2,128,2048]{3,2,1,0:T(8,128)(2,1)} %bitcast.119, bf16[4,2,128,2048]{3,2,1,0:T(8,128)(2,1)} %bitcast.120, ...), custom_call_target="tpu_custom_call" | custom-call | tf_op jit(solution)/shard_map/wgrad/pallas_call | solution.py:593
  550.8 3.0 all-gather.14.cloned.1.call-done.middle
  553.7 5.5 convolution_convert_fusion.2.out_grad
  559.3 24.6 %attend_back.1 = (f32[1024,512]{1,0:T(8,128)}, f32[1024,512]{1,0:T(8,128)}, bf16[1024,512]{1,0:T(8,128)(2,1)}, f32[1024,1]{1,0:T(8,128)}, f32[1024,1]{1,0:T(8,128)}, /*index=5*/f32[1,512]{1,0:T(1,128)}, f32[1,512]{1,0:T(1,128)}) custom-call(bf16[1024,512]{1,0:T(8,128)(2,1)} %get-tuple-element.162.query, bf16[1024,512]{1,0:T(8,128)(2,1)} %get-tuple-element.163.key, ...), custom_call_target="tpu_custom_call" | custom-call | tf_op jit(solution)/shard_map/attend_back/pallas_call | solution.py:325
  586.6 2.8 fusion.3
  589.5 2.8 fusion.2
  598.1 3.8 collective-permute-done.11
  604.0 14.1 %project_back.1 = (bf16[1024,2048]{1,0:T(8,128)(2,1)}, bf16[1024,512]{1,0:T(8,128)(2,1)}, bf16[1024,512]{1,0:T(8,128)(2,1)}, f32[1,2048]{1,0:T(1,128)}) custom-call(bf16[1024,2048]{1,0:T(8,128)(2,1)} %all-gather.6.cloned.1.call-done.rows_in, f32[1024,512]{1,0:T(8,128)} %get-tuple-element.176.dqn, f32[1024,512]{1,0:T(8,128)} %get-tuple-element.177.dkn, ...), custom_call_target="tpu_custom_call" | custom-call | flops 57982058496 | tf_op jit(solution)/shard_map/project_back/pallas_call | solution.py:141
  619.3 2.4 collective-permute-done.17
  621.7 17.3 %wgrad.11 = (bf16[4,1024,256]{2,1,0:T(8,128)(2,1)}, bf16[4,1024,256]{2,1,0:T(8,128)(2,1)}, bf16[4,1024,256]{2,1,0:T(8,128)(2,1)}, bf16[4,1024,256]{2,1,0:T(8,128)(2,1)}) custom-call(s32[4]{0:T(128)} %get-tuple-element.199.order, s32[2,4,4]{2,1,0:T(4,128)} %constant.74.clone.tables, bf16[4,2,128,2048]{3,2,1,0:T(8,128)(2,1)} %bitcast.121, ...), custom_call_target="tpu_custom_call" | custom-call | tf_op jit(solution)/shard_map/wgrad/pallas_call | solution.py:593
  641.7 10.5 %attention_wgrad.2 = (bf16[2,4,256,512]{3,2,1,0:T(8,128)(2,1)}, bf16[2,4,256,512]{3,2,1,0:T(8,128)(2,1)}) custom-call(s32[4]{0:T(128)} %get-tuple-element.190.order, s32[2,4,4]{2,1,0:T(4,128)} %constant.74.clone.tables, bf16[1024,2048]{1,0:T(8,128)(2,1)} %all-gather.6.cloned.1.call-done.rows_in, bf16[1024,2048]{1,0:T(8,128)(2,1)} %all-gather.14.cloned.1.call-done.middle, ...), custom_call_target="tpu_custom_call" | custom-call | tf_op jit(solution)/shard_map/attention_wgrad/pallas_call | solution.py:209
  652.8 1.6 fusion.16
  655.9 2.3 pad_maximum_fusion
  658.2 27.3 %collective-permute-done.20 = bf16[2,2,1024,256]{3,2,1,0:T(8,128)(2,1)} collective-permute-done((bf16[2,2,1024,256]{3,2,1,0:T(8,128)(2,1)}, bf16[2,2,1024,256]{3,2,1,0:T(8,128)(2,1)}, u32[]{:S(2)}, u32[]{:S(2)}) %collective-permute-start.20) | collective-permute-done | bytes 2097184 | tf_op jit(solution)/shard_map/ppermute | solution.py:653
  686.7 2.2 fusion.1
  691.6 2.1 fusion
  698.0 12.1 %attention_wgrad.3 = (bf16[2,4,128,512]{3,2,1,0:T(8,128)(2,1)}, bf16[2,4,128,512]{3,2,1,0:T(8,128)(2,1)}, bf16[2,4,128,512]{3,2,1,0:T(8,128)(2,1)}, bf16[2,4,128,512]{3,2,1,0:T(8,128)(2,1)}) custom-call(s32[4]{0:T(128)} %get-tuple-element.199.order, s32[2,4,4]{2,1,0:T(4,128)} %constant.74.clone.tables, ...), custom_call_target="tpu_custom_call" | custom-call | tf_op jit(solution)/shard_map/attention_wgrad/pallas_call | solution.py:209
  711.5 1.9 fusion.15
  714.8 2.0 collective-permute-start.31
  718.3 3.6 collective-permute-done.31
  722.0 2.8 collective-permute-start.32
  724.7 2.3 pad_maximum_fusion.1
  727.0 6.4 collective-permute-done.32
  733.6 1.8 collective-permute-done.28
  735.3 1.8 add_convert_fusion
  737.8 5.7 collective-permute-done.26
  745.2 2.0 collective-permute-start.33
  752.2 6.9 collective-permute-done.33
  760.5 2.3 pad_maximum_fusion.2
  762.8 2.1 collective-permute-done.34
  768.4 1.8 fusion.12
  770.3 3.2 fusion.11
  (220 shorter events, 62.0 us)
Async XLA Ops:
  7.2 135.9 %copy-start = (bf16[2048,512]{1,0:T(8,128)(2,1)S(1)}, bf16[2048,512]{1,0:T(8,128)(2,1)}, u32[]{:S(2)}) copy-start(bf16[2048,512]{1,0:T(8,128)(2,1)} %param.37) | copy-start | bytes 6291460
  7.2 89.0 %all-gather.6.cloned.1.call-start = ((), (), s32[]{:S(2)}) async-start(), calls=%async_computation.6 | async-start | bytes 5242880 | tf_op jit(solution)/shard_map/all_gather | solution.py:644
  12.6 164.9 %all-gather.8.cloned.1.call-start = ((), (), s32[]{:S(2)}) async-start(), calls=%async_computation.7 | async-start | bytes 5242880 | tf_op jit(solution)/shard_map/all_gather | solution.py:644
  96.2 22.0 %copy-start.30 = (s32[1,1024]{1,0:T(1,128)S(1)}, s32[1,1024]{1,0:T(1,128)}, u32[]{:S(2)}) copy-start(s32[1,1024]{1,0:T(1,128)} %seg_row.3) | copy-start | bytes 12292
  96.3 126.5 %reduce-scatter.7.cloned.1.call-start = ((), (), s32[]{:S(2)}) async-start(), calls=%async_computation.8 | async-start | bytes 2621440 | tf_op jit(solution)/shard_map/reduce_scatter | solution.py:648
  112.6 4.0 collective-permute-start
  117.3 6.8 collective-permute-start.1
  177.5 91.3 %reduce-scatter.9.cloned.1.call-start = ((), (), s32[]{:S(2)}) async-start(), calls=%async_computation.9 | async-start | bytes 2621440 | tf_op jit(solution)/shard_map/reduce_scatter | solution.py:648
  180.1 45.4 %copy-start.27 = (s32[1024,8]{0,1:T(8,128)S(1)}, s32[1024,8]{0,1:T(8,128)}, u32[]{:S(2)}) copy-start(s32[1024,8]{0,1:T(8,128)} %param.32) | copy-start | bytes 98308
  180.1 45.6 %copy-start.26 = (bf16[2048,16]{0,1:T(8,128)(2,1)S(1)}, bf16[2048,16]{0,1:T(8,128)(2,1)}, u32[]{:S(2)}) copy-start(bf16[2048,16]{0,1:T(8,128)(2,1)} %param.41) | copy-start | bytes 196612
  180.2 135.3 %all-gather.10.cloned.1.call-start = ((), (), s32[]{:S(2)}) async-start(), calls=%async_computation.10 | async-start | bytes 2621440 | tf_op jit(solution)/shard_map/all_gather | solution.py:644
  225.3 137.6 %all-gather.12.cloned.1.call-start = ((), (), s32[]{:S(2)}) async-start(), calls=%async_computation.11 | async-start | bytes 2621440 | tf_op jit(solution)/shard_map/all_gather | solution.py:644
  271.3 140.9 %reduce-scatter.13.cloned.1.call-start = ((), (), s32[]{:S(2)}) async-start(), calls=%async_computation.13 | async-start | bytes 2785280 | tf_op jit(solution)/shard_map/reduce_scatter | solution.py:648
  362.9 106.7 %reduce-scatter.11.cloned.1.call-start = ((), (), s32[]{:S(2)}) async-start(), calls=%async_computation.12 | async-start | bytes 2785280 | tf_op jit(solution)/shard_map/reduce_scatter | solution.py:648
  410.4 143.4 %all-gather.14.cloned.1.call-start = ((), (), s32[]{:S(2)}) async-start(), calls=%async_computation.15 | async-start | bytes 5242880 | tf_op jit(solution)/shard_map/all_gather | solution.py:644
  432.7 16.1 %collective-permute-start.2 = (bf16[2,2048,256]{2,1,0:T(8,128)(2,1)}, bf16[2,2048,256]{2,1,0:T(8,128)(2,1)S(1)}, u32[]{:S(2)}, u32[]{:S(2)}) collective-permute-start(bf16[2,2048,256]{2,1,0:T(8,128)(2,1)} %get-tuple-element.143), channel_id=1, source_target_pairs={{0,4},{4,0},{8,12},{12,8},{16,20},{20,16},{24,28},{28,24},{1,5},{5... | collective-permute-start | bytes 6291464 | tf_op jit(solution)/shard_map/ppermute | solution.py:653
  432.7 16.1 %collective-permute-start.3 = (bf16[2,2048,256]{2,1,0:T(8,128)(2,1)}, bf16[2,2048,256]{2,1,0:T(8,128)(2,1)S(1)}, u32[]{:S(2)}, u32[]{:S(2)}) collective-permute-start(bf16[2,2048,256]{2,1,0:T(8,128)(2,1)} %get-tuple-element.144), channel_id=1, source_target_pairs={{0,4},{4,0},{8,12},{12,8},{16,20},{20,16},{24,28},{28,24},{1,5},{5... | collective-permute-start | bytes 6291464 | tf_op jit(solution)/shard_map/ppermute | solution.py:653
  433.2 15.7 %collective-permute-start.4 = (bf16[2,2048,256]{2,1,0:T(8,128)(2,1)}, bf16[2,2048,256]{2,1,0:T(8,128)(2,1)}, u32[]{:S(2)}, u32[]{:S(2)}) collective-permute-start(bf16[2,2048,256]{2,1,0:T(8,128)(2,1)} %get-tuple-element.145), channel_id=1, source_target_pairs={{0,4},{4,0},{8,12},{12,8},{16,20},{20,16},{24,28},{28,24},{1,5},{5... | collective-permute-start | bytes 6291464 | tf_op jit(solution)/shard_map/ppermute | solution.py:653
  433.3 15.6 %collective-permute-start.5 = (bf16[2,2048,256]{2,1,0:T(8,128)(2,1)}, bf16[2,2048,256]{2,1,0:T(8,128)(2,1)}, u32[]{:S(2)}, u32[]{:S(2)}) collective-permute-start(bf16[2,2048,256]{2,1,0:T(8,128)(2,1)} %get-tuple-element.146), channel_id=1, source_target_pairs={{0,4},{4,0},{8,12},{12,8},{16,20},{20,16},{24,28},{28,24},{1,5},{5... | collective-permute-start | bytes 6291464 | tf_op jit(solution)/shard_map/ppermute | solution.py:653
  473.8 259.7 %reduce-scatter.15.cloned.1.call-start = ((), (), s32[]{:S(2)}) async-start(), calls=%async_computation.14 | async-start | bytes 5242880 | tf_op jit(solution)/shard_map/reduce_scatter | solution.py:648
  473.9 28.1 %collective-permute-start.8 = (bf16[4,2048,256]{2,1,0:T(8,128)(2,1)}, bf16[4,2048,256]{2,1,0:T(8,128)(2,1)}, u32[]{:S(2)}, u32[]{:S(2)}) collective-permute-start(bf16[4,2048,256]{2,1,0:T(8,128)(2,1)} %get-tuple-element.150), channel_id=1, source_target_pairs={{0,4},{4,0},{8,12},{12,8},{16,20},{20,16},{24,28},{28,24},{1,5},{5... | collective-permute-start | bytes 12582920 | tf_op jit(solution)/shard_map/ppermute | solution.py:653
  474.0 27.9 %collective-permute-start.9 = (bf16[4,2048,256]{2,1,0:T(8,128)(2,1)}, bf16[4,2048,256]{2,1,0:T(8,128)(2,1)}, u32[]{:S(2)}, u32[]{:S(2)}) collective-permute-start(bf16[4,2048,256]{2,1,0:T(8,128)(2,1)} %get-tuple-element.151), channel_id=1, source_target_pairs={{0,4},{4,0},{8,12},{12,8},{16,20},{20,16},{24,28},{28,24},{1,5},{5... | collective-permute-start | bytes 12582920 | tf_op jit(solution)/shard_map/ppermute | solution.py:653
  474.4 48.7 %collective-permute-start.6 = (bf16[2,2,1024,256]{3,2,1,0:T(8,128)(2,1)}, bf16[2,2,1024,256]{3,2,1,0:T(8,128)(2,1)}, u32[]{:S(2)}, u32[]{:S(2)}) collective-permute-start(bf16[2,2,1024,256]{3,2,1,0:T(8,128)(2,1)} %bitcast.170), channel_id=1, source_target_pairs={{0,16},{4,20},{8,24},{12,28},{16,0},{20,4},{24,8},{28,12},{1,17},{... | collective-permute-start | bytes 6291464 | tf_op jit(solution)/shard_map/ppermute | solution.py:653
  475.9 48.8 %collective-permute-start.7 = (bf16[2,2,1024,256]{3,2,1,0:T(8,128)(2,1)}, bf16[2,2,1024,256]{3,2,1,0:T(8,128)(2,1)}, u32[]{:S(2)}, u32[]{:S(2)}) collective-permute-start(bf16[2,2,1024,256]{3,2,1,0:T(8,128)(2,1)} %bitcast.168), channel_id=1, source_target_pairs={{0,8},{4,12},{8,0},{12,4},{16,24},{20,28},{24,16},{28,20},{1,9},{5... | collective-permute-start | bytes 6291464 | tf_op jit(solution)/shard_map/ppermute | solution.py:653
  519.4 67.0 %collective-permute-start.12 = (bf16[2,2,1024,256]{3,2,1,0:T(8,128)(2,1)}, bf16[2,2,1024,256]{3,2,1,0:T(8,128)(2,1)}, u32[]{:S(2)}, u32[]{:S(2)}) collective-permute-start(bf16[2,2,1024,256]{3,2,1,0:T(8,128)(2,1)} %bitcast.171), channel_id=1, source_target_pairs={{0,16},{4,20},{8,24},{12,28},{16,0},{20,4},{24,8},{28,12},{1,17},{... | collective-permute-start | bytes 6291464 | tf_op jit(solution)/shard_map/ppermute | solution.py:653
  519.5 67.0 %collective-permute-start.13 = (bf16[2,2,1024,256]{3,2,1,0:T(8,128)(2,1)}, bf16[2,2,1024,256]{3,2,1,0:T(8,128)(2,1)}, u32[]{:S(2)}, u32[]{:S(2)}) collective-permute-start(bf16[2,2,1024,256]{3,2,1,0:T(8,128)(2,1)} %bitcast.169), channel_id=1, source_target_pairs={{0,8},{4,12},{8,0},{12,4},{16,24},{20,28},{24,16},{28,20},{1,9},{5... | collective-permute-start | bytes 6291464 | tf_op jit(solution)/shard_map/ppermute | solution.py:653
  519.8 248.1 %reduce-scatter.17.cloned.1.call-start = ((), (), s32[]{:S(2)}) async-start(), calls=%async_computation.16 | async-start | bytes 5242880 | tf_op jit(solution)/shard_map/reduce_scatter | solution.py:648
  531.9 61.5 %collective-permute-start.14 = (bf16[1,2,1024,256]{3,2,1,0:T(8,128)(2,1)S(1)}, bf16[1,2,1024,256]{3,2,1,0:T(8,128)(2,1)}, u32[]{:S(2)}, u32[]{:S(2)}) collective-permute-start(bf16[1,2,1024,256]{3,2,1,0:T(8,128)(2,1)S(1)} %slice.128), channel_id=1, source_target_pairs={{0,8},{4,12},{8,0},{12,4},{16,24},{20,28},{24,16},{28,20},{1,9},{5... | collective-permute-start | bytes 3145736 | tf_op jit(solution)/shard_map/ppermute | solution.py:653
  534.6 58.8 %collective-permute-start.15 = (bf16[1,2,1024,256]{3,2,1,0:T(8,128)(2,1)}, bf16[1,2,1024,256]{3,2,1,0:T(8,128)(2,1)}, u32[]{:S(2)}, u32[]{:S(2)}) collective-permute-start(bf16[1,2,1024,256]{3,2,1,0:T(8,128)(2,1)} %slice_bitcast_fusion.5), channel_id=1, source_target_pairs={{0,16},{4,20},{8,24},{12,28},{16,0},{20,4},{24,8},{28,12},{1,17},{... | collective-permute-start | bytes 3145736 | tf_op jit(solution)/shard_map/ppermute | solution.py:653
  550.8 70.9 %collective-permute-start.18 = (bf16[4,2048,256]{2,1,0:T(8,128)(2,1)}, bf16[4,2048,256]{2,1,0:T(8,128)(2,1)}, u32[]{:S(2)}, u32[]{:S(2)}) collective-permute-start(bf16[4,2048,256]{2,1,0:T(8,128)(2,1)} %get-tuple-element.172), channel_id=1, source_target_pairs={{0,4},{4,0},{8,12},{12,8},{16,20},{20,16},{24,28},{28,24},{1,5},{5... | collective-permute-start | bytes 12582920 | tf_op jit(solution)/shard_map/ppermute | solution.py:653
  586.4 35.3 %collective-permute-start.19 = (bf16[4,2048,256]{2,1,0:T(8,128)(2,1)}, bf16[4,2048,256]{2,1,0:T(8,128)(2,1)}, u32[]{:S(2)}, u32[]{:S(2)}) collective-permute-start(bf16[4,2048,256]{2,1,0:T(8,128)(2,1)} %get-tuple-element.173), channel_id=1, source_target_pairs={{0,4},{4,0},{8,12},{12,8},{16,20},{20,16},{24,28},{28,24},{1,5},{5... | collective-permute-start | bytes 12582920 | tf_op jit(solution)/shard_map/ppermute | solution.py:653
  586.5 8.4 %collective-permute-start.10 = (f32[2,1024]{1,0:T(2,128)S(1)}, f32[2,1024]{1,0:T(2,128)S(1)}, u32[]{:S(2)}, u32[]{:S(2)}) collective-permute-start(f32[2,1024]{1,0:T(2,128)S(1)} %pad_maximum_fusion.4), channel_id=1, source_target_pairs={{0,1},{1,0},{2,3},{3,2},{4,5},{5,4},{6,7},{7,6},{8,9},{9,8},{10,11... | collective-permute-start | bytes 24584 | tf_op jit(solution)/shard_map/ppermute | solution.py:710
  593.4 25.8 %collective-permute-start.16 = (bf16[1,2,1024,256]{3,2,1,0:T(8,128)(2,1)}, bf16[1,2,1024,256]{3,2,1,0:T(8,128)(2,1)}, u32[]{:S(2)}, u32[]{:S(2)}) collective-permute-start(bf16[1,2,1024,256]{3,2,1,0:T(8,128)(2,1)} %slice.130), channel_id=1, source_target_pairs={{0,8},{4,12},{8,0},{12,4},{16,24},{20,28},{24,16},{28,20},{1,9},{5... | collective-permute-start | bytes 3145736 | tf_op jit(solution)/shard_map/ppermute | solution.py:653
  594.9 7.0 collective-permute-start.11
  596.7 25.0 %collective-permute-start.17 = (bf16[1,2,1024,256]{3,2,1,0:T(8,128)(2,1)}, bf16[1,2,1024,256]{3,2,1,0:T(8,128)(2,1)}, u32[]{:S(2)}, u32[]{:S(2)}) collective-permute-start(bf16[1,2,1024,256]{3,2,1,0:T(8,128)(2,1)} %slice_bitcast_fusion.4), channel_id=1, source_target_pairs={{0,16},{4,20},{8,24},{12,28},{16,0},{20,4},{24,8},{28,12},{1,17},{... | collective-permute-start | bytes 3145736 | tf_op jit(solution)/shard_map/ppermute | solution.py:653
  618.1 22.9 %copy-start.14 = (bf16[128,2048]{1,0:T(8,128)(2,1)S(1)}, bf16[128,2048]{1,0:T(8,128)(2,1)}, u32[]{:S(2)}) copy-start(bf16[128,2048]{1,0:T(8,128)(2,1)} %get-tuple-element.124.normed) | copy-start | bytes 1572868
  618.2 22.9 %copy-start.28 = (bf16[128,128]{1,0:T(8,128)(2,1)S(1)}, bf16[128,128]{1,0:T(8,128)(2,1)}, u32[]{:S(2)}) copy-start(bf16[128,128]{1,0:T(8,128)(2,1)} %get-tuple-element.210) | copy-start | bytes 98308
  618.2 23.2 %copy-start.33 = (f32[1,2048]{1,0:T(1,128)S(1)}, f32[1,2048]{1,0:T(1,128)}, u32[]{:S(2)}) copy-start(f32[1,2048]{1,0:T(1,128)} %get-tuple-element.208) | copy-start | bytes 24580
  618.2 23.2 %copy-start.34 = (f32[1,2048]{1,0:T(1,128)S(1)}, f32[1,2048]{1,0:T(1,128)}, u32[]{:S(2)}) copy-start(f32[1,2048]{1,0:T(1,128)} %get-tuple-element.209) | copy-start | bytes 24580
  618.2 23.2 %copy-start.15 = (bf16[128,2048]{1,0:T(8,128)(2,1)S(1)}, bf16[128,2048]{1,0:T(8,128)(2,1)}, u32[]{:S(2)}) copy-start(bf16[128,2048]{1,0:T(8,128)(2,1)} %get-tuple-element.132.normed) | copy-start | bytes 1572868
  618.2 23.2 %copy-start.29 = (bf16[128,128]{1,0:T(8,128)(2,1)S(1)}, bf16[128,128]{1,0:T(8,128)(2,1)}, u32[]{:S(2)}) copy-start(bf16[128,128]{1,0:T(8,128)(2,1)} %get-tuple-element.211) | copy-start | bytes 98308
  639.0 46.5 %collective-permute-start.20 = (bf16[2,2,1024,256]{3,2,1,0:T(8,128)(2,1)}, bf16[2,2,1024,256]{3,2,1,0:T(8,128)(2,1)}, u32[]{:S(2)}, u32[]{:S(2)}) collective-permute-start(bf16[2,2,1024,256]{3,2,1,0:T(8,128)(2,1)} %bitcast.173), channel_id=1, source_target_pairs={{0,16},{4,20},{8,24},{12,28},{16,0},{20,4},{24,8},{28,12},{1,17},{... | collective-permute-start | bytes 6291464 | tf_op jit(solution)/shard_map/ppermute | solution.py:653
  640.4 46.3 %collective-permute-start.21 = (bf16[2,2,1024,256]{3,2,1,0:T(8,128)(2,1)}, bf16[2,2,1024,256]{3,2,1,0:T(8,128)(2,1)}, u32[]{:S(2)}, u32[]{:S(2)}) collective-permute-start(bf16[2,2,1024,256]{3,2,1,0:T(8,128)(2,1)} %bitcast.172), channel_id=1, source_target_pairs={{0,8},{4,12},{8,0},{12,4},{16,24},{20,28},{24,16},{28,20},{1,9},{5... | collective-permute-start | bytes 6291464 | tf_op jit(solution)/shard_map/ppermute | solution.py:653
  641.7 11.1 %copy-start.8 = (bf16[2,2,1024,256]{3,2,1,0:T(8,128)(2,1)S(1)}, bf16[2,2,1024,256]{3,2,1,0:T(8,128)(2,1)}, u32[]{:S(2)}) copy-start(bf16[2,2,1024,256]{3,2,1,0:T(8,128)(2,1)} %copy-done.7) | copy-start | bytes 6291460
  652.3 44.4 %collective-permute-start.24 = (bf16[2,4,256,512]{3,2,1,0:T(8,128)(2,1)}, bf16[2,4,256,512]{3,2,1,0:T(8,128)(2,1)S(1)}, u32[]{:S(2)}, u32[]{:S(2)}) collective-permute-start(bf16[2,4,256,512]{3,2,1,0:T(8,128)(2,1)} %get-tuple-element.193), channel_id=1, source_target_pairs={{0,4},{4,0},{8,12},{12,8},{16,20},{20,16},{24,28},{28,24},{1,5},{5... | collective-permute-start | bytes 6291464 | tf_op jit(solution)/shard_map/ppermute | solution.py:653
  652.3 44.4 %collective-permute-start.25 = (bf16[2,4,256,512]{3,2,1,0:T(8,128)(2,1)}, bf16[2,4,256,512]{3,2,1,0:T(8,128)(2,1)}, u32[]{:S(2)}, u32[]{:S(2)}) collective-permute-start(bf16[2,4,256,512]{3,2,1,0:T(8,128)(2,1)} %get-tuple-element.194), channel_id=1, source_target_pairs={{0,4},{4,0},{8,12},{12,8},{16,20},{20,16},{24,28},{28,24},{1,5},{5... | collective-permute-start | bytes 6291464 | tf_op jit(solution)/shard_map/ppermute | solution.py:653
  655.9 30.8 %copy-start.21 = (bf16[4,1024,256]{2,1,0:T(8,128)(2,1)S(1)}, bf16[4,1024,256]{2,1,0:T(8,128)(2,1)}, u32[]{:S(2)}) copy-start(bf16[4,1024,256]{2,1,0:T(8,128)(2,1)} %get-tuple-element.186) | copy-start | bytes 6291460
  690.0 43.6 %collective-permute-start.22 = (bf16[1,2,1024,256]{3,2,1,0:T(8,128)(2,1)}, bf16[1,2,1024,256]{3,2,1,0:T(8,128)(2,1)}, u32[]{:S(2)}, u32[]{:S(2)}) collective-permute-start(bf16[1,2,1024,256]{3,2,1,0:T(8,128)(2,1)} %slice.132), channel_id=1, source_target_pairs={{0,8},{4,12},{8,0},{12,4},{16,24},{20,28},{24,16},{28,20},{1,9},{5... | collective-permute-start | bytes 3145736 | tf_op jit(solution)/shard_map/ppermute | solution.py:653
  696.1 14.8 %copy-start.37 = (f32[1,512]{1,0:T(1,128)S(1)}, f32[1,512]{1,0:T(1,128)}, u32[]{:S(2)}) copy-start(f32[1,512]{1,0:T(1,128)} %get-tuple-element.207) | copy-start | bytes 6148
  696.1 14.9 %copy-start.25 = (f32[2048]{0:T(1024)S(1)}, f32[2048]{0:T(1024)}, u32[]{:S(2)}) copy-start(f32[2048]{0:T(1024)} %param.33) | copy-start | bytes 24580
  696.1 14.9 %copy-start.35 = (f32[1,2048]{1,0:T(1,128)S(1)}, f32[1,2048]{1,0:T(1,128)}, u32[]{:S(2)}) copy-start(f32[1,2048]{1,0:T(1,128)} %get-tuple-element.205) | copy-start | bytes 24580
  696.1 37.5 %collective-permute-start.23 = (bf16[1,2,1024,256]{3,2,1,0:T(8,128)(2,1)}, bf16[1,2,1024,256]{3,2,1,0:T(8,128)(2,1)}, u32[]{:S(2)}, u32[]{:S(2)}) collective-permute-start(bf16[1,2,1024,256]{3,2,1,0:T(8,128)(2,1)} %slice_bitcast_fusion.3), channel_id=1, source_target_pairs={{0,16},{4,20},{8,24},{12,28},{16,0},{20,4},{24,8},{28,12},{1,17},{... | collective-permute-start | bytes 3145736 | tf_op jit(solution)/shard_map/ppermute | solution.py:653
  710.1 25.2 %collective-permute-start.28 = (bf16[2,4,128,512]{3,2,1,0:T(8,128)(2,1)}, bf16[2,4,128,512]{3,2,1,0:T(8,128)(2,1)}, u32[]{:S(2)}, u32[]{:S(2)}) collective-permute-start(bf16[2,4,128,512]{3,2,1,0:T(8,128)(2,1)} %get-tuple-element.201), channel_id=1, source_target_pairs={{0,8},{4,12},{8,0},{12,4},{16,24},{20,28},{24,16},{28,20},{1,9},{5... | collective-permute-start | bytes 3145736 | tf_op jit(solution)/shard_map/ppermute | solution.py:653
  711.4 5.4 copy-start.3
  711.4 3.3 collective-permute-start.30
  713.4 30.1 %collective-permute-start.26 = (bf16[2,4,128,512]{3,2,1,0:T(8,128)(2,1)}, bf16[2,4,128,512]{3,2,1,0:T(8,128)(2,1)}, u32[]{:S(2)}, u32[]{:S(2)}) collective-permute-start(bf16[2,4,128,512]{3,2,1,0:T(8,128)(2,1)} %get-tuple-element.200), channel_id=1, source_target_pairs={{0,16},{4,20},{8,24},{12,28},{16,0},{20,4},{24,8},{28,12},{1,17},{... | collective-permute-start | bytes 3145736 | tf_op jit(solution)/shard_map/ppermute | solution.py:653
  714.8 7.1 collective-permute-start.31
  722.0 11.5 %collective-permute-start.32 = (f32[20,2048]{1,0:T(8,128)S(1)}, f32[20,2048]{1,0:T(8,128)S(1)}, u32[]{:S(2)}, u32[]{:S(2)}) collective-permute-start(f32[20,2048]{1,0:T(8,128)S(1)} %add.187), channel_id=1, source_target_pairs={{0,2},{1,3},{2,0},{3,1},{4,6},{5,7},{6,4},{7,5},{8,10},{9,11},{10,... | collective-permute-start | bytes 491528 | tf_op jit(solution)/shard_map/ppermute | solution.py:710
  733.5 10.0 %copy-start.23 = (bf16[2,4,128,512]{3,2,1,0:T(8,128)(2,1)S(1)}, bf16[2,4,128,512]{3,2,1,0:T(8,128)(2,1)}, u32[]{:S(2)}) copy-start(bf16[2,4,128,512]{3,2,1,0:T(8,128)(2,1)} %get-tuple-element.203) | copy-start | bytes 3145732
  737.2 10.0 %copy-start.12 = (bf16[2,2,1024,256]{3,2,1,0:T(8,128)(2,1)S(1)}, bf16[2,2,1024,256]{3,2,1,0:T(8,128)(2,1)}, u32[]{:S(2)}) copy-start(bf16[2,2,1024,256]{3,2,1,0:T(8,128)(2,1)} %copy-done.11) | copy-start | bytes 6291460
  737.2 29.0 %collective-permute-start.29 = (bf16[1,4,128,512]{3,2,1,0:T(8,128)(2,1)S(1)}, bf16[1,4,128,512]{3,2,1,0:T(8,128)(2,1)S(1)}, u32[]{:S(2)}, u32[]{:S(2)}) collective-permute-start(bf16[1,4,128,512]{3,2,1,0:T(8,128)(2,1)S(1)} %slice_bitcast_fusion.6), channel_id=1, source_target_pairs={{0,16},{4,20},{8,24},{12,28},{16,0},{20,4},{24,8},{28,12},{1,17},{... | collective-permute-start | bytes 1572872 | tf_op jit(solution)/shard_map/ppermute | solution.py:653
  745.1 21.2 %collective-permute-start.27 = (bf16[1,4,128,512]{3,2,1,0:T(8,128)(2,1)S(1)}, bf16[1,4,128,512]{3,2,1,0:T(8,128)(2,1)S(1)}, u32[]{:S(2)}, u32[]{:S(2)}) collective-permute-start(bf16[1,4,128,512]{3,2,1,0:T(8,128)(2,1)S(1)} %slice.135), channel_id=1, source_target_pairs={{0,8},{4,12},{8,0},{12,4},{16,24},{20,28},{24,16},{28,20},{1,9},{5... | collective-permute-start | bytes 1572872 | tf_op jit(solution)/shard_map/ppermute | solution.py:653
  745.2 13.9 %collective-permute-start.33 = (f32[20,2048]{1,0:T(8,128)S(1)}, f32[20,2048]{1,0:T(8,128)S(1)}, u32[]{:S(2)}, u32[]{:S(2)}) collective-permute-start(f32[20,2048]{1,0:T(8,128)S(1)} %add.188), channel_id=1, source_target_pairs={{0,8},{4,12},{8,0},{12,4},{16,24},{20,28},{24,16},{28,20},{1,9},{5... | collective-permute-start | bytes 491528 | tf_op jit(solution)/shard_map/ppermute | solution.py:710
  759.1 5.7 collective-permute-start.34
  (24 other events, 58.8 us)
Sparse Core Ops, SparseCore 0:
  12.7 83.4 all-gather.5
  97.8 79.6 all-gather.7
  180.3 42.3 reduce-scatter.6
  225.5 43.1 reduce-scatter.8
  270.2 45.2 all-gather.9
  317.5 44.6 all-gather.11
  364.5 44.7 reduce-scatter.12
  411.5 45.3 reduce-scatter.10
  473.9 79.7 all-gather.13
  555.9 75.6 reduce-scatter.14
  634.0 77.2 reduce-scatter.16
